TPU v7x, 32 devices: a whole 2x2x4 slice. The times are simulated.
32 devices in a mesh: group: 2 (over x), expert: 16 (over z, y, core).
Axes of the slice: x: 2, y: 2, z: 4, core: 2. Of those that a mesh axis runs over, the one named last changes fastest.
Arguments:
- tokens: bfloat16 [4096, 1024], P(('group', 'expert')), parts along dimension 0, may hold values from -6 to 6
- cotangent: bfloat16 [4096, 1024], P(('group', 'expert')), parts along dimension 0, may hold values from -6 to 6
- routes: int32 [4096, 2], P(('group', 'expert')), parts along dimension 0, may hold values from 0 to 3, all different within a row; in each aligned block of 128 rows (0 to 127, 128 to 255, ...) at most 96 rows name the same one
- gate_nums: int32 [4096, 2], P(('group', 'expert')), parts along dimension 0, may hold values from 1 to 8
- gain: float32 [1024], replicated, may hold values from 0.5 to 1.5
- w_gate: bfloat16 [16, 1024, 1024], P('expert'), may hold values from -0.1875 to 0.1875
- w_up: bfloat16 [16, 1024, 1024], P('expert'), may hold values from -0.1875 to 0.1875
- w_down: bfloat16 [16, 1024, 1024], P('expert'), may hold values from -0.1875 to 0.1875
Outputs:
- mixed: bfloat16 [4096, 1024], P(('group', 'expert')), parts along dimension 0
- grad_down: bfloat16 [32, 1024, 1024], P(('group', 'expert')), parts along dimension 0
There are 2 independent parts, one for each index of `group`. A program takes and returns all parts, laid end to end along the dimension named above; an argument that names none is the same for every part. Nothing has to cross between parts.
Inputs may be any that keep to these rules, and one draw needn't show every extreme that they name: In each aligned block of 128 frames (the frames of one device) no expert is named by more than 96 routes, a bound that some block reaches; a frame names 2 different experts.
All inputs are finite; a program needn't handle non-finite values.
Results may differ from a plain program's by a relative error of at most 0.0072.
Values may be sent and summed in bfloat16 or wider, within the bound.
No kernel may reach another device: no remote copies, remote signals or barrier semaphores. Data moves between devices by JAX's collectives and lax.ppermute only.
A program may use at most 64 MiB of HBM per device.

v0:
```python
import jax
import jax.numpy as jnp
from jax import lax
from jax.sharding import PartitionSpec as P

HSPLIT = 4


def on_device(tokens, cotangent, routes, gate_nums, gain, w_gate, w_up, w_down):
    devices = lax.axis_size("expert")
    experts = devices // HSPLIT
    rows_here = tokens.shape[0]
    model_width = tokens.shape[1]
    top_count = routes.shape[1]
    capacity = HSPLIT * (3 * top_count * rows_here // (2 * experts * HSPLIT))
    slots_all = experts * capacity
    frames = tokens.astype(jnp.float32)
    inverse = lax.rsqrt(jnp.mean(frames * frames, -1, keepdims=True) + 1e-06)
    normed = (frames * inverse * gain).astype(jnp.bfloat16)
    numerators = gate_nums.astype(jnp.float32)
    gates = numerators / jnp.sum(numerators, -1, keepdims=True)
    scaled = (gates[:, :, None] * cotangent.astype(jnp.float32)[:, None, :]).astype(jnp.bfloat16)
    scaled = scaled.reshape(rows_here * top_count, model_width)
    flat_routes = routes.reshape(-1)
    onehot = (flat_routes[:, None] == jnp.arange(experts, dtype=jnp.int32)[None, :]).astype(
        jnp.int32
    )
    within = jnp.sum((jnp.cumsum(onehot, axis=0) - 1) * onehot, 1)
    slot_index = flat_routes * capacity + within
    matches = slot_index[None, :] == jnp.arange(slots_all, dtype=jnp.int32)[:, None]
    placing = matches.astype(jnp.bfloat16)
    placing_rows = jnp.sum(placing.reshape(slots_all, rows_here, top_count), -1)
    send_rows = jnp.dot(placing_rows, normed, preferred_element_type=jnp.float32).astype(
        jnp.bfloat16
    )
    send_grads = jnp.dot(placing, scaled, preferred_element_type=jnp.float32).astype(jnp.bfloat16)
    send_rows = jnp.repeat(send_rows.reshape(experts, capacity, model_width), HSPLIT, axis=0)
    send_grads = jnp.repeat(send_grads.reshape(experts, capacity, model_width), HSPLIT, axis=0)
    gate_block = w_gate[0]
    up_block = w_up[0]
    down_block = w_down[0]
    recv_rows, recv_grads = (
        lax.all_to_all(send_rows, "expert", split_axis=0, concat_axis=0, tiled=True),
        lax.all_to_all(send_grads, "expert", split_axis=0, concat_axis=0, tiled=True),
    )
    rows = recv_rows.reshape(-1, model_width)
    cot_rows = recv_grads.reshape(-1, model_width)
    pre_gate = jnp.dot(rows, gate_block, preferred_element_type=jnp.float32)
    pre_up = jnp.dot(rows, up_block, preferred_element_type=jnp.float32)
    hidden = (jax.nn.silu(pre_gate) * pre_up).astype(jnp.bfloat16)
    partial_value = jnp.dot(hidden, down_block, preferred_element_type=jnp.float32).astype(
        jnp.bfloat16
    )
    hidden, partial_value = (hidden, partial_value)
    returned = lax.all_to_all(
        partial_value.reshape(devices, capacity, model_width),
        "expert",
        split_axis=0,
        concat_axis=0,
        tiled=True,
    )
    summed = jnp.sum(
        returned.astype(jnp.float32).reshape(experts, HSPLIT, capacity, model_width), axis=1
    )
    summed = summed.reshape(slots_all, model_width)
    grad_down = lax.dot_general(
        hidden, cot_rows, (((0,), (0,)), ((), ())), preferred_element_type=jnp.float32
    )
    grad_down = grad_down.astype(jnp.bfloat16)[None]
    combine_map = (slot_index[:, None] == jnp.arange(slots_all, dtype=jnp.int32)[None, :]).astype(
        jnp.float32
    )
    combine_map = combine_map * gates.reshape(-1)[:, None]
    combine_map = jnp.sum(combine_map.reshape(rows_here, top_count, slots_all), axis=1)
    branch = jnp.dot(
        combine_map, summed, precision=lax.Precision.HIGHEST, preferred_element_type=jnp.float32
    )
    mixed = (frames + branch).astype(jnp.bfloat16)
    return (mixed, grad_down)


def solution(mesh):
    placed = (
        P(("group", "expert"), None),
        P(("group", "expert"), None),
        P(("group", "expert"), None),
        P(("group", "expert"), None),
        P(),
        P("expert", None, None),
        P("expert", None, None),
        P("expert", None, None),
    )
    return jax.shard_map(
        on_device,
        mesh=mesh,
        in_specs=placed,
        out_specs=(P(("group", "expert"), None), P(("group", "expert"), None, None)),
        check_vma=False,
    )
```

profile of v0, /device:TPU:15, one launch (start us, length us, event | category | flops | bytes accessed | tf_op | source)
XLA Modules:
  0.0 242.2 jit_solution(14818169659779772874)
XLA Ops:
  0.6 0.9 copy.32
  1.6 0.1 eq.63
  1.7 0.1 eq.59
  1.9 1.2 reduce-window.6
  3.2 0.1 copy.34
  3.3 0.1 copy.35
  3.4 0.1 add_bitcast_fusion
  3.5 0.1 reduce_sum.60
  3.7 0.7 multiply_add_fusion.1
  4.5 1.1 fusion.5
  5.6 1.4 convolution_convert_fusion.2
  7.0 2.1 broadcast_in_dim.6
  9.1 6.7 %all-to-all-start = ((bf16[16,96,1024]{2,1,0:T(8,128)(2,1)}), bf16[16,96,1024]{2,1,0:T(8,128)(2,1)}, u32[]{:S(2)}, u32[]{:S(2)}) async-start(bf16[16,96,1024]{2,1,0:T(8,128)(2,1)} %bitcast.45), calls=%async_computation | async-start | bytes 6291456 | tf_op jit(solution)/shard_map/all_to_all | solution.py:43
  15.8 0.1 copy.37
  15.9 0.1 mul.88
  16.0 0.3 mul.90
  16.3 1.7 mul.91
  18.0 1.7 convolution_convert_fusion.1
  19.7 66.0 %all-to-all-done = bf16[16,96,1024]{2,1,0:T(8,128)(2,1)} async-done(((bf16[16,96,1024]{2,1,0:T(8,128)(2,1)}), bf16[16,96,1024]{2,1,0:T(8,128)(2,1)}, u32[]{:S(2)}, u32[]{:S(2)}) %all-to-all-start) | async-done | bytes 3145760 | tf_op jit(solution)/shard_map/all_to_all | solution.py:43
  85.7 2.0 broadcast_in_dim.7
  87.8 4.9 %all-to-all-start.2 = ((bf16[16,96,1024]{2,1,0:T(8,128)(2,1)}), bf16[16,96,1024]{2,1,0:T(8,128)(2,1)}, u32[]{:S(2)}, u32[]{:S(2)}) async-start(bf16[16,96,1024]{2,1,0:T(8,128)(2,1)} %bitcast.46), calls=%async_computation.2 | async-start | bytes 6291456 | tf_op jit(solution)/shard_map/all_to_all | solution.py:44
  92.7 5.5 %fusion.2 = f32[1536,1024]{1,0:T(8,128)S(1)} fusion(bf16[1536,1024]{1,0:T(8,128)(2,1)} %bitcast.4, bf16[1,1024,1024]{2,1,0:T(8,128)(2,1)S(1)} %copy-done), kind=kOutput, calls=%fused_computation.5 | convolution fusion | flops 3221225472 | bytes 11534336 | tf_op jit(solution)/shard_map/dot_general | solution.py:48
  98.3 6.9 %multiply_convert_fusion = bf16[1536,1024]{1,0:T(8,128)(2,1)S(1)} fusion(f32[1536,1024]{1,0:T(8,128)S(1)} %fusion.2, bf16[1536,1024]{1,0:T(8,128)(2,1)} %bitcast.4, bf16[1,1024,1024]{2,1,0:T(8,128)(2,1)S(1)} %copy-done.4), kind=kOutput, calls=%fused_computation.1 | convolution fusion | flops 3230662656 | bytes 14680064 | tf_op jit(solution)/shard_map/dot_general | solution.py:49
  105.2 1.7 copy-done.6
  106.9 4.8 %convolution_convert_fusion = bf16[1536,1024]{1,0:T(8,128)(2,1)} fusion(bf16[1536,1024]{1,0:T(8,128)(2,1)S(1)} %multiply_convert_fusion, bf16[1,1024,1024]{2,1,0:T(8,128)(2,1)S(1)} %copy-done.5), kind=kOutput, calls=%fused_computation.2 | convolution fusion | flops 3222798336 | bytes 8388608 | tf_op jit(solution)/shard_map/dot_general | solution.py:51
  111.7 51.0 %all-to-all-done.2 = bf16[16,96,1024]{2,1,0:T(8,128)(2,1)} async-done(((bf16[16,96,1024]{2,1,0:T(8,128)(2,1)}), bf16[16,96,1024]{2,1,0:T(8,128)(2,1)}, u32[]{:S(2)}, u32[]{:S(2)}) %all-to-all-start.2) | async-done | bytes 3145760 | tf_op jit(solution)/shard_map/all_to_all | solution.py:44
  162.7 4.9 %all-to-all-start.1 = ((bf16[16,96,1024]{2,1,0:T(8,128)(2,1)}), bf16[16,96,1024]{2,1,0:T(8,128)(2,1)}, u32[]{:S(2)}, u32[]{:S(2)}) async-start(bf16[16,96,1024]{2,1,0:T(8,128)(2,1)} %bitcast.48), calls=%async_computation.1 | async-start | bytes 6291456 | tf_op jit(solution)/shard_map/all_to_all | solution.py:55
  167.6 0.1 select_reduce_fusion
  167.7 7.7 %convert_bitcast_fusion = bf16[1,1024,1024]{2,1,0:T(8,128)(2,1)} fusion(bf16[1536,1024]{1,0:T(8,128)(2,1)} %copy-done.6, bf16[1536,1024]{1,0:T(8,128)(2,1)} %bitcast.13), kind=kOutput, calls=%fused_computation.7 | convolution fusion | flops 3222274048 | bytes 8388608 | tf_op jit(solution)/shard_map/dot_general | solution.py:66
  175.4 62.2 %all-to-all-done.1 = bf16[16,96,1024]{2,1,0:T(8,128)(2,1)} async-done(((bf16[16,96,1024]{2,1,0:T(8,128)(2,1)}), bf16[16,96,1024]{2,1,0:T(8,128)(2,1)}, u32[]{:S(2)}, u32[]{:S(2)}) %all-to-all-start.1) | async-done | bytes 3145760 | tf_op jit(solution)/shard_map/all_to_all | solution.py:55
  237.6 2.8 %convert_reduce_fusion = f32[4,96,1024]{2,1,0:T(8,128)S(1)} fusion(bf16[16,96,1024]{2,1,0:T(8,128)(2,1)} %all-to-all-done.1), kind=kLoop, calls=%fused_computation | loop fusion | flops 2752512 | bytes 4718592 | tf_op jit(solution)/shard_map/reduce_sum | solution.py:62
  240.4 1.8 fusion.4
  (24 shorter events, 0.3 us)
Async XLA Ops:
  0.6 92.1 %copy-start = (bf16[1,1024,1024]{2,1,0:T(8,128)(2,1)S(1)}, bf16[1,1024,1024]{2,1,0:T(8,128)(2,1)}, u32[]{:S(2)}) copy-start(bf16[1,1024,1024]{2,1,0:T(8,128)(2,1)} %param.13) | copy-start | bytes 6291460
  9.1 6.7 %copy-start.3 = (s32[128,2]{0,1:T(2,128)S(1)}, s32[128,2]{0,1:T(2,128)}, u32[]{:S(2)}) copy-start(s32[128,2]{0,1:T(2,128)} %param.11) | copy-start | bytes 3076
  9.1 7.0 %copy-start.2 = (bf16[128,1024]{1,0:T(8,128)(2,1)S(1)}, bf16[128,1024]{1,0:T(8,128)(2,1)}, u32[]{:S(2)}) copy-start(bf16[128,1024]{1,0:T(8,128)(2,1)} %param.9) | copy-start | bytes 786436
  9.1 76.7 %all-to-all-start = ((bf16[16,96,1024]{2,1,0:T(8,128)(2,1)}), bf16[16,96,1024]{2,1,0:T(8,128)(2,1)}, u32[]{:S(2)}, u32[]{:S(2)}) async-start(bf16[16,96,1024]{2,1,0:T(8,128)(2,1)} %bitcast.45), calls=%async_computation | async-start | bytes 6291456 | tf_op jit(solution)/shard_map/all_to_all | solution.py:43
  87.8 74.9 %all-to-all-start.2 = ((bf16[16,96,1024]{2,1,0:T(8,128)(2,1)}), bf16[16,96,1024]{2,1,0:T(8,128)(2,1)}, u32[]{:S(2)}, u32[]{:S(2)}) async-start(bf16[16,96,1024]{2,1,0:T(8,128)(2,1)} %bitcast.46), calls=%async_computation.2 | async-start | bytes 6291456 | tf_op jit(solution)/shard_map/all_to_all | solution.py:44
  92.7 5.6 %copy-start.4 = (bf16[1,1024,1024]{2,1,0:T(8,128)(2,1)S(1)}, bf16[1,1024,1024]{2,1,0:T(8,128)(2,1)}, u32[]{:S(2)}) copy-start(bf16[1,1024,1024]{2,1,0:T(8,128)(2,1)} %param.14) | copy-start | bytes 6291460
  98.3 8.7 %copy-start.5 = (bf16[1,1024,1024]{2,1,0:T(8,128)(2,1)S(1)}, bf16[1,1024,1024]{2,1,0:T(8,128)(2,1)}, u32[]{:S(2)}) copy-start(bf16[1,1024,1024]{2,1,0:T(8,128)(2,1)} %param.15) | copy-start | bytes 6291460
  105.2 1.7 copy-start.6
  162.7 74.9 %all-to-all-start.1 = ((bf16[16,96,1024]{2,1,0:T(8,128)(2,1)}), bf16[16,96,1024]{2,1,0:T(8,128)(2,1)}, u32[]{:S(2)}, u32[]{:S(2)}) async-start(bf16[16,96,1024]{2,1,0:T(8,128)(2,1)} %bitcast.48), calls=%async_computation.1 | async-start | bytes 6291456 | tf_op jit(solution)/shard_map/all_to_all | solution.py:55
  175.4 65.0 %copy-start.1 = (bf16[128,1024]{1,0:T(8,128)(2,1)S(1)}, bf16[128,1024]{1,0:T(8,128)(2,1)}, u32[]{:S(2)}) copy-start(bf16[128,1024]{1,0:T(8,128)(2,1)} %param.8) | copy-start | bytes 786436
where the time goes:
time: 243 us; the launch traced here: 242 us
  waiting for transfers between devices  179 us (74%)
  matrix products  29.8 us (12%)
  starting transfers between devices  16.5 us (7%)
  local copies, waits for them, and re-layouts  9.73 us (4%)
  other arithmetic  6.14 us (3%)
    all_to_all x1, waiting for transfers between devices, on_device(): lax.all_to_all(send_rows, 'expert', split_axis=0, concat_axis=0, tiled=True)  66 us
    all_to_all x1, waiting for transfers between devices, on_device(): lax.all_to_all(partial_value.reshape(devices, capacity, model_width), 'ex...  62.2 us
    all_to_all x1, waiting for transfers between devices, on_device(): lax.all_to_all(send_grads, 'expert', split_axis=0, concat_axis=0, tiled=T...  51 us
    dot_general x1, matrix products, on_device(): lax.dot_general(hidden, cot_rows, (((0,), (0,)), ((), ())), preferred_ele...  7.65 us
    dot_general x1, matrix products, on_device(): pre_up = jnp.dot(rows, up_block, preferred_element_type=jnp.float32)  6.93 us
    all_to_all x1, starting transfers between devices, on_device(): lax.all_to_all(send_rows, 'expert', split_axis=0, concat_axis=0, tiled=True)  6.69 us
    dot_general x1, matrix products, on_device(): pre_gate = jnp.dot(rows, gate_block, preferred_element_type=jnp.float32)  5.54 us
    all_to_all x1, starting transfers between devices, on_device(): lax.all_to_all(partial_value.reshape(devices, capacity, model_width), 'ex...  4.91 us
  transfers between devices with their start and end apart: 3, of which 3 were waited for; matrix products, arithmetic and copies ran while one was open for 12% of the time, Pallas kernels for 0%

commit v1 on v0

v1 whole, which is shorter than its diff:
```python
import functools

import jax
import jax.numpy as jnp
from jax import lax
from jax.experimental import pallas as pl
from jax.experimental.pallas import tpu as pltpu
from jax.sharding import PartitionSpec as P

HSPLIT = 4
TILE = 256
F32 = jnp.float32
BF16 = jnp.bfloat16


def whole(count):
    return [pl.BlockSpec(memory_space=pltpu.VMEM)] * count


def params(mib):
    return pltpu.CompilerParams(vmem_limit_bytes=mib << 20)


def named_by(routes, plane, experts):
    rows = routes.shape[0]
    expert = lax.broadcasted_iota(jnp.int32, (rows, experts), 1) ^ plane
    member = jnp.zeros((rows, experts), jnp.bool_)
    for k in range(routes.shape[1]):
        member = member | (routes[:, k : k + 1] == expert)
    return member


def gate_of(routes, numerators, plane, experts):
    rows = routes.shape[0]
    expert = lax.broadcasted_iota(jnp.int32, (rows, experts), 1) ^ plane
    gates = numerators / jnp.sum(numerators, -1, keepdims=True)
    gate = jnp.zeros((rows, experts), F32)
    for k in range(routes.shape[1]):
        gate = gate + jnp.where(routes[:, k : k + 1] == expert, gates[:, k : k + 1], 0.0)
    return gate


def placing_of(member, capacity):
    rows, experts = member.shape
    ones = member.astype(F32).astype(BF16)
    first = lax.broadcasted_iota(jnp.int32, (rows, rows), 0)
    second = lax.broadcasted_iota(jnp.int32, (rows, rows), 1)
    upto = (first <= second).astype(F32).astype(BF16)
    same = (first == second).astype(F32).astype(BF16)
    over_rows = (((0,), (0,)), ((), ()))
    count = lax.dot_general(ones, upto, over_rows, preferred_element_type=F32)
    here = lax.dot_general(ones, same, over_rows, preferred_element_type=F32)
    place = jnp.where(here > 0.5, count, 0.0).astype(jnp.int32) - 1
    slots = lax.broadcasted_iota(jnp.int32, (capacity, rows), 0)
    return [
        (slots == place[s : s + 1, :]).astype(F32).astype(BF16) for s in range(experts)
    ]


def send_rows_kernel(experts, plane_ref, tokens_ref, gain_ref, routes_ref, *outs):
    frames = tokens_ref[...].astype(F32)
    inverse = lax.rsqrt(jnp.mean(frames * frames, -1, keepdims=True) + 1e-06)
    normed = (frames * inverse * gain_ref[...]).astype(BF16)
    member = named_by(routes_ref[...], plane_ref[0], experts)
    for out, placing in zip(outs, placing_of(member, outs[0].shape[0])):
        out[...] = jnp.dot(placing, normed, preferred_element_type=F32).astype(BF16)


def send_grads_kernel(experts, plane_ref, cot_ref, routes_ref, nums_ref, *outs):
    cot = cot_ref[...].astype(F32)
    routes = routes_ref[...]
    member = named_by(routes, plane_ref[0], experts)
    gate = gate_of(routes, nums_ref[...].astype(F32), plane_ref[0], experts)
    for s, (out, placing) in enumerate(zip(outs, placing_of(member, outs[0].shape[0]))):
        scaled = (gate[:, s : s + 1] * cot).astype(BF16)
        out[...] = jnp.dot(placing, scaled, preferred_element_type=F32).astype(BF16)


def ffn_kernel(shifts, *refs):
    pieces, refs = refs[: 4 * shifts], refs[4 * shifts :]
    gate_ref, up_ref, down_ref, hidden_ref = refs[:4]
    keeps, sends, rows_ref = refs[4 : 4 + shifts], refs[4 + shifts : 4 + 2 * shifts], refs[-1]
    capacity = pieces[0].shape[0]
    for i, piece in enumerate(pieces):
        rows_ref[i * capacity : (i + 1) * capacity, :] = piece[...]
    width = gate_ref.shape[2]

    @pl.loop(0, width // TILE)
    def _(j):
        columns = pl.ds(pl.multiple_of(j * TILE, TILE), TILE)
        rows = rows_ref[...]
        pre_gate = jnp.dot(rows, gate_ref[0, :, columns], preferred_element_type=F32)
        pre_up = jnp.dot(rows, up_ref[0, :, columns], preferred_element_type=F32)
        hidden_ref[:, columns] = (pre_gate * lax.logistic(pre_gate) * pre_up).astype(BF16)

    @pl.loop(0, down_ref.shape[2] // TILE)
    def _(j):
        columns = pl.ds(pl.multiple_of(j * TILE, TILE), TILE)
        value = jnp.dot(
            hidden_ref[...], down_ref[0, :, columns], preferred_element_type=F32
        ).astype(BF16)
        for i in range(shifts):
            at = 4 * i * capacity
            keeps[i][:, columns] = value[at : at + 2 * capacity]
            sends[i][:, columns] = value[at + 2 * capacity : at + 4 * capacity]


def grad_kernel(chunks, per_chunk, *refs):
    hiddens, pieces = refs[:chunks], refs[chunks : chunks + chunks * per_chunk]
    out_ref, cot_ref = refs[-2:]
    capacity = pieces[0].shape[0]
    for i, piece in enumerate(pieces):
        cot_ref[i * capacity : (i + 1) * capacity, :] = piece[...]
    rows = capacity * per_chunk

    @pl.loop(0, out_ref.shape[2] // TILE)
    def _(j):
        columns = pl.ds(pl.multiple_of(j * TILE, TILE), TILE)
        total = jnp.zeros((out_ref.shape[1], TILE), F32)
        for i, hidden in enumerate(hiddens):
            total = total + lax.dot_general(
                hidden[...],
                cot_ref[i * rows : (i + 1) * rows, columns],
                (((0,), (0,)), ((), ())),
                preferred_element_type=F32,
            )
        out_ref[0, :, columns] = total.astype(BF16)


def combine_kernel(experts, plane_ref, tokens_ref, routes_ref, nums_ref, *refs):
    values, out = refs[:-1], refs[-1]
    routes = routes_ref[...]
    rows = routes.shape[0]
    capacity = values[0].shape[0]
    member = named_by(routes, plane_ref[0], experts)
    gate = gate_of(routes, nums_ref[...].astype(F32), plane_ref[0], experts)
    first = lax.broadcasted_iota(jnp.int32, (rows, rows), 0)
    second = lax.broadcasted_iota(jnp.int32, (rows, rows), 1)
    before = (second <= first).astype(F32).astype(BF16)
    count = jnp.dot(before, member.astype(F32).astype(BF16), preferred_element_type=F32)
    place = jnp.where(member, count, 0.0).astype(jnp.int32) - 1
    slots = lax.broadcasted_iota(jnp.int32, (rows, capacity), 1)
    total = jnp.zeros(tokens_ref.shape, F32)
    for s, value in enumerate(values):
        picking = (slots == place[:, s : s + 1]).astype(F32).astype(BF16)
        picked = jnp.dot(picking, value[...], preferred_element_type=F32)
        total = total + gate[:, s : s + 1] * picked
    out[...] = (tokens_ref[...].astype(F32) + total).astype(BF16)


def on_device(tokens, cotangent, routes, gate_nums, gain, w_gate, w_up, w_down):
    devices = lax.axis_size("expert")
    experts = devices // HSPLIT
    rows_here, width = tokens.shape
    hidden_width = w_gate.shape[2]
    top_count = routes.shape[1]
    capacity = HSPLIT * (3 * top_count * rows_here // (2 * experts * HSPLIT))
    capacity = -(-capacity // 16) * 16
    chunks = min(4, experts)
    shifts = experts // chunks
    plane = (lax.axis_index("expert") // HSPLIT).astype(jnp.int32).reshape(1)
    scalar = pl.BlockSpec(memory_space=pltpu.SMEM)

    def swap(value, mask):
        return lax.ppermute(value, "expert", [(i, i ^ mask) for i in range(devices)])

    piece = jax.ShapeDtypeStruct((capacity, width), BF16)
    placed_flops = 2 * experts * capacity * rows_here * width
    send_rows = pl.pallas_call(
        functools.partial(send_rows_kernel, experts),
        out_shape=[piece] * experts,
        in_specs=[scalar] + whole(3),
        out_specs=whole(experts),
        compiler_params=params(16),
        cost_estimate=pl.CostEstimate(
            flops=placed_flops, bytes_accessed=2 << 20, transcendentals=0
        ),
        name="send_rows",
    )(plane, tokens, gain.reshape(1, -1), routes)
    send_grads = pl.pallas_call(
        functools.partial(send_grads_kernel, experts),
        out_shape=[piece] * experts,
        in_specs=[scalar] + whole(3),
        out_specs=whole(experts),
        compiler_params=params(16),
        cost_estimate=pl.CostEstimate(
            flops=placed_flops, bytes_accessed=2 << 20, transcendentals=0
        ),
        name="send_grads",
    )(plane, cotangent, routes, gate_nums)

    def spread(value, shift):
        mine = value if shift == 0 else swap(value, shift * HSPLIT)
        other = swap(mine, 2)
        return [mine, other, swap(mine, 1), swap(other, 1)]

    rows = [spread(send_rows[s], s) for s in range(experts)]
    grads = [spread(send_grads[s], s) for s in range(experts)]

    rows_chunk = 4 * shifts * capacity
    hiddens, returned = [], []
    for chunk in range(chunks):
        pieces = [p for s in range(chunk * shifts, (chunk + 1) * shifts) for p in rows[s]]
        half = jax.ShapeDtypeStruct((2 * capacity, width), BF16)
        outs = pl.pallas_call(
            functools.partial(ffn_kernel, shifts),
            out_shape=[jax.ShapeDtypeStruct((rows_chunk, hidden_width), BF16)] + [half] * (2 * shifts),
            in_specs=whole(len(pieces) + 3),
            out_specs=whole(1 + 2 * shifts),
            scratch_shapes=[pltpu.VMEM((rows_chunk, width), BF16)],
            compiler_params=params(28),
            cost_estimate=pl.CostEstimate(
                flops=6 * rows_chunk * width * hidden_width,
                bytes_accessed=8 << 20,
                transcendentals=0,
            ),
            name="ffn",
        )(*pieces, w_gate, w_up, w_down)
        hiddens.append(outs[0])
        for i in range(shifts):
            keep, send = outs[1 + i], outs[1 + shifts + i]
            received = swap(send, 1)
            both = keep.astype(F32) + received.astype(F32)
            to_send = both[capacity:].astype(BF16)
            other = swap(to_send, 2)
            mine = (both[:capacity] + other.astype(F32)).astype(BF16)
            shift = chunk * shifts + i
            returned.append(mine if shift == 0 else swap(mine, shift * HSPLIT))

    grad_pieces = [p for s in range(experts) for p in grads[s]]
    grad_down = pl.pallas_call(
        functools.partial(grad_kernel, chunks, 4 * shifts),
        out_shape=jax.ShapeDtypeStruct((1, hidden_width, width), BF16),
        in_specs=whole(chunks + len(grad_pieces)),
        out_specs=whole(1)[0],
        scratch_shapes=[pltpu.VMEM((chunks * rows_chunk, width), BF16)],
        compiler_params=params(32),
        cost_estimate=pl.CostEstimate(
            flops=2 * chunks * rows_chunk * width * hidden_width,
            bytes_accessed=8 << 20,
            transcendentals=0,
        ),
        name="grad",
    )(*hiddens, *grad_pieces)
    mixed = pl.pallas_call(
        functools.partial(combine_kernel, experts),
        out_shape=jax.ShapeDtypeStruct(tokens.shape, BF16),
        in_specs=[scalar] + whole(3 + experts),
        out_specs=whole(1)[0],
        compiler_params=params(16),
        cost_estimate=pl.CostEstimate(
            flops=placed_flops, bytes_accessed=2 << 20, transcendentals=0
        ),
        name="combine",
    )(plane, tokens, routes, gate_nums, *returned)
    return (mixed, grad_down)


def solution(mesh):
    placed = (
        P(("group", "expert"), None),
        P(("group", "expert"), None),
        P(("group", "expert"), None),
        P(("group", "expert"), None),
        P(),
        P("expert", None, None),
        P("expert", None, None),
        P("expert", None, None),
    )
    return jax.shard_map(
        on_device,
        mesh=mesh,
        in_specs=placed,
        out_specs=(P(("group", "expert"), None), P(("group", "expert"), None, None)),
        check_vma=False,
    )
```

time: 243 us -> 121 us (0.50)
  the two profiles are of different devices: /device:TPU:15 before, /device:TPU:0 now
where the time goes in v1:
time: 121 us; the launch traced here: 120 us
  waiting for transfers between devices  48.8 us (40%)
  starting transfers between devices  35.2 us (29%)
  Pallas kernels  25.6 us (21%)
  local copies, waits for them, and re-layouts  9.03 us (7%)
    ppermute x41, waiting for transfers between devices, swap(): lax.ppermute(value, 'expert', [(i, i ^ mask) for i in range(devices)])  48.8 us
    ppermute x41, starting transfers between devices, swap(): lax.ppermute(value, 'expert', [(i, i ^ mask) for i in range(devices)])  35.2 us
    pallas_call x4, Pallas kernels, on_device(): pl.pallas_call(functools.partial(ffn_kernel, shifts), out_shape=[jax.Shap...  16 us
    unnamed x22, local copies, waits for them, and re-layouts  8.94 us
    pallas_call x1, Pallas kernels, on_device(): pl.pallas_call(functools.partial(grad_kernel, chunks, 4 * shifts), out_sh...  6.71 us
  transfers between devices with their start and end apart: 41, of which 9 were waited for; matrix products, arithmetic and copies ran while one was open for 1% of the time, Pallas kernels for 20%

profile of v1, /device:TPU:0, one launch (start us, length us, event | category | flops | bytes accessed | tf_op | source)
XLA Modules:
  0.0 120.2 jit_solution(231065542726030544)
XLA Ops:
  0.6 0.8 copy.11.routes_ref
  1.4 0.9 copy-done.1
  3.7 3.0 %collective-permute-start = (bf16[96,1024]{1,0:T(8,128)(2,1)S(1)}, bf16[96,1024]{1,0:T(8,128)(2,1)S(1)}, u32[]{:S(2)}, u32[]{:S(2)}) collective-permute-start(bf16[96,1024]{1,0:T(8,128)(2,1)S(1)} %get-tuple-element.22.refs_0_), channel_id=1, source_target_pairs={{0,2},{1,3},{2,0},{3,1},{4,6},{5,7},{6,4},{7,5},{8,10},{9,11},{10,... | collective-permute-start | bytes 589832 | tf_op jit(solution)/shard_map/ppermute | solution.py:165
  6.7 1.6 %collective-permute-start.5 = (bf16[96,1024]{1,0:T(8,128)(2,1)S(1)}, bf16[96,1024]{1,0:T(8,128)(2,1)S(1)}, u32[]{:S(2)}, u32[]{:S(2)}) collective-permute-start(bf16[96,1024]{1,0:T(8,128)(2,1)S(1)} %get-tuple-element.25), channel_id=1, source_target_pairs={{0,4},{1,5},{2,6},{3,7},{4,0},{5,1},{6,2},{7,3},{8,12},{9,13},{10,... | collective-permute-start | bytes 589832 | tf_op jit(solution)/shard_map/ppermute | solution.py:165
  8.3 2.6 %collective-permute-start.12 = (bf16[96,1024]{1,0:T(8,128)(2,1)S(1)}, bf16[96,1024]{1,0:T(8,128)(2,1)S(1)}, u32[]{:S(2)}, u32[]{:S(2)}) collective-permute-start(bf16[96,1024]{1,0:T(8,128)(2,1)S(1)} %get-tuple-element.28), channel_id=1, source_target_pairs={{0,8},{1,9},{2,10},{3,11},{4,12},{5,13},{6,14},{7,15},{8,0},{9,1},... | collective-permute-start | bytes 589832 | tf_op jit(solution)/shard_map/ppermute | solution.py:165
  11.9 0.9 copy-done
  13.9 3.9 %collective-permute-done.5.refs_0_ = bf16[96,1024]{1,0:T(8,128)(2,1)S(1)} collective-permute-done((bf16[96,1024]{1,0:T(8,128)(2,1)S(1)}, bf16[96,1024]{1,0:T(8,128)(2,1)S(1)}, u32[]{:S(2)}, u32[]{:S(2)}) %collective-permute-start.5) | collective-permute-done | bytes 196640 | tf_op jit(solution)/shard_map/ppermute | solution.py:165
  17.9 7.6 %collective-permute-done.12.refs_0_ = bf16[96,1024]{1,0:T(8,128)(2,1)S(1)} collective-permute-done((bf16[96,1024]{1,0:T(8,128)(2,1)S(1)}, bf16[96,1024]{1,0:T(8,128)(2,1)S(1)}, u32[]{:S(2)}, u32[]{:S(2)}) %collective-permute-start.12) | collective-permute-done | bytes 196640 | tf_op jit(solution)/shard_map/ppermute | solution.py:165
  26.1 2.5 %collective-permute-start.37 = (bf16[96,1024]{1,0:T(8,128)(2,1)S(1)}, bf16[96,1024]{1,0:T(8,128)(2,1)S(1)}, u32[]{:S(2)}, u32[]{:S(2)}) collective-permute-start(bf16[96,1024]{1,0:T(8,128)(2,1)S(1)} %get-tuple-element.41), channel_id=1, source_target_pairs={{0,12},{1,13},{2,14},{3,15},{4,8},{5,9},{6,10},{7,11},{8,4},{9,5},... | collective-permute-start | bytes 589832 | tf_op jit(solution)/shard_map/ppermute | solution.py:165
  29.2 12.5 %collective-permute-done.33.refs_12_ = bf16[96,1024]{1,0:T(8,128)(2,1)S(1)} collective-permute-done((bf16[96,1024]{1,0:T(8,128)(2,1)S(1)}, bf16[96,1024]{1,0:T(8,128)(2,1)S(1)}, u32[]{:S(2)}, u32[]{:S(2)}) %collective-permute-start.33) | collective-permute-done | bytes 196640 | tf_op jit(solution)/shard_map/ppermute | solution.py:165
  42.6 1.6 %copy-done.3 = bf16[1,1024,1024]{2,1,0:T(8,128)(2,1)S(1)} copy-done((bf16[1,1024,1024]{2,1,0:T(8,128)(2,1)S(1)}, bf16[1,1024,1024]{2,1,0:T(8,128)(2,1)}, u32[]{:S(2)}) %copy-start.3) | copy-done | bytes 2097176
  44.2 1.6 %copy-done.5 = bf16[1,1024,1024]{2,1,0:T(8,128)(2,1)S(1)} copy-done((bf16[1,1024,1024]{2,1,0:T(8,128)(2,1)S(1)}, bf16[1,1024,1024]{2,1,0:T(8,128)(2,1)}, u32[]{:S(2)}) %copy-start.5) | copy-done | bytes 2097176
  45.8 1.6 %copy-done.7 = bf16[1,1024,1024]{2,1,0:T(8,128)(2,1)S(1)} copy-done((bf16[1,1024,1024]{2,1,0:T(8,128)(2,1)S(1)}, bf16[1,1024,1024]{2,1,0:T(8,128)(2,1)}, u32[]{:S(2)}) %copy-start.7) | copy-done | bytes 2097176
  47.4 4.0 %ffn.4 = (bf16[384,1024]{1,0:T(8,128)(2,1)S(1)}, bf16[192,1024]{1,0:T(8,128)(2,1)S(1)}, bf16[192,1024]{1,0:T(8,128)(2,1)S(1)}) custom-call(bf16[96,1024]{1,0:T(8,128)(2,1)S(1)} %get-tuple-element.22.refs_0_, bf16[96,1024]{1,0:T(8,128)(2,1)S(1)} %collective-permute-done.refs_1_, bf16[96,1024]{1,0:T(8,128)(2,1)S(1)} %collective-permute-done.1.refs_2_, ...), custom_call_target="tpu_custom_call" | custom-call | flops 2415919104 | bytes 8388608 | tf_op jit(solution)/shard_map/ffn/pallas_call | solution.py:205
  51.4 1.7 %collective-permute-start.20 = (bf16[96,1024]{1,0:T(8,128)(2,1)S(1)}, bf16[96,1024]{1,0:T(8,128)(2,1)S(1)}, u32[]{:S(2)}, u32[]{:S(2)}) collective-permute-start(bf16[96,1024]{1,0:T(8,128)(2,1)S(1)} %collective-permute-done.19.refs_0_), channel_id=1, source_target_pairs={{0,2},{1,3},{2,0},{3,1},{4,6},{5,7},{6,4},{7,5},{8,10},{9,11},{10,... | collective-permute-start | bytes 589832 | tf_op jit(solution)/shard_map/ppermute | solution.py:165
  54.1 4.0 %ffn.5 = (bf16[384,1024]{1,0:T(8,128)(2,1)S(1)}, bf16[192,1024]{1,0:T(8,128)(2,1)S(1)}, bf16[192,1024]{1,0:T(8,128)(2,1)S(1)}) custom-call(bf16[96,1024]{1,0:T(8,128)(2,1)S(1)} %collective-permute-done.5.refs_0_, bf16[96,1024]{1,0:T(8,128)(2,1)S(1)} %collective-permute-done.6.refs_1_, bf16[96,1024]{1,0:T(8,128)(2,1)S(1)} %collective-permute-done.7.refs_2_, ...), custom_call_target="tpu_custom_call" | custom-call | flops 2415919104 | bytes 8388608 | tf_op jit(solution)/shard_map/ffn/pallas_call | solution.py:205
  58.1 1.2 collective-permute-done.20.refs_1_
  59.3 1.6 %collective-permute-start.34 = (bf16[96,1024]{1,0:T(8,128)(2,1)S(1)}, bf16[96,1024]{1,0:T(8,128)(2,1)S(1)}, u32[]{:S(2)}, u32[]{:S(2)}) collective-permute-start(bf16[96,1024]{1,0:T(8,128)(2,1)S(1)} %collective-permute-done.33.refs_12_), channel_id=1, source_target_pairs={{0,2},{1,3},{2,0},{3,1},{4,6},{5,7},{6,4},{7,5},{8,10},{9,11},{10,... | collective-permute-start | bytes 589832 | tf_op jit(solution)/shard_map/ppermute | solution.py:165
  61.1 1.6 %collective-permute-done.30.refs_9_ = bf16[96,1024]{1,0:T(8,128)(2,1)S(1)} collective-permute-done((bf16[96,1024]{1,0:T(8,128)(2,1)S(1)}, bf16[96,1024]{1,0:T(8,128)(2,1)S(1)}, u32[]{:S(2)}, u32[]{:S(2)}) %collective-permute-start.30) | collective-permute-done | bytes 196640 | tf_op jit(solution)/shard_map/ppermute | solution.py:165
  62.7 1.6 %collective-permute-start.38 = (bf16[96,1024]{1,0:T(8,128)(2,1)S(1)}, bf16[96,1024]{1,0:T(8,128)(2,1)S(1)}, u32[]{:S(2)}, u32[]{:S(2)}) collective-permute-start(bf16[96,1024]{1,0:T(8,128)(2,1)S(1)} %collective-permute-done.37.refs_16_), channel_id=1, source_target_pairs={{0,2},{1,3},{2,0},{3,1},{4,6},{5,7},{6,4},{7,5},{8,10},{9,11},{10,... | collective-permute-start | bytes 589832 | tf_op jit(solution)/shard_map/ppermute | solution.py:165
  64.4 4.0 %ffn.6 = (bf16[384,1024]{1,0:T(8,128)(2,1)S(1)}, bf16[192,1024]{1,0:T(8,128)(2,1)S(1)}, bf16[192,1024]{1,0:T(8,128)(2,1)S(1)}) custom-call(bf16[96,1024]{1,0:T(8,128)(2,1)S(1)} %collective-permute-done.12.refs_0_, bf16[96,1024]{1,0:T(8,128)(2,1)S(1)} %collective-permute-done.13.refs_1_, bf16[96,1024]{1,0:T(8,128)(2,1)S(1)} %collective-permute-done.14.refs_2_, ...), custom_call_target="tpu_custom_call" | custom-call | flops 2415919104 | bytes 8388608 | tf_op jit(solution)/shard_map/ffn/pallas_call | solution.py:205
  69.5 1.5 %collective-permute-done.38.refs_17_ = bf16[96,1024]{1,0:T(8,128)(2,1)S(1)} collective-permute-done((bf16[96,1024]{1,0:T(8,128)(2,1)S(1)}, bf16[96,1024]{1,0:T(8,128)(2,1)S(1)}, u32[]{:S(2)}, u32[]{:S(2)}) %collective-permute-start.38) | collective-permute-done | bytes 196640 | tf_op jit(solution)/shard_map/ppermute | solution.py:165
  71.5 4.0 %ffn.7 = (bf16[384,1024]{1,0:T(8,128)(2,1)S(1)}, bf16[192,1024]{1,0:T(8,128)(2,1)S(1)}, bf16[192,1024]{1,0:T(8,128)(2,1)S(1)}) custom-call(bf16[96,1024]{1,0:T(8,128)(2,1)S(1)} %collective-permute-done.19.refs_0_, bf16[96,1024]{1,0:T(8,128)(2,1)S(1)} %collective-permute-done.20.refs_1_, bf16[96,1024]{1,0:T(8,128)(2,1)S(1)} %collective-permute-done.21.refs_2_, ...), custom_call_target="tpu_custom_call" | custom-call | flops 2415919104 | bytes 8388608 | tf_op jit(solution)/shard_map/ffn/pallas_call | solution.py:205
  76.2 6.7 %grad.1 = bf16[1,1024,1024]{2,1,0:T(8,128)(2,1)} custom-call(bf16[384,1024]{1,0:T(8,128)(2,1)S(1)} %get-tuple-element.34.refs_0_, bf16[384,1024]{1,0:T(8,128)(2,1)S(1)} %get-tuple-element.35.refs_1_, bf16[384,1024]{1,0:T(8,128)(2,1)S(1)} %get-tuple-element.36.refs_2_, bf16[384,1024]{1,0:T(8,128)(2,1)S(1)} %get-tuple-element.37.refs_3_, ...), custom_call_target="tpu_custom_call" | custom-call | flops 3221225472 | bytes 8388608 | tf_op jit(solution)/shard_map/grad/pallas_call | solution.py:231
  83.1 1.7 %collective-permute-start.4 = (bf16[96,1024]{1,0:T(8,128)(2,1)S(1)}, bf16[96,1024]{1,0:T(8,128)(2,1)S(1)}, u32[]{:S(2)}, u32[]{:S(2)}) collective-permute-start(bf16[96,1024]{1,0:T(8,128)(2,1)S(1)} %slice.63), channel_id=1, source_target_pairs={{0,2},{1,3},{2,0},{3,1},{4,6},{5,7},{6,4},{7,5},{8,10},{9,11},{10,... | collective-permute-start | bytes 589832 | tf_op jit(solution)/shard_map/ppermute | solution.py:165
  85.5 1.7 %collective-permute-start.17 = (bf16[96,1024]{1,0:T(8,128)(2,1)S(1)}, bf16[96,1024]{1,0:T(8,128)(2,1)S(1)}, u32[]{:S(2)}, u32[]{:S(2)}) collective-permute-start(bf16[96,1024]{1,0:T(8,128)(2,1)S(1)} %slice.61), channel_id=1, source_target_pairs={{0,2},{1,3},{2,0},{3,1},{4,6},{5,7},{6,4},{7,5},{8,10},{9,11},{10,... | collective-permute-start | bytes 589832 | tf_op jit(solution)/shard_map/ppermute | solution.py:165
  87.9 7.2 %collective-permute-done.10 = bf16[96,1024]{1,0:T(8,128)(2,1)S(1)} collective-permute-done((bf16[96,1024]{1,0:T(8,128)(2,1)S(1)}, bf16[96,1024]{1,0:T(8,128)(2,1)S(1)}, u32[]{:S(2)}, u32[]{:S(2)}) %collective-permute-start.10) | collective-permute-done | bytes 196640 | tf_op jit(solution)/shard_map/ppermute | solution.py:165
  95.1 4.3 %collective-permute-start.11 = (bf16[96,1024]{1,0:T(8,128)(2,1)S(1)}, bf16[96,1024]{1,0:T(8,128)(2,1)S(1)}, u32[]{:S(2)}, u32[]{:S(2)}) collective-permute-start(bf16[96,1024]{1,0:T(8,128)(2,1)S(1)} %fusion.2), channel_id=1, source_target_pairs={{0,4},{1,5},{2,6},{3,7},{4,0},{5,1},{6,2},{7,3},{8,12},{9,13},{10,... | collective-permute-start | bytes 589832 | tf_op jit(solution)/shard_map/ppermute | solution.py:165
  99.4 5.2 %collective-permute-start.18 = (bf16[96,1024]{1,0:T(8,128)(2,1)S(1)}, bf16[96,1024]{1,0:T(8,128)(2,1)S(1)}, u32[]{:S(2)}, u32[]{:S(2)}) collective-permute-start(bf16[96,1024]{1,0:T(8,128)(2,1)S(1)} %fusion.1), channel_id=1, source_target_pairs={{0,8},{1,9},{2,10},{3,11},{4,12},{5,13},{6,14},{7,15},{8,0},{9,1},... | collective-permute-start | bytes 589832 | tf_op jit(solution)/shard_map/ppermute | solution.py:165
  104.6 1.4 %collective-permute-start.25 = (bf16[96,1024]{1,0:T(8,128)(2,1)S(1)}, bf16[96,1024]{1,0:T(8,128)(2,1)S(1)}, u32[]{:S(2)}, u32[]{:S(2)}) collective-permute-start(bf16[96,1024]{1,0:T(8,128)(2,1)S(1)} %fusion), channel_id=1, source_target_pairs={{0,12},{1,13},{2,14},{3,15},{4,8},{5,9},{6,10},{7,11},{8,4},{9,5},... | collective-permute-start | bytes 589832 | tf_op jit(solution)/shard_map/ppermute | solution.py:165
  106.1 12.5 %collective-permute-done.18.refs_2_ = bf16[96,1024]{1,0:T(8,128)(2,1)S(1)} collective-permute-done((bf16[96,1024]{1,0:T(8,128)(2,1)S(1)}, bf16[96,1024]{1,0:T(8,128)(2,1)S(1)}, u32[]{:S(2)}, u32[]{:S(2)}) %collective-permute-start.18) | collective-permute-done | bytes 196640 | tf_op jit(solution)/shard_map/ppermute | solution.py:165
  118.6 1.6 %combine.1 = bf16[128,1024]{1,0:T(8,128)(2,1)} custom-call(s32[1]{0:T(128)} %bitcast.plane_ref, bf16[128,1024]{1,0:T(8,128)(2,1)S(1)} %copy-done.2, s32[128,2]{1,0:T(8,128)S(1)} %copy.11.routes_ref, s32[128,2]{1,0:T(8,128)S(1)} %copy.12.nums_ref, bf16[96,1024]{1,0:T(8,128)(2,1)S(1)} %fusion.3.refs_0_, bf16[96,1024]{1,0:T(8,128)(2,1)S(1)} %collective-permute-done.11.refs_1_, ...), custom_call_target="tpu_custom_call" | custom-call | flops 100663296 | bytes 2097152 | tf_op jit(solution)/shard_map/combine/pallas_call | solution.py:245
  (92 shorter events, 10.6 us)
Async XLA Ops:
  3.7 9.9 %collective-permute-start = (bf16[96,1024]{1,0:T(8,128)(2,1)S(1)}, bf16[96,1024]{1,0:T(8,128)(2,1)S(1)}, u32[]{:S(2)}, u32[]{:S(2)}) collective-permute-start(bf16[96,1024]{1,0:T(8,128)(2,1)S(1)} %get-tuple-element.22.refs_0_), channel_id=1, source_target_pairs={{0,2},{1,3},{2,0},{3,1},{4,6},{5,7},{6,4},{7,5},{8,10},{9,11},{10,... | collective-permute-start | bytes 589832 | tf_op jit(solution)/shard_map/ppermute | solution.py:165
  6.7 11.1 %collective-permute-start.5 = (bf16[96,1024]{1,0:T(8,128)(2,1)S(1)}, bf16[96,1024]{1,0:T(8,128)(2,1)S(1)}, u32[]{:S(2)}, u32[]{:S(2)}) collective-permute-start(bf16[96,1024]{1,0:T(8,128)(2,1)S(1)} %get-tuple-element.25), channel_id=1, source_target_pairs={{0,4},{1,5},{2,6},{3,7},{4,0},{5,1},{6,2},{7,3},{8,12},{9,13},{10,... | collective-permute-start | bytes 589832 | tf_op jit(solution)/shard_map/ppermute | solution.py:165
  8.3 17.2 %collective-permute-start.12 = (bf16[96,1024]{1,0:T(8,128)(2,1)S(1)}, bf16[96,1024]{1,0:T(8,128)(2,1)S(1)}, u32[]{:S(2)}, u32[]{:S(2)}) collective-permute-start(bf16[96,1024]{1,0:T(8,128)(2,1)S(1)} %get-tuple-element.28), channel_id=1, source_target_pairs={{0,8},{1,9},{2,10},{3,11},{4,12},{5,13},{6,14},{7,15},{8,0},{9,1},... | collective-permute-start | bytes 589832 | tf_op jit(solution)/shard_map/ppermute | solution.py:165
  10.9 14.6 %collective-permute-start.19 = (bf16[96,1024]{1,0:T(8,128)(2,1)S(1)}, bf16[96,1024]{1,0:T(8,128)(2,1)S(1)}, u32[]{:S(2)}, u32[]{:S(2)}) collective-permute-start(bf16[96,1024]{1,0:T(8,128)(2,1)S(1)} %get-tuple-element.31), channel_id=1, source_target_pairs={{0,12},{1,13},{2,14},{3,15},{4,8},{5,9},{6,10},{7,11},{8,4},{9,5},... | collective-permute-start | bytes 589832 | tf_op jit(solution)/shard_map/ppermute | solution.py:165
  13.6 11.9 %collective-permute-start.26 = (bf16[96,1024]{1,0:T(8,128)(2,1)S(1)}, bf16[96,1024]{1,0:T(8,128)(2,1)S(1)}, u32[]{:S(2)}, u32[]{:S(2)}) collective-permute-start(bf16[96,1024]{1,0:T(8,128)(2,1)S(1)} %get-tuple-element.38.refs_4_), channel_id=1, source_target_pairs={{0,2},{1,3},{2,0},{3,1},{4,6},{5,7},{6,4},{7,5},{8,10},{9,11},{10,... | collective-permute-start | bytes 589832 | tf_op jit(solution)/shard_map/ppermute | solution.py:165
  13.9 12.1 %collective-permute-start.27 = (bf16[96,1024]{1,0:T(8,128)(2,1)S(1)}, bf16[96,1024]{1,0:T(8,128)(2,1)S(1)}, u32[]{:S(2)}, u32[]{:S(2)}) collective-permute-start(bf16[96,1024]{1,0:T(8,128)(2,1)S(1)} %get-tuple-element.38.refs_4_), channel_id=1, source_target_pairs={{0,1},{1,0},{2,3},{3,2},{4,5},{5,4},{6,7},{7,6},{8,9},{9,8},{10,11... | collective-permute-start | bytes 589832 | tf_op jit(solution)/shard_map/ppermute | solution.py:165
  17.8 11.3 %collective-permute-start.29 = (bf16[96,1024]{1,0:T(8,128)(2,1)S(1)}, bf16[96,1024]{1,0:T(8,128)(2,1)S(1)}, u32[]{:S(2)}, u32[]{:S(2)}) collective-permute-start(bf16[96,1024]{1,0:T(8,128)(2,1)S(1)} %get-tuple-element.39), channel_id=1, source_target_pairs={{0,4},{1,5},{2,6},{3,7},{4,0},{5,1},{6,2},{7,3},{8,12},{9,13},{10,... | collective-permute-start | bytes 589832 | tf_op jit(solution)/shard_map/ppermute | solution.py:165
  25.5 16.3 %collective-permute-start.33 = (bf16[96,1024]{1,0:T(8,128)(2,1)S(1)}, bf16[96,1024]{1,0:T(8,128)(2,1)S(1)}, u32[]{:S(2)}, u32[]{:S(2)}) collective-permute-start(bf16[96,1024]{1,0:T(8,128)(2,1)S(1)} %get-tuple-element.40), channel_id=1, source_target_pairs={{0,8},{1,9},{2,10},{3,11},{4,12},{5,13},{6,14},{7,15},{8,0},{9,1},... | collective-permute-start | bytes 589832 | tf_op jit(solution)/shard_map/ppermute | solution.py:165
  25.5 16.6 %collective-permute-start.2 = (bf16[96,1024]{1,0:T(8,128)(2,1)S(1)}, bf16[96,1024]{1,0:T(8,128)(2,1)S(1)}, u32[]{:S(2)}, u32[]{:S(2)}) collective-permute-start(bf16[96,1024]{1,0:T(8,128)(2,1)S(1)} %collective-permute-done.refs_1_), channel_id=1, source_target_pairs={{0,1},{1,0},{2,3},{3,2},{4,5},{5,4},{6,7},{7,6},{8,9},{9,8},{10,11... | collective-permute-start | bytes 589832 | tf_op jit(solution)/shard_map/ppermute | solution.py:165
  25.5 16.6 %collective-permute-start.6 = (bf16[96,1024]{1,0:T(8,128)(2,1)S(1)}, bf16[96,1024]{1,0:T(8,128)(2,1)S(1)}, u32[]{:S(2)}, u32[]{:S(2)}) collective-permute-start(bf16[96,1024]{1,0:T(8,128)(2,1)S(1)} %collective-permute-done.5.refs_0_), channel_id=1, source_target_pairs={{0,2},{1,3},{2,0},{3,1},{4,6},{5,7},{6,4},{7,5},{8,10},{9,11},{10,... | collective-permute-start | bytes 589832 | tf_op jit(solution)/shard_map/ppermute | solution.py:165
  26.1 25.4 %collective-permute-start.37 = (bf16[96,1024]{1,0:T(8,128)(2,1)S(1)}, bf16[96,1024]{1,0:T(8,128)(2,1)S(1)}, u32[]{:S(2)}, u32[]{:S(2)}) collective-permute-start(bf16[96,1024]{1,0:T(8,128)(2,1)S(1)} %get-tuple-element.41), channel_id=1, source_target_pairs={{0,12},{1,13},{2,14},{3,15},{4,8},{5,9},{6,10},{7,11},{8,4},{9,5},... | collective-permute-start | bytes 589832 | tf_op jit(solution)/shard_map/ppermute | solution.py:165
  29.2 24.0 %collective-permute-start.7 = (bf16[96,1024]{1,0:T(8,128)(2,1)S(1)}, bf16[96,1024]{1,0:T(8,128)(2,1)S(1)}, u32[]{:S(2)}, u32[]{:S(2)}) collective-permute-start(bf16[96,1024]{1,0:T(8,128)(2,1)S(1)} %collective-permute-done.5.refs_0_), channel_id=1, source_target_pairs={{0,1},{1,0},{2,3},{3,2},{4,5},{5,4},{6,7},{7,6},{8,9},{9,8},{10,11... | collective-permute-start | bytes 589832 | tf_op jit(solution)/shard_map/ppermute | solution.py:165
  41.7 11.4 %collective-permute-start.13 = (bf16[96,1024]{1,0:T(8,128)(2,1)S(1)}, bf16[96,1024]{1,0:T(8,128)(2,1)S(1)}, u32[]{:S(2)}, u32[]{:S(2)}) collective-permute-start(bf16[96,1024]{1,0:T(8,128)(2,1)S(1)} %collective-permute-done.12.refs_0_), channel_id=1, source_target_pairs={{0,2},{1,3},{2,0},{3,1},{4,6},{5,7},{6,4},{7,5},{8,10},{9,11},{10,... | collective-permute-start | bytes 589832 | tf_op jit(solution)/shard_map/ppermute | solution.py:165
  42.1 11.5 %collective-permute-start.14 = (bf16[96,1024]{1,0:T(8,128)(2,1)S(1)}, bf16[96,1024]{1,0:T(8,128)(2,1)S(1)}, u32[]{:S(2)}, u32[]{:S(2)}) collective-permute-start(bf16[96,1024]{1,0:T(8,128)(2,1)S(1)} %collective-permute-done.12.refs_0_), channel_id=1, source_target_pairs={{0,1},{1,0},{2,3},{3,2},{4,5},{5,4},{6,7},{7,6},{8,9},{9,8},{10,11... | collective-permute-start | bytes 589832 | tf_op jit(solution)/shard_map/ppermute | solution.py:165
  42.1 11.9 %collective-permute-start.8 = (bf16[96,1024]{1,0:T(8,128)(2,1)S(1)}, bf16[96,1024]{1,0:T(8,128)(2,1)S(1)}, u32[]{:S(2)}, u32[]{:S(2)}) collective-permute-start(bf16[96,1024]{1,0:T(8,128)(2,1)S(1)} %collective-permute-done.6.refs_1_), channel_id=1, source_target_pairs={{0,1},{1,0},{2,3},{3,2},{4,5},{5,4},{6,7},{7,6},{8,9},{9,8},{10,11... | collective-permute-start | bytes 589832 | tf_op jit(solution)/shard_map/ppermute | solution.py:165
  53.7 9.1 %collective-permute-start.30 = (bf16[96,1024]{1,0:T(8,128)(2,1)S(1)}, bf16[96,1024]{1,0:T(8,128)(2,1)S(1)}, u32[]{:S(2)}, u32[]{:S(2)}) collective-permute-start(bf16[96,1024]{1,0:T(8,128)(2,1)S(1)} %collective-permute-done.29.refs_8_), channel_id=1, source_target_pairs={{0,2},{1,3},{2,0},{3,1},{4,6},{5,7},{6,4},{7,5},{8,10},{9,11},{10,... | collective-permute-start | bytes 589832 | tf_op jit(solution)/shard_map/ppermute | solution.py:165
  54.1 10.3 %collective-permute-start.15 = (bf16[96,1024]{1,0:T(8,128)(2,1)S(1)}, bf16[96,1024]{1,0:T(8,128)(2,1)S(1)}, u32[]{:S(2)}, u32[]{:S(2)}) collective-permute-start(bf16[96,1024]{1,0:T(8,128)(2,1)S(1)} %collective-permute-done.13.refs_1_), channel_id=1, source_target_pairs={{0,1},{1,0},{2,3},{3,2},{4,5},{5,4},{6,7},{7,6},{8,9},{9,8},{10,11... | collective-permute-start | bytes 589832 | tf_op jit(solution)/shard_map/ppermute | solution.py:165
  59.3 9.2 %collective-permute-start.31 = (bf16[96,1024]{1,0:T(8,128)(2,1)S(1)}, bf16[96,1024]{1,0:T(8,128)(2,1)S(1)}, u32[]{:S(2)}, u32[]{:S(2)}) collective-permute-start(bf16[96,1024]{1,0:T(8,128)(2,1)S(1)} %collective-permute-done.29.refs_8_), channel_id=1, source_target_pairs={{0,1},{1,0},{2,3},{3,2},{4,5},{5,4},{6,7},{7,6},{8,9},{9,8},{10,11... | collective-permute-start | bytes 589832 | tf_op jit(solution)/shard_map/ppermute | solution.py:165
  59.3 9.7 %collective-permute-start.34 = (bf16[96,1024]{1,0:T(8,128)(2,1)S(1)}, bf16[96,1024]{1,0:T(8,128)(2,1)S(1)}, u32[]{:S(2)}, u32[]{:S(2)}) collective-permute-start(bf16[96,1024]{1,0:T(8,128)(2,1)S(1)} %collective-permute-done.33.refs_12_), channel_id=1, source_target_pairs={{0,2},{1,3},{2,0},{3,1},{4,6},{5,7},{6,4},{7,5},{8,10},{9,11},{10,... | collective-permute-start | bytes 589832 | tf_op jit(solution)/shard_map/ppermute | solution.py:165
  60.9 8.2 %collective-permute-start.35 = (bf16[96,1024]{1,0:T(8,128)(2,1)S(1)}, bf16[96,1024]{1,0:T(8,128)(2,1)S(1)}, u32[]{:S(2)}, u32[]{:S(2)}) collective-permute-start(bf16[96,1024]{1,0:T(8,128)(2,1)S(1)} %collective-permute-done.33.refs_12_), channel_id=1, source_target_pairs={{0,1},{1,0},{2,3},{3,2},{4,5},{5,4},{6,7},{7,6},{8,9},{9,8},{10,11... | collective-permute-start | bytes 589832 | tf_op jit(solution)/shard_map/ppermute | solution.py:165
  62.7 8.3 %collective-permute-start.38 = (bf16[96,1024]{1,0:T(8,128)(2,1)S(1)}, bf16[96,1024]{1,0:T(8,128)(2,1)S(1)}, u32[]{:S(2)}, u32[]{:S(2)}) collective-permute-start(bf16[96,1024]{1,0:T(8,128)(2,1)S(1)} %collective-permute-done.37.refs_16_), channel_id=1, source_target_pairs={{0,2},{1,3},{2,0},{3,1},{4,6},{5,7},{6,4},{7,5},{8,10},{9,11},{10,... | collective-permute-start | bytes 589832 | tf_op jit(solution)/shard_map/ppermute | solution.py:165
  69.0 13.9 %collective-permute-start.3 = (bf16[192,1024]{1,0:T(8,128)(2,1)S(1)}, bf16[192,1024]{1,0:T(8,128)(2,1)S(1)}, u32[]{:S(2)}, u32[]{:S(2)}) collective-permute-start(bf16[192,1024]{1,0:T(8,128)(2,1)S(1)} %get-tuple-element.24), channel_id=1, source_target_pairs={{0,1},{1,0},{2,3},{3,2},{4,5},{5,4},{6,7},{7,6},{8,9},{9,8},{10,11... | collective-permute-start | bytes 1179656 | tf_op jit(solution)/shard_map/ppermute | solution.py:165
  75.6 9.2 %collective-permute-start.9 = (bf16[192,1024]{1,0:T(8,128)(2,1)S(1)}, bf16[192,1024]{1,0:T(8,128)(2,1)S(1)}, u32[]{:S(2)}, u32[]{:S(2)}) collective-permute-start(bf16[192,1024]{1,0:T(8,128)(2,1)S(1)} %get-tuple-element.27), channel_id=1, source_target_pairs={{0,1},{1,0},{2,3},{3,2},{4,5},{5,4},{6,7},{7,6},{8,9},{9,8},{10,11... | collective-permute-start | bytes 1179656 | tf_op jit(solution)/shard_map/ppermute | solution.py:165
  75.6 9.7 %collective-permute-start.16 = (bf16[192,1024]{1,0:T(8,128)(2,1)S(1)}, bf16[192,1024]{1,0:T(8,128)(2,1)S(1)}, u32[]{:S(2)}, u32[]{:S(2)}) collective-permute-start(bf16[192,1024]{1,0:T(8,128)(2,1)S(1)} %get-tuple-element.30), channel_id=1, source_target_pairs={{0,1},{1,0},{2,3},{3,2},{4,5},{5,4},{6,7},{7,6},{8,9},{9,8},{10,11... | collective-permute-start | bytes 1179656 | tf_op jit(solution)/shard_map/ppermute | solution.py:165
  76.1 11.1 %collective-permute-start.23 = (bf16[192,1024]{1,0:T(8,128)(2,1)S(1)}, bf16[192,1024]{1,0:T(8,128)(2,1)S(1)}, u32[]{:S(2)}, u32[]{:S(2)}) collective-permute-start(bf16[192,1024]{1,0:T(8,128)(2,1)S(1)} %get-tuple-element.33), channel_id=1, source_target_pairs={{0,1},{1,0},{2,3},{3,2},{4,5},{5,4},{6,7},{7,6},{8,9},{9,8},{10,11... | collective-permute-start | bytes 1179656 | tf_op jit(solution)/shard_map/ppermute | solution.py:165
  83.1 23.0 %collective-permute-start.4 = (bf16[96,1024]{1,0:T(8,128)(2,1)S(1)}, bf16[96,1024]{1,0:T(8,128)(2,1)S(1)}, u32[]{:S(2)}, u32[]{:S(2)}) collective-permute-start(bf16[96,1024]{1,0:T(8,128)(2,1)S(1)} %slice.63), channel_id=1, source_target_pairs={{0,2},{1,3},{2,0},{3,1},{4,6},{5,7},{6,4},{7,5},{8,10},{9,11},{10,... | collective-permute-start | bytes 589832 | tf_op jit(solution)/shard_map/ppermute | solution.py:165
  84.9 10.1 %collective-permute-start.10 = (bf16[96,1024]{1,0:T(8,128)(2,1)S(1)}, bf16[96,1024]{1,0:T(8,128)(2,1)S(1)}, u32[]{:S(2)}, u32[]{:S(2)}) collective-permute-start(bf16[96,1024]{1,0:T(8,128)(2,1)S(1)} %slice.62), channel_id=1, source_target_pairs={{0,2},{1,3},{2,0},{3,1},{4,6},{5,7},{6,4},{7,5},{8,10},{9,11},{10,... | collective-permute-start | bytes 589832 | tf_op jit(solution)/shard_map/ppermute | solution.py:165
  85.5 13.8 %collective-permute-start.17 = (bf16[96,1024]{1,0:T(8,128)(2,1)S(1)}, bf16[96,1024]{1,0:T(8,128)(2,1)S(1)}, u32[]{:S(2)}, u32[]{:S(2)}) collective-permute-start(bf16[96,1024]{1,0:T(8,128)(2,1)S(1)} %slice.61), channel_id=1, source_target_pairs={{0,2},{1,3},{2,0},{3,1},{4,6},{5,7},{6,4},{7,5},{8,10},{9,11},{10,... | collective-permute-start | bytes 589832 | tf_op jit(solution)/shard_map/ppermute | solution.py:165
  87.4 17.2 %collective-permute-start.24 = (bf16[96,1024]{1,0:T(8,128)(2,1)S(1)}, bf16[96,1024]{1,0:T(8,128)(2,1)S(1)}, u32[]{:S(2)}, u32[]{:S(2)}) collective-permute-start(bf16[96,1024]{1,0:T(8,128)(2,1)S(1)} %slice.60), channel_id=1, source_target_pairs={{0,2},{1,3},{2,0},{3,1},{4,6},{5,7},{6,4},{7,5},{8,10},{9,11},{10,... | collective-permute-start | bytes 589832 | tf_op jit(solution)/shard_map/ppermute | solution.py:165
  95.1 11.0 %collective-permute-start.11 = (bf16[96,1024]{1,0:T(8,128)(2,1)S(1)}, bf16[96,1024]{1,0:T(8,128)(2,1)S(1)}, u32[]{:S(2)}, u32[]{:S(2)}) collective-permute-start(bf16[96,1024]{1,0:T(8,128)(2,1)S(1)} %fusion.2), channel_id=1, source_target_pairs={{0,4},{1,5},{2,6},{3,7},{4,0},{5,1},{6,2},{7,3},{8,12},{9,13},{10,... | collective-permute-start | bytes 589832 | tf_op jit(solution)/shard_map/ppermute | solution.py:165
  99.4 19.2 %collective-permute-start.18 = (bf16[96,1024]{1,0:T(8,128)(2,1)S(1)}, bf16[96,1024]{1,0:T(8,128)(2,1)S(1)}, u32[]{:S(2)}, u32[]{:S(2)}) collective-permute-start(bf16[96,1024]{1,0:T(8,128)(2,1)S(1)} %fusion.1), channel_id=1, source_target_pairs={{0,8},{1,9},{2,10},{3,11},{4,12},{5,13},{6,14},{7,15},{8,0},{9,1},... | collective-permute-start | bytes 589832 | tf_op jit(solution)/shard_map/ppermute | solution.py:165
  104.6 14.0 %collective-permute-start.25 = (bf16[96,1024]{1,0:T(8,128)(2,1)S(1)}, bf16[96,1024]{1,0:T(8,128)(2,1)S(1)}, u32[]{:S(2)}, u32[]{:S(2)}) collective-permute-start(bf16[96,1024]{1,0:T(8,128)(2,1)S(1)} %fusion), channel_id=1, source_target_pairs={{0,12},{1,13},{2,14},{3,15},{4,8},{5,9},{6,10},{7,11},{8,4},{9,5},... | collective-permute-start | bytes 589832 | tf_op jit(solution)/shard_map/ppermute | solution.py:165
  (19 other events, 118.1 us)

commit v2 on v0

v2 whole, which is shorter than its diff:
```python
import functools

import jax
import jax.numpy as jnp
from jax import lax
from jax.experimental import pallas as pl
from jax.experimental.pallas import tpu as pltpu
from jax.sharding import PartitionSpec as P

HSPLIT = 4
GROUPS = 4
TILE = 256
LINK_WORK = 10 << 30
F32 = jnp.float32
BF16 = jnp.bfloat16


def after(value, *earlier):
    return lax.optimization_barrier((value,) + earlier)[0]


def whole(count):
    return [pl.BlockSpec(memory_space=pltpu.VMEM)] * count


def call(kernel, mib, name, moved=0, **keywords):
    return pl.pallas_call(
        kernel,
        compiler_params=pltpu.CompilerParams(vmem_limit_bytes=mib << 20),
        cost_estimate=pl.CostEstimate(flops=moved, bytes_accessed=0, transcendentals=0),
        name=name,
        **keywords,
    )


def experts_of(plane, experts, rows):
    return lax.broadcasted_iota(jnp.int32, (experts, rows), 0) ^ plane


def placing_of(routes, plane, experts, capacity):
    rows = routes.shape[1]
    expert = experts_of(plane, experts, rows)
    member = jnp.zeros((experts, rows), jnp.bool_)
    for k in range(routes.shape[0]):
        member = member | (routes[k : k + 1, :] == expert)
    first = lax.broadcasted_iota(jnp.int32, (rows, rows), 0)
    second = lax.broadcasted_iota(jnp.int32, (rows, rows), 1)
    upto = (first <= second).astype(F32).astype(BF16)
    ones = member.astype(F32)
    count = jnp.dot(ones.astype(BF16), upto, preferred_element_type=F32)
    place = (ones * count).astype(jnp.int32) - 1
    slots = lax.broadcasted_iota(jnp.int32, (capacity, rows), 0)
    return [(slots == place[s : s + 1, :]).astype(F32) for s in range(experts)]


def gates_of(routes, numbers, plane, experts):
    expert = experts_of(plane, experts, routes.shape[1])
    numerators = numbers.astype(F32)
    gates = numerators / jnp.sum(numerators, 0, keepdims=True)
    gate = jnp.zeros(expert.shape, F32)
    for k in range(routes.shape[0]):
        gate = gate + jnp.where(routes[k : k + 1, :] == expert, gates[k : k + 1, :], 0.0)
    return gate


def fetch(semaphores, *pairs):
    copies = [
        pltpu.make_async_copy(source, target, semaphores.at[i])
        for i, (source, target) in enumerate(pairs)
    ]
    for copy in copies:
        copy.start()
    return copies


def send_rows_kernel(experts, plane_ref, tokens_hbm, gain_hbm, routes_hbm, *refs):
    outs = refs[:experts]
    tokens_ref, gain_ref, routes_ref, semaphores = refs[experts:]
    copies = fetch(
        semaphores, (routes_hbm, routes_ref), (gain_hbm, gain_ref), (tokens_hbm, tokens_ref)
    )
    copies[0].wait()
    placings = placing_of(routes_ref[...], plane_ref[0], experts, outs[0].shape[0])
    copies[1].wait()
    copies[2].wait()
    frames = tokens_ref[...].astype(F32)
    inverse = lax.rsqrt(jnp.mean(frames * frames, -1, keepdims=True) + 1e-06)
    normed = (frames * inverse * gain_ref[...]).astype(BF16)
    for out, placing in zip(outs, placings):
        out[...] = jnp.dot(placing.astype(BF16), normed, preferred_element_type=F32).astype(BF16)


def send_grads_kernel(experts, plane_ref, cot_hbm, routes_hbm, nums_hbm, *refs):
    outs = refs[:experts]
    cot_ref, routes_ref, nums_ref, semaphores = refs[experts:]
    copies = fetch(
        semaphores, (routes_hbm, routes_ref), (nums_hbm, nums_ref), (cot_hbm, cot_ref)
    )
    copies[0].wait()
    copies[1].wait()
    routes = routes_ref[...]
    placings = placing_of(routes, plane_ref[0], experts, outs[0].shape[0])
    gates = gates_of(routes, nums_ref[...], plane_ref[0], experts)
    copies[2].wait()
    cot = cot_ref[...]
    for s, (out, placing) in enumerate(zip(outs, placings)):
        picked = jnp.dot(placing.astype(BF16), cot, preferred_element_type=F32)
        gate = jnp.sum(placing * gates[s : s + 1, :], -1, keepdims=True)
        out[...] = (gate * picked).astype(BF16)


def load_kernel(*refs):
    sources, outs, semaphores = refs[:3], refs[3:6], refs[6]
    copies = fetch(semaphores, *[(s.at[0], o) for s, o in zip(sources, outs)])
    for copy in copies:
        copy.wait()


def nothing(*refs):
    pass


def through(values, name, moved=0):
    count = len(values)
    return call(
        nothing,
        4,
        name,
        moved,
        out_shape=[jax.ShapeDtypeStruct(v.shape, v.dtype) for v in values],
        in_specs=whole(count),
        out_specs=whole(count),
        input_output_aliases={i: i for i in range(count)},
    )(*values)


def ffn_kernel(count, *refs):
    pieces, refs = refs[:count], refs[count:]
    gate_ref, up_ref, down_ref, turned_ref, keep_ref, send_ref, rows_ref, hidden_ref = refs
    at = 0
    for piece in pieces:
        rows_ref[at : at + piece.shape[0], :] = piece[...]
        at += piece.shape[0]
    rows = rows_ref[...]
    half = keep_ref.shape[0]
    for j in range(gate_ref.shape[1] // TILE):
        columns = slice(j * TILE, (j + 1) * TILE)
        pre_gate = jnp.dot(rows, gate_ref[:, columns], preferred_element_type=F32)
        pre_up = jnp.dot(rows, up_ref[:, columns], preferred_element_type=F32)
        hidden = pre_gate * lax.logistic(pre_gate) * pre_up
        hidden_ref[:, columns] = hidden.astype(BF16)
        turned_ref[columns, :] = hidden.T.astype(BF16)
    for j in range(down_ref.shape[1] // TILE):
        columns = slice(j * TILE, (j + 1) * TILE)
        value = jnp.dot(
            hidden_ref[...], down_ref[:, columns], preferred_element_type=F32
        ).astype(BF16)
        keep_ref[:, columns] = value[:half]
        send_ref[:, columns] = value[half:]


def grad_kernel(plan, turned_count, *refs):
    turned, pieces = refs[:turned_count], refs[turned_count:-3]
    out_ref, hidden_ref, cot_ref = refs[-3:]
    for i, start, rows, at in plan:
        cot_ref[at : at + rows, :] = pieces[i][start : start + rows, :]
    at = 0
    for value in turned:
        hidden_ref[:, at : at + value.shape[1]] = value[...]
        at += value.shape[1]
    for j in range(out_ref.shape[2] // TILE):
        columns = slice(j * TILE, (j + 1) * TILE)
        out_ref[0, :, columns] = jnp.dot(
            hidden_ref[...], cot_ref[:, columns], preferred_element_type=F32
        ).astype(BF16)


def combine_kernel(experts, plane_ref, tokens_ref, routes_ref, nums_ref, *refs):
    values, out = refs[:-1], refs[-1]
    routes = routes_ref[...]
    placings = placing_of(routes, plane_ref[0], experts, values[0].shape[0])
    gates = gates_of(routes, nums_ref[...], plane_ref[0], experts)
    fill = -experts % 8
    if fill:
        gates = jnp.concatenate([gates, jnp.zeros((fill, gates.shape[1]), F32)], 0)
    gates = gates.T
    total = tokens_ref[...].astype(F32)
    for s, value in enumerate(values):
        picked = lax.dot_general(
            placings[s].astype(BF16),
            value[...],
            (((0,), (0,)), ((), ())),
            preferred_element_type=F32,
        )
        total = total + gates[:, s : s + 1] * picked
    out[...] = total.astype(BF16)


def on_device(tokens, cotangent, routes, gate_nums, gain, w_gate, w_up, w_down):
    devices = lax.axis_size("expert")
    experts = devices // HSPLIT
    rows_here, width = tokens.shape
    hidden_width = w_gate.shape[2]
    top_count = routes.shape[1]
    capacity = HSPLIT * (3 * top_count * rows_here // (2 * experts * HSPLIT))
    capacity = -(-capacity // 16) * 16
    shifts = max(1, experts // GROUPS)
    groups = [list(range(g, g + shifts)) for g in range(0, experts, shifts)]
    height = shifts * capacity
    plane = (lax.axis_index("expert") // HSPLIT).astype(jnp.int32).reshape(1)
    routes, gate_nums, gain = routes.T, gate_nums.T, gain.reshape(1, -1)
    scalar = pl.BlockSpec(memory_space=pltpu.SMEM)
    anywhere = pl.BlockSpec(memory_space=pl.ANY)
    piece = jax.ShapeDtypeStruct((capacity, width), BF16)
    live = {}

    def swap(value, mask):
        return lax.ppermute(value, "expert", [(i, i ^ mask) for i in range(devices)])

    def sync():
        values = lax.optimization_barrier(tuple(live.values()))
        live.update(zip(list(live), values))

    def join(parts):
        return parts[0] if len(parts) == 1 else jnp.concatenate(parts, 0)

    flying = {}

    def launch(name, value, mask):
        flying[name] = swap(value, mask)

    def land():
        names = list(flying)
        landed = dict(zip(names, through([flying.pop(n) for n in names], "land", LINK_WORK)))
        for name, value in landed.items():
            if name[0] == "y":
                live[name[1:]] = join([live.pop(("sent",) + name[1:]), value])
            elif name[0] == "fold":
                gs = name[1]
                keep, crossed = live.pop(("keep", gs)), live.pop(("crossed", gs))
                rows = value.shape[0]
                total = keep[:rows].astype(F32) + crossed[:rows].astype(F32)
                total = (total + value.astype(F32)).astype(BF16)
                for i, s in enumerate([s for g in gs for s in groups[g]]):
                    live["R", s] = total[i * capacity : (i + 1) * capacity]
            else:
                live[name] = value
        return next(iter(landed.values()))

    def across(kind, g):
        for s in groups[g]:
            if s:
                launch((kind, s), live[kind, s], s * HSPLIT)

    def along(kind, *gs):
        own = join([live.pop((kind, s)) for g in gs for s in groups[g]])
        live["sent", kind, "own", gs] = own
        launch(("y", kind, "own", gs), own, 2)

    def core(kind, *gs):
        live[kind, "other", gs] = swap(live[kind, "own", gs], 1)

    def ffn(*gs):
        pieces = [live.pop(("N", "own", gs)), live.pop(("N", "other", gs))]
        half = jax.ShapeDtypeStruct(pieces[0].shape, BF16)
        rows = 2 * half.shape[0]
        live["turned", gs], live["keep", gs], live["send", gs] = call(
            functools.partial(ffn_kernel, len(pieces)),
            24,
            "ffn",
            out_shape=[jax.ShapeDtypeStruct((hidden_width, rows), BF16), half, half],
            in_specs=whole(len(pieces) + 3),
            out_specs=whole(3),
            scratch_shapes=[
                pltpu.VMEM((rows, width), BF16),
                pltpu.VMEM((rows, hidden_width), BF16),
            ],
        )(*pieces, live["w", 0], live["w", 1], live["w", 2])

    def cross(*gs):
        live["crossed", gs] = swap(live.pop(("send", gs)), 1)

    def fold_core(earlier, *gs):
        keep, crossed = live["keep", gs], after(live["crossed", gs], earlier)
        rows = keep.shape[0] // 2
        both = keep[rows:].astype(F32) + crossed[rows:].astype(F32)
        live["across", gs] = both.astype(BF16)

    def fold_row(*gs):
        launch(("fold", gs), live.pop(("across", gs)), 2)

    def back(g):
        across("R", g)

    def send_rows():
        values = call(
            functools.partial(send_rows_kernel, experts),
            16,
            "send_rows",
            out_shape=[piece] * experts,
            in_specs=[scalar] + [anywhere] * 3,
            out_specs=whole(experts),
            scratch_shapes=[
                pltpu.VMEM(tokens.shape, BF16),
                pltpu.VMEM(gain.shape, F32),
                pltpu.VMEM(routes.shape, jnp.int32),
                pltpu.SemaphoreType.DMA((3,)),
            ],
        )(plane, tokens, gain, routes)
        live.update({("N", s): value for s, value in enumerate(values)})

    def send_grads():
        values = call(
            functools.partial(send_grads_kernel, experts),
            16,
            "send_grads",
            out_shape=[piece] * experts,
            in_specs=[scalar] + [anywhere] * 3,
            out_specs=whole(experts),
            scratch_shapes=[
                pltpu.VMEM(cotangent.shape, BF16),
                pltpu.VMEM(routes.shape, jnp.int32),
                pltpu.VMEM(gate_nums.shape, jnp.int32),
                pltpu.SemaphoreType.DMA((3,)),
            ],
        )(plane, after(cotangent, live["N", experts - 1]), routes, gate_nums)
        live.update({("C", s): value for s, value in enumerate(values)})

    def load():
        weight = jax.ShapeDtypeStruct((width, hidden_width), BF16)
        values = call(
            load_kernel,
            16,
            "load",
            out_shape=[weight, weight, jax.ShapeDtypeStruct((hidden_width, width), BF16)],
            in_specs=[anywhere] * 3,
            out_specs=whole(3),
            scratch_shapes=[pltpu.SemaphoreType.DMA((3,))],
        )(after(w_gate, live["C", experts - 1]), w_up, w_down)
        live.update({("w", i): value for i, value in enumerate(values)})

    send_rows()
    if shifts > 1:
        across("N", 0)
        land()
    sync()
    along("N", 0)
    for g in (1, 2):
        across("N", g)
    send_grads()
    if shifts > 1:
        across("C", 0)
        land()
    along("C", 0)
    load()
    land()
    sync()
    across("N", 3)
    across("C", 1)
    along("N", 1, 2)
    core("N", 0)
    ffn(0)
    cross(0)
    fold_core(land(), 0)
    sync()
    across("C", 2)
    along("N", 3)
    fold_row(0)
    core("N", 1, 2)
    ffn(1, 2)
    cross(1, 2)
    fold_core(land(), 1, 2)
    sync()
    across("C", 3)
    fold_row(1, 2)
    core("N", 3)
    ffn(3)
    cross(3)
    core("C", 0)
    fold_core(land(), 3)
    sync()
    if shifts > 1:
        back(0)
    back(1)
    back(2)
    fold_row(3)
    along("C", 1)
    land()
    sync()
    back(3)
    along("C", 2, 3)
    core("C", 1)
    land()
    sync()
    core("C", 2, 3)

    places, at = {}, 0
    turned = [(0,), (1, 2), (3,)]
    for gs in turned:
        for half in ("own", "other"):
            for side in range(2):
                for g in gs:
                    places[half, side, g] = at
                    at += height
    pieces, plan = [], []
    for gs in [(0,), (1,), (2, 3)]:
        for half in ("own", "other"):
            for side in range(2):
                for i, g in enumerate(gs):
                    start = (side * len(gs) + i) * height
                    plan.append((len(pieces), start, height, places[half, side, g]))
            pieces.append(live["C", half, gs])
    grad_down = call(
        functools.partial(grad_kernel, plan, len(turned)),
        24,
        "grad",
        out_shape=jax.ShapeDtypeStruct((1, hidden_width, width), BF16),
        in_specs=whole(len(turned) + len(pieces)),
        out_specs=whole(1)[0],
        scratch_shapes=[
            pltpu.VMEM((hidden_width, at), BF16),
            pltpu.VMEM((at, width), BF16),
        ],
    )(*[live["turned", gs] for gs in turned], *pieces)
    mixed = call(
        functools.partial(combine_kernel, experts),
        16,
        "combine",
        out_shape=jax.ShapeDtypeStruct(tokens.shape, BF16),
        in_specs=[scalar] + whole(3 + experts),
        out_specs=whole(1)[0],
    )(plane, tokens, routes, gate_nums, *[live["R", s] for s in range(experts)])
    return (mixed, grad_down)


def solution(mesh):
    placed = (
        P(("group", "expert"), None),
        P(("group", "expert"), None),
        P(("group", "expert"), None),
        P(("group", "expert"), None),
        P(),
        P("expert", None, None),
        P("expert", None, None),
        P("expert", None, None),
    )
    return jax.shard_map(
        on_device,
        mesh=mesh,
        in_specs=placed,
        out_specs=(P(("group", "expert"), None), P(("group", "expert"), None, None)),
        check_vma=False,
    )
```

time: 243 us -> 88.2 us (0.36)
  the two profiles are of different devices: /device:TPU:15 before, /device:TPU:0 now
where the time goes in v2:
time: 88.2 us; the launch traced here: 87.8 us
  waiting for transfers between devices  32.5 us (37%)
  starting transfers between devices  25.1 us (28%)
  Pallas kernels  18.2 us (21%)
  local copies, waits for them, and re-layouts  10.2 us (12%)
  between operations  0.93 us (1%)
    ppermute x27, waiting for transfers between devices, swap(): lax.ppermute(value, 'expert', [(i, i ^ mask) for i in range(devices)])  32.5 us
    ppermute x27, starting transfers between devices, swap(): lax.ppermute(value, 'expert', [(i, i ^ mask) for i in range(devices)])  25.1 us
    pallas_call x3, Pallas kernels, ffn(): call(functools.partial(ffn_kernel, len(pieces)), 24, 'ffn', out_shape=[ja...  10.3 us
    unnamed x24, local copies, waits for them, and re-layouts  10.2 us
    pallas_call x1, Pallas kernels, on_device(): call(functools.partial(grad_kernel, plan, len(turned)), 24, 'grad', out_s...  4.75 us
  transfers between devices with their start and end apart: 27, of which 11 were waited for; matrix products, arithmetic and copies ran while one was open for 1% of the time, Pallas kernels for 14%

profile of v2, /device:TPU:0, one launch (start us, length us, event | category | flops | bytes accessed | tf_op | source)
XLA Modules:
  0.0 87.8 jit_solution(7287063801987101135)
XLA Ops:
  0.7 0.9 %copy-done.3 = bf16[128,1024]{1,0:T(8,128)(2,1)S(1)} copy-done((bf16[128,1024]{1,0:T(8,128)(2,1)S(1)}, bf16[128,1024]{1,0:T(8,128)(2,1)}, u32[]{:S(2)}) %copy-start.3) | copy-done | bytes 262168
  3.7 3.1 %collective-permute-start.1 = (bf16[96,1024]{1,0:T(8,128)(2,1)S(1)}, bf16[96,1024]{1,0:T(8,128)(2,1)S(1)}, u32[]{:S(2)}, u32[]{:S(2)}) collective-permute-start(bf16[96,1024]{1,0:T(8,128)(2,1)S(1)} %get-tuple-element.122), channel_id=1, source_target_pairs={{0,4},{1,5},{2,6},{3,7},{4,0},{5,1},{6,2},{7,3},{8,12},{9,13},{10,... | collective-permute-start | bytes 589832 | tf_op jit(solution)/shard_map/ppermute | solution.py:218
  6.8 2.6 %collective-permute-start.2 = (bf16[96,1024]{1,0:T(8,128)(2,1)S(1)}, bf16[96,1024]{1,0:T(8,128)(2,1)S(1)}, u32[]{:S(2)}, u32[]{:S(2)}) collective-permute-start(bf16[96,1024]{1,0:T(8,128)(2,1)S(1)} %get-tuple-element.123), channel_id=1, source_target_pairs={{0,8},{1,9},{2,10},{3,11},{4,12},{5,13},{6,14},{7,15},{8,0},{9,1},... | collective-permute-start | bytes 589832 | tf_op jit(solution)/shard_map/ppermute | solution.py:218
  9.3 1.5 %collective-permute-start = (bf16[96,1024]{1,0:T(8,128)(2,1)S(1)}, bf16[96,1024]{1,0:T(8,128)(2,1)S(1)}, u32[]{:S(2)}, u32[]{:S(2)}) collective-permute-start(bf16[96,1024]{1,0:T(8,128)(2,1)S(1)} %get-tuple-element.121), channel_id=1, source_target_pairs={{0,2},{1,3},{2,0},{3,1},{4,6},{5,7},{6,4},{7,5},{8,10},{9,11},{10,... | collective-permute-start | bytes 589832 | tf_op jit(solution)/shard_map/ppermute | solution.py:218
  10.9 0.9 %copy-done.5 = bf16[128,1024]{1,0:T(8,128)(2,1)S(1)} copy-done((bf16[128,1024]{1,0:T(8,128)(2,1)S(1)}, bf16[128,1024]{1,0:T(8,128)(2,1)}, u32[]{:S(2)}) %copy-start.5) | copy-done | bytes 262168
  14.3 1.6 %copy-done = bf16[1,1024,1024]{2,1,0:T(8,128)(2,1)S(1)} copy-done((bf16[1,1024,1024]{2,1,0:T(8,128)(2,1)S(1)}, bf16[1,1024,1024]{2,1,0:T(8,128)(2,1)}, u32[]{:S(2)}) %copy-start) | copy-done | bytes 2097176
  15.9 1.6 %copy-done.1 = bf16[1,1024,1024]{2,1,0:T(8,128)(2,1)S(1)} copy-done((bf16[1,1024,1024]{2,1,0:T(8,128)(2,1)S(1)}, bf16[1,1024,1024]{2,1,0:T(8,128)(2,1)}, u32[]{:S(2)}) %copy-start.1) | copy-done | bytes 2097176
  17.5 1.6 %copy-done.2 = bf16[1,1024,1024]{2,1,0:T(8,128)(2,1)S(1)} copy-done((bf16[1,1024,1024]{2,1,0:T(8,128)(2,1)S(1)}, bf16[1,1024,1024]{2,1,0:T(8,128)(2,1)}, u32[]{:S(2)}) %copy-start.2) | copy-done | bytes 2097176
  19.8 1.6 %collective-permute-start.6 = (bf16[192,1024]{1,0:T(8,128)(2,1)S(1)}, bf16[192,1024]{1,0:T(8,128)(2,1)S(1)}, u32[]{:S(2)}, u32[]{:S(2)}) collective-permute-start(bf16[192,1024]{1,0:T(8,128)(2,1)S(1)} %pad_maximum_fusion.4), channel_id=1, source_target_pairs={{0,2},{1,3},{2,0},{3,1},{4,6},{5,7},{6,4},{7,5},{8,10},{9,11},{10,... | collective-permute-start | bytes 1179656 | tf_op jit(solution)/shard_map/ppermute | solution.py:218
  21.4 1.1 %collective-permute-start.4 = (bf16[96,1024]{1,0:T(8,128)(2,1)S(1)}, bf16[96,1024]{1,0:T(8,128)(2,1)S(1)}, u32[]{:S(2)}, u32[]{:S(2)}) collective-permute-start(bf16[96,1024]{1,0:T(8,128)(2,1)S(1)} %get-tuple-element.138), channel_id=1, source_target_pairs={{0,12},{1,13},{2,14},{3,15},{4,8},{5,9},{6,10},{7,11},{8,4},{9,5},... | collective-permute-start | bytes 589832 | tf_op jit(solution)/shard_map/ppermute | solution.py:218
  22.5 2.6 %ffn.3 = (bf16[1024,384]{1,0:T(8,128)(2,1)S(1)}, bf16[192,1024]{1,0:T(8,128)(2,1)S(1)}, bf16[192,1024]{1,0:T(8,128)(2,1)S(1)}) custom-call(bf16[192,1024]{1,0:T(8,128)(2,1)S(1)} %get-tuple-element.150.refs_0_, bf16[192,1024]{1,0:T(8,128)(2,1)S(1)} %collective-permute-done.7.refs_1_, bf16[1024,1024]{1,0:T(8,128)(2,1)S(1)} %get-tuple-element.181.refs_2_, ...), custom_call_target="tpu_custom_call" | custom-call | tf_op jit(solution)/shard_map/ffn/pallas_call | solution.py:267
  25.2 5.8 %collective-permute-done.4.refs_0_ = bf16[96,1024]{1,0:T(8,128)(2,1)S(1)} collective-permute-done((bf16[96,1024]{1,0:T(8,128)(2,1)S(1)}, bf16[96,1024]{1,0:T(8,128)(2,1)S(1)}, u32[]{:S(2)}, u32[]{:S(2)}) %collective-permute-start.4) | collective-permute-done | bytes 196640 | tf_op jit(solution)/shard_map/ppermute | solution.py:218
  31.0 2.5 %collective-permute-done.5.refs_1_ = bf16[96,1024]{1,0:T(8,128)(2,1)S(1)} collective-permute-done((bf16[96,1024]{1,0:T(8,128)(2,1)S(1)}, bf16[96,1024]{1,0:T(8,128)(2,1)S(1)}, u32[]{:S(2)}, u32[]{:S(2)}) %collective-permute-start.5) | collective-permute-done | bytes 196640 | tf_op jit(solution)/shard_map/ppermute | solution.py:218
  33.7 1.6 %collective-permute-start.9 = (bf16[96,1024]{1,0:T(8,128)(2,1)S(1)}, bf16[96,1024]{1,0:T(8,128)(2,1)S(1)}, u32[]{:S(2)}, u32[]{:S(2)}) collective-permute-start(bf16[96,1024]{1,0:T(8,128)(2,1)S(1)} %get-tuple-element.157), channel_id=1, source_target_pairs={{0,8},{1,9},{2,10},{3,11},{4,12},{5,13},{6,14},{7,15},{8,0},{9,1},... | collective-permute-start | bytes 589832 | tf_op jit(solution)/shard_map/ppermute | solution.py:218
  35.8 1.6 %collective-permute-start.10 = (bf16[96,1024]{1,0:T(8,128)(2,1)S(1)}, bf16[96,1024]{1,0:T(8,128)(2,1)S(1)}, u32[]{:S(2)}, u32[]{:S(2)}) collective-permute-start(bf16[96,1024]{1,0:T(8,128)(2,1)S(1)} %get-tuple-element.158), channel_id=1, source_target_pairs={{0,2},{1,3},{2,0},{3,1},{4,6},{5,7},{6,4},{7,5},{8,10},{9,11},{10,... | collective-permute-start | bytes 589832 | tf_op jit(solution)/shard_map/ppermute | solution.py:218
  37.4 5.1 %ffn.4 = (bf16[1024,768]{1,0:T(8,128)(2,1)S(1)}, bf16[384,1024]{1,0:T(8,128)(2,1)S(1)}, bf16[384,1024]{1,0:T(8,128)(2,1)S(1)}) custom-call(bf16[384,1024]{1,0:T(8,128)(2,1)S(1)} %pad_maximum_fusion.refs_0_, bf16[384,1024]{1,0:T(8,128)(2,1)S(1)} %collective-permute-done.12.refs_1_, bf16[1024,1024]{1,0:T(8,128)(2,1)S(1)} %get-tuple-element.181.refs_2_, ...), custom_call_target="tpu_custom_call" | custom-call | tf_op jit(solution)/shard_map/ffn/pallas_call | solution.py:267
  42.5 3.4 %collective-permute-done.9.refs_0_ = bf16[96,1024]{1,0:T(8,128)(2,1)S(1)} collective-permute-done((bf16[96,1024]{1,0:T(8,128)(2,1)S(1)}, bf16[96,1024]{1,0:T(8,128)(2,1)S(1)}, u32[]{:S(2)}, u32[]{:S(2)}) %collective-permute-start.9) | collective-permute-done | bytes 196640 | tf_op jit(solution)/shard_map/ppermute | solution.py:218
  47.4 1.8 %collective-permute-start.14 = (bf16[96,1024]{1,0:T(8,128)(2,1)S(1)}, bf16[96,1024]{1,0:T(8,128)(2,1)S(1)}, u32[]{:S(2)}, u32[]{:S(2)}) collective-permute-start(bf16[96,1024]{1,0:T(8,128)(2,1)S(1)} %get-tuple-element.178), channel_id=1, source_target_pairs={{0,12},{1,13},{2,14},{3,15},{4,8},{5,9},{6,10},{7,11},{8,4},{9,5},... | collective-permute-start | bytes 589832 | tf_op jit(solution)/shard_map/ppermute | solution.py:218
  49.2 2.6 %ffn.5 = (bf16[1024,384]{1,0:T(8,128)(2,1)S(1)}, bf16[192,1024]{1,0:T(8,128)(2,1)S(1)}, bf16[192,1024]{1,0:T(8,128)(2,1)S(1)}) custom-call(bf16[192,1024]{1,0:T(8,128)(2,1)S(1)} %pad_maximum_fusion.5.refs_0_, bf16[192,1024]{1,0:T(8,128)(2,1)S(1)} %collective-permute-done.16.refs_1_, bf16[1024,1024]{1,0:T(8,128)(2,1)S(1)} %get-tuple-element.181.refs_2_, ...), custom_call_target="tpu_custom_call" | custom-call | tf_op jit(solution)/shard_map/ffn/pallas_call | solution.py:267
  52.4 3.9 %collective-permute-done.14.refs_0_ = bf16[96,1024]{1,0:T(8,128)(2,1)S(1)} collective-permute-done((bf16[96,1024]{1,0:T(8,128)(2,1)S(1)}, bf16[96,1024]{1,0:T(8,128)(2,1)S(1)}, u32[]{:S(2)}, u32[]{:S(2)}) %collective-permute-start.14) | collective-permute-done | bytes 196640 | tf_op jit(solution)/shard_map/ppermute | solution.py:218
  56.3 2.1 %collective-permute-done.15.refs_1_ = bf16[192,1024]{1,0:T(8,128)(2,1)S(1)} collective-permute-done((bf16[192,1024]{1,0:T(8,128)(2,1)S(1)}, bf16[192,1024]{1,0:T(8,128)(2,1)S(1)}, u32[]{:S(2)}, u32[]{:S(2)}) %collective-permute-start.15) | collective-permute-done | bytes 393248 | tf_op jit(solution)/shard_map/ppermute | solution.py:218
  58.7 1.5 %collective-permute-start.19 = (bf16[96,1024]{1,0:T(8,128)(2,1)S(1)}, bf16[96,1024]{1,0:T(8,128)(2,1)S(1)}, u32[]{:S(2)}, u32[]{:S(2)}) collective-permute-start(bf16[96,1024]{1,0:T(8,128)(2,1)S(1)} %get-tuple-element.204), channel_id=1, source_target_pairs={{0,4},{1,5},{2,6},{3,7},{4,0},{5,1},{6,2},{7,3},{8,12},{9,13},{10,... | collective-permute-start | bytes 589832 | tf_op jit(solution)/shard_map/ppermute | solution.py:218
  60.2 0.9 %collective-permute-start.20 = (bf16[96,1024]{1,0:T(8,128)(2,1)S(1)}, bf16[96,1024]{1,0:T(8,128)(2,1)S(1)}, u32[]{:S(2)}, u32[]{:S(2)}) collective-permute-start(bf16[96,1024]{1,0:T(8,128)(2,1)S(1)} %get-tuple-element.205), channel_id=1, source_target_pairs={{0,8},{1,9},{2,10},{3,11},{4,12},{5,13},{6,14},{7,15},{8,0},{9,1},... | collective-permute-start | bytes 589832 | tf_op jit(solution)/shard_map/ppermute | solution.py:218
  61.1 0.8 collective-permute-start.21
  61.9 1.2 %collective-permute-start.22 = (bf16[96,1024]{1,0:T(8,128)(2,1)S(1)}, bf16[96,1024]{1,0:T(8,128)(2,1)S(1)}, u32[]{:S(2)}, u32[]{:S(2)}) collective-permute-start(bf16[96,1024]{1,0:T(8,128)(2,1)S(1)} %get-tuple-element.207), channel_id=1, source_target_pairs={{0,2},{1,3},{2,0},{3,1},{4,6},{5,7},{6,4},{7,5},{8,10},{9,11},{10,... | collective-permute-start | bytes 589832 | tf_op jit(solution)/shard_map/ppermute | solution.py:218
  63.1 5.4 %collective-permute-done.19.refs_0_ = bf16[96,1024]{1,0:T(8,128)(2,1)S(1)} collective-permute-done((bf16[96,1024]{1,0:T(8,128)(2,1)S(1)}, bf16[96,1024]{1,0:T(8,128)(2,1)S(1)}, u32[]{:S(2)}, u32[]{:S(2)}) %collective-permute-start.19) | collective-permute-done | bytes 196640 | tf_op jit(solution)/shard_map/ppermute | solution.py:218
  68.5 2.8 %collective-permute-done.20.refs_1_ = bf16[96,1024]{1,0:T(8,128)(2,1)S(1)} collective-permute-done((bf16[96,1024]{1,0:T(8,128)(2,1)S(1)}, bf16[96,1024]{1,0:T(8,128)(2,1)S(1)}, u32[]{:S(2)}, u32[]{:S(2)}) %collective-permute-start.20) | collective-permute-done | bytes 196640 | tf_op jit(solution)/shard_map/ppermute | solution.py:218
  71.4 1.5 %collective-permute-start.24 = (bf16[192,1024]{1,0:T(8,128)(2,1)S(1)}, bf16[192,1024]{1,0:T(8,128)(2,1)S(1)}, u32[]{:S(2)}, u32[]{:S(2)}) collective-permute-start(bf16[192,1024]{1,0:T(8,128)(2,1)S(1)} %pad_maximum_fusion.7), channel_id=1, source_target_pairs={{0,2},{1,3},{2,0},{3,1},{4,6},{5,7},{6,4},{7,5},{8,10},{9,11},{10,... | collective-permute-start | bytes 1179656 | tf_op jit(solution)/shard_map/ppermute | solution.py:218
  72.9 1.6 %collective-permute-start.23 = (bf16[96,1024]{1,0:T(8,128)(2,1)S(1)}, bf16[96,1024]{1,0:T(8,128)(2,1)S(1)}, u32[]{:S(2)}, u32[]{:S(2)}) collective-permute-start(bf16[96,1024]{1,0:T(8,128)(2,1)S(1)} %add_convert_fusion.2), channel_id=1, source_target_pairs={{0,12},{1,13},{2,14},{3,15},{4,8},{5,9},{6,10},{7,11},{8,4},{9,5},... | collective-permute-start | bytes 589832 | tf_op jit(solution)/shard_map/ppermute | solution.py:218
  74.6 5.9 %collective-permute-done.23.refs_0_ = bf16[96,1024]{1,0:T(8,128)(2,1)S(1)} collective-permute-done((bf16[96,1024]{1,0:T(8,128)(2,1)S(1)}, bf16[96,1024]{1,0:T(8,128)(2,1)S(1)}, u32[]{:S(2)}, u32[]{:S(2)}) %collective-permute-start.23) | collective-permute-done | bytes 196640 | tf_op jit(solution)/shard_map/ppermute | solution.py:218
  81.6 1.4 %combine.1 = bf16[128,1024]{1,0:T(8,128)(2,1)} custom-call(s32[1]{0:T(128)} %bitcast.plane_ref, bf16[128,1024]{1,0:T(8,128)(2,1)S(1)} %copy-done.4, s32[2,128]{1,0:T(2,128)S(1)} %bitcast.6, s32[2,128]{1,0:T(2,128)S(1)} %bitcast.9, bf16[96,1024]{1,0:T(8,128)(2,1)S(1)} %add_convert_fusion.4.refs_0_, bf16[96,1024]{1,0:T(8,128)(2,1)S(1)} %get-tuple-element.229.refs_1_, ...), custom_call_target="tpu_custom_call" | custom-call | tf_op jit(solution)/shard_map/combine/pallas_call | solution.py:425
  83.1 4.7 %grad.1 = bf16[1,1024,1024]{2,1,0:T(8,128)(2,1)} custom-call(bf16[1024,384]{1,0:T(8,128)(2,1)S(1)} %get-tuple-element.232.refs_0_, bf16[1024,768]{1,0:T(8,128)(2,1)S(1)} %get-tuple-element.233.refs_1_, bf16[1024,384]{1,0:T(8,128)(2,1)S(1)} %get-tuple-element.234.refs_2_, bf16[192,1024]{1,0:T(8,128)(2,1)S(1)} %get-tuple-element.235.refs_3_, ...), custom_call_target="tpu_custom_call" | custom-call | tf_op jit(solution)/shard_map/grad/pallas_call | solution.py:413
  (74 shorter events, 9.7 us)
Async XLA Ops:
  0.6 1.0 %copy-start.3 = (bf16[128,1024]{1,0:T(8,128)(2,1)S(1)}, bf16[128,1024]{1,0:T(8,128)(2,1)}, u32[]{:S(2)}) copy-start(bf16[128,1024]{1,0:T(8,128)(2,1)} %tokens_ref.1) | copy-start | bytes 786436
  3.7 15.9 %collective-permute-start.1 = (bf16[96,1024]{1,0:T(8,128)(2,1)S(1)}, bf16[96,1024]{1,0:T(8,128)(2,1)S(1)}, u32[]{:S(2)}, u32[]{:S(2)}) collective-permute-start(bf16[96,1024]{1,0:T(8,128)(2,1)S(1)} %get-tuple-element.122), channel_id=1, source_target_pairs={{0,4},{1,5},{2,6},{3,7},{4,0},{5,1},{6,2},{7,3},{8,12},{9,13},{10,... | collective-permute-start | bytes 589832 | tf_op jit(solution)/shard_map/ppermute | solution.py:218
  6.8 12.8 %collective-permute-start.2 = (bf16[96,1024]{1,0:T(8,128)(2,1)S(1)}, bf16[96,1024]{1,0:T(8,128)(2,1)S(1)}, u32[]{:S(2)}, u32[]{:S(2)}) collective-permute-start(bf16[96,1024]{1,0:T(8,128)(2,1)S(1)} %get-tuple-element.123), channel_id=1, source_target_pairs={{0,8},{1,9},{2,10},{3,11},{4,12},{5,13},{6,14},{7,15},{8,0},{9,1},... | collective-permute-start | bytes 589832 | tf_op jit(solution)/shard_map/ppermute | solution.py:218
  9.3 10.3 %collective-permute-start = (bf16[96,1024]{1,0:T(8,128)(2,1)S(1)}, bf16[96,1024]{1,0:T(8,128)(2,1)S(1)}, u32[]{:S(2)}, u32[]{:S(2)}) collective-permute-start(bf16[96,1024]{1,0:T(8,128)(2,1)S(1)} %get-tuple-element.121), channel_id=1, source_target_pairs={{0,2},{1,3},{2,0},{3,1},{4,6},{5,7},{6,4},{7,5},{8,10},{9,11},{10,... | collective-permute-start | bytes 589832 | tf_op jit(solution)/shard_map/ppermute | solution.py:218
  13.8 5.9 %collective-permute-start.3 = (bf16[96,1024]{1,0:T(8,128)(2,1)S(1)}, bf16[96,1024]{1,0:T(8,128)(2,1)S(1)}, u32[]{:S(2)}, u32[]{:S(2)}) collective-permute-start(bf16[96,1024]{1,0:T(8,128)(2,1)S(1)} %get-tuple-element.126), channel_id=1, source_target_pairs={{0,2},{1,3},{2,0},{3,1},{4,6},{5,7},{6,4},{7,5},{8,10},{9,11},{10,... | collective-permute-start | bytes 589832 | tf_op jit(solution)/shard_map/ppermute | solution.py:218
  14.3 1.6 %copy-start = (bf16[1,1024,1024]{2,1,0:T(8,128)(2,1)S(1)}, bf16[1,1024,1024]{2,1,0:T(8,128)(2,1)}, u32[]{:S(2)}) copy-start(bf16[1,1024,1024]{2,1,0:T(8,128)(2,1)} %refs_0_) | copy-start | bytes 6291460
  15.9 1.6 %copy-start.1 = (bf16[1,1024,1024]{2,1,0:T(8,128)(2,1)S(1)}, bf16[1,1024,1024]{2,1,0:T(8,128)(2,1)}, u32[]{:S(2)}) copy-start(bf16[1,1024,1024]{2,1,0:T(8,128)(2,1)} %refs_1_.1) | copy-start | bytes 6291460
  17.5 1.6 %copy-start.2 = (bf16[1,1024,1024]{2,1,0:T(8,128)(2,1)S(1)}, bf16[1,1024,1024]{2,1,0:T(8,128)(2,1)}, u32[]{:S(2)}) copy-start(bf16[1,1024,1024]{2,1,0:T(8,128)(2,1)} %refs_2_.1) | copy-start | bytes 6291460
  19.7 2.8 %collective-permute-start.7 = (bf16[192,1024]{1,0:T(8,128)(2,1)S(1)}, bf16[192,1024]{1,0:T(8,128)(2,1)S(1)}, u32[]{:S(2)}, u32[]{:S(2)}) collective-permute-start(bf16[192,1024]{1,0:T(8,128)(2,1)S(1)} %get-tuple-element.150.refs_0_), channel_id=1, source_target_pairs={{0,1},{1,0},{2,3},{3,2},{4,5},{5,4},{6,7},{7,6},{8,9},{9,8},{10,11... | collective-permute-start | bytes 1179656 | tf_op jit(solution)/shard_map/ppermute | solution.py:218
  19.8 13.7 %collective-permute-start.6 = (bf16[192,1024]{1,0:T(8,128)(2,1)S(1)}, bf16[192,1024]{1,0:T(8,128)(2,1)S(1)}, u32[]{:S(2)}, u32[]{:S(2)}) collective-permute-start(bf16[192,1024]{1,0:T(8,128)(2,1)S(1)} %pad_maximum_fusion.4), channel_id=1, source_target_pairs={{0,2},{1,3},{2,0},{3,1},{4,6},{5,7},{6,4},{7,5},{8,10},{9,11},{10,... | collective-permute-start | bytes 1179656 | tf_op jit(solution)/shard_map/ppermute | solution.py:218
  21.4 9.6 %collective-permute-start.4 = (bf16[96,1024]{1,0:T(8,128)(2,1)S(1)}, bf16[96,1024]{1,0:T(8,128)(2,1)S(1)}, u32[]{:S(2)}, u32[]{:S(2)}) collective-permute-start(bf16[96,1024]{1,0:T(8,128)(2,1)S(1)} %get-tuple-element.138), channel_id=1, source_target_pairs={{0,12},{1,13},{2,14},{3,15},{4,8},{5,9},{6,10},{7,11},{8,4},{9,5},... | collective-permute-start | bytes 589832 | tf_op jit(solution)/shard_map/ppermute | solution.py:218
  22.5 11.0 %collective-permute-start.5 = (bf16[96,1024]{1,0:T(8,128)(2,1)S(1)}, bf16[96,1024]{1,0:T(8,128)(2,1)S(1)}, u32[]{:S(2)}, u32[]{:S(2)}) collective-permute-start(bf16[96,1024]{1,0:T(8,128)(2,1)S(1)} %get-tuple-element.139), channel_id=1, source_target_pairs={{0,4},{1,5},{2,6},{3,7},{4,0},{5,1},{6,2},{7,3},{8,12},{9,13},{10,... | collective-permute-start | bytes 589832 | tf_op jit(solution)/shard_map/ppermute | solution.py:218
  25.1 8.4 %collective-permute-start.8 = (bf16[192,1024]{1,0:T(8,128)(2,1)S(1)}, bf16[192,1024]{1,0:T(8,128)(2,1)S(1)}, u32[]{:S(2)}, u32[]{:S(2)}) collective-permute-start(bf16[192,1024]{1,0:T(8,128)(2,1)S(1)} %get-tuple-element.153), channel_id=1, source_target_pairs={{0,1},{1,0},{2,3},{3,2},{4,5},{5,4},{6,7},{7,6},{8,9},{9,8},{10,11... | collective-permute-start | bytes 1179656 | tf_op jit(solution)/shard_map/ppermute | solution.py:218
  33.6 3.8 %collective-permute-start.12 = (bf16[384,1024]{1,0:T(8,128)(2,1)S(1)}, bf16[384,1024]{1,0:T(8,128)(2,1)S(1)}, u32[]{:S(2)}, u32[]{:S(2)}) collective-permute-start(bf16[384,1024]{1,0:T(8,128)(2,1)S(1)} %pad_maximum_fusion.refs_0_), channel_id=1, source_target_pairs={{0,1},{1,0},{2,3},{3,2},{4,5},{5,4},{6,7},{7,6},{8,9},{9,8},{10,11... | collective-permute-start | bytes 2359304 | tf_op jit(solution)/shard_map/ppermute | solution.py:218
  33.7 12.2 %collective-permute-start.9 = (bf16[96,1024]{1,0:T(8,128)(2,1)S(1)}, bf16[96,1024]{1,0:T(8,128)(2,1)S(1)}, u32[]{:S(2)}, u32[]{:S(2)}) collective-permute-start(bf16[96,1024]{1,0:T(8,128)(2,1)S(1)} %get-tuple-element.157), channel_id=1, source_target_pairs={{0,8},{1,9},{2,10},{3,11},{4,12},{5,13},{6,14},{7,15},{8,0},{9,1},... | collective-permute-start | bytes 589832 | tf_op jit(solution)/shard_map/ppermute | solution.py:218
  35.3 10.6 %collective-permute-start.11 = (bf16[96,1024]{1,0:T(8,128)(2,1)S(1)}, bf16[96,1024]{1,0:T(8,128)(2,1)S(1)}, u32[]{:S(2)}, u32[]{:S(2)}) collective-permute-start(bf16[96,1024]{1,0:T(8,128)(2,1)S(1)} %add_convert_fusion.5), channel_id=1, source_target_pairs={{0,2},{1,3},{2,0},{3,1},{4,6},{5,7},{6,4},{7,5},{8,10},{9,11},{10,... | collective-permute-start | bytes 589832 | tf_op jit(solution)/shard_map/ppermute | solution.py:218
  35.8 10.7 %collective-permute-start.10 = (bf16[96,1024]{1,0:T(8,128)(2,1)S(1)}, bf16[96,1024]{1,0:T(8,128)(2,1)S(1)}, u32[]{:S(2)}, u32[]{:S(2)}) collective-permute-start(bf16[96,1024]{1,0:T(8,128)(2,1)S(1)} %get-tuple-element.158), channel_id=1, source_target_pairs={{0,2},{1,3},{2,0},{3,1},{4,6},{5,7},{6,4},{7,5},{8,10},{9,11},{10,... | collective-permute-start | bytes 589832 | tf_op jit(solution)/shard_map/ppermute | solution.py:218
  42.4 4.2 %collective-permute-start.13 = (bf16[384,1024]{1,0:T(8,128)(2,1)S(1)}, bf16[384,1024]{1,0:T(8,128)(2,1)S(1)}, u32[]{:S(2)}, u32[]{:S(2)}) collective-permute-start(bf16[384,1024]{1,0:T(8,128)(2,1)S(1)} %get-tuple-element.170), channel_id=1, source_target_pairs={{0,1},{1,0},{2,3},{3,2},{4,5},{5,4},{6,7},{7,6},{8,9},{9,8},{10,11... | collective-permute-start | bytes 2359304 | tf_op jit(solution)/shard_map/ppermute | solution.py:218
  46.8 2.5 %collective-permute-start.16 = (bf16[192,1024]{1,0:T(8,128)(2,1)S(1)}, bf16[192,1024]{1,0:T(8,128)(2,1)S(1)}, u32[]{:S(2)}, u32[]{:S(2)}) collective-permute-start(bf16[192,1024]{1,0:T(8,128)(2,1)S(1)} %pad_maximum_fusion.5.refs_0_), channel_id=1, source_target_pairs={{0,1},{1,0},{2,3},{3,2},{4,5},{5,4},{6,7},{7,6},{8,9},{9,8},{10,11... | collective-permute-start | bytes 1179656 | tf_op jit(solution)/shard_map/ppermute | solution.py:218
  46.8 11.5 %collective-permute-start.15 = (bf16[192,1024]{1,0:T(8,128)(2,1)S(1)}, bf16[192,1024]{1,0:T(8,128)(2,1)S(1)}, u32[]{:S(2)}, u32[]{:S(2)}) collective-permute-start(bf16[192,1024]{1,0:T(8,128)(2,1)S(1)} %add_convert_fusion.1), channel_id=1, source_target_pairs={{0,2},{1,3},{2,0},{3,1},{4,6},{5,7},{6,4},{7,5},{8,10},{9,11},{10,... | collective-permute-start | bytes 1179656 | tf_op jit(solution)/shard_map/ppermute | solution.py:218
  47.4 8.9 %collective-permute-start.14 = (bf16[96,1024]{1,0:T(8,128)(2,1)S(1)}, bf16[96,1024]{1,0:T(8,128)(2,1)S(1)}, u32[]{:S(2)}, u32[]{:S(2)}) collective-permute-start(bf16[96,1024]{1,0:T(8,128)(2,1)S(1)} %get-tuple-element.178), channel_id=1, source_target_pairs={{0,12},{1,13},{2,14},{3,15},{4,8},{5,9},{6,10},{7,11},{8,4},{9,5},... | collective-permute-start | bytes 589832 | tf_op jit(solution)/shard_map/ppermute | solution.py:218
  49.2 9.5 %collective-permute-start.18 = (bf16[192,1024]{1,0:T(8,128)(2,1)S(1)}, bf16[192,1024]{1,0:T(8,128)(2,1)S(1)}, u32[]{:S(2)}, u32[]{:S(2)}) collective-permute-start(bf16[192,1024]{1,0:T(8,128)(2,1)S(1)} %get-tuple-element.235.refs_3_), channel_id=1, source_target_pairs={{0,1},{1,0},{2,3},{3,2},{4,5},{5,4},{6,7},{7,6},{8,9},{9,8},{10,11... | collective-permute-start | bytes 1179656 | tf_op jit(solution)/shard_map/ppermute | solution.py:218
  51.8 6.8 %collective-permute-start.17 = (bf16[192,1024]{1,0:T(8,128)(2,1)S(1)}, bf16[192,1024]{1,0:T(8,128)(2,1)S(1)}, u32[]{:S(2)}, u32[]{:S(2)}) collective-permute-start(bf16[192,1024]{1,0:T(8,128)(2,1)S(1)} %get-tuple-element.191), channel_id=1, source_target_pairs={{0,1},{1,0},{2,3},{3,2},{4,5},{5,4},{6,7},{7,6},{8,9},{9,8},{10,11... | collective-permute-start | bytes 1179656 | tf_op jit(solution)/shard_map/ppermute | solution.py:218
  58.7 9.8 %collective-permute-start.19 = (bf16[96,1024]{1,0:T(8,128)(2,1)S(1)}, bf16[96,1024]{1,0:T(8,128)(2,1)S(1)}, u32[]{:S(2)}, u32[]{:S(2)}) collective-permute-start(bf16[96,1024]{1,0:T(8,128)(2,1)S(1)} %get-tuple-element.204), channel_id=1, source_target_pairs={{0,4},{1,5},{2,6},{3,7},{4,0},{5,1},{6,2},{7,3},{8,12},{9,13},{10,... | collective-permute-start | bytes 589832 | tf_op jit(solution)/shard_map/ppermute | solution.py:218
  60.2 11.1 %collective-permute-start.20 = (bf16[96,1024]{1,0:T(8,128)(2,1)S(1)}, bf16[96,1024]{1,0:T(8,128)(2,1)S(1)}, u32[]{:S(2)}, u32[]{:S(2)}) collective-permute-start(bf16[96,1024]{1,0:T(8,128)(2,1)S(1)} %get-tuple-element.205), channel_id=1, source_target_pairs={{0,8},{1,9},{2,10},{3,11},{4,12},{5,13},{6,14},{7,15},{8,0},{9,1},... | collective-permute-start | bytes 589832 | tf_op jit(solution)/shard_map/ppermute | solution.py:218
  61.1 10.2 %collective-permute-start.21 = (bf16[96,1024]{1,0:T(8,128)(2,1)S(1)}, bf16[96,1024]{1,0:T(8,128)(2,1)S(1)}, u32[]{:S(2)}, u32[]{:S(2)}) collective-permute-start(bf16[96,1024]{1,0:T(8,128)(2,1)S(1)} %add_convert_fusion.3), channel_id=1, source_target_pairs={{0,2},{1,3},{2,0},{3,1},{4,6},{5,7},{6,4},{7,5},{8,10},{9,11},{10,... | collective-permute-start | bytes 589832 | tf_op jit(solution)/shard_map/ppermute | solution.py:218
  61.9 9.3 %collective-permute-start.22 = (bf16[96,1024]{1,0:T(8,128)(2,1)S(1)}, bf16[96,1024]{1,0:T(8,128)(2,1)S(1)}, u32[]{:S(2)}, u32[]{:S(2)}) collective-permute-start(bf16[96,1024]{1,0:T(8,128)(2,1)S(1)} %get-tuple-element.207), channel_id=1, source_target_pairs={{0,2},{1,3},{2,0},{3,1},{4,6},{5,7},{6,4},{7,5},{8,10},{9,11},{10,... | collective-permute-start | bytes 589832 | tf_op jit(solution)/shard_map/ppermute | solution.py:218
  71.4 9.2 %collective-permute-start.24 = (bf16[192,1024]{1,0:T(8,128)(2,1)S(1)}, bf16[192,1024]{1,0:T(8,128)(2,1)S(1)}, u32[]{:S(2)}, u32[]{:S(2)}) collective-permute-start(bf16[192,1024]{1,0:T(8,128)(2,1)S(1)} %pad_maximum_fusion.7), channel_id=1, source_target_pairs={{0,2},{1,3},{2,0},{3,1},{4,6},{5,7},{6,4},{7,5},{8,10},{9,11},{10,... | collective-permute-start | bytes 1179656 | tf_op jit(solution)/shard_map/ppermute | solution.py:218
  72.9 7.6 %collective-permute-start.23 = (bf16[96,1024]{1,0:T(8,128)(2,1)S(1)}, bf16[96,1024]{1,0:T(8,128)(2,1)S(1)}, u32[]{:S(2)}, u32[]{:S(2)}) collective-permute-start(bf16[96,1024]{1,0:T(8,128)(2,1)S(1)} %add_convert_fusion.2), channel_id=1, source_target_pairs={{0,12},{1,13},{2,14},{3,15},{4,8},{5,9},{6,10},{7,11},{8,4},{9,5},... | collective-permute-start | bytes 589832 | tf_op jit(solution)/shard_map/ppermute | solution.py:218
  74.6 6.1 %collective-permute-start.25 = (bf16[192,1024]{1,0:T(8,128)(2,1)S(1)}, bf16[192,1024]{1,0:T(8,128)(2,1)S(1)}, u32[]{:S(2)}, u32[]{:S(2)}) collective-permute-start(bf16[192,1024]{1,0:T(8,128)(2,1)S(1)} %pad_maximum_fusion.6.refs_5_), channel_id=1, source_target_pairs={{0,1},{1,0},{2,3},{3,2},{4,5},{5,4},{6,7},{7,6},{8,9},{9,8},{10,11... | collective-permute-start | bytes 1179656 | tf_op jit(solution)/shard_map/ppermute | solution.py:218
  80.7 1.0 %copy-start.11 = (s32[128,2]{0,1:T(2,128)S(1)}, s32[128,2]{0,1:T(2,128)}, u32[]{:S(2)}) copy-start(s32[128,2]{0,1:T(2,128)} %param.11) | copy-start | bytes 3076
  80.7 2.4 %collective-permute-start.26 = (bf16[384,1024]{1,0:T(8,128)(2,1)S(1)}, bf16[384,1024]{1,0:T(8,128)(2,1)S(1)}, u32[]{:S(2)}, u32[]{:S(2)}) collective-permute-start(bf16[384,1024]{1,0:T(8,128)(2,1)S(1)} %pad_maximum_fusion.1.refs_7_), channel_id=1, source_target_pairs={{0,1},{1,0},{2,3},{3,2},{4,5},{5,4},{6,7},{7,6},{8,9},{9,8},{10,11... | collective-permute-start | bytes 2359304 | tf_op jit(solution)/shard_map/ppermute | solution.py:218
  (7 other events, 5.6 us)

commit v3 on v2

--- a/solution.py
+++ b/solution.py
@@ -9,8 +9,9 @@
 
 HSPLIT = 4
 GROUPS = 4
+JOINED = ((1, 2), (2, 3))
 TILE = 256
-LINK_WORK = 10 << 30
+LINK_WORK = int(8 * 2**30)
 F32 = jnp.float32
 BF16 = jnp.bfloat16
 
@@ -159,20 +160,21 @@
         send_ref[:, columns] = value[half:]
 
 
-def grad_kernel(plan, turned_count, *refs):
-    turned, pieces = refs[:turned_count], refs[turned_count:-3]
+def grad_kernel(plan, earlier_count, *refs):
+    earlier, refs = refs[:earlier_count], refs[earlier_count:]
     out_ref, hidden_ref, cot_ref = refs[-3:]
-    for i, start, rows, at in plan:
-        cot_ref[at : at + rows, :] = pieces[i][start : start + rows, :]
     at = 0
-    for value in turned:
-        hidden_ref[:, at : at + value.shape[1]] = value[...]
-        at += value.shape[1]
-    for j in range(out_ref.shape[2] // TILE):
+    for turned, column, piece, row, count in plan:
+        hidden_ref[:, at : at + count] = refs[turned][:, column : column + count]
+        cot_ref[at : at + count, :] = refs[piece][row : row + count, :]
+        at += count
+    for j in range(cot_ref.shape[1] // TILE):
         columns = slice(j * TILE, (j + 1) * TILE)
-        out_ref[0, :, columns] = jnp.dot(
-            hidden_ref[...], cot_ref[:, columns], preferred_element_type=F32
-        ).astype(BF16)
+        total = jnp.dot(hidden_ref[...], cot_ref[:, columns], preferred_element_type=F32)
+        if earlier:
+            out_ref[0, :, columns] = (earlier[0][0, :, columns] + total).astype(BF16)
+        else:
+            out_ref[0, :, columns] = total
 
 
 def combine_kernel(experts, plane_ref, tokens_ref, routes_ref, nums_ref, *refs):
@@ -224,15 +226,16 @@
     def join(parts):
         return parts[0] if len(parts) == 1 else jnp.concatenate(parts, 0)
 
-    flying = {}
+    flying, last = {}, []
 
     def launch(name, value, mask):
         flying[name] = swap(value, mask)
 
-    def land():
-        names = list(flying)
-        landed = dict(zip(names, through([flying.pop(n) for n in names], "land", LINK_WORK)))
-        for name, value in landed.items():
+    def land(*names):
+        values = tuple(flying.pop(n) for n in names) + tuple(last)
+        landed = through(lax.optimization_barrier(values)[: len(names)], "land", LINK_WORK)
+        last[:] = landed[:1]
+        for name, value in zip(names, landed):
             if name[0] == "y":
                 live[name[1:]] = join([live.pop(("sent",) + name[1:]), value])
             elif name[0] == "fold":
@@ -245,7 +248,13 @@
                     live["R", s] = total[i * capacity : (i + 1) * capacity]
             else:
                 live[name] = value
-        return next(iter(landed.values()))
+        return landed[0]
+
+    def planes(kind, *gs):
+        return [(kind, s) for g in gs for s in groups[g] if s]
+
+    def rows(kind, *gs):
+        return ("y", kind, "own", gs)
 
     def across(kind, g):
         for s in groups[g]:
@@ -258,6 +267,10 @@
         launch(("y", kind, "own", gs), own, 2)
 
     def core(kind, *gs):
+        own = join([live[kind, "own", (g,)] for g in gs])
+        live[kind, "other", gs] = swap(own, 1)
+
+    def core_joined(kind, gs):
         live[kind, "other", gs] = swap(live[kind, "own", gs], 1)
 
     def ffn(*gs):
@@ -276,6 +289,7 @@
                 pltpu.VMEM((rows, hidden_width), BF16),
             ],
         )(*pieces, live["w", 0], live["w", 1], live["w", 2])
+        last.append(live["turned", gs])
 
     def cross(*gs):
         live["crossed", gs] = swap(live.pop(("send", gs)), 1)
@@ -285,6 +299,7 @@
         rows = keep.shape[0] // 2
         both = keep[rows:].astype(F32) + crossed[rows:].astype(F32)
         live["across", gs] = both.astype(BF16)
+        last.append(live["across", gs])
 
     def fold_row(*gs):
         launch(("fold", gs), live.pop(("across", gs)), 2)
@@ -339,89 +354,119 @@
         )(after(w_gate, live["C", experts - 1]), w_up, w_down)
         live.update({("w", i): value for i, value in enumerate(values)})
 
+    def grad(turned, pieces, earlier):
+        columns = {}
+        for i, gs in enumerate(turned):
+            at = 0
+            for half in ("own", "other"):
+                for side in range(2):
+                    for g in gs:
+                        columns[half, side, g] = (i, at)
+                        at += height
+        plan = []
+        for i, (half, gs) in enumerate(pieces):
+            row = 0
+            for parts in [gs] if gs in JOINED else [(g,) for g in gs]:
+                for side in range(2):
+                    for g in parts:
+                        where, at = columns[half, side, g]
+                        plan.append((where, at, len(turned) + i, row, height))
+                        row += height
+        total = sum(step[-1] for step in plan)
+        kind = F32 if earlier is None else BF16
+        return call(
+            functools.partial(grad_kernel, plan, 0 if earlier is None else 1),
+            24,
+            "grad",
+            out_shape=jax.ShapeDtypeStruct((1, hidden_width, width), kind),
+            in_specs=whole(len(turned) + len(pieces) + (earlier is not None)),
+            out_specs=whole(1)[0],
+            scratch_shapes=[
+                pltpu.VMEM((hidden_width, total), BF16),
+                pltpu.VMEM((total, width), BF16),
+            ],
+        )(
+            *([] if earlier is None else [earlier]),
+            *[live["turned", gs] for gs in turned],
+            *[live["C", half, gs] for half, gs in pieces],
+        )
+
     send_rows()
     if shifts > 1:
         across("N", 0)
-        land()
-    sync()
-    along("N", 0)
+        land(*planes("N", 0))
+    sync()
     for g in (1, 2):
         across("N", g)
+    along("N", 0)
     send_grads()
     if shifts > 1:
         across("C", 0)
-        land()
+        land(*planes("C", 0))
     along("C", 0)
     load()
-    land()
-    sync()
+    land(rows("N", 0))
+    sync()
+    core_joined("N", (0,))
+    land(*planes("N", 1, 2))
+    sync()
+    along("N", 1, 2)
     across("N", 3)
     across("C", 1)
-    along("N", 1, 2)
-    core("N", 0)
+    land(rows("C", 0))
+    sync()
     ffn(0)
     cross(0)
-    fold_core(land(), 0)
-    sync()
+    fold_core(land(*planes("N", 3), *planes("C", 1)), 0)
+    sync()
+    fold_row(0)
     across("C", 2)
+    land(rows("N", 1, 2))
+    sync()
     along("N", 3)
-    fold_row(0)
-    core("N", 1, 2)
+    core_joined("N", (1, 2))
     ffn(1, 2)
     cross(1, 2)
-    fold_core(land(), 1, 2)
-    sync()
+    land(("fold", (0,)))
+    sync()
+    along("C", 1)
+    fold_core(land(*planes("C", 2)), 1, 2)
+    sync()
+    fold_row(1, 2)
     across("C", 3)
-    fold_row(1, 2)
-    core("N", 3)
+    land(rows("N", 3))
+    sync()
+    core_joined("N", (3,))
     ffn(3)
     cross(3)
-    core("C", 0)
-    fold_core(land(), 3)
-    sync()
+    fold_core(land(rows("C", 1)), 3)
+    sync()
+    fold_row(3)
+    core("C", 0, 1)
+    land(*planes("C", 3))
+    sync()
+    land(("fold", (1, 2)))
+    sync()
+    along("C", 2, 3)
     if shifts > 1:
         back(0)
     back(1)
     back(2)
-    fold_row(3)
-    along("C", 1)
-    land()
+    land(("fold", (3,)))
     sync()
     back(3)
-    along("C", 2, 3)
-    core("C", 1)
-    land()
-    sync()
-    core("C", 2, 3)
-
-    places, at = {}, 0
-    turned = [(0,), (1, 2), (3,)]
-    for gs in turned:
-        for half in ("own", "other"):
-            for side in range(2):
-                for g in gs:
-                    places[half, side, g] = at
-                    at += height
-    pieces, plan = [], []
-    for gs in [(0,), (1,), (2, 3)]:
-        for half in ("own", "other"):
-            for side in range(2):
-                for i, g in enumerate(gs):
-                    start = (side * len(gs) + i) * height
-                    plan.append((len(pieces), start, height, places[half, side, g]))
-            pieces.append(live["C", half, gs])
-    grad_down = call(
-        functools.partial(grad_kernel, plan, len(turned)),
-        24,
-        "grad",
-        out_shape=jax.ShapeDtypeStruct((1, hidden_width, width), BF16),
-        in_specs=whole(len(turned) + len(pieces)),
-        out_specs=whole(1)[0],
-        scratch_shapes=[
-            pltpu.VMEM((hidden_width, at), BF16),
-            pltpu.VMEM((at, width), BF16),
-        ],
-    )(*[live["turned", gs] for gs in turned], *pieces)
+    first = grad([(0,), (1, 2)], [("own", (0,)), ("own", (1,)), ("other", (0, 1))], None)
+    live["first"] = first
+    last.append(first)
+    if shifts > 1:
+        land(*planes("R", 0))
+    land(*planes("R", 1, 2))
+    sync()
+    land(rows("C", 2, 3))
+    sync()
+    core_joined("C", (2, 3))
+    land(*planes("R", 3))
+    grad_down = grad([(1, 2), (3,)], [("own", (2, 3)), ("other", (2, 3))], live["first"])
     mixed = call(
         functools.partial(combine_kernel, experts),
         16,

time: 88.2 us -> 94.2 us (1.068)
  waiting for transfers between devices: 32.5 us -> 36.2 us
  starting transfers between devices: 25.1 us -> 26.4 us
    ppermute x27 -> x26, waiting for transfers between devices: 32.5 us -> 36.2 us  [swap(): lax.ppermute(value, 'expert', [(i, i ^ mask) for i in range(devices)])]
    ppermute x27 -> x26, starting transfers between devices: 25.1 us -> 26.4 us  [swap(): lax.ppermute(value, 'expert', [(i, i ^ mask) for i in range(devices)])]
    pallas_call x1 -> x2, Pallas kernels: 4.75 us -> 5.59 us  [grad(): call(functools.partial(grad_kernel, plan, 0 if earlier is None else 1), 2...]
    unnamed x24 -> x26, local copies, waits for them, and re-layouts: 10.2 us -> 10.3 us
  transfers between devices with their start and end apart: 27 -> 26, of which waited for: 11 -> 11; matrix products, arithmetic and copies ran while one was open for 1% -> 1% of each run, Pallas kernels for 14% -> 16%
where the time goes in v3:
time: 94.2 us; the launch traced here: 93.8 us
  waiting for transfers between devices  36.2 us (38%)
  starting transfers between devices  26.4 us (28%)
  Pallas kernels  19 us (20%)
  local copies, waits for them, and re-layouts  10.3 us (11%)
  between operations  1.05 us (1%)
    ppermute x26, waiting for transfers between devices, swap(): lax.ppermute(value, 'expert', [(i, i ^ mask) for i in range(devices)])  36.2 us
    ppermute x26, starting transfers between devices, swap(): lax.ppermute(value, 'expert', [(i, i ^ mask) for i in range(devices)])  26.4 us
    pallas_call x3, Pallas kernels, ffn(): call(functools.partial(ffn_kernel, len(pieces)), 24, 'ffn', out_shape=[ja...  10.3 us
    unnamed x26, local copies, waits for them, and re-layouts  10.3 us
    pallas_call x2, Pallas kernels, grad(): call(functools.partial(grad_kernel, plan, 0 if earlier is None else 1), 2...  5.59 us
  transfers between devices with their start and end apart: 26, of which 11 were waited for; matrix products, arithmetic and copies ran while one was open for 1% of the time, Pallas kernels for 16%

profile of v3, /device:TPU:0, one launch (start us, length us, event | category | flops | bytes accessed | tf_op | source)
XLA Modules:
  0.0 93.8 jit_solution(9932609726815693400)
XLA Ops:
  0.7 0.9 %copy-done.3 = bf16[128,1024]{1,0:T(8,128)(2,1)S(1)} copy-done((bf16[128,1024]{1,0:T(8,128)(2,1)S(1)}, bf16[128,1024]{1,0:T(8,128)(2,1)}, u32[]{:S(2)}) %copy-start.3) | copy-done | bytes 262168
  3.0 0.7 send_rows.1
  3.7 3.0 %collective-permute-start.2 = (bf16[96,1024]{1,0:T(8,128)(2,1)S(1)}, bf16[96,1024]{1,0:T(8,128)(2,1)S(1)}, u32[]{:S(2)}, u32[]{:S(2)}) collective-permute-start(bf16[96,1024]{1,0:T(8,128)(2,1)S(1)} %get-tuple-element.205), channel_id=1, source_target_pairs={{0,2},{1,3},{2,0},{3,1},{4,6},{5,7},{6,4},{7,5},{8,10},{9,11},{10,... | collective-permute-start | bytes 589832 | tf_op jit(solution)/shard_map/ppermute | solution.py:220
  6.7 1.6 %collective-permute-start = (bf16[96,1024]{1,0:T(8,128)(2,1)S(1)}, bf16[96,1024]{1,0:T(8,128)(2,1)S(1)}, u32[]{:S(2)}, u32[]{:S(2)}) collective-permute-start(bf16[96,1024]{1,0:T(8,128)(2,1)S(1)} %get-tuple-element.203), channel_id=1, source_target_pairs={{0,4},{1,5},{2,6},{3,7},{4,0},{5,1},{6,2},{7,3},{8,12},{9,13},{10,... | collective-permute-start | bytes 589832 | tf_op jit(solution)/shard_map/ppermute | solution.py:220
  8.3 2.6 %collective-permute-start.1 = (bf16[96,1024]{1,0:T(8,128)(2,1)S(1)}, bf16[96,1024]{1,0:T(8,128)(2,1)S(1)}, u32[]{:S(2)}, u32[]{:S(2)}) collective-permute-start(bf16[96,1024]{1,0:T(8,128)(2,1)S(1)} %get-tuple-element.204), channel_id=1, source_target_pairs={{0,8},{1,9},{2,10},{3,11},{4,12},{5,13},{6,14},{7,15},{8,0},{9,1},... | collective-permute-start | bytes 589832 | tf_op jit(solution)/shard_map/ppermute | solution.py:220
  10.9 0.9 %copy-done.5 = bf16[128,1024]{1,0:T(8,128)(2,1)S(1)} copy-done((bf16[128,1024]{1,0:T(8,128)(2,1)S(1)}, bf16[128,1024]{1,0:T(8,128)(2,1)}, u32[]{:S(2)}) %copy-start.5) | copy-done | bytes 262168
  14.3 1.6 %copy-done = bf16[1,1024,1024]{2,1,0:T(8,128)(2,1)S(1)} copy-done((bf16[1,1024,1024]{2,1,0:T(8,128)(2,1)S(1)}, bf16[1,1024,1024]{2,1,0:T(8,128)(2,1)}, u32[]{:S(2)}) %copy-start) | copy-done | bytes 2097176
  15.9 1.6 %copy-done.1 = bf16[1,1024,1024]{2,1,0:T(8,128)(2,1)S(1)} copy-done((bf16[1,1024,1024]{2,1,0:T(8,128)(2,1)S(1)}, bf16[1,1024,1024]{2,1,0:T(8,128)(2,1)}, u32[]{:S(2)}) %copy-start.1) | copy-done | bytes 2097176
  17.5 1.6 %copy-done.2 = bf16[1,1024,1024]{2,1,0:T(8,128)(2,1)S(1)} copy-done((bf16[1,1024,1024]{2,1,0:T(8,128)(2,1)S(1)}, bf16[1,1024,1024]{2,1,0:T(8,128)(2,1)}, u32[]{:S(2)}) %copy-start.2) | copy-done | bytes 2097176
  19.8 1.7 %collective-permute-done.3.refs_1_ = bf16[192,1024]{1,0:T(8,128)(2,1)S(1)} collective-permute-done((bf16[192,1024]{1,0:T(8,128)(2,1)S(1)}, bf16[192,1024]{1,0:T(8,128)(2,1)S(1)}, u32[]{:S(2)}, u32[]{:S(2)}) %collective-permute-start.3) | collective-permute-done | bytes 393248 | tf_op jit(solution)/shard_map/ppermute | solution.py:220
  22.4 1.6 %collective-permute-start.10 = (bf16[192,1024]{1,0:T(8,128)(2,1)S(1)}, bf16[192,1024]{1,0:T(8,128)(2,1)S(1)}, u32[]{:S(2)}, u32[]{:S(2)}) collective-permute-start(bf16[192,1024]{1,0:T(8,128)(2,1)S(1)} %constant_dynamic-update-slice_fusion), channel_id=1, source_target_pairs={{0,2},{1,3},{2,0},{3,1},{4,6},{5,7},{6,4},{7,5},{8,10},{9,11},{10,... | collective-permute-start | bytes 1179656 | tf_op jit(solution)/shard_map/ppermute | solution.py:220
  24.0 2.6 %ffn.3 = (bf16[1024,384]{1,0:T(8,128)(2,1)S(1)}, bf16[192,1024]{1,0:T(8,128)(2,1)S(1)}, bf16[192,1024]{1,0:T(8,128)(2,1)S(1)}) custom-call(bf16[192,1024]{1,0:T(8,128)(2,1)S(1)} %pad_maximum_fusion.3.refs_0_, bf16[192,1024]{1,0:T(8,128)(2,1)S(1)} %collective-permute-done.3.refs_1_, bf16[1024,1024]{1,0:T(8,128)(2,1)S(1)} %get-tuple-element.317.refs_2_, ...), custom_call_target="tpu_custom_call" | custom-call | tf_op jit(solution)/shard_map/ffn/pallas_call | solution.py:280
  26.7 4.4 %collective-permute-done.4.refs_0_ = bf16[96,1024]{1,0:T(8,128)(2,1)S(1)} collective-permute-done((bf16[96,1024]{1,0:T(8,128)(2,1)S(1)}, bf16[96,1024]{1,0:T(8,128)(2,1)S(1)}, u32[]{:S(2)}, u32[]{:S(2)}) %collective-permute-start.4) | collective-permute-done | bytes 196640 | tf_op jit(solution)/shard_map/ppermute | solution.py:220
  31.1 1.6 %collective-permute-done.5.refs_1_ = bf16[96,1024]{1,0:T(8,128)(2,1)S(1)} collective-permute-done((bf16[96,1024]{1,0:T(8,128)(2,1)S(1)}, bf16[96,1024]{1,0:T(8,128)(2,1)S(1)}, u32[]{:S(2)}, u32[]{:S(2)}) %collective-permute-start.5) | collective-permute-done | bytes 196640 | tf_op jit(solution)/shard_map/ppermute | solution.py:220
  33.2 1.6 %collective-permute-start.9 = (bf16[96,1024]{1,0:T(8,128)(2,1)S(1)}, bf16[96,1024]{1,0:T(8,128)(2,1)S(1)}, u32[]{:S(2)}, u32[]{:S(2)}) collective-permute-start(bf16[96,1024]{1,0:T(8,128)(2,1)S(1)} %add_convert_fusion.5), channel_id=1, source_target_pairs={{0,2},{1,3},{2,0},{3,1},{4,6},{5,7},{6,4},{7,5},{8,10},{9,11},{10,... | collective-permute-start | bytes 589832 | tf_op jit(solution)/shard_map/ppermute | solution.py:220
  34.8 3.5 %collective-permute-start.8 = (bf16[96,1024]{1,0:T(8,128)(2,1)S(1)}, bf16[96,1024]{1,0:T(8,128)(2,1)S(1)}, u32[]{:S(2)}, u32[]{:S(2)}) collective-permute-start(bf16[96,1024]{1,0:T(8,128)(2,1)S(1)} %get-tuple-element.259), channel_id=1, source_target_pairs={{0,8},{1,9},{2,10},{3,11},{4,12},{5,13},{6,14},{7,15},{8,0},{9,1},... | collective-permute-start | bytes 589832 | tf_op jit(solution)/shard_map/ppermute | solution.py:220
  38.8 5.1 %ffn.4 = (bf16[1024,768]{1,0:T(8,128)(2,1)S(1)}, bf16[384,1024]{1,0:T(8,128)(2,1)S(1)}, bf16[384,1024]{1,0:T(8,128)(2,1)S(1)}) custom-call(bf16[384,1024]{1,0:T(8,128)(2,1)S(1)} %pad_maximum_fusion.refs_0_, bf16[384,1024]{1,0:T(8,128)(2,1)S(1)} %collective-permute-done.11.refs_1_, bf16[1024,1024]{1,0:T(8,128)(2,1)S(1)} %get-tuple-element.317.refs_2_, ...), custom_call_target="tpu_custom_call" | custom-call | tf_op jit(solution)/shard_map/ffn/pallas_call | solution.py:280
  44.0 3.8 %collective-permute-done.8.refs_0_ = bf16[96,1024]{1,0:T(8,128)(2,1)S(1)} collective-permute-done((bf16[96,1024]{1,0:T(8,128)(2,1)S(1)}, bf16[96,1024]{1,0:T(8,128)(2,1)S(1)}, u32[]{:S(2)}, u32[]{:S(2)}) %collective-permute-start.8) | collective-permute-done | bytes 196640 | tf_op jit(solution)/shard_map/ppermute | solution.py:220
  48.7 2.4 %collective-permute-start.17 = (bf16[96,1024]{1,0:T(8,128)(2,1)S(1)}, bf16[96,1024]{1,0:T(8,128)(2,1)S(1)}, u32[]{:S(2)}, u32[]{:S(2)}) collective-permute-start(bf16[96,1024]{1,0:T(8,128)(2,1)S(1)} %get-tuple-element.303), channel_id=1, source_target_pairs={{0,12},{1,13},{2,14},{3,15},{4,8},{5,9},{6,10},{7,11},{8,4},{9,5},... | collective-permute-start | bytes 589832 | tf_op jit(solution)/shard_map/ppermute | solution.py:220
  51.0 1.5 %collective-permute-start.19 = (bf16[192,1024]{1,0:T(8,128)(2,1)S(1)}, bf16[192,1024]{1,0:T(8,128)(2,1)S(1)}, u32[]{:S(2)}, u32[]{:S(2)}) collective-permute-start(bf16[192,1024]{1,0:T(8,128)(2,1)S(1)} %add_convert_fusion.1), channel_id=1, source_target_pairs={{0,2},{1,3},{2,0},{3,1},{4,6},{5,7},{6,4},{7,5},{8,10},{9,11},{10,... | collective-permute-start | bytes 1179656 | tf_op jit(solution)/shard_map/ppermute | solution.py:220
  52.6 2.6 %ffn.5 = (bf16[1024,384]{1,0:T(8,128)(2,1)S(1)}, bf16[192,1024]{1,0:T(8,128)(2,1)S(1)}, bf16[192,1024]{1,0:T(8,128)(2,1)S(1)}) custom-call(bf16[192,1024]{1,0:T(8,128)(2,1)S(1)} %pad_maximum_fusion.5.refs_0_, bf16[192,1024]{1,0:T(8,128)(2,1)S(1)} %collective-permute-done.14.refs_1_, bf16[1024,1024]{1,0:T(8,128)(2,1)S(1)} %get-tuple-element.317.refs_2_, ...), custom_call_target="tpu_custom_call" | custom-call | tf_op jit(solution)/shard_map/ffn/pallas_call | solution.py:280
  55.9 1.7 %collective-permute-done.15 = bf16[192,1024]{1,0:T(8,128)(2,1)S(1)} collective-permute-done((bf16[192,1024]{1,0:T(8,128)(2,1)S(1)}, bf16[192,1024]{1,0:T(8,128)(2,1)S(1)}, u32[]{:S(2)}, u32[]{:S(2)}) %collective-permute-start.15) | collective-permute-done | bytes 393248 | tf_op jit(solution)/shard_map/ppermute | solution.py:220
  57.7 6.2 %collective-permute-done.19.refs_0_ = bf16[192,1024]{1,0:T(8,128)(2,1)S(1)} collective-permute-done((bf16[192,1024]{1,0:T(8,128)(2,1)S(1)}, bf16[192,1024]{1,0:T(8,128)(2,1)S(1)}, u32[]{:S(2)}, u32[]{:S(2)}) %collective-permute-start.19) | collective-permute-done | bytes 393248 | tf_op jit(solution)/shard_map/ppermute | solution.py:220
  64.5 5.8 %collective-permute-done.20.refs_0_ = bf16[96,1024]{1,0:T(8,128)(2,1)S(1)} collective-permute-done((bf16[96,1024]{1,0:T(8,128)(2,1)S(1)}, bf16[96,1024]{1,0:T(8,128)(2,1)S(1)}, u32[]{:S(2)}, u32[]{:S(2)}) %collective-permute-start.20) | collective-permute-done | bytes 196640 | tf_op jit(solution)/shard_map/ppermute | solution.py:220
  70.7 2.9 %collective-permute-start.22 = (bf16[96,1024]{1,0:T(8,128)(2,1)S(1)}, bf16[96,1024]{1,0:T(8,128)(2,1)S(1)}, u32[]{:S(2)}, u32[]{:S(2)}) collective-permute-start(bf16[96,1024]{1,0:T(8,128)(2,1)S(1)} %get-tuple-element.368), channel_id=1, source_target_pairs={{0,8},{1,9},{2,10},{3,11},{4,12},{5,13},{6,14},{7,15},{8,0},{9,1},... | collective-permute-start | bytes 589832 | tf_op jit(solution)/shard_map/ppermute | solution.py:220
  74.3 1.5 %collective-permute-start.24 = (bf16[96,1024]{1,0:T(8,128)(2,1)S(1)}, bf16[96,1024]{1,0:T(8,128)(2,1)S(1)}, u32[]{:S(2)}, u32[]{:S(2)}) collective-permute-start(bf16[96,1024]{1,0:T(8,128)(2,1)S(1)} %add_convert_fusion.2), channel_id=1, source_target_pairs={{0,12},{1,13},{2,14},{3,15},{4,8},{5,9},{6,10},{7,11},{8,4},{9,5},... | collective-permute-start | bytes 589832 | tf_op jit(solution)/shard_map/ppermute | solution.py:220
  75.8 2.0 %grad.2.refs_0_ = f32[1,1024,1024]{2,1,0:T(8,128)S(1)} custom-call(bf16[1024,384]{1,0:T(8,128)(2,1)S(1)} %get-tuple-element.376.refs_0_, bf16[1024,768]{1,0:T(8,128)(2,1)S(1)} %get-tuple-element.401.refs_1_, bf16[192,1024]{1,0:T(8,128)(2,1)S(1)} %pad_maximum_fusion.4.refs_2_, bf16[192,1024]{1,0:T(8,128)(2,1)S(1)} %pad_maximum_fusion.6.refs_3_, ...), custom_call_target="tpu_custom_call" | custom-call | tf_op jit(solution)/shard_map/grad/pallas_call | solution.py:377
  77.7 1.6 %collective-permute-done.21.refs_0_ = bf16[96,1024]{1,0:T(8,128)(2,1)S(1)} collective-permute-done((bf16[96,1024]{1,0:T(8,128)(2,1)S(1)}, bf16[96,1024]{1,0:T(8,128)(2,1)S(1)}, u32[]{:S(2)}, u32[]{:S(2)}) %collective-permute-start.21) | collective-permute-done | bytes 196640 | tf_op jit(solution)/shard_map/ppermute | solution.py:220
  79.3 8.4 %collective-permute-done.22.refs_1_ = bf16[96,1024]{1,0:T(8,128)(2,1)S(1)} collective-permute-done((bf16[96,1024]{1,0:T(8,128)(2,1)S(1)}, bf16[96,1024]{1,0:T(8,128)(2,1)S(1)}, u32[]{:S(2)}, u32[]{:S(2)}) %collective-permute-start.22) | collective-permute-done | bytes 196640 | tf_op jit(solution)/shard_map/ppermute | solution.py:220
  87.9 0.8 copy-done.4
  88.8 1.4 %combine.1 = bf16[128,1024]{1,0:T(8,128)(2,1)} custom-call(s32[1]{0:T(128)} %bitcast.plane_ref, bf16[128,1024]{1,0:T(8,128)(2,1)S(1)} %copy-done.4, s32[2,128]{1,0:T(2,128)S(1)} %bitcast.6, s32[2,128]{1,0:T(2,128)S(1)} %bitcast.9, bf16[96,1024]{1,0:T(8,128)(2,1)S(1)} %add_convert_fusion.4.refs_0_, bf16[96,1024]{1,0:T(8,128)(2,1)S(1)} %get-tuple-element.397.refs_1_, ...), custom_call_target="tpu_custom_call" | custom-call | tf_op jit(solution)/shard_map/combine/pallas_call | solution.py:470
  90.2 3.6 %grad.3 = bf16[1,1024,1024]{2,1,0:T(8,128)(2,1)} custom-call(f32[1,1024,1024]{2,1,0:T(8,128)S(1)} %grad.2.refs_0_, bf16[1024,768]{1,0:T(8,128)(2,1)S(1)} %get-tuple-element.401.refs_1_, bf16[1024,384]{1,0:T(8,128)(2,1)S(1)} %get-tuple-element.402.refs_2_, bf16[384,1024]{1,0:T(8,128)(2,1)S(1)} %pad_maximum_fusion.2.refs_3_, ...), custom_call_target="tpu_custom_call" | custom-call | tf_op jit(solution)/shard_map/grad/pallas_call | solution.py:377
  (86 shorter events, 10.1 us)
Async XLA Ops:
  0.6 1.0 %copy-start.3 = (bf16[128,1024]{1,0:T(8,128)(2,1)S(1)}, bf16[128,1024]{1,0:T(8,128)(2,1)}, u32[]{:S(2)}) copy-start(bf16[128,1024]{1,0:T(8,128)(2,1)} %tokens_ref.1) | copy-start | bytes 786436
  3.7 15.9 %collective-permute-start.2 = (bf16[96,1024]{1,0:T(8,128)(2,1)S(1)}, bf16[96,1024]{1,0:T(8,128)(2,1)S(1)}, u32[]{:S(2)}, u32[]{:S(2)}) collective-permute-start(bf16[96,1024]{1,0:T(8,128)(2,1)S(1)} %get-tuple-element.205), channel_id=1, source_target_pairs={{0,2},{1,3},{2,0},{3,1},{4,6},{5,7},{6,4},{7,5},{8,10},{9,11},{10,... | collective-permute-start | bytes 589832 | tf_op jit(solution)/shard_map/ppermute | solution.py:220
  6.7 13.0 %collective-permute-start = (bf16[96,1024]{1,0:T(8,128)(2,1)S(1)}, bf16[96,1024]{1,0:T(8,128)(2,1)S(1)}, u32[]{:S(2)}, u32[]{:S(2)}) collective-permute-start(bf16[96,1024]{1,0:T(8,128)(2,1)S(1)} %get-tuple-element.203), channel_id=1, source_target_pairs={{0,4},{1,5},{2,6},{3,7},{4,0},{5,1},{6,2},{7,3},{8,12},{9,13},{10,... | collective-permute-start | bytes 589832 | tf_op jit(solution)/shard_map/ppermute | solution.py:220
  8.3 11.5 %collective-permute-start.1 = (bf16[96,1024]{1,0:T(8,128)(2,1)S(1)}, bf16[96,1024]{1,0:T(8,128)(2,1)S(1)}, u32[]{:S(2)}, u32[]{:S(2)}) collective-permute-start(bf16[96,1024]{1,0:T(8,128)(2,1)S(1)} %get-tuple-element.204), channel_id=1, source_target_pairs={{0,8},{1,9},{2,10},{3,11},{4,12},{5,13},{6,14},{7,15},{8,0},{9,1},... | collective-permute-start | bytes 589832 | tf_op jit(solution)/shard_map/ppermute | solution.py:220
  10.9 0.9 %copy-start.5 = (bf16[128,1024]{1,0:T(8,128)(2,1)S(1)}, bf16[128,1024]{1,0:T(8,128)(2,1)}, u32[]{:S(2)}) copy-start(bf16[128,1024]{1,0:T(8,128)(2,1)} %cot_hbm) | copy-start | bytes 786436
  13.8 6.0 %collective-permute-start.6 = (bf16[96,1024]{1,0:T(8,128)(2,1)S(1)}, bf16[96,1024]{1,0:T(8,128)(2,1)S(1)}, u32[]{:S(2)}, u32[]{:S(2)}) collective-permute-start(bf16[96,1024]{1,0:T(8,128)(2,1)S(1)} %get-tuple-element.241), channel_id=1, source_target_pairs={{0,2},{1,3},{2,0},{3,1},{4,6},{5,7},{6,4},{7,5},{8,10},{9,11},{10,... | collective-permute-start | bytes 589832 | tf_op jit(solution)/shard_map/ppermute | solution.py:220
  14.3 1.6 %copy-start = (bf16[1,1024,1024]{2,1,0:T(8,128)(2,1)S(1)}, bf16[1,1024,1024]{2,1,0:T(8,128)(2,1)}, u32[]{:S(2)}) copy-start(bf16[1,1024,1024]{2,1,0:T(8,128)(2,1)} %refs_0_) | copy-start | bytes 6291460
  15.9 1.6 %copy-start.1 = (bf16[1,1024,1024]{2,1,0:T(8,128)(2,1)S(1)}, bf16[1,1024,1024]{2,1,0:T(8,128)(2,1)}, u32[]{:S(2)}) copy-start(bf16[1,1024,1024]{2,1,0:T(8,128)(2,1)} %refs_1_.1) | copy-start | bytes 6291460
  17.5 1.6 %copy-start.2 = (bf16[1,1024,1024]{2,1,0:T(8,128)(2,1)S(1)}, bf16[1,1024,1024]{2,1,0:T(8,128)(2,1)}, u32[]{:S(2)}) copy-start(bf16[1,1024,1024]{2,1,0:T(8,128)(2,1)} %refs_2_.1) | copy-start | bytes 6291460
  19.6 1.8 %collective-permute-start.3 = (bf16[192,1024]{1,0:T(8,128)(2,1)S(1)}, bf16[192,1024]{1,0:T(8,128)(2,1)S(1)}, u32[]{:S(2)}, u32[]{:S(2)}) collective-permute-start(bf16[192,1024]{1,0:T(8,128)(2,1)S(1)} %pad_maximum_fusion.3.refs_0_), channel_id=1, source_target_pairs={{0,1},{1,0},{2,3},{3,2},{4,5},{5,4},{6,7},{7,6},{8,9},{9,8},{10,11... | collective-permute-start | bytes 1179656 | tf_op jit(solution)/shard_map/ppermute | solution.py:220
  21.4 9.7 %collective-permute-start.4 = (bf16[96,1024]{1,0:T(8,128)(2,1)S(1)}, bf16[96,1024]{1,0:T(8,128)(2,1)S(1)}, u32[]{:S(2)}, u32[]{:S(2)}) collective-permute-start(bf16[96,1024]{1,0:T(8,128)(2,1)S(1)} %get-tuple-element.229), channel_id=1, source_target_pairs={{0,12},{1,13},{2,14},{3,15},{4,8},{5,9},{6,10},{7,11},{8,4},{9,5},... | collective-permute-start | bytes 589832 | tf_op jit(solution)/shard_map/ppermute | solution.py:220
  22.1 10.7 %collective-permute-start.5 = (bf16[96,1024]{1,0:T(8,128)(2,1)S(1)}, bf16[96,1024]{1,0:T(8,128)(2,1)S(1)}, u32[]{:S(2)}, u32[]{:S(2)}) collective-permute-start(bf16[96,1024]{1,0:T(8,128)(2,1)S(1)} %get-tuple-element.230), channel_id=1, source_target_pairs={{0,4},{1,5},{2,6},{3,7},{4,0},{5,1},{6,2},{7,3},{8,12},{9,13},{10,... | collective-permute-start | bytes 589832 | tf_op jit(solution)/shard_map/ppermute | solution.py:220
  22.4 10.7 %collective-permute-start.10 = (bf16[192,1024]{1,0:T(8,128)(2,1)S(1)}, bf16[192,1024]{1,0:T(8,128)(2,1)S(1)}, u32[]{:S(2)}, u32[]{:S(2)}) collective-permute-start(bf16[192,1024]{1,0:T(8,128)(2,1)S(1)} %constant_dynamic-update-slice_fusion), channel_id=1, source_target_pairs={{0,2},{1,3},{2,0},{3,1},{4,6},{5,7},{6,4},{7,5},{8,10},{9,11},{10,... | collective-permute-start | bytes 1179656 | tf_op jit(solution)/shard_map/ppermute | solution.py:220
  26.7 6.1 %collective-permute-start.7 = (bf16[192,1024]{1,0:T(8,128)(2,1)S(1)}, bf16[192,1024]{1,0:T(8,128)(2,1)S(1)}, u32[]{:S(2)}, u32[]{:S(2)}) collective-permute-start(bf16[192,1024]{1,0:T(8,128)(2,1)S(1)} %get-tuple-element.257), channel_id=1, source_target_pairs={{0,1},{1,0},{2,3},{3,2},{4,5},{5,4},{6,7},{7,6},{8,9},{9,8},{10,11... | collective-permute-start | bytes 1179656 | tf_op jit(solution)/shard_map/ppermute | solution.py:220
  33.1 5.7 %collective-permute-start.11 = (bf16[384,1024]{1,0:T(8,128)(2,1)S(1)}, bf16[384,1024]{1,0:T(8,128)(2,1)S(1)}, u32[]{:S(2)}, u32[]{:S(2)}) collective-permute-start(bf16[384,1024]{1,0:T(8,128)(2,1)S(1)} %pad_maximum_fusion.refs_0_), channel_id=1, source_target_pairs={{0,1},{1,0},{2,3},{3,2},{4,5},{5,4},{6,7},{7,6},{8,9},{9,8},{10,11... | collective-permute-start | bytes 2359304 | tf_op jit(solution)/shard_map/ppermute | solution.py:220
  33.2 10.6 %collective-permute-start.9 = (bf16[96,1024]{1,0:T(8,128)(2,1)S(1)}, bf16[96,1024]{1,0:T(8,128)(2,1)S(1)}, u32[]{:S(2)}, u32[]{:S(2)}) collective-permute-start(bf16[96,1024]{1,0:T(8,128)(2,1)S(1)} %add_convert_fusion.5), channel_id=1, source_target_pairs={{0,2},{1,3},{2,0},{3,1},{4,6},{5,7},{6,4},{7,5},{8,10},{9,11},{10,... | collective-permute-start | bytes 589832 | tf_op jit(solution)/shard_map/ppermute | solution.py:220
  34.8 12.9 %collective-permute-start.8 = (bf16[96,1024]{1,0:T(8,128)(2,1)S(1)}, bf16[96,1024]{1,0:T(8,128)(2,1)S(1)}, u32[]{:S(2)}, u32[]{:S(2)}) collective-permute-start(bf16[96,1024]{1,0:T(8,128)(2,1)S(1)} %get-tuple-element.259), channel_id=1, source_target_pairs={{0,8},{1,9},{2,10},{3,11},{4,12},{5,13},{6,14},{7,15},{8,0},{9,1},... | collective-permute-start | bytes 589832 | tf_op jit(solution)/shard_map/ppermute | solution.py:220
  38.3 9.7 %collective-permute-start.13 = (bf16[96,1024]{1,0:T(8,128)(2,1)S(1)}, bf16[96,1024]{1,0:T(8,128)(2,1)S(1)}, u32[]{:S(2)}, u32[]{:S(2)}) collective-permute-start(bf16[96,1024]{1,0:T(8,128)(2,1)S(1)} %get-tuple-element.314), channel_id=1, source_target_pairs={{0,2},{1,3},{2,0},{3,1},{4,6},{5,7},{6,4},{7,5},{8,10},{9,11},{10,... | collective-permute-start | bytes 589832 | tf_op jit(solution)/shard_map/ppermute | solution.py:220
  43.9 3.9 %collective-permute-start.12 = (bf16[384,1024]{1,0:T(8,128)(2,1)S(1)}, bf16[384,1024]{1,0:T(8,128)(2,1)S(1)}, u32[]{:S(2)}, u32[]{:S(2)}) collective-permute-start(bf16[384,1024]{1,0:T(8,128)(2,1)S(1)} %get-tuple-element.286), channel_id=1, source_target_pairs={{0,1},{1,0},{2,3},{3,2},{4,5},{5,4},{6,7},{7,6},{8,9},{9,8},{10,11... | collective-permute-start | bytes 2359304 | tf_op jit(solution)/shard_map/ppermute | solution.py:220
  48.0 4.5 %collective-permute-start.14 = (bf16[192,1024]{1,0:T(8,128)(2,1)S(1)}, bf16[192,1024]{1,0:T(8,128)(2,1)S(1)}, u32[]{:S(2)}, u32[]{:S(2)}) collective-permute-start(bf16[192,1024]{1,0:T(8,128)(2,1)S(1)} %pad_maximum_fusion.5.refs_0_), channel_id=1, source_target_pairs={{0,1},{1,0},{2,3},{3,2},{4,5},{5,4},{6,7},{7,6},{8,9},{9,8},{10,11... | collective-permute-start | bytes 1179656 | tf_op jit(solution)/shard_map/ppermute | solution.py:220
  48.1 7.8 %collective-permute-start.16 = (bf16[96,1024]{1,0:T(8,128)(2,1)S(1)}, bf16[96,1024]{1,0:T(8,128)(2,1)S(1)}, u32[]{:S(2)}, u32[]{:S(2)}) collective-permute-start(bf16[96,1024]{1,0:T(8,128)(2,1)S(1)} %get-tuple-element.330), channel_id=1, source_target_pairs={{0,2},{1,3},{2,0},{3,1},{4,6},{5,7},{6,4},{7,5},{8,10},{9,11},{10,... | collective-permute-start | bytes 589832 | tf_op jit(solution)/shard_map/ppermute | solution.py:220
  48.7 9.0 %collective-permute-start.17 = (bf16[96,1024]{1,0:T(8,128)(2,1)S(1)}, bf16[96,1024]{1,0:T(8,128)(2,1)S(1)}, u32[]{:S(2)}, u32[]{:S(2)}) collective-permute-start(bf16[96,1024]{1,0:T(8,128)(2,1)S(1)} %get-tuple-element.303), channel_id=1, source_target_pairs={{0,12},{1,13},{2,14},{3,15},{4,8},{5,9},{6,10},{7,11},{8,4},{9,5},... | collective-permute-start | bytes 589832 | tf_op jit(solution)/shard_map/ppermute | solution.py:220
  51.0 12.8 %collective-permute-start.19 = (bf16[192,1024]{1,0:T(8,128)(2,1)S(1)}, bf16[192,1024]{1,0:T(8,128)(2,1)S(1)}, u32[]{:S(2)}, u32[]{:S(2)}) collective-permute-start(bf16[192,1024]{1,0:T(8,128)(2,1)S(1)} %add_convert_fusion.1), channel_id=1, source_target_pairs={{0,2},{1,3},{2,0},{3,1},{4,6},{5,7},{6,4},{7,5},{8,10},{9,11},{10,... | collective-permute-start | bytes 1179656 | tf_op jit(solution)/shard_map/ppermute | solution.py:220
  55.9 1.7 %collective-permute-start.15 = (bf16[192,1024]{1,0:T(8,128)(2,1)S(1)}, bf16[192,1024]{1,0:T(8,128)(2,1)S(1)}, u32[]{:S(2)}, u32[]{:S(2)}) collective-permute-start(bf16[192,1024]{1,0:T(8,128)(2,1)S(1)} %get-tuple-element.329), channel_id=1, source_target_pairs={{0,1},{1,0},{2,3},{3,2},{4,5},{5,4},{6,7},{7,6},{8,9},{9,8},{10,11... | collective-permute-start | bytes 1179656 | tf_op jit(solution)/shard_map/ppermute | solution.py:220
  63.9 6.5 %collective-permute-start.20 = (bf16[96,1024]{1,0:T(8,128)(2,1)S(1)}, bf16[96,1024]{1,0:T(8,128)(2,1)S(1)}, u32[]{:S(2)}, u32[]{:S(2)}) collective-permute-start(bf16[96,1024]{1,0:T(8,128)(2,1)S(1)} %add_convert_fusion.3), channel_id=1, source_target_pairs={{0,2},{1,3},{2,0},{3,1},{4,6},{5,7},{6,4},{7,5},{8,10},{9,11},{10,... | collective-permute-start | bytes 589832 | tf_op jit(solution)/shard_map/ppermute | solution.py:220
  64.4 5.9 %collective-permute-start.18 = (bf16[384,1024]{1,0:T(8,128)(2,1)S(1)}, bf16[384,1024]{1,0:T(8,128)(2,1)S(1)}, u32[]{:S(2)}, u32[]{:S(2)}) collective-permute-start(bf16[384,1024]{1,0:T(8,128)(2,1)S(1)} %pad_maximum_fusion.1), channel_id=1, source_target_pairs={{0,1},{1,0},{2,3},{3,2},{4,5},{5,4},{6,7},{7,6},{8,9},{9,8},{10,11... | collective-permute-start | bytes 2359304 | tf_op jit(solution)/shard_map/ppermute | solution.py:220
  70.6 8.8 %collective-permute-start.21 = (bf16[96,1024]{1,0:T(8,128)(2,1)S(1)}, bf16[96,1024]{1,0:T(8,128)(2,1)S(1)}, u32[]{:S(2)}, u32[]{:S(2)}) collective-permute-start(bf16[96,1024]{1,0:T(8,128)(2,1)S(1)} %get-tuple-element.367), channel_id=1, source_target_pairs={{0,4},{1,5},{2,6},{3,7},{4,0},{5,1},{6,2},{7,3},{8,12},{9,13},{10,... | collective-permute-start | bytes 589832 | tf_op jit(solution)/shard_map/ppermute | solution.py:220
  70.7 17.1 %collective-permute-start.22 = (bf16[96,1024]{1,0:T(8,128)(2,1)S(1)}, bf16[96,1024]{1,0:T(8,128)(2,1)S(1)}, u32[]{:S(2)}, u32[]{:S(2)}) collective-permute-start(bf16[96,1024]{1,0:T(8,128)(2,1)S(1)} %get-tuple-element.368), channel_id=1, source_target_pairs={{0,8},{1,9},{2,10},{3,11},{4,12},{5,13},{6,14},{7,15},{8,0},{9,1},... | collective-permute-start | bytes 589832 | tf_op jit(solution)/shard_map/ppermute | solution.py:220
  73.6 14.1 %collective-permute-start.23 = (bf16[192,1024]{1,0:T(8,128)(2,1)S(1)}, bf16[192,1024]{1,0:T(8,128)(2,1)S(1)}, u32[]{:S(2)}, u32[]{:S(2)}) collective-permute-start(bf16[192,1024]{1,0:T(8,128)(2,1)S(1)} %constant_dynamic-update-slice_fusion.2), channel_id=1, source_target_pairs={{0,2},{1,3},{2,0},{3,1},{4,6},{5,7},{6,4},{7,5},{8,10},{9,11},{10,... | collective-permute-start | bytes 1179656 | tf_op jit(solution)/shard_map/ppermute | solution.py:220
  74.3 13.7 %collective-permute-start.24 = (bf16[96,1024]{1,0:T(8,128)(2,1)S(1)}, bf16[96,1024]{1,0:T(8,128)(2,1)S(1)}, u32[]{:S(2)}, u32[]{:S(2)}) collective-permute-start(bf16[96,1024]{1,0:T(8,128)(2,1)S(1)} %add_convert_fusion.2), channel_id=1, source_target_pairs={{0,12},{1,13},{2,14},{3,15},{4,8},{5,9},{6,10},{7,11},{8,4},{9,5},... | collective-permute-start | bytes 589832 | tf_op jit(solution)/shard_map/ppermute | solution.py:220
  87.8 1.0 %copy-start.4 = (bf16[128,1024]{1,0:T(8,128)(2,1)S(1)}, bf16[128,1024]{1,0:T(8,128)(2,1)}, u32[]{:S(2)}) copy-start(bf16[128,1024]{1,0:T(8,128)(2,1)} %tokens_ref.1) | copy-start | bytes 786436
  87.8 2.4 %collective-permute-start.25 = (bf16[384,1024]{1,0:T(8,128)(2,1)S(1)}, bf16[384,1024]{1,0:T(8,128)(2,1)S(1)}, u32[]{:S(2)}, u32[]{:S(2)}) collective-permute-start(bf16[384,1024]{1,0:T(8,128)(2,1)S(1)} %pad_maximum_fusion.2.refs_3_), channel_id=1, source_target_pairs={{0,1},{1,0},{2,3},{3,2},{4,5},{5,4},{6,7},{7,6},{8,9},{9,8},{10,11... | collective-permute-start | bytes 2359304 | tf_op jit(solution)/shard_map/ppermute | solution.py:220
  (6 other events, 4.6 us)

commit v4 on v0

v4 whole, which is shorter than its diff:
```python
import functools

import jax
import jax.numpy as jnp
from jax import lax
from jax.experimental import pallas as pl
from jax.experimental.pallas import tpu as pltpu
from jax.sharding import PartitionSpec as P

HSPLIT = 4
TILE = 256
PER_STEP = 4
F32 = jnp.float32
BF16 = jnp.bfloat16
OVER_ROWS = (((0,), (0,)), ((), ()))


def whole(count):
    return [pl.BlockSpec(memory_space=pltpu.VMEM)] * count


def call(kernel, mib, name, flops, **keywords):
    return pl.pallas_call(
        kernel,
        compiler_params=pltpu.CompilerParams(vmem_limit_bytes=mib << 20),
        cost_estimate=pl.CostEstimate(flops=flops, bytes_accessed=4 << 20, transcendentals=0),
        name=name,
        **keywords,
    )


def placing_of(meta, expert, capacity):
    rows = meta.shape[1]
    top = meta.shape[0] // 2
    routes, numerators = meta[:top], meta[top:].astype(F32)
    named = (routes == expert).astype(F32)
    member = jnp.sum(named, 0, keepdims=True)
    gates = numerators / jnp.sum(numerators, 0, keepdims=True)
    gate = jnp.sum(named * gates, 0, keepdims=True)
    first = lax.broadcasted_iota(jnp.int32, (rows, rows), 0)
    second = lax.broadcasted_iota(jnp.int32, (rows, rows), 1)
    upto = (first <= second).astype(F32).astype(BF16)
    count = jnp.dot(
        jnp.broadcast_to(member, (16, rows)).astype(BF16), upto, preferred_element_type=F32
    )[:1]
    place = (member * count).astype(jnp.int32) - 1
    slots = lax.broadcasted_iota(jnp.int32, (capacity, rows), 0)
    placing = (slots == place).astype(F32)
    return placing.astype(BF16), jnp.sum(placing * gate, -1, keepdims=True)


def normed_kernel(tokens_ref, gain_ref, out_ref):
    frames = tokens_ref[...].astype(F32)
    inverse = lax.rsqrt(jnp.mean(frames * frames, -1, keepdims=True) + 1e-06)
    out_ref[...] = (frames * inverse * gain_ref[...]).astype(BF16)


def ffn_kernel(
    capacity, expert_ref, meta_ref, frames_ref, gate_ref, up_ref, down_ref, turned_ref, out_ref, *scratch
):
    rows_ref, hidden_ref, value_ref = scratch
    block = meta_ref.shape[2]
    height = PER_STEP * capacity

    @pl.loop(0, meta_ref.shape[0] // PER_STEP)
    def _(step):
        placings = [
            placing_of(meta_ref[step * PER_STEP + b], expert_ref[0], capacity)
            for b in range(PER_STEP)
        ]
        for b, (placing, _) in enumerate(placings):
            at = pl.multiple_of((step * PER_STEP + b) * block, block)
            rows_ref[b * capacity : (b + 1) * capacity, :] = jnp.dot(
                placing, frames_ref[pl.ds(at, block), :], preferred_element_type=F32
            ).astype(BF16)
        rows = rows_ref[...]
        for j in range(gate_ref.shape[2] // TILE):
            columns = slice(j * TILE, (j + 1) * TILE)
            pre_gate = jnp.dot(rows, gate_ref[0, :, columns], preferred_element_type=F32)
            pre_up = jnp.dot(rows, up_ref[0, :, columns], preferred_element_type=F32)
            hidden = pre_gate * lax.logistic(pre_gate) * pre_up
            hidden_ref[:, columns] = hidden.astype(BF16)
            at = pl.multiple_of(step * height, 128)
            turned_ref[columns, pl.ds(at, height)] = hidden.T.astype(BF16)
        for j in range(down_ref.shape[2] // TILE):
            columns = slice(j * TILE, (j + 1) * TILE)
            value_ref[...] = jnp.dot(
                hidden_ref[...], down_ref[0, :, columns], preferred_element_type=F32
            )
            for b, (placing, gate) in enumerate(placings):
                at = pl.multiple_of((step * PER_STEP + b) * block, block)
                value = (value_ref[b * capacity : (b + 1) * capacity, :] * gate).astype(BF16)
                out_ref[pl.ds(at, block), columns] = lax.dot_general(
                    placing, value, OVER_ROWS, preferred_element_type=F32
                ).astype(BF16)


def grad_kernel(capacity, expert_ref, meta_ref, cot_ref, turned_ref, out_ref, rows_ref):
    block = meta_ref.shape[2]

    @pl.loop(0, meta_ref.shape[0])
    def _(b):
        placing, gate = placing_of(meta_ref[b], expert_ref[0], capacity)
        at = pl.multiple_of(b * block, block)
        picked = jnp.dot(placing, cot_ref[pl.ds(at, block), :], preferred_element_type=F32)
        to = pl.multiple_of(b * capacity, 16)
        rows_ref[pl.ds(to, capacity), :] = (picked * gate).astype(BF16)

    for j in range(out_ref.shape[2] // TILE):
        columns = slice(j * TILE, (j + 1) * TILE)
        out_ref[0, :, columns] = jnp.dot(
            turned_ref[...], rows_ref[:, columns], preferred_element_type=F32
        ).astype(BF16)


def on_device(tokens, cotangent, routes, gate_nums, gain, w_gate, w_up, w_down):
    devices = lax.axis_size("expert")
    experts = devices // HSPLIT
    block, width = tokens.shape
    hidden_width = w_gate.shape[2]
    top_count = routes.shape[1]
    capacity = HSPLIT * (3 * top_count * block // (2 * experts * HSPLIT))
    capacity = -(-capacity // 32) * 32
    rows = devices * capacity
    expert = (lax.axis_index("expert") // HSPLIT).astype(jnp.int32).reshape(1)
    scalar = pl.BlockSpec(memory_space=pltpu.SMEM)

    meta = jnp.concatenate([routes.T, gate_nums.T], 0)[None]
    normed = call(
        normed_kernel,
        16,
        "normed",
        0,
        out_shape=jax.ShapeDtypeStruct(tokens.shape, BF16),
        in_specs=whole(2),
        out_specs=whole(1)[0],
    )(tokens, gain.reshape(1, -1))
    meta = lax.all_gather(meta, "expert", axis=0, tiled=True)
    frames = lax.all_gather(normed, "expert", axis=0, tiled=True)
    cots = lax.all_gather(cotangent, "expert", axis=0, tiled=True)
    turned, dense = call(
        functools.partial(ffn_kernel, capacity),
        40,
        "ffn",
        6 * rows * width * hidden_width,
        out_shape=[
            jax.ShapeDtypeStruct((hidden_width, rows), BF16),
            jax.ShapeDtypeStruct((devices * block, width), BF16),
        ],
        in_specs=[scalar] + whole(5),
        out_specs=whole(2),
        scratch_shapes=[
            pltpu.VMEM((PER_STEP * capacity, width), BF16),
            pltpu.VMEM((PER_STEP * capacity, hidden_width), BF16),
            pltpu.VMEM((PER_STEP * capacity, TILE), F32),
        ],
    )(expert, meta, frames, w_gate, w_up, w_down)
    branch = lax.psum_scatter(dense, "expert", scatter_dimension=0, tiled=True)
    grad_down = call(
        functools.partial(grad_kernel, capacity),
        40,
        "grad",
        2 * rows * width * hidden_width,
        out_shape=jax.ShapeDtypeStruct((1, hidden_width, width), BF16),
        in_specs=[scalar] + whole(3),
        out_specs=whole(1)[0],
        scratch_shapes=[pltpu.VMEM((rows, width), BF16)],
    )(expert, meta, cots, turned)
    mixed = (tokens.astype(F32) + branch.astype(F32)).astype(BF16)
    return (mixed, grad_down)


def solution(mesh):
    placed = (
        P(("group", "expert"), None),
        P(("group", "expert"), None),
        P(("group", "expert"), None),
        P(("group", "expert"), None),
        P(),
        P("expert", None, None),
        P("expert", None, None),
        P("expert", None, None),
    )
    return jax.shard_map(
        on_device,
        mesh=mesh,
        in_specs=placed,
        out_specs=(P(("group", "expert"), None), P(("group", "expert"), None, None)),
        check_vma=False,
    )
```

time: 243 us -> 199 us (0.82)
  the two profiles are of different devices: /device:TPU:15 before, /device:TPU:0 now
where the time goes in v4:
time: 199 us
  waiting for transfers between devices  118 us (59%)
  Pallas kernels  31 us (16%)
  blocking collectives  23.3 us (12%)
  between operations  13.8 us (7%)
  local copies, waits for them, and re-layouts  10.6 us (5%)
  other arithmetic  2.42 us (1%)
    reduce_scatter x1, waiting for transfers between devices, on_device(): branch = lax.psum_scatter(dense, 'expert', scatter_dimension=0, tiled=True)  62.9 us
    all_gather x1, waiting for transfers between devices, on_device(): frames = lax.all_gather(normed, 'expert', axis=0, tiled=True)  29.5 us
    all_gather x1, waiting for transfers between devices, on_device(): cots = lax.all_gather(cotangent, 'expert', axis=0, tiled=True)  24.6 us
    all_gather x1, blocking collectives, on_device(): meta = lax.all_gather(meta, 'expert', axis=0, tiled=True)  23.3 us
    pallas_call x1, Pallas kernels, on_device(): call(functools.partial(ffn_kernel, capacity), 40, 'ffn', 6 * rows * width...  20.1 us
    unnamed x16, local copies, waits for them, and re-layouts  10.6 us
    pallas_call x1, Pallas kernels, on_device(): call(functools.partial(grad_kernel, capacity), 40, 'grad', 2 * rows * wid...  10 us
  transfers between devices with their start and end apart: 3, of which 3 were waited for; matrix products, arithmetic and copies ran while one was open for 0% of the time, Pallas kernels for 15%

profile of v4, /device:TPU:0, one launch (start us, length us, event | category | flops | bytes accessed | tf_op | source)
XLA Modules:
  0.0 198.8 jit_solution(2950562589717584565)
XLA Ops:
  7.2 0.0 all-gather.5.cloned.1.call-start
  7.2 0.0 copy-start.1
  7.2 0.9 copy-done.1
  8.2 0.0 copy-start.3
  8.2 0.7 copy-done.3
  8.9 0.9 normed.1
  9.7 0.0 all-gather.5.cloned.1.call-update
  9.7 0.0 all-gather.7.cloned.1.call-start
  9.8 0.7 all-gather.7.cloned.1.call-update
  10.5 0.0 reduce-scatter.2.cloned.1.call-start
  10.5 0.7 add_bitcast_fusion
  11.3 23.3 %all-gather.1.meta_ref = s32[16,4,128]{2,1,0:T(4,128)S(1)} all-gather(s32[1,4,128]{2,1,0:T(4,128)S(1)} %add_bitcast_fusion), channel_id=2, replica_groups=mesh['group'=2,'expert'=16] {'expert'}, dimensions={0}, use_global_device_ids=true | all-gather | bytes 34816 | tf_op jit(solution)/shard_map/all_gather | solution.py:138
  34.5 29.5 %all-gather.5.cloned.1.call-done.frames_ref = bf16[2048,1024]{1,0:T(8,128)(2,1)} async-done(((bf16[128,1024]{1,0:T(8,128)(2,1)}), bf16[2048,1024]{1,0:T(8,128)(2,1)}) %all-gather.5.cloned.1.call-update) | async-done | bytes 4194320 | tf_op jit(solution)/shard_map/all_gather | solution.py:139
  64.0 0.0 copy-start.5
  64.0 1.6 copy-done.5
  65.6 0.0 copy-start.6
  65.6 1.6 copy-done.6
  67.2 0.0 copy-start.7
  67.2 1.6 copy-done.7
  68.8 20.1 %ffn.1 = (bf16[1024,1536]{1,0:T(8,128)(2,1)S(1)}, bf16[2048,1024]{1,0:T(8,128)(2,1)S(1)}) custom-call(s32[1]{0:T(128)} %bitcast.expert_ref, s32[16,4,128]{2,1,0:T(4,128)S(1)} %all-gather.1.meta_ref, bf16[2048,1024]{1,0:T(8,128)(2,1)} %all-gather.5.cloned.1.call-done.frames_ref, bf16[1,1024,1024]{2,1,0:T(8,128)(2,1)S(1)} %copy-done.5, ...), custom_call_target="tpu_custom_call" | custom-call | flops 9663676416 | bytes 4194304 | tf_op jit(solution)/shard_map/ffn/pallas_call | solution.py:141
  88.9 0.0 copy-start
  88.9 2.0 copy-done
  90.9 0.0 reduce-scatter.2.cloned.1.call-update
  90.9 24.6 %all-gather.7.cloned.1.call-done.cot_ref = bf16[2048,1024]{1,0:T(8,128)(2,1)} async-done(((bf16[128,1024]{1,0:T(8,128)(2,1)}), bf16[2048,1024]{1,0:T(8,128)(2,1)}) %all-gather.7.cloned.1.call-update) | async-done | bytes 4194320 | tf_op jit(solution)/shard_map/all_gather | solution.py:140
  115.5 0.0 copy-start.4
  115.5 2.2 %copy-done.4 = bf16[2048,1024]{1,0:T(8,128)(2,1)S(1)} copy-done((bf16[2048,1024]{1,0:T(8,128)(2,1)S(1)}, bf16[2048,1024]{1,0:T(8,128)(2,1)}, u32[]{:S(2)}) %copy-start.4) | copy-done | bytes 4194328
  117.6 0.0 copy-start.2
  117.6 10.0 %grad.1 = bf16[1,1024,1024]{2,1,0:T(8,128)(2,1)} custom-call(s32[1]{0:T(128)} %bitcast.expert_ref, s32[16,4,128]{2,1,0:T(4,128)S(1)} %all-gather.1.meta_ref, bf16[2048,1024]{1,0:T(8,128)(2,1)S(1)} %copy-done.4, bf16[1024,1536]{1,0:T(8,128)(2,1)S(1)} %get-tuple-element.5.turned_ref), custom_call_target="tpu_custom_call" | custom-call | flops 3221225472 | bytes 4194304 | tf_op jit(solution)/shard_map/grad/pallas_call | solution.py:159
  127.7 62.9 %reduce-scatter.2.cloned.1.call-done = bf16[128,1024]{1,0:T(8,128)(2,1)} async-done(((bf16[2048,1024]{1,0:T(8,128)(2,1)}), bf16[128,1024]{1,0:T(8,128)(2,1)}) %reduce-scatter.2.cloned.1.call-update) | async-done | bytes 262160 | tf_op jit(solution)/shard_map/reduce_scatter | solution.py:158
  190.6 0.0 copy-done.2
  190.6 1.7 add_convert_fusion
Async XLA Ops:
  7.2 56.9 %all-gather.5.cloned.1.call-start = ((), (), s32[]{:S(2)}) async-start(), calls=%async_computation.1 | async-start | bytes 4456448 | tf_op jit(solution)/shard_map/all_gather | solution.py:139
  7.2 1.0 copy-start.1
  8.2 0.7 copy-start.3
  9.7 105.7 %all-gather.7.cloned.1.call-start = ((), (), s32[]{:S(2)}) async-start(), calls=%async_computation.3 | async-start | bytes 4456448 | tf_op jit(solution)/shard_map/all_gather | solution.py:140
  10.5 180.1 %reduce-scatter.2.cloned.1.call-start = ((), (), s32[]{:S(2)}) async-start(), calls=%async_computation.2 | async-start | bytes 4456448 | tf_op jit(solution)/shard_map/reduce_scatter | solution.py:158
  64.0 1.6 copy-start.5
  65.6 1.6 copy-start.6
  67.2 1.6 copy-start.7
  88.9 2.0 copy-start
  115.5 2.2 %copy-start.4 = (bf16[2048,1024]{1,0:T(8,128)(2,1)S(1)}, bf16[2048,1024]{1,0:T(8,128)(2,1)}, u32[]{:S(2)}) copy-start(bf16[2048,1024]{1,0:T(8,128)(2,1)} %all-gather.7.cloned.1.call-done.cot_ref) | copy-start | bytes 12582916
  117.6 72.9 %copy-start.2 = (bf16[128,1024]{1,0:T(8,128)(2,1)S(1)}, bf16[128,1024]{1,0:T(8,128)(2,1)}, u32[]{:S(2)}) copy-start(bf16[128,1024]{1,0:T(8,128)(2,1)} %tokens_ref.1) | copy-start | bytes 786436
Sparse Core Ops, SparseCore 0:
  10.7 53.2 all-gather.4
  66.2 49.2 all-gather.6
  119.3 71.2 reduce-scatter.1

commit v5 on v2

--- a/solution.py
+++ b/solution.py
@@ -9,6 +9,7 @@
 
 HSPLIT = 4
 GROUPS = 4
+JOINED = ((1, 2), (2, 3))
 TILE = 256
 LINK_WORK = 10 << 30
 F32 = jnp.float32
@@ -73,37 +74,27 @@
     return copies
 
 
-def send_rows_kernel(experts, plane_ref, tokens_hbm, gain_hbm, routes_hbm, *refs):
-    outs = refs[:experts]
-    tokens_ref, gain_ref, routes_ref, semaphores = refs[experts:]
-    copies = fetch(
-        semaphores, (routes_hbm, routes_ref), (gain_hbm, gain_ref), (tokens_hbm, tokens_ref)
-    )
+def send_kernel(experts, plane_ref, *refs):
+    sources, refs = refs[:5], refs[5:]
+    row_outs, grad_outs = refs[:experts], refs[experts : 2 * experts]
+    targets, semaphores = refs[2 * experts : -1], refs[-1]
+    tokens_ref, cot_ref, routes_ref, nums_ref, gain_ref = targets
+    copies = fetch(semaphores, *zip(sources, targets))
+    copies[2].wait()
+    copies[3].wait()
+    routes = routes_ref[...]
+    placings = placing_of(routes, plane_ref[0], experts, row_outs[0].shape[0])
+    gates = gates_of(routes, nums_ref[...], plane_ref[0], experts)
+    copies[4].wait()
     copies[0].wait()
-    placings = placing_of(routes_ref[...], plane_ref[0], experts, outs[0].shape[0])
-    copies[1].wait()
-    copies[2].wait()
     frames = tokens_ref[...].astype(F32)
     inverse = lax.rsqrt(jnp.mean(frames * frames, -1, keepdims=True) + 1e-06)
     normed = (frames * inverse * gain_ref[...]).astype(BF16)
-    for out, placing in zip(outs, placings):
+    for out, placing in zip(row_outs, placings):
         out[...] = jnp.dot(placing.astype(BF16), normed, preferred_element_type=F32).astype(BF16)
-
-
-def send_grads_kernel(experts, plane_ref, cot_hbm, routes_hbm, nums_hbm, *refs):
-    outs = refs[:experts]
-    cot_ref, routes_ref, nums_ref, semaphores = refs[experts:]
-    copies = fetch(
-        semaphores, (routes_hbm, routes_ref), (nums_hbm, nums_ref), (cot_hbm, cot_ref)
-    )
-    copies[0].wait()
     copies[1].wait()
-    routes = routes_ref[...]
-    placings = placing_of(routes, plane_ref[0], experts, outs[0].shape[0])
-    gates = gates_of(routes, nums_ref[...], plane_ref[0], experts)
-    copies[2].wait()
     cot = cot_ref[...]
-    for s, (out, placing) in enumerate(zip(outs, placings)):
+    for s, (out, placing) in enumerate(zip(grad_outs, placings)):
         picked = jnp.dot(placing.astype(BF16), cot, preferred_element_type=F32)
         gate = jnp.sum(placing * gates[s : s + 1, :], -1, keepdims=True)
         out[...] = (gate * picked).astype(BF16)
@@ -159,20 +150,38 @@
         send_ref[:, columns] = value[half:]
 
 
-def grad_kernel(plan, turned_count, *refs):
-    turned, pieces = refs[:turned_count], refs[turned_count:-3]
+def gather_grad(plan, refs, hidden_ref, cot_ref):
+    at = 0
+    for turned, column, piece, row, count in plan:
+        hidden_ref[:, at : at + count] = refs[turned][:, column : column + count]
+        cot_ref[at : at + count, :] = refs[piece][row : row + count, :]
+        at += count
+
+
+def first_grad_kernel(plan, *refs):
     out_ref, hidden_ref, cot_ref = refs[-3:]
-    for i, start, rows, at in plan:
-        cot_ref[at : at + rows, :] = pieces[i][start : start + rows, :]
-    at = 0
-    for value in turned:
-        hidden_ref[:, at : at + value.shape[1]] = value[...]
-        at += value.shape[1]
-    for j in range(out_ref.shape[2] // TILE):
-        columns = slice(j * TILE, (j + 1) * TILE)
-        out_ref[0, :, columns] = jnp.dot(
-            hidden_ref[...], cot_ref[:, columns], preferred_element_type=F32
-        ).astype(BF16)
+    gather_grad(plan, refs, hidden_ref, cot_ref)
+    for j in range(out_ref.shape[0] // TILE):
+        part = slice(j * TILE, (j + 1) * TILE)
+        out_ref[part, :] = jnp.dot(
+            hidden_ref[part, :], cot_ref[...], preferred_element_type=F32
+        )
+
+
+def last_grad_kernel(plan, first_ref, *refs):
+    out_hbm, out_ref, hidden_ref, cot_ref, semaphores = refs[-5:]
+    gather_grad(plan, refs, hidden_ref, cot_ref)
+    copies = []
+    for j in range(first_ref.shape[0] // TILE):
+        part = slice(j * TILE, (j + 1) * TILE)
+        total = jnp.dot(hidden_ref[part, :], cot_ref[...], preferred_element_type=F32)
+        out_ref[part, :] = (first_ref[part, :] + total).astype(BF16)
+        copies.append(
+            pltpu.make_async_copy(out_ref.at[part, :], out_hbm.at[0, part, :], semaphores.at[j])
+        )
+        copies[-1].start()
+    for copy in copies:
+        copy.wait()
 
 
 def combine_kernel(experts, plane_ref, tokens_ref, routes_ref, nums_ref, *refs):
@@ -229,36 +238,48 @@
     def launch(name, value, mask):
         flying[name] = swap(value, mask)
 
-    def land():
+    def land(*earlier):
         names = list(flying)
-        landed = dict(zip(names, through([flying.pop(n) for n in names], "land", LINK_WORK)))
-        for name, value in landed.items():
-            if name[0] == "y":
-                live[name[1:]] = join([live.pop(("sent",) + name[1:]), value])
-            elif name[0] == "fold":
-                gs = name[1]
+        values = [flying.pop(name) for name in names]
+        values = lax.optimization_barrier(tuple(values) + earlier)[: len(names)]
+        values = through(values, "land", LINK_WORK)
+        for name, value in zip(names, values):
+            if name[0] != "y":
+                live[name] = value
+                continue
+            at = 0
+            for kind, gs in name[1:]:
+                here = live.pop(("sent", kind, gs))
+                came = value[at : at + here.shape[0]]
+                at += here.shape[0]
+                if kind != "fold":
+                    live[kind, "own", gs] = join([here, came])
+                    continue
                 keep, crossed = live.pop(("keep", gs)), live.pop(("crossed", gs))
-                rows = value.shape[0]
+                rows = came.shape[0]
                 total = keep[:rows].astype(F32) + crossed[:rows].astype(F32)
-                total = (total + value.astype(F32)).astype(BF16)
+                total = (total + came.astype(F32)).astype(BF16)
                 for i, s in enumerate([s for g in gs for s in groups[g]]):
                     live["R", s] = total[i * capacity : (i + 1) * capacity]
-            else:
-                live[name] = value
-        return next(iter(landed.values()))
-
-    def across(kind, g):
-        for s in groups[g]:
+        return values[0]
+
+    def across(kind, *gs):
+        for s in [s for g in gs for s in groups[g]]:
             if s:
                 launch((kind, s), live[kind, s], s * HSPLIT)
 
-    def along(kind, *gs):
-        own = join([live.pop((kind, s)) for g in gs for s in groups[g]])
-        live["sent", kind, "own", gs] = own
-        launch(("y", kind, "own", gs), own, 2)
-
-    def core(kind, *gs):
-        live[kind, "other", gs] = swap(live[kind, "own", gs], 1)
+    def along(*items):
+        for kind, gs in items:
+            if kind == "fold":
+                value = live.pop(("across", gs))
+            else:
+                value = join([live.pop((kind, s)) for g in gs for s in groups[g]])
+            live["sent", kind, gs] = value
+        launch(("y",) + items, join([live["sent", kind, gs] for kind, gs in items]), 2)
+
+    def core(kind, *tuples):
+        gs = tuple(g for part in tuples for g in part)
+        live[kind, "other", gs] = swap(join([live[kind, "own", part] for part in tuples]), 1)
 
     def ffn(*gs):
         pieces = [live.pop(("N", "own", gs)), live.pop(("N", "other", gs))]
@@ -286,45 +307,23 @@
         both = keep[rows:].astype(F32) + crossed[rows:].astype(F32)
         live["across", gs] = both.astype(BF16)
 
-    def fold_row(*gs):
-        launch(("fold", gs), live.pop(("across", gs)), 2)
-
-    def back(g):
-        across("R", g)
-
-    def send_rows():
+    def in_hbm(*values):
+        return [pltpu.with_memory_space_constraint(v, pltpu.HBM) for v in values]
+
+    def send():
+        sources = (tokens, cotangent, routes, gate_nums, gain)
         values = call(
-            functools.partial(send_rows_kernel, experts),
+            functools.partial(send_kernel, experts),
             16,
-            "send_rows",
-            out_shape=[piece] * experts,
-            in_specs=[scalar] + [anywhere] * 3,
-            out_specs=whole(experts),
-            scratch_shapes=[
-                pltpu.VMEM(tokens.shape, BF16),
-                pltpu.VMEM(gain.shape, F32),
-                pltpu.VMEM(routes.shape, jnp.int32),
-                pltpu.SemaphoreType.DMA((3,)),
-            ],
-        )(plane, tokens, gain, routes)
-        live.update({("N", s): value for s, value in enumerate(values)})
-
-    def send_grads():
-        values = call(
-            functools.partial(send_grads_kernel, experts),
-            16,
-            "send_grads",
-            out_shape=[piece] * experts,
-            in_specs=[scalar] + [anywhere] * 3,
-            out_specs=whole(experts),
-            scratch_shapes=[
-                pltpu.VMEM(cotangent.shape, BF16),
-                pltpu.VMEM(routes.shape, jnp.int32),
-                pltpu.VMEM(gate_nums.shape, jnp.int32),
-                pltpu.SemaphoreType.DMA((3,)),
-            ],
-        )(plane, after(cotangent, live["N", experts - 1]), routes, gate_nums)
-        live.update({("C", s): value for s, value in enumerate(values)})
+            "send",
+            out_shape=[piece] * (2 * experts),
+            in_specs=[scalar] + [anywhere] * len(sources),
+            out_specs=whole(2 * experts),
+            scratch_shapes=[pltpu.VMEM(v.shape, v.dtype) for v in sources]
+            + [pltpu.SemaphoreType.DMA((len(sources),))],
+        )(plane, *in_hbm(*sources))
+        live.update({("N", s): value for s, value in enumerate(values[:experts])})
+        live.update({("C", s): value for s, value in enumerate(values[experts:])})
 
     def load():
         weight = jax.ShapeDtypeStruct((width, hidden_width), BF16)
@@ -336,92 +335,106 @@
             in_specs=[anywhere] * 3,
             out_specs=whole(3),
             scratch_shapes=[pltpu.SemaphoreType.DMA((3,))],
-        )(after(w_gate, live["C", experts - 1]), w_up, w_down)
+        )(*in_hbm(after(w_gate, live["C", experts - 1]), w_up, w_down))
         live.update({("w", i): value for i, value in enumerate(values)})
 
-    send_rows()
+    def grad_call(turned, pieces):
+        columns = {}
+        for i, gs in enumerate(turned):
+            at = 0
+            for half in ("own", "other"):
+                for side in range(2):
+                    for g in gs:
+                        columns[half, side, g] = (i, at)
+                        at += height
+        plan = []
+        for i, (half, gs) in enumerate(pieces):
+            row = 0
+            for parts in [gs] if gs in JOINED else [(g,) for g in gs]:
+                for side in range(2):
+                    for g in parts:
+                        where, at = columns[half, side, g]
+                        plan.append((where, at, len(turned) + i, row, height))
+                        row += height
+        total = sum(step[-1] for step in plan)
+        sides = [pltpu.VMEM((hidden_width, total), BF16), pltpu.VMEM((total, width), BF16)]
+        values = [live["turned", gs] for gs in turned]
+        values += [live["C", half, gs] for half, gs in pieces]
+        return plan, sides, values
+
+    def first_grad(turned, pieces):
+        plan, sides, values = grad_call(turned, pieces)
+        live["first"] = call(
+            functools.partial(first_grad_kernel, plan),
+            24,
+            "first_grad",
+            out_shape=jax.ShapeDtypeStruct((hidden_width, width), F32),
+            in_specs=whole(len(values)),
+            out_specs=whole(1)[0],
+            scratch_shapes=sides,
+        )(*values)
+
+    def last_grad(turned, pieces):
+        plan, sides, values = grad_call(turned, pieces)
+        return call(
+            functools.partial(last_grad_kernel, plan),
+            24,
+            "last_grad",
+            out_shape=jax.ShapeDtypeStruct((1, hidden_width, width), BF16),
+            in_specs=whole(1 + len(values)),
+            out_specs=anywhere,
+            scratch_shapes=[pltpu.VMEM((hidden_width, width), BF16)]
+            + sides
+            + [pltpu.SemaphoreType.DMA((hidden_width // TILE,))],
+        )(live["first"], *values)
+
+    send()
     if shifts > 1:
         across("N", 0)
-        land()
-    sync()
-    along("N", 0)
-    for g in (1, 2):
-        across("N", g)
-    send_grads()
-    if shifts > 1:
         across("C", 0)
         land()
-    along("C", 0)
+    sync()
+    across("N", 1, 2)
+    along(("N", (0,)), ("C", (0,)))
     load()
     land()
     sync()
     across("N", 3)
     across("C", 1)
-    along("N", 1, 2)
-    core("N", 0)
+    along(("N", (1, 2)))
+    core("N", (0,))
     ffn(0)
     cross(0)
     fold_core(land(), 0)
     sync()
     across("C", 2)
-    along("N", 3)
-    fold_row(0)
-    core("N", 1, 2)
+    along(("N", (3,)), ("fold", (0,)))
+    core("N", (1, 2))
     ffn(1, 2)
     cross(1, 2)
     fold_core(land(), 1, 2)
     sync()
     across("C", 3)
-    fold_row(1, 2)
-    core("N", 3)
+    along(("fold", (1, 2)))
+    core("N", (3,))
     ffn(3)
     cross(3)
-    core("C", 0)
     fold_core(land(), 3)
     sync()
     if shifts > 1:
-        back(0)
-    back(1)
-    back(2)
-    fold_row(3)
-    along("C", 1)
+        across("R", 0)
+    across("R", 1, 2)
+    along(("fold", (3,)), ("C", (1,)))
     land()
     sync()
-    back(3)
-    along("C", 2, 3)
-    core("C", 1)
-    land()
-    sync()
-    core("C", 2, 3)
-
-    places, at = {}, 0
-    turned = [(0,), (1, 2), (3,)]
-    for gs in turned:
-        for half in ("own", "other"):
-            for side in range(2):
-                for g in gs:
-                    places[half, side, g] = at
-                    at += height
-    pieces, plan = [], []
-    for gs in [(0,), (1,), (2, 3)]:
-        for half in ("own", "other"):
-            for side in range(2):
-                for i, g in enumerate(gs):
-                    start = (side * len(gs) + i) * height
-                    plan.append((len(pieces), start, height, places[half, side, g]))
-            pieces.append(live["C", half, gs])
-    grad_down = call(
-        functools.partial(grad_kernel, plan, len(turned)),
-        24,
-        "grad",
-        out_shape=jax.ShapeDtypeStruct((1, hidden_width, width), BF16),
-        in_specs=whole(len(turned) + len(pieces)),
-        out_specs=whole(1)[0],
-        scratch_shapes=[
-            pltpu.VMEM((hidden_width, at), BF16),
-            pltpu.VMEM((at, width), BF16),
-        ],
-    )(*[live["turned", gs] for gs in turned], *pieces)
+    across("R", 3)
+    along(("C", (2, 3)))
+    core("C", (0,), (1,))
+    first_grad([(0,), (1, 2)], [("own", (0,)), ("own", (1,)), ("other", (0, 1))])
+    land(live["first"])
+    sync()
+    core("C", (2, 3))
+    grad_down = last_grad([(1, 2), (3,)], [("own", (2, 3)), ("other", (2, 3))])
     mixed = call(
         functools.partial(combine_kernel, experts),
         16,

time: 88.2 us -> 104 us (1.18)
  waiting for transfers between devices: 32.5 us -> 59.2 us
  local copies, waits for them, and re-layouts: 10.2 us -> 0.9 us
  starting transfers between devices: 25.1 us -> 20.6 us
  Pallas kernels: 18.2 us -> 21.4 us
    ppermute x27 -> x23, waiting for transfers between devices: 32.5 us -> 59.2 us  [swap(): lax.ppermute(value, 'expert', [(i, i ^ mask) for i in range(devices)])]
    unnamed x24 -> x6, local copies, waits for them, and re-layouts: 10.2 us -> 0.82 us
    ppermute x27 -> x23, starting transfers between devices: 25.1 us -> 20.6 us  [swap(): lax.ppermute(value, 'expert', [(i, i ^ mask) for i in range(devices)])]
    pallas_call x1, Pallas kernels: 0.45 us -> 2.88 us  [load(): call(load_kernel, 16, 'load', out_shape=[weight, weight, jax.ShapeDtypeSt...]
  transfers between devices with their start and end apart: 27 -> 23, of which waited for: 11 -> 15; matrix products, arithmetic and copies ran while one was open for 1% -> 0% of each run, Pallas kernels for 14% -> 6%
where the time goes in v5:
time: 104 us
  waiting for transfers between devices  59.2 us (57%)
  Pallas kernels  21.4 us (21%)
  starting transfers between devices  20.6 us (20%)
  between operations  1.06 us (1%)
    ppermute x23, waiting for transfers between devices, swap(): lax.ppermute(value, 'expert', [(i, i ^ mask) for i in range(devices)])  59.2 us
    ppermute x23, starting transfers between devices, swap(): lax.ppermute(value, 'expert', [(i, i ^ mask) for i in range(devices)])  20.6 us
    pallas_call x3, Pallas kernels, ffn(): call(functools.partial(ffn_kernel, len(pieces)), 24, 'ffn', out_shape=[ja...  10.3 us
    pallas_call x1, Pallas kernels, load(): call(load_kernel, 16, 'load', out_shape=[weight, weight, jax.ShapeDtypeSt...  2.88 us
    pallas_call x1, Pallas kernels, last_grad(): call(functools.partial(last_grad_kernel, plan), 24, 'last_grad', out_shap...  2.81 us
    pallas_call x1, Pallas kernels, first_grad(): call(functools.partial(first_grad_kernel, plan), 24, 'first_grad', out_sh...  2.14 us
  transfers between devices with their start and end apart: 23, of which 15 were waited for; matrix products, arithmetic and copies ran while one was open for 0% of the time, Pallas kernels for 6%

profile of v5, /device:TPU:0, one launch (start us, length us, event | category | flops | bytes accessed | tf_op | source)
XLA Modules:
  0.0 104.1 jit_solution(5941512329234530892)
XLA Ops:
  0.6 1.9 %send.1 = (bf16[96,1024]{1,0:T(8,128)(2,1)S(1)}, bf16[96,1024]{1,0:T(8,128)(2,1)S(1)}, bf16[96,1024]{1,0:T(8,128)(2,1)S(1)}, bf16[96,1024]{1,0:T(8,128)(2,1)S(1)...) custom-call(s32[1]{0:T(128)} %bitcast.plane_ref, ...), custom_call_target="tpu_custom_call" | custom-call | tf_op jit(solution)/shard_map/send/pallas_call | solution.py:315
  2.6 3.0 %collective-permute-start.2 = (bf16[192,1024]{1,0:T(8,128)(2,1)S(1)}, bf16[192,1024]{1,0:T(8,128)(2,1)S(1)}, u32[]{:S(2)}, u32[]{:S(2)}) collective-permute-start(bf16[192,1024]{1,0:T(8,128)(2,1)S(1)} %pad_maximum_fusion.4), channel_id=1, source_target_pairs={{0,2},{1,3},{2,0},{3,1},{4,6},{5,7},{6,4},{7,5},{8,10},{9,11},{10,... | collective-permute-start | bytes 1179656 | tf_op jit(solution)/shard_map/ppermute | solution.py:227
  5.6 1.6 %collective-permute-start = (bf16[96,1024]{1,0:T(8,128)(2,1)S(1)}, bf16[96,1024]{1,0:T(8,128)(2,1)S(1)}, u32[]{:S(2)}, u32[]{:S(2)}) collective-permute-start(bf16[96,1024]{1,0:T(8,128)(2,1)S(1)} %get-tuple-element.126), channel_id=1, source_target_pairs={{0,4},{1,5},{2,6},{3,7},{4,0},{5,1},{6,2},{7,3},{8,12},{9,13},{10,... | collective-permute-start | bytes 589832 | tf_op jit(solution)/shard_map/ppermute | solution.py:227
  7.2 2.6 %collective-permute-start.1 = (bf16[96,1024]{1,0:T(8,128)(2,1)S(1)}, bf16[96,1024]{1,0:T(8,128)(2,1)S(1)}, u32[]{:S(2)}, u32[]{:S(2)}) collective-permute-start(bf16[96,1024]{1,0:T(8,128)(2,1)S(1)} %get-tuple-element.127), channel_id=1, source_target_pairs={{0,8},{1,9},{2,10},{3,11},{4,12},{5,13},{6,14},{7,15},{8,0},{9,1},... | collective-permute-start | bytes 589832 | tf_op jit(solution)/shard_map/ppermute | solution.py:227
  9.8 2.9 %load.1 = (bf16[1024,1024]{1,0:T(8,128)(2,1)S(1)}, bf16[1024,1024]{1,0:T(8,128)(2,1)S(1)}, bf16[1024,1024]{1,0:T(8,128)(2,1)S(1)}) custom-call(bf16[1,1024,1024]{2,1,0:T(8,128)(2,1)} %refs_0_.2, bf16[1,1024,1024]{2,1,0:T(8,128)(2,1)} %refs_1_.3, bf16[1,1024,1024]{2,1,0:T(8,128)(2,1)} %refs_2_.1), custom_call_target="tpu_custom_call" | custom-call | tf_op jit(solution)/shard_map/load/pallas_call | solution.py:330
  12.7 3.4 %collective-permute-done.refs_0_ = bf16[96,1024]{1,0:T(8,128)(2,1)S(1)} collective-permute-done((bf16[96,1024]{1,0:T(8,128)(2,1)S(1)}, bf16[96,1024]{1,0:T(8,128)(2,1)S(1)}, u32[]{:S(2)}, u32[]{:S(2)}) %collective-permute-start) | collective-permute-done | bytes 196640 | tf_op jit(solution)/shard_map/ppermute | solution.py:227
  16.1 2.4 %collective-permute-done.1.refs_1_ = bf16[96,1024]{1,0:T(8,128)(2,1)S(1)} collective-permute-done((bf16[96,1024]{1,0:T(8,128)(2,1)S(1)}, bf16[96,1024]{1,0:T(8,128)(2,1)S(1)}, u32[]{:S(2)}, u32[]{:S(2)}) %collective-permute-start.1) | collective-permute-done | bytes 196640 | tf_op jit(solution)/shard_map/ppermute | solution.py:227
  19.2 2.5 %collective-permute-start.3 = (bf16[96,1024]{1,0:T(8,128)(2,1)S(1)}, bf16[96,1024]{1,0:T(8,128)(2,1)S(1)}, u32[]{:S(2)}, u32[]{:S(2)}) collective-permute-start(bf16[96,1024]{1,0:T(8,128)(2,1)S(1)} %get-tuple-element.144), channel_id=1, source_target_pairs={{0,12},{1,13},{2,14},{3,15},{4,8},{5,9},{6,10},{7,11},{8,4},{9,5},... | collective-permute-start | bytes 589832 | tf_op jit(solution)/shard_map/ppermute | solution.py:227
  21.7 7.1 %collective-permute-done.3.refs_0_ = bf16[96,1024]{1,0:T(8,128)(2,1)S(1)} collective-permute-done((bf16[96,1024]{1,0:T(8,128)(2,1)S(1)}, bf16[96,1024]{1,0:T(8,128)(2,1)S(1)}, u32[]{:S(2)}, u32[]{:S(2)}) %collective-permute-start.3) | collective-permute-done | bytes 196640 | tf_op jit(solution)/shard_map/ppermute | solution.py:227
  28.8 3.8 %collective-permute-done.4.refs_1_ = bf16[96,1024]{1,0:T(8,128)(2,1)S(1)} collective-permute-done((bf16[96,1024]{1,0:T(8,128)(2,1)S(1)}, bf16[96,1024]{1,0:T(8,128)(2,1)S(1)}, u32[]{:S(2)}, u32[]{:S(2)}) %collective-permute-start.4) | collective-permute-done | bytes 196640 | tf_op jit(solution)/shard_map/ppermute | solution.py:227
  32.6 2.6 %ffn.3 = (bf16[1024,384]{1,0:T(8,128)(2,1)S(1)}, bf16[192,1024]{1,0:T(8,128)(2,1)S(1)}, bf16[192,1024]{1,0:T(8,128)(2,1)S(1)}) custom-call(bf16[192,1024]{1,0:T(8,128)(2,1)S(1)} %get-tuple-element.159.refs_0_, bf16[192,1024]{1,0:T(8,128)(2,1)S(1)} %collective-permute-done.6.refs_1_, bf16[1024,1024]{1,0:T(8,128)(2,1)S(1)} %get-tuple-element.193.refs_2_, ...), custom_call_target="tpu_custom_call" | custom-call | tf_op jit(solution)/shard_map/ffn/pallas_call | solution.py:288
  35.4 1.6 %collective-permute-done.7 = bf16[192,1024]{1,0:T(8,128)(2,1)S(1)} collective-permute-done((bf16[192,1024]{1,0:T(8,128)(2,1)S(1)}, bf16[192,1024]{1,0:T(8,128)(2,1)S(1)}, u32[]{:S(2)}, u32[]{:S(2)}) %collective-permute-start.7) | collective-permute-done | bytes 393248 | tf_op jit(solution)/shard_map/ppermute | solution.py:227
  37.3 1.6 %collective-permute-start.9 = (bf16[192,1024]{1,0:T(8,128)(2,1)S(1)}, bf16[192,1024]{1,0:T(8,128)(2,1)S(1)}, u32[]{:S(2)}, u32[]{:S(2)}) collective-permute-start(bf16[192,1024]{1,0:T(8,128)(2,1)S(1)} %pad_maximum_fusion.6), channel_id=1, source_target_pairs={{0,2},{1,3},{2,0},{3,1},{4,6},{5,7},{6,4},{7,5},{8,10},{9,11},{10,... | collective-permute-start | bytes 1179656 | tf_op jit(solution)/shard_map/ppermute | solution.py:227
  39.5 11.4 %collective-permute-done.8.refs_0_ = bf16[96,1024]{1,0:T(8,128)(2,1)S(1)} collective-permute-done((bf16[96,1024]{1,0:T(8,128)(2,1)S(1)}, bf16[96,1024]{1,0:T(8,128)(2,1)S(1)}, u32[]{:S(2)}, u32[]{:S(2)}) %collective-permute-start.8) | collective-permute-done | bytes 196640 | tf_op jit(solution)/shard_map/ppermute | solution.py:227
  50.9 5.1 %ffn.4 = (bf16[1024,768]{1,0:T(8,128)(2,1)S(1)}, bf16[384,1024]{1,0:T(8,128)(2,1)S(1)}, bf16[384,1024]{1,0:T(8,128)(2,1)S(1)}) custom-call(bf16[384,1024]{1,0:T(8,128)(2,1)S(1)} %pad_maximum_fusion.refs_0_, bf16[384,1024]{1,0:T(8,128)(2,1)S(1)} %collective-permute-done.10.refs_1_, bf16[1024,1024]{1,0:T(8,128)(2,1)S(1)} %get-tuple-element.193.refs_2_, ...), custom_call_target="tpu_custom_call" | custom-call | tf_op jit(solution)/shard_map/ffn/pallas_call | solution.py:288
  56.2 2.1 %collective-permute-done.11 = bf16[384,1024]{1,0:T(8,128)(2,1)S(1)} collective-permute-done((bf16[384,1024]{1,0:T(8,128)(2,1)S(1)}, bf16[384,1024]{1,0:T(8,128)(2,1)S(1)}, u32[]{:S(2)}, u32[]{:S(2)}) %collective-permute-start.11) | collective-permute-done | bytes 786464 | tf_op jit(solution)/shard_map/ppermute | solution.py:227
  59.0 1.5 %collective-permute-start.12 = (bf16[96,1024]{1,0:T(8,128)(2,1)S(1)}, bf16[96,1024]{1,0:T(8,128)(2,1)S(1)}, u32[]{:S(2)}, u32[]{:S(2)}) collective-permute-start(bf16[96,1024]{1,0:T(8,128)(2,1)S(1)} %get-tuple-element.188), channel_id=1, source_target_pairs={{0,12},{1,13},{2,14},{3,15},{4,8},{5,9},{6,10},{7,11},{8,4},{9,5},... | collective-permute-start | bytes 589832 | tf_op jit(solution)/shard_map/ppermute | solution.py:227
  60.5 7.8 %collective-permute-done.12.refs_0_ = bf16[96,1024]{1,0:T(8,128)(2,1)S(1)} collective-permute-done((bf16[96,1024]{1,0:T(8,128)(2,1)S(1)}, bf16[96,1024]{1,0:T(8,128)(2,1)S(1)}, u32[]{:S(2)}, u32[]{:S(2)}) %collective-permute-start.12) | collective-permute-done | bytes 196640 | tf_op jit(solution)/shard_map/ppermute | solution.py:227
  68.3 1.4 %collective-permute-done.13.refs_1_ = bf16[192,1024]{1,0:T(8,128)(2,1)S(1)} collective-permute-done((bf16[192,1024]{1,0:T(8,128)(2,1)S(1)}, bf16[192,1024]{1,0:T(8,128)(2,1)S(1)}, u32[]{:S(2)}, u32[]{:S(2)}) %collective-permute-start.13) | collective-permute-done | bytes 393248 | tf_op jit(solution)/shard_map/ppermute | solution.py:227
  69.7 2.6 %ffn.5 = (bf16[1024,384]{1,0:T(8,128)(2,1)S(1)}, bf16[192,1024]{1,0:T(8,128)(2,1)S(1)}, bf16[192,1024]{1,0:T(8,128)(2,1)S(1)}) custom-call(bf16[192,1024]{1,0:T(8,128)(2,1)S(1)} %pad_maximum_fusion.5.refs_0_, bf16[192,1024]{1,0:T(8,128)(2,1)S(1)} %collective-permute-done.14.refs_1_, bf16[1024,1024]{1,0:T(8,128)(2,1)S(1)} %get-tuple-element.193.refs_2_, ...), custom_call_target="tpu_custom_call" | custom-call | tf_op jit(solution)/shard_map/ffn/pallas_call | solution.py:288
  72.6 1.5 %collective-permute-done.15 = bf16[192,1024]{1,0:T(8,128)(2,1)S(1)} collective-permute-done((bf16[192,1024]{1,0:T(8,128)(2,1)S(1)}, bf16[192,1024]{1,0:T(8,128)(2,1)S(1)}, u32[]{:S(2)}, u32[]{:S(2)}) %collective-permute-start.15) | collective-permute-done | bytes 393248 | tf_op jit(solution)/shard_map/ppermute | solution.py:227
  75.3 1.5 %collective-permute-start.17 = (bf16[96,1024]{1,0:T(8,128)(2,1)S(1)}, bf16[96,1024]{1,0:T(8,128)(2,1)S(1)}, u32[]{:S(2)}, u32[]{:S(2)}) collective-permute-start(bf16[96,1024]{1,0:T(8,128)(2,1)S(1)} %get-tuple-element.216), channel_id=1, source_target_pairs={{0,8},{1,9},{2,10},{3,11},{4,12},{5,13},{6,14},{7,15},{8,0},{9,1},... | collective-permute-start | bytes 589832 | tf_op jit(solution)/shard_map/ppermute | solution.py:227
  76.8 8.6 %collective-permute-done.16.refs_0_ = bf16[96,1024]{1,0:T(8,128)(2,1)S(1)} collective-permute-done((bf16[96,1024]{1,0:T(8,128)(2,1)S(1)}, bf16[96,1024]{1,0:T(8,128)(2,1)S(1)}, u32[]{:S(2)}, u32[]{:S(2)}) %collective-permute-start.16) | collective-permute-done | bytes 196640 | tf_op jit(solution)/shard_map/ppermute | solution.py:227
  85.4 1.4 %collective-permute-done.17.refs_1_ = bf16[96,1024]{1,0:T(8,128)(2,1)S(1)} collective-permute-done((bf16[96,1024]{1,0:T(8,128)(2,1)S(1)}, bf16[96,1024]{1,0:T(8,128)(2,1)S(1)}, u32[]{:S(2)}, u32[]{:S(2)}) %collective-permute-start.17) | collective-permute-done | bytes 196640 | tf_op jit(solution)/shard_map/ppermute | solution.py:227
  87.2 1.4 %collective-permute-start.20 = (bf16[192,1024]{1,0:T(8,128)(2,1)S(1)}, bf16[192,1024]{1,0:T(8,128)(2,1)S(1)}, u32[]{:S(2)}, u32[]{:S(2)}) collective-permute-start(bf16[192,1024]{1,0:T(8,128)(2,1)S(1)} %pad_maximum_fusion.11), channel_id=1, source_target_pairs={{0,2},{1,3},{2,0},{3,1},{4,6},{5,7},{6,4},{7,5},{8,10},{9,11},{10,... | collective-permute-start | bytes 1179656 | tf_op jit(solution)/shard_map/ppermute | solution.py:227
  88.6 1.5 %collective-permute-start.19 = (bf16[96,1024]{1,0:T(8,128)(2,1)S(1)}, bf16[96,1024]{1,0:T(8,128)(2,1)S(1)}, u32[]{:S(2)}, u32[]{:S(2)}) collective-permute-start(bf16[96,1024]{1,0:T(8,128)(2,1)S(1)} %add_convert_fusion.2), channel_id=1, source_target_pairs={{0,12},{1,13},{2,14},{3,15},{4,8},{5,9},{6,10},{7,11},{8,4},{9,5},... | collective-permute-start | bytes 589832 | tf_op jit(solution)/shard_map/ppermute | solution.py:227
  90.1 2.1 %first_grad.1.first_ref = f32[1024,1024]{1,0:T(8,128)S(1)} custom-call(bf16[1024,384]{1,0:T(8,128)(2,1)S(1)} %get-tuple-element.228.refs_0_, bf16[1024,768]{1,0:T(8,128)(2,1)S(1)} %get-tuple-element.247.refs_1_.refs_0_, bf16[192,1024]{1,0:T(8,128)(2,1)S(1)} %get-tuple-element.227.refs_2_, bf16[192,1024]{1,0:T(8,128)(2,1)S(1)} %pad_maximum_fusion.10.refs_3_, ...), custom_call_target="tpu_custom_call" | custom-call | tf_op jit(solution)/shard_map/first_grad/pallas_call | solution.py:367
  92.2 5.3 %collective-permute-done.19.refs_0_ = bf16[96,1024]{1,0:T(8,128)(2,1)S(1)} collective-permute-done((bf16[96,1024]{1,0:T(8,128)(2,1)S(1)}, bf16[96,1024]{1,0:T(8,128)(2,1)S(1)}, u32[]{:S(2)}, u32[]{:S(2)}) %collective-permute-start.19) | collective-permute-done | bytes 196640 | tf_op jit(solution)/shard_map/ppermute | solution.py:227
  97.5 1.2 %collective-permute-done.20.refs_1_ = bf16[192,1024]{1,0:T(8,128)(2,1)S(1)} collective-permute-done((bf16[192,1024]{1,0:T(8,128)(2,1)S(1)}, bf16[192,1024]{1,0:T(8,128)(2,1)S(1)}, u32[]{:S(2)}, u32[]{:S(2)}) %collective-permute-start.20) | collective-permute-done | bytes 393248 | tf_op jit(solution)/shard_map/ppermute | solution.py:227
  98.9 0.8 copy-done
  99.7 1.4 %combine.1 = bf16[128,1024]{1,0:T(8,128)(2,1)} custom-call(s32[1]{0:T(128)} %bitcast.plane_ref, bf16[128,1024]{1,0:T(8,128)(2,1)S(1)} %copy-done, s32[2,128]{1,0:T(2,128)S(1)} %bitcast.5, s32[2,128]{1,0:T(2,128)S(1)} %bitcast.7, bf16[96,1024]{1,0:T(8,128)(2,1)S(1)} %add_convert_fusion.4.refs_0_, bf16[96,1024]{1,0:T(8,128)(2,1)S(1)} %get-tuple-element.243.refs_1_, ...), custom_call_target="tpu_custom_call" | custom-call | tf_op jit(solution)/shard_map/combine/pallas_call | solution.py:438
  101.2 2.8 %last_grad.1 = bf16[1,1024,1024]{2,1,0:T(8,128)(2,1)} custom-call(f32[1024,1024]{1,0:T(8,128)S(1)} %first_grad.1.first_ref, bf16[1024,768]{1,0:T(8,128)(2,1)S(1)} %get-tuple-element.247.refs_1_.refs_0_, bf16[1024,384]{1,0:T(8,128)(2,1)S(1)} %get-tuple-element.248.refs_1_, bf16[384,1024]{1,0:T(8,128)(2,1)S(1)} %pad_maximum_fusion.2.refs_2_, ...), custom_call_target="tpu_custom_call" | custom-call | tf_op jit(solution)/shard_map/last_grad/pallas_call | solution.py:379
  (55 shorter events, 4.6 us)
Async XLA Ops:
  2.6 15.9 %collective-permute-start.2 = (bf16[192,1024]{1,0:T(8,128)(2,1)S(1)}, bf16[192,1024]{1,0:T(8,128)(2,1)S(1)}, u32[]{:S(2)}, u32[]{:S(2)}) collective-permute-start(bf16[192,1024]{1,0:T(8,128)(2,1)S(1)} %pad_maximum_fusion.4), channel_id=1, source_target_pairs={{0,2},{1,3},{2,0},{3,1},{4,6},{5,7},{6,4},{7,5},{8,10},{9,11},{10,... | collective-permute-start | bytes 1179656 | tf_op jit(solution)/shard_map/ppermute | solution.py:227
  5.6 10.5 %collective-permute-start = (bf16[96,1024]{1,0:T(8,128)(2,1)S(1)}, bf16[96,1024]{1,0:T(8,128)(2,1)S(1)}, u32[]{:S(2)}, u32[]{:S(2)}) collective-permute-start(bf16[96,1024]{1,0:T(8,128)(2,1)S(1)} %get-tuple-element.126), channel_id=1, source_target_pairs={{0,4},{1,5},{2,6},{3,7},{4,0},{5,1},{6,2},{7,3},{8,12},{9,13},{10,... | collective-permute-start | bytes 589832 | tf_op jit(solution)/shard_map/ppermute | solution.py:227
  7.2 11.2 %collective-permute-start.1 = (bf16[96,1024]{1,0:T(8,128)(2,1)S(1)}, bf16[96,1024]{1,0:T(8,128)(2,1)S(1)}, u32[]{:S(2)}, u32[]{:S(2)}) collective-permute-start(bf16[96,1024]{1,0:T(8,128)(2,1)S(1)} %get-tuple-element.127), channel_id=1, source_target_pairs={{0,8},{1,9},{2,10},{3,11},{4,12},{5,13},{6,14},{7,15},{8,0},{9,1},... | collective-permute-start | bytes 589832 | tf_op jit(solution)/shard_map/ppermute | solution.py:227
  18.6 14.0 %collective-permute-start.5 = (bf16[192,1024]{1,0:T(8,128)(2,1)S(1)}, bf16[192,1024]{1,0:T(8,128)(2,1)S(1)}, u32[]{:S(2)}, u32[]{:S(2)}) collective-permute-start(bf16[192,1024]{1,0:T(8,128)(2,1)S(1)} %pad_maximum_fusion.8), channel_id=1, source_target_pairs={{0,2},{1,3},{2,0},{3,1},{4,6},{5,7},{6,4},{7,5},{8,10},{9,11},{10,... | collective-permute-start | bytes 1179656 | tf_op jit(solution)/shard_map/ppermute | solution.py:227
  19.2 13.4 %collective-permute-start.6 = (bf16[192,1024]{1,0:T(8,128)(2,1)S(1)}, bf16[192,1024]{1,0:T(8,128)(2,1)S(1)}, u32[]{:S(2)}, u32[]{:S(2)}) collective-permute-start(bf16[192,1024]{1,0:T(8,128)(2,1)S(1)} %get-tuple-element.159.refs_0_), channel_id=1, source_target_pairs={{0,1},{1,0},{2,3},{3,2},{4,5},{5,4},{6,7},{7,6},{8,9},{9,8},{10,11... | collective-permute-start | bytes 1179656 | tf_op jit(solution)/shard_map/ppermute | solution.py:227
  19.2 9.6 %collective-permute-start.3 = (bf16[96,1024]{1,0:T(8,128)(2,1)S(1)}, bf16[96,1024]{1,0:T(8,128)(2,1)S(1)}, u32[]{:S(2)}, u32[]{:S(2)}) collective-permute-start(bf16[96,1024]{1,0:T(8,128)(2,1)S(1)} %get-tuple-element.144), channel_id=1, source_target_pairs={{0,12},{1,13},{2,14},{3,15},{4,8},{5,9},{6,10},{7,11},{8,4},{9,5},... | collective-permute-start | bytes 589832 | tf_op jit(solution)/shard_map/ppermute | solution.py:227
  21.7 11.0 %collective-permute-start.4 = (bf16[96,1024]{1,0:T(8,128)(2,1)S(1)}, bf16[96,1024]{1,0:T(8,128)(2,1)S(1)}, u32[]{:S(2)}, u32[]{:S(2)}) collective-permute-start(bf16[96,1024]{1,0:T(8,128)(2,1)S(1)} %get-tuple-element.145), channel_id=1, source_target_pairs={{0,4},{1,5},{2,6},{3,7},{4,0},{5,1},{6,2},{7,3},{8,12},{9,13},{10,... | collective-permute-start | bytes 589832 | tf_op jit(solution)/shard_map/ppermute | solution.py:227
  35.2 1.8 %collective-permute-start.7 = (bf16[192,1024]{1,0:T(8,128)(2,1)S(1)}, bf16[192,1024]{1,0:T(8,128)(2,1)S(1)}, u32[]{:S(2)}, u32[]{:S(2)}) collective-permute-start(bf16[192,1024]{1,0:T(8,128)(2,1)S(1)} %get-tuple-element.162), channel_id=1, source_target_pairs={{0,1},{1,0},{2,3},{3,2},{4,5},{5,4},{6,7},{7,6},{8,9},{9,8},{10,11... | collective-permute-start | bytes 1179656 | tf_op jit(solution)/shard_map/ppermute | solution.py:227
  37.1 13.8 %collective-permute-start.10 = (bf16[384,1024]{1,0:T(8,128)(2,1)S(1)}, bf16[384,1024]{1,0:T(8,128)(2,1)S(1)}, u32[]{:S(2)}, u32[]{:S(2)}) collective-permute-start(bf16[384,1024]{1,0:T(8,128)(2,1)S(1)} %pad_maximum_fusion.refs_0_), channel_id=1, source_target_pairs={{0,1},{1,0},{2,3},{3,2},{4,5},{5,4},{6,7},{7,6},{8,9},{9,8},{10,11... | collective-permute-start | bytes 2359304 | tf_op jit(solution)/shard_map/ppermute | solution.py:227
  37.3 13.6 %collective-permute-start.9 = (bf16[192,1024]{1,0:T(8,128)(2,1)S(1)}, bf16[192,1024]{1,0:T(8,128)(2,1)S(1)}, u32[]{:S(2)}, u32[]{:S(2)}) collective-permute-start(bf16[192,1024]{1,0:T(8,128)(2,1)S(1)} %pad_maximum_fusion.6), channel_id=1, source_target_pairs={{0,2},{1,3},{2,0},{3,1},{4,6},{5,7},{6,4},{7,5},{8,10},{9,11},{10,... | collective-permute-start | bytes 1179656 | tf_op jit(solution)/shard_map/ppermute | solution.py:227
  38.9 12.0 %collective-permute-start.8 = (bf16[96,1024]{1,0:T(8,128)(2,1)S(1)}, bf16[96,1024]{1,0:T(8,128)(2,1)S(1)}, u32[]{:S(2)}, u32[]{:S(2)}) collective-permute-start(bf16[96,1024]{1,0:T(8,128)(2,1)S(1)} %get-tuple-element.166), channel_id=1, source_target_pairs={{0,8},{1,9},{2,10},{3,11},{4,12},{5,13},{6,14},{7,15},{8,0},{9,1},... | collective-permute-start | bytes 589832 | tf_op jit(solution)/shard_map/ppermute | solution.py:227
  56.0 2.4 %collective-permute-start.11 = (bf16[384,1024]{1,0:T(8,128)(2,1)S(1)}, bf16[384,1024]{1,0:T(8,128)(2,1)S(1)}, u32[]{:S(2)}, u32[]{:S(2)}) collective-permute-start(bf16[384,1024]{1,0:T(8,128)(2,1)S(1)} %get-tuple-element.181), channel_id=1, source_target_pairs={{0,1},{1,0},{2,3},{3,2},{4,5},{5,4},{6,7},{7,6},{8,9},{9,8},{10,11... | collective-permute-start | bytes 2359304 | tf_op jit(solution)/shard_map/ppermute | solution.py:227
  58.5 11.2 %collective-permute-start.13 = (bf16[192,1024]{1,0:T(8,128)(2,1)S(1)}, bf16[192,1024]{1,0:T(8,128)(2,1)S(1)}, u32[]{:S(2)}, u32[]{:S(2)}) collective-permute-start(bf16[192,1024]{1,0:T(8,128)(2,1)S(1)} %add_convert_fusion.1), channel_id=1, source_target_pairs={{0,2},{1,3},{2,0},{3,1},{4,6},{5,7},{6,4},{7,5},{8,10},{9,11},{10,... | collective-permute-start | bytes 1179656 | tf_op jit(solution)/shard_map/ppermute | solution.py:227
  59.0 10.6 %collective-permute-start.14 = (bf16[192,1024]{1,0:T(8,128)(2,1)S(1)}, bf16[192,1024]{1,0:T(8,128)(2,1)S(1)}, u32[]{:S(2)}, u32[]{:S(2)}) collective-permute-start(bf16[192,1024]{1,0:T(8,128)(2,1)S(1)} %pad_maximum_fusion.5.refs_0_), channel_id=1, source_target_pairs={{0,1},{1,0},{2,3},{3,2},{4,5},{5,4},{6,7},{7,6},{8,9},{9,8},{10,11... | collective-permute-start | bytes 1179656 | tf_op jit(solution)/shard_map/ppermute | solution.py:227
  59.0 9.2 %collective-permute-start.12 = (bf16[96,1024]{1,0:T(8,128)(2,1)S(1)}, bf16[96,1024]{1,0:T(8,128)(2,1)S(1)}, u32[]{:S(2)}, u32[]{:S(2)}) collective-permute-start(bf16[96,1024]{1,0:T(8,128)(2,1)S(1)} %get-tuple-element.188), channel_id=1, source_target_pairs={{0,12},{1,13},{2,14},{3,15},{4,8},{5,9},{6,10},{7,11},{8,4},{9,5},... | collective-permute-start | bytes 589832 | tf_op jit(solution)/shard_map/ppermute | solution.py:227
  72.3 1.8 %collective-permute-start.15 = (bf16[192,1024]{1,0:T(8,128)(2,1)S(1)}, bf16[192,1024]{1,0:T(8,128)(2,1)S(1)}, u32[]{:S(2)}, u32[]{:S(2)}) collective-permute-start(bf16[192,1024]{1,0:T(8,128)(2,1)S(1)} %get-tuple-element.203), channel_id=1, source_target_pairs={{0,1},{1,0},{2,3},{3,2},{4,5},{5,4},{6,7},{7,6},{8,9},{9,8},{10,11... | collective-permute-start | bytes 1179656 | tf_op jit(solution)/shard_map/ppermute | solution.py:227
  74.2 12.6 %collective-permute-start.18 = (bf16[192,1024]{1,0:T(8,128)(2,1)S(1)}, bf16[192,1024]{1,0:T(8,128)(2,1)S(1)}, u32[]{:S(2)}, u32[]{:S(2)}) collective-permute-start(bf16[192,1024]{1,0:T(8,128)(2,1)S(1)} %pad_maximum_fusion.9), channel_id=1, source_target_pairs={{0,2},{1,3},{2,0},{3,1},{4,6},{5,7},{6,4},{7,5},{8,10},{9,11},{10,... | collective-permute-start | bytes 1179656 | tf_op jit(solution)/shard_map/ppermute | solution.py:227
  74.8 10.7 %collective-permute-start.16 = (bf16[96,1024]{1,0:T(8,128)(2,1)S(1)}, bf16[96,1024]{1,0:T(8,128)(2,1)S(1)}, u32[]{:S(2)}, u32[]{:S(2)}) collective-permute-start(bf16[96,1024]{1,0:T(8,128)(2,1)S(1)} %get-tuple-element.215), channel_id=1, source_target_pairs={{0,4},{1,5},{2,6},{3,7},{4,0},{5,1},{6,2},{7,3},{8,12},{9,13},{10,... | collective-permute-start | bytes 589832 | tf_op jit(solution)/shard_map/ppermute | solution.py:227
  75.3 11.5 %collective-permute-start.17 = (bf16[96,1024]{1,0:T(8,128)(2,1)S(1)}, bf16[96,1024]{1,0:T(8,128)(2,1)S(1)}, u32[]{:S(2)}, u32[]{:S(2)}) collective-permute-start(bf16[96,1024]{1,0:T(8,128)(2,1)S(1)} %get-tuple-element.216), channel_id=1, source_target_pairs={{0,8},{1,9},{2,10},{3,11},{4,12},{5,13},{6,14},{7,15},{8,0},{9,1},... | collective-permute-start | bytes 589832 | tf_op jit(solution)/shard_map/ppermute | solution.py:227
  87.0 3.1 %collective-permute-start.21 = (bf16[384,1024]{1,0:T(8,128)(2,1)S(1)}, bf16[384,1024]{1,0:T(8,128)(2,1)S(1)}, u32[]{:S(2)}, u32[]{:S(2)}) collective-permute-start(bf16[384,1024]{1,0:T(8,128)(2,1)S(1)} %pad_maximum_fusion.1), channel_id=1, source_target_pairs={{0,1},{1,0},{2,3},{3,2},{4,5},{5,4},{6,7},{7,6},{8,9},{9,8},{10,11... | collective-permute-start | bytes 2359304 | tf_op jit(solution)/shard_map/ppermute | solution.py:227
  87.2 11.6 %collective-permute-start.20 = (bf16[192,1024]{1,0:T(8,128)(2,1)S(1)}, bf16[192,1024]{1,0:T(8,128)(2,1)S(1)}, u32[]{:S(2)}, u32[]{:S(2)}) collective-permute-start(bf16[192,1024]{1,0:T(8,128)(2,1)S(1)} %pad_maximum_fusion.11), channel_id=1, source_target_pairs={{0,2},{1,3},{2,0},{3,1},{4,6},{5,7},{6,4},{7,5},{8,10},{9,11},{10,... | collective-permute-start | bytes 1179656 | tf_op jit(solution)/shard_map/ppermute | solution.py:227
  88.6 8.9 %collective-permute-start.19 = (bf16[96,1024]{1,0:T(8,128)(2,1)S(1)}, bf16[96,1024]{1,0:T(8,128)(2,1)S(1)}, u32[]{:S(2)}, u32[]{:S(2)}) collective-permute-start(bf16[96,1024]{1,0:T(8,128)(2,1)S(1)} %add_convert_fusion.2), channel_id=1, source_target_pairs={{0,12},{1,13},{2,14},{3,15},{4,8},{5,9},{6,10},{7,11},{8,4},{9,5},... | collective-permute-start | bytes 589832 | tf_op jit(solution)/shard_map/ppermute | solution.py:227
  98.7 1.0 copy-start
  98.7 1.0 copy-start.1
  98.7 1.0 copy-start.2
  98.8 2.4 %collective-permute-start.22 = (bf16[384,1024]{1,0:T(8,128)(2,1)S(1)}, bf16[384,1024]{1,0:T(8,128)(2,1)S(1)}, u32[]{:S(2)}, u32[]{:S(2)}) collective-permute-start(bf16[384,1024]{1,0:T(8,128)(2,1)S(1)} %pad_maximum_fusion.2.refs_2_), channel_id=1, source_target_pairs={{0,1},{1,0},{2,3},{3,2},{4,5},{5,4},{6,7},{7,6},{8,9},{9,8},{10,11... | collective-permute-start | bytes 2359304 | tf_op jit(solution)/shard_map/ppermute | solution.py:227

commit v6 on v5

--- a/solution.py
+++ b/solution.py
@@ -241,7 +241,8 @@
     def land(*earlier):
         names = list(flying)
         values = [flying.pop(name) for name in names]
-        values = lax.optimization_barrier(tuple(values) + earlier)[: len(names)]
+        if earlier:
+            values = lax.optimization_barrier(tuple(values) + earlier)[: len(names)]
         values = through(values, "land", LINK_WORK)
         for name, value in zip(names, values):
             if name[0] != "y":

time: 104 us -> 87.9 us (0.85)
  waiting for transfers between devices: 59.2 us -> 42.6 us
    ppermute x23, waiting for transfers between devices: 59.2 us -> 42.6 us  [swap(): lax.ppermute(value, 'expert', [(i, i ^ mask) for i in range(devices)])]
  transfers between devices with their start and end apart: 23 -> 23, of which waited for: 15 -> 13; matrix products, arithmetic and copies ran while one was open for 0% -> 1% of each run, Pallas kernels for 6% -> 19%
where the time goes in v6:
time: 87.9 us; the launch traced here: 87.8 us
  waiting for transfers between devices  42.6 us (48%)
  Pallas kernels  21.4 us (24%)
  starting transfers between devices  20.8 us (24%)
  between operations  1.09 us (1%)
  other arithmetic  0.99 us (1%)
  local copies, waits for them, and re-layouts  0.9 us (1%)
    ppermute x23, waiting for transfers between devices, swap(): lax.ppermute(value, 'expert', [(i, i ^ mask) for i in range(devices)])  42.6 us
    ppermute x23, starting transfers between devices, swap(): lax.ppermute(value, 'expert', [(i, i ^ mask) for i in range(devices)])  20.8 us
    pallas_call x3, Pallas kernels, ffn(): call(functools.partial(ffn_kernel, len(pieces)), 24, 'ffn', out_shape=[ja...  10.3 us
    pallas_call x1, Pallas kernels, load(): call(load_kernel, 16, 'load', out_shape=[weight, weight, jax.ShapeDtypeSt...  2.88 us
    pallas_call x1, Pallas kernels, last_grad(): call(functools.partial(last_grad_kernel, plan), 24, 'last_grad', out_shap...  2.81 us
    pallas_call x1, Pallas kernels, first_grad(): call(functools.partial(first_grad_kernel, plan), 24, 'first_grad', out_sh...  2.13 us
    pallas_call x1, Pallas kernels, send(): call(functools.partial(send_kernel, experts), 16, 'send', out_shape=[piec...  1.92 us
  transfers between devices with their start and end apart: 23, of which 13 were waited for; matrix products, arithmetic and copies ran while one was open for 1% of the time, Pallas kernels for 19%

profile of v6, /device:TPU:0, one launch (start us, length us, event | category | flops | bytes accessed | tf_op | source)
XLA Modules:
  0.0 87.8 jit_solution(1210682802471188454)
XLA Ops:
  0.6 1.9 %send.1 = (bf16[96,1024]{1,0:T(8,128)(2,1)S(1)}, bf16[96,1024]{1,0:T(8,128)(2,1)S(1)}, bf16[96,1024]{1,0:T(8,128)(2,1)S(1)}, bf16[96,1024]{1,0:T(8,128)(2,1)S(1)...) custom-call(s32[1]{0:T(128)} %bitcast.plane_ref, ...), custom_call_target="tpu_custom_call" | custom-call | tf_op jit(solution)/shard_map/send/pallas_call | solution.py:316
  2.6 3.0 %collective-permute-start.2 = (bf16[192,1024]{1,0:T(8,128)(2,1)S(1)}, bf16[192,1024]{1,0:T(8,128)(2,1)S(1)}, u32[]{:S(2)}, u32[]{:S(2)}) collective-permute-start(bf16[192,1024]{1,0:T(8,128)(2,1)S(1)} %pad_maximum_fusion.4), channel_id=1, source_target_pairs={{0,2},{1,3},{2,0},{3,1},{4,6},{5,7},{6,4},{7,5},{8,10},{9,11},{10,... | collective-permute-start | bytes 1179656 | tf_op jit(solution)/shard_map/ppermute | solution.py:227
  5.6 1.6 %collective-permute-start = (bf16[96,1024]{1,0:T(8,128)(2,1)S(1)}, bf16[96,1024]{1,0:T(8,128)(2,1)S(1)}, u32[]{:S(2)}, u32[]{:S(2)}) collective-permute-start(bf16[96,1024]{1,0:T(8,128)(2,1)S(1)} %get-tuple-element.113), channel_id=1, source_target_pairs={{0,4},{1,5},{2,6},{3,7},{4,0},{5,1},{6,2},{7,3},{8,12},{9,13},{10,... | collective-permute-start | bytes 589832 | tf_op jit(solution)/shard_map/ppermute | solution.py:227
  7.2 2.6 %collective-permute-start.1 = (bf16[96,1024]{1,0:T(8,128)(2,1)S(1)}, bf16[96,1024]{1,0:T(8,128)(2,1)S(1)}, u32[]{:S(2)}, u32[]{:S(2)}) collective-permute-start(bf16[96,1024]{1,0:T(8,128)(2,1)S(1)} %get-tuple-element.114), channel_id=1, source_target_pairs={{0,8},{1,9},{2,10},{3,11},{4,12},{5,13},{6,14},{7,15},{8,0},{9,1},... | collective-permute-start | bytes 589832 | tf_op jit(solution)/shard_map/ppermute | solution.py:227
  9.8 2.9 %load.1 = (bf16[1024,1024]{1,0:T(8,128)(2,1)S(1)}, bf16[1024,1024]{1,0:T(8,128)(2,1)S(1)}, bf16[1024,1024]{1,0:T(8,128)(2,1)S(1)}) custom-call(bf16[1,1024,1024]{2,1,0:T(8,128)(2,1)} %refs_0_.2, bf16[1,1024,1024]{2,1,0:T(8,128)(2,1)} %refs_1_.3, bf16[1,1024,1024]{2,1,0:T(8,128)(2,1)} %refs_2_.1), custom_call_target="tpu_custom_call" | custom-call | tf_op jit(solution)/shard_map/load/pallas_call | solution.py:331
  12.7 3.4 %collective-permute-done.refs_0_ = bf16[96,1024]{1,0:T(8,128)(2,1)S(1)} collective-permute-done((bf16[96,1024]{1,0:T(8,128)(2,1)S(1)}, bf16[96,1024]{1,0:T(8,128)(2,1)S(1)}, u32[]{:S(2)}, u32[]{:S(2)}) %collective-permute-start) | collective-permute-done | bytes 196640 | tf_op jit(solution)/shard_map/ppermute | solution.py:227
  16.1 2.4 %collective-permute-done.1.refs_1_ = bf16[96,1024]{1,0:T(8,128)(2,1)S(1)} collective-permute-done((bf16[96,1024]{1,0:T(8,128)(2,1)S(1)}, bf16[96,1024]{1,0:T(8,128)(2,1)S(1)}, u32[]{:S(2)}, u32[]{:S(2)}) %collective-permute-start.1) | collective-permute-done | bytes 196640 | tf_op jit(solution)/shard_map/ppermute | solution.py:227
  18.7 0.6 collective-permute-start.5
  19.3 2.5 %collective-permute-start.3 = (bf16[96,1024]{1,0:T(8,128)(2,1)S(1)}, bf16[96,1024]{1,0:T(8,128)(2,1)S(1)}, u32[]{:S(2)}, u32[]{:S(2)}) collective-permute-start(bf16[96,1024]{1,0:T(8,128)(2,1)S(1)} %get-tuple-element.128), channel_id=1, source_target_pairs={{0,12},{1,13},{2,14},{3,15},{4,8},{5,9},{6,10},{7,11},{8,4},{9,5},... | collective-permute-start | bytes 589832 | tf_op jit(solution)/shard_map/ppermute | solution.py:227
  21.7 2.6 %ffn.3 = (bf16[1024,384]{1,0:T(8,128)(2,1)S(1)}, bf16[192,1024]{1,0:T(8,128)(2,1)S(1)}, bf16[192,1024]{1,0:T(8,128)(2,1)S(1)}) custom-call(bf16[192,1024]{1,0:T(8,128)(2,1)S(1)} %get-tuple-element.140.refs_0_, bf16[192,1024]{1,0:T(8,128)(2,1)S(1)} %collective-permute-done.6.refs_1_, bf16[1024,1024]{1,0:T(8,128)(2,1)S(1)} %get-tuple-element.170.refs_2_, ...), custom_call_target="tpu_custom_call" | custom-call | tf_op jit(solution)/shard_map/ffn/pallas_call | solution.py:289
  24.4 4.4 %collective-permute-done.3.refs_0_ = bf16[96,1024]{1,0:T(8,128)(2,1)S(1)} collective-permute-done((bf16[96,1024]{1,0:T(8,128)(2,1)S(1)}, bf16[96,1024]{1,0:T(8,128)(2,1)S(1)}, u32[]{:S(2)}, u32[]{:S(2)}) %collective-permute-start.3) | collective-permute-done | bytes 196640 | tf_op jit(solution)/shard_map/ppermute | solution.py:227
  28.9 3.5 %collective-permute-done.4.refs_1_ = bf16[96,1024]{1,0:T(8,128)(2,1)S(1)} collective-permute-done((bf16[96,1024]{1,0:T(8,128)(2,1)S(1)}, bf16[96,1024]{1,0:T(8,128)(2,1)S(1)}, u32[]{:S(2)}, u32[]{:S(2)}) %collective-permute-start.4) | collective-permute-done | bytes 196640 | tf_op jit(solution)/shard_map/ppermute | solution.py:227
  32.6 1.6 %collective-permute-start.9 = (bf16[192,1024]{1,0:T(8,128)(2,1)S(1)}, bf16[192,1024]{1,0:T(8,128)(2,1)S(1)}, u32[]{:S(2)}, u32[]{:S(2)}) collective-permute-start(bf16[192,1024]{1,0:T(8,128)(2,1)S(1)} %pad_maximum_fusion.6), channel_id=1, source_target_pairs={{0,2},{1,3},{2,0},{3,1},{4,6},{5,7},{6,4},{7,5},{8,10},{9,11},{10,... | collective-permute-start | bytes 1179656 | tf_op jit(solution)/shard_map/ppermute | solution.py:227
  34.9 5.1 %ffn.4 = (bf16[1024,768]{1,0:T(8,128)(2,1)S(1)}, bf16[384,1024]{1,0:T(8,128)(2,1)S(1)}, bf16[384,1024]{1,0:T(8,128)(2,1)S(1)}) custom-call(bf16[384,1024]{1,0:T(8,128)(2,1)S(1)} %pad_maximum_fusion.refs_0_, bf16[384,1024]{1,0:T(8,128)(2,1)S(1)} %collective-permute-done.10.refs_1_, bf16[1024,1024]{1,0:T(8,128)(2,1)S(1)} %get-tuple-element.170.refs_2_, ...), custom_call_target="tpu_custom_call" | custom-call | tf_op jit(solution)/shard_map/ffn/pallas_call | solution.py:289
  40.1 6.2 %collective-permute-done.8.refs_0_ = bf16[96,1024]{1,0:T(8,128)(2,1)S(1)} collective-permute-done((bf16[96,1024]{1,0:T(8,128)(2,1)S(1)}, bf16[96,1024]{1,0:T(8,128)(2,1)S(1)}, u32[]{:S(2)}, u32[]{:S(2)}) %collective-permute-start.8) | collective-permute-done | bytes 196640 | tf_op jit(solution)/shard_map/ppermute | solution.py:227
  46.7 0.6 collective-permute-start.13
  47.3 1.5 %collective-permute-start.12 = (bf16[96,1024]{1,0:T(8,128)(2,1)S(1)}, bf16[96,1024]{1,0:T(8,128)(2,1)S(1)}, u32[]{:S(2)}, u32[]{:S(2)}) collective-permute-start(bf16[96,1024]{1,0:T(8,128)(2,1)S(1)} %get-tuple-element.167), channel_id=1, source_target_pairs={{0,12},{1,13},{2,14},{3,15},{4,8},{5,9},{6,10},{7,11},{8,4},{9,5},... | collective-permute-start | bytes 589832 | tf_op jit(solution)/shard_map/ppermute | solution.py:227
  48.7 2.6 %ffn.5 = (bf16[1024,384]{1,0:T(8,128)(2,1)S(1)}, bf16[192,1024]{1,0:T(8,128)(2,1)S(1)}, bf16[192,1024]{1,0:T(8,128)(2,1)S(1)}) custom-call(bf16[192,1024]{1,0:T(8,128)(2,1)S(1)} %pad_maximum_fusion.5.refs_0_, bf16[192,1024]{1,0:T(8,128)(2,1)S(1)} %collective-permute-done.14.refs_1_, bf16[1024,1024]{1,0:T(8,128)(2,1)S(1)} %get-tuple-element.170.refs_2_, ...), custom_call_target="tpu_custom_call" | custom-call | tf_op jit(solution)/shard_map/ffn/pallas_call | solution.py:289
  51.4 4.7 %collective-permute-done.12.refs_0_ = bf16[96,1024]{1,0:T(8,128)(2,1)S(1)} collective-permute-done((bf16[96,1024]{1,0:T(8,128)(2,1)S(1)}, bf16[96,1024]{1,0:T(8,128)(2,1)S(1)}, u32[]{:S(2)}, u32[]{:S(2)}) %collective-permute-start.12) | collective-permute-done | bytes 196640 | tf_op jit(solution)/shard_map/ppermute | solution.py:227
  56.2 2.1 %collective-permute-done.13.refs_1_ = bf16[192,1024]{1,0:T(8,128)(2,1)S(1)} collective-permute-done((bf16[192,1024]{1,0:T(8,128)(2,1)S(1)}, bf16[192,1024]{1,0:T(8,128)(2,1)S(1)}, u32[]{:S(2)}, u32[]{:S(2)}) %collective-permute-start.13) | collective-permute-done | bytes 393248 | tf_op jit(solution)/shard_map/ppermute | solution.py:227
  58.6 0.6 collective-permute-start.18
  59.2 2.0 %collective-permute-start.17 = (bf16[96,1024]{1,0:T(8,128)(2,1)S(1)}, bf16[96,1024]{1,0:T(8,128)(2,1)S(1)}, u32[]{:S(2)}, u32[]{:S(2)}) collective-permute-start(bf16[96,1024]{1,0:T(8,128)(2,1)S(1)} %get-tuple-element.193), channel_id=1, source_target_pairs={{0,8},{1,9},{2,10},{3,11},{4,12},{5,13},{6,14},{7,15},{8,0},{9,1},... | collective-permute-start | bytes 589832 | tf_op jit(solution)/shard_map/ppermute | solution.py:227
  61.2 7.4 %collective-permute-done.16.refs_0_ = bf16[96,1024]{1,0:T(8,128)(2,1)S(1)} collective-permute-done((bf16[96,1024]{1,0:T(8,128)(2,1)S(1)}, bf16[96,1024]{1,0:T(8,128)(2,1)S(1)}, u32[]{:S(2)}, u32[]{:S(2)}) %collective-permute-start.16) | collective-permute-done | bytes 196640 | tf_op jit(solution)/shard_map/ppermute | solution.py:227
  68.6 1.9 %collective-permute-done.17.refs_1_ = bf16[96,1024]{1,0:T(8,128)(2,1)S(1)} collective-permute-done((bf16[96,1024]{1,0:T(8,128)(2,1)S(1)}, bf16[96,1024]{1,0:T(8,128)(2,1)S(1)}, u32[]{:S(2)}, u32[]{:S(2)}) %collective-permute-start.17) | collective-permute-done | bytes 196640 | tf_op jit(solution)/shard_map/ppermute | solution.py:227
  70.8 1.6 %collective-permute-start.20 = (bf16[192,1024]{1,0:T(8,128)(2,1)S(1)}, bf16[192,1024]{1,0:T(8,128)(2,1)S(1)}, u32[]{:S(2)}, u32[]{:S(2)}) collective-permute-start(bf16[192,1024]{1,0:T(8,128)(2,1)S(1)} %pad_maximum_fusion.11), channel_id=1, source_target_pairs={{0,2},{1,3},{2,0},{3,1},{4,6},{5,7},{6,4},{7,5},{8,10},{9,11},{10,... | collective-permute-start | bytes 1179656 | tf_op jit(solution)/shard_map/ppermute | solution.py:227
  72.4 1.5 %collective-permute-start.19 = (bf16[96,1024]{1,0:T(8,128)(2,1)S(1)}, bf16[96,1024]{1,0:T(8,128)(2,1)S(1)}, u32[]{:S(2)}, u32[]{:S(2)}) collective-permute-start(bf16[96,1024]{1,0:T(8,128)(2,1)S(1)} %add_convert_fusion.2), channel_id=1, source_target_pairs={{0,12},{1,13},{2,14},{3,15},{4,8},{5,9},{6,10},{7,11},{8,4},{9,5},... | collective-permute-start | bytes 589832 | tf_op jit(solution)/shard_map/ppermute | solution.py:227
  73.9 2.1 %first_grad.1.first_ref = f32[1024,1024]{1,0:T(8,128)S(1)} custom-call(bf16[1024,384]{1,0:T(8,128)(2,1)S(1)} %get-tuple-element.202.refs_0_, bf16[1024,768]{1,0:T(8,128)(2,1)S(1)} %get-tuple-element.221.refs_1_.refs_0_, bf16[192,1024]{1,0:T(8,128)(2,1)S(1)} %get-tuple-element.201.refs_2_, bf16[192,1024]{1,0:T(8,128)(2,1)S(1)} %pad_maximum_fusion.10.refs_3_, ...), custom_call_target="tpu_custom_call" | custom-call | tf_op jit(solution)/shard_map/first_grad/pallas_call | solution.py:368
  76.0 5.3 %collective-permute-done.19.refs_0_ = bf16[96,1024]{1,0:T(8,128)(2,1)S(1)} collective-permute-done((bf16[96,1024]{1,0:T(8,128)(2,1)S(1)}, bf16[96,1024]{1,0:T(8,128)(2,1)S(1)}, u32[]{:S(2)}, u32[]{:S(2)}) %collective-permute-start.19) | collective-permute-done | bytes 196640 | tf_op jit(solution)/shard_map/ppermute | solution.py:227
  81.3 1.1 %collective-permute-done.20.refs_1_ = bf16[192,1024]{1,0:T(8,128)(2,1)S(1)} collective-permute-done((bf16[192,1024]{1,0:T(8,128)(2,1)S(1)}, bf16[192,1024]{1,0:T(8,128)(2,1)S(1)}, u32[]{:S(2)}, u32[]{:S(2)}) %collective-permute-start.20) | collective-permute-done | bytes 393248 | tf_op jit(solution)/shard_map/ppermute | solution.py:227
  82.6 0.8 copy-done
  83.4 1.4 %combine.1 = bf16[128,1024]{1,0:T(8,128)(2,1)} custom-call(s32[1]{0:T(128)} %bitcast.plane_ref, bf16[128,1024]{1,0:T(8,128)(2,1)S(1)} %copy-done, s32[2,128]{1,0:T(2,128)S(1)} %bitcast.5, s32[2,128]{1,0:T(2,128)S(1)} %bitcast.7, bf16[96,1024]{1,0:T(8,128)(2,1)S(1)} %add_convert_fusion.4.refs_0_, bf16[96,1024]{1,0:T(8,128)(2,1)S(1)} %get-tuple-element.217.refs_1_, ...), custom_call_target="tpu_custom_call" | custom-call | tf_op jit(solution)/shard_map/combine/pallas_call | solution.py:439
  84.8 2.8 %last_grad.1 = bf16[1,1024,1024]{2,1,0:T(8,128)(2,1)} custom-call(f32[1024,1024]{1,0:T(8,128)S(1)} %first_grad.1.first_ref, bf16[1024,768]{1,0:T(8,128)(2,1)S(1)} %get-tuple-element.221.refs_1_.refs_0_, bf16[1024,384]{1,0:T(8,128)(2,1)S(1)} %get-tuple-element.222.refs_1_, bf16[384,1024]{1,0:T(8,128)(2,1)S(1)} %pad_maximum_fusion.2.refs_2_, ...), custom_call_target="tpu_custom_call" | custom-call | tf_op jit(solution)/shard_map/last_grad/pallas_call | solution.py:380
  (55 shorter events, 2.6 us)
Async XLA Ops:
  2.6 15.9 %collective-permute-start.2 = (bf16[192,1024]{1,0:T(8,128)(2,1)S(1)}, bf16[192,1024]{1,0:T(8,128)(2,1)S(1)}, u32[]{:S(2)}, u32[]{:S(2)}) collective-permute-start(bf16[192,1024]{1,0:T(8,128)(2,1)S(1)} %pad_maximum_fusion.4), channel_id=1, source_target_pairs={{0,2},{1,3},{2,0},{3,1},{4,6},{5,7},{6,4},{7,5},{8,10},{9,11},{10,... | collective-permute-start | bytes 1179656 | tf_op jit(solution)/shard_map/ppermute | solution.py:227
  5.6 10.5 %collective-permute-start = (bf16[96,1024]{1,0:T(8,128)(2,1)S(1)}, bf16[96,1024]{1,0:T(8,128)(2,1)S(1)}, u32[]{:S(2)}, u32[]{:S(2)}) collective-permute-start(bf16[96,1024]{1,0:T(8,128)(2,1)S(1)} %get-tuple-element.113), channel_id=1, source_target_pairs={{0,4},{1,5},{2,6},{3,7},{4,0},{5,1},{6,2},{7,3},{8,12},{9,13},{10,... | collective-permute-start | bytes 589832 | tf_op jit(solution)/shard_map/ppermute | solution.py:227
  7.2 11.2 %collective-permute-start.1 = (bf16[96,1024]{1,0:T(8,128)(2,1)S(1)}, bf16[96,1024]{1,0:T(8,128)(2,1)S(1)}, u32[]{:S(2)}, u32[]{:S(2)}) collective-permute-start(bf16[96,1024]{1,0:T(8,128)(2,1)S(1)} %get-tuple-element.114), channel_id=1, source_target_pairs={{0,8},{1,9},{2,10},{3,11},{4,12},{5,13},{6,14},{7,15},{8,0},{9,1},... | collective-permute-start | bytes 589832 | tf_op jit(solution)/shard_map/ppermute | solution.py:227
  18.6 3.2 %collective-permute-start.6 = (bf16[192,1024]{1,0:T(8,128)(2,1)S(1)}, bf16[192,1024]{1,0:T(8,128)(2,1)S(1)}, u32[]{:S(2)}, u32[]{:S(2)}) collective-permute-start(bf16[192,1024]{1,0:T(8,128)(2,1)S(1)} %get-tuple-element.140.refs_0_), channel_id=1, source_target_pairs={{0,1},{1,0},{2,3},{3,2},{4,5},{5,4},{6,7},{7,6},{8,9},{9,8},{10,11... | collective-permute-start | bytes 1179656 | tf_op jit(solution)/shard_map/ppermute | solution.py:227
  18.7 13.7 %collective-permute-start.5 = (bf16[192,1024]{1,0:T(8,128)(2,1)S(1)}, bf16[192,1024]{1,0:T(8,128)(2,1)S(1)}, u32[]{:S(2)}, u32[]{:S(2)}) collective-permute-start(bf16[192,1024]{1,0:T(8,128)(2,1)S(1)} %pad_maximum_fusion.8), channel_id=1, source_target_pairs={{0,2},{1,3},{2,0},{3,1},{4,6},{5,7},{6,4},{7,5},{8,10},{9,11},{10,... | collective-permute-start | bytes 1179656 | tf_op jit(solution)/shard_map/ppermute | solution.py:227
  19.3 9.6 %collective-permute-start.3 = (bf16[96,1024]{1,0:T(8,128)(2,1)S(1)}, bf16[96,1024]{1,0:T(8,128)(2,1)S(1)}, u32[]{:S(2)}, u32[]{:S(2)}) collective-permute-start(bf16[96,1024]{1,0:T(8,128)(2,1)S(1)} %get-tuple-element.128), channel_id=1, source_target_pairs={{0,12},{1,13},{2,14},{3,15},{4,8},{5,9},{6,10},{7,11},{8,4},{9,5},... | collective-permute-start | bytes 589832 | tf_op jit(solution)/shard_map/ppermute | solution.py:227
  21.7 10.7 %collective-permute-start.4 = (bf16[96,1024]{1,0:T(8,128)(2,1)S(1)}, bf16[96,1024]{1,0:T(8,128)(2,1)S(1)}, u32[]{:S(2)}, u32[]{:S(2)}) collective-permute-start(bf16[96,1024]{1,0:T(8,128)(2,1)S(1)} %get-tuple-element.129), channel_id=1, source_target_pairs={{0,4},{1,5},{2,6},{3,7},{4,0},{5,1},{6,2},{7,3},{8,12},{9,13},{10,... | collective-permute-start | bytes 589832 | tf_op jit(solution)/shard_map/ppermute | solution.py:227
  24.4 8.1 %collective-permute-start.7 = (bf16[192,1024]{1,0:T(8,128)(2,1)S(1)}, bf16[192,1024]{1,0:T(8,128)(2,1)S(1)}, u32[]{:S(2)}, u32[]{:S(2)}) collective-permute-start(bf16[192,1024]{1,0:T(8,128)(2,1)S(1)} %get-tuple-element.143), channel_id=1, source_target_pairs={{0,1},{1,0},{2,3},{3,2},{4,5},{5,4},{6,7},{7,6},{8,9},{9,8},{10,11... | collective-permute-start | bytes 1179656 | tf_op jit(solution)/shard_map/ppermute | solution.py:227
  32.5 2.4 %collective-permute-start.10 = (bf16[384,1024]{1,0:T(8,128)(2,1)S(1)}, bf16[384,1024]{1,0:T(8,128)(2,1)S(1)}, u32[]{:S(2)}, u32[]{:S(2)}) collective-permute-start(bf16[384,1024]{1,0:T(8,128)(2,1)S(1)} %pad_maximum_fusion.refs_0_), channel_id=1, source_target_pairs={{0,1},{1,0},{2,3},{3,2},{4,5},{5,4},{6,7},{7,6},{8,9},{9,8},{10,11... | collective-permute-start | bytes 2359304 | tf_op jit(solution)/shard_map/ppermute | solution.py:227
  32.6 13.7 %collective-permute-start.9 = (bf16[192,1024]{1,0:T(8,128)(2,1)S(1)}, bf16[192,1024]{1,0:T(8,128)(2,1)S(1)}, u32[]{:S(2)}, u32[]{:S(2)}) collective-permute-start(bf16[192,1024]{1,0:T(8,128)(2,1)S(1)} %pad_maximum_fusion.6), channel_id=1, source_target_pairs={{0,2},{1,3},{2,0},{3,1},{4,6},{5,7},{6,4},{7,5},{8,10},{9,11},{10,... | collective-permute-start | bytes 1179656 | tf_op jit(solution)/shard_map/ppermute | solution.py:227
  34.2 12.1 %collective-permute-start.8 = (bf16[96,1024]{1,0:T(8,128)(2,1)S(1)}, bf16[96,1024]{1,0:T(8,128)(2,1)S(1)}, u32[]{:S(2)}, u32[]{:S(2)}) collective-permute-start(bf16[96,1024]{1,0:T(8,128)(2,1)S(1)} %get-tuple-element.147), channel_id=1, source_target_pairs={{0,8},{1,9},{2,10},{3,11},{4,12},{5,13},{6,14},{7,15},{8,0},{9,1},... | collective-permute-start | bytes 589832 | tf_op jit(solution)/shard_map/ppermute | solution.py:227
  39.9 6.6 %collective-permute-start.11 = (bf16[384,1024]{1,0:T(8,128)(2,1)S(1)}, bf16[384,1024]{1,0:T(8,128)(2,1)S(1)}, u32[]{:S(2)}, u32[]{:S(2)}) collective-permute-start(bf16[384,1024]{1,0:T(8,128)(2,1)S(1)} %get-tuple-element.160), channel_id=1, source_target_pairs={{0,1},{1,0},{2,3},{3,2},{4,5},{5,4},{6,7},{7,6},{8,9},{9,8},{10,11... | collective-permute-start | bytes 2359304 | tf_op jit(solution)/shard_map/ppermute | solution.py:227
  46.6 2.1 %collective-permute-start.14 = (bf16[192,1024]{1,0:T(8,128)(2,1)S(1)}, bf16[192,1024]{1,0:T(8,128)(2,1)S(1)}, u32[]{:S(2)}, u32[]{:S(2)}) collective-permute-start(bf16[192,1024]{1,0:T(8,128)(2,1)S(1)} %pad_maximum_fusion.5.refs_0_), channel_id=1, source_target_pairs={{0,1},{1,0},{2,3},{3,2},{4,5},{5,4},{6,7},{7,6},{8,9},{9,8},{10,11... | collective-permute-start | bytes 1179656 | tf_op jit(solution)/shard_map/ppermute | solution.py:227
  46.7 11.5 %collective-permute-start.13 = (bf16[192,1024]{1,0:T(8,128)(2,1)S(1)}, bf16[192,1024]{1,0:T(8,128)(2,1)S(1)}, u32[]{:S(2)}, u32[]{:S(2)}) collective-permute-start(bf16[192,1024]{1,0:T(8,128)(2,1)S(1)} %add_convert_fusion.1), channel_id=1, source_target_pairs={{0,2},{1,3},{2,0},{3,1},{4,6},{5,7},{6,4},{7,5},{8,10},{9,11},{10,... | collective-permute-start | bytes 1179656 | tf_op jit(solution)/shard_map/ppermute | solution.py:227
  47.3 8.9 %collective-permute-start.12 = (bf16[96,1024]{1,0:T(8,128)(2,1)S(1)}, bf16[96,1024]{1,0:T(8,128)(2,1)S(1)}, u32[]{:S(2)}, u32[]{:S(2)}) collective-permute-start(bf16[96,1024]{1,0:T(8,128)(2,1)S(1)} %get-tuple-element.167), channel_id=1, source_target_pairs={{0,12},{1,13},{2,14},{3,15},{4,8},{5,9},{6,10},{7,11},{8,4},{9,5},... | collective-permute-start | bytes 589832 | tf_op jit(solution)/shard_map/ppermute | solution.py:227
  51.4 7.1 %collective-permute-start.15 = (bf16[192,1024]{1,0:T(8,128)(2,1)S(1)}, bf16[192,1024]{1,0:T(8,128)(2,1)S(1)}, u32[]{:S(2)}, u32[]{:S(2)}) collective-permute-start(bf16[192,1024]{1,0:T(8,128)(2,1)S(1)} %get-tuple-element.180), channel_id=1, source_target_pairs={{0,1},{1,0},{2,3},{3,2},{4,5},{5,4},{6,7},{7,6},{8,9},{9,8},{10,11... | collective-permute-start | bytes 1179656 | tf_op jit(solution)/shard_map/ppermute | solution.py:227
  58.6 11.9 %collective-permute-start.18 = (bf16[192,1024]{1,0:T(8,128)(2,1)S(1)}, bf16[192,1024]{1,0:T(8,128)(2,1)S(1)}, u32[]{:S(2)}, u32[]{:S(2)}) collective-permute-start(bf16[192,1024]{1,0:T(8,128)(2,1)S(1)} %pad_maximum_fusion.9), channel_id=1, source_target_pairs={{0,2},{1,3},{2,0},{3,1},{4,6},{5,7},{6,4},{7,5},{8,10},{9,11},{10,... | collective-permute-start | bytes 1179656 | tf_op jit(solution)/shard_map/ppermute | solution.py:227
  59.2 9.5 %collective-permute-start.16 = (bf16[96,1024]{1,0:T(8,128)(2,1)S(1)}, bf16[96,1024]{1,0:T(8,128)(2,1)S(1)}, u32[]{:S(2)}, u32[]{:S(2)}) collective-permute-start(bf16[96,1024]{1,0:T(8,128)(2,1)S(1)} %get-tuple-element.192), channel_id=1, source_target_pairs={{0,4},{1,5},{2,6},{3,7},{4,0},{5,1},{6,2},{7,3},{8,12},{9,13},{10,... | collective-permute-start | bytes 589832 | tf_op jit(solution)/shard_map/ppermute | solution.py:227
  59.2 11.3 %collective-permute-start.17 = (bf16[96,1024]{1,0:T(8,128)(2,1)S(1)}, bf16[96,1024]{1,0:T(8,128)(2,1)S(1)}, u32[]{:S(2)}, u32[]{:S(2)}) collective-permute-start(bf16[96,1024]{1,0:T(8,128)(2,1)S(1)} %get-tuple-element.193), channel_id=1, source_target_pairs={{0,8},{1,9},{2,10},{3,11},{4,12},{5,13},{6,14},{7,15},{8,0},{9,1},... | collective-permute-start | bytes 589832 | tf_op jit(solution)/shard_map/ppermute | solution.py:227
  70.7 3.2 %collective-permute-start.21 = (bf16[384,1024]{1,0:T(8,128)(2,1)S(1)}, bf16[384,1024]{1,0:T(8,128)(2,1)S(1)}, u32[]{:S(2)}, u32[]{:S(2)}) collective-permute-start(bf16[384,1024]{1,0:T(8,128)(2,1)S(1)} %pad_maximum_fusion.1), channel_id=1, source_target_pairs={{0,1},{1,0},{2,3},{3,2},{4,5},{5,4},{6,7},{7,6},{8,9},{9,8},{10,11... | collective-permute-start | bytes 2359304 | tf_op jit(solution)/shard_map/ppermute | solution.py:227
  70.8 11.6 %collective-permute-start.20 = (bf16[192,1024]{1,0:T(8,128)(2,1)S(1)}, bf16[192,1024]{1,0:T(8,128)(2,1)S(1)}, u32[]{:S(2)}, u32[]{:S(2)}) collective-permute-start(bf16[192,1024]{1,0:T(8,128)(2,1)S(1)} %pad_maximum_fusion.11), channel_id=1, source_target_pairs={{0,2},{1,3},{2,0},{3,1},{4,6},{5,7},{6,4},{7,5},{8,10},{9,11},{10,... | collective-permute-start | bytes 1179656 | tf_op jit(solution)/shard_map/ppermute | solution.py:227
  72.4 8.9 %collective-permute-start.19 = (bf16[96,1024]{1,0:T(8,128)(2,1)S(1)}, bf16[96,1024]{1,0:T(8,128)(2,1)S(1)}, u32[]{:S(2)}, u32[]{:S(2)}) collective-permute-start(bf16[96,1024]{1,0:T(8,128)(2,1)S(1)} %add_convert_fusion.2), channel_id=1, source_target_pairs={{0,12},{1,13},{2,14},{3,15},{4,8},{5,9},{6,10},{7,11},{8,4},{9,5},... | collective-permute-start | bytes 589832 | tf_op jit(solution)/shard_map/ppermute | solution.py:227
  82.4 1.0 %copy-start = (bf16[128,1024]{1,0:T(8,128)(2,1)S(1)}, bf16[128,1024]{1,0:T(8,128)(2,1)}, u32[]{:S(2)}) copy-start(bf16[128,1024]{1,0:T(8,128)(2,1)} %tokens_ref.1) | copy-start | bytes 786436
  82.4 1.0 %copy-start.1 = (s32[128,2]{0,1:T(2,128)S(1)}, s32[128,2]{0,1:T(2,128)}, u32[]{:S(2)}) copy-start(s32[128,2]{0,1:T(2,128)} %param.10) | copy-start | bytes 3076
  82.4 1.0 %copy-start.2 = (s32[128,2]{0,1:T(2,128)S(1)}, s32[128,2]{0,1:T(2,128)}, u32[]{:S(2)}) copy-start(s32[128,2]{0,1:T(2,128)} %param.11) | copy-start | bytes 3076
  82.5 2.4 %collective-permute-start.22 = (bf16[384,1024]{1,0:T(8,128)(2,1)S(1)}, bf16[384,1024]{1,0:T(8,128)(2,1)S(1)}, u32[]{:S(2)}, u32[]{:S(2)}) collective-permute-start(bf16[384,1024]{1,0:T(8,128)(2,1)S(1)} %pad_maximum_fusion.2.refs_2_), channel_id=1, source_target_pairs={{0,1},{1,0},{2,3},{3,2},{4,5},{5,4},{6,7},{7,6},{8,9},{9,8},{10,11... | collective-permute-start | bytes 2359304 | tf_op jit(solution)/shard_map/ppermute | solution.py:227

commit v7 on v6

--- a/solution.py
+++ b/solution.py
@@ -35,7 +35,8 @@
 
 
 def experts_of(plane, experts, rows):
-    return lax.broadcasted_iota(jnp.int32, (experts, rows), 0) ^ plane
+    ahead = lax.broadcasted_iota(jnp.int32, (experts, rows), 0) + plane
+    return jnp.where(ahead >= experts, ahead - experts, ahead)
 
 
 def placing_of(routes, plane, experts, capacity):
@@ -214,7 +215,8 @@
     capacity = HSPLIT * (3 * top_count * rows_here // (2 * experts * HSPLIT))
     capacity = -(-capacity // 16) * 16
     shifts = max(1, experts // GROUPS)
-    groups = [list(range(g, g + shifts)) for g in range(0, experts, shifts)]
+    turns = sorted(range(experts), key=lambda s: (min(s, experts - s), s))
+    groups = [turns[g : g + shifts] for g in range(0, experts, shifts)]
     height = shifts * capacity
     plane = (lax.axis_index("expert") // HSPLIT).astype(jnp.int32).reshape(1)
     routes, gate_nums, gain = routes.T, gate_nums.T, gain.reshape(1, -1)
@@ -226,6 +228,10 @@
     def swap(value, mask):
         return lax.ppermute(value, "expert", [(i, i ^ mask) for i in range(devices)])
 
+    def turn(value, steps):
+        to = [(i, (i + steps * HSPLIT) % devices) for i in range(devices)]
+        return lax.ppermute(value, "expert", to)
+
     def sync():
         values = lax.optimization_barrier(tuple(live.values()))
         live.update(zip(list(live), values))
@@ -234,9 +240,6 @@
         return parts[0] if len(parts) == 1 else jnp.concatenate(parts, 0)
 
     flying = {}
-
-    def launch(name, value, mask):
-        flying[name] = swap(value, mask)
 
     def land(*earlier):
         names = list(flying)
@@ -267,7 +270,7 @@
     def across(kind, *gs):
         for s in [s for g in gs for s in groups[g]]:
             if s:
-                launch((kind, s), live[kind, s], s * HSPLIT)
+                flying[kind, s] = turn(live[kind, s], -s if kind == "R" else s)
 
     def along(*items):
         for kind, gs in items:
@@ -276,7 +279,7 @@
             else:
                 value = join([live.pop((kind, s)) for g in gs for s in groups[g]])
             live["sent", kind, gs] = value
-        launch(("y",) + items, join([live["sent", kind, gs] for kind, gs in items]), 2)
+        flying[("y",) + items] = swap(join([live["sent", kind, gs] for kind, gs in items]), 2)
 
     def core(kind, *tuples):
         gs = tuple(g for part in tuples for g in part)
@@ -336,7 +339,7 @@
             in_specs=[anywhere] * 3,
             out_specs=whole(3),
             scratch_shapes=[pltpu.SemaphoreType.DMA((3,))],
-        )(*in_hbm(after(w_gate, live["C", experts - 1]), w_up, w_down))
+        )(*in_hbm(after(w_gate, live["C", groups[-1][-1]]), w_up, w_down))
         live.update({("w", i): value for i, value in enumerate(values)})
 
     def grad_call(turned, pieces):
@@ -401,14 +404,13 @@
     land()
     sync()
     across("N", 3)
-    across("C", 1)
     along(("N", (1, 2)))
     core("N", (0,))
     ffn(0)
     cross(0)
     fold_core(land(), 0)
     sync()
-    across("C", 2)
+    across("C", 1, 2)
     along(("N", (3,)), ("fold", (0,)))
     core("N", (1, 2))
     ffn(1, 2)

time: 87.9 us -> 88.2 us (level)
  starting transfers between devices: 20.8 us -> 23.3 us
  waiting for transfers between devices: 42.6 us -> 40.5 us
    ppermute x23 -> x14, waiting for transfers between devices: 42.6 us -> 0.59 us  [swap(): lax.ppermute(value, 'expert', [(i, i ^ mask) for i in range(devices)])]
    ppermute x0 -> x9, waiting for transfers between devices: none -> 39.9 us  [turn(): return lax.ppermute(value, 'expert', to)]
    ppermute x0 -> x9, starting transfers between devices: none -> 14.2 us  [turn(): return lax.ppermute(value, 'expert', to)]
    ppermute x23 -> x14, starting transfers between devices: 20.8 us -> 9.07 us  [swap(): lax.ppermute(value, 'expert', [(i, i ^ mask) for i in range(devices)])]
  transfers between devices with their start and end apart: 23 -> 23, of which waited for: 13 -> 11; matrix products, arithmetic and copies ran while one was open for 1% -> 1% of each run, Pallas kernels for 19% -> 19%
where the time goes in v7:
time: 88.2 us; the launch traced here: 88 us
  waiting for transfers between devices  40.5 us (46%)
  starting transfers between devices  23.3 us (26%)
  Pallas kernels  21.2 us (24%)
  between operations  1.12 us (1%)
  other arithmetic  0.99 us (1%)
  local copies, waits for them, and re-layouts  0.89 us (1%)
    ppermute x9, waiting for transfers between devices, turn(): return lax.ppermute(value, 'expert', to)  39.9 us
    ppermute x9, starting transfers between devices, turn(): return lax.ppermute(value, 'expert', to)  14.2 us
    pallas_call x3, Pallas kernels, ffn(): call(functools.partial(ffn_kernel, len(pieces)), 24, 'ffn', out_shape=[ja...  10.3 us
    ppermute x14, starting transfers between devices, swap(): lax.ppermute(value, 'expert', [(i, i ^ mask) for i in range(devices)])  9.07 us
    pallas_call x1, Pallas kernels, load(): call(load_kernel, 16, 'load', out_shape=[weight, weight, jax.ShapeDtypeSt...  2.88 us
    pallas_call x1, Pallas kernels, last_grad(): call(functools.partial(last_grad_kernel, plan), 24, 'last_grad', out_shap...  2.81 us
    pallas_call x1, Pallas kernels, first_grad(): call(functools.partial(first_grad_kernel, plan), 24, 'first_grad', out_sh...  1.95 us
    pallas_call x1, Pallas kernels, send(): call(functools.partial(send_kernel, experts), 16, 'send', out_shape=[piec...  1.92 us
  transfers between devices with their start and end apart: 23, of which 11 were waited for; matrix products, arithmetic and copies ran while one was open for 1% of the time, Pallas kernels for 19%

profile of v7, /device:TPU:0, one launch (start us, length us, event | category | flops | bytes accessed | tf_op | source)
XLA Modules:
  0.0 88.0 jit_solution(6764077270495244088)
XLA Ops:
  0.6 1.9 %send.1 = (bf16[96,1024]{1,0:T(8,128)(2,1)S(1)}, bf16[96,1024]{1,0:T(8,128)(2,1)S(1)}, bf16[96,1024]{1,0:T(8,128)(2,1)S(1)}, bf16[96,1024]{1,0:T(8,128)(2,1)S(1)...) custom-call(s32[1]{0:T(128)} %bitcast.plane_ref, ...), custom_call_target="tpu_custom_call" | custom-call | tf_op jit(solution)/shard_map/send/pallas_call | solution.py:319
  2.6 3.0 %collective-permute-start.2 = (bf16[192,1024]{1,0:T(8,128)(2,1)S(1)}, bf16[192,1024]{1,0:T(8,128)(2,1)S(1)}, u32[]{:S(2)}, u32[]{:S(2)}) collective-permute-start(bf16[192,1024]{1,0:T(8,128)(2,1)S(1)} %pad_maximum_fusion.4), channel_id=1, source_target_pairs={{0,2},{1,3},{2,0},{3,1},{4,6},{5,7},{6,4},{7,5},{8,10},{9,11},{10,... | collective-permute-start | bytes 1179656 | tf_op jit(solution)/shard_map/ppermute | solution.py:229
  5.6 1.6 %collective-permute-start = (bf16[96,1024]{1,0:T(8,128)(2,1)S(1)}, bf16[96,1024]{1,0:T(8,128)(2,1)S(1)}, u32[]{:S(2)}, u32[]{:S(2)}) collective-permute-start(bf16[96,1024]{1,0:T(8,128)(2,1)S(1)} %get-tuple-element.113), channel_id=1, source_target_pairs={{0,4},{1,5},{2,6},{3,7},{4,8},{5,9},{6,10},{7,11},{8,12},{9,13},{1... | collective-permute-start | bytes 589832 | tf_op jit(solution)/shard_map/ppermute | solution.py:233
  7.2 2.2 %collective-permute-start.1 = (bf16[96,1024]{1,0:T(8,128)(2,1)S(1)}, bf16[96,1024]{1,0:T(8,128)(2,1)S(1)}, u32[]{:S(2)}, u32[]{:S(2)}) collective-permute-start(bf16[96,1024]{1,0:T(8,128)(2,1)S(1)} %get-tuple-element.114), channel_id=1, source_target_pairs={{0,12},{1,13},{2,14},{3,15},{4,0},{5,1},{6,2},{7,3},{8,4},{9,5},{1... | collective-permute-start | bytes 589832 | tf_op jit(solution)/shard_map/ppermute | solution.py:233
  9.5 2.9 %load.1 = (bf16[1024,1024]{1,0:T(8,128)(2,1)S(1)}, bf16[1024,1024]{1,0:T(8,128)(2,1)S(1)}, bf16[1024,1024]{1,0:T(8,128)(2,1)S(1)}) custom-call(bf16[1,1024,1024]{2,1,0:T(8,128)(2,1)} %refs_0_.2, bf16[1,1024,1024]{2,1,0:T(8,128)(2,1)} %refs_1_.3, bf16[1,1024,1024]{2,1,0:T(8,128)(2,1)} %refs_2_.1), custom_call_target="tpu_custom_call" | custom-call | tf_op jit(solution)/shard_map/load/pallas_call | solution.py:334
  12.4 2.9 %collective-permute-done.refs_0_ = bf16[96,1024]{1,0:T(8,128)(2,1)S(1)} collective-permute-done((bf16[96,1024]{1,0:T(8,128)(2,1)S(1)}, bf16[96,1024]{1,0:T(8,128)(2,1)S(1)}, u32[]{:S(2)}, u32[]{:S(2)}) %collective-permute-start) | collective-permute-done | bytes 196640 | tf_op jit(solution)/shard_map/ppermute | solution.py:233
  15.3 2.2 %collective-permute-done.1.refs_1_ = bf16[96,1024]{1,0:T(8,128)(2,1)S(1)} collective-permute-done((bf16[96,1024]{1,0:T(8,128)(2,1)S(1)}, bf16[96,1024]{1,0:T(8,128)(2,1)S(1)}, u32[]{:S(2)}, u32[]{:S(2)}) %collective-permute-start.1) | collective-permute-done | bytes 196640 | tf_op jit(solution)/shard_map/ppermute | solution.py:233
  17.7 0.6 collective-permute-start.4
  18.3 1.3 %collective-permute-start.3 = (bf16[96,1024]{1,0:T(8,128)(2,1)S(1)}, bf16[96,1024]{1,0:T(8,128)(2,1)S(1)}, u32[]{:S(2)}, u32[]{:S(2)}) collective-permute-start(bf16[96,1024]{1,0:T(8,128)(2,1)S(1)} %get-tuple-element.128), channel_id=1, source_target_pairs={{0,8},{1,9},{2,10},{3,11},{4,12},{5,13},{6,14},{7,15},{8,0},{9,1},... | collective-permute-start | bytes 589832 | tf_op jit(solution)/shard_map/ppermute | solution.py:233
  19.6 2.6 %ffn.3 = (bf16[1024,384]{1,0:T(8,128)(2,1)S(1)}, bf16[192,1024]{1,0:T(8,128)(2,1)S(1)}, bf16[192,1024]{1,0:T(8,128)(2,1)S(1)}) custom-call(bf16[192,1024]{1,0:T(8,128)(2,1)S(1)} %get-tuple-element.139.refs_0_, bf16[192,1024]{1,0:T(8,128)(2,1)S(1)} %collective-permute-done.5.refs_1_, bf16[1024,1024]{1,0:T(8,128)(2,1)S(1)} %get-tuple-element.170.refs_2_, ...), custom_call_target="tpu_custom_call" | custom-call | tf_op jit(solution)/shard_map/ffn/pallas_call | solution.py:292
  22.3 8.1 %collective-permute-done.3.refs_0_ = bf16[96,1024]{1,0:T(8,128)(2,1)S(1)} collective-permute-done((bf16[96,1024]{1,0:T(8,128)(2,1)S(1)}, bf16[96,1024]{1,0:T(8,128)(2,1)S(1)}, u32[]{:S(2)}, u32[]{:S(2)}) %collective-permute-start.3) | collective-permute-done | bytes 196640 | tf_op jit(solution)/shard_map/ppermute | solution.py:233
  30.7 1.6 %collective-permute-start.9 = (bf16[192,1024]{1,0:T(8,128)(2,1)S(1)}, bf16[192,1024]{1,0:T(8,128)(2,1)S(1)}, u32[]{:S(2)}, u32[]{:S(2)}) collective-permute-start(bf16[192,1024]{1,0:T(8,128)(2,1)S(1)} %pad_maximum_fusion.6), channel_id=1, source_target_pairs={{0,2},{1,3},{2,0},{3,1},{4,6},{5,7},{6,4},{7,5},{8,10},{9,11},{10,... | collective-permute-start | bytes 1179656 | tf_op jit(solution)/shard_map/ppermute | solution.py:229
  32.3 3.8 %collective-permute-start.8 = (bf16[96,1024]{1,0:T(8,128)(2,1)S(1)}, bf16[96,1024]{1,0:T(8,128)(2,1)S(1)}, u32[]{:S(2)}, u32[]{:S(2)}) collective-permute-start(bf16[96,1024]{1,0:T(8,128)(2,1)S(1)} %get-tuple-element.146), channel_id=1, source_target_pairs={{0,12},{1,13},{2,14},{3,15},{4,0},{5,1},{6,2},{7,3},{8,4},{9,5},{1... | collective-permute-start | bytes 589832 | tf_op jit(solution)/shard_map/ppermute | solution.py:233
  36.1 5.0 %ffn.4 = (bf16[1024,768]{1,0:T(8,128)(2,1)S(1)}, bf16[384,1024]{1,0:T(8,128)(2,1)S(1)}, bf16[384,1024]{1,0:T(8,128)(2,1)S(1)}) custom-call(bf16[384,1024]{1,0:T(8,128)(2,1)S(1)} %pad_maximum_fusion.refs_0_, bf16[384,1024]{1,0:T(8,128)(2,1)S(1)} %collective-permute-done.10.refs_1_, bf16[1024,1024]{1,0:T(8,128)(2,1)S(1)} %get-tuple-element.170.refs_2_, ...), custom_call_target="tpu_custom_call" | custom-call | tf_op jit(solution)/shard_map/ffn/pallas_call | solution.py:292
  41.2 0.6 collective-permute-done.7.refs_0_
  41.9 1.6 %collective-permute-done.8.refs_1_ = bf16[96,1024]{1,0:T(8,128)(2,1)S(1)} collective-permute-done((bf16[96,1024]{1,0:T(8,128)(2,1)S(1)}, bf16[96,1024]{1,0:T(8,128)(2,1)S(1)}, u32[]{:S(2)}, u32[]{:S(2)}) %collective-permute-start.8) | collective-permute-done | bytes 196640 | tf_op jit(solution)/shard_map/ppermute | solution.py:233
  43.9 0.6 collective-permute-start.13
  44.4 2.4 %collective-permute-start.12 = (bf16[96,1024]{1,0:T(8,128)(2,1)S(1)}, bf16[96,1024]{1,0:T(8,128)(2,1)S(1)}, u32[]{:S(2)}, u32[]{:S(2)}) collective-permute-start(bf16[96,1024]{1,0:T(8,128)(2,1)S(1)} %get-tuple-element.166), channel_id=1, source_target_pairs={{0,8},{1,9},{2,10},{3,11},{4,12},{5,13},{6,14},{7,15},{8,0},{9,1},... | collective-permute-start | bytes 589832 | tf_op jit(solution)/shard_map/ppermute | solution.py:233
  46.9 2.6 %ffn.5 = (bf16[1024,384]{1,0:T(8,128)(2,1)S(1)}, bf16[192,1024]{1,0:T(8,128)(2,1)S(1)}, bf16[192,1024]{1,0:T(8,128)(2,1)S(1)}) custom-call(bf16[192,1024]{1,0:T(8,128)(2,1)S(1)} %pad_maximum_fusion.5.refs_0_, bf16[192,1024]{1,0:T(8,128)(2,1)S(1)} %collective-permute-done.14.refs_1_, bf16[1024,1024]{1,0:T(8,128)(2,1)S(1)} %get-tuple-element.170.refs_2_, ...), custom_call_target="tpu_custom_call" | custom-call | tf_op jit(solution)/shard_map/ffn/pallas_call | solution.py:292
  49.6 7.0 %collective-permute-done.12.refs_0_ = bf16[96,1024]{1,0:T(8,128)(2,1)S(1)} collective-permute-done((bf16[96,1024]{1,0:T(8,128)(2,1)S(1)}, bf16[96,1024]{1,0:T(8,128)(2,1)S(1)}, u32[]{:S(2)}, u32[]{:S(2)}) %collective-permute-start.12) | collective-permute-done | bytes 196640 | tf_op jit(solution)/shard_map/ppermute | solution.py:233
  56.9 1.6 %collective-permute-start.18 = (bf16[192,1024]{1,0:T(8,128)(2,1)S(1)}, bf16[192,1024]{1,0:T(8,128)(2,1)S(1)}, u32[]{:S(2)}, u32[]{:S(2)}) collective-permute-start(bf16[192,1024]{1,0:T(8,128)(2,1)S(1)} %pad_maximum_fusion.9), channel_id=1, source_target_pairs={{0,2},{1,3},{2,0},{3,1},{4,6},{5,7},{6,4},{7,5},{8,10},{9,11},{10,... | collective-permute-start | bytes 1179656 | tf_op jit(solution)/shard_map/ppermute | solution.py:229
  58.5 2.2 %collective-permute-start.16 = (bf16[96,1024]{1,0:T(8,128)(2,1)S(1)}, bf16[96,1024]{1,0:T(8,128)(2,1)S(1)}, u32[]{:S(2)}, u32[]{:S(2)}) collective-permute-start(bf16[96,1024]{1,0:T(8,128)(2,1)S(1)} %get-tuple-element.192), channel_id=1, source_target_pairs={{0,12},{1,13},{2,14},{3,15},{4,0},{5,1},{6,2},{7,3},{8,4},{9,5},{1... | collective-permute-start | bytes 589832 | tf_op jit(solution)/shard_map/ppermute | solution.py:233
  60.7 5.4 %collective-permute-done.16.refs_0_ = bf16[96,1024]{1,0:T(8,128)(2,1)S(1)} collective-permute-done((bf16[96,1024]{1,0:T(8,128)(2,1)S(1)}, bf16[96,1024]{1,0:T(8,128)(2,1)S(1)}, u32[]{:S(2)}, u32[]{:S(2)}) %collective-permute-start.16) | collective-permute-done | bytes 196640 | tf_op jit(solution)/shard_map/ppermute | solution.py:233
  66.0 3.0 %collective-permute-done.17.refs_1_ = bf16[96,1024]{1,0:T(8,128)(2,1)S(1)} collective-permute-done((bf16[96,1024]{1,0:T(8,128)(2,1)S(1)}, bf16[96,1024]{1,0:T(8,128)(2,1)S(1)}, u32[]{:S(2)}, u32[]{:S(2)}) %collective-permute-start.17) | collective-permute-done | bytes 196640 | tf_op jit(solution)/shard_map/ppermute | solution.py:233
  69.3 1.2 %collective-permute-start.20 = (bf16[192,1024]{1,0:T(8,128)(2,1)S(1)}, bf16[192,1024]{1,0:T(8,128)(2,1)S(1)}, u32[]{:S(2)}, u32[]{:S(2)}) collective-permute-start(bf16[192,1024]{1,0:T(8,128)(2,1)S(1)} %pad_maximum_fusion.11), channel_id=1, source_target_pairs={{0,2},{1,3},{2,0},{3,1},{4,6},{5,7},{6,4},{7,5},{8,10},{9,11},{10,... | collective-permute-start | bytes 1179656 | tf_op jit(solution)/shard_map/ppermute | solution.py:229
  70.5 0.6 collective-permute-start.19
  71.1 0.4 collective-permute-done.21.refs_4_
  71.6 2.0 %first_grad.1.first_ref = f32[1024,1024]{1,0:T(8,128)S(1)} custom-call(bf16[1024,384]{1,0:T(8,128)(2,1)S(1)} %get-tuple-element.202.refs_0_, bf16[1024,768]{1,0:T(8,128)(2,1)S(1)} %get-tuple-element.221.refs_1_.refs_0_, bf16[192,1024]{1,0:T(8,128)(2,1)S(1)} %get-tuple-element.201.refs_2_, bf16[192,1024]{1,0:T(8,128)(2,1)S(1)} %pad_maximum_fusion.10.refs_3_, ...), custom_call_target="tpu_custom_call" | custom-call | tf_op jit(solution)/shard_map/first_grad/pallas_call | solution.py:371
  73.5 9.1 %collective-permute-done.19.refs_0_ = bf16[96,1024]{1,0:T(8,128)(2,1)S(1)} collective-permute-done((bf16[96,1024]{1,0:T(8,128)(2,1)S(1)}, bf16[96,1024]{1,0:T(8,128)(2,1)S(1)}, u32[]{:S(2)}, u32[]{:S(2)}) %collective-permute-start.19) | collective-permute-done | bytes 196640 | tf_op jit(solution)/shard_map/ppermute | solution.py:233
  82.8 0.8 copy-done
  83.6 1.4 %combine.1 = bf16[128,1024]{1,0:T(8,128)(2,1)} custom-call(s32[1]{0:T(128)} %bitcast.plane_ref, bf16[128,1024]{1,0:T(8,128)(2,1)S(1)} %copy-done, s32[2,128]{1,0:T(2,128)S(1)} %bitcast.5, s32[2,128]{1,0:T(2,128)S(1)} %bitcast.7, bf16[96,1024]{1,0:T(8,128)(2,1)S(1)} %add_convert_fusion.4.refs_0_, bf16[96,1024]{1,0:T(8,128)(2,1)S(1)} %get-tuple-element.217.refs_1_, ...), custom_call_target="tpu_custom_call" | custom-call | tf_op jit(solution)/shard_map/combine/pallas_call | solution.py:441
  85.0 2.8 %last_grad.1 = bf16[1,1024,1024]{2,1,0:T(8,128)(2,1)} custom-call(f32[1024,1024]{1,0:T(8,128)S(1)} %first_grad.1.first_ref, bf16[1024,768]{1,0:T(8,128)(2,1)S(1)} %get-tuple-element.221.refs_1_.refs_0_, bf16[1024,384]{1,0:T(8,128)(2,1)S(1)} %get-tuple-element.222.refs_1_, bf16[384,1024]{1,0:T(8,128)(2,1)S(1)} %pad_maximum_fusion.2.refs_2_, ...), custom_call_target="tpu_custom_call" | custom-call | tf_op jit(solution)/shard_map/last_grad/pallas_call | solution.py:383
  (55 shorter events, 1.8 us)
Async XLA Ops:
  2.6 14.9 %collective-permute-start.2 = (bf16[192,1024]{1,0:T(8,128)(2,1)S(1)}, bf16[192,1024]{1,0:T(8,128)(2,1)S(1)}, u32[]{:S(2)}, u32[]{:S(2)}) collective-permute-start(bf16[192,1024]{1,0:T(8,128)(2,1)S(1)} %pad_maximum_fusion.4), channel_id=1, source_target_pairs={{0,2},{1,3},{2,0},{3,1},{4,6},{5,7},{6,4},{7,5},{8,10},{9,11},{10,... | collective-permute-start | bytes 1179656 | tf_op jit(solution)/shard_map/ppermute | solution.py:229
  5.6 9.7 %collective-permute-start = (bf16[96,1024]{1,0:T(8,128)(2,1)S(1)}, bf16[96,1024]{1,0:T(8,128)(2,1)S(1)}, u32[]{:S(2)}, u32[]{:S(2)}) collective-permute-start(bf16[96,1024]{1,0:T(8,128)(2,1)S(1)} %get-tuple-element.113), channel_id=1, source_target_pairs={{0,4},{1,5},{2,6},{3,7},{4,8},{5,9},{6,10},{7,11},{8,12},{9,13},{1... | collective-permute-start | bytes 589832 | tf_op jit(solution)/shard_map/ppermute | solution.py:233
  7.2 10.3 %collective-permute-start.1 = (bf16[96,1024]{1,0:T(8,128)(2,1)S(1)}, bf16[96,1024]{1,0:T(8,128)(2,1)S(1)}, u32[]{:S(2)}, u32[]{:S(2)}) collective-permute-start(bf16[96,1024]{1,0:T(8,128)(2,1)S(1)} %get-tuple-element.114), channel_id=1, source_target_pairs={{0,12},{1,13},{2,14},{3,15},{4,0},{5,1},{6,2},{7,3},{8,4},{9,5},{1... | collective-permute-start | bytes 589832 | tf_op jit(solution)/shard_map/ppermute | solution.py:233
  17.6 2.0 %collective-permute-start.5 = (bf16[192,1024]{1,0:T(8,128)(2,1)S(1)}, bf16[192,1024]{1,0:T(8,128)(2,1)S(1)}, u32[]{:S(2)}, u32[]{:S(2)}) collective-permute-start(bf16[192,1024]{1,0:T(8,128)(2,1)S(1)} %get-tuple-element.139.refs_0_), channel_id=1, source_target_pairs={{0,1},{1,0},{2,3},{3,2},{4,5},{5,4},{6,7},{7,6},{8,9},{9,8},{10,11... | collective-permute-start | bytes 1179656 | tf_op jit(solution)/shard_map/ppermute | solution.py:229
  17.7 12.7 %collective-permute-start.4 = (bf16[192,1024]{1,0:T(8,128)(2,1)S(1)}, bf16[192,1024]{1,0:T(8,128)(2,1)S(1)}, u32[]{:S(2)}, u32[]{:S(2)}) collective-permute-start(bf16[192,1024]{1,0:T(8,128)(2,1)S(1)} %pad_maximum_fusion.8), channel_id=1, source_target_pairs={{0,2},{1,3},{2,0},{3,1},{4,6},{5,7},{6,4},{7,5},{8,10},{9,11},{10,... | collective-permute-start | bytes 1179656 | tf_op jit(solution)/shard_map/ppermute | solution.py:229
  18.3 12.1 %collective-permute-start.3 = (bf16[96,1024]{1,0:T(8,128)(2,1)S(1)}, bf16[96,1024]{1,0:T(8,128)(2,1)S(1)}, u32[]{:S(2)}, u32[]{:S(2)}) collective-permute-start(bf16[96,1024]{1,0:T(8,128)(2,1)S(1)} %get-tuple-element.128), channel_id=1, source_target_pairs={{0,8},{1,9},{2,10},{3,11},{4,12},{5,13},{6,14},{7,15},{8,0},{9,1},... | collective-permute-start | bytes 589832 | tf_op jit(solution)/shard_map/ppermute | solution.py:233
  22.2 8.3 %collective-permute-start.6 = (bf16[192,1024]{1,0:T(8,128)(2,1)S(1)}, bf16[192,1024]{1,0:T(8,128)(2,1)S(1)}, u32[]{:S(2)}, u32[]{:S(2)}) collective-permute-start(bf16[192,1024]{1,0:T(8,128)(2,1)S(1)} %get-tuple-element.142), channel_id=1, source_target_pairs={{0,1},{1,0},{2,3},{3,2},{4,5},{5,4},{6,7},{7,6},{8,9},{9,8},{10,11... | collective-permute-start | bytes 1179656 | tf_op jit(solution)/shard_map/ppermute | solution.py:229
  30.6 5.5 %collective-permute-start.10 = (bf16[384,1024]{1,0:T(8,128)(2,1)S(1)}, bf16[384,1024]{1,0:T(8,128)(2,1)S(1)}, u32[]{:S(2)}, u32[]{:S(2)}) collective-permute-start(bf16[384,1024]{1,0:T(8,128)(2,1)S(1)} %pad_maximum_fusion.refs_0_), channel_id=1, source_target_pairs={{0,1},{1,0},{2,3},{3,2},{4,5},{5,4},{6,7},{7,6},{8,9},{9,8},{10,11... | collective-permute-start | bytes 2359304 | tf_op jit(solution)/shard_map/ppermute | solution.py:229
  30.7 12.8 %collective-permute-start.9 = (bf16[192,1024]{1,0:T(8,128)(2,1)S(1)}, bf16[192,1024]{1,0:T(8,128)(2,1)S(1)}, u32[]{:S(2)}, u32[]{:S(2)}) collective-permute-start(bf16[192,1024]{1,0:T(8,128)(2,1)S(1)} %pad_maximum_fusion.6), channel_id=1, source_target_pairs={{0,2},{1,3},{2,0},{3,1},{4,6},{5,7},{6,4},{7,5},{8,10},{9,11},{10,... | collective-permute-start | bytes 1179656 | tf_op jit(solution)/shard_map/ppermute | solution.py:229
  32.3 9.6 %collective-permute-start.7 = (bf16[96,1024]{1,0:T(8,128)(2,1)S(1)}, bf16[96,1024]{1,0:T(8,128)(2,1)S(1)}, u32[]{:S(2)}, u32[]{:S(2)}) collective-permute-start(bf16[96,1024]{1,0:T(8,128)(2,1)S(1)} %get-tuple-element.145), channel_id=1, source_target_pairs={{0,4},{1,5},{2,6},{3,7},{4,8},{5,9},{6,10},{7,11},{8,12},{9,13},{1... | collective-permute-start | bytes 589832 | tf_op jit(solution)/shard_map/ppermute | solution.py:233
  32.3 11.2 %collective-permute-start.8 = (bf16[96,1024]{1,0:T(8,128)(2,1)S(1)}, bf16[96,1024]{1,0:T(8,128)(2,1)S(1)}, u32[]{:S(2)}, u32[]{:S(2)}) collective-permute-start(bf16[96,1024]{1,0:T(8,128)(2,1)S(1)} %get-tuple-element.146), channel_id=1, source_target_pairs={{0,12},{1,13},{2,14},{3,15},{4,0},{5,1},{6,2},{7,3},{8,4},{9,5},{1... | collective-permute-start | bytes 589832 | tf_op jit(solution)/shard_map/ppermute | solution.py:233
  41.2 2.5 %collective-permute-start.11 = (bf16[384,1024]{1,0:T(8,128)(2,1)S(1)}, bf16[384,1024]{1,0:T(8,128)(2,1)S(1)}, u32[]{:S(2)}, u32[]{:S(2)}) collective-permute-start(bf16[384,1024]{1,0:T(8,128)(2,1)S(1)} %get-tuple-element.160), channel_id=1, source_target_pairs={{0,1},{1,0},{2,3},{3,2},{4,5},{5,4},{6,7},{7,6},{8,9},{9,8},{10,11... | collective-permute-start | bytes 2359304 | tf_op jit(solution)/shard_map/ppermute | solution.py:229
  43.8 3.1 %collective-permute-start.14 = (bf16[192,1024]{1,0:T(8,128)(2,1)S(1)}, bf16[192,1024]{1,0:T(8,128)(2,1)S(1)}, u32[]{:S(2)}, u32[]{:S(2)}) collective-permute-start(bf16[192,1024]{1,0:T(8,128)(2,1)S(1)} %pad_maximum_fusion.5.refs_0_), channel_id=1, source_target_pairs={{0,1},{1,0},{2,3},{3,2},{4,5},{5,4},{6,7},{7,6},{8,9},{9,8},{10,11... | collective-permute-start | bytes 1179656 | tf_op jit(solution)/shard_map/ppermute | solution.py:229
  43.9 12.7 %collective-permute-start.13 = (bf16[192,1024]{1,0:T(8,128)(2,1)S(1)}, bf16[192,1024]{1,0:T(8,128)(2,1)S(1)}, u32[]{:S(2)}, u32[]{:S(2)}) collective-permute-start(bf16[192,1024]{1,0:T(8,128)(2,1)S(1)} %add_convert_fusion.1), channel_id=1, source_target_pairs={{0,2},{1,3},{2,0},{3,1},{4,6},{5,7},{6,4},{7,5},{8,10},{9,11},{10,... | collective-permute-start | bytes 1179656 | tf_op jit(solution)/shard_map/ppermute | solution.py:229
  44.4 12.1 %collective-permute-start.12 = (bf16[96,1024]{1,0:T(8,128)(2,1)S(1)}, bf16[96,1024]{1,0:T(8,128)(2,1)S(1)}, u32[]{:S(2)}, u32[]{:S(2)}) collective-permute-start(bf16[96,1024]{1,0:T(8,128)(2,1)S(1)} %get-tuple-element.166), channel_id=1, source_target_pairs={{0,8},{1,9},{2,10},{3,11},{4,12},{5,13},{6,14},{7,15},{8,0},{9,1},... | collective-permute-start | bytes 589832 | tf_op jit(solution)/shard_map/ppermute | solution.py:233
  49.5 7.3 %collective-permute-start.15 = (bf16[192,1024]{1,0:T(8,128)(2,1)S(1)}, bf16[192,1024]{1,0:T(8,128)(2,1)S(1)}, u32[]{:S(2)}, u32[]{:S(2)}) collective-permute-start(bf16[192,1024]{1,0:T(8,128)(2,1)S(1)} %get-tuple-element.180), channel_id=1, source_target_pairs={{0,1},{1,0},{2,3},{3,2},{4,5},{5,4},{6,7},{7,6},{8,9},{9,8},{10,11... | collective-permute-start | bytes 1179656 | tf_op jit(solution)/shard_map/ppermute | solution.py:229
  56.9 12.1 %collective-permute-start.18 = (bf16[192,1024]{1,0:T(8,128)(2,1)S(1)}, bf16[192,1024]{1,0:T(8,128)(2,1)S(1)}, u32[]{:S(2)}, u32[]{:S(2)}) collective-permute-start(bf16[192,1024]{1,0:T(8,128)(2,1)S(1)} %pad_maximum_fusion.9), channel_id=1, source_target_pairs={{0,2},{1,3},{2,0},{3,1},{4,6},{5,7},{6,4},{7,5},{8,10},{9,11},{10,... | collective-permute-start | bytes 1179656 | tf_op jit(solution)/shard_map/ppermute | solution.py:229
  58.5 7.6 %collective-permute-start.16 = (bf16[96,1024]{1,0:T(8,128)(2,1)S(1)}, bf16[96,1024]{1,0:T(8,128)(2,1)S(1)}, u32[]{:S(2)}, u32[]{:S(2)}) collective-permute-start(bf16[96,1024]{1,0:T(8,128)(2,1)S(1)} %get-tuple-element.192), channel_id=1, source_target_pairs={{0,12},{1,13},{2,14},{3,15},{4,0},{5,1},{6,2},{7,3},{8,4},{9,5},{1... | collective-permute-start | bytes 589832 | tf_op jit(solution)/shard_map/ppermute | solution.py:233
  60.7 8.3 %collective-permute-start.17 = (bf16[96,1024]{1,0:T(8,128)(2,1)S(1)}, bf16[96,1024]{1,0:T(8,128)(2,1)S(1)}, u32[]{:S(2)}, u32[]{:S(2)}) collective-permute-start(bf16[96,1024]{1,0:T(8,128)(2,1)S(1)} %get-tuple-element.193), channel_id=1, source_target_pairs={{0,4},{1,5},{2,6},{3,7},{4,8},{5,9},{6,10},{7,11},{8,12},{9,13},{1... | collective-permute-start | bytes 589832 | tf_op jit(solution)/shard_map/ppermute | solution.py:233
  69.2 2.4 %collective-permute-start.21 = (bf16[384,1024]{1,0:T(8,128)(2,1)S(1)}, bf16[384,1024]{1,0:T(8,128)(2,1)S(1)}, u32[]{:S(2)}, u32[]{:S(2)}) collective-permute-start(bf16[384,1024]{1,0:T(8,128)(2,1)S(1)} %pad_maximum_fusion.1), channel_id=1, source_target_pairs={{0,1},{1,0},{2,3},{3,2},{4,5},{5,4},{6,7},{7,6},{8,9},{9,8},{10,11... | collective-permute-start | bytes 2359304 | tf_op jit(solution)/shard_map/ppermute | solution.py:229
  69.3 13.3 %collective-permute-start.20 = (bf16[192,1024]{1,0:T(8,128)(2,1)S(1)}, bf16[192,1024]{1,0:T(8,128)(2,1)S(1)}, u32[]{:S(2)}, u32[]{:S(2)}) collective-permute-start(bf16[192,1024]{1,0:T(8,128)(2,1)S(1)} %pad_maximum_fusion.11), channel_id=1, source_target_pairs={{0,2},{1,3},{2,0},{3,1},{4,6},{5,7},{6,4},{7,5},{8,10},{9,11},{10,... | collective-permute-start | bytes 1179656 | tf_op jit(solution)/shard_map/ppermute | solution.py:229
  70.5 12.1 %collective-permute-start.19 = (bf16[96,1024]{1,0:T(8,128)(2,1)S(1)}, bf16[96,1024]{1,0:T(8,128)(2,1)S(1)}, u32[]{:S(2)}, u32[]{:S(2)}) collective-permute-start(bf16[96,1024]{1,0:T(8,128)(2,1)S(1)} %add_convert_fusion.2), channel_id=1, source_target_pairs={{0,8},{1,9},{2,10},{3,11},{4,12},{5,13},{6,14},{7,15},{8,0},{9,1},... | collective-permute-start | bytes 589832 | tf_op jit(solution)/shard_map/ppermute | solution.py:233
  82.6 1.0 %copy-start = (bf16[128,1024]{1,0:T(8,128)(2,1)S(1)}, bf16[128,1024]{1,0:T(8,128)(2,1)}, u32[]{:S(2)}) copy-start(bf16[128,1024]{1,0:T(8,128)(2,1)} %tokens_ref.1) | copy-start | bytes 786436
  82.6 1.0 %copy-start.1 = (s32[128,2]{0,1:T(2,128)S(1)}, s32[128,2]{0,1:T(2,128)}, u32[]{:S(2)}) copy-start(s32[128,2]{0,1:T(2,128)} %param.10) | copy-start | bytes 3076
  82.6 0.9 %copy-start.2 = (s32[128,2]{0,1:T(2,128)S(1)}, s32[128,2]{0,1:T(2,128)}, u32[]{:S(2)}) copy-start(s32[128,2]{0,1:T(2,128)} %param.11) | copy-start | bytes 3076
  82.7 2.4 %collective-permute-start.22 = (bf16[384,1024]{1,0:T(8,128)(2,1)S(1)}, bf16[384,1024]{1,0:T(8,128)(2,1)S(1)}, u32[]{:S(2)}, u32[]{:S(2)}) collective-permute-start(bf16[384,1024]{1,0:T(8,128)(2,1)S(1)} %pad_maximum_fusion.2.refs_2_), channel_id=1, source_target_pairs={{0,1},{1,0},{2,3},{3,2},{4,5},{5,4},{6,7},{7,6},{8,9},{9,8},{10,11... | collective-permute-start | bytes 2359304 | tf_op jit(solution)/shard_map/ppermute | solution.py:229

commit v8 on v7

--- a/solution.py
+++ b/solution.py
@@ -12,6 +12,7 @@
 JOINED = ((1, 2), (2, 3))
 TILE = 256
 LINK_WORK = 10 << 30
+LAST_WORK = 0
 F32 = jnp.float32
 BF16 = jnp.bfloat16
 
@@ -241,12 +242,21 @@
 
     flying = {}
 
-    def land(*earlier):
+    def land(*earlier, sooner=()):
+        names = [name for name in flying if name[0] != "y"]
+        first = list(flying) != names and len(names) > 0
+        if first:
+            values = [flying.pop(name) for name in names]
+            if sooner:
+                values = lax.optimization_barrier(tuple(values) + sooner)[: len(names)]
+            values = through(values, "land_planes", LINK_WORK)
+            live.update(zip(names, values))
+            earlier += (values[0],)
         names = list(flying)
         values = [flying.pop(name) for name in names]
         if earlier:
             values = lax.optimization_barrier(tuple(values) + earlier)[: len(names)]
-        values = through(values, "land", LINK_WORK)
+        values = through(values, "land", LAST_WORK if first else LINK_WORK)
         for name, value in zip(names, values):
             if name[0] != "y":
                 live[name] = value
@@ -422,7 +432,7 @@
     core("N", (3,))
     ffn(3)
     cross(3)
-    fold_core(land(), 3)
+    fold_core(land(live["crossed", (3,)]), 3)
     sync()
     if shifts > 1:
         across("R", 0)
@@ -434,7 +444,7 @@
     along(("C", (2, 3)))
     core("C", (0,), (1,))
     first_grad([(0,), (1, 2)], [("own", (0,)), ("own", (1,)), ("other", (0, 1))])
-    land(live["first"])
+    land(sooner=(live["first"],))
     sync()
     core("C", (2, 3))
     grad_down = last_grad([(1, 2), (3,)], [("own", (2, 3)), ("other", (2, 3))])

time: 88.2 us -> 89.7 us (1.017)
  waiting for transfers between devices: 40.5 us -> 41.6 us
  starting transfers between devices: 23.3 us -> 24.4 us
    ppermute x14, waiting for transfers between devices: 0.59 us -> 6.65 us  [swap(): lax.ppermute(value, 'expert', [(i, i ^ mask) for i in range(devices)])]
    ppermute x9, waiting for transfers between devices: 39.9 us -> 35 us  [turn(): return lax.ppermute(value, 'expert', to)]
    ppermute x14, starting transfers between devices: 9.07 us -> 10.2 us  [swap(): lax.ppermute(value, 'expert', [(i, i ^ mask) for i in range(devices)])]
  transfers between devices with their start and end apart: 23 -> 23, of which waited for: 11 -> 15; matrix products, arithmetic and copies ran while one was open for 1% -> 0% of each run, Pallas kernels for 19% -> 18%
where the time goes in v8:
time: 89.7 us; the launch traced here: 89.5 us
  waiting for transfers between devices  41.6 us (46%)
  starting transfers between devices  24.4 us (27%)
  Pallas kernels  21.2 us (24%)
  between operations  1.08 us (1%)
  other arithmetic  0.99 us (1%)
    ppermute x9, waiting for transfers between devices, turn(): return lax.ppermute(value, 'expert', to)  35 us
    ppermute x9, starting transfers between devices, turn(): return lax.ppermute(value, 'expert', to)  14.2 us
    pallas_call x3, Pallas kernels, ffn(): call(functools.partial(ffn_kernel, len(pieces)), 24, 'ffn', out_shape=[ja...  10.3 us
    ppermute x14, starting transfers between devices, swap(): lax.ppermute(value, 'expert', [(i, i ^ mask) for i in range(devices)])  10.2 us
    ppermute x14, waiting for transfers between devices, swap(): lax.ppermute(value, 'expert', [(i, i ^ mask) for i in range(devices)])  6.65 us
    pallas_call x1, Pallas kernels, load(): call(load_kernel, 16, 'load', out_shape=[weight, weight, jax.ShapeDtypeSt...  2.88 us
    pallas_call x1, Pallas kernels, last_grad(): call(functools.partial(last_grad_kernel, plan), 24, 'last_grad', out_shap...  2.81 us
    pallas_call x1, Pallas kernels, first_grad(): call(functools.partial(first_grad_kernel, plan), 24, 'first_grad', out_sh...  1.95 us
  transfers between devices with their start and end apart: 23, of which 15 were waited for; matrix products, arithmetic and copies ran while one was open for 0% of the time, Pallas kernels for 18%

profile of v8, /device:TPU:0, one launch (start us, length us, event | category | flops | bytes accessed | tf_op | source)
XLA Modules:
  0.0 89.5 jit_solution(28478539525982)
XLA Ops:
  0.6 1.9 %send.1 = (bf16[96,1024]{1,0:T(8,128)(2,1)S(1)}, bf16[96,1024]{1,0:T(8,128)(2,1)S(1)}, bf16[96,1024]{1,0:T(8,128)(2,1)S(1)}, bf16[96,1024]{1,0:T(8,128)(2,1)S(1)...) custom-call(s32[1]{0:T(128)} %bitcast.plane_ref, ...), custom_call_target="tpu_custom_call" | custom-call | tf_op jit(solution)/shard_map/send/pallas_call | solution.py:329
  2.6 3.1 %collective-permute-start = (bf16[96,1024]{1,0:T(8,128)(2,1)S(1)}, bf16[96,1024]{1,0:T(8,128)(2,1)S(1)}, u32[]{:S(2)}, u32[]{:S(2)}) collective-permute-start(bf16[96,1024]{1,0:T(8,128)(2,1)S(1)} %get-tuple-element.109), channel_id=1, source_target_pairs={{0,4},{1,5},{2,6},{3,7},{4,8},{5,9},{6,10},{7,11},{8,12},{9,13},{1... | collective-permute-start | bytes 589832 | tf_op jit(solution)/shard_map/ppermute | solution.py:234
  5.7 2.1 %collective-permute-start.1 = (bf16[96,1024]{1,0:T(8,128)(2,1)S(1)}, bf16[96,1024]{1,0:T(8,128)(2,1)S(1)}, u32[]{:S(2)}, u32[]{:S(2)}) collective-permute-start(bf16[96,1024]{1,0:T(8,128)(2,1)S(1)} %get-tuple-element.110), channel_id=1, source_target_pairs={{0,12},{1,13},{2,14},{3,15},{4,0},{5,1},{6,2},{7,3},{8,4},{9,5},{1... | collective-permute-start | bytes 589832 | tf_op jit(solution)/shard_map/ppermute | solution.py:234
  7.8 1.7 %collective-permute-start.2 = (bf16[192,1024]{1,0:T(8,128)(2,1)S(1)}, bf16[192,1024]{1,0:T(8,128)(2,1)S(1)}, u32[]{:S(2)}, u32[]{:S(2)}) collective-permute-start(bf16[192,1024]{1,0:T(8,128)(2,1)S(1)} %pad_maximum_fusion.3), channel_id=1, source_target_pairs={{0,2},{1,3},{2,0},{3,1},{4,6},{5,7},{6,4},{7,5},{8,10},{9,11},{10,... | collective-permute-start | bytes 1179656 | tf_op jit(solution)/shard_map/ppermute | solution.py:230
  9.5 2.9 %load.1 = (bf16[1024,1024]{1,0:T(8,128)(2,1)S(1)}, bf16[1024,1024]{1,0:T(8,128)(2,1)S(1)}, bf16[1024,1024]{1,0:T(8,128)(2,1)S(1)}) custom-call(bf16[1,1024,1024]{2,1,0:T(8,128)(2,1)} %refs_0_.2, bf16[1,1024,1024]{2,1,0:T(8,128)(2,1)} %refs_1_.3, bf16[1,1024,1024]{2,1,0:T(8,128)(2,1)} %refs_2_.1), custom_call_target="tpu_custom_call" | custom-call | tf_op jit(solution)/shard_map/load/pallas_call | solution.py:344
  12.4 1.1 %collective-permute-done.refs_0_ = bf16[96,1024]{1,0:T(8,128)(2,1)S(1)} collective-permute-done((bf16[96,1024]{1,0:T(8,128)(2,1)S(1)}, bf16[96,1024]{1,0:T(8,128)(2,1)S(1)}, u32[]{:S(2)}, u32[]{:S(2)}) %collective-permute-start) | collective-permute-done | bytes 196640 | tf_op jit(solution)/shard_map/ppermute | solution.py:234
  13.5 2.8 %collective-permute-done.1.refs_1_ = bf16[96,1024]{1,0:T(8,128)(2,1)S(1)} collective-permute-done((bf16[96,1024]{1,0:T(8,128)(2,1)S(1)}, bf16[96,1024]{1,0:T(8,128)(2,1)S(1)}, u32[]{:S(2)}, u32[]{:S(2)}) %collective-permute-start.1) | collective-permute-done | bytes 196640 | tf_op jit(solution)/shard_map/ppermute | solution.py:234
  16.2 2.2 %collective-permute-done.2.refs_0_ = bf16[192,1024]{1,0:T(8,128)(2,1)S(1)} collective-permute-done((bf16[192,1024]{1,0:T(8,128)(2,1)S(1)}, bf16[192,1024]{1,0:T(8,128)(2,1)S(1)}, u32[]{:S(2)}, u32[]{:S(2)}) %collective-permute-start.2) | collective-permute-done | bytes 393248 | tf_op jit(solution)/shard_map/ppermute | solution.py:230
  18.6 0.7 collective-permute-start.3
  19.4 1.6 %collective-permute-start.6 = (bf16[192,1024]{1,0:T(8,128)(2,1)S(1)}, bf16[192,1024]{1,0:T(8,128)(2,1)S(1)}, u32[]{:S(2)}, u32[]{:S(2)}) collective-permute-start(bf16[192,1024]{1,0:T(8,128)(2,1)S(1)} %pad_maximum_fusion.8), channel_id=1, source_target_pairs={{0,2},{1,3},{2,0},{3,1},{4,6},{5,7},{6,4},{7,5},{8,10},{9,11},{10,... | collective-permute-start | bytes 1179656 | tf_op jit(solution)/shard_map/ppermute | solution.py:230
  20.9 2.6 %ffn.3 = (bf16[1024,384]{1,0:T(8,128)(2,1)S(1)}, bf16[192,1024]{1,0:T(8,128)(2,1)S(1)}, bf16[192,1024]{1,0:T(8,128)(2,1)S(1)}) custom-call(bf16[192,1024]{1,0:T(8,128)(2,1)S(1)} %get-tuple-element.132.refs_0_, bf16[192,1024]{1,0:T(8,128)(2,1)S(1)} %collective-permute-done.4.refs_1_, bf16[1024,1024]{1,0:T(8,128)(2,1)S(1)} %get-tuple-element.163.refs_2_, ...), custom_call_target="tpu_custom_call" | custom-call | tf_op jit(solution)/shard_map/ffn/pallas_call | solution.py:302
  23.7 6.5 %collective-permute-done.3.refs_0_ = bf16[96,1024]{1,0:T(8,128)(2,1)S(1)} collective-permute-done((bf16[96,1024]{1,0:T(8,128)(2,1)S(1)}, bf16[96,1024]{1,0:T(8,128)(2,1)S(1)}, u32[]{:S(2)}, u32[]{:S(2)}) %collective-permute-start.3) | collective-permute-done | bytes 196640 | tf_op jit(solution)/shard_map/ppermute | solution.py:234
  30.8 1.6 %collective-permute-start.7 = (bf16[96,1024]{1,0:T(8,128)(2,1)S(1)}, bf16[96,1024]{1,0:T(8,128)(2,1)S(1)}, u32[]{:S(2)}, u32[]{:S(2)}) collective-permute-start(bf16[96,1024]{1,0:T(8,128)(2,1)S(1)} %get-tuple-element.140), channel_id=1, source_target_pairs={{0,4},{1,5},{2,6},{3,7},{4,8},{5,9},{6,10},{7,11},{8,12},{9,13},{1... | collective-permute-start | bytes 589832 | tf_op jit(solution)/shard_map/ppermute | solution.py:234
  32.4 2.2 %collective-permute-start.8 = (bf16[96,1024]{1,0:T(8,128)(2,1)S(1)}, bf16[96,1024]{1,0:T(8,128)(2,1)S(1)}, u32[]{:S(2)}, u32[]{:S(2)}) collective-permute-start(bf16[96,1024]{1,0:T(8,128)(2,1)S(1)} %get-tuple-element.141), channel_id=1, source_target_pairs={{0,12},{1,13},{2,14},{3,15},{4,0},{5,1},{6,2},{7,3},{8,4},{9,5},{1... | collective-permute-start | bytes 589832 | tf_op jit(solution)/shard_map/ppermute | solution.py:234
  34.7 1.6 %collective-permute-start.11 = (bf16[192,1024]{1,0:T(8,128)(2,1)S(1)}, bf16[192,1024]{1,0:T(8,128)(2,1)S(1)}, u32[]{:S(2)}, u32[]{:S(2)}) collective-permute-start(bf16[192,1024]{1,0:T(8,128)(2,1)S(1)} %pad_maximum_fusion.5), channel_id=1, source_target_pairs={{0,2},{1,3},{2,0},{3,1},{4,6},{5,7},{6,4},{7,5},{8,10},{9,11},{10,... | collective-permute-start | bytes 1179656 | tf_op jit(solution)/shard_map/ppermute | solution.py:230
  36.3 5.1 %ffn.4 = (bf16[1024,768]{1,0:T(8,128)(2,1)S(1)}, bf16[384,1024]{1,0:T(8,128)(2,1)S(1)}, bf16[384,1024]{1,0:T(8,128)(2,1)S(1)}) custom-call(bf16[384,1024]{1,0:T(8,128)(2,1)S(1)} %pad_maximum_fusion.refs_0_, bf16[384,1024]{1,0:T(8,128)(2,1)S(1)} %collective-permute-done.9.refs_1_, bf16[1024,1024]{1,0:T(8,128)(2,1)S(1)} %get-tuple-element.163.refs_2_, ...), custom_call_target="tpu_custom_call" | custom-call | tf_op jit(solution)/shard_map/ffn/pallas_call | solution.py:302
  41.5 2.2 %collective-permute-done.8.refs_1_ = bf16[96,1024]{1,0:T(8,128)(2,1)S(1)} collective-permute-done((bf16[96,1024]{1,0:T(8,128)(2,1)S(1)}, bf16[96,1024]{1,0:T(8,128)(2,1)S(1)}, u32[]{:S(2)}, u32[]{:S(2)}) %collective-permute-start.8) | collective-permute-done | bytes 196640 | tf_op jit(solution)/shard_map/ppermute | solution.py:234
  43.6 2.1 %collective-permute-done.11.refs_0_ = bf16[192,1024]{1,0:T(8,128)(2,1)S(1)} collective-permute-done((bf16[192,1024]{1,0:T(8,128)(2,1)S(1)}, bf16[192,1024]{1,0:T(8,128)(2,1)S(1)}, u32[]{:S(2)}, u32[]{:S(2)}) %collective-permute-start.11) | collective-permute-done | bytes 393248 | tf_op jit(solution)/shard_map/ppermute | solution.py:230
  46.6 1.5 %collective-permute-start.15 = (bf16[192,1024]{1,0:T(8,128)(2,1)S(1)}, bf16[192,1024]{1,0:T(8,128)(2,1)S(1)}, u32[]{:S(2)}, u32[]{:S(2)}) collective-permute-start(bf16[192,1024]{1,0:T(8,128)(2,1)S(1)} %add_convert_fusion.1), channel_id=1, source_target_pairs={{0,2},{1,3},{2,0},{3,1},{4,6},{5,7},{6,4},{7,5},{8,10},{9,11},{10,... | collective-permute-start | bytes 1179656 | tf_op jit(solution)/shard_map/ppermute | solution.py:230
  48.1 2.6 %ffn.5 = (bf16[1024,384]{1,0:T(8,128)(2,1)S(1)}, bf16[192,1024]{1,0:T(8,128)(2,1)S(1)}, bf16[192,1024]{1,0:T(8,128)(2,1)S(1)}) custom-call(bf16[192,1024]{1,0:T(8,128)(2,1)S(1)} %pad_maximum_fusion.6.refs_0_, bf16[192,1024]{1,0:T(8,128)(2,1)S(1)} %collective-permute-done.13.refs_1_, bf16[1024,1024]{1,0:T(8,128)(2,1)S(1)} %get-tuple-element.163.refs_2_, ...), custom_call_target="tpu_custom_call" | custom-call | tf_op jit(solution)/shard_map/ffn/pallas_call | solution.py:302
  50.8 6.9 %collective-permute-done.12.refs_0_ = bf16[96,1024]{1,0:T(8,128)(2,1)S(1)} collective-permute-done((bf16[96,1024]{1,0:T(8,128)(2,1)S(1)}, bf16[96,1024]{1,0:T(8,128)(2,1)S(1)}, u32[]{:S(2)}, u32[]{:S(2)}) %collective-permute-start.12) | collective-permute-done | bytes 196640 | tf_op jit(solution)/shard_map/ppermute | solution.py:234
  58.1 1.7 %collective-permute-start.16 = (bf16[96,1024]{1,0:T(8,128)(2,1)S(1)}, bf16[96,1024]{1,0:T(8,128)(2,1)S(1)}, u32[]{:S(2)}, u32[]{:S(2)}) collective-permute-start(bf16[96,1024]{1,0:T(8,128)(2,1)S(1)} %get-tuple-element.186), channel_id=1, source_target_pairs={{0,12},{1,13},{2,14},{3,15},{4,0},{5,1},{6,2},{7,3},{8,4},{9,5},{1... | collective-permute-start | bytes 589832 | tf_op jit(solution)/shard_map/ppermute | solution.py:234
  60.2 1.6 %collective-permute-start.18 = (bf16[192,1024]{1,0:T(8,128)(2,1)S(1)}, bf16[192,1024]{1,0:T(8,128)(2,1)S(1)}, u32[]{:S(2)}, u32[]{:S(2)}) collective-permute-start(bf16[192,1024]{1,0:T(8,128)(2,1)S(1)} %pad_maximum_fusion.9), channel_id=1, source_target_pairs={{0,2},{1,3},{2,0},{3,1},{4,6},{5,7},{6,4},{7,5},{8,10},{9,11},{10,... | collective-permute-start | bytes 1179656 | tf_op jit(solution)/shard_map/ppermute | solution.py:230
  61.8 3.6 %collective-permute-done.16.refs_0_ = bf16[96,1024]{1,0:T(8,128)(2,1)S(1)} collective-permute-done((bf16[96,1024]{1,0:T(8,128)(2,1)S(1)}, bf16[96,1024]{1,0:T(8,128)(2,1)S(1)}, u32[]{:S(2)}, u32[]{:S(2)}) %collective-permute-start.16) | collective-permute-done | bytes 196640 | tf_op jit(solution)/shard_map/ppermute | solution.py:234
  65.4 5.0 %collective-permute-done.17.refs_1_ = bf16[96,1024]{1,0:T(8,128)(2,1)S(1)} collective-permute-done((bf16[96,1024]{1,0:T(8,128)(2,1)S(1)}, bf16[96,1024]{1,0:T(8,128)(2,1)S(1)}, u32[]{:S(2)}, u32[]{:S(2)}) %collective-permute-start.17) | collective-permute-done | bytes 196640 | tf_op jit(solution)/shard_map/ppermute | solution.py:234
  71.0 1.9 %collective-permute-start.19 = (bf16[96,1024]{1,0:T(8,128)(2,1)S(1)}, bf16[96,1024]{1,0:T(8,128)(2,1)S(1)}, u32[]{:S(2)}, u32[]{:S(2)}) collective-permute-start(bf16[96,1024]{1,0:T(8,128)(2,1)S(1)} %add_convert_fusion.2), channel_id=1, source_target_pairs={{0,8},{1,9},{2,10},{3,11},{4,12},{5,13},{6,14},{7,15},{8,0},{9,1},... | collective-permute-start | bytes 589832 | tf_op jit(solution)/shard_map/ppermute | solution.py:234
  72.9 1.6 %collective-permute-start.21 = (bf16[192,1024]{1,0:T(8,128)(2,1)S(1)}, bf16[192,1024]{1,0:T(8,128)(2,1)S(1)}, u32[]{:S(2)}, u32[]{:S(2)}) collective-permute-start(bf16[192,1024]{1,0:T(8,128)(2,1)S(1)} %pad_maximum_fusion.11), channel_id=1, source_target_pairs={{0,2},{1,3},{2,0},{3,1},{4,6},{5,7},{6,4},{7,5},{8,10},{9,11},{10,... | collective-permute-start | bytes 1179656 | tf_op jit(solution)/shard_map/ppermute | solution.py:230
  74.5 1.9 %first_grad.1.first_ref = f32[1024,1024]{1,0:T(8,128)S(1)} custom-call(bf16[1024,384]{1,0:T(8,128)(2,1)S(1)} %get-tuple-element.196.refs_0_, bf16[1024,768]{1,0:T(8,128)(2,1)S(1)} %get-tuple-element.213.refs_1_.refs_0_, bf16[192,1024]{1,0:T(8,128)(2,1)S(1)} %get-tuple-element.195.refs_2_, bf16[192,1024]{1,0:T(8,128)(2,1)S(1)} %pad_maximum_fusion.10.refs_3_, ...), custom_call_target="tpu_custom_call" | custom-call | tf_op jit(solution)/shard_map/first_grad/pallas_call | solution.py:381
  76.4 7.0 %collective-permute-done.19.refs_0_ = bf16[96,1024]{1,0:T(8,128)(2,1)S(1)} collective-permute-done((bf16[96,1024]{1,0:T(8,128)(2,1)S(1)}, bf16[96,1024]{1,0:T(8,128)(2,1)S(1)}, u32[]{:S(2)}, u32[]{:S(2)}) %collective-permute-start.19) | collective-permute-done | bytes 196640 | tf_op jit(solution)/shard_map/ppermute | solution.py:234
  84.4 1.4 %combine.1 = bf16[128,1024]{1,0:T(8,128)(2,1)} custom-call(s32[1]{0:T(128)} %bitcast.plane_ref, bf16[128,1024]{1,0:T(8,128)(2,1)S(1)} %copy-done, s32[2,128]{1,0:T(2,128)S(1)} %bitcast.5, s32[2,128]{1,0:T(2,128)S(1)} %bitcast.7, bf16[96,1024]{1,0:T(8,128)(2,1)S(1)} %add_convert_fusion.4.refs_0_, bf16[96,1024]{1,0:T(8,128)(2,1)S(1)} %get-tuple-element.209.refs_1_, ...), custom_call_target="tpu_custom_call" | custom-call | tf_op jit(solution)/shard_map/combine/pallas_call | solution.py:451
  85.8 0.8 collective-permute-done.22.refs_3_
  86.5 2.8 %last_grad.1 = bf16[1,1024,1024]{2,1,0:T(8,128)(2,1)} custom-call(f32[1024,1024]{1,0:T(8,128)S(1)} %first_grad.1.first_ref, bf16[1024,768]{1,0:T(8,128)(2,1)S(1)} %get-tuple-element.213.refs_1_.refs_0_, bf16[1024,384]{1,0:T(8,128)(2,1)S(1)} %get-tuple-element.214.refs_1_, bf16[384,1024]{1,0:T(8,128)(2,1)S(1)} %pad_maximum_fusion.2.refs_2_, ...), custom_call_target="tpu_custom_call" | custom-call | tf_op jit(solution)/shard_map/last_grad/pallas_call | solution.py:393
  (61 shorter events, 4.2 us)
Async XLA Ops:
  2.6 10.9 %collective-permute-start = (bf16[96,1024]{1,0:T(8,128)(2,1)S(1)}, bf16[96,1024]{1,0:T(8,128)(2,1)S(1)}, u32[]{:S(2)}, u32[]{:S(2)}) collective-permute-start(bf16[96,1024]{1,0:T(8,128)(2,1)S(1)} %get-tuple-element.109), channel_id=1, source_target_pairs={{0,4},{1,5},{2,6},{3,7},{4,8},{5,9},{6,10},{7,11},{8,12},{9,13},{1... | collective-permute-start | bytes 589832 | tf_op jit(solution)/shard_map/ppermute | solution.py:234
  5.7 10.6 %collective-permute-start.1 = (bf16[96,1024]{1,0:T(8,128)(2,1)S(1)}, bf16[96,1024]{1,0:T(8,128)(2,1)S(1)}, u32[]{:S(2)}, u32[]{:S(2)}) collective-permute-start(bf16[96,1024]{1,0:T(8,128)(2,1)S(1)} %get-tuple-element.110), channel_id=1, source_target_pairs={{0,12},{1,13},{2,14},{3,15},{4,0},{5,1},{6,2},{7,3},{8,4},{9,5},{1... | collective-permute-start | bytes 589832 | tf_op jit(solution)/shard_map/ppermute | solution.py:234
  7.8 10.6 %collective-permute-start.2 = (bf16[192,1024]{1,0:T(8,128)(2,1)S(1)}, bf16[192,1024]{1,0:T(8,128)(2,1)S(1)}, u32[]{:S(2)}, u32[]{:S(2)}) collective-permute-start(bf16[192,1024]{1,0:T(8,128)(2,1)S(1)} %pad_maximum_fusion.3), channel_id=1, source_target_pairs={{0,2},{1,3},{2,0},{3,1},{4,6},{5,7},{6,4},{7,5},{8,10},{9,11},{10,... | collective-permute-start | bytes 1179656 | tf_op jit(solution)/shard_map/ppermute | solution.py:230
  18.5 2.4 %collective-permute-start.4 = (bf16[192,1024]{1,0:T(8,128)(2,1)S(1)}, bf16[192,1024]{1,0:T(8,128)(2,1)S(1)}, u32[]{:S(2)}, u32[]{:S(2)}) collective-permute-start(bf16[192,1024]{1,0:T(8,128)(2,1)S(1)} %get-tuple-element.132.refs_0_), channel_id=1, source_target_pairs={{0,1},{1,0},{2,3},{3,2},{4,5},{5,4},{6,7},{7,6},{8,9},{9,8},{10,11... | collective-permute-start | bytes 1179656 | tf_op jit(solution)/shard_map/ppermute | solution.py:230
  18.6 11.5 %collective-permute-start.3 = (bf16[96,1024]{1,0:T(8,128)(2,1)S(1)}, bf16[96,1024]{1,0:T(8,128)(2,1)S(1)}, u32[]{:S(2)}, u32[]{:S(2)}) collective-permute-start(bf16[96,1024]{1,0:T(8,128)(2,1)S(1)} %get-tuple-element.124), channel_id=1, source_target_pairs={{0,8},{1,9},{2,10},{3,11},{4,12},{5,13},{6,14},{7,15},{8,0},{9,1},... | collective-permute-start | bytes 589832 | tf_op jit(solution)/shard_map/ppermute | solution.py:234
  19.4 11.3 %collective-permute-start.6 = (bf16[192,1024]{1,0:T(8,128)(2,1)S(1)}, bf16[192,1024]{1,0:T(8,128)(2,1)S(1)}, u32[]{:S(2)}, u32[]{:S(2)}) collective-permute-start(bf16[192,1024]{1,0:T(8,128)(2,1)S(1)} %pad_maximum_fusion.8), channel_id=1, source_target_pairs={{0,2},{1,3},{2,0},{3,1},{4,6},{5,7},{6,4},{7,5},{8,10},{9,11},{10,... | collective-permute-start | bytes 1179656 | tf_op jit(solution)/shard_map/ppermute | solution.py:230
  23.6 7.1 %collective-permute-start.5 = (bf16[192,1024]{1,0:T(8,128)(2,1)S(1)}, bf16[192,1024]{1,0:T(8,128)(2,1)S(1)}, u32[]{:S(2)}, u32[]{:S(2)}) collective-permute-start(bf16[192,1024]{1,0:T(8,128)(2,1)S(1)} %get-tuple-element.135), channel_id=1, source_target_pairs={{0,1},{1,0},{2,3},{3,2},{4,5},{5,4},{6,7},{7,6},{8,9},{9,8},{10,11... | collective-permute-start | bytes 1179656 | tf_op jit(solution)/shard_map/ppermute | solution.py:230
  30.7 5.6 %collective-permute-start.9 = (bf16[384,1024]{1,0:T(8,128)(2,1)S(1)}, bf16[384,1024]{1,0:T(8,128)(2,1)S(1)}, u32[]{:S(2)}, u32[]{:S(2)}) collective-permute-start(bf16[384,1024]{1,0:T(8,128)(2,1)S(1)} %pad_maximum_fusion.refs_0_), channel_id=1, source_target_pairs={{0,1},{1,0},{2,3},{3,2},{4,5},{5,4},{6,7},{7,6},{8,9},{9,8},{10,11... | collective-permute-start | bytes 2359304 | tf_op jit(solution)/shard_map/ppermute | solution.py:230
  30.8 10.6 %collective-permute-start.7 = (bf16[96,1024]{1,0:T(8,128)(2,1)S(1)}, bf16[96,1024]{1,0:T(8,128)(2,1)S(1)}, u32[]{:S(2)}, u32[]{:S(2)}) collective-permute-start(bf16[96,1024]{1,0:T(8,128)(2,1)S(1)} %get-tuple-element.140), channel_id=1, source_target_pairs={{0,4},{1,5},{2,6},{3,7},{4,8},{5,9},{6,10},{7,11},{8,12},{9,13},{1... | collective-permute-start | bytes 589832 | tf_op jit(solution)/shard_map/ppermute | solution.py:234
  32.4 11.2 %collective-permute-start.8 = (bf16[96,1024]{1,0:T(8,128)(2,1)S(1)}, bf16[96,1024]{1,0:T(8,128)(2,1)S(1)}, u32[]{:S(2)}, u32[]{:S(2)}) collective-permute-start(bf16[96,1024]{1,0:T(8,128)(2,1)S(1)} %get-tuple-element.141), channel_id=1, source_target_pairs={{0,12},{1,13},{2,14},{3,15},{4,0},{5,1},{6,2},{7,3},{8,4},{9,5},{1... | collective-permute-start | bytes 589832 | tf_op jit(solution)/shard_map/ppermute | solution.py:234
  34.7 11.0 %collective-permute-start.11 = (bf16[192,1024]{1,0:T(8,128)(2,1)S(1)}, bf16[192,1024]{1,0:T(8,128)(2,1)S(1)}, u32[]{:S(2)}, u32[]{:S(2)}) collective-permute-start(bf16[192,1024]{1,0:T(8,128)(2,1)S(1)} %pad_maximum_fusion.5), channel_id=1, source_target_pairs={{0,2},{1,3},{2,0},{3,1},{4,6},{5,7},{6,4},{7,5},{8,10},{9,11},{10,... | collective-permute-start | bytes 1179656 | tf_op jit(solution)/shard_map/ppermute | solution.py:230
  41.4 4.5 %collective-permute-start.10 = (bf16[384,1024]{1,0:T(8,128)(2,1)S(1)}, bf16[384,1024]{1,0:T(8,128)(2,1)S(1)}, u32[]{:S(2)}, u32[]{:S(2)}) collective-permute-start(bf16[384,1024]{1,0:T(8,128)(2,1)S(1)} %get-tuple-element.153), channel_id=1, source_target_pairs={{0,1},{1,0},{2,3},{3,2},{4,5},{5,4},{6,7},{7,6},{8,9},{9,8},{10,11... | collective-permute-start | bytes 2359304 | tf_op jit(solution)/shard_map/ppermute | solution.py:230
  46.0 2.1 %collective-permute-start.13 = (bf16[192,1024]{1,0:T(8,128)(2,1)S(1)}, bf16[192,1024]{1,0:T(8,128)(2,1)S(1)}, u32[]{:S(2)}, u32[]{:S(2)}) collective-permute-start(bf16[192,1024]{1,0:T(8,128)(2,1)S(1)} %pad_maximum_fusion.6.refs_0_), channel_id=1, source_target_pairs={{0,1},{1,0},{2,3},{3,2},{4,5},{5,4},{6,7},{7,6},{8,9},{9,8},{10,11... | collective-permute-start | bytes 1179656 | tf_op jit(solution)/shard_map/ppermute | solution.py:230
  46.1 11.6 %collective-permute-start.12 = (bf16[96,1024]{1,0:T(8,128)(2,1)S(1)}, bf16[96,1024]{1,0:T(8,128)(2,1)S(1)}, u32[]{:S(2)}, u32[]{:S(2)}) collective-permute-start(bf16[96,1024]{1,0:T(8,128)(2,1)S(1)} %get-tuple-element.161), channel_id=1, source_target_pairs={{0,8},{1,9},{2,10},{3,11},{4,12},{5,13},{6,14},{7,15},{8,0},{9,1},... | collective-permute-start | bytes 589832 | tf_op jit(solution)/shard_map/ppermute | solution.py:234
  46.6 11.2 %collective-permute-start.15 = (bf16[192,1024]{1,0:T(8,128)(2,1)S(1)}, bf16[192,1024]{1,0:T(8,128)(2,1)S(1)}, u32[]{:S(2)}, u32[]{:S(2)}) collective-permute-start(bf16[192,1024]{1,0:T(8,128)(2,1)S(1)} %add_convert_fusion.1), channel_id=1, source_target_pairs={{0,2},{1,3},{2,0},{3,1},{4,6},{5,7},{6,4},{7,5},{8,10},{9,11},{10,... | collective-permute-start | bytes 1179656 | tf_op jit(solution)/shard_map/ppermute | solution.py:230
  50.7 7.0 %collective-permute-start.14 = (bf16[192,1024]{1,0:T(8,128)(2,1)S(1)}, bf16[192,1024]{1,0:T(8,128)(2,1)S(1)}, u32[]{:S(2)}, u32[]{:S(2)}) collective-permute-start(bf16[192,1024]{1,0:T(8,128)(2,1)S(1)} %get-tuple-element.173), channel_id=1, source_target_pairs={{0,1},{1,0},{2,3},{3,2},{4,5},{5,4},{6,7},{7,6},{8,9},{9,8},{10,11... | collective-permute-start | bytes 1179656 | tf_op jit(solution)/shard_map/ppermute | solution.py:230
  58.1 7.3 %collective-permute-start.16 = (bf16[96,1024]{1,0:T(8,128)(2,1)S(1)}, bf16[96,1024]{1,0:T(8,128)(2,1)S(1)}, u32[]{:S(2)}, u32[]{:S(2)}) collective-permute-start(bf16[96,1024]{1,0:T(8,128)(2,1)S(1)} %get-tuple-element.186), channel_id=1, source_target_pairs={{0,12},{1,13},{2,14},{3,15},{4,0},{5,1},{6,2},{7,3},{8,4},{9,5},{1... | collective-permute-start | bytes 589832 | tf_op jit(solution)/shard_map/ppermute | solution.py:234
  59.8 10.6 %collective-permute-start.17 = (bf16[96,1024]{1,0:T(8,128)(2,1)S(1)}, bf16[96,1024]{1,0:T(8,128)(2,1)S(1)}, u32[]{:S(2)}, u32[]{:S(2)}) collective-permute-start(bf16[96,1024]{1,0:T(8,128)(2,1)S(1)} %get-tuple-element.187), channel_id=1, source_target_pairs={{0,4},{1,5},{2,6},{3,7},{4,8},{5,9},{6,10},{7,11},{8,12},{9,13},{1... | collective-permute-start | bytes 589832 | tf_op jit(solution)/shard_map/ppermute | solution.py:234
  60.2 10.5 %collective-permute-start.18 = (bf16[192,1024]{1,0:T(8,128)(2,1)S(1)}, bf16[192,1024]{1,0:T(8,128)(2,1)S(1)}, u32[]{:S(2)}, u32[]{:S(2)}) collective-permute-start(bf16[192,1024]{1,0:T(8,128)(2,1)S(1)} %pad_maximum_fusion.9), channel_id=1, source_target_pairs={{0,2},{1,3},{2,0},{3,1},{4,6},{5,7},{6,4},{7,5},{8,10},{9,11},{10,... | collective-permute-start | bytes 1179656 | tf_op jit(solution)/shard_map/ppermute | solution.py:230
  70.9 3.6 %collective-permute-start.20 = (bf16[384,1024]{1,0:T(8,128)(2,1)S(1)}, bf16[384,1024]{1,0:T(8,128)(2,1)S(1)}, u32[]{:S(2)}, u32[]{:S(2)}) collective-permute-start(bf16[384,1024]{1,0:T(8,128)(2,1)S(1)} %pad_maximum_fusion.1), channel_id=1, source_target_pairs={{0,1},{1,0},{2,3},{3,2},{4,5},{5,4},{6,7},{7,6},{8,9},{9,8},{10,11... | collective-permute-start | bytes 2359304 | tf_op jit(solution)/shard_map/ppermute | solution.py:230
  71.0 12.4 %collective-permute-start.19 = (bf16[96,1024]{1,0:T(8,128)(2,1)S(1)}, bf16[96,1024]{1,0:T(8,128)(2,1)S(1)}, u32[]{:S(2)}, u32[]{:S(2)}) collective-permute-start(bf16[96,1024]{1,0:T(8,128)(2,1)S(1)} %add_convert_fusion.2), channel_id=1, source_target_pairs={{0,8},{1,9},{2,10},{3,11},{4,12},{5,13},{6,14},{7,15},{8,0},{9,1},... | collective-permute-start | bytes 589832 | tf_op jit(solution)/shard_map/ppermute | solution.py:234
  72.9 11.3 %collective-permute-start.21 = (bf16[192,1024]{1,0:T(8,128)(2,1)S(1)}, bf16[192,1024]{1,0:T(8,128)(2,1)S(1)}, u32[]{:S(2)}, u32[]{:S(2)}) collective-permute-start(bf16[192,1024]{1,0:T(8,128)(2,1)S(1)} %pad_maximum_fusion.11), channel_id=1, source_target_pairs={{0,2},{1,3},{2,0},{3,1},{4,6},{5,7},{6,4},{7,5},{8,10},{9,11},{10,... | collective-permute-start | bytes 1179656 | tf_op jit(solution)/shard_map/ppermute | solution.py:230
  83.4 1.0 %copy-start = (bf16[128,1024]{1,0:T(8,128)(2,1)S(1)}, bf16[128,1024]{1,0:T(8,128)(2,1)}, u32[]{:S(2)}) copy-start(bf16[128,1024]{1,0:T(8,128)(2,1)} %tokens_ref.1) | copy-start | bytes 786436
  83.4 1.0 %copy-start.1 = (s32[128,2]{0,1:T(2,128)S(1)}, s32[128,2]{0,1:T(2,128)}, u32[]{:S(2)}) copy-start(s32[128,2]{0,1:T(2,128)} %param.10) | copy-start | bytes 3076
  83.4 1.0 %copy-start.2 = (s32[128,2]{0,1:T(2,128)S(1)}, s32[128,2]{0,1:T(2,128)}, u32[]{:S(2)}) copy-start(s32[128,2]{0,1:T(2,128)} %param.11) | copy-start | bytes 3076
  84.2 2.4 %collective-permute-start.22 = (bf16[384,1024]{1,0:T(8,128)(2,1)S(1)}, bf16[384,1024]{1,0:T(8,128)(2,1)S(1)}, u32[]{:S(2)}, u32[]{:S(2)}) collective-permute-start(bf16[384,1024]{1,0:T(8,128)(2,1)S(1)} %pad_maximum_fusion.2.refs_2_), channel_id=1, source_target_pairs={{0,1},{1,0},{2,3},{3,2},{4,5},{5,4},{6,7},{7,6},{8,9},{9,8},{10,11... | collective-permute-start | bytes 2359304 | tf_op jit(solution)/shard_map/ppermute | solution.py:230

commit v9 on v7

--- a/solution.py
+++ b/solution.py
@@ -9,7 +9,22 @@
 
 HSPLIT = 4
 GROUPS = 4
-JOINED = ((1, 2), (2, 3))
+PLAN = (
+    ("yN0 zN1 zN2 loadW0", ""),
+    ("yC0 zN3", "yN0 zN1 zN2"),
+    ("cN0 yN1 zC1", "yC0 zN3 cN0"),
+    ("ffnN0 cR0 cC0 yN3 zC2", "yN1 zC1 cR0 cC0"),
+    ("cN1 yN2 zC3", "yN3 zC2 cN1"),
+    ("ffnN1 cR1 cN3 yR0", "yN2 zC3 cR1 cN3"),
+    ("ffnN3 cR3 cN2 yR1", "yR0 cR3 cN2"),
+    ("ffnN2 cR2 totalR0 yR3", "yR1 cR2"),
+    ("totalR1 zR1 yR2", "yR3"),
+    ("totalR3 zR3 yC1", "yR2 zR1"),
+    ("totalR2 zR2 yC2", "yC1 zR3"),
+    ("cC1 yC3", "yC2 zR2 cC1"),
+    ("cC2", "yC3 cC2"),
+    ("cC3 gradC0", None),
+)
 TILE = 256
 LINK_WORK = 10 << 30
 F32 = jnp.float32
@@ -108,6 +123,27 @@
         copy.wait()
 
 
+def pair_kernel(first_ref, second_ref, out_ref):
+    rows = first_ref.shape[0]
+    out_ref[:rows, :] = first_ref[...]
+    out_ref[rows:, :] = second_ref[...]
+
+
+def fold_kernel(keep_ref, crossed_ref, out_ref):
+    rows = out_ref.shape[0]
+    total = keep_ref[rows:, :].astype(F32) + crossed_ref[rows:, :].astype(F32)
+    out_ref[...] = total.astype(BF16)
+
+
+def total_kernel(keep_ref, crossed_ref, came_ref, *outs):
+    at = 0
+    for out in outs:
+        part = slice(at, at + out.shape[0])
+        total = keep_ref[part, :].astype(F32) + crossed_ref[part, :].astype(F32)
+        out[...] = (total + came_ref[part, :].astype(F32)).astype(BF16)
+        at += out.shape[0]
+
+
 def nothing(*refs):
     pass
 
@@ -239,54 +275,68 @@
     def join(parts):
         return parts[0] if len(parts) == 1 else jnp.concatenate(parts, 0)
 
-    flying = {}
-
-    def land(*earlier):
-        names = list(flying)
+    flying, slow = {}, []
+
+    def small(kernel, name, outs, *values):
+        return call(
+            kernel,
+            8,
+            name,
+            out_shape=[jax.ShapeDtypeStruct((rows, width), BF16) for rows in outs],
+            in_specs=whole(len(values)),
+            out_specs=whole(len(outs)),
+        )(*values)
+
+    def land(*names):
+        names = [n for name in names for n in flights_of(name)]
+        quick = [name for name in names if name[0] == "c"]
+        names = [name for name in names if name[0] != "c"]
         values = [flying.pop(name) for name in names]
-        if earlier:
-            values = lax.optimization_barrier(tuple(values) + earlier)[: len(names)]
+        if not names:
+            names, values = [("C", groups[-1][-1])], [live["C", groups[-1][-1]]]
         values = through(values, "land", LINK_WORK)
-        for name, value in zip(names, values):
-            if name[0] != "y":
-                live[name] = value
-                continue
-            at = 0
-            for kind, gs in name[1:]:
-                here = live.pop(("sent", kind, gs))
-                came = value[at : at + here.shape[0]]
-                at += here.shape[0]
-                if kind != "fold":
-                    live[kind, "own", gs] = join([here, came])
-                    continue
-                keep, crossed = live.pop(("keep", gs)), live.pop(("crossed", gs))
-                rows = came.shape[0]
-                total = keep[:rows].astype(F32) + crossed[:rows].astype(F32)
-                total = (total + came.astype(F32)).astype(BF16)
-                for i, s in enumerate([s for g in gs for s in groups[g]]):
-                    live["R", s] = total[i * capacity : (i + 1) * capacity]
-        return values[0]
-
-    def across(kind, *gs):
-        for s in [s for g in gs for s in groups[g]]:
+        landed = list(zip(names, values))
+        if quick:
+            cores = tuple(flying.pop(name) for name in quick) + (values[0],)
+            cores = lax.optimization_barrier(cores)[: len(quick)]
+            landed += list(zip(quick, through(cores, "land_core")))
+        live.update(landed)
+        sync()
+
+    def flights_of(name):
+        axis, kind, g = name
+        return [(kind, s) for s in groups[g] if s] if axis == "z" else [name]
+
+    def z(kind, g):
+        for s in groups[g]:
             if s:
                 flying[kind, s] = turn(live[kind, s], -s if kind == "R" else s)
 
-    def along(*items):
-        for kind, gs in items:
-            if kind == "fold":
-                value = live.pop(("across", gs))
-            else:
-                value = join([live.pop((kind, s)) for g in gs for s in groups[g]])
-            live["sent", kind, gs] = value
-        flying[("y",) + items] = swap(join([live["sent", kind, gs] for kind, gs in items]), 2)
-
-    def core(kind, *tuples):
-        gs = tuple(g for part in tuples for g in part)
-        live[kind, "other", gs] = swap(join([live[kind, "own", part] for part in tuples]), 1)
+    def y(kind, g):
+        if kind == "R":
+            keep, crossed = live["keep", (g,)], live["c", "R", g]
+            (value,) = small(fold_kernel, "fold", [height], keep, crossed)
+        else:
+            value = join([live.pop((kind, s)) for s in groups[g]])
+            live["sent", kind, g] = value
+        flying["y", kind, g] = swap(value, 2)
+
+    def c(kind, g):
+        if kind == "R":
+            value = live.pop(("send", (g,)))
+        else:
+            here, came = live.pop(("sent", kind, g)), live.pop(("y", kind, g))
+            (value,) = small(pair_kernel, "pair", [2 * height], here, came)
+            live[kind, "own", (g,)] = value
+        flying["c", kind, g] = swap(value, 1)
+
+    def total(g):
+        values = live.pop(("keep", (g,))), live.pop(("c", "R", g)), live.pop(("y", "R", g))
+        outs = small(total_kernel, "total", [capacity] * shifts, *values)
+        live.update({("R", s): out for s, out in zip(groups[g], outs)})
 
     def ffn(*gs):
-        pieces = [live.pop(("N", "own", gs)), live.pop(("N", "other", gs))]
+        pieces = [live.pop(("N", "own", gs)), live.pop(("c", "N", gs[0]))]
         half = jax.ShapeDtypeStruct(pieces[0].shape, BF16)
         rows = 2 * half.shape[0]
         live["turned", gs], live["keep", gs], live["send", gs] = call(
@@ -302,15 +352,6 @@
             ],
         )(*pieces, live["w", 0], live["w", 1], live["w", 2])
 
-    def cross(*gs):
-        live["crossed", gs] = swap(live.pop(("send", gs)), 1)
-
-    def fold_core(earlier, *gs):
-        keep, crossed = live["keep", gs], after(live["crossed", gs], earlier)
-        rows = keep.shape[0] // 2
-        both = keep[rows:].astype(F32) + crossed[rows:].astype(F32)
-        live["across", gs] = both.astype(BF16)
-
     def in_hbm(*values):
         return [pltpu.with_memory_space_constraint(v, pltpu.HBM) for v in values]
 
@@ -352,18 +393,16 @@
                         columns[half, side, g] = (i, at)
                         at += height
         plan = []
-        for i, (half, gs) in enumerate(pieces):
-            row = 0
-            for parts in [gs] if gs in JOINED else [(g,) for g in gs]:
-                for side in range(2):
-                    for g in parts:
-                        where, at = columns[half, side, g]
-                        plan.append((where, at, len(turned) + i, row, height))
-                        row += height
-        total = sum(step[-1] for step in plan)
-        sides = [pltpu.VMEM((hidden_width, total), BF16), pltpu.VMEM((total, width), BF16)]
+        for i, name in enumerate(pieces):
+            half = "other" if name[0] == "c" else "own"
+            g = name[-1] if half == "other" else name[-1][0]
+            for side in range(2):
+                where, at = columns[half, side, g]
+                plan.append((where, at, len(turned) + i, side * height, height))
+        rows = sum(step[-1] for step in plan)
+        sides = [pltpu.VMEM((hidden_width, rows), BF16), pltpu.VMEM((rows, width), BF16)]
         values = [live["turned", gs] for gs in turned]
-        values += [live["C", half, gs] for half, gs in pieces]
+        values += [live[name] for name in pieces]
         return plan, sides, values
 
     def first_grad(turned, pieces):
@@ -392,52 +431,32 @@
             + [pltpu.SemaphoreType.DMA((hidden_width // TILE,))],
         )(live["first"], *values)
 
+    steps = {
+        "z": z,
+        "y": y,
+        "c": c,
+        "ffn": lambda kind, g: ffn(g),
+        "total": lambda kind, g: total(g),
+        "load": lambda kind, g: load(),
+        "grad": lambda kind, g: first_grad(
+            [(0,), (1,), (2,)],
+            [("C", "own", (i,)) for i in range(3)] + [("c", "C", i) for i in range(3)],
+        ),
+    }
     send()
     if shifts > 1:
-        across("N", 0)
-        across("C", 0)
-        land()
+        z("N", 0)
+        z("C", 0)
+        land(("z", "N", 0), ("z", "C", 0))
     sync()
-    across("N", 1, 2)
-    along(("N", (0,)), ("C", (0,)))
-    load()
-    land()
-    sync()
-    across("N", 3)
-    along(("N", (1, 2)))
-    core("N", (0,))
-    ffn(0)
-    cross(0)
-    fold_core(land(), 0)
-    sync()
-    across("C", 1, 2)
-    along(("N", (3,)), ("fold", (0,)))
-    core("N", (1, 2))
-    ffn(1, 2)
-    cross(1, 2)
-    fold_core(land(), 1, 2)
-    sync()
-    across("C", 3)
-    along(("fold", (1, 2)))
-    core("N", (3,))
-    ffn(3)
-    cross(3)
-    fold_core(land(), 3)
-    sync()
-    if shifts > 1:
-        across("R", 0)
-    across("R", 1, 2)
-    along(("fold", (3,)), ("C", (1,)))
-    land()
-    sync()
-    across("R", 3)
-    along(("C", (2, 3)))
-    core("C", (0,), (1,))
-    first_grad([(0,), (1, 2)], [("own", (0,)), ("own", (1,)), ("other", (0, 1))])
-    land(live["first"])
-    sync()
-    core("C", (2, 3))
-    grad_down = last_grad([(1, 2), (3,)], [("own", (2, 3)), ("other", (2, 3))])
+    for starts, lands in PLAN:
+        for act in starts.split():
+            steps[act[:-2]](act[-2], int(act[-1]))
+        if lands is None:
+            break
+        land(*[(act[:-2], act[-2], int(act[-1])) for act in lands.split()])
+    live["c", "C", 3] = flying.pop(("c", "C", 3))
+    grad_down = last_grad([(3,)], [("C", "own", (3,)), ("c", "C", 3)])
     mixed = call(
         functools.partial(combine_kernel, experts),
         16,

time: 88.2 us -> 89.8 us (1.018)
  starting transfers between devices: 23.3 us -> 27.3 us
  waiting for transfers between devices: 40.5 us -> 38.8 us
  Pallas kernels: 21.2 us -> 22.4 us
  other arithmetic: 0.99 us -> 0 us
    ppermute x9, waiting for transfers between devices: 39.9 us -> 25 us  [turn(): return lax.ppermute(value, 'expert', to)]
    ppermute x14 -> x24, waiting for transfers between devices: 0.59 us -> 13.8 us  [swap(): lax.ppermute(value, 'expert', [(i, i ^ mask) for i in range(devices)])]
    ppermute x14 -> x24, starting transfers between devices: 9.07 us -> 17.6 us  [swap(): lax.ppermute(value, 'expert', [(i, i ^ mask) for i in range(devices)])]
    ppermute x9, starting transfers between devices: 14.2 us -> 9.73 us  [turn(): return lax.ppermute(value, 'expert', to)]
    pallas_call x1, Pallas kernels: 1.95 us -> 2.92 us  [first_grad(): call(functools.partial(first_grad_kernel, plan), 24, 'first_grad', out_sh...]
    pallas_call x3 -> x4, Pallas kernels: 10.3 us -> 10.5 us  [ffn(): call(functools.partial(ffn_kernel, len(pieces)), 24, 'ffn', out_shape=[ja...]
  transfers between devices with their start and end apart: 23 -> 33, of which waited for: 11 -> 12; matrix products, arithmetic and copies ran while one was open for 1% -> 0% of each run, Pallas kernels for 19% -> 20%
where the time goes in v9:
time: 89.8 us; the launch traced here: 89.6 us
  waiting for transfers between devices  38.8 us (43%)
  starting transfers between devices  27.3 us (30%)
  Pallas kernels  22.4 us (25%)
  between operations  1.11 us (1%)
    ppermute x9, waiting for transfers between devices, turn(): return lax.ppermute(value, 'expert', to)  25 us
    ppermute x24, starting transfers between devices, swap(): lax.ppermute(value, 'expert', [(i, i ^ mask) for i in range(devices)])  17.6 us
    ppermute x24, waiting for transfers between devices, swap(): lax.ppermute(value, 'expert', [(i, i ^ mask) for i in range(devices)])  13.8 us
    pallas_call x4, Pallas kernels, ffn(): call(functools.partial(ffn_kernel, len(pieces)), 24, 'ffn', out_shape=[ja...  10.5 us
    ppermute x9, starting transfers between devices, turn(): return lax.ppermute(value, 'expert', to)  9.73 us
    pallas_call x1, Pallas kernels, first_grad(): call(functools.partial(first_grad_kernel, plan), 24, 'first_grad', out_sh...  2.92 us
    pallas_call x1, Pallas kernels, load(): call(load_kernel, 16, 'load', out_shape=[weight, weight, jax.ShapeDtypeSt...  2.88 us
    pallas_call x1, Pallas kernels, last_grad(): call(functools.partial(last_grad_kernel, plan), 24, 'last_grad', out_shap...  2.1 us
  transfers between devices with their start and end apart: 33, of which 12 were waited for; matrix products, arithmetic and copies ran while one was open for 0% of the time, Pallas kernels for 20%

profile of v9, /device:TPU:0, one launch (start us, length us, event | category | flops | bytes accessed | tf_op | source)
XLA Modules:
  0.0 89.6 jit_solution(8782974910262067863)
XLA Ops:
  0.6 1.9 %send.1 = (bf16[96,1024]{1,0:T(8,128)(2,1)S(1)}, bf16[96,1024]{1,0:T(8,128)(2,1)S(1)}, bf16[96,1024]{1,0:T(8,128)(2,1)S(1)}, bf16[96,1024]{1,0:T(8,128)(2,1)S(1)...) custom-call(s32[1]{0:T(128)} %bitcast.plane_ref, ...), custom_call_target="tpu_custom_call" | custom-call | tf_op jit(solution)/shard_map/send/pallas_call | solution.py:360
  2.6 3.1 %collective-permute-start.3 = (bf16[96,1024]{1,0:T(8,128)(2,1)S(1)}, bf16[96,1024]{1,0:T(8,128)(2,1)S(1)}, u32[]{:S(2)}, u32[]{:S(2)}) collective-permute-start(bf16[96,1024]{1,0:T(8,128)(2,1)S(1)} %get-tuple-element.249), channel_id=1, source_target_pairs={{0,4},{1,5},{2,6},{3,7},{4,8},{5,9},{6,10},{7,11},{8,12},{9,13},{1... | collective-permute-start | bytes 589832 | tf_op jit(solution)/shard_map/ppermute | solution.py:269
  5.7 2.1 %collective-permute-start.4 = (bf16[96,1024]{1,0:T(8,128)(2,1)S(1)}, bf16[96,1024]{1,0:T(8,128)(2,1)S(1)}, u32[]{:S(2)}, u32[]{:S(2)}) collective-permute-start(bf16[96,1024]{1,0:T(8,128)(2,1)S(1)} %get-tuple-element.251), channel_id=1, source_target_pairs={{0,12},{1,13},{2,14},{3,15},{4,0},{5,1},{6,2},{7,3},{8,4},{9,5},{1... | collective-permute-start | bytes 589832 | tf_op jit(solution)/shard_map/ppermute | solution.py:269
  7.8 1.7 %collective-permute-start.2 = (bf16[96,1024]{1,0:T(8,128)(2,1)S(1)}, bf16[96,1024]{1,0:T(8,128)(2,1)S(1)}, u32[]{:S(2)}, u32[]{:S(2)}) collective-permute-start(bf16[96,1024]{1,0:T(8,128)(2,1)S(1)} %get-tuple-element.282.first_ref), channel_id=1, source_target_pairs={{0,2},{1,3},{2,0},{3,1},{4,6},{5,7},{6,4},{7,5},{8,10},{9,11},{10,... | collective-permute-start | bytes 589832 | tf_op jit(solution)/shard_map/ppermute | solution.py:265
  9.4 2.9 %load.1 = (bf16[1024,1024]{1,0:T(8,128)(2,1)S(1)}, bf16[1024,1024]{1,0:T(8,128)(2,1)S(1)}, bf16[1024,1024]{1,0:T(8,128)(2,1)S(1)}) custom-call(bf16[1,1024,1024]{2,1,0:T(8,128)(2,1)} %refs_0_.2, bf16[1,1024,1024]{2,1,0:T(8,128)(2,1)} %refs_1_.3, bf16[1,1024,1024]{2,1,0:T(8,128)(2,1)} %refs_2_.1), custom_call_target="tpu_custom_call" | custom-call | tf_op jit(solution)/shard_map/load/pallas_call | solution.py:375
  13.7 2.5 %collective-permute-done.4.refs_2_ = bf16[96,1024]{1,0:T(8,128)(2,1)S(1)} collective-permute-done((bf16[96,1024]{1,0:T(8,128)(2,1)S(1)}, bf16[96,1024]{1,0:T(8,128)(2,1)S(1)}, u32[]{:S(2)}, u32[]{:S(2)}) %collective-permute-start.4) | collective-permute-done | bytes 196640 | tf_op jit(solution)/shard_map/ppermute | solution.py:269
  16.2 2.1 %collective-permute-start.7 = (bf16[96,1024]{1,0:T(8,128)(2,1)S(1)}, bf16[96,1024]{1,0:T(8,128)(2,1)S(1)}, u32[]{:S(2)}, u32[]{:S(2)}) collective-permute-start(bf16[96,1024]{1,0:T(8,128)(2,1)S(1)} %get-tuple-element.275), channel_id=1, source_target_pairs={{0,4},{1,5},{2,6},{3,7},{4,8},{5,9},{6,10},{7,11},{8,12},{9,13},{1... | collective-permute-start | bytes 589832 | tf_op jit(solution)/shard_map/ppermute | solution.py:269
  18.3 1.8 %collective-permute-start.6 = (bf16[96,1024]{1,0:T(8,128)(2,1)S(1)}, bf16[96,1024]{1,0:T(8,128)(2,1)S(1)}, u32[]{:S(2)}, u32[]{:S(2)}) collective-permute-start(bf16[96,1024]{1,0:T(8,128)(2,1)S(1)} %get-tuple-element.320.first_ref), channel_id=1, source_target_pairs={{0,2},{1,3},{2,0},{3,1},{4,6},{5,7},{6,4},{7,5},{8,10},{9,11},{10,... | collective-permute-start | bytes 589832 | tf_op jit(solution)/shard_map/ppermute | solution.py:265
  20.2 9.3 %collective-permute-done.1.refs_1_ = bf16[96,1024]{1,0:T(8,128)(2,1)S(1)} collective-permute-done((bf16[96,1024]{1,0:T(8,128)(2,1)S(1)}, bf16[96,1024]{1,0:T(8,128)(2,1)S(1)}, u32[]{:S(2)}, u32[]{:S(2)}) %collective-permute-start.1) | collective-permute-done | bytes 196640 | tf_op jit(solution)/shard_map/ppermute | solution.py:269
  29.5 1.6 %collective-permute-start.10 = (bf16[96,1024]{1,0:T(8,128)(2,1)S(1)}, bf16[96,1024]{1,0:T(8,128)(2,1)S(1)}, u32[]{:S(2)}, u32[]{:S(2)}) collective-permute-start(bf16[96,1024]{1,0:T(8,128)(2,1)S(1)} %get-tuple-element.341.first_ref), channel_id=1, source_target_pairs={{0,2},{1,3},{2,0},{3,1},{4,6},{5,7},{6,4},{7,5},{8,10},{9,11},{10,... | collective-permute-start | bytes 589832 | tf_op jit(solution)/shard_map/ppermute | solution.py:265
  31.1 2.6 %ffn.4 = (bf16[1024,384]{1,0:T(8,128)(2,1)S(1)}, bf16[192,1024]{1,0:T(8,128)(2,1)S(1)}, bf16[192,1024]{1,0:T(8,128)(2,1)S(1)}) custom-call(bf16[192,1024]{1,0:T(8,128)(2,1)S(1)} %pair.8.refs_0_, bf16[192,1024]{1,0:T(8,128)(2,1)S(1)} %land_core.8.refs_1_, bf16[1024,1024]{1,0:T(8,128)(2,1)S(1)} %get-tuple-element.377.refs_2_, ...), custom_call_target="tpu_custom_call" | custom-call | tf_op jit(solution)/shard_map/ffn/pallas_call | solution.py:342
  34.3 1.3 %collective-permute-done.8.refs_0_ = bf16[192,1024]{1,0:T(8,128)(2,1)S(1)} collective-permute-done((bf16[192,1024]{1,0:T(8,128)(2,1)S(1)}, bf16[192,1024]{1,0:T(8,128)(2,1)S(1)}, u32[]{:S(2)}, u32[]{:S(2)}) %collective-permute-start.8) | collective-permute-done | bytes 393248 | tf_op jit(solution)/shard_map/ppermute | solution.py:265
  36.4 1.6 %collective-permute-done.12.refs_0_ = bf16[192,1024]{1,0:T(8,128)(2,1)S(1)} collective-permute-done((bf16[192,1024]{1,0:T(8,128)(2,1)S(1)}, bf16[192,1024]{1,0:T(8,128)(2,1)S(1)}, u32[]{:S(2)}, u32[]{:S(2)}) %collective-permute-start.12) | collective-permute-done | bytes 393248 | tf_op jit(solution)/shard_map/ppermute | solution.py:265
  38.1 1.6 %collective-permute-start.17 = (bf16[96,1024]{1,0:T(8,128)(2,1)S(1)}, bf16[96,1024]{1,0:T(8,128)(2,1)S(1)}, u32[]{:S(2)}, u32[]{:S(2)}) collective-permute-start(bf16[96,1024]{1,0:T(8,128)(2,1)S(1)} %fold.4), channel_id=1, source_target_pairs={{0,2},{1,3},{2,0},{3,1},{4,6},{5,7},{6,4},{7,5},{8,10},{9,11},{10,... | collective-permute-start | bytes 589832 | tf_op jit(solution)/shard_map/ppermute | solution.py:265
  39.8 2.6 %ffn.5 = (bf16[1024,384]{1,0:T(8,128)(2,1)S(1)}, bf16[192,1024]{1,0:T(8,128)(2,1)S(1)}, bf16[192,1024]{1,0:T(8,128)(2,1)S(1)}) custom-call(bf16[192,1024]{1,0:T(8,128)(2,1)S(1)} %pair.10.refs_0_, bf16[192,1024]{1,0:T(8,128)(2,1)S(1)} %land_core.10.refs_1_, bf16[1024,1024]{1,0:T(8,128)(2,1)S(1)} %get-tuple-element.377.refs_2_, ...), custom_call_target="tpu_custom_call" | custom-call | tf_op jit(solution)/shard_map/ffn/pallas_call | solution.py:342
  43.0 5.0 %collective-permute-done.14.refs_1_ = bf16[96,1024]{1,0:T(8,128)(2,1)S(1)} collective-permute-done((bf16[96,1024]{1,0:T(8,128)(2,1)S(1)}, bf16[96,1024]{1,0:T(8,128)(2,1)S(1)}, u32[]{:S(2)}, u32[]{:S(2)}) %collective-permute-start.14) | collective-permute-done | bytes 196640 | tf_op jit(solution)/shard_map/ppermute | solution.py:269
  48.7 2.6 %ffn.6 = (bf16[1024,384]{1,0:T(8,128)(2,1)S(1)}, bf16[192,1024]{1,0:T(8,128)(2,1)S(1)}, bf16[192,1024]{1,0:T(8,128)(2,1)S(1)}) custom-call(bf16[192,1024]{1,0:T(8,128)(2,1)S(1)} %pair.11.refs_0_, bf16[192,1024]{1,0:T(8,128)(2,1)S(1)} %get-tuple-element.364.refs_1_, bf16[1024,1024]{1,0:T(8,128)(2,1)S(1)} %get-tuple-element.377.refs_2_, ...), custom_call_target="tpu_custom_call" | custom-call | tf_op jit(solution)/shard_map/ffn/pallas_call | solution.py:342
  51.9 1.3 %collective-permute-done.18.refs_0_ = bf16[192,1024]{1,0:T(8,128)(2,1)S(1)} collective-permute-done((bf16[192,1024]{1,0:T(8,128)(2,1)S(1)}, bf16[192,1024]{1,0:T(8,128)(2,1)S(1)}, u32[]{:S(2)}, u32[]{:S(2)}) %collective-permute-start.18) | collective-permute-done | bytes 393248 | tf_op jit(solution)/shard_map/ppermute | solution.py:265
  53.3 1.6 %collective-permute-start.22 = (bf16[96,1024]{1,0:T(8,128)(2,1)S(1)}, bf16[96,1024]{1,0:T(8,128)(2,1)S(1)}, u32[]{:S(2)}, u32[]{:S(2)}) collective-permute-start(bf16[96,1024]{1,0:T(8,128)(2,1)S(1)} %fold.6), channel_id=1, source_target_pairs={{0,2},{1,3},{2,0},{3,1},{4,6},{5,7},{6,4},{7,5},{8,10},{9,11},{10,... | collective-permute-start | bytes 589832 | tf_op jit(solution)/shard_map/ppermute | solution.py:265
  54.9 2.6 %ffn.7 = (bf16[1024,384]{1,0:T(8,128)(2,1)S(1)}, bf16[192,1024]{1,0:T(8,128)(2,1)S(1)}, bf16[192,1024]{1,0:T(8,128)(2,1)S(1)}) custom-call(bf16[192,1024]{1,0:T(8,128)(2,1)S(1)} %pair.12.refs_0_, bf16[192,1024]{1,0:T(8,128)(2,1)S(1)} %get-tuple-element.390.refs_1_, bf16[1024,1024]{1,0:T(8,128)(2,1)S(1)} %get-tuple-element.377.refs_2_, ...), custom_call_target="tpu_custom_call" | custom-call | tf_op jit(solution)/shard_map/ffn/pallas_call | solution.py:342
  57.8 1.6 %collective-permute-done.21.refs_0_ = bf16[192,1024]{1,0:T(8,128)(2,1)S(1)} collective-permute-done((bf16[192,1024]{1,0:T(8,128)(2,1)S(1)}, bf16[192,1024]{1,0:T(8,128)(2,1)S(1)}, u32[]{:S(2)}, u32[]{:S(2)}) %collective-permute-start.21) | collective-permute-done | bytes 393248 | tf_op jit(solution)/shard_map/ppermute | solution.py:265
  61.4 1.6 %collective-permute-start.25 = (bf16[96,1024]{1,0:T(8,128)(2,1)S(1)}, bf16[96,1024]{1,0:T(8,128)(2,1)S(1)}, u32[]{:S(2)}, u32[]{:S(2)}) collective-permute-start(bf16[96,1024]{1,0:T(8,128)(2,1)S(1)} %get-tuple-element.459.first_ref), channel_id=1, source_target_pairs={{0,2},{1,3},{2,0},{3,1},{4,6},{5,7},{6,4},{7,5},{8,10},{9,11},{10,... | collective-permute-start | bytes 589832 | tf_op jit(solution)/shard_map/ppermute | solution.py:265
  63.0 4.2 %collective-permute-done.23.refs_0_ = bf16[96,1024]{1,0:T(8,128)(2,1)S(1)} collective-permute-done((bf16[96,1024]{1,0:T(8,128)(2,1)S(1)}, bf16[96,1024]{1,0:T(8,128)(2,1)S(1)}, u32[]{:S(2)}, u32[]{:S(2)}) %collective-permute-start.23) | collective-permute-done | bytes 196640 | tf_op jit(solution)/shard_map/ppermute | solution.py:265
  67.2 1.3 %collective-permute-done.24.refs_1_ = bf16[96,1024]{1,0:T(8,128)(2,1)S(1)} collective-permute-done((bf16[96,1024]{1,0:T(8,128)(2,1)S(1)}, bf16[96,1024]{1,0:T(8,128)(2,1)S(1)}, u32[]{:S(2)}, u32[]{:S(2)}) %collective-permute-start.24) | collective-permute-done | bytes 196640 | tf_op jit(solution)/shard_map/ppermute | solution.py:269
  68.8 1.6 %collective-permute-start.27 = (bf16[96,1024]{1,0:T(8,128)(2,1)S(1)}, bf16[96,1024]{1,0:T(8,128)(2,1)S(1)}, u32[]{:S(2)}, u32[]{:S(2)}) collective-permute-start(bf16[96,1024]{1,0:T(8,128)(2,1)S(1)} %get-tuple-element.477.first_ref), channel_id=1, source_target_pairs={{0,2},{1,3},{2,0},{3,1},{4,6},{5,7},{6,4},{7,5},{8,10},{9,11},{10,... | collective-permute-start | bytes 589832 | tf_op jit(solution)/shard_map/ppermute | solution.py:265
  70.4 6.8 %collective-permute-done.26.refs_1_ = bf16[96,1024]{1,0:T(8,128)(2,1)S(1)} collective-permute-done((bf16[96,1024]{1,0:T(8,128)(2,1)S(1)}, bf16[96,1024]{1,0:T(8,128)(2,1)S(1)}, u32[]{:S(2)}, u32[]{:S(2)}) %collective-permute-start.26) | collective-permute-done | bytes 196640 | tf_op jit(solution)/shard_map/ppermute | solution.py:269
  77.2 1.5 %collective-permute-start.30 = (bf16[96,1024]{1,0:T(8,128)(2,1)S(1)}, bf16[96,1024]{1,0:T(8,128)(2,1)S(1)}, u32[]{:S(2)}, u32[]{:S(2)}) collective-permute-start(bf16[96,1024]{1,0:T(8,128)(2,1)S(1)} %get-tuple-element.494.first_ref), channel_id=1, source_target_pairs={{0,2},{1,3},{2,0},{3,1},{4,6},{5,7},{6,4},{7,5},{8,10},{9,11},{10,... | collective-permute-start | bytes 589832 | tf_op jit(solution)/shard_map/ppermute | solution.py:265
  78.9 1.7 %collective-permute-done.29.refs_0_ = bf16[192,1024]{1,0:T(8,128)(2,1)S(1)} collective-permute-done((bf16[192,1024]{1,0:T(8,128)(2,1)S(1)}, bf16[192,1024]{1,0:T(8,128)(2,1)S(1)}, u32[]{:S(2)}, u32[]{:S(2)}) %collective-permute-start.29) | collective-permute-done | bytes 393248 | tf_op jit(solution)/shard_map/ppermute | solution.py:265
  80.8 2.1 %collective-permute-done.30.refs_0_ = bf16[96,1024]{1,0:T(8,128)(2,1)S(1)} collective-permute-done((bf16[96,1024]{1,0:T(8,128)(2,1)S(1)}, bf16[96,1024]{1,0:T(8,128)(2,1)S(1)}, u32[]{:S(2)}, u32[]{:S(2)}) %collective-permute-start.30) | collective-permute-done | bytes 196640 | tf_op jit(solution)/shard_map/ppermute | solution.py:265
  83.0 1.4 %combine.1 = bf16[128,1024]{1,0:T(8,128)(2,1)} custom-call(s32[1]{0:T(128)} %bitcast.plane_ref, bf16[128,1024]{1,0:T(8,128)(2,1)S(1)} %copy-done, s32[2,128]{1,0:T(2,128)S(1)} %bitcast.5, s32[2,128]{1,0:T(2,128)S(1)} %bitcast.7, bf16[96,1024]{1,0:T(8,128)(2,1)S(1)} %total.4.refs_0_, bf16[96,1024]{1,0:T(8,128)(2,1)S(1)} %get-tuple-element.481.refs_1_, ...), custom_call_target="tpu_custom_call" | custom-call | tf_op jit(solution)/shard_map/combine/pallas_call | solution.py:460
  84.4 2.9 %first_grad.1.first_ref = f32[1024,1024]{1,0:T(8,128)S(1)} custom-call(bf16[1024,384]{1,0:T(8,128)(2,1)S(1)} %get-tuple-element.484.refs_0_, bf16[1024,384]{1,0:T(8,128)(2,1)S(1)} %get-tuple-element.485.refs_1_, bf16[1024,384]{1,0:T(8,128)(2,1)S(1)} %get-tuple-element.486.refs_2_, bf16[192,1024]{1,0:T(8,128)(2,1)S(1)} %pair.9.refs_3_, ...), custom_call_target="tpu_custom_call" | custom-call | tf_op jit(solution)/shard_map/first_grad/pallas_call | solution.py:410
  87.4 2.1 %last_grad.1 = bf16[1,1024,1024]{2,1,0:T(8,128)(2,1)} custom-call(f32[1024,1024]{1,0:T(8,128)S(1)} %first_grad.1.first_ref, bf16[1024,384]{1,0:T(8,128)(2,1)S(1)} %get-tuple-element.493.refs_0_, bf16[192,1024]{1,0:T(8,128)(2,1)S(1)} %pair.15.refs_1_, bf16[192,1024]{1,0:T(8,128)(2,1)S(1)} %collective-permute-done.32.refs_2_), custom_call_target="tpu_custom_call" | custom-call | tf_op jit(solution)/shard_map/last_grad/pallas_call | solution.py:422
  (86 shorter events, 8.0 us)
Async XLA Ops:
  2.6 11.1 %collective-permute-start.3 = (bf16[96,1024]{1,0:T(8,128)(2,1)S(1)}, bf16[96,1024]{1,0:T(8,128)(2,1)S(1)}, u32[]{:S(2)}, u32[]{:S(2)}) collective-permute-start(bf16[96,1024]{1,0:T(8,128)(2,1)S(1)} %get-tuple-element.249), channel_id=1, source_target_pairs={{0,4},{1,5},{2,6},{3,7},{4,8},{5,9},{6,10},{7,11},{8,12},{9,13},{1... | collective-permute-start | bytes 589832 | tf_op jit(solution)/shard_map/ppermute | solution.py:269
  5.7 10.6 %collective-permute-start.4 = (bf16[96,1024]{1,0:T(8,128)(2,1)S(1)}, bf16[96,1024]{1,0:T(8,128)(2,1)S(1)}, u32[]{:S(2)}, u32[]{:S(2)}) collective-permute-start(bf16[96,1024]{1,0:T(8,128)(2,1)S(1)} %get-tuple-element.251), channel_id=1, source_target_pairs={{0,12},{1,13},{2,14},{3,15},{4,0},{5,1},{6,2},{7,3},{8,4},{9,5},{1... | collective-permute-start | bytes 589832 | tf_op jit(solution)/shard_map/ppermute | solution.py:269
  7.8 8.5 %collective-permute-start.2 = (bf16[96,1024]{1,0:T(8,128)(2,1)S(1)}, bf16[96,1024]{1,0:T(8,128)(2,1)S(1)}, u32[]{:S(2)}, u32[]{:S(2)}) collective-permute-start(bf16[96,1024]{1,0:T(8,128)(2,1)S(1)} %get-tuple-element.282.first_ref), channel_id=1, source_target_pairs={{0,2},{1,3},{2,0},{3,1},{4,6},{5,7},{6,4},{7,5},{8,10},{9,11},{10,... | collective-permute-start | bytes 589832 | tf_op jit(solution)/shard_map/ppermute | solution.py:265
  12.3 7.9 %collective-permute-start = (bf16[96,1024]{1,0:T(8,128)(2,1)S(1)}, bf16[96,1024]{1,0:T(8,128)(2,1)S(1)}, u32[]{:S(2)}, u32[]{:S(2)}) collective-permute-start(bf16[96,1024]{1,0:T(8,128)(2,1)S(1)} %get-tuple-element.299.first_ref), channel_id=1, source_target_pairs={{0,2},{1,3},{2,0},{3,1},{4,6},{5,7},{6,4},{7,5},{8,10},{9,11},{10,... | collective-permute-start | bytes 589832 | tf_op jit(solution)/shard_map/ppermute | solution.py:265
  12.7 16.7 %collective-permute-start.1 = (bf16[96,1024]{1,0:T(8,128)(2,1)S(1)}, bf16[96,1024]{1,0:T(8,128)(2,1)S(1)}, u32[]{:S(2)}, u32[]{:S(2)}) collective-permute-start(bf16[96,1024]{1,0:T(8,128)(2,1)S(1)} %get-tuple-element.262), channel_id=1, source_target_pairs={{0,8},{1,9},{2,10},{3,11},{4,12},{5,13},{6,14},{7,15},{8,0},{9,1},... | collective-permute-start | bytes 589832 | tf_op jit(solution)/shard_map/ppermute | solution.py:269
  16.2 17.5 %collective-permute-start.7 = (bf16[96,1024]{1,0:T(8,128)(2,1)S(1)}, bf16[96,1024]{1,0:T(8,128)(2,1)S(1)}, u32[]{:S(2)}, u32[]{:S(2)}) collective-permute-start(bf16[96,1024]{1,0:T(8,128)(2,1)S(1)} %get-tuple-element.275), channel_id=1, source_target_pairs={{0,4},{1,5},{2,6},{3,7},{4,8},{5,9},{6,10},{7,11},{8,12},{9,13},{1... | collective-permute-start | bytes 589832 | tf_op jit(solution)/shard_map/ppermute | solution.py:269
  18.3 16.0 %collective-permute-start.6 = (bf16[96,1024]{1,0:T(8,128)(2,1)S(1)}, bf16[96,1024]{1,0:T(8,128)(2,1)S(1)}, u32[]{:S(2)}, u32[]{:S(2)}) collective-permute-start(bf16[96,1024]{1,0:T(8,128)(2,1)S(1)} %get-tuple-element.320.first_ref), channel_id=1, source_target_pairs={{0,2},{1,3},{2,0},{3,1},{4,6},{5,7},{6,4},{7,5},{8,10},{9,11},{10,... | collective-permute-start | bytes 589832 | tf_op jit(solution)/shard_map/ppermute | solution.py:265
  20.1 9.4 %collective-permute-start.5 = (bf16[192,1024]{1,0:T(8,128)(2,1)S(1)}, bf16[192,1024]{1,0:T(8,128)(2,1)S(1)}, u32[]{:S(2)}, u32[]{:S(2)}) collective-permute-start(bf16[192,1024]{1,0:T(8,128)(2,1)S(1)} %pair.8.refs_0_), channel_id=1, source_target_pairs={{0,1},{1,0},{2,3},{3,2},{4,5},{5,4},{6,7},{7,6},{8,9},{9,8},{10,11... | collective-permute-start | bytes 1179656 | tf_op jit(solution)/shard_map/ppermute | solution.py:265
  29.4 6.9 %collective-permute-start.11 = (bf16[96,1024]{1,0:T(8,128)(2,1)S(1)}, bf16[96,1024]{1,0:T(8,128)(2,1)S(1)}, u32[]{:S(2)}, u32[]{:S(2)}) collective-permute-start(bf16[96,1024]{1,0:T(8,128)(2,1)S(1)} %get-tuple-element.290), channel_id=1, source_target_pairs={{0,12},{1,13},{2,14},{3,15},{4,0},{5,1},{6,2},{7,3},{8,4},{9,5},{1... | collective-permute-start | bytes 589832 | tf_op jit(solution)/shard_map/ppermute | solution.py:269
  29.5 6.9 %collective-permute-start.10 = (bf16[96,1024]{1,0:T(8,128)(2,1)S(1)}, bf16[96,1024]{1,0:T(8,128)(2,1)S(1)}, u32[]{:S(2)}, u32[]{:S(2)}) collective-permute-start(bf16[96,1024]{1,0:T(8,128)(2,1)S(1)} %get-tuple-element.341.first_ref), channel_id=1, source_target_pairs={{0,2},{1,3},{2,0},{3,1},{4,6},{5,7},{6,4},{7,5},{8,10},{9,11},{10,... | collective-permute-start | bytes 589832 | tf_op jit(solution)/shard_map/ppermute | solution.py:265
  31.1 3.3 %collective-permute-start.9 = (bf16[192,1024]{1,0:T(8,128)(2,1)S(1)}, bf16[192,1024]{1,0:T(8,128)(2,1)S(1)}, u32[]{:S(2)}, u32[]{:S(2)}) collective-permute-start(bf16[192,1024]{1,0:T(8,128)(2,1)S(1)} %pair.9.refs_3_), channel_id=1, source_target_pairs={{0,1},{1,0},{2,3},{3,2},{4,5},{5,4},{6,7},{7,6},{8,9},{9,8},{10,11... | collective-permute-start | bytes 1179656 | tf_op jit(solution)/shard_map/ppermute | solution.py:265
  33.8 1.9 %collective-permute-start.8 = (bf16[192,1024]{1,0:T(8,128)(2,1)S(1)}, bf16[192,1024]{1,0:T(8,128)(2,1)S(1)}, u32[]{:S(2)}, u32[]{:S(2)}) collective-permute-start(bf16[192,1024]{1,0:T(8,128)(2,1)S(1)} %get-tuple-element.303), channel_id=1, source_target_pairs={{0,1},{1,0},{2,3},{3,2},{4,5},{5,4},{6,7},{7,6},{8,9},{9,8},{10,11... | collective-permute-start | bytes 1179656 | tf_op jit(solution)/shard_map/ppermute | solution.py:265
  35.7 12.3 %collective-permute-start.14 = (bf16[96,1024]{1,0:T(8,128)(2,1)S(1)}, bf16[96,1024]{1,0:T(8,128)(2,1)S(1)}, u32[]{:S(2)}, u32[]{:S(2)}) collective-permute-start(bf16[96,1024]{1,0:T(8,128)(2,1)S(1)} %land.13), channel_id=1, source_target_pairs={{0,8},{1,9},{2,10},{3,11},{4,12},{5,13},{6,14},{7,15},{8,0},{9,1},... | collective-permute-start | bytes 589832 | tf_op jit(solution)/shard_map/ppermute | solution.py:269
  35.7 12.3 %collective-permute-start.13 = (bf16[96,1024]{1,0:T(8,128)(2,1)S(1)}, bf16[96,1024]{1,0:T(8,128)(2,1)S(1)}, u32[]{:S(2)}, u32[]{:S(2)}) collective-permute-start(bf16[96,1024]{1,0:T(8,128)(2,1)S(1)} %get-tuple-element.367.first_ref), channel_id=1, source_target_pairs={{0,2},{1,3},{2,0},{3,1},{4,6},{5,7},{6,4},{7,5},{8,10},{9,11},{10,... | collective-permute-start | bytes 589832 | tf_op jit(solution)/shard_map/ppermute | solution.py:265
  36.2 1.8 %collective-permute-start.12 = (bf16[192,1024]{1,0:T(8,128)(2,1)S(1)}, bf16[192,1024]{1,0:T(8,128)(2,1)S(1)}, u32[]{:S(2)}, u32[]{:S(2)}) collective-permute-start(bf16[192,1024]{1,0:T(8,128)(2,1)S(1)} %pair.10.refs_0_), channel_id=1, source_target_pairs={{0,1},{1,0},{2,3},{3,2},{4,5},{5,4},{6,7},{7,6},{8,9},{9,8},{10,11... | collective-permute-start | bytes 1179656 | tf_op jit(solution)/shard_map/ppermute | solution.py:265
  38.1 13.8 %collective-permute-start.17 = (bf16[96,1024]{1,0:T(8,128)(2,1)S(1)}, bf16[96,1024]{1,0:T(8,128)(2,1)S(1)}, u32[]{:S(2)}, u32[]{:S(2)}) collective-permute-start(bf16[96,1024]{1,0:T(8,128)(2,1)S(1)} %fold.4), channel_id=1, source_target_pairs={{0,2},{1,3},{2,0},{3,1},{4,6},{5,7},{6,4},{7,5},{8,10},{9,11},{10,... | collective-permute-start | bytes 589832 | tf_op jit(solution)/shard_map/ppermute | solution.py:265
  39.7 8.3 %collective-permute-start.16 = (bf16[192,1024]{1,0:T(8,128)(2,1)S(1)}, bf16[192,1024]{1,0:T(8,128)(2,1)S(1)}, u32[]{:S(2)}, u32[]{:S(2)}) collective-permute-start(bf16[192,1024]{1,0:T(8,128)(2,1)S(1)} %pair.11.refs_0_), channel_id=1, source_target_pairs={{0,1},{1,0},{2,3},{3,2},{4,5},{5,4},{6,7},{7,6},{8,9},{9,8},{10,11... | collective-permute-start | bytes 1179656 | tf_op jit(solution)/shard_map/ppermute | solution.py:265
  42.4 5.6 %collective-permute-start.15 = (bf16[192,1024]{1,0:T(8,128)(2,1)S(1)}, bf16[192,1024]{1,0:T(8,128)(2,1)S(1)}, u32[]{:S(2)}, u32[]{:S(2)}) collective-permute-start(bf16[192,1024]{1,0:T(8,128)(2,1)S(1)} %get-tuple-element.344), channel_id=1, source_target_pairs={{0,1},{1,0},{2,3},{3,2},{4,5},{5,4},{6,7},{7,6},{8,9},{9,8},{10,11... | collective-permute-start | bytes 1179656 | tf_op jit(solution)/shard_map/ppermute | solution.py:265
  48.1 9.6 %collective-permute-start.20 = (bf16[96,1024]{1,0:T(8,128)(2,1)S(1)}, bf16[96,1024]{1,0:T(8,128)(2,1)S(1)}, u32[]{:S(2)}, u32[]{:S(2)}) collective-permute-start(bf16[96,1024]{1,0:T(8,128)(2,1)S(1)} %fold.5), channel_id=1, source_target_pairs={{0,2},{1,3},{2,0},{3,1},{4,6},{5,7},{6,4},{7,5},{8,10},{9,11},{10,... | collective-permute-start | bytes 589832 | tf_op jit(solution)/shard_map/ppermute | solution.py:265
  48.7 3.3 %collective-permute-start.19 = (bf16[192,1024]{1,0:T(8,128)(2,1)S(1)}, bf16[192,1024]{1,0:T(8,128)(2,1)S(1)}, u32[]{:S(2)}, u32[]{:S(2)}) collective-permute-start(bf16[192,1024]{1,0:T(8,128)(2,1)S(1)} %pair.12.refs_0_), channel_id=1, source_target_pairs={{0,1},{1,0},{2,3},{3,2},{4,5},{5,4},{6,7},{7,6},{8,9},{9,8},{10,11... | collective-permute-start | bytes 1179656 | tf_op jit(solution)/shard_map/ppermute | solution.py:265
  51.4 1.9 %collective-permute-start.18 = (bf16[192,1024]{1,0:T(8,128)(2,1)S(1)}, bf16[192,1024]{1,0:T(8,128)(2,1)S(1)}, u32[]{:S(2)}, u32[]{:S(2)}) collective-permute-start(bf16[192,1024]{1,0:T(8,128)(2,1)S(1)} %get-tuple-element.369), channel_id=1, source_target_pairs={{0,1},{1,0},{2,3},{3,2},{4,5},{5,4},{6,7},{7,6},{8,9},{9,8},{10,11... | collective-permute-start | bytes 1179656 | tf_op jit(solution)/shard_map/ppermute | solution.py:265
  53.3 7.9 %collective-permute-start.22 = (bf16[96,1024]{1,0:T(8,128)(2,1)S(1)}, bf16[96,1024]{1,0:T(8,128)(2,1)S(1)}, u32[]{:S(2)}, u32[]{:S(2)}) collective-permute-start(bf16[96,1024]{1,0:T(8,128)(2,1)S(1)} %fold.6), channel_id=1, source_target_pairs={{0,2},{1,3},{2,0},{3,1},{4,6},{5,7},{6,4},{7,5},{8,10},{9,11},{10,... | collective-permute-start | bytes 589832 | tf_op jit(solution)/shard_map/ppermute | solution.py:265
  57.6 1.8 %collective-permute-start.21 = (bf16[192,1024]{1,0:T(8,128)(2,1)S(1)}, bf16[192,1024]{1,0:T(8,128)(2,1)S(1)}, u32[]{:S(2)}, u32[]{:S(2)}) collective-permute-start(bf16[192,1024]{1,0:T(8,128)(2,1)S(1)} %get-tuple-element.396), channel_id=1, source_target_pairs={{0,1},{1,0},{2,3},{3,2},{4,5},{5,4},{6,7},{7,6},{8,9},{9,8},{10,11... | collective-permute-start | bytes 1179656 | tf_op jit(solution)/shard_map/ppermute | solution.py:265
  59.4 7.8 %collective-permute-start.23 = (bf16[96,1024]{1,0:T(8,128)(2,1)S(1)}, bf16[96,1024]{1,0:T(8,128)(2,1)S(1)}, u32[]{:S(2)}, u32[]{:S(2)}) collective-permute-start(bf16[96,1024]{1,0:T(8,128)(2,1)S(1)} %fold.7), channel_id=1, source_target_pairs={{0,2},{1,3},{2,0},{3,1},{4,6},{5,7},{6,4},{7,5},{8,10},{9,11},{10,... | collective-permute-start | bytes 589832 | tf_op jit(solution)/shard_map/ppermute | solution.py:265
  60.0 8.4 %collective-permute-start.24 = (bf16[96,1024]{1,0:T(8,128)(2,1)S(1)}, bf16[96,1024]{1,0:T(8,128)(2,1)S(1)}, u32[]{:S(2)}, u32[]{:S(2)}) collective-permute-start(bf16[96,1024]{1,0:T(8,128)(2,1)S(1)} %total.5), channel_id=1, source_target_pairs={{0,12},{1,13},{2,14},{3,15},{4,0},{5,1},{6,2},{7,3},{8,4},{9,5},{1... | collective-permute-start | bytes 589832 | tf_op jit(solution)/shard_map/ppermute | solution.py:269
  61.4 15.9 %collective-permute-start.26 = (bf16[96,1024]{1,0:T(8,128)(2,1)S(1)}, bf16[96,1024]{1,0:T(8,128)(2,1)S(1)}, u32[]{:S(2)}, u32[]{:S(2)}) collective-permute-start(bf16[96,1024]{1,0:T(8,128)(2,1)S(1)} %total.6), channel_id=1, source_target_pairs={{0,8},{1,9},{2,10},{3,11},{4,12},{5,13},{6,14},{7,15},{8,0},{9,1},... | collective-permute-start | bytes 589832 | tf_op jit(solution)/shard_map/ppermute | solution.py:269
  61.4 15.8 %collective-permute-start.25 = (bf16[96,1024]{1,0:T(8,128)(2,1)S(1)}, bf16[96,1024]{1,0:T(8,128)(2,1)S(1)}, u32[]{:S(2)}, u32[]{:S(2)}) collective-permute-start(bf16[96,1024]{1,0:T(8,128)(2,1)S(1)} %get-tuple-element.459.first_ref), channel_id=1, source_target_pairs={{0,2},{1,3},{2,0},{3,1},{4,6},{5,7},{6,4},{7,5},{8,10},{9,11},{10,... | collective-permute-start | bytes 589832 | tf_op jit(solution)/shard_map/ppermute | solution.py:265
  68.6 10.3 %collective-permute-start.28 = (bf16[96,1024]{1,0:T(8,128)(2,1)S(1)}, bf16[96,1024]{1,0:T(8,128)(2,1)S(1)}, u32[]{:S(2)}, u32[]{:S(2)}) collective-permute-start(bf16[96,1024]{1,0:T(8,128)(2,1)S(1)} %total.7), channel_id=1, source_target_pairs={{0,4},{1,5},{2,6},{3,7},{4,8},{5,9},{6,10},{7,11},{8,12},{9,13},{1... | collective-permute-start | bytes 589832 | tf_op jit(solution)/shard_map/ppermute | solution.py:269
  68.8 10.1 %collective-permute-start.27 = (bf16[96,1024]{1,0:T(8,128)(2,1)S(1)}, bf16[96,1024]{1,0:T(8,128)(2,1)S(1)}, u32[]{:S(2)}, u32[]{:S(2)}) collective-permute-start(bf16[96,1024]{1,0:T(8,128)(2,1)S(1)} %get-tuple-element.477.first_ref), channel_id=1, source_target_pairs={{0,2},{1,3},{2,0},{3,1},{4,6},{5,7},{6,4},{7,5},{8,10},{9,11},{10,... | collective-permute-start | bytes 589832 | tf_op jit(solution)/shard_map/ppermute | solution.py:265
  77.2 5.7 %collective-permute-start.30 = (bf16[96,1024]{1,0:T(8,128)(2,1)S(1)}, bf16[96,1024]{1,0:T(8,128)(2,1)S(1)}, u32[]{:S(2)}, u32[]{:S(2)}) collective-permute-start(bf16[96,1024]{1,0:T(8,128)(2,1)S(1)} %get-tuple-element.494.first_ref), channel_id=1, source_target_pairs={{0,2},{1,3},{2,0},{3,1},{4,6},{5,7},{6,4},{7,5},{8,10},{9,11},{10,... | collective-permute-start | bytes 589832 | tf_op jit(solution)/shard_map/ppermute | solution.py:265
  80.6 2.3 %collective-permute-start.31 = (bf16[192,1024]{1,0:T(8,128)(2,1)S(1)}, bf16[192,1024]{1,0:T(8,128)(2,1)S(1)}, u32[]{:S(2)}, u32[]{:S(2)}) collective-permute-start(bf16[192,1024]{1,0:T(8,128)(2,1)S(1)} %pair.14.refs_5_), channel_id=1, source_target_pairs={{0,1},{1,0},{2,3},{3,2},{4,5},{5,4},{6,7},{7,6},{8,9},{9,8},{10,11... | collective-permute-start | bytes 1179656 | tf_op jit(solution)/shard_map/ppermute | solution.py:265
  82.9 4.4 %collective-permute-start.32 = (bf16[192,1024]{1,0:T(8,128)(2,1)S(1)}, bf16[192,1024]{1,0:T(8,128)(2,1)S(1)}, u32[]{:S(2)}, u32[]{:S(2)}) collective-permute-start(bf16[192,1024]{1,0:T(8,128)(2,1)S(1)} %pair.15.refs_1_), channel_id=1, source_target_pairs={{0,1},{1,0},{2,3},{3,2},{4,5},{5,4},{6,7},{7,6},{8,9},{9,8},{10,11... | collective-permute-start | bytes 1179656 | tf_op jit(solution)/shard_map/ppermute | solution.py:265
  (4 other events, 9.0 us)

commit v10 on v9

--- a/solution.py
+++ b/solution.py
@@ -10,20 +10,20 @@
 HSPLIT = 4
 GROUPS = 4
 PLAN = (
-    ("yN0 zN1 zN2 loadW0", ""),
-    ("yC0 zN3", "yN0 zN1 zN2"),
-    ("cN0 yN1 zC1", "yC0 zN3 cN0"),
-    ("ffnN0 cR0 cC0 yN3 zC2", "yN1 zC1 cR0 cC0"),
-    ("cN1 yN2 zC3", "yN3 zC2 cN1"),
-    ("ffnN1 cR1 cN3 yR0", "yN2 zC3 cR1 cN3"),
-    ("ffnN3 cR3 cN2 yR1", "yR0 cR3 cN2"),
-    ("ffnN2 cR2 totalR0 yR3", "yR1 cR2"),
-    ("totalR1 zR1 yR2", "yR3"),
-    ("totalR3 zR3 yC1", "yR2 zR1"),
-    ("totalR2 zR2 yC2", "yC1 zR3"),
-    ("cC1 yC3", "yC2 zR2 cC1"),
-    ("cC2", "yC3 cC2"),
-    ("cC3 gradC0", None),
+    ("zN1 zN2 yN0 loadW0", ""),
+    ("yC0", "yN0 zN1 zN2"),
+    ("cN0 yN1 zN3", "yC0 cN0"),
+    ("ffnN0 cR0 yN2", "yN1 zN3 cR0"),
+    ("cN1 yN3 zC1 zC2", "yN2 cN1"),
+    ("ffnN1 cR1N2 yR0", "yN3 zC1 zC2 cR1N2"),
+    ("ffnN2 cR2N3 yR1 zC3", "yR0 cR2N3"),
+    ("ffnN3 cR3 totalR0 yR2", "yR1 zC3 cR3"),
+    ("totalR1 zR1 yR3 cC0", "yR2 cC0"),
+    ("totalR2 zR2 yC1", "yR3 zR1"),
+    ("totalR3 zR3 yC2", "yC1 zR2"),
+    ("cC1 yC3", "yC2 cC1"),
+    ("cC2 gradC0", "yC3 zR3 cC2"),
+    ("cC3", None),
 )
 TILE = 256
 LINK_WORK = 10 << 30
@@ -129,6 +129,12 @@
     out_ref[rows:, :] = second_ref[...]
 
 
+def split_kernel(both_ref, first_ref, second_ref):
+    rows = first_ref.shape[0]
+    first_ref[...] = both_ref[:rows, :]
+    second_ref[...] = both_ref[rows:, :]
+
+
 def fold_kernel(keep_ref, crossed_ref, out_ref):
     rows = out_ref.shape[0]
     total = keep_ref[rows:, :].astype(F32) + crossed_ref[rows:, :].astype(F32)
@@ -302,8 +308,15 @@
             landed += list(zip(quick, through(cores, "land_core")))
         live.update(landed)
         sync()
+        for name in quick:
+            values = [live.pop(name)]
+            if len(name) > 2:
+                values = small(split_kernel, "split", [2 * height] * 2, *values)
+            live.update({("c",) + item: value for item, value in zip(name[1:], values)})
 
     def flights_of(name):
+        if name[0] == "c":
+            return [name]
         axis, kind, g = name
         return [(kind, s) for s in groups[g] if s] if axis == "z" else [name]
 
@@ -321,14 +334,19 @@
             live["sent", kind, g] = value
         flying["y", kind, g] = swap(value, 2)
 
-    def c(kind, g):
-        if kind == "R":
-            value = live.pop(("send", (g,)))
-        else:
+    def c(*items):
+        values = []
+        for kind, g in items:
+            if kind == "R":
+                values.append(live.pop(("send", (g,))))
+                continue
             here, came = live.pop(("sent", kind, g)), live.pop(("y", kind, g))
             (value,) = small(pair_kernel, "pair", [2 * height], here, came)
             live[kind, "own", (g,)] = value
-        flying["c", kind, g] = swap(value, 1)
+            values.append(value)
+        if len(values) > 1:
+            values = small(pair_kernel, "pair", [4 * height], *values)
+        flying[("c",) + items] = swap(values[0], 1)
 
     def total(g):
         values = live.pop(("keep", (g,))), live.pop(("c", "R", g)), live.pop(("y", "R", g))
@@ -439,10 +457,15 @@
         "total": lambda kind, g: total(g),
         "load": lambda kind, g: load(),
         "grad": lambda kind, g: first_grad(
-            [(0,), (1,), (2,)],
-            [("C", "own", (i,)) for i in range(3)] + [("c", "C", i) for i in range(3)],
+            [(0,), (1,)],
+            [("C", "own", (0,)), ("C", "own", (1,)), ("c", "C", 0), ("c", "C", 1)],
         ),
     }
+    def name_of(act):
+        marks = act.lstrip("abcdefghijklmnopqrstuvwxyz")
+        items = [(marks[i], int(marks[i + 1])) for i in range(0, len(marks), 2)]
+        return (act[: len(act) - len(marks)],) + tuple(items)
+
     send()
     if shifts > 1:
         z("N", 0)
@@ -451,12 +474,16 @@
     sync()
     for starts, lands in PLAN:
         for act in starts.split():
-            steps[act[:-2]](act[-2], int(act[-1]))
+            name = name_of(act)
+            steps[name[0]](*(name[1:] if name[0] == "c" else name[1]))
         if lands is None:
             break
-        land(*[(act[:-2], act[-2], int(act[-1])) for act in lands.split()])
-    live["c", "C", 3] = flying.pop(("c", "C", 3))
-    grad_down = last_grad([(3,)], [("C", "own", (3,)), ("c", "C", 3)])
+        land(*[n if n[0] == "c" else (n[0],) + n[1] for n in map(name_of, lands.split())])
+    live["c", "C", 3] = flying.pop(("c", ("C", 3)))
+    grad_down = last_grad(
+        [(2,), (3,)],
+        [("C", "own", (2,)), ("C", "own", (3,)), ("c", "C", 2), ("c", "C", 3)],
+    )
     mixed = call(
         functools.partial(combine_kernel, experts),
         16,

time: 89.8 us -> 83.6 us (0.931)
  waiting for transfers between devices: 38.8 us -> 31.7 us
  starting transfers between devices: 27.3 us -> 28.4 us
    ppermute x9, waiting for transfers between devices: 25 us -> 16.3 us  [turn(): return lax.ppermute(value, 'expert', to)]
    ppermute x9, starting transfers between devices: 9.73 us -> 15.9 us  [turn(): return lax.ppermute(value, 'expert', to)]
    ppermute x24 -> x22, starting transfers between devices: 17.6 us -> 12.5 us  [swap(): lax.ppermute(value, 'expert', [(i, i ^ mask) for i in range(devices)])]
    ppermute x24 -> x22, waiting for transfers between devices: 13.8 us -> 15.4 us  [swap(): lax.ppermute(value, 'expert', [(i, i ^ mask) for i in range(devices)])]
    pallas_call x1, Pallas kernels: 2.92 us -> 1.87 us  [first_grad(): call(functools.partial(first_grad_kernel, plan), 24, 'first_grad', out_sh...]
  transfers between devices with their start and end apart: 33 -> 31, of which waited for: 12 -> 17; matrix products, arithmetic and copies ran while one was open for 0% -> 0% of each run, Pallas kernels for 20% -> 21%
where the time goes in v10:
time: 83.6 us; the launch traced here: 83.5 us
  waiting for transfers between devices  31.7 us (38%)
  starting transfers between devices  28.4 us (34%)
  Pallas kernels  22.2 us (27%)
  between operations  1.2 us (1%)
    ppermute x9, waiting for transfers between devices, turn(): return lax.ppermute(value, 'expert', to)  16.3 us
    ppermute x9, starting transfers between devices, turn(): return lax.ppermute(value, 'expert', to)  15.9 us
    ppermute x22, waiting for transfers between devices, swap(): lax.ppermute(value, 'expert', [(i, i ^ mask) for i in range(devices)])  15.4 us
    ppermute x22, starting transfers between devices, swap(): lax.ppermute(value, 'expert', [(i, i ^ mask) for i in range(devices)])  12.5 us
    pallas_call x4, Pallas kernels, ffn(): call(functools.partial(ffn_kernel, len(pieces)), 24, 'ffn', out_shape=[ja...  10.5 us
    pallas_call x1, Pallas kernels, load(): call(load_kernel, 16, 'load', out_shape=[weight, weight, jax.ShapeDtypeSt...  2.88 us
    pallas_call x1, Pallas kernels, last_grad(): call(functools.partial(last_grad_kernel, plan), 24, 'last_grad', out_shap...  2.71 us
    pallas_call x1, Pallas kernels, send(): call(functools.partial(send_kernel, experts), 16, 'send', out_shape=[piec...  1.92 us
  transfers between devices with their start and end apart: 31, of which 17 were waited for; matrix products, arithmetic and copies ran while one was open for 0% of the time, Pallas kernels for 21%

profile of v10, /device:TPU:0, one launch (start us, length us, event | category | flops | bytes accessed | tf_op | source)
XLA Modules:
  0.0 83.5 jit_solution(5230973656496687166)
XLA Ops:
  0.6 1.9 %send.1 = (bf16[96,1024]{1,0:T(8,128)(2,1)S(1)}, bf16[96,1024]{1,0:T(8,128)(2,1)S(1)}, bf16[96,1024]{1,0:T(8,128)(2,1)S(1)}, bf16[96,1024]{1,0:T(8,128)(2,1)S(1)...) custom-call(s32[1]{0:T(128)} %bitcast.plane_ref, ...), custom_call_target="tpu_custom_call" | custom-call | tf_op jit(solution)/shard_map/send/pallas_call | solution.py:378
  2.6 3.0 %collective-permute-start = (bf16[96,1024]{1,0:T(8,128)(2,1)S(1)}, bf16[96,1024]{1,0:T(8,128)(2,1)S(1)}, u32[]{:S(2)}, u32[]{:S(2)}) collective-permute-start(bf16[96,1024]{1,0:T(8,128)(2,1)S(1)} %get-tuple-element.271.first_ref), channel_id=1, source_target_pairs={{0,2},{1,3},{2,0},{3,1},{4,6},{5,7},{6,4},{7,5},{8,10},{9,11},{10,... | collective-permute-start | bytes 589832 | tf_op jit(solution)/shard_map/ppermute | solution.py:271
  5.6 1.6 %collective-permute-start.1 = (bf16[96,1024]{1,0:T(8,128)(2,1)S(1)}, bf16[96,1024]{1,0:T(8,128)(2,1)S(1)}, u32[]{:S(2)}, u32[]{:S(2)}) collective-permute-start(bf16[96,1024]{1,0:T(8,128)(2,1)S(1)} %get-tuple-element.237), channel_id=1, source_target_pairs={{0,4},{1,5},{2,6},{3,7},{4,8},{5,9},{6,10},{7,11},{8,12},{9,13},{1... | collective-permute-start | bytes 589832 | tf_op jit(solution)/shard_map/ppermute | solution.py:275
  7.2 2.2 %collective-permute-start.2 = (bf16[96,1024]{1,0:T(8,128)(2,1)S(1)}, bf16[96,1024]{1,0:T(8,128)(2,1)S(1)}, u32[]{:S(2)}, u32[]{:S(2)}) collective-permute-start(bf16[96,1024]{1,0:T(8,128)(2,1)S(1)} %get-tuple-element.238), channel_id=1, source_target_pairs={{0,12},{1,13},{2,14},{3,15},{4,0},{5,1},{6,2},{7,3},{8,4},{9,5},{1... | collective-permute-start | bytes 589832 | tf_op jit(solution)/shard_map/ppermute | solution.py:275
  9.4 2.9 %load.1 = (bf16[1024,1024]{1,0:T(8,128)(2,1)S(1)}, bf16[1024,1024]{1,0:T(8,128)(2,1)S(1)}, bf16[1024,1024]{1,0:T(8,128)(2,1)S(1)}) custom-call(bf16[1,1024,1024]{2,1,0:T(8,128)(2,1)} %refs_0_.2, bf16[1,1024,1024]{2,1,0:T(8,128)(2,1)} %refs_1_.3, bf16[1,1024,1024]{2,1,0:T(8,128)(2,1)} %refs_2_.1), custom_call_target="tpu_custom_call" | custom-call | tf_op jit(solution)/shard_map/load/pallas_call | solution.py:393
  12.7 2.6 %collective-permute-done.1.refs_1_ = bf16[96,1024]{1,0:T(8,128)(2,1)S(1)} collective-permute-done((bf16[96,1024]{1,0:T(8,128)(2,1)S(1)}, bf16[96,1024]{1,0:T(8,128)(2,1)S(1)}, u32[]{:S(2)}, u32[]{:S(2)}) %collective-permute-start.1) | collective-permute-done | bytes 196640 | tf_op jit(solution)/shard_map/ppermute | solution.py:275
  15.3 2.2 %collective-permute-done.2.refs_2_ = bf16[96,1024]{1,0:T(8,128)(2,1)S(1)} collective-permute-done((bf16[96,1024]{1,0:T(8,128)(2,1)S(1)}, bf16[96,1024]{1,0:T(8,128)(2,1)S(1)}, u32[]{:S(2)}, u32[]{:S(2)}) %collective-permute-start.2) | collective-permute-done | bytes 196640 | tf_op jit(solution)/shard_map/ppermute | solution.py:275
  18.0 1.3 %collective-permute-start.4 = (bf16[96,1024]{1,0:T(8,128)(2,1)S(1)}, bf16[96,1024]{1,0:T(8,128)(2,1)S(1)}, u32[]{:S(2)}, u32[]{:S(2)}) collective-permute-start(bf16[96,1024]{1,0:T(8,128)(2,1)S(1)} %get-tuple-element.261), channel_id=1, source_target_pairs={{0,8},{1,9},{2,10},{3,11},{4,12},{5,13},{6,14},{7,15},{8,0},{9,1},... | collective-permute-start | bytes 589832 | tf_op jit(solution)/shard_map/ppermute | solution.py:275
  19.4 1.7 %collective-permute-done.6.refs_0_ = bf16[192,1024]{1,0:T(8,128)(2,1)S(1)} collective-permute-done((bf16[192,1024]{1,0:T(8,128)(2,1)S(1)}, bf16[192,1024]{1,0:T(8,128)(2,1)S(1)}, u32[]{:S(2)}, u32[]{:S(2)}) %collective-permute-start.6) | collective-permute-done | bytes 393248 | tf_op jit(solution)/shard_map/ppermute | solution.py:271
  21.1 1.5 %collective-permute-start.11 = (bf16[96,1024]{1,0:T(8,128)(2,1)S(1)}, bf16[96,1024]{1,0:T(8,128)(2,1)S(1)}, u32[]{:S(2)}, u32[]{:S(2)}) collective-permute-start(bf16[96,1024]{1,0:T(8,128)(2,1)S(1)} %get-tuple-element.323.first_ref), channel_id=1, source_target_pairs={{0,2},{1,3},{2,0},{3,1},{4,6},{5,7},{6,4},{7,5},{8,10},{9,11},{10,... | collective-permute-start | bytes 589832 | tf_op jit(solution)/shard_map/ppermute | solution.py:271
  22.6 2.6 %ffn.4 = (bf16[1024,384]{1,0:T(8,128)(2,1)S(1)}, bf16[192,1024]{1,0:T(8,128)(2,1)S(1)}, bf16[192,1024]{1,0:T(8,128)(2,1)S(1)}) custom-call(bf16[192,1024]{1,0:T(8,128)(2,1)S(1)} %pair.10.refs_0_, bf16[192,1024]{1,0:T(8,128)(2,1)S(1)} %land_core.9.refs_1_, bf16[1024,1024]{1,0:T(8,128)(2,1)S(1)} %get-tuple-element.354.refs_2_, ...), custom_call_target="tpu_custom_call" | custom-call | tf_op jit(solution)/shard_map/ffn/pallas_call | solution.py:360
  25.3 3.7 %collective-permute-done.4.refs_1_ = bf16[96,1024]{1,0:T(8,128)(2,1)S(1)} collective-permute-done((bf16[96,1024]{1,0:T(8,128)(2,1)S(1)}, bf16[96,1024]{1,0:T(8,128)(2,1)S(1)}, u32[]{:S(2)}, u32[]{:S(2)}) %collective-permute-start.4) | collective-permute-done | bytes 196640 | tf_op jit(solution)/shard_map/ppermute | solution.py:275
  29.0 1.5 %collective-permute-start.8 = (bf16[96,1024]{1,0:T(8,128)(2,1)S(1)}, bf16[96,1024]{1,0:T(8,128)(2,1)S(1)}, u32[]{:S(2)}, u32[]{:S(2)}) collective-permute-start(bf16[96,1024]{1,0:T(8,128)(2,1)S(1)} %get-tuple-element.347.first_ref), channel_id=1, source_target_pairs={{0,2},{1,3},{2,0},{3,1},{4,6},{5,7},{6,4},{7,5},{8,10},{9,11},{10,... | collective-permute-start | bytes 589832 | tf_op jit(solution)/shard_map/ppermute | solution.py:271
  30.5 3.8 %collective-permute-start.10 = (bf16[96,1024]{1,0:T(8,128)(2,1)S(1)}, bf16[96,1024]{1,0:T(8,128)(2,1)S(1)}, u32[]{:S(2)}, u32[]{:S(2)}) collective-permute-start(bf16[96,1024]{1,0:T(8,128)(2,1)S(1)} %get-tuple-element.293), channel_id=1, source_target_pairs={{0,12},{1,13},{2,14},{3,15},{4,0},{5,1},{6,2},{7,3},{8,4},{9,5},{1... | collective-permute-start | bytes 589832 | tf_op jit(solution)/shard_map/ppermute | solution.py:275
  34.5 1.7 %collective-permute-done.12.refs_0_ = bf16[192,1024]{1,0:T(8,128)(2,1)S(1)} collective-permute-done((bf16[192,1024]{1,0:T(8,128)(2,1)S(1)}, bf16[192,1024]{1,0:T(8,128)(2,1)S(1)}, u32[]{:S(2)}, u32[]{:S(2)}) %collective-permute-start.12) | collective-permute-done | bytes 393248 | tf_op jit(solution)/shard_map/ppermute | solution.py:271
  36.8 2.6 %ffn.5 = (bf16[1024,384]{1,0:T(8,128)(2,1)S(1)}, bf16[192,1024]{1,0:T(8,128)(2,1)S(1)}, bf16[192,1024]{1,0:T(8,128)(2,1)S(1)}) custom-call(bf16[192,1024]{1,0:T(8,128)(2,1)S(1)} %pair.11.refs_0_, bf16[192,1024]{1,0:T(8,128)(2,1)S(1)} %land_core.11.refs_1_, bf16[1024,1024]{1,0:T(8,128)(2,1)S(1)} %get-tuple-element.354.refs_2_, ...), custom_call_target="tpu_custom_call" | custom-call | tf_op jit(solution)/shard_map/ffn/pallas_call | solution.py:360
  40.0 1.8 %collective-permute-done.13.refs_0_ = bf16[384,1024]{1,0:T(8,128)(2,1)S(1)} collective-permute-done((bf16[384,1024]{1,0:T(8,128)(2,1)S(1)}, bf16[384,1024]{1,0:T(8,128)(2,1)S(1)}, u32[]{:S(2)}, u32[]{:S(2)}) %collective-permute-start.13) | collective-permute-done | bytes 786464 | tf_op jit(solution)/shard_map/ppermute | solution.py:271
  43.6 2.6 %ffn.6 = (bf16[1024,384]{1,0:T(8,128)(2,1)S(1)}, bf16[192,1024]{1,0:T(8,128)(2,1)S(1)}, bf16[192,1024]{1,0:T(8,128)(2,1)S(1)}) custom-call(bf16[192,1024]{1,0:T(8,128)(2,1)S(1)} %pair.12.second_ref.refs_0_, bf16[192,1024]{1,0:T(8,128)(2,1)S(1)} %get-tuple-element.344.refs_1_, bf16[1024,1024]{1,0:T(8,128)(2,1)S(1)} %get-tuple-element.354.refs_2_, ...), custom_call_target="tpu_custom_call" | custom-call | tf_op jit(solution)/shard_map/ffn/pallas_call | solution.py:360
  46.4 2.3 %collective-permute-done.15.refs_0_ = bf16[384,1024]{1,0:T(8,128)(2,1)S(1)} collective-permute-done((bf16[384,1024]{1,0:T(8,128)(2,1)S(1)}, bf16[384,1024]{1,0:T(8,128)(2,1)S(1)}, u32[]{:S(2)}, u32[]{:S(2)}) %collective-permute-start.15) | collective-permute-done | bytes 786464 | tf_op jit(solution)/shard_map/ppermute | solution.py:271
  48.8 1.1 %collective-permute-start.19 = (bf16[96,1024]{1,0:T(8,128)(2,1)S(1)}, bf16[96,1024]{1,0:T(8,128)(2,1)S(1)}, u32[]{:S(2)}, u32[]{:S(2)}) collective-permute-start(bf16[96,1024]{1,0:T(8,128)(2,1)S(1)} %fold.6), channel_id=1, source_target_pairs={{0,2},{1,3},{2,0},{3,1},{4,6},{5,7},{6,4},{7,5},{8,10},{9,11},{10,... | collective-permute-start | bytes 589832 | tf_op jit(solution)/shard_map/ppermute | solution.py:271
  49.9 2.6 %ffn.7 = (bf16[1024,384]{1,0:T(8,128)(2,1)S(1)}, bf16[192,1024]{1,0:T(8,128)(2,1)S(1)}, bf16[192,1024]{1,0:T(8,128)(2,1)S(1)}) custom-call(bf16[192,1024]{1,0:T(8,128)(2,1)S(1)} %pair.14.second_ref.refs_0_, bf16[192,1024]{1,0:T(8,128)(2,1)S(1)} %get-tuple-element.368.refs_1_, bf16[1024,1024]{1,0:T(8,128)(2,1)S(1)} %get-tuple-element.354.refs_2_, ...), custom_call_target="tpu_custom_call" | custom-call | tf_op jit(solution)/shard_map/ffn/pallas_call | solution.py:360
  52.7 1.6 %collective-permute-done.18.refs_0_ = bf16[192,1024]{1,0:T(8,128)(2,1)S(1)} collective-permute-done((bf16[192,1024]{1,0:T(8,128)(2,1)S(1)}, bf16[192,1024]{1,0:T(8,128)(2,1)S(1)}, u32[]{:S(2)}, u32[]{:S(2)}) %collective-permute-start.18) | collective-permute-done | bytes 393248 | tf_op jit(solution)/shard_map/ppermute | solution.py:271
  56.5 1.7 %collective-permute-done.20.refs_0_ = bf16[192,1024]{1,0:T(8,128)(2,1)S(1)} collective-permute-done((bf16[192,1024]{1,0:T(8,128)(2,1)S(1)}, bf16[192,1024]{1,0:T(8,128)(2,1)S(1)}, u32[]{:S(2)}, u32[]{:S(2)}) %collective-permute-start.20) | collective-permute-done | bytes 393248 | tf_op jit(solution)/shard_map/ppermute | solution.py:271
  58.3 1.3 %collective-permute-start.24 = (bf16[96,1024]{1,0:T(8,128)(2,1)S(1)}, bf16[96,1024]{1,0:T(8,128)(2,1)S(1)}, u32[]{:S(2)}, u32[]{:S(2)}) collective-permute-start(bf16[96,1024]{1,0:T(8,128)(2,1)S(1)} %total.6), channel_id=1, source_target_pairs={{0,4},{1,5},{2,6},{3,7},{4,8},{5,9},{6,10},{7,11},{8,12},{9,13},{1... | collective-permute-start | bytes 589832 | tf_op jit(solution)/shard_map/ppermute | solution.py:275
  59.7 1.1 %collective-permute-start.23 = (bf16[96,1024]{1,0:T(8,128)(2,1)S(1)}, bf16[96,1024]{1,0:T(8,128)(2,1)S(1)}, u32[]{:S(2)}, u32[]{:S(2)}) collective-permute-start(bf16[96,1024]{1,0:T(8,128)(2,1)S(1)} %get-tuple-element.438.first_ref), channel_id=1, source_target_pairs={{0,2},{1,3},{2,0},{3,1},{4,6},{5,7},{6,4},{7,5},{8,10},{9,11},{10,... | collective-permute-start | bytes 589832 | tf_op jit(solution)/shard_map/ppermute | solution.py:271
  62.2 4.1 %collective-permute-start.28 = (bf16[96,1024]{1,0:T(8,128)(2,1)S(1)}, bf16[96,1024]{1,0:T(8,128)(2,1)S(1)}, u32[]{:S(2)}, u32[]{:S(2)}) collective-permute-start(bf16[96,1024]{1,0:T(8,128)(2,1)S(1)} %total.7), channel_id=1, source_target_pairs={{0,8},{1,9},{2,10},{3,11},{4,12},{5,13},{6,14},{7,15},{8,0},{9,1},... | collective-permute-start | bytes 589832 | tf_op jit(solution)/shard_map/ppermute | solution.py:275
  66.4 3.6 %collective-permute-done.24.refs_1_ = bf16[96,1024]{1,0:T(8,128)(2,1)S(1)} collective-permute-done((bf16[96,1024]{1,0:T(8,128)(2,1)S(1)}, bf16[96,1024]{1,0:T(8,128)(2,1)S(1)}, u32[]{:S(2)}, u32[]{:S(2)}) %collective-permute-start.24) | collective-permute-done | bytes 196640 | tf_op jit(solution)/shard_map/ppermute | solution.py:275
  70.1 3.7 %collective-permute-done.25.refs_0_ = bf16[96,1024]{1,0:T(8,128)(2,1)S(1)} collective-permute-done((bf16[96,1024]{1,0:T(8,128)(2,1)S(1)}, bf16[96,1024]{1,0:T(8,128)(2,1)S(1)}, u32[]{:S(2)}, u32[]{:S(2)}) %collective-permute-start.25) | collective-permute-done | bytes 196640 | tf_op jit(solution)/shard_map/ppermute | solution.py:271
  73.9 3.0 %collective-permute-done.28.refs_1_ = bf16[96,1024]{1,0:T(8,128)(2,1)S(1)} collective-permute-done((bf16[96,1024]{1,0:T(8,128)(2,1)S(1)}, bf16[96,1024]{1,0:T(8,128)(2,1)S(1)}, u32[]{:S(2)}, u32[]{:S(2)}) %collective-permute-start.28) | collective-permute-done | bytes 196640 | tf_op jit(solution)/shard_map/ppermute | solution.py:275
  76.9 1.9 %first_grad.1.first_ref = f32[1024,1024]{1,0:T(8,128)S(1)} custom-call(bf16[1024,384]{1,0:T(8,128)(2,1)S(1)} %get-tuple-element.442.refs_0_, bf16[1024,384]{1,0:T(8,128)(2,1)S(1)} %get-tuple-element.443.refs_1_, bf16[192,1024]{1,0:T(8,128)(2,1)S(1)} %pair.16.refs_2_, bf16[192,1024]{1,0:T(8,128)(2,1)S(1)} %pair.17.refs_3_, ...), custom_call_target="tpu_custom_call" | custom-call | tf_op jit(solution)/shard_map/first_grad/pallas_call | solution.py:428
  78.9 1.4 %combine.1 = bf16[128,1024]{1,0:T(8,128)(2,1)} custom-call(s32[1]{0:T(128)} %bitcast.plane_ref, bf16[128,1024]{1,0:T(8,128)(2,1)S(1)} %copy-done, s32[2,128]{1,0:T(2,128)S(1)} %bitcast.5, s32[2,128]{1,0:T(2,128)S(1)} %bitcast.7, bf16[96,1024]{1,0:T(8,128)(2,1)S(1)} %total.4.refs_0_, bf16[96,1024]{1,0:T(8,128)(2,1)S(1)} %get-tuple-element.460.refs_1_, ...), custom_call_target="tpu_custom_call" | custom-call | tf_op jit(solution)/shard_map/combine/pallas_call | solution.py:487
  80.6 2.7 %last_grad.1 = bf16[1,1024,1024]{2,1,0:T(8,128)(2,1)} custom-call(f32[1024,1024]{1,0:T(8,128)S(1)} %first_grad.1.first_ref, bf16[1024,384]{1,0:T(8,128)(2,1)S(1)} %get-tuple-element.464.refs_0_, bf16[1024,384]{1,0:T(8,128)(2,1)S(1)} %get-tuple-element.465.refs_1_, bf16[192,1024]{1,0:T(8,128)(2,1)S(1)} %pair.18.refs_2_, bf16[192,1024]{1,0:T(8,128)(2,1)S(1)} %pair.19.refs_3_, ...), custom_call_target="tpu_custom_call" | custom-call | tf_op jit(solution)/shard_map/last_grad/pallas_call | solution.py:440
  (87 shorter events, 8.9 us)
Async XLA Ops:
  2.6 10.1 %collective-permute-start = (bf16[96,1024]{1,0:T(8,128)(2,1)S(1)}, bf16[96,1024]{1,0:T(8,128)(2,1)S(1)}, u32[]{:S(2)}, u32[]{:S(2)}) collective-permute-start(bf16[96,1024]{1,0:T(8,128)(2,1)S(1)} %get-tuple-element.271.first_ref), channel_id=1, source_target_pairs={{0,2},{1,3},{2,0},{3,1},{4,6},{5,7},{6,4},{7,5},{8,10},{9,11},{10,... | collective-permute-start | bytes 589832 | tf_op jit(solution)/shard_map/ppermute | solution.py:271
  5.6 9.7 %collective-permute-start.1 = (bf16[96,1024]{1,0:T(8,128)(2,1)S(1)}, bf16[96,1024]{1,0:T(8,128)(2,1)S(1)}, u32[]{:S(2)}, u32[]{:S(2)}) collective-permute-start(bf16[96,1024]{1,0:T(8,128)(2,1)S(1)} %get-tuple-element.237), channel_id=1, source_target_pairs={{0,4},{1,5},{2,6},{3,7},{4,8},{5,9},{6,10},{7,11},{8,12},{9,13},{1... | collective-permute-start | bytes 589832 | tf_op jit(solution)/shard_map/ppermute | solution.py:275
  7.2 10.3 %collective-permute-start.2 = (bf16[96,1024]{1,0:T(8,128)(2,1)S(1)}, bf16[96,1024]{1,0:T(8,128)(2,1)S(1)}, u32[]{:S(2)}, u32[]{:S(2)}) collective-permute-start(bf16[96,1024]{1,0:T(8,128)(2,1)S(1)} %get-tuple-element.238), channel_id=1, source_target_pairs={{0,12},{1,13},{2,14},{3,15},{4,0},{5,1},{6,2},{7,3},{8,4},{9,5},{1... | collective-permute-start | bytes 589832 | tf_op jit(solution)/shard_map/ppermute | solution.py:275
  12.3 7.1 %collective-permute-start.5 = (bf16[96,1024]{1,0:T(8,128)(2,1)S(1)}, bf16[96,1024]{1,0:T(8,128)(2,1)S(1)}, u32[]{:S(2)}, u32[]{:S(2)}) collective-permute-start(bf16[96,1024]{1,0:T(8,128)(2,1)S(1)} %get-tuple-element.392.first_ref), channel_id=1, source_target_pairs={{0,2},{1,3},{2,0},{3,1},{4,6},{5,7},{6,4},{7,5},{8,10},{9,11},{10,... | collective-permute-start | bytes 589832 | tf_op jit(solution)/shard_map/ppermute | solution.py:271
  17.5 7.8 %collective-permute-start.3 = (bf16[96,1024]{1,0:T(8,128)(2,1)S(1)}, bf16[96,1024]{1,0:T(8,128)(2,1)S(1)}, u32[]{:S(2)}, u32[]{:S(2)}) collective-permute-start(bf16[96,1024]{1,0:T(8,128)(2,1)S(1)} %get-tuple-element.305.first_ref), channel_id=1, source_target_pairs={{0,2},{1,3},{2,0},{3,1},{4,6},{5,7},{6,4},{7,5},{8,10},{9,11},{10,... | collective-permute-start | bytes 589832 | tf_op jit(solution)/shard_map/ppermute | solution.py:271
  18.0 11.0 %collective-permute-start.4 = (bf16[96,1024]{1,0:T(8,128)(2,1)S(1)}, bf16[96,1024]{1,0:T(8,128)(2,1)S(1)}, u32[]{:S(2)}, u32[]{:S(2)}) collective-permute-start(bf16[96,1024]{1,0:T(8,128)(2,1)S(1)} %get-tuple-element.261), channel_id=1, source_target_pairs={{0,8},{1,9},{2,10},{3,11},{4,12},{5,13},{6,14},{7,15},{8,0},{9,1},... | collective-permute-start | bytes 589832 | tf_op jit(solution)/shard_map/ppermute | solution.py:275
  19.3 1.8 %collective-permute-start.6 = (bf16[192,1024]{1,0:T(8,128)(2,1)S(1)}, bf16[192,1024]{1,0:T(8,128)(2,1)S(1)}, u32[]{:S(2)}, u32[]{:S(2)}) collective-permute-start(bf16[192,1024]{1,0:T(8,128)(2,1)S(1)} %pair.10.refs_0_), channel_id=1, source_target_pairs={{0,1},{1,0},{2,3},{3,2},{4,5},{5,4},{6,7},{7,6},{8,9},{9,8},{10,11... | collective-permute-start | bytes 1179656 | tf_op jit(solution)/shard_map/ppermute | solution.py:271
  21.1 13.4 %collective-permute-start.11 = (bf16[96,1024]{1,0:T(8,128)(2,1)S(1)}, bf16[96,1024]{1,0:T(8,128)(2,1)S(1)}, u32[]{:S(2)}, u32[]{:S(2)}) collective-permute-start(bf16[96,1024]{1,0:T(8,128)(2,1)S(1)} %get-tuple-element.323.first_ref), channel_id=1, source_target_pairs={{0,2},{1,3},{2,0},{3,1},{4,6},{5,7},{6,4},{7,5},{8,10},{9,11},{10,... | collective-permute-start | bytes 589832 | tf_op jit(solution)/shard_map/ppermute | solution.py:271
  25.3 3.8 %collective-permute-start.7 = (bf16[192,1024]{1,0:T(8,128)(2,1)S(1)}, bf16[192,1024]{1,0:T(8,128)(2,1)S(1)}, u32[]{:S(2)}, u32[]{:S(2)}) collective-permute-start(bf16[192,1024]{1,0:T(8,128)(2,1)S(1)} %get-tuple-element.289), channel_id=1, source_target_pairs={{0,1},{1,0},{2,3},{3,2},{4,5},{5,4},{6,7},{7,6},{8,9},{9,8},{10,11... | collective-permute-start | bytes 1179656 | tf_op jit(solution)/shard_map/ppermute | solution.py:271
  29.0 10.6 %collective-permute-start.8 = (bf16[96,1024]{1,0:T(8,128)(2,1)S(1)}, bf16[96,1024]{1,0:T(8,128)(2,1)S(1)}, u32[]{:S(2)}, u32[]{:S(2)}) collective-permute-start(bf16[96,1024]{1,0:T(8,128)(2,1)S(1)} %get-tuple-element.347.first_ref), channel_id=1, source_target_pairs={{0,2},{1,3},{2,0},{3,1},{4,6},{5,7},{6,4},{7,5},{8,10},{9,11},{10,... | collective-permute-start | bytes 589832 | tf_op jit(solution)/shard_map/ppermute | solution.py:271
  30.5 9.3 %collective-permute-start.9 = (bf16[96,1024]{1,0:T(8,128)(2,1)S(1)}, bf16[96,1024]{1,0:T(8,128)(2,1)S(1)}, u32[]{:S(2)}, u32[]{:S(2)}) collective-permute-start(bf16[96,1024]{1,0:T(8,128)(2,1)S(1)} %get-tuple-element.292), channel_id=1, source_target_pairs={{0,4},{1,5},{2,6},{3,7},{4,8},{5,9},{6,10},{7,11},{8,12},{9,13},{1... | collective-permute-start | bytes 589832 | tf_op jit(solution)/shard_map/ppermute | solution.py:275
  30.5 9.5 %collective-permute-start.10 = (bf16[96,1024]{1,0:T(8,128)(2,1)S(1)}, bf16[96,1024]{1,0:T(8,128)(2,1)S(1)}, u32[]{:S(2)}, u32[]{:S(2)}) collective-permute-start(bf16[96,1024]{1,0:T(8,128)(2,1)S(1)} %get-tuple-element.293), channel_id=1, source_target_pairs={{0,12},{1,13},{2,14},{3,15},{4,0},{5,1},{6,2},{7,3},{8,4},{9,5},{1... | collective-permute-start | bytes 589832 | tf_op jit(solution)/shard_map/ppermute | solution.py:275
  34.4 1.8 %collective-permute-start.12 = (bf16[192,1024]{1,0:T(8,128)(2,1)S(1)}, bf16[192,1024]{1,0:T(8,128)(2,1)S(1)}, u32[]{:S(2)}, u32[]{:S(2)}) collective-permute-start(bf16[192,1024]{1,0:T(8,128)(2,1)S(1)} %pair.11.refs_0_), channel_id=1, source_target_pairs={{0,1},{1,0},{2,3},{3,2},{4,5},{5,4},{6,7},{7,6},{8,9},{9,8},{10,11... | collective-permute-start | bytes 1179656 | tf_op jit(solution)/shard_map/ppermute | solution.py:271
  36.2 10.1 %collective-permute-start.14 = (bf16[96,1024]{1,0:T(8,128)(2,1)S(1)}, bf16[96,1024]{1,0:T(8,128)(2,1)S(1)}, u32[]{:S(2)}, u32[]{:S(2)}) collective-permute-start(bf16[96,1024]{1,0:T(8,128)(2,1)S(1)} %fold.4), channel_id=1, source_target_pairs={{0,2},{1,3},{2,0},{3,1},{4,6},{5,7},{6,4},{7,5},{8,10},{9,11},{10,... | collective-permute-start | bytes 589832 | tf_op jit(solution)/shard_map/ppermute | solution.py:271
  39.5 2.4 %collective-permute-start.13 = (bf16[384,1024]{1,0:T(8,128)(2,1)S(1)}, bf16[384,1024]{1,0:T(8,128)(2,1)S(1)}, u32[]{:S(2)}, u32[]{:S(2)}) collective-permute-start(bf16[384,1024]{1,0:T(8,128)(2,1)S(1)} %pair.13), channel_id=1, source_target_pairs={{0,1},{1,0},{2,3},{3,2},{4,5},{5,4},{6,7},{7,6},{8,9},{9,8},{10,11... | collective-permute-start | bytes 2359304 | tf_op jit(solution)/shard_map/ppermute | solution.py:271
  41.9 10.7 %collective-permute-start.17 = (bf16[96,1024]{1,0:T(8,128)(2,1)S(1)}, bf16[96,1024]{1,0:T(8,128)(2,1)S(1)}, u32[]{:S(2)}, u32[]{:S(2)}) collective-permute-start(bf16[96,1024]{1,0:T(8,128)(2,1)S(1)} %land.14), channel_id=1, source_target_pairs={{0,8},{1,9},{2,10},{3,11},{4,12},{5,13},{6,14},{7,15},{8,0},{9,1},... | collective-permute-start | bytes 589832 | tf_op jit(solution)/shard_map/ppermute | solution.py:275
  42.5 10.1 %collective-permute-start.16 = (bf16[96,1024]{1,0:T(8,128)(2,1)S(1)}, bf16[96,1024]{1,0:T(8,128)(2,1)S(1)}, u32[]{:S(2)}, u32[]{:S(2)}) collective-permute-start(bf16[96,1024]{1,0:T(8,128)(2,1)S(1)} %fold.5), channel_id=1, source_target_pairs={{0,2},{1,3},{2,0},{3,1},{4,6},{5,7},{6,4},{7,5},{8,10},{9,11},{10,... | collective-permute-start | bytes 589832 | tf_op jit(solution)/shard_map/ppermute | solution.py:271
  46.3 2.4 %collective-permute-start.15 = (bf16[384,1024]{1,0:T(8,128)(2,1)S(1)}, bf16[384,1024]{1,0:T(8,128)(2,1)S(1)}, u32[]{:S(2)}, u32[]{:S(2)}) collective-permute-start(bf16[384,1024]{1,0:T(8,128)(2,1)S(1)} %pair.15), channel_id=1, source_target_pairs={{0,1},{1,0},{2,3},{3,2},{4,5},{5,4},{6,7},{7,6},{8,9},{9,8},{10,11... | collective-permute-start | bytes 2359304 | tf_op jit(solution)/shard_map/ppermute | solution.py:271
  48.8 7.8 %collective-permute-start.19 = (bf16[96,1024]{1,0:T(8,128)(2,1)S(1)}, bf16[96,1024]{1,0:T(8,128)(2,1)S(1)}, u32[]{:S(2)}, u32[]{:S(2)}) collective-permute-start(bf16[96,1024]{1,0:T(8,128)(2,1)S(1)} %fold.6), channel_id=1, source_target_pairs={{0,2},{1,3},{2,0},{3,1},{4,6},{5,7},{6,4},{7,5},{8,10},{9,11},{10,... | collective-permute-start | bytes 589832 | tf_op jit(solution)/shard_map/ppermute | solution.py:271
  52.5 1.8 %collective-permute-start.18 = (bf16[192,1024]{1,0:T(8,128)(2,1)S(1)}, bf16[192,1024]{1,0:T(8,128)(2,1)S(1)}, u32[]{:S(2)}, u32[]{:S(2)}) collective-permute-start(bf16[192,1024]{1,0:T(8,128)(2,1)S(1)} %get-tuple-element.375), channel_id=1, source_target_pairs={{0,1},{1,0},{2,3},{3,2},{4,5},{5,4},{6,7},{7,6},{8,9},{9,8},{10,11... | collective-permute-start | bytes 1179656 | tf_op jit(solution)/shard_map/ppermute | solution.py:271
  54.3 7.0 %collective-permute-start.21 = (bf16[96,1024]{1,0:T(8,128)(2,1)S(1)}, bf16[96,1024]{1,0:T(8,128)(2,1)S(1)}, u32[]{:S(2)}, u32[]{:S(2)}) collective-permute-start(bf16[96,1024]{1,0:T(8,128)(2,1)S(1)} %fold.7), channel_id=1, source_target_pairs={{0,2},{1,3},{2,0},{3,1},{4,6},{5,7},{6,4},{7,5},{8,10},{9,11},{10,... | collective-permute-start | bytes 589832 | tf_op jit(solution)/shard_map/ppermute | solution.py:271
  55.4 6.7 %collective-permute-start.22 = (bf16[96,1024]{1,0:T(8,128)(2,1)S(1)}, bf16[96,1024]{1,0:T(8,128)(2,1)S(1)}, u32[]{:S(2)}, u32[]{:S(2)}) collective-permute-start(bf16[96,1024]{1,0:T(8,128)(2,1)S(1)} %total.5), channel_id=1, source_target_pairs={{0,12},{1,13},{2,14},{3,15},{4,0},{5,1},{6,2},{7,3},{8,4},{9,5},{1... | collective-permute-start | bytes 589832 | tf_op jit(solution)/shard_map/ppermute | solution.py:275
  56.4 1.8 %collective-permute-start.20 = (bf16[192,1024]{1,0:T(8,128)(2,1)S(1)}, bf16[192,1024]{1,0:T(8,128)(2,1)S(1)}, u32[]{:S(2)}, u32[]{:S(2)}) collective-permute-start(bf16[192,1024]{1,0:T(8,128)(2,1)S(1)} %pair.16.refs_2_), channel_id=1, source_target_pairs={{0,1},{1,0},{2,3},{3,2},{4,5},{5,4},{6,7},{7,6},{8,9},{9,8},{10,11... | collective-permute-start | bytes 1179656 | tf_op jit(solution)/shard_map/ppermute | solution.py:271
  58.3 11.6 %collective-permute-start.24 = (bf16[96,1024]{1,0:T(8,128)(2,1)S(1)}, bf16[96,1024]{1,0:T(8,128)(2,1)S(1)}, u32[]{:S(2)}, u32[]{:S(2)}) collective-permute-start(bf16[96,1024]{1,0:T(8,128)(2,1)S(1)} %total.6), channel_id=1, source_target_pairs={{0,4},{1,5},{2,6},{3,7},{4,8},{5,9},{6,10},{7,11},{8,12},{9,13},{1... | collective-permute-start | bytes 589832 | tf_op jit(solution)/shard_map/ppermute | solution.py:275
  59.7 10.3 %collective-permute-start.23 = (bf16[96,1024]{1,0:T(8,128)(2,1)S(1)}, bf16[96,1024]{1,0:T(8,128)(2,1)S(1)}, u32[]{:S(2)}, u32[]{:S(2)}) collective-permute-start(bf16[96,1024]{1,0:T(8,128)(2,1)S(1)} %get-tuple-element.438.first_ref), channel_id=1, source_target_pairs={{0,2},{1,3},{2,0},{3,1},{4,6},{5,7},{6,4},{7,5},{8,10},{9,11},{10,... | collective-permute-start | bytes 589832 | tf_op jit(solution)/shard_map/ppermute | solution.py:271
  62.2 14.6 %collective-permute-start.28 = (bf16[96,1024]{1,0:T(8,128)(2,1)S(1)}, bf16[96,1024]{1,0:T(8,128)(2,1)S(1)}, u32[]{:S(2)}, u32[]{:S(2)}) collective-permute-start(bf16[96,1024]{1,0:T(8,128)(2,1)S(1)} %total.7), channel_id=1, source_target_pairs={{0,8},{1,9},{2,10},{3,11},{4,12},{5,13},{6,14},{7,15},{8,0},{9,1},... | collective-permute-start | bytes 589832 | tf_op jit(solution)/shard_map/ppermute | solution.py:275
  66.4 7.4 %collective-permute-start.25 = (bf16[96,1024]{1,0:T(8,128)(2,1)S(1)}, bf16[96,1024]{1,0:T(8,128)(2,1)S(1)}, u32[]{:S(2)}, u32[]{:S(2)}) collective-permute-start(bf16[96,1024]{1,0:T(8,128)(2,1)S(1)} %get-tuple-element.455.first_ref), channel_id=1, source_target_pairs={{0,2},{1,3},{2,0},{3,1},{4,6},{5,7},{6,4},{7,5},{8,10},{9,11},{10,... | collective-permute-start | bytes 589832 | tf_op jit(solution)/shard_map/ppermute | solution.py:271
  70.0 6.9 %collective-permute-start.27 = (bf16[96,1024]{1,0:T(8,128)(2,1)S(1)}, bf16[96,1024]{1,0:T(8,128)(2,1)S(1)}, u32[]{:S(2)}, u32[]{:S(2)}) collective-permute-start(bf16[96,1024]{1,0:T(8,128)(2,1)S(1)} %get-tuple-element.467.first_ref), channel_id=1, source_target_pairs={{0,2},{1,3},{2,0},{3,1},{4,6},{5,7},{6,4},{7,5},{8,10},{9,11},{10,... | collective-permute-start | bytes 589832 | tf_op jit(solution)/shard_map/ppermute | solution.py:271
  70.0 3.8 %collective-permute-start.26 = (bf16[192,1024]{1,0:T(8,128)(2,1)S(1)}, bf16[192,1024]{1,0:T(8,128)(2,1)S(1)}, u32[]{:S(2)}, u32[]{:S(2)}) collective-permute-start(bf16[192,1024]{1,0:T(8,128)(2,1)S(1)} %pair.17.refs_3_), channel_id=1, source_target_pairs={{0,1},{1,0},{2,3},{3,2},{4,5},{5,4},{6,7},{7,6},{8,9},{9,8},{10,11... | collective-permute-start | bytes 1179656 | tf_op jit(solution)/shard_map/ppermute | solution.py:271
  73.8 5.0 %collective-permute-start.29 = (bf16[192,1024]{1,0:T(8,128)(2,1)S(1)}, bf16[192,1024]{1,0:T(8,128)(2,1)S(1)}, u32[]{:S(2)}, u32[]{:S(2)}) collective-permute-start(bf16[192,1024]{1,0:T(8,128)(2,1)S(1)} %pair.18.refs_2_), channel_id=1, source_target_pairs={{0,1},{1,0},{2,3},{3,2},{4,5},{5,4},{6,7},{7,6},{8,9},{9,8},{10,11... | collective-permute-start | bytes 1179656 | tf_op jit(solution)/shard_map/ppermute | solution.py:271
  76.9 2.0 %copy-start.2 = (s32[128,2]{0,1:T(2,128)S(1)}, s32[128,2]{0,1:T(2,128)}, u32[]{:S(2)}) copy-start(s32[128,2]{0,1:T(2,128)} %param.11) | copy-start | bytes 3076
  78.8 1.8 %collective-permute-start.30 = (bf16[192,1024]{1,0:T(8,128)(2,1)S(1)}, bf16[192,1024]{1,0:T(8,128)(2,1)S(1)}, u32[]{:S(2)}, u32[]{:S(2)}) collective-permute-start(bf16[192,1024]{1,0:T(8,128)(2,1)S(1)} %pair.19.refs_3_), channel_id=1, source_target_pairs={{0,1},{1,0},{2,3},{3,2},{4,5},{5,4},{6,7},{7,6},{8,9},{9,8},{10,11... | collective-permute-start | bytes 1179656 | tf_op jit(solution)/shard_map/ppermute | solution.py:271
  (2 other events, 4.1 us)

commit v11 on v10

--- a/solution.py
+++ b/solution.py
@@ -11,17 +11,17 @@
 GROUPS = 4
 PLAN = (
     ("zN1 zN2 yN0 loadW0", ""),
-    ("yC0", "yN0 zN1 zN2"),
-    ("cN0 yN1 zN3", "yC0 cN0"),
-    ("ffnN0 cR0 yN2", "yN1 zN3 cR0"),
-    ("cN1 yN3 zC1 zC2", "yN2 cN1"),
-    ("ffnN1 cR1N2 yR0", "yN3 zC1 zC2 cR1N2"),
-    ("ffnN2 cR2N3 yR1 zC3", "yR0 cR2N3"),
-    ("ffnN3 cR3 totalR0 yR2", "yR1 zC3 cR3"),
+    ("yC0 zN3", "yN0 zN1 zN2"),
+    ("cN0 yN1", "yC0 cN0"),
+    ("ffnN0 yN2", "yN1 zN3"),
+    ("cR0N1 yN3 zC1 zC2", "yN2 cR0N1"),
+    ("ffnN1 cN2 yR0", "yN3 zC1 zC2 cN2"),
+    ("cR1N3 ffnN2 yC1 zC3", "yR0 cR1N3"),
+    ("cR2 ffnN3 yR1 totalR0", "yC1 zC3 cR2"),
+    ("cR3 yR2", "yR1 cR3"),
     ("totalR1 zR1 yR3 cC0", "yR2 cC0"),
-    ("totalR2 zR2 yC1", "yR3 zR1"),
-    ("totalR3 zR3 yC2", "yC1 zR2"),
-    ("cC1 yC3", "yC2 cC1"),
+    ("totalR2 zR2 yC2", "yR3 zR1"),
+    ("totalR3 zR3 yC3 cC1", "yC2 zR2 cC1"),
     ("cC2 gradC0", "yC3 zR3 cC2"),
     ("cC3", None),
 )
@@ -154,7 +154,7 @@
     pass
 
 
-def through(values, name, moved=0):
+def through(values, name, moved=0, earlier=()):
     count = len(values)
     return call(
         nothing,
@@ -162,10 +162,10 @@
         name,
         moved,
         out_shape=[jax.ShapeDtypeStruct(v.shape, v.dtype) for v in values],
-        in_specs=whole(count),
+        in_specs=whole(count) + [pl.BlockSpec(memory_space=pl.ANY)] * len(earlier),
         out_specs=whole(count),
         input_output_aliases={i: i for i in range(count)},
-    )(*values)
+    )(*values, *earlier)
 
 
 def ffn_kernel(count, *refs):
@@ -293,14 +293,14 @@
             out_specs=whole(len(outs)),
         )(*values)
 
-    def land(*names):
+    def land(*names, earlier=()):
         names = [n for name in names for n in flights_of(name)]
         quick = [name for name in names if name[0] == "c"]
         names = [name for name in names if name[0] != "c"]
         values = [flying.pop(name) for name in names]
         if not names:
             names, values = [("C", groups[-1][-1])], [live["C", groups[-1][-1]]]
-        values = through(values, "land", LINK_WORK)
+        values = through(values, "land", LINK_WORK, earlier)
         landed = list(zip(names, values))
         if quick:
             cores = tuple(flying.pop(name) for name in quick) + (values[0],)
@@ -473,12 +473,18 @@
         land(("z", "N", 0), ("z", "C", 0))
     sync()
     for starts, lands in PLAN:
+        kernels = []
         for act in starts.split():
             name = name_of(act)
             steps[name[0]](*(name[1:] if name[0] == "c" else name[1]))
+            if name[0] == "ffn":
+                kernels.append(live["turned", name[1][1:]])
+            if name[0] == "grad":
+                kernels.append(live["first"])
         if lands is None:
             break
-        land(*[n if n[0] == "c" else (n[0],) + n[1] for n in map(name_of, lands.split())])
+        names = [n if n[0] == "c" else (n[0],) + n[1] for n in map(name_of, lands.split())]
+        land(*names, earlier=kernels)
     live["c", "C", 3] = flying.pop(("c", ("C", 3)))
     grad_down = last_grad(
         [(2,), (3,)],

time: 83.6 us -> 81.3 us (0.972)
  starting transfers between devices: 28.4 us -> 25.9 us
    ppermute x9, waiting for transfers between devices: 16.3 us -> 21.6 us  [turn(): return lax.ppermute(value, 'expert', to)]
    ppermute x22, waiting for transfers between devices: 15.4 us -> 10.3 us  [swap(): lax.ppermute(value, 'expert', [(i, i ^ mask) for i in range(devices)])]
    ppermute x9, starting transfers between devices: 15.9 us -> 11.7 us  [turn(): return lax.ppermute(value, 'expert', to)]
    ppermute x22, starting transfers between devices: 12.5 us -> 14.3 us  [swap(): lax.ppermute(value, 'expert', [(i, i ^ mask) for i in range(devices)])]
  transfers between devices with their start and end apart: 31 -> 31, of which waited for: 17 -> 15; matrix products, arithmetic and copies ran while one was open for 0% -> 0% of each run, Pallas kernels for 21% -> 22%
where the time goes in v11:
time: 81.3 us; the launch traced here: 81.2 us
  waiting for transfers between devices  31.9 us (39%)
  starting transfers between devices  25.9 us (32%)
  Pallas kernels  22.2 us (27%)
  between operations  1.17 us (1%)
    ppermute x9, waiting for transfers between devices, turn(): return lax.ppermute(value, 'expert', to)  21.6 us
    ppermute x22, starting transfers between devices, swap(): lax.ppermute(value, 'expert', [(i, i ^ mask) for i in range(devices)])  14.3 us
    ppermute x9, starting transfers between devices, turn(): return lax.ppermute(value, 'expert', to)  11.7 us
    pallas_call x4, Pallas kernels, ffn(): call(functools.partial(ffn_kernel, len(pieces)), 24, 'ffn', out_shape=[ja...  10.5 us
    ppermute x22, waiting for transfers between devices, swap(): lax.ppermute(value, 'expert', [(i, i ^ mask) for i in range(devices)])  10.3 us
    pallas_call x1, Pallas kernels, load(): call(load_kernel, 16, 'load', out_shape=[weight, weight, jax.ShapeDtypeSt...  2.88 us
    pallas_call x1, Pallas kernels, last_grad(): call(functools.partial(last_grad_kernel, plan), 24, 'last_grad', out_shap...  2.71 us
    pallas_call x1, Pallas kernels, send(): call(functools.partial(send_kernel, experts), 16, 'send', out_shape=[piec...  1.92 us
  transfers between devices with their start and end apart: 31, of which 15 were waited for; matrix products, arithmetic and copies ran while one was open for 0% of the time, Pallas kernels for 22%

profile of v11, /device:TPU:0, one launch (start us, length us, event | category | flops | bytes accessed | tf_op | source)
XLA Modules:
  0.0 81.2 jit_solution(13727968906617458464)
XLA Ops:
  0.6 1.9 %send.1 = (bf16[96,1024]{1,0:T(8,128)(2,1)S(1)}, bf16[96,1024]{1,0:T(8,128)(2,1)S(1)}, bf16[96,1024]{1,0:T(8,128)(2,1)S(1)}, bf16[96,1024]{1,0:T(8,128)(2,1)S(1)...) custom-call(s32[1]{0:T(128)} %bitcast.plane_ref, ...), custom_call_target="tpu_custom_call" | custom-call | tf_op jit(solution)/shard_map/send/pallas_call | solution.py:378
  2.6 3.0 %collective-permute-start = (bf16[96,1024]{1,0:T(8,128)(2,1)S(1)}, bf16[96,1024]{1,0:T(8,128)(2,1)S(1)}, u32[]{:S(2)}, u32[]{:S(2)}) collective-permute-start(bf16[96,1024]{1,0:T(8,128)(2,1)S(1)} %get-tuple-element.275.first_ref), channel_id=1, source_target_pairs={{0,2},{1,3},{2,0},{3,1},{4,6},{5,7},{6,4},{7,5},{8,10},{9,11},{10,... | collective-permute-start | bytes 589832 | tf_op jit(solution)/shard_map/ppermute | solution.py:271
  5.6 1.6 %collective-permute-start.1 = (bf16[96,1024]{1,0:T(8,128)(2,1)S(1)}, bf16[96,1024]{1,0:T(8,128)(2,1)S(1)}, u32[]{:S(2)}, u32[]{:S(2)}) collective-permute-start(bf16[96,1024]{1,0:T(8,128)(2,1)S(1)} %get-tuple-element.243), channel_id=1, source_target_pairs={{0,4},{1,5},{2,6},{3,7},{4,8},{5,9},{6,10},{7,11},{8,12},{9,13},{1... | collective-permute-start | bytes 589832 | tf_op jit(solution)/shard_map/ppermute | solution.py:275
  7.2 2.2 %collective-permute-start.2 = (bf16[96,1024]{1,0:T(8,128)(2,1)S(1)}, bf16[96,1024]{1,0:T(8,128)(2,1)S(1)}, u32[]{:S(2)}, u32[]{:S(2)}) collective-permute-start(bf16[96,1024]{1,0:T(8,128)(2,1)S(1)} %get-tuple-element.244), channel_id=1, source_target_pairs={{0,12},{1,13},{2,14},{3,15},{4,0},{5,1},{6,2},{7,3},{8,4},{9,5},{1... | collective-permute-start | bytes 589832 | tf_op jit(solution)/shard_map/ppermute | solution.py:275
  9.4 2.9 %load.1 = (bf16[1024,1024]{1,0:T(8,128)(2,1)S(1)}, bf16[1024,1024]{1,0:T(8,128)(2,1)S(1)}, bf16[1024,1024]{1,0:T(8,128)(2,1)S(1)}) custom-call(bf16[1,1024,1024]{2,1,0:T(8,128)(2,1)} %refs_0_.2, bf16[1,1024,1024]{2,1,0:T(8,128)(2,1)} %refs_1_.3, bf16[1,1024,1024]{2,1,0:T(8,128)(2,1)} %refs_2_.1), custom_call_target="tpu_custom_call" | custom-call | tf_op jit(solution)/shard_map/load/pallas_call | solution.py:393
  12.3 0.9 %collective-permute-start.4 = (bf16[96,1024]{1,0:T(8,128)(2,1)S(1)}, bf16[96,1024]{1,0:T(8,128)(2,1)S(1)}, u32[]{:S(2)}, u32[]{:S(2)}) collective-permute-start(bf16[96,1024]{1,0:T(8,128)(2,1)S(1)} %get-tuple-element.255), channel_id=1, source_target_pairs={{0,8},{1,9},{2,10},{3,11},{4,12},{5,13},{6,14},{7,15},{8,0},{9,1},... | collective-permute-start | bytes 589832 | tf_op jit(solution)/shard_map/ppermute | solution.py:275
  13.7 1.6 %collective-permute-done.1.refs_1_ = bf16[96,1024]{1,0:T(8,128)(2,1)S(1)} collective-permute-done((bf16[96,1024]{1,0:T(8,128)(2,1)S(1)}, bf16[96,1024]{1,0:T(8,128)(2,1)S(1)}, u32[]{:S(2)}, u32[]{:S(2)}) %collective-permute-start.1) | collective-permute-done | bytes 196640 | tf_op jit(solution)/shard_map/ppermute | solution.py:275
  15.3 2.2 %collective-permute-done.2.refs_2_ = bf16[96,1024]{1,0:T(8,128)(2,1)S(1)} collective-permute-done((bf16[96,1024]{1,0:T(8,128)(2,1)S(1)}, bf16[96,1024]{1,0:T(8,128)(2,1)S(1)}, u32[]{:S(2)}, u32[]{:S(2)}) %collective-permute-start.2) | collective-permute-done | bytes 196640 | tf_op jit(solution)/shard_map/ppermute | solution.py:275
  18.9 1.0 %collective-permute-done.6.refs_0_ = bf16[192,1024]{1,0:T(8,128)(2,1)S(1)} collective-permute-done((bf16[192,1024]{1,0:T(8,128)(2,1)S(1)}, bf16[192,1024]{1,0:T(8,128)(2,1)S(1)}, u32[]{:S(2)}, u32[]{:S(2)}) %collective-permute-start.6) | collective-permute-done | bytes 393248 | tf_op jit(solution)/shard_map/ppermute | solution.py:271
  19.8 1.5 %collective-permute-start.10 = (bf16[96,1024]{1,0:T(8,128)(2,1)S(1)}, bf16[96,1024]{1,0:T(8,128)(2,1)S(1)}, u32[]{:S(2)}, u32[]{:S(2)}) collective-permute-start(bf16[96,1024]{1,0:T(8,128)(2,1)S(1)} %get-tuple-element.329.first_ref), channel_id=1, source_target_pairs={{0,2},{1,3},{2,0},{3,1},{4,6},{5,7},{6,4},{7,5},{8,10},{9,11},{10,... | collective-permute-start | bytes 589832 | tf_op jit(solution)/shard_map/ppermute | solution.py:271
  21.3 2.6 %ffn.4 = (bf16[1024,384]{1,0:T(8,128)(2,1)S(1)}, bf16[192,1024]{1,0:T(8,128)(2,1)S(1)}, bf16[192,1024]{1,0:T(8,128)(2,1)S(1)}) custom-call(bf16[192,1024]{1,0:T(8,128)(2,1)S(1)} %pair.10.refs_0_, bf16[192,1024]{1,0:T(8,128)(2,1)S(1)} %land_core.9.refs_1_, bf16[1024,1024]{1,0:T(8,128)(2,1)S(1)} %get-tuple-element.358.refs_2_, ...), custom_call_target="tpu_custom_call" | custom-call | tf_op jit(solution)/shard_map/ffn/pallas_call | solution.py:360
  24.0 2.5 %collective-permute-done.4.refs_1_ = bf16[96,1024]{1,0:T(8,128)(2,1)S(1)} collective-permute-done((bf16[96,1024]{1,0:T(8,128)(2,1)S(1)}, bf16[96,1024]{1,0:T(8,128)(2,1)S(1)}, u32[]{:S(2)}, u32[]{:S(2)}) %collective-permute-start.4) | collective-permute-done | bytes 196640 | tf_op jit(solution)/shard_map/ppermute | solution.py:275
  27.0 0.9 %collective-permute-start.8 = (bf16[96,1024]{1,0:T(8,128)(2,1)S(1)}, bf16[96,1024]{1,0:T(8,128)(2,1)S(1)}, u32[]{:S(2)}, u32[]{:S(2)}) collective-permute-start(bf16[96,1024]{1,0:T(8,128)(2,1)S(1)} %get-tuple-element.296), channel_id=1, source_target_pairs={{0,4},{1,5},{2,6},{3,7},{4,8},{5,9},{6,10},{7,11},{8,12},{9,13},{1... | collective-permute-start | bytes 589832 | tf_op jit(solution)/shard_map/ppermute | solution.py:275
  27.9 2.9 %collective-permute-start.9 = (bf16[96,1024]{1,0:T(8,128)(2,1)S(1)}, bf16[96,1024]{1,0:T(8,128)(2,1)S(1)}, u32[]{:S(2)}, u32[]{:S(2)}) collective-permute-start(bf16[96,1024]{1,0:T(8,128)(2,1)S(1)} %get-tuple-element.297), channel_id=1, source_target_pairs={{0,12},{1,13},{2,14},{3,15},{4,0},{5,1},{6,2},{7,3},{8,4},{9,5},{1... | collective-permute-start | bytes 589832 | tf_op jit(solution)/shard_map/ppermute | solution.py:275
  31.0 2.3 %collective-permute-done.11.refs_0_ = bf16[384,1024]{1,0:T(8,128)(2,1)S(1)} collective-permute-done((bf16[384,1024]{1,0:T(8,128)(2,1)S(1)}, bf16[384,1024]{1,0:T(8,128)(2,1)S(1)}, u32[]{:S(2)}, u32[]{:S(2)}) %collective-permute-start.11) | collective-permute-done | bytes 786464 | tf_op jit(solution)/shard_map/ppermute | solution.py:271
  33.6 1.6 %collective-permute-start.15 = (bf16[96,1024]{1,0:T(8,128)(2,1)S(1)}, bf16[96,1024]{1,0:T(8,128)(2,1)S(1)}, u32[]{:S(2)}, u32[]{:S(2)}) collective-permute-start(bf16[96,1024]{1,0:T(8,128)(2,1)S(1)} %fold.4), channel_id=1, source_target_pairs={{0,2},{1,3},{2,0},{3,1},{4,6},{5,7},{6,4},{7,5},{8,10},{9,11},{10,... | collective-permute-start | bytes 589832 | tf_op jit(solution)/shard_map/ppermute | solution.py:271
  35.2 2.6 %ffn.5 = (bf16[1024,384]{1,0:T(8,128)(2,1)S(1)}, bf16[192,1024]{1,0:T(8,128)(2,1)S(1)}, bf16[192,1024]{1,0:T(8,128)(2,1)S(1)}) custom-call(bf16[192,1024]{1,0:T(8,128)(2,1)S(1)} %pair.11.second_ref.refs_0_, bf16[192,1024]{1,0:T(8,128)(2,1)S(1)} %get-tuple-element.313.refs_1_, bf16[1024,1024]{1,0:T(8,128)(2,1)S(1)} %get-tuple-element.358.refs_2_, ...), custom_call_target="tpu_custom_call" | custom-call | tf_op jit(solution)/shard_map/ffn/pallas_call | solution.py:360
  37.8 1.5 %collective-permute-done.9.refs_2_ = bf16[96,1024]{1,0:T(8,128)(2,1)S(1)} collective-permute-done((bf16[96,1024]{1,0:T(8,128)(2,1)S(1)}, bf16[96,1024]{1,0:T(8,128)(2,1)S(1)}, u32[]{:S(2)}, u32[]{:S(2)}) %collective-permute-start.9) | collective-permute-done | bytes 196640 | tf_op jit(solution)/shard_map/ppermute | solution.py:275
  39.3 1.5 %collective-permute-start.13 = (bf16[96,1024]{1,0:T(8,128)(2,1)S(1)}, bf16[96,1024]{1,0:T(8,128)(2,1)S(1)}, u32[]{:S(2)}, u32[]{:S(2)}) collective-permute-start(bf16[96,1024]{1,0:T(8,128)(2,1)S(1)} %get-tuple-element.450.first_ref), channel_id=1, source_target_pairs={{0,2},{1,3},{2,0},{3,1},{4,6},{5,7},{6,4},{7,5},{8,10},{9,11},{10,... | collective-permute-start | bytes 589832 | tf_op jit(solution)/shard_map/ppermute | solution.py:271
  40.8 1.5 %collective-permute-start.14 = (bf16[96,1024]{1,0:T(8,128)(2,1)S(1)}, bf16[96,1024]{1,0:T(8,128)(2,1)S(1)}, u32[]{:S(2)}, u32[]{:S(2)}) collective-permute-start(bf16[96,1024]{1,0:T(8,128)(2,1)S(1)} %land.14), channel_id=1, source_target_pairs={{0,8},{1,9},{2,10},{3,11},{4,12},{5,13},{6,14},{7,15},{8,0},{9,1},... | collective-permute-start | bytes 589832 | tf_op jit(solution)/shard_map/ppermute | solution.py:275
  42.5 2.6 %ffn.6 = (bf16[1024,384]{1,0:T(8,128)(2,1)S(1)}, bf16[192,1024]{1,0:T(8,128)(2,1)S(1)}, bf16[192,1024]{1,0:T(8,128)(2,1)S(1)}) custom-call(bf16[192,1024]{1,0:T(8,128)(2,1)S(1)} %pair.13.refs_0_, bf16[192,1024]{1,0:T(8,128)(2,1)S(1)} %land_core.11.refs_1_, bf16[1024,1024]{1,0:T(8,128)(2,1)S(1)} %get-tuple-element.358.refs_2_, ...), custom_call_target="tpu_custom_call" | custom-call | tf_op jit(solution)/shard_map/ffn/pallas_call | solution.py:360
  46.5 2.6 %ffn.7 = (bf16[1024,384]{1,0:T(8,128)(2,1)S(1)}, bf16[192,1024]{1,0:T(8,128)(2,1)S(1)}, bf16[192,1024]{1,0:T(8,128)(2,1)S(1)}) custom-call(bf16[192,1024]{1,0:T(8,128)(2,1)S(1)} %pair.14.second_ref.refs_0_, bf16[192,1024]{1,0:T(8,128)(2,1)S(1)} %get-tuple-element.357.refs_1_, bf16[1024,1024]{1,0:T(8,128)(2,1)S(1)} %get-tuple-element.358.refs_2_, ...), custom_call_target="tpu_custom_call" | custom-call | tf_op jit(solution)/shard_map/ffn/pallas_call | solution.py:360
  49.1 3.1 %collective-permute-done.14.refs_1_ = bf16[96,1024]{1,0:T(8,128)(2,1)S(1)} collective-permute-done((bf16[96,1024]{1,0:T(8,128)(2,1)S(1)}, bf16[96,1024]{1,0:T(8,128)(2,1)S(1)}, u32[]{:S(2)}, u32[]{:S(2)}) %collective-permute-start.14) | collective-permute-done | bytes 196640 | tf_op jit(solution)/shard_map/ppermute | solution.py:275
  52.9 1.7 %collective-permute-done.19.refs_0_ = bf16[192,1024]{1,0:T(8,128)(2,1)S(1)} collective-permute-done((bf16[192,1024]{1,0:T(8,128)(2,1)S(1)}, bf16[192,1024]{1,0:T(8,128)(2,1)S(1)}, u32[]{:S(2)}, u32[]{:S(2)}) %collective-permute-start.19) | collective-permute-done | bytes 393248 | tf_op jit(solution)/shard_map/ppermute | solution.py:271
  54.7 1.6 %collective-permute-start.22 = (bf16[96,1024]{1,0:T(8,128)(2,1)S(1)}, bf16[96,1024]{1,0:T(8,128)(2,1)S(1)}, u32[]{:S(2)}, u32[]{:S(2)}) collective-permute-start(bf16[96,1024]{1,0:T(8,128)(2,1)S(1)} %fold.7), channel_id=1, source_target_pairs={{0,2},{1,3},{2,0},{3,1},{4,6},{5,7},{6,4},{7,5},{8,10},{9,11},{10,... | collective-permute-start | bytes 589832 | tf_op jit(solution)/shard_map/ppermute | solution.py:271
  57.3 2.5 %collective-permute-done.20.refs_0_ = bf16[96,1024]{1,0:T(8,128)(2,1)S(1)} collective-permute-done((bf16[96,1024]{1,0:T(8,128)(2,1)S(1)}, bf16[96,1024]{1,0:T(8,128)(2,1)S(1)}, u32[]{:S(2)}, u32[]{:S(2)}) %collective-permute-start.20) | collective-permute-done | bytes 196640 | tf_op jit(solution)/shard_map/ppermute | solution.py:271
  61.1 1.8 %collective-permute-done.22.refs_0_ = bf16[96,1024]{1,0:T(8,128)(2,1)S(1)} collective-permute-done((bf16[96,1024]{1,0:T(8,128)(2,1)S(1)}, bf16[96,1024]{1,0:T(8,128)(2,1)S(1)}, u32[]{:S(2)}, u32[]{:S(2)}) %collective-permute-start.22) | collective-permute-done | bytes 196640 | tf_op jit(solution)/shard_map/ppermute | solution.py:271
  63.9 5.9 %collective-permute-done.25.refs_1_ = bf16[96,1024]{1,0:T(8,128)(2,1)S(1)} collective-permute-done((bf16[96,1024]{1,0:T(8,128)(2,1)S(1)}, bf16[96,1024]{1,0:T(8,128)(2,1)S(1)}, u32[]{:S(2)}, u32[]{:S(2)}) %collective-permute-start.25) | collective-permute-done | bytes 196640 | tf_op jit(solution)/shard_map/ppermute | solution.py:275
  69.9 1.9 %first_grad.1.refs_2_.first_ref = f32[1024,1024]{1,0:T(8,128)S(1)} custom-call(bf16[1024,384]{1,0:T(8,128)(2,1)S(1)} %get-tuple-element.454.refs_2_.refs_0_, bf16[1024,384]{1,0:T(8,128)(2,1)S(1)} %get-tuple-element.455.refs_3_.refs_1_, bf16[192,1024]{1,0:T(8,128)(2,1)S(1)} %pair.16.refs_2_, bf16[192,1024]{1,0:T(8,128)(2,1)S(1)} %pair.17.refs_3_, ...), custom_call_target="tpu_custom_call" | custom-call | tf_op jit(solution)/shard_map/first_grad/pallas_call | solution.py:428
  71.8 4.6 %collective-permute-done.28.refs_1_ = bf16[96,1024]{1,0:T(8,128)(2,1)S(1)} collective-permute-done((bf16[96,1024]{1,0:T(8,128)(2,1)S(1)}, bf16[96,1024]{1,0:T(8,128)(2,1)S(1)}, u32[]{:S(2)}, u32[]{:S(2)}) %collective-permute-start.28) | collective-permute-done | bytes 196640 | tf_op jit(solution)/shard_map/ppermute | solution.py:275
  76.6 1.4 %combine.1 = bf16[128,1024]{1,0:T(8,128)(2,1)} custom-call(s32[1]{0:T(128)} %bitcast.plane_ref, bf16[128,1024]{1,0:T(8,128)(2,1)S(1)} %copy-done, s32[2,128]{1,0:T(2,128)S(1)} %bitcast.5, s32[2,128]{1,0:T(2,128)S(1)} %bitcast.7, bf16[96,1024]{1,0:T(8,128)(2,1)S(1)} %total.4.refs_0_, bf16[96,1024]{1,0:T(8,128)(2,1)S(1)} %get-tuple-element.472.refs_1_, ...), custom_call_target="tpu_custom_call" | custom-call | tf_op jit(solution)/shard_map/combine/pallas_call | solution.py:493
  78.3 2.7 %last_grad.1 = bf16[1,1024,1024]{2,1,0:T(8,128)(2,1)} custom-call(f32[1024,1024]{1,0:T(8,128)S(1)} %first_grad.1.refs_2_.first_ref, bf16[1024,384]{1,0:T(8,128)(2,1)S(1)} %get-tuple-element.476.refs_1_.refs_0_, bf16[1024,384]{1,0:T(8,128)(2,1)S(1)} %get-tuple-element.477.refs_2_.refs_1_, bf16[192,1024]{1,0:T(8,128)(2,1)S(1)} %pair.18.refs_2_, ...), custom_call_target="tpu_custom_call" | custom-call | tf_op jit(solution)/shard_map/last_grad/pallas_call | solution.py:440
  (87 shorter events, 8.9 us)
Async XLA Ops:
  2.6 11.1 %collective-permute-start = (bf16[96,1024]{1,0:T(8,128)(2,1)S(1)}, bf16[96,1024]{1,0:T(8,128)(2,1)S(1)}, u32[]{:S(2)}, u32[]{:S(2)}) collective-permute-start(bf16[96,1024]{1,0:T(8,128)(2,1)S(1)} %get-tuple-element.275.first_ref), channel_id=1, source_target_pairs={{0,2},{1,3},{2,0},{3,1},{4,6},{5,7},{6,4},{7,5},{8,10},{9,11},{10,... | collective-permute-start | bytes 589832 | tf_op jit(solution)/shard_map/ppermute | solution.py:271
  5.6 9.7 %collective-permute-start.1 = (bf16[96,1024]{1,0:T(8,128)(2,1)S(1)}, bf16[96,1024]{1,0:T(8,128)(2,1)S(1)}, u32[]{:S(2)}, u32[]{:S(2)}) collective-permute-start(bf16[96,1024]{1,0:T(8,128)(2,1)S(1)} %get-tuple-element.243), channel_id=1, source_target_pairs={{0,4},{1,5},{2,6},{3,7},{4,8},{5,9},{6,10},{7,11},{8,12},{9,13},{1... | collective-permute-start | bytes 589832 | tf_op jit(solution)/shard_map/ppermute | solution.py:275
  7.2 10.3 %collective-permute-start.2 = (bf16[96,1024]{1,0:T(8,128)(2,1)S(1)}, bf16[96,1024]{1,0:T(8,128)(2,1)S(1)}, u32[]{:S(2)}, u32[]{:S(2)}) collective-permute-start(bf16[96,1024]{1,0:T(8,128)(2,1)S(1)} %get-tuple-element.244), channel_id=1, source_target_pairs={{0,12},{1,13},{2,14},{3,15},{4,0},{5,1},{6,2},{7,3},{8,4},{9,5},{1... | collective-permute-start | bytes 589832 | tf_op jit(solution)/shard_map/ppermute | solution.py:275
  12.3 14.2 %collective-permute-start.4 = (bf16[96,1024]{1,0:T(8,128)(2,1)S(1)}, bf16[96,1024]{1,0:T(8,128)(2,1)S(1)}, u32[]{:S(2)}, u32[]{:S(2)}) collective-permute-start(bf16[96,1024]{1,0:T(8,128)(2,1)S(1)} %get-tuple-element.255), channel_id=1, source_target_pairs={{0,8},{1,9},{2,10},{3,11},{4,12},{5,13},{6,14},{7,15},{8,0},{9,1},... | collective-permute-start | bytes 589832 | tf_op jit(solution)/shard_map/ppermute | solution.py:275
  13.2 5.7 %collective-permute-start.5 = (bf16[96,1024]{1,0:T(8,128)(2,1)S(1)}, bf16[96,1024]{1,0:T(8,128)(2,1)S(1)}, u32[]{:S(2)}, u32[]{:S(2)}) collective-permute-start(bf16[96,1024]{1,0:T(8,128)(2,1)S(1)} %get-tuple-element.415.first_ref), channel_id=1, source_target_pairs={{0,2},{1,3},{2,0},{3,1},{4,6},{5,7},{6,4},{7,5},{8,10},{9,11},{10,... | collective-permute-start | bytes 589832 | tf_op jit(solution)/shard_map/ppermute | solution.py:271
  17.5 9.0 %collective-permute-start.3 = (bf16[96,1024]{1,0:T(8,128)(2,1)S(1)}, bf16[96,1024]{1,0:T(8,128)(2,1)S(1)}, u32[]{:S(2)}, u32[]{:S(2)}) collective-permute-start(bf16[96,1024]{1,0:T(8,128)(2,1)S(1)} %get-tuple-element.307.first_ref), channel_id=1, source_target_pairs={{0,2},{1,3},{2,0},{3,1},{4,6},{5,7},{6,4},{7,5},{8,10},{9,11},{10,... | collective-permute-start | bytes 589832 | tf_op jit(solution)/shard_map/ppermute | solution.py:271
  18.0 1.8 %collective-permute-start.6 = (bf16[192,1024]{1,0:T(8,128)(2,1)S(1)}, bf16[192,1024]{1,0:T(8,128)(2,1)S(1)}, u32[]{:S(2)}, u32[]{:S(2)}) collective-permute-start(bf16[192,1024]{1,0:T(8,128)(2,1)S(1)} %pair.10.refs_0_), channel_id=1, source_target_pairs={{0,1},{1,0},{2,3},{3,2},{4,5},{5,4},{6,7},{7,6},{8,9},{9,8},{10,11... | collective-permute-start | bytes 1179656 | tf_op jit(solution)/shard_map/ppermute | solution.py:271
  19.8 11.2 %collective-permute-start.10 = (bf16[96,1024]{1,0:T(8,128)(2,1)S(1)}, bf16[96,1024]{1,0:T(8,128)(2,1)S(1)}, u32[]{:S(2)}, u32[]{:S(2)}) collective-permute-start(bf16[96,1024]{1,0:T(8,128)(2,1)S(1)} %get-tuple-element.329.first_ref), channel_id=1, source_target_pairs={{0,2},{1,3},{2,0},{3,1},{4,6},{5,7},{6,4},{7,5},{8,10},{9,11},{10,... | collective-permute-start | bytes 589832 | tf_op jit(solution)/shard_map/ppermute | solution.py:271
  26.5 11.3 %collective-permute-start.7 = (bf16[96,1024]{1,0:T(8,128)(2,1)S(1)}, bf16[96,1024]{1,0:T(8,128)(2,1)S(1)}, u32[]{:S(2)}, u32[]{:S(2)}) collective-permute-start(bf16[96,1024]{1,0:T(8,128)(2,1)S(1)} %get-tuple-element.346.first_ref), channel_id=1, source_target_pairs={{0,2},{1,3},{2,0},{3,1},{4,6},{5,7},{6,4},{7,5},{8,10},{9,11},{10,... | collective-permute-start | bytes 589832 | tf_op jit(solution)/shard_map/ppermute | solution.py:271
  27.0 10.8 %collective-permute-start.8 = (bf16[96,1024]{1,0:T(8,128)(2,1)S(1)}, bf16[96,1024]{1,0:T(8,128)(2,1)S(1)}, u32[]{:S(2)}, u32[]{:S(2)}) collective-permute-start(bf16[96,1024]{1,0:T(8,128)(2,1)S(1)} %get-tuple-element.296), channel_id=1, source_target_pairs={{0,4},{1,5},{2,6},{3,7},{4,8},{5,9},{6,10},{7,11},{8,12},{9,13},{1... | collective-permute-start | bytes 589832 | tf_op jit(solution)/shard_map/ppermute | solution.py:275
  27.9 11.4 %collective-permute-start.9 = (bf16[96,1024]{1,0:T(8,128)(2,1)S(1)}, bf16[96,1024]{1,0:T(8,128)(2,1)S(1)}, u32[]{:S(2)}, u32[]{:S(2)}) collective-permute-start(bf16[96,1024]{1,0:T(8,128)(2,1)S(1)} %get-tuple-element.297), channel_id=1, source_target_pairs={{0,12},{1,13},{2,14},{3,15},{4,0},{5,1},{6,2},{7,3},{8,4},{9,5},{1... | collective-permute-start | bytes 589832 | tf_op jit(solution)/shard_map/ppermute | solution.py:275
  30.9 2.4 %collective-permute-start.11 = (bf16[384,1024]{1,0:T(8,128)(2,1)S(1)}, bf16[384,1024]{1,0:T(8,128)(2,1)S(1)}, u32[]{:S(2)}, u32[]{:S(2)}) collective-permute-start(bf16[384,1024]{1,0:T(8,128)(2,1)S(1)} %pair.12), channel_id=1, source_target_pairs={{0,1},{1,0},{2,3},{3,2},{4,5},{5,4},{6,7},{7,6},{8,9},{9,8},{10,11... | collective-permute-start | bytes 2359304 | tf_op jit(solution)/shard_map/ppermute | solution.py:271
  33.3 6.0 %collective-permute-start.12 = (bf16[192,1024]{1,0:T(8,128)(2,1)S(1)}, bf16[192,1024]{1,0:T(8,128)(2,1)S(1)}, u32[]{:S(2)}, u32[]{:S(2)}) collective-permute-start(bf16[192,1024]{1,0:T(8,128)(2,1)S(1)} %pair.13.refs_0_), channel_id=1, source_target_pairs={{0,1},{1,0},{2,3},{3,2},{4,5},{5,4},{6,7},{7,6},{8,9},{9,8},{10,11... | collective-permute-start | bytes 1179656 | tf_op jit(solution)/shard_map/ppermute | solution.py:271
  33.6 11.6 %collective-permute-start.15 = (bf16[96,1024]{1,0:T(8,128)(2,1)S(1)}, bf16[96,1024]{1,0:T(8,128)(2,1)S(1)}, u32[]{:S(2)}, u32[]{:S(2)}) collective-permute-start(bf16[96,1024]{1,0:T(8,128)(2,1)S(1)} %fold.4), channel_id=1, source_target_pairs={{0,2},{1,3},{2,0},{3,1},{4,6},{5,7},{6,4},{7,5},{8,10},{9,11},{10,... | collective-permute-start | bytes 589832 | tf_op jit(solution)/shard_map/ppermute | solution.py:271
  39.3 9.8 %collective-permute-start.13 = (bf16[96,1024]{1,0:T(8,128)(2,1)S(1)}, bf16[96,1024]{1,0:T(8,128)(2,1)S(1)}, u32[]{:S(2)}, u32[]{:S(2)}) collective-permute-start(bf16[96,1024]{1,0:T(8,128)(2,1)S(1)} %get-tuple-element.450.first_ref), channel_id=1, source_target_pairs={{0,2},{1,3},{2,0},{3,1},{4,6},{5,7},{6,4},{7,5},{8,10},{9,11},{10,... | collective-permute-start | bytes 589832 | tf_op jit(solution)/shard_map/ppermute | solution.py:271
  40.8 11.3 %collective-permute-start.14 = (bf16[96,1024]{1,0:T(8,128)(2,1)S(1)}, bf16[96,1024]{1,0:T(8,128)(2,1)S(1)}, u32[]{:S(2)}, u32[]{:S(2)}) collective-permute-start(bf16[96,1024]{1,0:T(8,128)(2,1)S(1)} %land.14), channel_id=1, source_target_pairs={{0,8},{1,9},{2,10},{3,11},{4,12},{5,13},{6,14},{7,15},{8,0},{9,1},... | collective-permute-start | bytes 589832 | tf_op jit(solution)/shard_map/ppermute | solution.py:275
  42.5 2.7 %collective-permute-start.16 = (bf16[384,1024]{1,0:T(8,128)(2,1)S(1)}, bf16[384,1024]{1,0:T(8,128)(2,1)S(1)}, u32[]{:S(2)}, u32[]{:S(2)}) collective-permute-start(bf16[384,1024]{1,0:T(8,128)(2,1)S(1)} %pair.15), channel_id=1, source_target_pairs={{0,1},{1,0},{2,3},{3,2},{4,5},{5,4},{6,7},{7,6},{8,9},{9,8},{10,11... | collective-permute-start | bytes 2359304 | tf_op jit(solution)/shard_map/ppermute | solution.py:271
  45.2 7.0 %collective-permute-start.17 = (bf16[192,1024]{1,0:T(8,128)(2,1)S(1)}, bf16[192,1024]{1,0:T(8,128)(2,1)S(1)}, u32[]{:S(2)}, u32[]{:S(2)}) collective-permute-start(bf16[192,1024]{1,0:T(8,128)(2,1)S(1)} %get-tuple-element.379), channel_id=1, source_target_pairs={{0,1},{1,0},{2,3},{3,2},{4,5},{5,4},{6,7},{7,6},{8,9},{9,8},{10,11... | collective-permute-start | bytes 1179656 | tf_op jit(solution)/shard_map/ppermute | solution.py:271
  45.9 7.0 %collective-permute-start.18 = (bf16[96,1024]{1,0:T(8,128)(2,1)S(1)}, bf16[96,1024]{1,0:T(8,128)(2,1)S(1)}, u32[]{:S(2)}, u32[]{:S(2)}) collective-permute-start(bf16[96,1024]{1,0:T(8,128)(2,1)S(1)} %fold.5), channel_id=1, source_target_pairs={{0,2},{1,3},{2,0},{3,1},{4,6},{5,7},{6,4},{7,5},{8,10},{9,11},{10,... | collective-permute-start | bytes 589832 | tf_op jit(solution)/shard_map/ppermute | solution.py:271
  52.3 7.4 %collective-permute-start.20 = (bf16[96,1024]{1,0:T(8,128)(2,1)S(1)}, bf16[96,1024]{1,0:T(8,128)(2,1)S(1)}, u32[]{:S(2)}, u32[]{:S(2)}) collective-permute-start(bf16[96,1024]{1,0:T(8,128)(2,1)S(1)} %fold.6), channel_id=1, source_target_pairs={{0,2},{1,3},{2,0},{3,1},{4,6},{5,7},{6,4},{7,5},{8,10},{9,11},{10,... | collective-permute-start | bytes 589832 | tf_op jit(solution)/shard_map/ppermute | solution.py:271
  52.9 1.7 %collective-permute-start.19 = (bf16[192,1024]{1,0:T(8,128)(2,1)S(1)}, bf16[192,1024]{1,0:T(8,128)(2,1)S(1)}, u32[]{:S(2)}, u32[]{:S(2)}) collective-permute-start(bf16[192,1024]{1,0:T(8,128)(2,1)S(1)} %get-tuple-element.397), channel_id=1, source_target_pairs={{0,1},{1,0},{2,3},{3,2},{4,5},{5,4},{6,7},{7,6},{8,9},{9,8},{10,11... | collective-permute-start | bytes 1179656 | tf_op jit(solution)/shard_map/ppermute | solution.py:271
  54.7 8.2 %collective-permute-start.22 = (bf16[96,1024]{1,0:T(8,128)(2,1)S(1)}, bf16[96,1024]{1,0:T(8,128)(2,1)S(1)}, u32[]{:S(2)}, u32[]{:S(2)}) collective-permute-start(bf16[96,1024]{1,0:T(8,128)(2,1)S(1)} %fold.7), channel_id=1, source_target_pairs={{0,2},{1,3},{2,0},{3,1},{4,6},{5,7},{6,4},{7,5},{8,10},{9,11},{10,... | collective-permute-start | bytes 589832 | tf_op jit(solution)/shard_map/ppermute | solution.py:271
  56.3 6.7 %collective-permute-start.23 = (bf16[96,1024]{1,0:T(8,128)(2,1)S(1)}, bf16[96,1024]{1,0:T(8,128)(2,1)S(1)}, u32[]{:S(2)}, u32[]{:S(2)}) collective-permute-start(bf16[96,1024]{1,0:T(8,128)(2,1)S(1)} %total.5), channel_id=1, source_target_pairs={{0,12},{1,13},{2,14},{3,15},{4,0},{5,1},{6,2},{7,3},{8,4},{9,5},{1... | collective-permute-start | bytes 589832 | tf_op jit(solution)/shard_map/ppermute | solution.py:275
  57.2 2.5 %collective-permute-start.21 = (bf16[192,1024]{1,0:T(8,128)(2,1)S(1)}, bf16[192,1024]{1,0:T(8,128)(2,1)S(1)}, u32[]{:S(2)}, u32[]{:S(2)}) collective-permute-start(bf16[192,1024]{1,0:T(8,128)(2,1)S(1)} %pair.16.refs_2_), channel_id=1, source_target_pairs={{0,1},{1,0},{2,3},{3,2},{4,5},{5,4},{6,7},{7,6},{8,9},{9,8},{10,11... | collective-permute-start | bytes 1179656 | tf_op jit(solution)/shard_map/ppermute | solution.py:271
  59.8 10.0 %collective-permute-start.25 = (bf16[96,1024]{1,0:T(8,128)(2,1)S(1)}, bf16[96,1024]{1,0:T(8,128)(2,1)S(1)}, u32[]{:S(2)}, u32[]{:S(2)}) collective-permute-start(bf16[96,1024]{1,0:T(8,128)(2,1)S(1)} %total.6), channel_id=1, source_target_pairs={{0,4},{1,5},{2,6},{3,7},{4,8},{5,9},{6,10},{7,11},{8,12},{9,13},{1... | collective-permute-start | bytes 589832 | tf_op jit(solution)/shard_map/ppermute | solution.py:275
  60.5 9.3 %collective-permute-start.24 = (bf16[96,1024]{1,0:T(8,128)(2,1)S(1)}, bf16[96,1024]{1,0:T(8,128)(2,1)S(1)}, u32[]{:S(2)}, u32[]{:S(2)}) collective-permute-start(bf16[96,1024]{1,0:T(8,128)(2,1)S(1)} %get-tuple-element.467.first_ref), channel_id=1, source_target_pairs={{0,2},{1,3},{2,0},{3,1},{4,6},{5,7},{6,4},{7,5},{8,10},{9,11},{10,... | collective-permute-start | bytes 589832 | tf_op jit(solution)/shard_map/ppermute | solution.py:271
  63.1 13.3 %collective-permute-start.28 = (bf16[96,1024]{1,0:T(8,128)(2,1)S(1)}, bf16[96,1024]{1,0:T(8,128)(2,1)S(1)}, u32[]{:S(2)}, u32[]{:S(2)}) collective-permute-start(bf16[96,1024]{1,0:T(8,128)(2,1)S(1)} %total.7), channel_id=1, source_target_pairs={{0,8},{1,9},{2,10},{3,11},{4,12},{5,13},{6,14},{7,15},{8,0},{9,1},... | collective-permute-start | bytes 589832 | tf_op jit(solution)/shard_map/ppermute | solution.py:275
  63.2 13.3 %collective-permute-start.27 = (bf16[96,1024]{1,0:T(8,128)(2,1)S(1)}, bf16[96,1024]{1,0:T(8,128)(2,1)S(1)}, u32[]{:S(2)}, u32[]{:S(2)}) collective-permute-start(bf16[96,1024]{1,0:T(8,128)(2,1)S(1)} %get-tuple-element.479.first_ref), channel_id=1, source_target_pairs={{0,2},{1,3},{2,0},{3,1},{4,6},{5,7},{6,4},{7,5},{8,10},{9,11},{10,... | collective-permute-start | bytes 589832 | tf_op jit(solution)/shard_map/ppermute | solution.py:271
  63.8 6.0 %collective-permute-start.26 = (bf16[192,1024]{1,0:T(8,128)(2,1)S(1)}, bf16[192,1024]{1,0:T(8,128)(2,1)S(1)}, u32[]{:S(2)}, u32[]{:S(2)}) collective-permute-start(bf16[192,1024]{1,0:T(8,128)(2,1)S(1)} %pair.17.refs_3_), channel_id=1, source_target_pairs={{0,1},{1,0},{2,3},{3,2},{4,5},{5,4},{6,7},{7,6},{8,9},{9,8},{10,11... | collective-permute-start | bytes 1179656 | tf_op jit(solution)/shard_map/ppermute | solution.py:271
  69.8 6.6 %collective-permute-start.29 = (bf16[192,1024]{1,0:T(8,128)(2,1)S(1)}, bf16[192,1024]{1,0:T(8,128)(2,1)S(1)}, u32[]{:S(2)}, u32[]{:S(2)}) collective-permute-start(bf16[192,1024]{1,0:T(8,128)(2,1)S(1)} %pair.18.refs_2_), channel_id=1, source_target_pairs={{0,1},{1,0},{2,3},{3,2},{4,5},{5,4},{6,7},{7,6},{8,9},{9,8},{10,11... | collective-permute-start | bytes 1179656 | tf_op jit(solution)/shard_map/ppermute | solution.py:271
  71.8 4.8 %copy-start = (bf16[128,1024]{1,0:T(8,128)(2,1)S(1)}, bf16[128,1024]{1,0:T(8,128)(2,1)}, u32[]{:S(2)}) copy-start(bf16[128,1024]{1,0:T(8,128)(2,1)} %tokens_ref.1) | copy-start | bytes 786436
  76.5 1.8 %collective-permute-start.30 = (bf16[192,1024]{1,0:T(8,128)(2,1)S(1)}, bf16[192,1024]{1,0:T(8,128)(2,1)S(1)}, u32[]{:S(2)}, u32[]{:S(2)}) collective-permute-start(bf16[192,1024]{1,0:T(8,128)(2,1)S(1)} %pair.19.refs_3_), channel_id=1, source_target_pairs={{0,1},{1,0},{2,3},{3,2},{4,5},{5,4},{6,7},{7,6},{8,9},{9,8},{10,11... | collective-permute-start | bytes 1179656 | tf_op jit(solution)/shard_map/ppermute | solution.py:271
  (2 other events, 9.6 us)

commit v12 on v11

--- a/solution.py
+++ b/solution.py
@@ -10,19 +10,19 @@
 HSPLIT = 4
 GROUPS = 4
 PLAN = (
-    ("zN1 zN2 yN0 loadW0", ""),
-    ("yC0 zN3", "yN0 zN1 zN2"),
+    ("yN0 zN1 zN2", ""),
+    ("yC0 zN3 loadW0", "yN0 zN1 zN2"),
     ("cN0 yN1", "yC0 cN0"),
-    ("ffnN0 yN2", "yN1 zN3"),
-    ("cR0N1 yN3 zC1 zC2", "yN2 cR0N1"),
-    ("ffnN1 cN2 yR0", "yN3 zC1 zC2 cN2"),
-    ("cR1N3 ffnN2 yC1 zC3", "yR0 cR1N3"),
-    ("cR2 ffnN3 yR1 totalR0", "yC1 zC3 cR2"),
-    ("cR3 yR2", "yR1 cR3"),
+    ("ffnN0 yN2 zC1", "yN1 zN3"),
+    ("cR0N1 yN3 zC2", "yN2 zC1 cR0N1"),
+    ("cN2 ffnN1 cR1 yR0", "yN3 zC2 cN2 cR1"),
+    ("cN3 ffnN2 cR2 yR1 zC3", "yR0 cN3 cR2"),
+    ("ffnN3 cR3 yR2 totalR0", "yR1 zC3 cR3"),
     ("totalR1 zR1 yR3 cC0", "yR2 cC0"),
-    ("totalR2 zR2 yC2", "yR3 zR1"),
-    ("totalR3 zR3 yC3 cC1", "yC2 zR2 cC1"),
-    ("cC2 gradC0", "yC3 zR3 cC2"),
+    ("totalR2 zR2 yC1", "yR3 zR1"),
+    ("totalR3 zR3 yC2", "yC1 zR2"),
+    ("cC1 yC3", "yC2 zR3 cC1"),
+    ("cC2 gradC0", "yC3 cC2"),
     ("cC3", None),
 )
 TILE = 256

time: 81.3 us -> 84.7 us (1.042)
  starting transfers between devices: 25.9 us -> 31.5 us
  waiting for transfers between devices: 31.9 us -> 29.5 us
    ppermute x9, starting transfers between devices: 11.7 us -> 17.4 us  [turn(): return lax.ppermute(value, 'expert', to)]
    ppermute x9, waiting for transfers between devices: 21.6 us -> 19.8 us  [turn(): return lax.ppermute(value, 'expert', to)]
    ppermute x22 -> x23, waiting for transfers between devices: 10.3 us -> 9.67 us  [swap(): lax.ppermute(value, 'expert', [(i, i ^ mask) for i in range(devices)])]
    ppermute x22 -> x23, starting transfers between devices: 14.3 us -> 14.1 us  [swap(): lax.ppermute(value, 'expert', [(i, i ^ mask) for i in range(devices)])]
  transfers between devices with their start and end apart: 31 -> 32, of which waited for: 15 -> 14; matrix products, arithmetic and copies ran while one was open for 0% -> 0% of each run, Pallas kernels for 22% -> 21%
where the time goes in v12:
time: 84.7 us; the launch traced here: 84.5 us
  starting transfers between devices  31.5 us (37%)
  waiting for transfers between devices  29.5 us (35%)
  Pallas kernels  22 us (26%)
  between operations  1.13 us (1%)
    ppermute x9, waiting for transfers between devices, turn(): return lax.ppermute(value, 'expert', to)  19.8 us
    ppermute x9, starting transfers between devices, turn(): return lax.ppermute(value, 'expert', to)  17.4 us
    ppermute x23, starting transfers between devices, swap(): lax.ppermute(value, 'expert', [(i, i ^ mask) for i in range(devices)])  14.1 us
    pallas_call x4, Pallas kernels, ffn(): call(functools.partial(ffn_kernel, len(pieces)), 24, 'ffn', out_shape=[ja...  10.5 us
    ppermute x23, waiting for transfers between devices, swap(): lax.ppermute(value, 'expert', [(i, i ^ mask) for i in range(devices)])  9.67 us
    pallas_call x1, Pallas kernels, load(): call(load_kernel, 16, 'load', out_shape=[weight, weight, jax.ShapeDtypeSt...  2.88 us
    pallas_call x1, Pallas kernels, last_grad(): call(functools.partial(last_grad_kernel, plan), 24, 'last_grad', out_shap...  2.7 us
    pallas_call x1, Pallas kernels, send(): call(functools.partial(send_kernel, experts), 16, 'send', out_shape=[piec...  1.92 us
  transfers between devices with their start and end apart: 32, of which 14 were waited for; matrix products, arithmetic and copies ran while one was open for 0% of the time, Pallas kernels for 21%

profile of v12, /device:TPU:0, one launch (start us, length us, event | category | flops | bytes accessed | tf_op | source)
XLA Modules:
  0.0 84.5 jit_solution(5262456516233680950)
XLA Ops:
  0.6 1.9 %send.1 = (bf16[96,1024]{1,0:T(8,128)(2,1)S(1)}, bf16[96,1024]{1,0:T(8,128)(2,1)S(1)}, bf16[96,1024]{1,0:T(8,128)(2,1)S(1)}, bf16[96,1024]{1,0:T(8,128)(2,1)S(1)...) custom-call(s32[1]{0:T(128)} %bitcast.plane_ref, ...), custom_call_target="tpu_custom_call" | custom-call | tf_op jit(solution)/shard_map/send/pallas_call | solution.py:378
  2.6 3.0 %collective-permute-start = (bf16[96,1024]{1,0:T(8,128)(2,1)S(1)}, bf16[96,1024]{1,0:T(8,128)(2,1)S(1)}, u32[]{:S(2)}, u32[]{:S(2)}) collective-permute-start(bf16[96,1024]{1,0:T(8,128)(2,1)S(1)} %get-tuple-element.267.first_ref), channel_id=1, source_target_pairs={{0,2},{1,3},{2,0},{3,1},{4,6},{5,7},{6,4},{7,5},{8,10},{9,11},{10,... | collective-permute-start | bytes 589832 | tf_op jit(solution)/shard_map/ppermute | solution.py:271
  5.6 1.6 %collective-permute-start.1 = (bf16[96,1024]{1,0:T(8,128)(2,1)S(1)}, bf16[96,1024]{1,0:T(8,128)(2,1)S(1)}, u32[]{:S(2)}, u32[]{:S(2)}) collective-permute-start(bf16[96,1024]{1,0:T(8,128)(2,1)S(1)} %get-tuple-element.239), channel_id=1, source_target_pairs={{0,4},{1,5},{2,6},{3,7},{4,8},{5,9},{6,10},{7,11},{8,12},{9,13},{1... | collective-permute-start | bytes 589832 | tf_op jit(solution)/shard_map/ppermute | solution.py:275
  7.2 2.2 %collective-permute-start.2 = (bf16[96,1024]{1,0:T(8,128)(2,1)S(1)}, bf16[96,1024]{1,0:T(8,128)(2,1)S(1)}, u32[]{:S(2)}, u32[]{:S(2)}) collective-permute-start(bf16[96,1024]{1,0:T(8,128)(2,1)S(1)} %get-tuple-element.240), channel_id=1, source_target_pairs={{0,12},{1,13},{2,14},{3,15},{4,0},{5,1},{6,2},{7,3},{8,4},{9,5},{1... | collective-permute-start | bytes 589832 | tf_op jit(solution)/shard_map/ppermute | solution.py:275
  9.4 0.8 collective-permute-start.8
  10.7 2.9 %load.1 = (bf16[1024,1024]{1,0:T(8,128)(2,1)S(1)}, bf16[1024,1024]{1,0:T(8,128)(2,1)S(1)}, bf16[1024,1024]{1,0:T(8,128)(2,1)S(1)}) custom-call(bf16[1,1024,1024]{2,1,0:T(8,128)(2,1)} %refs_0_.2, bf16[1,1024,1024]{2,1,0:T(8,128)(2,1)} %refs_1_.3, bf16[1,1024,1024]{2,1,0:T(8,128)(2,1)} %refs_2_.1), custom_call_target="tpu_custom_call" | custom-call | tf_op jit(solution)/shard_map/load/pallas_call | solution.py:393
  13.6 1.6 %collective-permute-done.1.refs_1_ = bf16[96,1024]{1,0:T(8,128)(2,1)S(1)} collective-permute-done((bf16[96,1024]{1,0:T(8,128)(2,1)S(1)}, bf16[96,1024]{1,0:T(8,128)(2,1)S(1)}, u32[]{:S(2)}, u32[]{:S(2)}) %collective-permute-start.1) | collective-permute-done | bytes 196640 | tf_op jit(solution)/shard_map/ppermute | solution.py:275
  15.3 2.2 %collective-permute-done.2.refs_2_ = bf16[96,1024]{1,0:T(8,128)(2,1)S(1)} collective-permute-done((bf16[96,1024]{1,0:T(8,128)(2,1)S(1)}, bf16[96,1024]{1,0:T(8,128)(2,1)S(1)}, u32[]{:S(2)}, u32[]{:S(2)}) %collective-permute-start.2) | collective-permute-done | bytes 196640 | tf_op jit(solution)/shard_map/ppermute | solution.py:275
  18.1 1.7 %collective-permute-done.4.refs_0_ = bf16[192,1024]{1,0:T(8,128)(2,1)S(1)} collective-permute-done((bf16[192,1024]{1,0:T(8,128)(2,1)S(1)}, bf16[192,1024]{1,0:T(8,128)(2,1)S(1)}, u32[]{:S(2)}, u32[]{:S(2)}) %collective-permute-start.4) | collective-permute-done | bytes 393248 | tf_op jit(solution)/shard_map/ppermute | solution.py:271
  19.8 1.5 %collective-permute-start.5 = (bf16[96,1024]{1,0:T(8,128)(2,1)S(1)}, bf16[96,1024]{1,0:T(8,128)(2,1)S(1)}, u32[]{:S(2)}, u32[]{:S(2)}) collective-permute-start(bf16[96,1024]{1,0:T(8,128)(2,1)S(1)} %get-tuple-element.321.first_ref), channel_id=1, source_target_pairs={{0,2},{1,3},{2,0},{3,1},{4,6},{5,7},{6,4},{7,5},{8,10},{9,11},{10,... | collective-permute-start | bytes 589832 | tf_op jit(solution)/shard_map/ppermute | solution.py:271
  21.3 5.1 %collective-permute-start.6 = (bf16[96,1024]{1,0:T(8,128)(2,1)S(1)}, bf16[96,1024]{1,0:T(8,128)(2,1)S(1)}, u32[]{:S(2)}, u32[]{:S(2)}) collective-permute-start(bf16[96,1024]{1,0:T(8,128)(2,1)S(1)} %get-tuple-element.272), channel_id=1, source_target_pairs={{0,4},{1,5},{2,6},{3,7},{4,8},{5,9},{6,10},{7,11},{8,12},{9,13},{1... | collective-permute-start | bytes 589832 | tf_op jit(solution)/shard_map/ppermute | solution.py:275
  26.4 2.6 %ffn.4 = (bf16[1024,384]{1,0:T(8,128)(2,1)S(1)}, bf16[192,1024]{1,0:T(8,128)(2,1)S(1)}, bf16[192,1024]{1,0:T(8,128)(2,1)S(1)}) custom-call(bf16[192,1024]{1,0:T(8,128)(2,1)S(1)} %pair.9.refs_0_, bf16[192,1024]{1,0:T(8,128)(2,1)S(1)} %land_core.8.refs_1_, bf16[1024,1024]{1,0:T(8,128)(2,1)S(1)} %get-tuple-element.358.refs_2_, ...), custom_call_target="tpu_custom_call" | custom-call | tf_op jit(solution)/shard_map/ffn/pallas_call | solution.py:360
  29.0 1.7 %collective-permute-done.8.refs_1_ = bf16[96,1024]{1,0:T(8,128)(2,1)S(1)} collective-permute-done((bf16[96,1024]{1,0:T(8,128)(2,1)S(1)}, bf16[96,1024]{1,0:T(8,128)(2,1)S(1)}, u32[]{:S(2)}, u32[]{:S(2)}) %collective-permute-start.8) | collective-permute-done | bytes 196640 | tf_op jit(solution)/shard_map/ppermute | solution.py:275
  31.5 2.2 %collective-permute-done.9.refs_0_ = bf16[384,1024]{1,0:T(8,128)(2,1)S(1)} collective-permute-done((bf16[384,1024]{1,0:T(8,128)(2,1)S(1)}, bf16[384,1024]{1,0:T(8,128)(2,1)S(1)}, u32[]{:S(2)}, u32[]{:S(2)}) %collective-permute-start.9) | collective-permute-done | bytes 786464 | tf_op jit(solution)/shard_map/ppermute | solution.py:271
  34.1 1.6 %collective-permute-start.14 = (bf16[96,1024]{1,0:T(8,128)(2,1)S(1)}, bf16[96,1024]{1,0:T(8,128)(2,1)S(1)}, u32[]{:S(2)}, u32[]{:S(2)}) collective-permute-start(bf16[96,1024]{1,0:T(8,128)(2,1)S(1)} %fold.4), channel_id=1, source_target_pairs={{0,2},{1,3},{2,0},{3,1},{4,6},{5,7},{6,4},{7,5},{8,10},{9,11},{10,... | collective-permute-start | bytes 589832 | tf_op jit(solution)/shard_map/ppermute | solution.py:271
  35.7 2.6 %ffn.5 = (bf16[1024,384]{1,0:T(8,128)(2,1)S(1)}, bf16[192,1024]{1,0:T(8,128)(2,1)S(1)}, bf16[192,1024]{1,0:T(8,128)(2,1)S(1)}) custom-call(bf16[192,1024]{1,0:T(8,128)(2,1)S(1)} %pair.10.second_ref.refs_0_, bf16[192,1024]{1,0:T(8,128)(2,1)S(1)} %get-tuple-element.309.refs_1_, bf16[1024,1024]{1,0:T(8,128)(2,1)S(1)} %get-tuple-element.358.refs_2_, ...), custom_call_target="tpu_custom_call" | custom-call | tf_op jit(solution)/shard_map/ffn/pallas_call | solution.py:360
  38.4 1.6 %collective-permute-done.13.refs_1_ = bf16[192,1024]{1,0:T(8,128)(2,1)S(1)} collective-permute-done((bf16[192,1024]{1,0:T(8,128)(2,1)S(1)}, bf16[192,1024]{1,0:T(8,128)(2,1)S(1)}, u32[]{:S(2)}, u32[]{:S(2)}) %collective-permute-start.13) | collective-permute-done | bytes 393248 | tf_op jit(solution)/shard_map/ppermute | solution.py:271
  40.7 5.4 %collective-permute-start.18 = (bf16[96,1024]{1,0:T(8,128)(2,1)S(1)}, bf16[96,1024]{1,0:T(8,128)(2,1)S(1)}, u32[]{:S(2)}, u32[]{:S(2)}) collective-permute-start(bf16[96,1024]{1,0:T(8,128)(2,1)S(1)} %land.14), channel_id=1, source_target_pairs={{0,8},{1,9},{2,10},{3,11},{4,12},{5,13},{6,14},{7,15},{8,0},{9,1},... | collective-permute-start | bytes 589832 | tf_op jit(solution)/shard_map/ppermute | solution.py:275
  46.2 2.6 %ffn.6 = (bf16[1024,384]{1,0:T(8,128)(2,1)S(1)}, bf16[192,1024]{1,0:T(8,128)(2,1)S(1)}, bf16[192,1024]{1,0:T(8,128)(2,1)S(1)}) custom-call(bf16[192,1024]{1,0:T(8,128)(2,1)S(1)} %pair.12.refs_0_, bf16[192,1024]{1,0:T(8,128)(2,1)S(1)} %get-tuple-element.347.refs_1_, bf16[1024,1024]{1,0:T(8,128)(2,1)S(1)} %get-tuple-element.358.refs_2_, ...), custom_call_target="tpu_custom_call" | custom-call | tf_op jit(solution)/shard_map/ffn/pallas_call | solution.py:360
  49.3 1.3 %collective-permute-done.16.refs_1_ = bf16[192,1024]{1,0:T(8,128)(2,1)S(1)} collective-permute-done((bf16[192,1024]{1,0:T(8,128)(2,1)S(1)}, bf16[192,1024]{1,0:T(8,128)(2,1)S(1)}, u32[]{:S(2)}, u32[]{:S(2)}) %collective-permute-start.16) | collective-permute-done | bytes 393248 | tf_op jit(solution)/shard_map/ppermute | solution.py:271
  51.3 2.6 %ffn.7 = (bf16[1024,384]{1,0:T(8,128)(2,1)S(1)}, bf16[192,1024]{1,0:T(8,128)(2,1)S(1)}, bf16[192,1024]{1,0:T(8,128)(2,1)S(1)}) custom-call(bf16[192,1024]{1,0:T(8,128)(2,1)S(1)} %pair.13.refs_0_, bf16[192,1024]{1,0:T(8,128)(2,1)S(1)} %get-tuple-element.357.refs_1_, bf16[1024,1024]{1,0:T(8,128)(2,1)S(1)} %get-tuple-element.358.refs_2_, ...), custom_call_target="tpu_custom_call" | custom-call | tf_op jit(solution)/shard_map/ffn/pallas_call | solution.py:360
  54.1 1.2 %collective-permute-done.18.refs_1_ = bf16[96,1024]{1,0:T(8,128)(2,1)S(1)} collective-permute-done((bf16[96,1024]{1,0:T(8,128)(2,1)S(1)}, bf16[96,1024]{1,0:T(8,128)(2,1)S(1)}, u32[]{:S(2)}, u32[]{:S(2)}) %collective-permute-start.18) | collective-permute-done | bytes 196640 | tf_op jit(solution)/shard_map/ppermute | solution.py:275
  55.8 1.6 %collective-permute-start.22 = (bf16[96,1024]{1,0:T(8,128)(2,1)S(1)}, bf16[96,1024]{1,0:T(8,128)(2,1)S(1)}, u32[]{:S(2)}, u32[]{:S(2)}) collective-permute-start(bf16[96,1024]{1,0:T(8,128)(2,1)S(1)} %fold.7), channel_id=1, source_target_pairs={{0,2},{1,3},{2,0},{3,1},{4,6},{5,7},{6,4},{7,5},{8,10},{9,11},{10,... | collective-permute-start | bytes 589832 | tf_op jit(solution)/shard_map/ppermute | solution.py:271
  58.1 1.7 %collective-permute-done.21.refs_0_ = bf16[192,1024]{1,0:T(8,128)(2,1)S(1)} collective-permute-done((bf16[192,1024]{1,0:T(8,128)(2,1)S(1)}, bf16[192,1024]{1,0:T(8,128)(2,1)S(1)}, u32[]{:S(2)}, u32[]{:S(2)}) %collective-permute-start.21) | collective-permute-done | bytes 393248 | tf_op jit(solution)/shard_map/ppermute | solution.py:271
  59.9 1.8 %collective-permute-start.25 = (bf16[96,1024]{1,0:T(8,128)(2,1)S(1)}, bf16[96,1024]{1,0:T(8,128)(2,1)S(1)}, u32[]{:S(2)}, u32[]{:S(2)}) collective-permute-start(bf16[96,1024]{1,0:T(8,128)(2,1)S(1)} %total.6), channel_id=1, source_target_pairs={{0,4},{1,5},{2,6},{3,7},{4,8},{5,9},{6,10},{7,11},{8,12},{9,13},{1... | collective-permute-start | bytes 589832 | tf_op jit(solution)/shard_map/ppermute | solution.py:275
  62.2 0.6 collective-permute-done.22.refs_0_
  62.8 1.4 %collective-permute-done.23.refs_1_ = bf16[96,1024]{1,0:T(8,128)(2,1)S(1)} collective-permute-done((bf16[96,1024]{1,0:T(8,128)(2,1)S(1)}, bf16[96,1024]{1,0:T(8,128)(2,1)S(1)}, u32[]{:S(2)}, u32[]{:S(2)}) %collective-permute-start.23) | collective-permute-done | bytes 196640 | tf_op jit(solution)/shard_map/ppermute | solution.py:275
  64.9 4.9 %collective-permute-done.25.refs_1_ = bf16[96,1024]{1,0:T(8,128)(2,1)S(1)} collective-permute-done((bf16[96,1024]{1,0:T(8,128)(2,1)S(1)}, bf16[96,1024]{1,0:T(8,128)(2,1)S(1)}, u32[]{:S(2)}, u32[]{:S(2)}) %collective-permute-start.25) | collective-permute-done | bytes 196640 | tf_op jit(solution)/shard_map/ppermute | solution.py:275
  70.4 6.9 %collective-permute-done.27.refs_1_ = bf16[96,1024]{1,0:T(8,128)(2,1)S(1)} collective-permute-done((bf16[96,1024]{1,0:T(8,128)(2,1)S(1)}, bf16[96,1024]{1,0:T(8,128)(2,1)S(1)}, u32[]{:S(2)}, u32[]{:S(2)}) %collective-permute-start.27) | collective-permute-done | bytes 196640 | tf_op jit(solution)/shard_map/ppermute | solution.py:275
  77.4 1.9 %first_grad.1.refs_1_.first_ref = f32[1024,1024]{1,0:T(8,128)S(1)} custom-call(bf16[1024,384]{1,0:T(8,128)(2,1)S(1)} %get-tuple-element.447.refs_2_.refs_0_, bf16[1024,384]{1,0:T(8,128)(2,1)S(1)} %get-tuple-element.448.refs_2_.refs_1_, bf16[192,1024]{1,0:T(8,128)(2,1)S(1)} %pair.14.refs_2_, bf16[192,1024]{1,0:T(8,128)(2,1)S(1)} %pair.15.refs_3_, ...), custom_call_target="tpu_custom_call" | custom-call | tf_op jit(solution)/shard_map/first_grad/pallas_call | solution.py:428
  80.2 1.4 %combine.1 = bf16[128,1024]{1,0:T(8,128)(2,1)} custom-call(s32[1]{0:T(128)} %bitcast.plane_ref, bf16[128,1024]{1,0:T(8,128)(2,1)S(1)} %copy-done, s32[2,128]{1,0:T(2,128)S(1)} %bitcast.5, s32[2,128]{1,0:T(2,128)S(1)} %bitcast.7, bf16[96,1024]{1,0:T(8,128)(2,1)S(1)} %total.4.refs_0_, bf16[96,1024]{1,0:T(8,128)(2,1)S(1)} %get-tuple-element.464.refs_1_, ...), custom_call_target="tpu_custom_call" | custom-call | tf_op jit(solution)/shard_map/combine/pallas_call | solution.py:493
  81.6 2.7 %last_grad.1 = bf16[1,1024,1024]{2,1,0:T(8,128)(2,1)} custom-call(f32[1024,1024]{1,0:T(8,128)S(1)} %first_grad.1.refs_1_.first_ref, bf16[1024,384]{1,0:T(8,128)(2,1)S(1)} %get-tuple-element.468.refs_1_.refs_0_, bf16[1024,384]{1,0:T(8,128)(2,1)S(1)} %get-tuple-element.469.refs_2_.refs_1_, bf16[192,1024]{1,0:T(8,128)(2,1)S(1)} %pair.16.refs_2_, ...), custom_call_target="tpu_custom_call" | custom-call | tf_op jit(solution)/shard_map/last_grad/pallas_call | solution.py:440
  (86 shorter events, 8.6 us)
Async XLA Ops:
  2.6 11.1 %collective-permute-start = (bf16[96,1024]{1,0:T(8,128)(2,1)S(1)}, bf16[96,1024]{1,0:T(8,128)(2,1)S(1)}, u32[]{:S(2)}, u32[]{:S(2)}) collective-permute-start(bf16[96,1024]{1,0:T(8,128)(2,1)S(1)} %get-tuple-element.267.first_ref), channel_id=1, source_target_pairs={{0,2},{1,3},{2,0},{3,1},{4,6},{5,7},{6,4},{7,5},{8,10},{9,11},{10,... | collective-permute-start | bytes 589832 | tf_op jit(solution)/shard_map/ppermute | solution.py:271
  5.6 9.7 %collective-permute-start.1 = (bf16[96,1024]{1,0:T(8,128)(2,1)S(1)}, bf16[96,1024]{1,0:T(8,128)(2,1)S(1)}, u32[]{:S(2)}, u32[]{:S(2)}) collective-permute-start(bf16[96,1024]{1,0:T(8,128)(2,1)S(1)} %get-tuple-element.239), channel_id=1, source_target_pairs={{0,4},{1,5},{2,6},{3,7},{4,8},{5,9},{6,10},{7,11},{8,12},{9,13},{1... | collective-permute-start | bytes 589832 | tf_op jit(solution)/shard_map/ppermute | solution.py:275
  7.2 10.3 %collective-permute-start.2 = (bf16[96,1024]{1,0:T(8,128)(2,1)S(1)}, bf16[96,1024]{1,0:T(8,128)(2,1)S(1)}, u32[]{:S(2)}, u32[]{:S(2)}) collective-permute-start(bf16[96,1024]{1,0:T(8,128)(2,1)S(1)} %get-tuple-element.240), channel_id=1, source_target_pairs={{0,12},{1,13},{2,14},{3,15},{4,0},{5,1},{6,2},{7,3},{8,4},{9,5},{1... | collective-permute-start | bytes 589832 | tf_op jit(solution)/shard_map/ppermute | solution.py:275
  9.4 21.3 %collective-permute-start.8 = (bf16[96,1024]{1,0:T(8,128)(2,1)S(1)}, bf16[96,1024]{1,0:T(8,128)(2,1)S(1)}, u32[]{:S(2)}, u32[]{:S(2)}) collective-permute-start(bf16[96,1024]{1,0:T(8,128)(2,1)S(1)} %get-tuple-element.247), channel_id=1, source_target_pairs={{0,8},{1,9},{2,10},{3,11},{4,12},{5,13},{6,14},{7,15},{8,0},{9,1},... | collective-permute-start | bytes 589832 | tf_op jit(solution)/shard_map/ppermute | solution.py:275
  10.2 7.9 %collective-permute-start.3 = (bf16[96,1024]{1,0:T(8,128)(2,1)S(1)}, bf16[96,1024]{1,0:T(8,128)(2,1)S(1)}, u32[]{:S(2)}, u32[]{:S(2)}) collective-permute-start(bf16[96,1024]{1,0:T(8,128)(2,1)S(1)} %get-tuple-element.395.first_ref), channel_id=1, source_target_pairs={{0,2},{1,3},{2,0},{3,1},{4,6},{5,7},{6,4},{7,5},{8,10},{9,11},{10,... | collective-permute-start | bytes 589832 | tf_op jit(solution)/shard_map/ppermute | solution.py:271
  17.5 13.2 %collective-permute-start.7 = (bf16[96,1024]{1,0:T(8,128)(2,1)S(1)}, bf16[96,1024]{1,0:T(8,128)(2,1)S(1)}, u32[]{:S(2)}, u32[]{:S(2)}) collective-permute-start(bf16[96,1024]{1,0:T(8,128)(2,1)S(1)} %get-tuple-element.299.first_ref), channel_id=1, source_target_pairs={{0,2},{1,3},{2,0},{3,1},{4,6},{5,7},{6,4},{7,5},{8,10},{9,11},{10,... | collective-permute-start | bytes 589832 | tf_op jit(solution)/shard_map/ppermute | solution.py:271
  18.0 1.8 %collective-permute-start.4 = (bf16[192,1024]{1,0:T(8,128)(2,1)S(1)}, bf16[192,1024]{1,0:T(8,128)(2,1)S(1)}, u32[]{:S(2)}, u32[]{:S(2)}) collective-permute-start(bf16[192,1024]{1,0:T(8,128)(2,1)S(1)} %pair.9.refs_0_), channel_id=1, source_target_pairs={{0,1},{1,0},{2,3},{3,2},{4,5},{5,4},{6,7},{7,6},{8,9},{9,8},{10,11... | collective-permute-start | bytes 1179656 | tf_op jit(solution)/shard_map/ppermute | solution.py:271
  19.8 11.6 %collective-permute-start.5 = (bf16[96,1024]{1,0:T(8,128)(2,1)S(1)}, bf16[96,1024]{1,0:T(8,128)(2,1)S(1)}, u32[]{:S(2)}, u32[]{:S(2)}) collective-permute-start(bf16[96,1024]{1,0:T(8,128)(2,1)S(1)} %get-tuple-element.321.first_ref), channel_id=1, source_target_pairs={{0,2},{1,3},{2,0},{3,1},{4,6},{5,7},{6,4},{7,5},{8,10},{9,11},{10,... | collective-permute-start | bytes 589832 | tf_op jit(solution)/shard_map/ppermute | solution.py:271
  21.3 10.1 %collective-permute-start.6 = (bf16[96,1024]{1,0:T(8,128)(2,1)S(1)}, bf16[96,1024]{1,0:T(8,128)(2,1)S(1)}, u32[]{:S(2)}, u32[]{:S(2)}) collective-permute-start(bf16[96,1024]{1,0:T(8,128)(2,1)S(1)} %get-tuple-element.272), channel_id=1, source_target_pairs={{0,4},{1,5},{2,6},{3,7},{4,8},{5,9},{6,10},{7,11},{8,12},{9,13},{1... | collective-permute-start | bytes 589832 | tf_op jit(solution)/shard_map/ppermute | solution.py:275
  30.7 7.7 %collective-permute-start.11 = (bf16[96,1024]{1,0:T(8,128)(2,1)S(1)}, bf16[96,1024]{1,0:T(8,128)(2,1)S(1)}, u32[]{:S(2)}, u32[]{:S(2)}) collective-permute-start(bf16[96,1024]{1,0:T(8,128)(2,1)S(1)} %get-tuple-element.290), channel_id=1, source_target_pairs={{0,12},{1,13},{2,14},{3,15},{4,0},{5,1},{6,2},{7,3},{8,4},{9,5},{1... | collective-permute-start | bytes 589832 | tf_op jit(solution)/shard_map/ppermute | solution.py:275
  30.7 7.7 %collective-permute-start.10 = (bf16[96,1024]{1,0:T(8,128)(2,1)S(1)}, bf16[96,1024]{1,0:T(8,128)(2,1)S(1)}, u32[]{:S(2)}, u32[]{:S(2)}) collective-permute-start(bf16[96,1024]{1,0:T(8,128)(2,1)S(1)} %get-tuple-element.344.first_ref), channel_id=1, source_target_pairs={{0,2},{1,3},{2,0},{3,1},{4,6},{5,7},{6,4},{7,5},{8,10},{9,11},{10,... | collective-permute-start | bytes 589832 | tf_op jit(solution)/shard_map/ppermute | solution.py:271
  31.4 2.4 %collective-permute-start.9 = (bf16[384,1024]{1,0:T(8,128)(2,1)S(1)}, bf16[384,1024]{1,0:T(8,128)(2,1)S(1)}, u32[]{:S(2)}, u32[]{:S(2)}) collective-permute-start(bf16[384,1024]{1,0:T(8,128)(2,1)S(1)} %pair.11), channel_id=1, source_target_pairs={{0,1},{1,0},{2,3},{3,2},{4,5},{5,4},{6,7},{7,6},{8,9},{9,8},{10,11... | collective-permute-start | bytes 2359304 | tf_op jit(solution)/shard_map/ppermute | solution.py:271
  33.7 4.7 %collective-permute-start.12 = (bf16[192,1024]{1,0:T(8,128)(2,1)S(1)}, bf16[192,1024]{1,0:T(8,128)(2,1)S(1)}, u32[]{:S(2)}, u32[]{:S(2)}) collective-permute-start(bf16[192,1024]{1,0:T(8,128)(2,1)S(1)} %pair.12.refs_0_), channel_id=1, source_target_pairs={{0,1},{1,0},{2,3},{3,2},{4,5},{5,4},{6,7},{7,6},{8,9},{9,8},{10,11... | collective-permute-start | bytes 1179656 | tf_op jit(solution)/shard_map/ppermute | solution.py:271
  34.1 15.3 %collective-permute-start.14 = (bf16[96,1024]{1,0:T(8,128)(2,1)S(1)}, bf16[96,1024]{1,0:T(8,128)(2,1)S(1)}, u32[]{:S(2)}, u32[]{:S(2)}) collective-permute-start(bf16[96,1024]{1,0:T(8,128)(2,1)S(1)} %fold.4), channel_id=1, source_target_pairs={{0,2},{1,3},{2,0},{3,1},{4,6},{5,7},{6,4},{7,5},{8,10},{9,11},{10,... | collective-permute-start | bytes 589832 | tf_op jit(solution)/shard_map/ppermute | solution.py:271
  38.3 1.8 %collective-permute-start.13 = (bf16[192,1024]{1,0:T(8,128)(2,1)S(1)}, bf16[192,1024]{1,0:T(8,128)(2,1)S(1)}, u32[]{:S(2)}, u32[]{:S(2)}) collective-permute-start(bf16[192,1024]{1,0:T(8,128)(2,1)S(1)} %get-tuple-element.325), channel_id=1, source_target_pairs={{0,1},{1,0},{2,3},{3,2},{4,5},{5,4},{6,7},{7,6},{8,9},{9,8},{10,11... | collective-permute-start | bytes 1179656 | tf_op jit(solution)/shard_map/ppermute | solution.py:271
  40.1 14.0 %collective-permute-start.17 = (bf16[96,1024]{1,0:T(8,128)(2,1)S(1)}, bf16[96,1024]{1,0:T(8,128)(2,1)S(1)}, u32[]{:S(2)}, u32[]{:S(2)}) collective-permute-start(bf16[96,1024]{1,0:T(8,128)(2,1)S(1)} %fold.5), channel_id=1, source_target_pairs={{0,2},{1,3},{2,0},{3,1},{4,6},{5,7},{6,4},{7,5},{8,10},{9,11},{10,... | collective-permute-start | bytes 589832 | tf_op jit(solution)/shard_map/ppermute | solution.py:271
  40.7 14.6 %collective-permute-start.18 = (bf16[96,1024]{1,0:T(8,128)(2,1)S(1)}, bf16[96,1024]{1,0:T(8,128)(2,1)S(1)}, u32[]{:S(2)}, u32[]{:S(2)}) collective-permute-start(bf16[96,1024]{1,0:T(8,128)(2,1)S(1)} %land.14), channel_id=1, source_target_pairs={{0,8},{1,9},{2,10},{3,11},{4,12},{5,13},{6,14},{7,15},{8,0},{9,1},... | collective-permute-start | bytes 589832 | tf_op jit(solution)/shard_map/ppermute | solution.py:275
  46.1 3.3 %collective-permute-start.15 = (bf16[192,1024]{1,0:T(8,128)(2,1)S(1)}, bf16[192,1024]{1,0:T(8,128)(2,1)S(1)}, u32[]{:S(2)}, u32[]{:S(2)}) collective-permute-start(bf16[192,1024]{1,0:T(8,128)(2,1)S(1)} %pair.13.refs_0_), channel_id=1, source_target_pairs={{0,1},{1,0},{2,3},{3,2},{4,5},{5,4},{6,7},{7,6},{8,9},{9,8},{10,11... | collective-permute-start | bytes 1179656 | tf_op jit(solution)/shard_map/ppermute | solution.py:271
  48.8 1.9 %collective-permute-start.16 = (bf16[192,1024]{1,0:T(8,128)(2,1)S(1)}, bf16[192,1024]{1,0:T(8,128)(2,1)S(1)}, u32[]{:S(2)}, u32[]{:S(2)}) collective-permute-start(bf16[192,1024]{1,0:T(8,128)(2,1)S(1)} %get-tuple-element.350), channel_id=1, source_target_pairs={{0,1},{1,0},{2,3},{3,2},{4,5},{5,4},{6,7},{7,6},{8,9},{9,8},{10,11... | collective-permute-start | bytes 1179656 | tf_op jit(solution)/shard_map/ppermute | solution.py:271
  50.7 7.4 %collective-permute-start.20 = (bf16[96,1024]{1,0:T(8,128)(2,1)S(1)}, bf16[96,1024]{1,0:T(8,128)(2,1)S(1)}, u32[]{:S(2)}, u32[]{:S(2)}) collective-permute-start(bf16[96,1024]{1,0:T(8,128)(2,1)S(1)} %fold.6), channel_id=1, source_target_pairs={{0,2},{1,3},{2,0},{3,1},{4,6},{5,7},{6,4},{7,5},{8,10},{9,11},{10,... | collective-permute-start | bytes 589832 | tf_op jit(solution)/shard_map/ppermute | solution.py:271
  53.9 1.8 %collective-permute-start.19 = (bf16[192,1024]{1,0:T(8,128)(2,1)S(1)}, bf16[192,1024]{1,0:T(8,128)(2,1)S(1)}, u32[]{:S(2)}, u32[]{:S(2)}) collective-permute-start(bf16[192,1024]{1,0:T(8,128)(2,1)S(1)} %get-tuple-element.378), channel_id=1, source_target_pairs={{0,1},{1,0},{2,3},{3,2},{4,5},{5,4},{6,7},{7,6},{8,9},{9,8},{10,11... | collective-permute-start | bytes 1179656 | tf_op jit(solution)/shard_map/ppermute | solution.py:271
  55.8 7.0 %collective-permute-start.22 = (bf16[96,1024]{1,0:T(8,128)(2,1)S(1)}, bf16[96,1024]{1,0:T(8,128)(2,1)S(1)}, u32[]{:S(2)}, u32[]{:S(2)}) collective-permute-start(bf16[96,1024]{1,0:T(8,128)(2,1)S(1)} %fold.7), channel_id=1, source_target_pairs={{0,2},{1,3},{2,0},{3,1},{4,6},{5,7},{6,4},{7,5},{8,10},{9,11},{10,... | collective-permute-start | bytes 589832 | tf_op jit(solution)/shard_map/ppermute | solution.py:271
  57.4 6.7 %collective-permute-start.23 = (bf16[96,1024]{1,0:T(8,128)(2,1)S(1)}, bf16[96,1024]{1,0:T(8,128)(2,1)S(1)}, u32[]{:S(2)}, u32[]{:S(2)}) collective-permute-start(bf16[96,1024]{1,0:T(8,128)(2,1)S(1)} %total.5), channel_id=1, source_target_pairs={{0,12},{1,13},{2,14},{3,15},{4,0},{5,1},{6,2},{7,3},{8,4},{9,5},{1... | collective-permute-start | bytes 589832 | tf_op jit(solution)/shard_map/ppermute | solution.py:275
  58.0 1.8 %collective-permute-start.21 = (bf16[192,1024]{1,0:T(8,128)(2,1)S(1)}, bf16[192,1024]{1,0:T(8,128)(2,1)S(1)}, u32[]{:S(2)}, u32[]{:S(2)}) collective-permute-start(bf16[192,1024]{1,0:T(8,128)(2,1)S(1)} %pair.14.refs_2_), channel_id=1, source_target_pairs={{0,1},{1,0},{2,3},{3,2},{4,5},{5,4},{6,7},{7,6},{8,9},{9,8},{10,11... | collective-permute-start | bytes 1179656 | tf_op jit(solution)/shard_map/ppermute | solution.py:271
  59.9 9.9 %collective-permute-start.25 = (bf16[96,1024]{1,0:T(8,128)(2,1)S(1)}, bf16[96,1024]{1,0:T(8,128)(2,1)S(1)}, u32[]{:S(2)}, u32[]{:S(2)}) collective-permute-start(bf16[96,1024]{1,0:T(8,128)(2,1)S(1)} %total.6), channel_id=1, source_target_pairs={{0,4},{1,5},{2,6},{3,7},{4,8},{5,9},{6,10},{7,11},{8,12},{9,13},{1... | collective-permute-start | bytes 589832 | tf_op jit(solution)/shard_map/ppermute | solution.py:275
  61.7 8.1 %collective-permute-start.24 = (bf16[96,1024]{1,0:T(8,128)(2,1)S(1)}, bf16[96,1024]{1,0:T(8,128)(2,1)S(1)}, u32[]{:S(2)}, u32[]{:S(2)}) collective-permute-start(bf16[96,1024]{1,0:T(8,128)(2,1)S(1)} %get-tuple-element.442.first_ref), channel_id=1, source_target_pairs={{0,2},{1,3},{2,0},{3,1},{4,6},{5,7},{6,4},{7,5},{8,10},{9,11},{10,... | collective-permute-start | bytes 589832 | tf_op jit(solution)/shard_map/ppermute | solution.py:271
  64.2 13.0 %collective-permute-start.27 = (bf16[96,1024]{1,0:T(8,128)(2,1)S(1)}, bf16[96,1024]{1,0:T(8,128)(2,1)S(1)}, u32[]{:S(2)}, u32[]{:S(2)}) collective-permute-start(bf16[96,1024]{1,0:T(8,128)(2,1)S(1)} %total.7), channel_id=1, source_target_pairs={{0,8},{1,9},{2,10},{3,11},{4,12},{5,13},{6,14},{7,15},{8,0},{9,1},... | collective-permute-start | bytes 589832 | tf_op jit(solution)/shard_map/ppermute | solution.py:275
  64.3 13.0 %collective-permute-start.26 = (bf16[96,1024]{1,0:T(8,128)(2,1)S(1)}, bf16[96,1024]{1,0:T(8,128)(2,1)S(1)}, u32[]{:S(2)}, u32[]{:S(2)}) collective-permute-start(bf16[96,1024]{1,0:T(8,128)(2,1)S(1)} %get-tuple-element.460.first_ref), channel_id=1, source_target_pairs={{0,2},{1,3},{2,0},{3,1},{4,6},{5,7},{6,4},{7,5},{8,10},{9,11},{10,... | collective-permute-start | bytes 589832 | tf_op jit(solution)/shard_map/ppermute | solution.py:271
  69.8 9.6 %collective-permute-start.29 = (bf16[96,1024]{1,0:T(8,128)(2,1)S(1)}, bf16[96,1024]{1,0:T(8,128)(2,1)S(1)}, u32[]{:S(2)}, u32[]{:S(2)}) collective-permute-start(bf16[96,1024]{1,0:T(8,128)(2,1)S(1)} %get-tuple-element.471.first_ref), channel_id=1, source_target_pairs={{0,2},{1,3},{2,0},{3,1},{4,6},{5,7},{6,4},{7,5},{8,10},{9,11},{10,... | collective-permute-start | bytes 589832 | tf_op jit(solution)/shard_map/ppermute | solution.py:271
  70.3 7.0 %collective-permute-start.28 = (bf16[192,1024]{1,0:T(8,128)(2,1)S(1)}, bf16[192,1024]{1,0:T(8,128)(2,1)S(1)}, u32[]{:S(2)}, u32[]{:S(2)}) collective-permute-start(bf16[192,1024]{1,0:T(8,128)(2,1)S(1)} %pair.15.refs_3_), channel_id=1, source_target_pairs={{0,1},{1,0},{2,3},{3,2},{4,5},{5,4},{6,7},{7,6},{8,9},{9,8},{10,11... | collective-permute-start | bytes 1179656 | tf_op jit(solution)/shard_map/ppermute | solution.py:271
  77.3 2.0 %collective-permute-start.30 = (bf16[192,1024]{1,0:T(8,128)(2,1)S(1)}, bf16[192,1024]{1,0:T(8,128)(2,1)S(1)}, u32[]{:S(2)}, u32[]{:S(2)}) collective-permute-start(bf16[192,1024]{1,0:T(8,128)(2,1)S(1)} %pair.16.refs_2_), channel_id=1, source_target_pairs={{0,1},{1,0},{2,3},{3,2},{4,5},{5,4},{6,7},{7,6},{8,9},{9,8},{10,11... | collective-permute-start | bytes 1179656 | tf_op jit(solution)/shard_map/ppermute | solution.py:271
  79.4 2.2 %collective-permute-start.31 = (bf16[192,1024]{1,0:T(8,128)(2,1)S(1)}, bf16[192,1024]{1,0:T(8,128)(2,1)S(1)}, u32[]{:S(2)}, u32[]{:S(2)}) collective-permute-start(bf16[192,1024]{1,0:T(8,128)(2,1)S(1)} %pair.17.refs_3_), channel_id=1, source_target_pairs={{0,1},{1,0},{2,3},{3,2},{4,5},{5,4},{6,7},{7,6},{8,9},{9,8},{10,11... | collective-permute-start | bytes 1179656 | tf_op jit(solution)/shard_map/ppermute | solution.py:271
  (3 other events, 2.8 us)

commit v13 on v11

--- a/solution.py
+++ b/solution.py
@@ -10,20 +10,20 @@
 HSPLIT = 4
 GROUPS = 4
 PLAN = (
-    ("zN1 zN2 yN0 loadW0", ""),
-    ("yC0 zN3", "yN0 zN1 zN2"),
+    ("yN0 zN1 zN2 loadW0", ""),
+    ("yC0 zN3", "zN1 zN2 yN0"),
     ("cN0 yN1", "yC0 cN0"),
     ("ffnN0 yN2", "yN1 zN3"),
     ("cR0N1 yN3 zC1 zC2", "yN2 cR0N1"),
     ("ffnN1 cN2 yR0", "yN3 zC1 zC2 cN2"),
     ("cR1N3 ffnN2 yC1 zC3", "yR0 cR1N3"),
     ("cR2 ffnN3 yR1 totalR0", "yC1 zC3 cR2"),
-    ("cR3 yR2", "yR1 cR3"),
-    ("totalR1 zR1 yR3 cC0", "yR2 cC0"),
-    ("totalR2 zR2 yC2", "yR3 zR1"),
-    ("totalR3 zR3 yC3 cC1", "yC2 zR2 cC1"),
-    ("cC2 gradC0", "yC3 zR3 cC2"),
-    ("cC3", None),
+    ("", "yR1"),
+    ("yR2 totalR1 zR1 cR3", "cR3"),
+    ("yR3 yC2", "yR2 zR1"),
+    ("totalR2 zR2 yC3 cC0", "yR3 yC2 cC0"),
+    ("totalR3 zR3 cC1C2", "yC3 zR2 cC1C2"),
+    ("cC3 gradC0", "zR3 cC3"),
 )
 TILE = 256
 LINK_WORK = 10 << 30
@@ -457,8 +457,8 @@
         "total": lambda kind, g: total(g),
         "load": lambda kind, g: load(),
         "grad": lambda kind, g: first_grad(
-            [(0,), (1,)],
-            [("C", "own", (0,)), ("C", "own", (1,)), ("c", "C", 0), ("c", "C", 1)],
+            [(0,), (1,), (2,)],
+            [("C", "own", (i,)) for i in range(3)] + [("c", "C", i) for i in range(3)],
         ),
     }
     def name_of(act):
@@ -481,14 +481,11 @@
                 kernels.append(live["turned", name[1][1:]])
             if name[0] == "grad":
                 kernels.append(live["first"])
-        if lands is None:
-            break
         names = [n if n[0] == "c" else (n[0],) + n[1] for n in map(name_of, lands.split())]
         land(*names, earlier=kernels)
-    live["c", "C", 3] = flying.pop(("c", ("C", 3)))
     grad_down = last_grad(
-        [(2,), (3,)],
-        [("C", "own", (2,)), ("C", "own", (3,)), ("c", "C", 2), ("c", "C", 3)],
+        [(3,)],
+        [("C", "own", (3,)), ("c", "C", 3)],
     )
     mixed = call(
         functools.partial(combine_kernel, experts),

time: 81.3 us -> 82.9 us (1.020)
  starting transfers between devices: 25.9 us -> 27.6 us
    ppermute x9, waiting for transfers between devices: 21.6 us -> 13.5 us  [turn(): return lax.ppermute(value, 'expert', to)]
    ppermute x22 -> x21, waiting for transfers between devices: 10.3 us -> 17.8 us  [swap(): lax.ppermute(value, 'expert', [(i, i ^ mask) for i in range(devices)])]
    ppermute x9, starting transfers between devices: 11.7 us -> 13.8 us  [turn(): return lax.ppermute(value, 'expert', to)]
    pallas_call x1, Pallas kernels: 1.87 us -> 2.93 us  [first_grad(): call(functools.partial(first_grad_kernel, plan), 24, 'first_grad', out_sh...]
    ppermute x22 -> x21, starting transfers between devices: 14.3 us -> 13.8 us  [swap(): lax.ppermute(value, 'expert', [(i, i ^ mask) for i in range(devices)])]
  transfers between devices with their start and end apart: 31 -> 30, of which waited for: 15 -> 14; matrix products, arithmetic and copies ran while one was open for 0% -> 0% of each run, Pallas kernels for 22% -> 21%
where the time goes in v13:
time: 82.9 us; the launch traced here: 82.7 us
  waiting for transfers between devices  31.3 us (38%)
  starting transfers between devices  27.6 us (33%)
  Pallas kernels  22.7 us (27%)
  between operations  1.16 us (1%)
    ppermute x21, waiting for transfers between devices, swap(): lax.ppermute(value, 'expert', [(i, i ^ mask) for i in range(devices)])  17.8 us
    ppermute x21, starting transfers between devices, swap(): lax.ppermute(value, 'expert', [(i, i ^ mask) for i in range(devices)])  13.8 us
    ppermute x9, starting transfers between devices, turn(): return lax.ppermute(value, 'expert', to)  13.8 us
    ppermute x9, waiting for transfers between devices, turn(): return lax.ppermute(value, 'expert', to)  13.5 us
    pallas_call x4, Pallas kernels, ffn(): call(functools.partial(ffn_kernel, len(pieces)), 24, 'ffn', out_shape=[ja...  10.5 us
    pallas_call x1, Pallas kernels, first_grad(): call(functools.partial(first_grad_kernel, plan), 24, 'first_grad', out_sh...  2.93 us
    pallas_call x1, Pallas kernels, load(): call(load_kernel, 16, 'load', out_shape=[weight, weight, jax.ShapeDtypeSt...  2.88 us
    pallas_call x1, Pallas kernels, last_grad(): call(functools.partial(last_grad_kernel, plan), 24, 'last_grad', out_shap...  2.1 us
  transfers between devices with their start and end apart: 30, of which 14 were waited for; matrix products, arithmetic and copies ran while one was open for 0% of the time, Pallas kernels for 21%

profile of v13, /device:TPU:0, one launch (start us, length us, event | category | flops | bytes accessed | tf_op | source)
XLA Modules:
  0.0 82.7 jit_solution(14116737249275089659)
XLA Ops:
  0.6 1.9 %send.1 = (bf16[96,1024]{1,0:T(8,128)(2,1)S(1)}, bf16[96,1024]{1,0:T(8,128)(2,1)S(1)}, bf16[96,1024]{1,0:T(8,128)(2,1)S(1)}, bf16[96,1024]{1,0:T(8,128)(2,1)S(1)...) custom-call(s32[1]{0:T(128)} %bitcast.plane_ref, ...), custom_call_target="tpu_custom_call" | custom-call | tf_op jit(solution)/shard_map/send/pallas_call | solution.py:378
  2.6 3.1 %collective-permute-start = (bf16[96,1024]{1,0:T(8,128)(2,1)S(1)}, bf16[96,1024]{1,0:T(8,128)(2,1)S(1)}, u32[]{:S(2)}, u32[]{:S(2)}) collective-permute-start(bf16[96,1024]{1,0:T(8,128)(2,1)S(1)} %get-tuple-element.258), channel_id=1, source_target_pairs={{0,4},{1,5},{2,6},{3,7},{4,8},{5,9},{6,10},{7,11},{8,12},{9,13},{1... | collective-permute-start | bytes 589832 | tf_op jit(solution)/shard_map/ppermute | solution.py:275
  5.7 2.1 %collective-permute-start.1 = (bf16[96,1024]{1,0:T(8,128)(2,1)S(1)}, bf16[96,1024]{1,0:T(8,128)(2,1)S(1)}, u32[]{:S(2)}, u32[]{:S(2)}) collective-permute-start(bf16[96,1024]{1,0:T(8,128)(2,1)S(1)} %get-tuple-element.259), channel_id=1, source_target_pairs={{0,12},{1,13},{2,14},{3,15},{4,0},{5,1},{6,2},{7,3},{8,4},{9,5},{1... | collective-permute-start | bytes 589832 | tf_op jit(solution)/shard_map/ppermute | solution.py:275
  7.8 1.7 %collective-permute-start.2 = (bf16[96,1024]{1,0:T(8,128)(2,1)S(1)}, bf16[96,1024]{1,0:T(8,128)(2,1)S(1)}, u32[]{:S(2)}, u32[]{:S(2)}) collective-permute-start(bf16[96,1024]{1,0:T(8,128)(2,1)S(1)} %get-tuple-element.291.first_ref), channel_id=1, source_target_pairs={{0,2},{1,3},{2,0},{3,1},{4,6},{5,7},{6,4},{7,5},{8,10},{9,11},{10,... | collective-permute-start | bytes 589832 | tf_op jit(solution)/shard_map/ppermute | solution.py:271
  9.4 2.9 %load.1 = (bf16[1024,1024]{1,0:T(8,128)(2,1)S(1)}, bf16[1024,1024]{1,0:T(8,128)(2,1)S(1)}, bf16[1024,1024]{1,0:T(8,128)(2,1)S(1)}) custom-call(bf16[1,1024,1024]{2,1,0:T(8,128)(2,1)} %refs_0_.2, bf16[1,1024,1024]{2,1,0:T(8,128)(2,1)} %refs_1_.3, bf16[1,1024,1024]{2,1,0:T(8,128)(2,1)} %refs_2_.1), custom_call_target="tpu_custom_call" | custom-call | tf_op jit(solution)/shard_map/load/pallas_call | solution.py:393
  13.7 2.5 %collective-permute-done.1.refs_1_ = bf16[96,1024]{1,0:T(8,128)(2,1)S(1)} collective-permute-done((bf16[96,1024]{1,0:T(8,128)(2,1)S(1)}, bf16[96,1024]{1,0:T(8,128)(2,1)S(1)}, u32[]{:S(2)}, u32[]{:S(2)}) %collective-permute-start.1) | collective-permute-done | bytes 196640 | tf_op jit(solution)/shard_map/ppermute | solution.py:275
  16.2 1.5 %collective-permute-start.3 = (bf16[96,1024]{1,0:T(8,128)(2,1)S(1)}, bf16[96,1024]{1,0:T(8,128)(2,1)S(1)}, u32[]{:S(2)}, u32[]{:S(2)}) collective-permute-start(bf16[96,1024]{1,0:T(8,128)(2,1)S(1)} %get-tuple-element.323.first_ref), channel_id=1, source_target_pairs={{0,2},{1,3},{2,0},{3,1},{4,6},{5,7},{6,4},{7,5},{8,10},{9,11},{10,... | collective-permute-start | bytes 589832 | tf_op jit(solution)/shard_map/ppermute | solution.py:271
  17.9 1.5 %collective-permute-done.5.refs_0_ = bf16[96,1024]{1,0:T(8,128)(2,1)S(1)} collective-permute-done((bf16[96,1024]{1,0:T(8,128)(2,1)S(1)}, bf16[96,1024]{1,0:T(8,128)(2,1)S(1)}, u32[]{:S(2)}, u32[]{:S(2)}) %collective-permute-start.5) | collective-permute-done | bytes 196640 | tf_op jit(solution)/shard_map/ppermute | solution.py:271
  20.1 2.6 %ffn.4 = (bf16[1024,384]{1,0:T(8,128)(2,1)S(1)}, bf16[192,1024]{1,0:T(8,128)(2,1)S(1)}, bf16[192,1024]{1,0:T(8,128)(2,1)S(1)}) custom-call(bf16[192,1024]{1,0:T(8,128)(2,1)S(1)} %pair.11.refs_0_, bf16[192,1024]{1,0:T(8,128)(2,1)S(1)} %land_core.9.refs_1_, bf16[1024,1024]{1,0:T(8,128)(2,1)S(1)} %get-tuple-element.374.refs_2_, ...), custom_call_target="tpu_custom_call" | custom-call | tf_op jit(solution)/shard_map/ffn/pallas_call | solution.py:360
  22.7 2.5 %collective-permute-done.4.refs_1_ = bf16[96,1024]{1,0:T(8,128)(2,1)S(1)} collective-permute-done((bf16[96,1024]{1,0:T(8,128)(2,1)S(1)}, bf16[96,1024]{1,0:T(8,128)(2,1)S(1)}, u32[]{:S(2)}, u32[]{:S(2)}) %collective-permute-start.4) | collective-permute-done | bytes 196640 | tf_op jit(solution)/shard_map/ppermute | solution.py:275
  25.2 1.5 %collective-permute-start.7 = (bf16[96,1024]{1,0:T(8,128)(2,1)S(1)}, bf16[96,1024]{1,0:T(8,128)(2,1)S(1)}, u32[]{:S(2)}, u32[]{:S(2)}) collective-permute-start(bf16[96,1024]{1,0:T(8,128)(2,1)S(1)} %get-tuple-element.362.first_ref), channel_id=1, source_target_pairs={{0,2},{1,3},{2,0},{3,1},{4,6},{5,7},{6,4},{7,5},{8,10},{9,11},{10,... | collective-permute-start | bytes 589832 | tf_op jit(solution)/shard_map/ppermute | solution.py:271
  26.8 1.1 %collective-permute-start.8 = (bf16[96,1024]{1,0:T(8,128)(2,1)S(1)}, bf16[96,1024]{1,0:T(8,128)(2,1)S(1)}, u32[]{:S(2)}, u32[]{:S(2)}) collective-permute-start(bf16[96,1024]{1,0:T(8,128)(2,1)S(1)} %get-tuple-element.312), channel_id=1, source_target_pairs={{0,4},{1,5},{2,6},{3,7},{4,8},{5,9},{6,10},{7,11},{8,12},{9,13},{1... | collective-permute-start | bytes 589832 | tf_op jit(solution)/shard_map/ppermute | solution.py:275
  27.9 2.7 %collective-permute-start.9 = (bf16[96,1024]{1,0:T(8,128)(2,1)S(1)}, bf16[96,1024]{1,0:T(8,128)(2,1)S(1)}, u32[]{:S(2)}, u32[]{:S(2)}) collective-permute-start(bf16[96,1024]{1,0:T(8,128)(2,1)S(1)} %get-tuple-element.313), channel_id=1, source_target_pairs={{0,12},{1,13},{2,14},{3,15},{4,0},{5,1},{6,2},{7,3},{8,4},{9,5},{1... | collective-permute-start | bytes 589832 | tf_op jit(solution)/shard_map/ppermute | solution.py:275
  30.8 2.3 %collective-permute-done.11.refs_0_ = bf16[384,1024]{1,0:T(8,128)(2,1)S(1)} collective-permute-done((bf16[384,1024]{1,0:T(8,128)(2,1)S(1)}, bf16[384,1024]{1,0:T(8,128)(2,1)S(1)}, u32[]{:S(2)}, u32[]{:S(2)}) %collective-permute-start.11) | collective-permute-done | bytes 786464 | tf_op jit(solution)/shard_map/ppermute | solution.py:271
  34.0 2.6 %ffn.5 = (bf16[1024,384]{1,0:T(8,128)(2,1)S(1)}, bf16[192,1024]{1,0:T(8,128)(2,1)S(1)}, bf16[192,1024]{1,0:T(8,128)(2,1)S(1)}) custom-call(bf16[192,1024]{1,0:T(8,128)(2,1)S(1)} %pair.12.second_ref.refs_0_, bf16[192,1024]{1,0:T(8,128)(2,1)S(1)} %get-tuple-element.329.refs_1_, bf16[1024,1024]{1,0:T(8,128)(2,1)S(1)} %get-tuple-element.374.refs_2_, ...), custom_call_target="tpu_custom_call" | custom-call | tf_op jit(solution)/shard_map/ffn/pallas_call | solution.py:360
  36.6 2.4 %collective-permute-done.9.refs_2_ = bf16[96,1024]{1,0:T(8,128)(2,1)S(1)} collective-permute-done((bf16[96,1024]{1,0:T(8,128)(2,1)S(1)}, bf16[96,1024]{1,0:T(8,128)(2,1)S(1)}, u32[]{:S(2)}, u32[]{:S(2)}) %collective-permute-start.9) | collective-permute-done | bytes 196640 | tf_op jit(solution)/shard_map/ppermute | solution.py:275
  39.5 1.5 %collective-permute-start.14 = (bf16[96,1024]{1,0:T(8,128)(2,1)S(1)}, bf16[96,1024]{1,0:T(8,128)(2,1)S(1)}, u32[]{:S(2)}, u32[]{:S(2)}) collective-permute-start(bf16[96,1024]{1,0:T(8,128)(2,1)S(1)} %land.15), channel_id=1, source_target_pairs={{0,8},{1,9},{2,10},{3,11},{4,12},{5,13},{6,14},{7,15},{8,0},{9,1},... | collective-permute-start | bytes 589832 | tf_op jit(solution)/shard_map/ppermute | solution.py:275
  41.2 2.6 %ffn.6 = (bf16[1024,384]{1,0:T(8,128)(2,1)S(1)}, bf16[192,1024]{1,0:T(8,128)(2,1)S(1)}, bf16[192,1024]{1,0:T(8,128)(2,1)S(1)}) custom-call(bf16[192,1024]{1,0:T(8,128)(2,1)S(1)} %pair.14.refs_0_, bf16[192,1024]{1,0:T(8,128)(2,1)S(1)} %land_core.11.refs_1_, bf16[1024,1024]{1,0:T(8,128)(2,1)S(1)} %get-tuple-element.374.refs_2_, ...), custom_call_target="tpu_custom_call" | custom-call | tf_op jit(solution)/shard_map/ffn/pallas_call | solution.py:360
  44.6 1.6 %collective-permute-start.18 = (bf16[96,1024]{1,0:T(8,128)(2,1)S(1)}, bf16[96,1024]{1,0:T(8,128)(2,1)S(1)}, u32[]{:S(2)}, u32[]{:S(2)}) collective-permute-start(bf16[96,1024]{1,0:T(8,128)(2,1)S(1)} %fold.5), channel_id=1, source_target_pairs={{0,2},{1,3},{2,0},{3,1},{4,6},{5,7},{6,4},{7,5},{8,10},{9,11},{10,... | collective-permute-start | bytes 589832 | tf_op jit(solution)/shard_map/ppermute | solution.py:271
  46.2 2.6 %ffn.7 = (bf16[1024,384]{1,0:T(8,128)(2,1)S(1)}, bf16[192,1024]{1,0:T(8,128)(2,1)S(1)}, bf16[192,1024]{1,0:T(8,128)(2,1)S(1)}) custom-call(bf16[192,1024]{1,0:T(8,128)(2,1)S(1)} %pair.15.second_ref.refs_0_, bf16[192,1024]{1,0:T(8,128)(2,1)S(1)} %get-tuple-element.373.refs_1_, bf16[1024,1024]{1,0:T(8,128)(2,1)S(1)} %get-tuple-element.374.refs_2_, ...), custom_call_target="tpu_custom_call" | custom-call | tf_op jit(solution)/shard_map/ffn/pallas_call | solution.py:360
  48.8 2.1 %collective-permute-done.14.refs_1_ = bf16[96,1024]{1,0:T(8,128)(2,1)S(1)} collective-permute-done((bf16[96,1024]{1,0:T(8,128)(2,1)S(1)}, bf16[96,1024]{1,0:T(8,128)(2,1)S(1)}, u32[]{:S(2)}, u32[]{:S(2)}) %collective-permute-start.14) | collective-permute-done | bytes 196640 | tf_op jit(solution)/shard_map/ppermute | solution.py:275
  51.5 1.6 %collective-permute-start.20 = (bf16[96,1024]{1,0:T(8,128)(2,1)S(1)}, bf16[96,1024]{1,0:T(8,128)(2,1)S(1)}, u32[]{:S(2)}, u32[]{:S(2)}) collective-permute-start(bf16[96,1024]{1,0:T(8,128)(2,1)S(1)} %fold.6), channel_id=1, source_target_pairs={{0,2},{1,3},{2,0},{3,1},{4,6},{5,7},{6,4},{7,5},{8,10},{9,11},{10,... | collective-permute-start | bytes 589832 | tf_op jit(solution)/shard_map/ppermute | solution.py:271
  53.2 1.7 %collective-permute-start.21 = (bf16[96,1024]{1,0:T(8,128)(2,1)S(1)}, bf16[96,1024]{1,0:T(8,128)(2,1)S(1)}, u32[]{:S(2)}, u32[]{:S(2)}) collective-permute-start(bf16[96,1024]{1,0:T(8,128)(2,1)S(1)} %total.5), channel_id=1, source_target_pairs={{0,12},{1,13},{2,14},{3,15},{4,0},{5,1},{6,2},{7,3},{8,4},{9,5},{1... | collective-permute-start | bytes 589832 | tf_op jit(solution)/shard_map/ppermute | solution.py:275
  54.9 1.7 %collective-permute-done.19.refs_0_ = bf16[192,1024]{1,0:T(8,128)(2,1)S(1)} collective-permute-done((bf16[192,1024]{1,0:T(8,128)(2,1)S(1)}, bf16[192,1024]{1,0:T(8,128)(2,1)S(1)}, u32[]{:S(2)}, u32[]{:S(2)}) %collective-permute-start.19) | collective-permute-done | bytes 393248 | tf_op jit(solution)/shard_map/ppermute | solution.py:271
  57.3 1.5 %collective-permute-start.23 = (bf16[96,1024]{1,0:T(8,128)(2,1)S(1)}, bf16[96,1024]{1,0:T(8,128)(2,1)S(1)}, u32[]{:S(2)}, u32[]{:S(2)}) collective-permute-start(bf16[96,1024]{1,0:T(8,128)(2,1)S(1)} %get-tuple-element.485.first_ref), channel_id=1, source_target_pairs={{0,2},{1,3},{2,0},{3,1},{4,6},{5,7},{6,4},{7,5},{8,10},{9,11},{10,... | collective-permute-start | bytes 589832 | tf_op jit(solution)/shard_map/ppermute | solution.py:271
  60.2 4.4 %collective-permute-done.22.refs_0_ = bf16[96,1024]{1,0:T(8,128)(2,1)S(1)} collective-permute-done((bf16[96,1024]{1,0:T(8,128)(2,1)S(1)}, bf16[96,1024]{1,0:T(8,128)(2,1)S(1)}, u32[]{:S(2)}, u32[]{:S(2)}) %collective-permute-start.22) | collective-permute-done | bytes 196640 | tf_op jit(solution)/shard_map/ppermute | solution.py:271
  64.5 4.2 %collective-permute-done.23.refs_1_ = bf16[96,1024]{1,0:T(8,128)(2,1)S(1)} collective-permute-done((bf16[96,1024]{1,0:T(8,128)(2,1)S(1)}, bf16[96,1024]{1,0:T(8,128)(2,1)S(1)}, u32[]{:S(2)}, u32[]{:S(2)}) %collective-permute-start.23) | collective-permute-done | bytes 196640 | tf_op jit(solution)/shard_map/ppermute | solution.py:271
  69.2 2.9 %collective-permute-done.25.refs_0_ = bf16[96,1024]{1,0:T(8,128)(2,1)S(1)} collective-permute-done((bf16[96,1024]{1,0:T(8,128)(2,1)S(1)}, bf16[96,1024]{1,0:T(8,128)(2,1)S(1)}, u32[]{:S(2)}, u32[]{:S(2)}) %collective-permute-start.25) | collective-permute-done | bytes 196640 | tf_op jit(solution)/shard_map/ppermute | solution.py:271
  72.3 2.9 %first_grad.1.refs_1_.first_ref = f32[1024,1024]{1,0:T(8,128)S(1)} custom-call(bf16[1024,384]{1,0:T(8,128)(2,1)S(1)} %get-tuple-element.489.refs_2_.refs_0_, bf16[1024,384]{1,0:T(8,128)(2,1)S(1)} %get-tuple-element.490.refs_3_.refs_1_, bf16[1024,384]{1,0:T(8,128)(2,1)S(1)} %get-tuple-element.491.refs_1_.refs_2_, bf16[192,1024]{1,0:T(8,128)(2,1)S(1)} %pair.17.refs_3_, ...), custom_call_target="tpu_custom_call" | custom-call | tf_op jit(solution)/shard_map/first_grad/pallas_call | solution.py:428
  75.3 3.8 %collective-permute-done.28.refs_0_ = bf16[96,1024]{1,0:T(8,128)(2,1)S(1)} collective-permute-done((bf16[96,1024]{1,0:T(8,128)(2,1)S(1)}, bf16[96,1024]{1,0:T(8,128)(2,1)S(1)}, u32[]{:S(2)}, u32[]{:S(2)}) %collective-permute-start.28) | collective-permute-done | bytes 196640 | tf_op jit(solution)/shard_map/ppermute | solution.py:275
  79.1 1.4 %combine.1 = bf16[128,1024]{1,0:T(8,128)(2,1)} custom-call(s32[1]{0:T(128)} %bitcast.plane_ref, bf16[128,1024]{1,0:T(8,128)(2,1)S(1)} %copy-done, s32[2,128]{1,0:T(2,128)S(1)} %bitcast.5, s32[2,128]{1,0:T(2,128)S(1)} %bitcast.7, bf16[96,1024]{1,0:T(8,128)(2,1)S(1)} %total.4.refs_0_, bf16[96,1024]{1,0:T(8,128)(2,1)S(1)} %get-tuple-element.507.refs_1_, ...), custom_call_target="tpu_custom_call" | custom-call | tf_op jit(solution)/shard_map/combine/pallas_call | solution.py:490
  80.5 2.1 %last_grad.1 = bf16[1,1024,1024]{2,1,0:T(8,128)(2,1)} custom-call(f32[1024,1024]{1,0:T(8,128)S(1)} %first_grad.1.refs_1_.first_ref, bf16[1024,384]{1,0:T(8,128)(2,1)S(1)} %get-tuple-element.511.refs_2_.refs_0_, bf16[192,1024]{1,0:T(8,128)(2,1)S(1)} %pair.21.refs_1_, bf16[192,1024]{1,0:T(8,128)(2,1)S(1)} %land_core.17.refs_2_), custom_call_target="tpu_custom_call" | custom-call | tf_op jit(solution)/shard_map/last_grad/pallas_call | solution.py:440
  (88 shorter events, 7.8 us)
Async XLA Ops:
  2.6 11.1 %collective-permute-start = (bf16[96,1024]{1,0:T(8,128)(2,1)S(1)}, bf16[96,1024]{1,0:T(8,128)(2,1)S(1)}, u32[]{:S(2)}, u32[]{:S(2)}) collective-permute-start(bf16[96,1024]{1,0:T(8,128)(2,1)S(1)} %get-tuple-element.258), channel_id=1, source_target_pairs={{0,4},{1,5},{2,6},{3,7},{4,8},{5,9},{6,10},{7,11},{8,12},{9,13},{1... | collective-permute-start | bytes 589832 | tf_op jit(solution)/shard_map/ppermute | solution.py:275
  5.7 10.6 %collective-permute-start.1 = (bf16[96,1024]{1,0:T(8,128)(2,1)S(1)}, bf16[96,1024]{1,0:T(8,128)(2,1)S(1)}, u32[]{:S(2)}, u32[]{:S(2)}) collective-permute-start(bf16[96,1024]{1,0:T(8,128)(2,1)S(1)} %get-tuple-element.259), channel_id=1, source_target_pairs={{0,12},{1,13},{2,14},{3,15},{4,0},{5,1},{6,2},{7,3},{8,4},{9,5},{1... | collective-permute-start | bytes 589832 | tf_op jit(solution)/shard_map/ppermute | solution.py:275
  7.8 8.5 %collective-permute-start.2 = (bf16[96,1024]{1,0:T(8,128)(2,1)S(1)}, bf16[96,1024]{1,0:T(8,128)(2,1)S(1)}, u32[]{:S(2)}, u32[]{:S(2)}) collective-permute-start(bf16[96,1024]{1,0:T(8,128)(2,1)S(1)} %get-tuple-element.291.first_ref), channel_id=1, source_target_pairs={{0,2},{1,3},{2,0},{3,1},{4,6},{5,7},{6,4},{7,5},{8,10},{9,11},{10,... | collective-permute-start | bytes 589832 | tf_op jit(solution)/shard_map/ppermute | solution.py:271
  12.3 12.9 %collective-permute-start.4 = (bf16[96,1024]{1,0:T(8,128)(2,1)S(1)}, bf16[96,1024]{1,0:T(8,128)(2,1)S(1)}, u32[]{:S(2)}, u32[]{:S(2)}) collective-permute-start(bf16[96,1024]{1,0:T(8,128)(2,1)S(1)} %get-tuple-element.271), channel_id=1, source_target_pairs={{0,8},{1,9},{2,10},{3,11},{4,12},{5,13},{6,14},{7,15},{8,0},{9,1},... | collective-permute-start | bytes 589832 | tf_op jit(solution)/shard_map/ppermute | solution.py:275
  13.2 6.2 %collective-permute-start.5 = (bf16[96,1024]{1,0:T(8,128)(2,1)S(1)}, bf16[96,1024]{1,0:T(8,128)(2,1)S(1)}, u32[]{:S(2)}, u32[]{:S(2)}) collective-permute-start(bf16[96,1024]{1,0:T(8,128)(2,1)S(1)} %get-tuple-element.465.first_ref), channel_id=1, source_target_pairs={{0,2},{1,3},{2,0},{3,1},{4,6},{5,7},{6,4},{7,5},{8,10},{9,11},{10,... | collective-permute-start | bytes 589832 | tf_op jit(solution)/shard_map/ppermute | solution.py:271
  16.2 9.0 %collective-permute-start.3 = (bf16[96,1024]{1,0:T(8,128)(2,1)S(1)}, bf16[96,1024]{1,0:T(8,128)(2,1)S(1)}, u32[]{:S(2)}, u32[]{:S(2)}) collective-permute-start(bf16[96,1024]{1,0:T(8,128)(2,1)S(1)} %get-tuple-element.323.first_ref), channel_id=1, source_target_pairs={{0,2},{1,3},{2,0},{3,1},{4,6},{5,7},{6,4},{7,5},{8,10},{9,11},{10,... | collective-permute-start | bytes 589832 | tf_op jit(solution)/shard_map/ppermute | solution.py:271
  17.8 1.8 %collective-permute-start.6 = (bf16[192,1024]{1,0:T(8,128)(2,1)S(1)}, bf16[192,1024]{1,0:T(8,128)(2,1)S(1)}, u32[]{:S(2)}, u32[]{:S(2)}) collective-permute-start(bf16[192,1024]{1,0:T(8,128)(2,1)S(1)} %pair.11.refs_0_), channel_id=1, source_target_pairs={{0,1},{1,0},{2,3},{3,2},{4,5},{5,4},{6,7},{7,6},{8,9},{9,8},{10,11... | collective-permute-start | bytes 1179656 | tf_op jit(solution)/shard_map/ppermute | solution.py:271
  19.6 11.2 %collective-permute-start.10 = (bf16[96,1024]{1,0:T(8,128)(2,1)S(1)}, bf16[96,1024]{1,0:T(8,128)(2,1)S(1)}, u32[]{:S(2)}, u32[]{:S(2)}) collective-permute-start(bf16[96,1024]{1,0:T(8,128)(2,1)S(1)} %get-tuple-element.345.first_ref), channel_id=1, source_target_pairs={{0,2},{1,3},{2,0},{3,1},{4,6},{5,7},{6,4},{7,5},{8,10},{9,11},{10,... | collective-permute-start | bytes 589832 | tf_op jit(solution)/shard_map/ppermute | solution.py:271
  25.2 11.3 %collective-permute-start.7 = (bf16[96,1024]{1,0:T(8,128)(2,1)S(1)}, bf16[96,1024]{1,0:T(8,128)(2,1)S(1)}, u32[]{:S(2)}, u32[]{:S(2)}) collective-permute-start(bf16[96,1024]{1,0:T(8,128)(2,1)S(1)} %get-tuple-element.362.first_ref), channel_id=1, source_target_pairs={{0,2},{1,3},{2,0},{3,1},{4,6},{5,7},{6,4},{7,5},{8,10},{9,11},{10,... | collective-permute-start | bytes 589832 | tf_op jit(solution)/shard_map/ppermute | solution.py:271
  26.8 9.8 %collective-permute-start.8 = (bf16[96,1024]{1,0:T(8,128)(2,1)S(1)}, bf16[96,1024]{1,0:T(8,128)(2,1)S(1)}, u32[]{:S(2)}, u32[]{:S(2)}) collective-permute-start(bf16[96,1024]{1,0:T(8,128)(2,1)S(1)} %get-tuple-element.312), channel_id=1, source_target_pairs={{0,4},{1,5},{2,6},{3,7},{4,8},{5,9},{6,10},{7,11},{8,12},{9,13},{1... | collective-permute-start | bytes 589832 | tf_op jit(solution)/shard_map/ppermute | solution.py:275
  27.9 11.2 %collective-permute-start.9 = (bf16[96,1024]{1,0:T(8,128)(2,1)S(1)}, bf16[96,1024]{1,0:T(8,128)(2,1)S(1)}, u32[]{:S(2)}, u32[]{:S(2)}) collective-permute-start(bf16[96,1024]{1,0:T(8,128)(2,1)S(1)} %get-tuple-element.313), channel_id=1, source_target_pairs={{0,12},{1,13},{2,14},{3,15},{4,0},{5,1},{6,2},{7,3},{8,4},{9,5},{1... | collective-permute-start | bytes 589832 | tf_op jit(solution)/shard_map/ppermute | solution.py:275
  30.7 2.4 %collective-permute-start.11 = (bf16[384,1024]{1,0:T(8,128)(2,1)S(1)}, bf16[384,1024]{1,0:T(8,128)(2,1)S(1)}, u32[]{:S(2)}, u32[]{:S(2)}) collective-permute-start(bf16[384,1024]{1,0:T(8,128)(2,1)S(1)} %pair.13), channel_id=1, source_target_pairs={{0,1},{1,0},{2,3},{3,2},{4,5},{5,4},{6,7},{7,6},{8,9},{9,8},{10,11... | collective-permute-start | bytes 2359304 | tf_op jit(solution)/shard_map/ppermute | solution.py:271
  33.1 6.0 %collective-permute-start.12 = (bf16[192,1024]{1,0:T(8,128)(2,1)S(1)}, bf16[192,1024]{1,0:T(8,128)(2,1)S(1)}, u32[]{:S(2)}, u32[]{:S(2)}) collective-permute-start(bf16[192,1024]{1,0:T(8,128)(2,1)S(1)} %pair.14.refs_0_), channel_id=1, source_target_pairs={{0,1},{1,0},{2,3},{3,2},{4,5},{5,4},{6,7},{7,6},{8,9},{9,8},{10,11... | collective-permute-start | bytes 1179656 | tf_op jit(solution)/shard_map/ppermute | solution.py:271
  33.4 10.5 %collective-permute-start.15 = (bf16[96,1024]{1,0:T(8,128)(2,1)S(1)}, bf16[96,1024]{1,0:T(8,128)(2,1)S(1)}, u32[]{:S(2)}, u32[]{:S(2)}) collective-permute-start(bf16[96,1024]{1,0:T(8,128)(2,1)S(1)} %fold.4), channel_id=1, source_target_pairs={{0,2},{1,3},{2,0},{3,1},{4,6},{5,7},{6,4},{7,5},{8,10},{9,11},{10,... | collective-permute-start | bytes 589832 | tf_op jit(solution)/shard_map/ppermute | solution.py:271
  39.0 9.8 %collective-permute-start.13 = (bf16[96,1024]{1,0:T(8,128)(2,1)S(1)}, bf16[96,1024]{1,0:T(8,128)(2,1)S(1)}, u32[]{:S(2)}, u32[]{:S(2)}) collective-permute-start(bf16[96,1024]{1,0:T(8,128)(2,1)S(1)} %get-tuple-element.483.first_ref), channel_id=1, source_target_pairs={{0,2},{1,3},{2,0},{3,1},{4,6},{5,7},{6,4},{7,5},{8,10},{9,11},{10,... | collective-permute-start | bytes 589832 | tf_op jit(solution)/shard_map/ppermute | solution.py:271
  39.5 11.3 %collective-permute-start.14 = (bf16[96,1024]{1,0:T(8,128)(2,1)S(1)}, bf16[96,1024]{1,0:T(8,128)(2,1)S(1)}, u32[]{:S(2)}, u32[]{:S(2)}) collective-permute-start(bf16[96,1024]{1,0:T(8,128)(2,1)S(1)} %land.15), channel_id=1, source_target_pairs={{0,8},{1,9},{2,10},{3,11},{4,12},{5,13},{6,14},{7,15},{8,0},{9,1},... | collective-permute-start | bytes 589832 | tf_op jit(solution)/shard_map/ppermute | solution.py:275
  41.2 2.7 %collective-permute-start.16 = (bf16[384,1024]{1,0:T(8,128)(2,1)S(1)}, bf16[384,1024]{1,0:T(8,128)(2,1)S(1)}, u32[]{:S(2)}, u32[]{:S(2)}) collective-permute-start(bf16[384,1024]{1,0:T(8,128)(2,1)S(1)} %pair.16), channel_id=1, source_target_pairs={{0,1},{1,0},{2,3},{3,2},{4,5},{5,4},{6,7},{7,6},{8,9},{9,8},{10,11... | collective-permute-start | bytes 2359304 | tf_op jit(solution)/shard_map/ppermute | solution.py:271
  43.9 7.6 %collective-permute-start.17 = (bf16[192,1024]{1,0:T(8,128)(2,1)S(1)}, bf16[192,1024]{1,0:T(8,128)(2,1)S(1)}, u32[]{:S(2)}, u32[]{:S(2)}) collective-permute-start(bf16[192,1024]{1,0:T(8,128)(2,1)S(1)} %get-tuple-element.395), channel_id=1, source_target_pairs={{0,1},{1,0},{2,3},{3,2},{4,5},{5,4},{6,7},{7,6},{8,9},{9,8},{10,11... | collective-permute-start | bytes 1179656 | tf_op jit(solution)/shard_map/ppermute | solution.py:271
  44.6 6.9 %collective-permute-start.18 = (bf16[96,1024]{1,0:T(8,128)(2,1)S(1)}, bf16[96,1024]{1,0:T(8,128)(2,1)S(1)}, u32[]{:S(2)}, u32[]{:S(2)}) collective-permute-start(bf16[96,1024]{1,0:T(8,128)(2,1)S(1)} %fold.5), channel_id=1, source_target_pairs={{0,2},{1,3},{2,0},{3,1},{4,6},{5,7},{6,4},{7,5},{8,10},{9,11},{10,... | collective-permute-start | bytes 589832 | tf_op jit(solution)/shard_map/ppermute | solution.py:271
  51.5 7.3 %collective-permute-start.20 = (bf16[96,1024]{1,0:T(8,128)(2,1)S(1)}, bf16[96,1024]{1,0:T(8,128)(2,1)S(1)}, u32[]{:S(2)}, u32[]{:S(2)}) collective-permute-start(bf16[96,1024]{1,0:T(8,128)(2,1)S(1)} %fold.6), channel_id=1, source_target_pairs={{0,2},{1,3},{2,0},{3,1},{4,6},{5,7},{6,4},{7,5},{8,10},{9,11},{10,... | collective-permute-start | bytes 589832 | tf_op jit(solution)/shard_map/ppermute | solution.py:271
  53.2 5.8 %collective-permute-start.21 = (bf16[96,1024]{1,0:T(8,128)(2,1)S(1)}, bf16[96,1024]{1,0:T(8,128)(2,1)S(1)}, u32[]{:S(2)}, u32[]{:S(2)}) collective-permute-start(bf16[96,1024]{1,0:T(8,128)(2,1)S(1)} %total.5), channel_id=1, source_target_pairs={{0,12},{1,13},{2,14},{3,15},{4,0},{5,1},{6,2},{7,3},{8,4},{9,5},{1... | collective-permute-start | bytes 589832 | tf_op jit(solution)/shard_map/ppermute | solution.py:275
  54.9 1.7 %collective-permute-start.19 = (bf16[192,1024]{1,0:T(8,128)(2,1)S(1)}, bf16[192,1024]{1,0:T(8,128)(2,1)S(1)}, u32[]{:S(2)}, u32[]{:S(2)}) collective-permute-start(bf16[192,1024]{1,0:T(8,128)(2,1)S(1)} %get-tuple-element.431), channel_id=1, source_target_pairs={{0,1},{1,0},{2,3},{3,2},{4,5},{5,4},{6,7},{7,6},{8,9},{9,8},{10,11... | collective-permute-start | bytes 1179656 | tf_op jit(solution)/shard_map/ppermute | solution.py:271
  56.7 7.8 %collective-permute-start.22 = (bf16[96,1024]{1,0:T(8,128)(2,1)S(1)}, bf16[96,1024]{1,0:T(8,128)(2,1)S(1)}, u32[]{:S(2)}, u32[]{:S(2)}) collective-permute-start(bf16[96,1024]{1,0:T(8,128)(2,1)S(1)} %fold.7), channel_id=1, source_target_pairs={{0,2},{1,3},{2,0},{3,1},{4,6},{5,7},{6,4},{7,5},{8,10},{9,11},{10,... | collective-permute-start | bytes 589832 | tf_op jit(solution)/shard_map/ppermute | solution.py:271
  57.3 11.5 %collective-permute-start.23 = (bf16[96,1024]{1,0:T(8,128)(2,1)S(1)}, bf16[96,1024]{1,0:T(8,128)(2,1)S(1)}, u32[]{:S(2)}, u32[]{:S(2)}) collective-permute-start(bf16[96,1024]{1,0:T(8,128)(2,1)S(1)} %get-tuple-element.485.first_ref), channel_id=1, source_target_pairs={{0,2},{1,3},{2,0},{3,1},{4,6},{5,7},{6,4},{7,5},{8,10},{9,11},{10,... | collective-permute-start | bytes 589832 | tf_op jit(solution)/shard_map/ppermute | solution.py:271
  59.0 10.1 %collective-permute-start.26 = (bf16[96,1024]{1,0:T(8,128)(2,1)S(1)}, bf16[96,1024]{1,0:T(8,128)(2,1)S(1)}, u32[]{:S(2)}, u32[]{:S(2)}) collective-permute-start(bf16[96,1024]{1,0:T(8,128)(2,1)S(1)} %total.6), channel_id=1, source_target_pairs={{0,4},{1,5},{2,6},{3,7},{4,8},{5,9},{6,10},{7,11},{8,12},{9,13},{1... | collective-permute-start | bytes 589832 | tf_op jit(solution)/shard_map/ppermute | solution.py:275
  59.5 12.6 %collective-permute-start.25 = (bf16[96,1024]{1,0:T(8,128)(2,1)S(1)}, bf16[96,1024]{1,0:T(8,128)(2,1)S(1)}, u32[]{:S(2)}, u32[]{:S(2)}) collective-permute-start(bf16[96,1024]{1,0:T(8,128)(2,1)S(1)} %land.23.first_ref), channel_id=1, source_target_pairs={{0,2},{1,3},{2,0},{3,1},{4,6},{5,7},{6,4},{7,5},{8,10},{9,11},{10,... | collective-permute-start | bytes 589832 | tf_op jit(solution)/shard_map/ppermute | solution.py:271
  60.1 8.7 %collective-permute-start.24 = (bf16[192,1024]{1,0:T(8,128)(2,1)S(1)}, bf16[192,1024]{1,0:T(8,128)(2,1)S(1)}, u32[]{:S(2)}, u32[]{:S(2)}) collective-permute-start(bf16[192,1024]{1,0:T(8,128)(2,1)S(1)} %pair.17.refs_3_), channel_id=1, source_target_pairs={{0,1},{1,0},{2,3},{3,2},{4,5},{5,4},{6,7},{7,6},{8,9},{9,8},{10,11... | collective-permute-start | bytes 1179656 | tf_op jit(solution)/shard_map/ppermute | solution.py:271
  68.8 10.2 %collective-permute-start.28 = (bf16[96,1024]{1,0:T(8,128)(2,1)S(1)}, bf16[96,1024]{1,0:T(8,128)(2,1)S(1)}, u32[]{:S(2)}, u32[]{:S(2)}) collective-permute-start(bf16[96,1024]{1,0:T(8,128)(2,1)S(1)} %total.7), channel_id=1, source_target_pairs={{0,8},{1,9},{2,10},{3,11},{4,12},{5,13},{6,14},{7,15},{8,0},{9,1},... | collective-permute-start | bytes 589832 | tf_op jit(solution)/shard_map/ppermute | solution.py:275
  69.1 3.0 %collective-permute-start.27 = (bf16[384,1024]{1,0:T(8,128)(2,1)S(1)}, bf16[384,1024]{1,0:T(8,128)(2,1)S(1)}, u32[]{:S(2)}, u32[]{:S(2)}) collective-permute-start(bf16[384,1024]{1,0:T(8,128)(2,1)S(1)} %pair.20), channel_id=1, source_target_pairs={{0,1},{1,0},{2,3},{3,2},{4,5},{5,4},{6,7},{7,6},{8,9},{9,8},{10,11... | collective-permute-start | bytes 2359304 | tf_op jit(solution)/shard_map/ppermute | solution.py:271
  72.2 6.9 %collective-permute-start.29 = (bf16[192,1024]{1,0:T(8,128)(2,1)S(1)}, bf16[192,1024]{1,0:T(8,128)(2,1)S(1)}, u32[]{:S(2)}, u32[]{:S(2)}) collective-permute-start(bf16[192,1024]{1,0:T(8,128)(2,1)S(1)} %pair.21.refs_1_), channel_id=1, source_target_pairs={{0,1},{1,0},{2,3},{3,2},{4,5},{5,4},{6,7},{7,6},{8,9},{9,8},{10,11... | collective-permute-start | bytes 1179656 | tf_op jit(solution)/shard_map/ppermute | solution.py:271
  75.2 3.8 %copy-start = (bf16[128,1024]{1,0:T(8,128)(2,1)S(1)}, bf16[128,1024]{1,0:T(8,128)(2,1)}, u32[]{:S(2)}) copy-start(bf16[128,1024]{1,0:T(8,128)(2,1)} %tokens_ref.1) | copy-start | bytes 786436
  75.3 3.8 %copy-start.1 = (s32[128,2]{0,1:T(2,128)S(1)}, s32[128,2]{0,1:T(2,128)}, u32[]{:S(2)}) copy-start(s32[128,2]{0,1:T(2,128)} %param.10) | copy-start | bytes 3076
  (1 other events, 3.8 us)

commit v14 on v13

--- a/solution.py
+++ b/solution.py
@@ -20,10 +20,10 @@
     ("cR2 ffnN3 yR1 totalR0", "yC1 zC3 cR2"),
     ("", "yR1"),
     ("yR2 totalR1 zR1 cR3", "cR3"),
-    ("yR3 yC2", "yR2 zR1"),
-    ("totalR2 zR2 yC3 cC0", "yR3 yC2 cC0"),
-    ("totalR3 zR3 cC1C2", "yC3 zR2 cC1C2"),
-    ("cC3 gradC0", "zR3 cC3"),
+    ("yR3", "yR2 zR1"),
+    ("totalR2 zR2 yC2 yC3 cC0", "yR3 cC0"),
+    ("totalR3 zR3 cC1", "yC2 yC3 zR2 cC1"),
+    ("cC2C3 gradC0", "zR3 cC2C3"),
 )
 TILE = 256
 LINK_WORK = 10 << 30
@@ -297,18 +297,21 @@
         names = [n for name in names for n in flights_of(name)]
         quick = [name for name in names if name[0] == "c"]
         names = [name for name in names if name[0] != "c"]
+        if not names:
+            names, quick = quick, []
+        cores = [name for name in names + quick if name[0] == "c"]
         values = [flying.pop(name) for name in names]
         if not names:
             names, values = [("C", groups[-1][-1])], [live["C", groups[-1][-1]]]
         values = through(values, "land", LINK_WORK, earlier)
         landed = list(zip(names, values))
         if quick:
-            cores = tuple(flying.pop(name) for name in quick) + (values[0],)
-            cores = lax.optimization_barrier(cores)[: len(quick)]
-            landed += list(zip(quick, through(cores, "land_core")))
+            crossed = tuple(flying.pop(name) for name in quick) + (values[0],)
+            crossed = lax.optimization_barrier(crossed)[: len(quick)]
+            landed += list(zip(quick, through(crossed, "land_core")))
         live.update(landed)
         sync()
-        for name in quick:
+        for name in cores:
             values = [live.pop(name)]
             if len(name) > 2:
                 values = small(split_kernel, "split", [2 * height] * 2, *values)
@@ -457,8 +460,8 @@
         "total": lambda kind, g: total(g),
         "load": lambda kind, g: load(),
         "grad": lambda kind, g: first_grad(
-            [(0,), (1,), (2,)],
-            [("C", "own", (i,)) for i in range(3)] + [("c", "C", i) for i in range(3)],
+            [(0,), (1,)],
+            [("C", "own", (0,)), ("C", "own", (1,)), ("c", "C", 0), ("c", "C", 1)],
         ),
     }
     def name_of(act):
@@ -484,8 +487,8 @@
         names = [n if n[0] == "c" else (n[0],) + n[1] for n in map(name_of, lands.split())]
         land(*names, earlier=kernels)
     grad_down = last_grad(
-        [(3,)],
-        [("C", "own", (3,)), ("c", "C", 3)],
+        [(2,), (3,)],
+        [("C", "own", (2,)), ("C", "own", (3,)), ("c", "C", 2), ("c", "C", 3)],
     )
     mixed = call(
         functools.partial(combine_kernel, experts),

time: 82.9 us -> 83.4 us (level)
  waiting for transfers between devices: 31.3 us -> 27.7 us
  starting transfers between devices: 27.6 us -> 31.2 us
  local copies, waits for them, and re-layouts: 0.02 us -> 0.88 us
    ppermute x21, waiting for transfers between devices: 17.8 us -> 12.8 us  [swap(): lax.ppermute(value, 'expert', [(i, i ^ mask) for i in range(devices)])]
    ppermute x9, starting transfers between devices: 13.8 us -> 17.4 us  [turn(): return lax.ppermute(value, 'expert', to)]
    ppermute x9, waiting for transfers between devices: 13.5 us -> 14.9 us  [turn(): return lax.ppermute(value, 'expert', to)]
    pallas_call x1, Pallas kernels: 2.93 us -> 1.88 us  [first_grad(): call(functools.partial(first_grad_kernel, plan), 24, 'first_grad', out_sh...]
    unnamed x6, local copies, waits for them, and re-layouts: 0.02 us -> 0.88 us
  transfers between devices with their start and end apart: 30 -> 30, of which waited for: 14 -> 14; matrix products, arithmetic and copies ran while one was open for 0% -> 0% of each run, Pallas kernels for 21% -> 19%
where the time goes in v14:
time: 83.4 us; the launch traced here: 83.2 us
  starting transfers between devices  31.2 us (37%)
  waiting for transfers between devices  27.7 us (33%)
  Pallas kernels  22.3 us (27%)
  between operations  1.14 us (1%)
  local copies, waits for them, and re-layouts  0.88 us (1%)
    ppermute x9, starting transfers between devices, turn(): return lax.ppermute(value, 'expert', to)  17.4 us
    ppermute x9, waiting for transfers between devices, turn(): return lax.ppermute(value, 'expert', to)  14.9 us
    ppermute x21, starting transfers between devices, swap(): lax.ppermute(value, 'expert', [(i, i ^ mask) for i in range(devices)])  13.8 us
    ppermute x21, waiting for transfers between devices, swap(): lax.ppermute(value, 'expert', [(i, i ^ mask) for i in range(devices)])  12.8 us
    pallas_call x4, Pallas kernels, ffn(): call(functools.partial(ffn_kernel, len(pieces)), 24, 'ffn', out_shape=[ja...  10.5 us
    pallas_call x1, Pallas kernels, load(): call(load_kernel, 16, 'load', out_shape=[weight, weight, jax.ShapeDtypeSt...  2.88 us
    pallas_call x1, Pallas kernels, last_grad(): call(functools.partial(last_grad_kernel, plan), 24, 'last_grad', out_shap...  2.7 us
    pallas_call x1, Pallas kernels, send(): call(functools.partial(send_kernel, experts), 16, 'send', out_shape=[piec...  1.92 us
  transfers between devices with their start and end apart: 30, of which 14 were waited for; matrix products, arithmetic and copies ran while one was open for 0% of the time, Pallas kernels for 19%

profile of v14, /device:TPU:0, one launch (start us, length us, event | category | flops | bytes accessed | tf_op | source)
XLA Modules:
  0.0 83.2 jit_solution(318071902506662433)
XLA Ops:
  0.6 1.9 %send.1 = (bf16[96,1024]{1,0:T(8,128)(2,1)S(1)}, bf16[96,1024]{1,0:T(8,128)(2,1)S(1)}, bf16[96,1024]{1,0:T(8,128)(2,1)S(1)}, bf16[96,1024]{1,0:T(8,128)(2,1)S(1)...) custom-call(s32[1]{0:T(128)} %bitcast.plane_ref, ...), custom_call_target="tpu_custom_call" | custom-call | tf_op jit(solution)/shard_map/send/pallas_call | solution.py:381
  2.6 3.1 %collective-permute-start = (bf16[96,1024]{1,0:T(8,128)(2,1)S(1)}, bf16[96,1024]{1,0:T(8,128)(2,1)S(1)}, u32[]{:S(2)}, u32[]{:S(2)}) collective-permute-start(bf16[96,1024]{1,0:T(8,128)(2,1)S(1)} %get-tuple-element.258), channel_id=1, source_target_pairs={{0,4},{1,5},{2,6},{3,7},{4,8},{5,9},{6,10},{7,11},{8,12},{9,13},{1... | collective-permute-start | bytes 589832 | tf_op jit(solution)/shard_map/ppermute | solution.py:275
  5.7 2.1 %collective-permute-start.1 = (bf16[96,1024]{1,0:T(8,128)(2,1)S(1)}, bf16[96,1024]{1,0:T(8,128)(2,1)S(1)}, u32[]{:S(2)}, u32[]{:S(2)}) collective-permute-start(bf16[96,1024]{1,0:T(8,128)(2,1)S(1)} %get-tuple-element.259), channel_id=1, source_target_pairs={{0,12},{1,13},{2,14},{3,15},{4,0},{5,1},{6,2},{7,3},{8,4},{9,5},{1... | collective-permute-start | bytes 589832 | tf_op jit(solution)/shard_map/ppermute | solution.py:275
  7.8 1.7 %collective-permute-start.2 = (bf16[96,1024]{1,0:T(8,128)(2,1)S(1)}, bf16[96,1024]{1,0:T(8,128)(2,1)S(1)}, u32[]{:S(2)}, u32[]{:S(2)}) collective-permute-start(bf16[96,1024]{1,0:T(8,128)(2,1)S(1)} %get-tuple-element.291.first_ref), channel_id=1, source_target_pairs={{0,2},{1,3},{2,0},{3,1},{4,6},{5,7},{6,4},{7,5},{8,10},{9,11},{10,... | collective-permute-start | bytes 589832 | tf_op jit(solution)/shard_map/ppermute | solution.py:271
  9.4 2.9 %load.1 = (bf16[1024,1024]{1,0:T(8,128)(2,1)S(1)}, bf16[1024,1024]{1,0:T(8,128)(2,1)S(1)}, bf16[1024,1024]{1,0:T(8,128)(2,1)S(1)}) custom-call(bf16[1,1024,1024]{2,1,0:T(8,128)(2,1)} %refs_0_.2, bf16[1,1024,1024]{2,1,0:T(8,128)(2,1)} %refs_1_.3, bf16[1,1024,1024]{2,1,0:T(8,128)(2,1)} %refs_2_.1), custom_call_target="tpu_custom_call" | custom-call | tf_op jit(solution)/shard_map/load/pallas_call | solution.py:396
  13.7 2.5 %collective-permute-done.1.refs_1_ = bf16[96,1024]{1,0:T(8,128)(2,1)S(1)} collective-permute-done((bf16[96,1024]{1,0:T(8,128)(2,1)S(1)}, bf16[96,1024]{1,0:T(8,128)(2,1)S(1)}, u32[]{:S(2)}, u32[]{:S(2)}) %collective-permute-start.1) | collective-permute-done | bytes 196640 | tf_op jit(solution)/shard_map/ppermute | solution.py:275
  16.2 1.5 %collective-permute-start.3 = (bf16[96,1024]{1,0:T(8,128)(2,1)S(1)}, bf16[96,1024]{1,0:T(8,128)(2,1)S(1)}, u32[]{:S(2)}, u32[]{:S(2)}) collective-permute-start(bf16[96,1024]{1,0:T(8,128)(2,1)S(1)} %get-tuple-element.323.first_ref), channel_id=1, source_target_pairs={{0,2},{1,3},{2,0},{3,1},{4,6},{5,7},{6,4},{7,5},{8,10},{9,11},{10,... | collective-permute-start | bytes 589832 | tf_op jit(solution)/shard_map/ppermute | solution.py:271
  17.9 1.5 %collective-permute-done.5.refs_0_ = bf16[96,1024]{1,0:T(8,128)(2,1)S(1)} collective-permute-done((bf16[96,1024]{1,0:T(8,128)(2,1)S(1)}, bf16[96,1024]{1,0:T(8,128)(2,1)S(1)}, u32[]{:S(2)}, u32[]{:S(2)}) %collective-permute-start.5) | collective-permute-done | bytes 196640 | tf_op jit(solution)/shard_map/ppermute | solution.py:271
  20.1 2.6 %ffn.4 = (bf16[1024,384]{1,0:T(8,128)(2,1)S(1)}, bf16[192,1024]{1,0:T(8,128)(2,1)S(1)}, bf16[192,1024]{1,0:T(8,128)(2,1)S(1)}) custom-call(bf16[192,1024]{1,0:T(8,128)(2,1)S(1)} %pair.11.refs_0_, bf16[192,1024]{1,0:T(8,128)(2,1)S(1)} %land_core.8.refs_1_, bf16[1024,1024]{1,0:T(8,128)(2,1)S(1)} %get-tuple-element.374.refs_2_, ...), custom_call_target="tpu_custom_call" | custom-call | tf_op jit(solution)/shard_map/ffn/pallas_call | solution.py:363
  22.7 2.5 %collective-permute-done.4.refs_1_ = bf16[96,1024]{1,0:T(8,128)(2,1)S(1)} collective-permute-done((bf16[96,1024]{1,0:T(8,128)(2,1)S(1)}, bf16[96,1024]{1,0:T(8,128)(2,1)S(1)}, u32[]{:S(2)}, u32[]{:S(2)}) %collective-permute-start.4) | collective-permute-done | bytes 196640 | tf_op jit(solution)/shard_map/ppermute | solution.py:275
  25.2 1.5 %collective-permute-start.7 = (bf16[96,1024]{1,0:T(8,128)(2,1)S(1)}, bf16[96,1024]{1,0:T(8,128)(2,1)S(1)}, u32[]{:S(2)}, u32[]{:S(2)}) collective-permute-start(bf16[96,1024]{1,0:T(8,128)(2,1)S(1)} %get-tuple-element.362.first_ref), channel_id=1, source_target_pairs={{0,2},{1,3},{2,0},{3,1},{4,6},{5,7},{6,4},{7,5},{8,10},{9,11},{10,... | collective-permute-start | bytes 589832 | tf_op jit(solution)/shard_map/ppermute | solution.py:271
  26.8 1.1 %collective-permute-start.8 = (bf16[96,1024]{1,0:T(8,128)(2,1)S(1)}, bf16[96,1024]{1,0:T(8,128)(2,1)S(1)}, u32[]{:S(2)}, u32[]{:S(2)}) collective-permute-start(bf16[96,1024]{1,0:T(8,128)(2,1)S(1)} %get-tuple-element.312), channel_id=1, source_target_pairs={{0,4},{1,5},{2,6},{3,7},{4,8},{5,9},{6,10},{7,11},{8,12},{9,13},{1... | collective-permute-start | bytes 589832 | tf_op jit(solution)/shard_map/ppermute | solution.py:275
  27.9 2.7 %collective-permute-start.9 = (bf16[96,1024]{1,0:T(8,128)(2,1)S(1)}, bf16[96,1024]{1,0:T(8,128)(2,1)S(1)}, u32[]{:S(2)}, u32[]{:S(2)}) collective-permute-start(bf16[96,1024]{1,0:T(8,128)(2,1)S(1)} %get-tuple-element.313), channel_id=1, source_target_pairs={{0,12},{1,13},{2,14},{3,15},{4,0},{5,1},{6,2},{7,3},{8,4},{9,5},{1... | collective-permute-start | bytes 589832 | tf_op jit(solution)/shard_map/ppermute | solution.py:275
  30.8 2.3 %collective-permute-done.11.refs_0_ = bf16[384,1024]{1,0:T(8,128)(2,1)S(1)} collective-permute-done((bf16[384,1024]{1,0:T(8,128)(2,1)S(1)}, bf16[384,1024]{1,0:T(8,128)(2,1)S(1)}, u32[]{:S(2)}, u32[]{:S(2)}) %collective-permute-start.11) | collective-permute-done | bytes 786464 | tf_op jit(solution)/shard_map/ppermute | solution.py:271
  34.0 2.6 %ffn.5 = (bf16[1024,384]{1,0:T(8,128)(2,1)S(1)}, bf16[192,1024]{1,0:T(8,128)(2,1)S(1)}, bf16[192,1024]{1,0:T(8,128)(2,1)S(1)}) custom-call(bf16[192,1024]{1,0:T(8,128)(2,1)S(1)} %pair.12.second_ref.refs_0_, bf16[192,1024]{1,0:T(8,128)(2,1)S(1)} %get-tuple-element.329.refs_1_, bf16[1024,1024]{1,0:T(8,128)(2,1)S(1)} %get-tuple-element.374.refs_2_, ...), custom_call_target="tpu_custom_call" | custom-call | tf_op jit(solution)/shard_map/ffn/pallas_call | solution.py:363
  36.6 2.4 %collective-permute-done.9.refs_2_ = bf16[96,1024]{1,0:T(8,128)(2,1)S(1)} collective-permute-done((bf16[96,1024]{1,0:T(8,128)(2,1)S(1)}, bf16[96,1024]{1,0:T(8,128)(2,1)S(1)}, u32[]{:S(2)}, u32[]{:S(2)}) %collective-permute-start.9) | collective-permute-done | bytes 196640 | tf_op jit(solution)/shard_map/ppermute | solution.py:275
  39.5 1.5 %collective-permute-start.14 = (bf16[96,1024]{1,0:T(8,128)(2,1)S(1)}, bf16[96,1024]{1,0:T(8,128)(2,1)S(1)}, u32[]{:S(2)}, u32[]{:S(2)}) collective-permute-start(bf16[96,1024]{1,0:T(8,128)(2,1)S(1)} %land.15), channel_id=1, source_target_pairs={{0,8},{1,9},{2,10},{3,11},{4,12},{5,13},{6,14},{7,15},{8,0},{9,1},... | collective-permute-start | bytes 589832 | tf_op jit(solution)/shard_map/ppermute | solution.py:275
  41.2 2.6 %ffn.6 = (bf16[1024,384]{1,0:T(8,128)(2,1)S(1)}, bf16[192,1024]{1,0:T(8,128)(2,1)S(1)}, bf16[192,1024]{1,0:T(8,128)(2,1)S(1)}) custom-call(bf16[192,1024]{1,0:T(8,128)(2,1)S(1)} %pair.14.refs_0_, bf16[192,1024]{1,0:T(8,128)(2,1)S(1)} %land_core.10.refs_1_, bf16[1024,1024]{1,0:T(8,128)(2,1)S(1)} %get-tuple-element.374.refs_2_, ...), custom_call_target="tpu_custom_call" | custom-call | tf_op jit(solution)/shard_map/ffn/pallas_call | solution.py:363
  44.6 1.6 %collective-permute-start.18 = (bf16[96,1024]{1,0:T(8,128)(2,1)S(1)}, bf16[96,1024]{1,0:T(8,128)(2,1)S(1)}, u32[]{:S(2)}, u32[]{:S(2)}) collective-permute-start(bf16[96,1024]{1,0:T(8,128)(2,1)S(1)} %fold.5), channel_id=1, source_target_pairs={{0,2},{1,3},{2,0},{3,1},{4,6},{5,7},{6,4},{7,5},{8,10},{9,11},{10,... | collective-permute-start | bytes 589832 | tf_op jit(solution)/shard_map/ppermute | solution.py:271
  46.2 2.6 %ffn.7 = (bf16[1024,384]{1,0:T(8,128)(2,1)S(1)}, bf16[192,1024]{1,0:T(8,128)(2,1)S(1)}, bf16[192,1024]{1,0:T(8,128)(2,1)S(1)}) custom-call(bf16[192,1024]{1,0:T(8,128)(2,1)S(1)} %pair.15.second_ref.refs_0_, bf16[192,1024]{1,0:T(8,128)(2,1)S(1)} %get-tuple-element.373.refs_1_, bf16[1024,1024]{1,0:T(8,128)(2,1)S(1)} %get-tuple-element.374.refs_2_, ...), custom_call_target="tpu_custom_call" | custom-call | tf_op jit(solution)/shard_map/ffn/pallas_call | solution.py:363
  48.8 2.1 %collective-permute-done.14.refs_1_ = bf16[96,1024]{1,0:T(8,128)(2,1)S(1)} collective-permute-done((bf16[96,1024]{1,0:T(8,128)(2,1)S(1)}, bf16[96,1024]{1,0:T(8,128)(2,1)S(1)}, u32[]{:S(2)}, u32[]{:S(2)}) %collective-permute-start.14) | collective-permute-done | bytes 196640 | tf_op jit(solution)/shard_map/ppermute | solution.py:275
  51.5 1.6 %collective-permute-start.20 = (bf16[96,1024]{1,0:T(8,128)(2,1)S(1)}, bf16[96,1024]{1,0:T(8,128)(2,1)S(1)}, u32[]{:S(2)}, u32[]{:S(2)}) collective-permute-start(bf16[96,1024]{1,0:T(8,128)(2,1)S(1)} %fold.6), channel_id=1, source_target_pairs={{0,2},{1,3},{2,0},{3,1},{4,6},{5,7},{6,4},{7,5},{8,10},{9,11},{10,... | collective-permute-start | bytes 589832 | tf_op jit(solution)/shard_map/ppermute | solution.py:271
  53.2 1.7 %collective-permute-start.21 = (bf16[96,1024]{1,0:T(8,128)(2,1)S(1)}, bf16[96,1024]{1,0:T(8,128)(2,1)S(1)}, u32[]{:S(2)}, u32[]{:S(2)}) collective-permute-start(bf16[96,1024]{1,0:T(8,128)(2,1)S(1)} %total.5), channel_id=1, source_target_pairs={{0,12},{1,13},{2,14},{3,15},{4,0},{5,1},{6,2},{7,3},{8,4},{9,5},{1... | collective-permute-start | bytes 589832 | tf_op jit(solution)/shard_map/ppermute | solution.py:275
  55.6 3.8 %collective-permute-done.20.refs_0_ = bf16[96,1024]{1,0:T(8,128)(2,1)S(1)} collective-permute-done((bf16[96,1024]{1,0:T(8,128)(2,1)S(1)}, bf16[96,1024]{1,0:T(8,128)(2,1)S(1)}, u32[]{:S(2)}, u32[]{:S(2)}) %collective-permute-start.20) | collective-permute-done | bytes 196640 | tf_op jit(solution)/shard_map/ppermute | solution.py:271
  61.4 1.5 %collective-permute-start.25 = (bf16[96,1024]{1,0:T(8,128)(2,1)S(1)}, bf16[96,1024]{1,0:T(8,128)(2,1)S(1)}, u32[]{:S(2)}, u32[]{:S(2)}) collective-permute-start(bf16[96,1024]{1,0:T(8,128)(2,1)S(1)} %get-tuple-element.499.first_ref), channel_id=1, source_target_pairs={{0,2},{1,3},{2,0},{3,1},{4,6},{5,7},{6,4},{7,5},{8,10},{9,11},{10,... | collective-permute-start | bytes 589832 | tf_op jit(solution)/shard_map/ppermute | solution.py:271
  63.5 1.2 %collective-permute-done.23.refs_0_ = bf16[192,1024]{1,0:T(8,128)(2,1)S(1)} collective-permute-done((bf16[192,1024]{1,0:T(8,128)(2,1)S(1)}, bf16[192,1024]{1,0:T(8,128)(2,1)S(1)}, u32[]{:S(2)}, u32[]{:S(2)}) %collective-permute-start.23) | collective-permute-done | bytes 393248 | tf_op jit(solution)/shard_map/ppermute | solution.py:271
  64.8 3.8 %collective-permute-start.28 = (bf16[96,1024]{1,0:T(8,128)(2,1)S(1)}, bf16[96,1024]{1,0:T(8,128)(2,1)S(1)}, u32[]{:S(2)}, u32[]{:S(2)}) collective-permute-start(bf16[96,1024]{1,0:T(8,128)(2,1)S(1)} %total.7), channel_id=1, source_target_pairs={{0,8},{1,9},{2,10},{3,11},{4,12},{5,13},{6,14},{7,15},{8,0},{9,1},... | collective-permute-start | bytes 589832 | tf_op jit(solution)/shard_map/ppermute | solution.py:275
  68.7 2.8 %collective-permute-done.25.refs_1_ = bf16[96,1024]{1,0:T(8,128)(2,1)S(1)} collective-permute-done((bf16[96,1024]{1,0:T(8,128)(2,1)S(1)}, bf16[96,1024]{1,0:T(8,128)(2,1)S(1)}, u32[]{:S(2)}, u32[]{:S(2)}) %collective-permute-start.25) | collective-permute-done | bytes 196640 | tf_op jit(solution)/shard_map/ppermute | solution.py:271
  71.8 1.9 %first_grad.1.refs_1_.first_ref = f32[1024,1024]{1,0:T(8,128)S(1)} custom-call(bf16[1024,384]{1,0:T(8,128)(2,1)S(1)} %get-tuple-element.486.refs_2_.refs_0_, bf16[1024,384]{1,0:T(8,128)(2,1)S(1)} %get-tuple-element.487.refs_3_.refs_1_, bf16[192,1024]{1,0:T(8,128)(2,1)S(1)} %pair.17.refs_2_, bf16[192,1024]{1,0:T(8,128)(2,1)S(1)} %pair.18.refs_3_, ...), custom_call_target="tpu_custom_call" | custom-call | tf_op jit(solution)/shard_map/first_grad/pallas_call | solution.py:431
  73.7 4.4 %collective-permute-done.28.refs_0_ = bf16[96,1024]{1,0:T(8,128)(2,1)S(1)} collective-permute-done((bf16[96,1024]{1,0:T(8,128)(2,1)S(1)}, bf16[96,1024]{1,0:T(8,128)(2,1)S(1)}, u32[]{:S(2)}, u32[]{:S(2)}) %collective-permute-start.28) | collective-permute-done | bytes 196640 | tf_op jit(solution)/shard_map/ppermute | solution.py:275
  79.0 1.4 %combine.1 = bf16[128,1024]{1,0:T(8,128)(2,1)} custom-call(s32[1]{0:T(128)} %bitcast.plane_ref, bf16[128,1024]{1,0:T(8,128)(2,1)S(1)} %copy-done, s32[2,128]{1,0:T(2,128)S(1)} %bitcast.5, s32[2,128]{1,0:T(2,128)S(1)} %bitcast.7, bf16[96,1024]{1,0:T(8,128)(2,1)S(1)} %total.4.refs_0_, bf16[96,1024]{1,0:T(8,128)(2,1)S(1)} %get-tuple-element.503.refs_1_, ...), custom_call_target="tpu_custom_call" | custom-call | tf_op jit(solution)/shard_map/combine/pallas_call | solution.py:493
  80.4 2.7 %last_grad.1 = bf16[1,1024,1024]{2,1,0:T(8,128)(2,1)} custom-call(f32[1024,1024]{1,0:T(8,128)S(1)} %first_grad.1.refs_1_.first_ref, bf16[1024,384]{1,0:T(8,128)(2,1)S(1)} %get-tuple-element.507.refs_1_.refs_0_, bf16[1024,384]{1,0:T(8,128)(2,1)S(1)} %get-tuple-element.508.refs_2_.refs_1_, bf16[192,1024]{1,0:T(8,128)(2,1)S(1)} %pair.19.first_ref.refs_2_, ...), custom_call_target="tpu_custom_call" | custom-call | tf_op jit(solution)/shard_map/last_grad/pallas_call | solution.py:443
  (87 shorter events, 9.9 us)
Async XLA Ops:
  2.6 11.1 %collective-permute-start = (bf16[96,1024]{1,0:T(8,128)(2,1)S(1)}, bf16[96,1024]{1,0:T(8,128)(2,1)S(1)}, u32[]{:S(2)}, u32[]{:S(2)}) collective-permute-start(bf16[96,1024]{1,0:T(8,128)(2,1)S(1)} %get-tuple-element.258), channel_id=1, source_target_pairs={{0,4},{1,5},{2,6},{3,7},{4,8},{5,9},{6,10},{7,11},{8,12},{9,13},{1... | collective-permute-start | bytes 589832 | tf_op jit(solution)/shard_map/ppermute | solution.py:275
  5.7 10.6 %collective-permute-start.1 = (bf16[96,1024]{1,0:T(8,128)(2,1)S(1)}, bf16[96,1024]{1,0:T(8,128)(2,1)S(1)}, u32[]{:S(2)}, u32[]{:S(2)}) collective-permute-start(bf16[96,1024]{1,0:T(8,128)(2,1)S(1)} %get-tuple-element.259), channel_id=1, source_target_pairs={{0,12},{1,13},{2,14},{3,15},{4,0},{5,1},{6,2},{7,3},{8,4},{9,5},{1... | collective-permute-start | bytes 589832 | tf_op jit(solution)/shard_map/ppermute | solution.py:275
  7.8 8.5 %collective-permute-start.2 = (bf16[96,1024]{1,0:T(8,128)(2,1)S(1)}, bf16[96,1024]{1,0:T(8,128)(2,1)S(1)}, u32[]{:S(2)}, u32[]{:S(2)}) collective-permute-start(bf16[96,1024]{1,0:T(8,128)(2,1)S(1)} %get-tuple-element.291.first_ref), channel_id=1, source_target_pairs={{0,2},{1,3},{2,0},{3,1},{4,6},{5,7},{6,4},{7,5},{8,10},{9,11},{10,... | collective-permute-start | bytes 589832 | tf_op jit(solution)/shard_map/ppermute | solution.py:271
  12.3 12.9 %collective-permute-start.4 = (bf16[96,1024]{1,0:T(8,128)(2,1)S(1)}, bf16[96,1024]{1,0:T(8,128)(2,1)S(1)}, u32[]{:S(2)}, u32[]{:S(2)}) collective-permute-start(bf16[96,1024]{1,0:T(8,128)(2,1)S(1)} %get-tuple-element.271), channel_id=1, source_target_pairs={{0,8},{1,9},{2,10},{3,11},{4,12},{5,13},{6,14},{7,15},{8,0},{9,1},... | collective-permute-start | bytes 589832 | tf_op jit(solution)/shard_map/ppermute | solution.py:275
  13.2 6.2 %collective-permute-start.5 = (bf16[96,1024]{1,0:T(8,128)(2,1)S(1)}, bf16[96,1024]{1,0:T(8,128)(2,1)S(1)}, u32[]{:S(2)}, u32[]{:S(2)}) collective-permute-start(bf16[96,1024]{1,0:T(8,128)(2,1)S(1)} %get-tuple-element.464.first_ref), channel_id=1, source_target_pairs={{0,2},{1,3},{2,0},{3,1},{4,6},{5,7},{6,4},{7,5},{8,10},{9,11},{10,... | collective-permute-start | bytes 589832 | tf_op jit(solution)/shard_map/ppermute | solution.py:271
  16.2 9.0 %collective-permute-start.3 = (bf16[96,1024]{1,0:T(8,128)(2,1)S(1)}, bf16[96,1024]{1,0:T(8,128)(2,1)S(1)}, u32[]{:S(2)}, u32[]{:S(2)}) collective-permute-start(bf16[96,1024]{1,0:T(8,128)(2,1)S(1)} %get-tuple-element.323.first_ref), channel_id=1, source_target_pairs={{0,2},{1,3},{2,0},{3,1},{4,6},{5,7},{6,4},{7,5},{8,10},{9,11},{10,... | collective-permute-start | bytes 589832 | tf_op jit(solution)/shard_map/ppermute | solution.py:271
  17.8 1.8 %collective-permute-start.6 = (bf16[192,1024]{1,0:T(8,128)(2,1)S(1)}, bf16[192,1024]{1,0:T(8,128)(2,1)S(1)}, u32[]{:S(2)}, u32[]{:S(2)}) collective-permute-start(bf16[192,1024]{1,0:T(8,128)(2,1)S(1)} %pair.11.refs_0_), channel_id=1, source_target_pairs={{0,1},{1,0},{2,3},{3,2},{4,5},{5,4},{6,7},{7,6},{8,9},{9,8},{10,11... | collective-permute-start | bytes 1179656 | tf_op jit(solution)/shard_map/ppermute | solution.py:271
  19.6 11.2 %collective-permute-start.10 = (bf16[96,1024]{1,0:T(8,128)(2,1)S(1)}, bf16[96,1024]{1,0:T(8,128)(2,1)S(1)}, u32[]{:S(2)}, u32[]{:S(2)}) collective-permute-start(bf16[96,1024]{1,0:T(8,128)(2,1)S(1)} %get-tuple-element.345.first_ref), channel_id=1, source_target_pairs={{0,2},{1,3},{2,0},{3,1},{4,6},{5,7},{6,4},{7,5},{8,10},{9,11},{10,... | collective-permute-start | bytes 589832 | tf_op jit(solution)/shard_map/ppermute | solution.py:271
  25.2 11.3 %collective-permute-start.7 = (bf16[96,1024]{1,0:T(8,128)(2,1)S(1)}, bf16[96,1024]{1,0:T(8,128)(2,1)S(1)}, u32[]{:S(2)}, u32[]{:S(2)}) collective-permute-start(bf16[96,1024]{1,0:T(8,128)(2,1)S(1)} %get-tuple-element.362.first_ref), channel_id=1, source_target_pairs={{0,2},{1,3},{2,0},{3,1},{4,6},{5,7},{6,4},{7,5},{8,10},{9,11},{10,... | collective-permute-start | bytes 589832 | tf_op jit(solution)/shard_map/ppermute | solution.py:271
  26.8 9.8 %collective-permute-start.8 = (bf16[96,1024]{1,0:T(8,128)(2,1)S(1)}, bf16[96,1024]{1,0:T(8,128)(2,1)S(1)}, u32[]{:S(2)}, u32[]{:S(2)}) collective-permute-start(bf16[96,1024]{1,0:T(8,128)(2,1)S(1)} %get-tuple-element.312), channel_id=1, source_target_pairs={{0,4},{1,5},{2,6},{3,7},{4,8},{5,9},{6,10},{7,11},{8,12},{9,13},{1... | collective-permute-start | bytes 589832 | tf_op jit(solution)/shard_map/ppermute | solution.py:275
  27.9 11.2 %collective-permute-start.9 = (bf16[96,1024]{1,0:T(8,128)(2,1)S(1)}, bf16[96,1024]{1,0:T(8,128)(2,1)S(1)}, u32[]{:S(2)}, u32[]{:S(2)}) collective-permute-start(bf16[96,1024]{1,0:T(8,128)(2,1)S(1)} %get-tuple-element.313), channel_id=1, source_target_pairs={{0,12},{1,13},{2,14},{3,15},{4,0},{5,1},{6,2},{7,3},{8,4},{9,5},{1... | collective-permute-start | bytes 589832 | tf_op jit(solution)/shard_map/ppermute | solution.py:275
  30.7 2.4 %collective-permute-start.11 = (bf16[384,1024]{1,0:T(8,128)(2,1)S(1)}, bf16[384,1024]{1,0:T(8,128)(2,1)S(1)}, u32[]{:S(2)}, u32[]{:S(2)}) collective-permute-start(bf16[384,1024]{1,0:T(8,128)(2,1)S(1)} %pair.13), channel_id=1, source_target_pairs={{0,1},{1,0},{2,3},{3,2},{4,5},{5,4},{6,7},{7,6},{8,9},{9,8},{10,11... | collective-permute-start | bytes 2359304 | tf_op jit(solution)/shard_map/ppermute | solution.py:271
  33.1 6.0 %collective-permute-start.12 = (bf16[192,1024]{1,0:T(8,128)(2,1)S(1)}, bf16[192,1024]{1,0:T(8,128)(2,1)S(1)}, u32[]{:S(2)}, u32[]{:S(2)}) collective-permute-start(bf16[192,1024]{1,0:T(8,128)(2,1)S(1)} %pair.14.refs_0_), channel_id=1, source_target_pairs={{0,1},{1,0},{2,3},{3,2},{4,5},{5,4},{6,7},{7,6},{8,9},{9,8},{10,11... | collective-permute-start | bytes 1179656 | tf_op jit(solution)/shard_map/ppermute | solution.py:271
  33.4 10.5 %collective-permute-start.15 = (bf16[96,1024]{1,0:T(8,128)(2,1)S(1)}, bf16[96,1024]{1,0:T(8,128)(2,1)S(1)}, u32[]{:S(2)}, u32[]{:S(2)}) collective-permute-start(bf16[96,1024]{1,0:T(8,128)(2,1)S(1)} %fold.4), channel_id=1, source_target_pairs={{0,2},{1,3},{2,0},{3,1},{4,6},{5,7},{6,4},{7,5},{8,10},{9,11},{10,... | collective-permute-start | bytes 589832 | tf_op jit(solution)/shard_map/ppermute | solution.py:271
  39.0 9.8 %collective-permute-start.13 = (bf16[96,1024]{1,0:T(8,128)(2,1)S(1)}, bf16[96,1024]{1,0:T(8,128)(2,1)S(1)}, u32[]{:S(2)}, u32[]{:S(2)}) collective-permute-start(bf16[96,1024]{1,0:T(8,128)(2,1)S(1)} %get-tuple-element.481.first_ref), channel_id=1, source_target_pairs={{0,2},{1,3},{2,0},{3,1},{4,6},{5,7},{6,4},{7,5},{8,10},{9,11},{10,... | collective-permute-start | bytes 589832 | tf_op jit(solution)/shard_map/ppermute | solution.py:271
  39.5 11.3 %collective-permute-start.14 = (bf16[96,1024]{1,0:T(8,128)(2,1)S(1)}, bf16[96,1024]{1,0:T(8,128)(2,1)S(1)}, u32[]{:S(2)}, u32[]{:S(2)}) collective-permute-start(bf16[96,1024]{1,0:T(8,128)(2,1)S(1)} %land.15), channel_id=1, source_target_pairs={{0,8},{1,9},{2,10},{3,11},{4,12},{5,13},{6,14},{7,15},{8,0},{9,1},... | collective-permute-start | bytes 589832 | tf_op jit(solution)/shard_map/ppermute | solution.py:275
  41.2 2.7 %collective-permute-start.16 = (bf16[384,1024]{1,0:T(8,128)(2,1)S(1)}, bf16[384,1024]{1,0:T(8,128)(2,1)S(1)}, u32[]{:S(2)}, u32[]{:S(2)}) collective-permute-start(bf16[384,1024]{1,0:T(8,128)(2,1)S(1)} %pair.16), channel_id=1, source_target_pairs={{0,1},{1,0},{2,3},{3,2},{4,5},{5,4},{6,7},{7,6},{8,9},{9,8},{10,11... | collective-permute-start | bytes 2359304 | tf_op jit(solution)/shard_map/ppermute | solution.py:271
  43.9 7.6 %collective-permute-start.17 = (bf16[192,1024]{1,0:T(8,128)(2,1)S(1)}, bf16[192,1024]{1,0:T(8,128)(2,1)S(1)}, u32[]{:S(2)}, u32[]{:S(2)}) collective-permute-start(bf16[192,1024]{1,0:T(8,128)(2,1)S(1)} %get-tuple-element.395), channel_id=1, source_target_pairs={{0,1},{1,0},{2,3},{3,2},{4,5},{5,4},{6,7},{7,6},{8,9},{9,8},{10,11... | collective-permute-start | bytes 1179656 | tf_op jit(solution)/shard_map/ppermute | solution.py:271
  44.6 6.9 %collective-permute-start.18 = (bf16[96,1024]{1,0:T(8,128)(2,1)S(1)}, bf16[96,1024]{1,0:T(8,128)(2,1)S(1)}, u32[]{:S(2)}, u32[]{:S(2)}) collective-permute-start(bf16[96,1024]{1,0:T(8,128)(2,1)S(1)} %fold.5), channel_id=1, source_target_pairs={{0,2},{1,3},{2,0},{3,1},{4,6},{5,7},{6,4},{7,5},{8,10},{9,11},{10,... | collective-permute-start | bytes 589832 | tf_op jit(solution)/shard_map/ppermute | solution.py:271
  51.5 3.4 %collective-permute-start.19 = (bf16[192,1024]{1,0:T(8,128)(2,1)S(1)}, bf16[192,1024]{1,0:T(8,128)(2,1)S(1)}, u32[]{:S(2)}, u32[]{:S(2)}) collective-permute-start(bf16[192,1024]{1,0:T(8,128)(2,1)S(1)} %get-tuple-element.431), channel_id=1, source_target_pairs={{0,1},{1,0},{2,3},{3,2},{4,5},{5,4},{6,7},{7,6},{8,9},{9,8},{10,11... | collective-permute-start | bytes 1179656 | tf_op jit(solution)/shard_map/ppermute | solution.py:271
  51.5 7.8 %collective-permute-start.20 = (bf16[96,1024]{1,0:T(8,128)(2,1)S(1)}, bf16[96,1024]{1,0:T(8,128)(2,1)S(1)}, u32[]{:S(2)}, u32[]{:S(2)}) collective-permute-start(bf16[96,1024]{1,0:T(8,128)(2,1)S(1)} %fold.6), channel_id=1, source_target_pairs={{0,2},{1,3},{2,0},{3,1},{4,6},{5,7},{6,4},{7,5},{8,10},{9,11},{10,... | collective-permute-start | bytes 589832 | tf_op jit(solution)/shard_map/ppermute | solution.py:271
  53.2 7.1 %collective-permute-start.21 = (bf16[96,1024]{1,0:T(8,128)(2,1)S(1)}, bf16[96,1024]{1,0:T(8,128)(2,1)S(1)}, u32[]{:S(2)}, u32[]{:S(2)}) collective-permute-start(bf16[96,1024]{1,0:T(8,128)(2,1)S(1)} %total.5), channel_id=1, source_target_pairs={{0,12},{1,13},{2,14},{3,15},{4,0},{5,1},{6,2},{7,3},{8,4},{9,5},{1... | collective-permute-start | bytes 589832 | tf_op jit(solution)/shard_map/ppermute | solution.py:275
  55.0 8.5 %collective-permute-start.22 = (bf16[96,1024]{1,0:T(8,128)(2,1)S(1)}, bf16[96,1024]{1,0:T(8,128)(2,1)S(1)}, u32[]{:S(2)}, u32[]{:S(2)}) collective-permute-start(bf16[96,1024]{1,0:T(8,128)(2,1)S(1)} %fold.7), channel_id=1, source_target_pairs={{0,2},{1,3},{2,0},{3,1},{4,6},{5,7},{6,4},{7,5},{8,10},{9,11},{10,... | collective-permute-start | bytes 589832 | tf_op jit(solution)/shard_map/ppermute | solution.py:271
  60.4 8.4 %collective-permute-start.26 = (bf16[96,1024]{1,0:T(8,128)(2,1)S(1)}, bf16[96,1024]{1,0:T(8,128)(2,1)S(1)}, u32[]{:S(2)}, u32[]{:S(2)}) collective-permute-start(bf16[96,1024]{1,0:T(8,128)(2,1)S(1)} %total.6), channel_id=1, source_target_pairs={{0,4},{1,5},{2,6},{3,7},{4,8},{5,9},{6,10},{7,11},{8,12},{9,13},{1... | collective-permute-start | bytes 589832 | tf_op jit(solution)/shard_map/ppermute | solution.py:275
  60.9 7.9 %collective-permute-start.24 = (bf16[96,1024]{1,0:T(8,128)(2,1)S(1)}, bf16[96,1024]{1,0:T(8,128)(2,1)S(1)}, u32[]{:S(2)}, u32[]{:S(2)}) collective-permute-start(bf16[96,1024]{1,0:T(8,128)(2,1)S(1)} %get-tuple-element.497.first_ref), channel_id=1, source_target_pairs={{0,2},{1,3},{2,0},{3,1},{4,6},{5,7},{6,4},{7,5},{8,10},{9,11},{10,... | collective-permute-start | bytes 589832 | tf_op jit(solution)/shard_map/ppermute | solution.py:271
  61.4 10.1 %collective-permute-start.25 = (bf16[96,1024]{1,0:T(8,128)(2,1)S(1)}, bf16[96,1024]{1,0:T(8,128)(2,1)S(1)}, u32[]{:S(2)}, u32[]{:S(2)}) collective-permute-start(bf16[96,1024]{1,0:T(8,128)(2,1)S(1)} %get-tuple-element.499.first_ref), channel_id=1, source_target_pairs={{0,2},{1,3},{2,0},{3,1},{4,6},{5,7},{6,4},{7,5},{8,10},{9,11},{10,... | collective-permute-start | bytes 589832 | tf_op jit(solution)/shard_map/ppermute | solution.py:271
  62.9 1.8 %collective-permute-start.23 = (bf16[192,1024]{1,0:T(8,128)(2,1)S(1)}, bf16[192,1024]{1,0:T(8,128)(2,1)S(1)}, u32[]{:S(2)}, u32[]{:S(2)}) collective-permute-start(bf16[192,1024]{1,0:T(8,128)(2,1)S(1)} %pair.17.refs_2_), channel_id=1, source_target_pairs={{0,1},{1,0},{2,3},{3,2},{4,5},{5,4},{6,7},{7,6},{8,9},{9,8},{10,11... | collective-permute-start | bytes 1179656 | tf_op jit(solution)/shard_map/ppermute | solution.py:271
  64.8 13.2 %collective-permute-start.28 = (bf16[96,1024]{1,0:T(8,128)(2,1)S(1)}, bf16[96,1024]{1,0:T(8,128)(2,1)S(1)}, u32[]{:S(2)}, u32[]{:S(2)}) collective-permute-start(bf16[96,1024]{1,0:T(8,128)(2,1)S(1)} %total.7), channel_id=1, source_target_pairs={{0,8},{1,9},{2,10},{3,11},{4,12},{5,13},{6,14},{7,15},{8,0},{9,1},... | collective-permute-start | bytes 589832 | tf_op jit(solution)/shard_map/ppermute | solution.py:275
  68.6 2.9 %collective-permute-start.27 = (bf16[192,1024]{1,0:T(8,128)(2,1)S(1)}, bf16[192,1024]{1,0:T(8,128)(2,1)S(1)}, u32[]{:S(2)}, u32[]{:S(2)}) collective-permute-start(bf16[192,1024]{1,0:T(8,128)(2,1)S(1)} %pair.18.refs_3_), channel_id=1, source_target_pairs={{0,1},{1,0},{2,3},{3,2},{4,5},{5,4},{6,7},{7,6},{8,9},{9,8},{10,11... | collective-permute-start | bytes 1179656 | tf_op jit(solution)/shard_map/ppermute | solution.py:271
  71.7 6.4 %collective-permute-start.29 = (bf16[384,1024]{1,0:T(8,128)(2,1)S(1)}, bf16[384,1024]{1,0:T(8,128)(2,1)S(1)}, u32[]{:S(2)}, u32[]{:S(2)}) collective-permute-start(bf16[384,1024]{1,0:T(8,128)(2,1)S(1)} %pair.21), channel_id=1, source_target_pairs={{0,1},{1,0},{2,3},{3,2},{4,5},{5,4},{6,7},{7,6},{8,9},{9,8},{10,11... | collective-permute-start | bytes 2359304 | tf_op jit(solution)/shard_map/ppermute | solution.py:271
  78.0 1.0 %copy-start.1 = (s32[128,2]{0,1:T(2,128)S(1)}, s32[128,2]{0,1:T(2,128)}, u32[]{:S(2)}) copy-start(s32[128,2]{0,1:T(2,128)} %param.10) | copy-start | bytes 3076
  78.0 1.0 %copy-start.2 = (s32[128,2]{0,1:T(2,128)S(1)}, s32[128,2]{0,1:T(2,128)}, u32[]{:S(2)}) copy-start(s32[128,2]{0,1:T(2,128)} %param.11) | copy-start | bytes 3076
  (1 other events, 1.0 us)

commit v15 on v13

--- a/solution.py
+++ b/solution.py
@@ -16,12 +16,11 @@
     ("ffnN0 yN2", "yN1 zN3"),
     ("cR0N1 yN3 zC1 zC2", "yN2 cR0N1"),
     ("ffnN1 cN2 yR0", "yN3 zC1 zC2 cN2"),
-    ("cR1N3 ffnN2 yC1 zC3", "yR0 cR1N3"),
-    ("cR2 ffnN3 yR1 totalR0", "yC1 zC3 cR2"),
-    ("", "yR1"),
-    ("yR2 totalR1 zR1 cR3", "cR3"),
-    ("yR3 yC2", "yR2 zR1"),
-    ("totalR2 zR2 yC3 cC0", "yR3 yC2 cC0"),
+    ("cR1N3 ffnN2 yC1C2 zC3", "yR0 cR1N3"),
+    ("cR2 ffnN3 cR3 yR1 totalR0", "yC1C2 zC3 cR2"),
+    ("", "yR1 cR3"),
+    ("yR2 yR3 totalR1 zR1", "yR2 zR1"),
+    ("totalR2 zR2 yC3 cC0", "yR3 cC0"),
     ("totalR3 zR3 cC1C2", "yC3 zR2 cC1C2"),
     ("cC3 gradC0", "zR3 cC3"),
 )
@@ -297,42 +296,51 @@
         names = [n for name in names for n in flights_of(name)]
         quick = [name for name in names if name[0] == "c"]
         names = [name for name in names if name[0] != "c"]
+        if not names:
+            names, quick = quick, []
+        joined = [name for name in names + quick if name[0] in "cy"]
         values = [flying.pop(name) for name in names]
         if not names:
             names, values = [("C", groups[-1][-1])], [live["C", groups[-1][-1]]]
         values = through(values, "land", LINK_WORK, earlier)
         landed = list(zip(names, values))
         if quick:
-            cores = tuple(flying.pop(name) for name in quick) + (values[0],)
-            cores = lax.optimization_barrier(cores)[: len(quick)]
-            landed += list(zip(quick, through(cores, "land_core")))
+            crossed = tuple(flying.pop(name) for name in quick) + (values[0],)
+            crossed = lax.optimization_barrier(crossed)[: len(quick)]
+            landed += list(zip(quick, through(crossed, "land_core")))
         live.update(landed)
         sync()
-        for name in quick:
+        for name in joined:
             values = [live.pop(name)]
             if len(name) > 2:
-                values = small(split_kernel, "split", [2 * height] * 2, *values)
-            live.update({("c",) + item: value for item, value in zip(name[1:], values)})
+                values = small(split_kernel, "split", [values[0].shape[0] // 2] * 2, *values)
+            live.update({(name[0],) + item: value for item, value in zip(name[1:], values)})
 
     def flights_of(name):
-        if name[0] == "c":
+        if name[0] != "z":
             return [name]
-        axis, kind, g = name
-        return [(kind, s) for s in groups[g] if s] if axis == "z" else [name]
+        kind, g = name[1]
+        return [(kind, s) for s in groups[g] if s]
 
     def z(kind, g):
         for s in groups[g]:
             if s:
                 flying[kind, s] = turn(live[kind, s], -s if kind == "R" else s)
 
-    def y(kind, g):
+    def y(*items):
+        values = [to_row(*item) for item in items]
+        if len(values) > 1:
+            values = small(pair_kernel, "pair", [2 * height], *values)
+        flying[("y",) + items] = swap(values[0], 2)
+
+    def to_row(kind, g):
         if kind == "R":
             keep, crossed = live["keep", (g,)], live["c", "R", g]
             (value,) = small(fold_kernel, "fold", [height], keep, crossed)
         else:
             value = join([live.pop((kind, s)) for s in groups[g]])
             live["sent", kind, g] = value
-        flying["y", kind, g] = swap(value, 2)
+        return value
 
     def c(*items):
         values = []
@@ -470,19 +478,18 @@
     if shifts > 1:
         z("N", 0)
         z("C", 0)
-        land(("z", "N", 0), ("z", "C", 0))
+        land(("z", ("N", 0)), ("z", ("C", 0)))
     sync()
     for starts, lands in PLAN:
         kernels = []
         for act in starts.split():
             name = name_of(act)
-            steps[name[0]](*(name[1:] if name[0] == "c" else name[1]))
+            steps[name[0]](*(name[1:] if name[0] in ("c", "y") else name[1]))
             if name[0] == "ffn":
                 kernels.append(live["turned", name[1][1:]])
             if name[0] == "grad":
                 kernels.append(live["first"])
-        names = [n if n[0] == "c" else (n[0],) + n[1] for n in map(name_of, lands.split())]
-        land(*names, earlier=kernels)
+        land(*map(name_of, lands.split()), earlier=kernels)
     grad_down = last_grad(
         [(3,)],
         [("C", "own", (3,)), ("c", "C", 3)],

time: 82.9 us -> 84.3 us (1.017)
  starting transfers between devices: 27.6 us -> 33.2 us
  waiting for transfers between devices: 31.3 us -> 27 us
    ppermute x9, starting transfers between devices: 13.8 us -> 19.5 us  [turn(): return lax.ppermute(value, 'expert', to)]
    ppermute x21 -> x20, waiting for transfers between devices: 17.8 us -> 12.9 us  [swap(): lax.ppermute(value, 'expert', [(i, i ^ mask) for i in range(devices)])]
    ppermute x21 -> x20, starting transfers between devices: 13.8 us -> 13.6 us  [swap(): lax.ppermute(value, 'expert', [(i, i ^ mask) for i in range(devices)])]
  transfers between devices with their start and end apart: 30 -> 29, of which waited for: 14 -> 15; matrix products, arithmetic and copies ran while one was open for 0% -> 0% of each run, Pallas kernels for 21% -> 21%
where the time goes in v15:
time: 84.3 us; the launch traced here: 84.1 us
  starting transfers between devices  33.2 us (39%)
  waiting for transfers between devices  27 us (32%)
  Pallas kernels  22.8 us (27%)
  between operations  1.19 us (1%)
    ppermute x9, starting transfers between devices, turn(): return lax.ppermute(value, 'expert', to)  19.5 us
    ppermute x9, waiting for transfers between devices, turn(): return lax.ppermute(value, 'expert', to)  14.1 us
    ppermute x20, starting transfers between devices, swap(): lax.ppermute(value, 'expert', [(i, i ^ mask) for i in range(devices)])  13.6 us
    ppermute x20, waiting for transfers between devices, swap(): lax.ppermute(value, 'expert', [(i, i ^ mask) for i in range(devices)])  12.9 us
    pallas_call x4, Pallas kernels, ffn(): call(functools.partial(ffn_kernel, len(pieces)), 24, 'ffn', out_shape=[ja...  10.5 us
    pallas_call x1, Pallas kernels, first_grad(): call(functools.partial(first_grad_kernel, plan), 24, 'first_grad', out_sh...  2.94 us
    pallas_call x1, Pallas kernels, load(): call(load_kernel, 16, 'load', out_shape=[weight, weight, jax.ShapeDtypeSt...  2.88 us
    pallas_call x1, Pallas kernels, last_grad(): call(functools.partial(last_grad_kernel, plan), 24, 'last_grad', out_shap...  2.1 us
  transfers between devices with their start and end apart: 29, of which 15 were waited for; matrix products, arithmetic and copies ran while one was open for 0% of the time, Pallas kernels for 21%

profile of v15, /device:TPU:0, one launch (start us, length us, event | category | flops | bytes accessed | tf_op | source)
XLA Modules:
  0.0 84.1 jit_solution(13994939140580476022)
XLA Ops:
  0.6 1.9 %send.1 = (bf16[96,1024]{1,0:T(8,128)(2,1)S(1)}, bf16[96,1024]{1,0:T(8,128)(2,1)S(1)}, bf16[96,1024]{1,0:T(8,128)(2,1)S(1)}, bf16[96,1024]{1,0:T(8,128)(2,1)S(1)...) custom-call(s32[1]{0:T(128)} %bitcast.plane_ref, ...), custom_call_target="tpu_custom_call" | custom-call | tf_op jit(solution)/shard_map/send/pallas_call | solution.py:386
  2.6 3.1 %collective-permute-start = (bf16[96,1024]{1,0:T(8,128)(2,1)S(1)}, bf16[96,1024]{1,0:T(8,128)(2,1)S(1)}, u32[]{:S(2)}, u32[]{:S(2)}) collective-permute-start(bf16[96,1024]{1,0:T(8,128)(2,1)S(1)} %get-tuple-element.244), channel_id=1, source_target_pairs={{0,4},{1,5},{2,6},{3,7},{4,8},{5,9},{6,10},{7,11},{8,12},{9,13},{1... | collective-permute-start | bytes 589832 | tf_op jit(solution)/shard_map/ppermute | solution.py:274
  5.7 2.1 %collective-permute-start.1 = (bf16[96,1024]{1,0:T(8,128)(2,1)S(1)}, bf16[96,1024]{1,0:T(8,128)(2,1)S(1)}, u32[]{:S(2)}, u32[]{:S(2)}) collective-permute-start(bf16[96,1024]{1,0:T(8,128)(2,1)S(1)} %get-tuple-element.245), channel_id=1, source_target_pairs={{0,12},{1,13},{2,14},{3,15},{4,0},{5,1},{6,2},{7,3},{8,4},{9,5},{1... | collective-permute-start | bytes 589832 | tf_op jit(solution)/shard_map/ppermute | solution.py:274
  7.8 1.7 %collective-permute-start.2 = (bf16[96,1024]{1,0:T(8,128)(2,1)S(1)}, bf16[96,1024]{1,0:T(8,128)(2,1)S(1)}, u32[]{:S(2)}, u32[]{:S(2)}) collective-permute-start(bf16[96,1024]{1,0:T(8,128)(2,1)S(1)} %get-tuple-element.277.first_ref), channel_id=1, source_target_pairs={{0,2},{1,3},{2,0},{3,1},{4,6},{5,7},{6,4},{7,5},{8,10},{9,11},{10,... | collective-permute-start | bytes 589832 | tf_op jit(solution)/shard_map/ppermute | solution.py:270
  9.4 2.9 %load.1 = (bf16[1024,1024]{1,0:T(8,128)(2,1)S(1)}, bf16[1024,1024]{1,0:T(8,128)(2,1)S(1)}, bf16[1024,1024]{1,0:T(8,128)(2,1)S(1)}) custom-call(bf16[1,1024,1024]{2,1,0:T(8,128)(2,1)} %refs_0_.2, bf16[1,1024,1024]{2,1,0:T(8,128)(2,1)} %refs_1_.3, bf16[1,1024,1024]{2,1,0:T(8,128)(2,1)} %refs_2_.1), custom_call_target="tpu_custom_call" | custom-call | tf_op jit(solution)/shard_map/load/pallas_call | solution.py:401
  13.7 2.5 %collective-permute-done.1.refs_1_ = bf16[96,1024]{1,0:T(8,128)(2,1)S(1)} collective-permute-done((bf16[96,1024]{1,0:T(8,128)(2,1)S(1)}, bf16[96,1024]{1,0:T(8,128)(2,1)S(1)}, u32[]{:S(2)}, u32[]{:S(2)}) %collective-permute-start.1) | collective-permute-done | bytes 196640 | tf_op jit(solution)/shard_map/ppermute | solution.py:274
  16.2 1.5 %collective-permute-start.3 = (bf16[96,1024]{1,0:T(8,128)(2,1)S(1)}, bf16[96,1024]{1,0:T(8,128)(2,1)S(1)}, u32[]{:S(2)}, u32[]{:S(2)}) collective-permute-start(bf16[96,1024]{1,0:T(8,128)(2,1)S(1)} %get-tuple-element.309.first_ref), channel_id=1, source_target_pairs={{0,2},{1,3},{2,0},{3,1},{4,6},{5,7},{6,4},{7,5},{8,10},{9,11},{10,... | collective-permute-start | bytes 589832 | tf_op jit(solution)/shard_map/ppermute | solution.py:270
  17.9 1.5 %collective-permute-done.5.refs_0_ = bf16[96,1024]{1,0:T(8,128)(2,1)S(1)} collective-permute-done((bf16[96,1024]{1,0:T(8,128)(2,1)S(1)}, bf16[96,1024]{1,0:T(8,128)(2,1)S(1)}, u32[]{:S(2)}, u32[]{:S(2)}) %collective-permute-start.5) | collective-permute-done | bytes 196640 | tf_op jit(solution)/shard_map/ppermute | solution.py:270
  20.1 2.6 %ffn.4 = (bf16[1024,384]{1,0:T(8,128)(2,1)S(1)}, bf16[192,1024]{1,0:T(8,128)(2,1)S(1)}, bf16[192,1024]{1,0:T(8,128)(2,1)S(1)}) custom-call(bf16[192,1024]{1,0:T(8,128)(2,1)S(1)} %pair.12.refs_0_, bf16[192,1024]{1,0:T(8,128)(2,1)S(1)} %land_core.9.refs_1_, bf16[1024,1024]{1,0:T(8,128)(2,1)S(1)} %get-tuple-element.360.refs_2_, ...), custom_call_target="tpu_custom_call" | custom-call | tf_op jit(solution)/shard_map/ffn/pallas_call | solution.py:368
  22.7 2.5 %collective-permute-done.4.refs_1_ = bf16[96,1024]{1,0:T(8,128)(2,1)S(1)} collective-permute-done((bf16[96,1024]{1,0:T(8,128)(2,1)S(1)}, bf16[96,1024]{1,0:T(8,128)(2,1)S(1)}, u32[]{:S(2)}, u32[]{:S(2)}) %collective-permute-start.4) | collective-permute-done | bytes 196640 | tf_op jit(solution)/shard_map/ppermute | solution.py:274
  25.2 1.5 %collective-permute-start.7 = (bf16[96,1024]{1,0:T(8,128)(2,1)S(1)}, bf16[96,1024]{1,0:T(8,128)(2,1)S(1)}, u32[]{:S(2)}, u32[]{:S(2)}) collective-permute-start(bf16[96,1024]{1,0:T(8,128)(2,1)S(1)} %get-tuple-element.348.first_ref), channel_id=1, source_target_pairs={{0,2},{1,3},{2,0},{3,1},{4,6},{5,7},{6,4},{7,5},{8,10},{9,11},{10,... | collective-permute-start | bytes 589832 | tf_op jit(solution)/shard_map/ppermute | solution.py:270
  27.9 2.7 %collective-permute-start.9 = (bf16[96,1024]{1,0:T(8,128)(2,1)S(1)}, bf16[96,1024]{1,0:T(8,128)(2,1)S(1)}, u32[]{:S(2)}, u32[]{:S(2)}) collective-permute-start(bf16[96,1024]{1,0:T(8,128)(2,1)S(1)} %get-tuple-element.299), channel_id=1, source_target_pairs={{0,12},{1,13},{2,14},{3,15},{4,0},{5,1},{6,2},{7,3},{8,4},{9,5},{1... | collective-permute-start | bytes 589832 | tf_op jit(solution)/shard_map/ppermute | solution.py:274
  30.8 2.3 %collective-permute-done.11.refs_0_ = bf16[384,1024]{1,0:T(8,128)(2,1)S(1)} collective-permute-done((bf16[384,1024]{1,0:T(8,128)(2,1)S(1)}, bf16[384,1024]{1,0:T(8,128)(2,1)S(1)}, u32[]{:S(2)}, u32[]{:S(2)}) %collective-permute-start.11) | collective-permute-done | bytes 786464 | tf_op jit(solution)/shard_map/ppermute | solution.py:270
  34.0 2.6 %ffn.5 = (bf16[1024,384]{1,0:T(8,128)(2,1)S(1)}, bf16[192,1024]{1,0:T(8,128)(2,1)S(1)}, bf16[192,1024]{1,0:T(8,128)(2,1)S(1)}) custom-call(bf16[192,1024]{1,0:T(8,128)(2,1)S(1)} %pair.13.second_ref.refs_0_, bf16[192,1024]{1,0:T(8,128)(2,1)S(1)} %get-tuple-element.315.refs_1_, bf16[1024,1024]{1,0:T(8,128)(2,1)S(1)} %get-tuple-element.360.refs_2_, ...), custom_call_target="tpu_custom_call" | custom-call | tf_op jit(solution)/shard_map/ffn/pallas_call | solution.py:368
  36.6 2.4 %collective-permute-done.9.refs_2_ = bf16[96,1024]{1,0:T(8,128)(2,1)S(1)} collective-permute-done((bf16[96,1024]{1,0:T(8,128)(2,1)S(1)}, bf16[96,1024]{1,0:T(8,128)(2,1)S(1)}, u32[]{:S(2)}, u32[]{:S(2)}) %collective-permute-start.9) | collective-permute-done | bytes 196640 | tf_op jit(solution)/shard_map/ppermute | solution.py:274
  39.0 1.5 %collective-permute-start.14 = (bf16[96,1024]{1,0:T(8,128)(2,1)S(1)}, bf16[96,1024]{1,0:T(8,128)(2,1)S(1)}, u32[]{:S(2)}, u32[]{:S(2)}) collective-permute-start(bf16[96,1024]{1,0:T(8,128)(2,1)S(1)} %land.14), channel_id=1, source_target_pairs={{0,8},{1,9},{2,10},{3,11},{4,12},{5,13},{6,14},{7,15},{8,0},{9,1},... | collective-permute-start | bytes 589832 | tf_op jit(solution)/shard_map/ppermute | solution.py:274
  41.3 2.6 %ffn.6 = (bf16[1024,384]{1,0:T(8,128)(2,1)S(1)}, bf16[192,1024]{1,0:T(8,128)(2,1)S(1)}, bf16[192,1024]{1,0:T(8,128)(2,1)S(1)}) custom-call(bf16[192,1024]{1,0:T(8,128)(2,1)S(1)} %pair.15.refs_0_, bf16[192,1024]{1,0:T(8,128)(2,1)S(1)} %land_core.11.refs_1_, bf16[1024,1024]{1,0:T(8,128)(2,1)S(1)} %get-tuple-element.360.refs_2_, ...), custom_call_target="tpu_custom_call" | custom-call | tf_op jit(solution)/shard_map/ffn/pallas_call | solution.py:368
  44.7 1.6 %collective-permute-start.18 = (bf16[96,1024]{1,0:T(8,128)(2,1)S(1)}, bf16[96,1024]{1,0:T(8,128)(2,1)S(1)}, u32[]{:S(2)}, u32[]{:S(2)}) collective-permute-start(bf16[96,1024]{1,0:T(8,128)(2,1)S(1)} %fold.5), channel_id=1, source_target_pairs={{0,2},{1,3},{2,0},{3,1},{4,6},{5,7},{6,4},{7,5},{8,10},{9,11},{10,... | collective-permute-start | bytes 589832 | tf_op jit(solution)/shard_map/ppermute | solution.py:270
  46.3 2.6 %ffn.7 = (bf16[1024,384]{1,0:T(8,128)(2,1)S(1)}, bf16[192,1024]{1,0:T(8,128)(2,1)S(1)}, bf16[192,1024]{1,0:T(8,128)(2,1)S(1)}) custom-call(bf16[192,1024]{1,0:T(8,128)(2,1)S(1)} %pair.17.second_ref.refs_0_, bf16[192,1024]{1,0:T(8,128)(2,1)S(1)} %get-tuple-element.359.refs_1_, bf16[1024,1024]{1,0:T(8,128)(2,1)S(1)} %get-tuple-element.360.refs_2_, ...), custom_call_target="tpu_custom_call" | custom-call | tf_op jit(solution)/shard_map/ffn/pallas_call | solution.py:368
  49.0 1.7 %collective-permute-done.14.refs_1_ = bf16[96,1024]{1,0:T(8,128)(2,1)S(1)} collective-permute-done((bf16[96,1024]{1,0:T(8,128)(2,1)S(1)}, bf16[96,1024]{1,0:T(8,128)(2,1)S(1)}, u32[]{:S(2)}, u32[]{:S(2)}) %collective-permute-start.14) | collective-permute-done | bytes 196640 | tf_op jit(solution)/shard_map/ppermute | solution.py:274
  50.6 1.5 %collective-permute-done.13.refs_0_ = bf16[192,1024]{1,0:T(8,128)(2,1)S(1)} collective-permute-done((bf16[192,1024]{1,0:T(8,128)(2,1)S(1)}, bf16[192,1024]{1,0:T(8,128)(2,1)S(1)}, u32[]{:S(2)}, u32[]{:S(2)}) %collective-permute-start.13) | collective-permute-done | bytes 393248 | tf_op jit(solution)/shard_map/ppermute | solution.py:270
  52.3 2.0 %collective-permute-done.18.refs_0_ = bf16[96,1024]{1,0:T(8,128)(2,1)S(1)} collective-permute-done((bf16[96,1024]{1,0:T(8,128)(2,1)S(1)}, bf16[96,1024]{1,0:T(8,128)(2,1)S(1)}, u32[]{:S(2)}, u32[]{:S(2)}) %collective-permute-start.18) | collective-permute-done | bytes 196640 | tf_op jit(solution)/shard_map/ppermute | solution.py:270
  55.1 3.1 %collective-permute-start.21 = (bf16[96,1024]{1,0:T(8,128)(2,1)S(1)}, bf16[96,1024]{1,0:T(8,128)(2,1)S(1)}, u32[]{:S(2)}, u32[]{:S(2)}) collective-permute-start(bf16[96,1024]{1,0:T(8,128)(2,1)S(1)} %total.5), channel_id=1, source_target_pairs={{0,12},{1,13},{2,14},{3,15},{4,0},{5,1},{6,2},{7,3},{8,4},{9,5},{1... | collective-permute-start | bytes 589832 | tf_op jit(solution)/shard_map/ppermute | solution.py:274
  58.2 1.6 %collective-permute-start.22 = (bf16[96,1024]{1,0:T(8,128)(2,1)S(1)}, bf16[96,1024]{1,0:T(8,128)(2,1)S(1)}, u32[]{:S(2)}, u32[]{:S(2)}) collective-permute-start(bf16[96,1024]{1,0:T(8,128)(2,1)S(1)} %fold.7), channel_id=1, source_target_pairs={{0,2},{1,3},{2,0},{3,1},{4,6},{5,7},{6,4},{7,5},{8,10},{9,11},{10,... | collective-permute-start | bytes 589832 | tf_op jit(solution)/shard_map/ppermute | solution.py:270
  59.8 1.4 %collective-permute-done.20.refs_0_ = bf16[96,1024]{1,0:T(8,128)(2,1)S(1)} collective-permute-done((bf16[96,1024]{1,0:T(8,128)(2,1)S(1)}, bf16[96,1024]{1,0:T(8,128)(2,1)S(1)}, u32[]{:S(2)}, u32[]{:S(2)}) %collective-permute-start.20) | collective-permute-done | bytes 196640 | tf_op jit(solution)/shard_map/ppermute | solution.py:270
  61.1 1.8 %collective-permute-done.21.refs_1_ = bf16[96,1024]{1,0:T(8,128)(2,1)S(1)} collective-permute-done((bf16[96,1024]{1,0:T(8,128)(2,1)S(1)}, bf16[96,1024]{1,0:T(8,128)(2,1)S(1)}, u32[]{:S(2)}, u32[]{:S(2)}) %collective-permute-start.21) | collective-permute-done | bytes 196640 | tf_op jit(solution)/shard_map/ppermute | solution.py:274
  63.2 1.6 %collective-permute-start.24 = (bf16[96,1024]{1,0:T(8,128)(2,1)S(1)}, bf16[96,1024]{1,0:T(8,128)(2,1)S(1)}, u32[]{:S(2)}, u32[]{:S(2)}) collective-permute-start(bf16[96,1024]{1,0:T(8,128)(2,1)S(1)} %get-tuple-element.475.first_ref), channel_id=1, source_target_pairs={{0,2},{1,3},{2,0},{3,1},{4,6},{5,7},{6,4},{7,5},{8,10},{9,11},{10,... | collective-permute-start | bytes 589832 | tf_op jit(solution)/shard_map/ppermute | solution.py:270
  66.7 4.8 %collective-permute-start.27 = (bf16[96,1024]{1,0:T(8,128)(2,1)S(1)}, bf16[96,1024]{1,0:T(8,128)(2,1)S(1)}, u32[]{:S(2)}, u32[]{:S(2)}) collective-permute-start(bf16[96,1024]{1,0:T(8,128)(2,1)S(1)} %total.7), channel_id=1, source_target_pairs={{0,8},{1,9},{2,10},{3,11},{4,12},{5,13},{6,14},{7,15},{8,0},{9,1},... | collective-permute-start | bytes 589832 | tf_op jit(solution)/shard_map/ppermute | solution.py:274
  71.8 2.2 %collective-permute-done.26.refs_0_ = bf16[384,1024]{1,0:T(8,128)(2,1)S(1)} collective-permute-done((bf16[384,1024]{1,0:T(8,128)(2,1)S(1)}, bf16[384,1024]{1,0:T(8,128)(2,1)S(1)}, u32[]{:S(2)}, u32[]{:S(2)}) %collective-permute-start.26) | collective-permute-done | bytes 786464 | tf_op jit(solution)/shard_map/ppermute | solution.py:270
  74.3 2.9 %first_grad.1.refs_1_.first_ref = f32[1024,1024]{1,0:T(8,128)S(1)} custom-call(bf16[1024,384]{1,0:T(8,128)(2,1)S(1)} %get-tuple-element.461.refs_2_.refs_0_, bf16[1024,384]{1,0:T(8,128)(2,1)S(1)} %get-tuple-element.462.refs_3_.refs_1_, bf16[1024,384]{1,0:T(8,128)(2,1)S(1)} %get-tuple-element.463.refs_1_.refs_2_, bf16[192,1024]{1,0:T(8,128)(2,1)S(1)} %pair.19.refs_3_, ...), custom_call_target="tpu_custom_call" | custom-call | tf_op jit(solution)/shard_map/first_grad/pallas_call | solution.py:436
  77.3 3.2 %collective-permute-done.27.refs_0_ = bf16[96,1024]{1,0:T(8,128)(2,1)S(1)} collective-permute-done((bf16[96,1024]{1,0:T(8,128)(2,1)S(1)}, bf16[96,1024]{1,0:T(8,128)(2,1)S(1)}, u32[]{:S(2)}, u32[]{:S(2)}) %collective-permute-start.27) | collective-permute-done | bytes 196640 | tf_op jit(solution)/shard_map/ppermute | solution.py:274
  81.9 2.1 %last_grad.1 = bf16[1,1024,1024]{2,1,0:T(8,128)(2,1)} custom-call(f32[1024,1024]{1,0:T(8,128)S(1)} %first_grad.1.refs_1_.first_ref, bf16[1024,384]{1,0:T(8,128)(2,1)S(1)} %get-tuple-element.483.refs_2_.refs_0_, bf16[192,1024]{1,0:T(8,128)(2,1)S(1)} %pair.23.refs_1_, bf16[192,1024]{1,0:T(8,128)(2,1)S(1)} %land_core.17.refs_2_), custom_call_target="tpu_custom_call" | custom-call | tf_op jit(solution)/shard_map/last_grad/pallas_call | solution.py:448
  (87 shorter events, 10.7 us)
Async XLA Ops:
  2.6 11.1 %collective-permute-start = (bf16[96,1024]{1,0:T(8,128)(2,1)S(1)}, bf16[96,1024]{1,0:T(8,128)(2,1)S(1)}, u32[]{:S(2)}, u32[]{:S(2)}) collective-permute-start(bf16[96,1024]{1,0:T(8,128)(2,1)S(1)} %get-tuple-element.244), channel_id=1, source_target_pairs={{0,4},{1,5},{2,6},{3,7},{4,8},{5,9},{6,10},{7,11},{8,12},{9,13},{1... | collective-permute-start | bytes 589832 | tf_op jit(solution)/shard_map/ppermute | solution.py:274
  5.7 10.6 %collective-permute-start.1 = (bf16[96,1024]{1,0:T(8,128)(2,1)S(1)}, bf16[96,1024]{1,0:T(8,128)(2,1)S(1)}, u32[]{:S(2)}, u32[]{:S(2)}) collective-permute-start(bf16[96,1024]{1,0:T(8,128)(2,1)S(1)} %get-tuple-element.245), channel_id=1, source_target_pairs={{0,12},{1,13},{2,14},{3,15},{4,0},{5,1},{6,2},{7,3},{8,4},{9,5},{1... | collective-permute-start | bytes 589832 | tf_op jit(solution)/shard_map/ppermute | solution.py:274
  7.8 8.5 %collective-permute-start.2 = (bf16[96,1024]{1,0:T(8,128)(2,1)S(1)}, bf16[96,1024]{1,0:T(8,128)(2,1)S(1)}, u32[]{:S(2)}, u32[]{:S(2)}) collective-permute-start(bf16[96,1024]{1,0:T(8,128)(2,1)S(1)} %get-tuple-element.277.first_ref), channel_id=1, source_target_pairs={{0,2},{1,3},{2,0},{3,1},{4,6},{5,7},{6,4},{7,5},{8,10},{9,11},{10,... | collective-permute-start | bytes 589832 | tf_op jit(solution)/shard_map/ppermute | solution.py:270
  12.3 12.9 %collective-permute-start.4 = (bf16[96,1024]{1,0:T(8,128)(2,1)S(1)}, bf16[96,1024]{1,0:T(8,128)(2,1)S(1)}, u32[]{:S(2)}, u32[]{:S(2)}) collective-permute-start(bf16[96,1024]{1,0:T(8,128)(2,1)S(1)} %get-tuple-element.257), channel_id=1, source_target_pairs={{0,8},{1,9},{2,10},{3,11},{4,12},{5,13},{6,14},{7,15},{8,0},{9,1},... | collective-permute-start | bytes 589832 | tf_op jit(solution)/shard_map/ppermute | solution.py:274
  13.2 6.2 %collective-permute-start.5 = (bf16[96,1024]{1,0:T(8,128)(2,1)S(1)}, bf16[96,1024]{1,0:T(8,128)(2,1)S(1)}, u32[]{:S(2)}, u32[]{:S(2)}) collective-permute-start(bf16[96,1024]{1,0:T(8,128)(2,1)S(1)} %get-tuple-element.439.first_ref), channel_id=1, source_target_pairs={{0,2},{1,3},{2,0},{3,1},{4,6},{5,7},{6,4},{7,5},{8,10},{9,11},{10,... | collective-permute-start | bytes 589832 | tf_op jit(solution)/shard_map/ppermute | solution.py:270
  16.2 9.0 %collective-permute-start.3 = (bf16[96,1024]{1,0:T(8,128)(2,1)S(1)}, bf16[96,1024]{1,0:T(8,128)(2,1)S(1)}, u32[]{:S(2)}, u32[]{:S(2)}) collective-permute-start(bf16[96,1024]{1,0:T(8,128)(2,1)S(1)} %get-tuple-element.309.first_ref), channel_id=1, source_target_pairs={{0,2},{1,3},{2,0},{3,1},{4,6},{5,7},{6,4},{7,5},{8,10},{9,11},{10,... | collective-permute-start | bytes 589832 | tf_op jit(solution)/shard_map/ppermute | solution.py:270
  17.8 1.8 %collective-permute-start.6 = (bf16[192,1024]{1,0:T(8,128)(2,1)S(1)}, bf16[192,1024]{1,0:T(8,128)(2,1)S(1)}, u32[]{:S(2)}, u32[]{:S(2)}) collective-permute-start(bf16[192,1024]{1,0:T(8,128)(2,1)S(1)} %pair.12.refs_0_), channel_id=1, source_target_pairs={{0,1},{1,0},{2,3},{3,2},{4,5},{5,4},{6,7},{7,6},{8,9},{9,8},{10,11... | collective-permute-start | bytes 1179656 | tf_op jit(solution)/shard_map/ppermute | solution.py:270
  19.6 11.2 %collective-permute-start.10 = (bf16[96,1024]{1,0:T(8,128)(2,1)S(1)}, bf16[96,1024]{1,0:T(8,128)(2,1)S(1)}, u32[]{:S(2)}, u32[]{:S(2)}) collective-permute-start(bf16[96,1024]{1,0:T(8,128)(2,1)S(1)} %get-tuple-element.331.first_ref), channel_id=1, source_target_pairs={{0,2},{1,3},{2,0},{3,1},{4,6},{5,7},{6,4},{7,5},{8,10},{9,11},{10,... | collective-permute-start | bytes 589832 | tf_op jit(solution)/shard_map/ppermute | solution.py:270
  25.2 11.3 %collective-permute-start.7 = (bf16[96,1024]{1,0:T(8,128)(2,1)S(1)}, bf16[96,1024]{1,0:T(8,128)(2,1)S(1)}, u32[]{:S(2)}, u32[]{:S(2)}) collective-permute-start(bf16[96,1024]{1,0:T(8,128)(2,1)S(1)} %get-tuple-element.348.first_ref), channel_id=1, source_target_pairs={{0,2},{1,3},{2,0},{3,1},{4,6},{5,7},{6,4},{7,5},{8,10},{9,11},{10,... | collective-permute-start | bytes 589832 | tf_op jit(solution)/shard_map/ppermute | solution.py:270
  26.8 9.8 %collective-permute-start.8 = (bf16[96,1024]{1,0:T(8,128)(2,1)S(1)}, bf16[96,1024]{1,0:T(8,128)(2,1)S(1)}, u32[]{:S(2)}, u32[]{:S(2)}) collective-permute-start(bf16[96,1024]{1,0:T(8,128)(2,1)S(1)} %get-tuple-element.298), channel_id=1, source_target_pairs={{0,4},{1,5},{2,6},{3,7},{4,8},{5,9},{6,10},{7,11},{8,12},{9,13},{1... | collective-permute-start | bytes 589832 | tf_op jit(solution)/shard_map/ppermute | solution.py:274
  27.9 11.2 %collective-permute-start.9 = (bf16[96,1024]{1,0:T(8,128)(2,1)S(1)}, bf16[96,1024]{1,0:T(8,128)(2,1)S(1)}, u32[]{:S(2)}, u32[]{:S(2)}) collective-permute-start(bf16[96,1024]{1,0:T(8,128)(2,1)S(1)} %get-tuple-element.299), channel_id=1, source_target_pairs={{0,12},{1,13},{2,14},{3,15},{4,0},{5,1},{6,2},{7,3},{8,4},{9,5},{1... | collective-permute-start | bytes 589832 | tf_op jit(solution)/shard_map/ppermute | solution.py:274
  30.7 2.4 %collective-permute-start.11 = (bf16[384,1024]{1,0:T(8,128)(2,1)S(1)}, bf16[384,1024]{1,0:T(8,128)(2,1)S(1)}, u32[]{:S(2)}, u32[]{:S(2)}) collective-permute-start(bf16[384,1024]{1,0:T(8,128)(2,1)S(1)} %pair.14), channel_id=1, source_target_pairs={{0,1},{1,0},{2,3},{3,2},{4,5},{5,4},{6,7},{7,6},{8,9},{9,8},{10,11... | collective-permute-start | bytes 2359304 | tf_op jit(solution)/shard_map/ppermute | solution.py:270
  33.1 6.0 %collective-permute-start.12 = (bf16[192,1024]{1,0:T(8,128)(2,1)S(1)}, bf16[192,1024]{1,0:T(8,128)(2,1)S(1)}, u32[]{:S(2)}, u32[]{:S(2)}) collective-permute-start(bf16[192,1024]{1,0:T(8,128)(2,1)S(1)} %pair.15.refs_0_), channel_id=1, source_target_pairs={{0,1},{1,0},{2,3},{3,2},{4,5},{5,4},{6,7},{7,6},{8,9},{9,8},{10,11... | collective-permute-start | bytes 1179656 | tf_op jit(solution)/shard_map/ppermute | solution.py:270
  33.4 10.6 %collective-permute-start.15 = (bf16[96,1024]{1,0:T(8,128)(2,1)S(1)}, bf16[96,1024]{1,0:T(8,128)(2,1)S(1)}, u32[]{:S(2)}, u32[]{:S(2)}) collective-permute-start(bf16[96,1024]{1,0:T(8,128)(2,1)S(1)} %fold.4), channel_id=1, source_target_pairs={{0,2},{1,3},{2,0},{3,1},{4,6},{5,7},{6,4},{7,5},{8,10},{9,11},{10,... | collective-permute-start | bytes 589832 | tf_op jit(solution)/shard_map/ppermute | solution.py:270
  39.0 11.6 %collective-permute-start.14 = (bf16[96,1024]{1,0:T(8,128)(2,1)S(1)}, bf16[96,1024]{1,0:T(8,128)(2,1)S(1)}, u32[]{:S(2)}, u32[]{:S(2)}) collective-permute-start(bf16[96,1024]{1,0:T(8,128)(2,1)S(1)} %land.14), channel_id=1, source_target_pairs={{0,8},{1,9},{2,10},{3,11},{4,12},{5,13},{6,14},{7,15},{8,0},{9,1},... | collective-permute-start | bytes 589832 | tf_op jit(solution)/shard_map/ppermute | solution.py:274
  40.6 11.6 %collective-permute-start.13 = (bf16[192,1024]{1,0:T(8,128)(2,1)S(1)}, bf16[192,1024]{1,0:T(8,128)(2,1)S(1)}, u32[]{:S(2)}, u32[]{:S(2)}) collective-permute-start(bf16[192,1024]{1,0:T(8,128)(2,1)S(1)} %pair.16), channel_id=1, source_target_pairs={{0,2},{1,3},{2,0},{3,1},{4,6},{5,7},{6,4},{7,5},{8,10},{9,11},{10,... | collective-permute-start | bytes 1179656 | tf_op jit(solution)/shard_map/ppermute | solution.py:270
  41.3 2.7 %collective-permute-start.16 = (bf16[384,1024]{1,0:T(8,128)(2,1)S(1)}, bf16[384,1024]{1,0:T(8,128)(2,1)S(1)}, u32[]{:S(2)}, u32[]{:S(2)}) collective-permute-start(bf16[384,1024]{1,0:T(8,128)(2,1)S(1)} %pair.18), channel_id=1, source_target_pairs={{0,1},{1,0},{2,3},{3,2},{4,5},{5,4},{6,7},{7,6},{8,9},{9,8},{10,11... | collective-permute-start | bytes 2359304 | tf_op jit(solution)/shard_map/ppermute | solution.py:270
  44.0 10.3 %collective-permute-start.17 = (bf16[192,1024]{1,0:T(8,128)(2,1)S(1)}, bf16[192,1024]{1,0:T(8,128)(2,1)S(1)}, u32[]{:S(2)}, u32[]{:S(2)}) collective-permute-start(bf16[192,1024]{1,0:T(8,128)(2,1)S(1)} %get-tuple-element.380), channel_id=1, source_target_pairs={{0,1},{1,0},{2,3},{3,2},{4,5},{5,4},{6,7},{7,6},{8,9},{9,8},{10,11... | collective-permute-start | bytes 1179656 | tf_op jit(solution)/shard_map/ppermute | solution.py:270
  44.7 9.6 %collective-permute-start.18 = (bf16[96,1024]{1,0:T(8,128)(2,1)S(1)}, bf16[96,1024]{1,0:T(8,128)(2,1)S(1)}, u32[]{:S(2)}, u32[]{:S(2)}) collective-permute-start(bf16[96,1024]{1,0:T(8,128)(2,1)S(1)} %fold.5), channel_id=1, source_target_pairs={{0,2},{1,3},{2,0},{3,1},{4,6},{5,7},{6,4},{7,5},{8,10},{9,11},{10,... | collective-permute-start | bytes 589832 | tf_op jit(solution)/shard_map/ppermute | solution.py:270
  48.9 5.4 %collective-permute-start.19 = (bf16[192,1024]{1,0:T(8,128)(2,1)S(1)}, bf16[192,1024]{1,0:T(8,128)(2,1)S(1)}, u32[]{:S(2)}, u32[]{:S(2)}) collective-permute-start(bf16[192,1024]{1,0:T(8,128)(2,1)S(1)} %get-tuple-element.400), channel_id=1, source_target_pairs={{0,1},{1,0},{2,3},{3,2},{4,5},{5,4},{6,7},{7,6},{8,9},{9,8},{10,11... | collective-permute-start | bytes 1179656 | tf_op jit(solution)/shard_map/ppermute | solution.py:270
  54.4 6.7 %collective-permute-start.20 = (bf16[96,1024]{1,0:T(8,128)(2,1)S(1)}, bf16[96,1024]{1,0:T(8,128)(2,1)S(1)}, u32[]{:S(2)}, u32[]{:S(2)}) collective-permute-start(bf16[96,1024]{1,0:T(8,128)(2,1)S(1)} %fold.6), channel_id=1, source_target_pairs={{0,2},{1,3},{2,0},{3,1},{4,6},{5,7},{6,4},{7,5},{8,10},{9,11},{10,... | collective-permute-start | bytes 589832 | tf_op jit(solution)/shard_map/ppermute | solution.py:270
  55.1 7.8 %collective-permute-start.21 = (bf16[96,1024]{1,0:T(8,128)(2,1)S(1)}, bf16[96,1024]{1,0:T(8,128)(2,1)S(1)}, u32[]{:S(2)}, u32[]{:S(2)}) collective-permute-start(bf16[96,1024]{1,0:T(8,128)(2,1)S(1)} %total.5), channel_id=1, source_target_pairs={{0,12},{1,13},{2,14},{3,15},{4,0},{5,1},{6,2},{7,3},{8,4},{9,5},{1... | collective-permute-start | bytes 589832 | tf_op jit(solution)/shard_map/ppermute | solution.py:274
  58.2 7.9 %collective-permute-start.22 = (bf16[96,1024]{1,0:T(8,128)(2,1)S(1)}, bf16[96,1024]{1,0:T(8,128)(2,1)S(1)}, u32[]{:S(2)}, u32[]{:S(2)}) collective-permute-start(bf16[96,1024]{1,0:T(8,128)(2,1)S(1)} %fold.7), channel_id=1, source_target_pairs={{0,2},{1,3},{2,0},{3,1},{4,6},{5,7},{6,4},{7,5},{8,10},{9,11},{10,... | collective-permute-start | bytes 589832 | tf_op jit(solution)/shard_map/ppermute | solution.py:270
  63.0 8.8 %collective-permute-start.25 = (bf16[96,1024]{1,0:T(8,128)(2,1)S(1)}, bf16[96,1024]{1,0:T(8,128)(2,1)S(1)}, u32[]{:S(2)}, u32[]{:S(2)}) collective-permute-start(bf16[96,1024]{1,0:T(8,128)(2,1)S(1)} %total.6), channel_id=1, source_target_pairs={{0,4},{1,5},{2,6},{3,7},{4,8},{5,9},{6,10},{7,11},{8,12},{9,13},{1... | collective-permute-start | bytes 589832 | tf_op jit(solution)/shard_map/ppermute | solution.py:274
  63.2 8.6 %collective-permute-start.24 = (bf16[96,1024]{1,0:T(8,128)(2,1)S(1)}, bf16[96,1024]{1,0:T(8,128)(2,1)S(1)}, u32[]{:S(2)}, u32[]{:S(2)}) collective-permute-start(bf16[96,1024]{1,0:T(8,128)(2,1)S(1)} %get-tuple-element.475.first_ref), channel_id=1, source_target_pairs={{0,2},{1,3},{2,0},{3,1},{4,6},{5,7},{6,4},{7,5},{8,10},{9,11},{10,... | collective-permute-start | bytes 589832 | tf_op jit(solution)/shard_map/ppermute | solution.py:270
  64.9 1.8 %collective-permute-start.23 = (bf16[192,1024]{1,0:T(8,128)(2,1)S(1)}, bf16[192,1024]{1,0:T(8,128)(2,1)S(1)}, u32[]{:S(2)}, u32[]{:S(2)}) collective-permute-start(bf16[192,1024]{1,0:T(8,128)(2,1)S(1)} %pair.19.refs_3_), channel_id=1, source_target_pairs={{0,1},{1,0},{2,3},{3,2},{4,5},{5,4},{6,7},{7,6},{8,9},{9,8},{10,11... | collective-permute-start | bytes 1179656 | tf_op jit(solution)/shard_map/ppermute | solution.py:270
  66.7 13.8 %collective-permute-start.27 = (bf16[96,1024]{1,0:T(8,128)(2,1)S(1)}, bf16[96,1024]{1,0:T(8,128)(2,1)S(1)}, u32[]{:S(2)}, u32[]{:S(2)}) collective-permute-start(bf16[96,1024]{1,0:T(8,128)(2,1)S(1)} %total.7), channel_id=1, source_target_pairs={{0,8},{1,9},{2,10},{3,11},{4,12},{5,13},{6,14},{7,15},{8,0},{9,1},... | collective-permute-start | bytes 589832 | tf_op jit(solution)/shard_map/ppermute | solution.py:274
  71.7 2.4 %collective-permute-start.26 = (bf16[384,1024]{1,0:T(8,128)(2,1)S(1)}, bf16[384,1024]{1,0:T(8,128)(2,1)S(1)}, u32[]{:S(2)}, u32[]{:S(2)}) collective-permute-start(bf16[384,1024]{1,0:T(8,128)(2,1)S(1)} %pair.22), channel_id=1, source_target_pairs={{0,1},{1,0},{2,3},{3,2},{4,5},{5,4},{6,7},{7,6},{8,9},{9,8},{10,11... | collective-permute-start | bytes 2359304 | tf_op jit(solution)/shard_map/ppermute | solution.py:270
  74.1 6.4 %collective-permute-start.28 = (bf16[192,1024]{1,0:T(8,128)(2,1)S(1)}, bf16[192,1024]{1,0:T(8,128)(2,1)S(1)}, u32[]{:S(2)}, u32[]{:S(2)}) collective-permute-start(bf16[192,1024]{1,0:T(8,128)(2,1)S(1)} %pair.23.refs_1_), channel_id=1, source_target_pairs={{0,1},{1,0},{2,3},{3,2},{4,5},{5,4},{6,7},{7,6},{8,9},{9,8},{10,11... | collective-permute-start | bytes 1179656 | tf_op jit(solution)/shard_map/ppermute | solution.py:270
  77.3 3.2 %copy-start = (bf16[128,1024]{1,0:T(8,128)(2,1)S(1)}, bf16[128,1024]{1,0:T(8,128)(2,1)}, u32[]{:S(2)}) copy-start(bf16[128,1024]{1,0:T(8,128)(2,1)} %tokens_ref.1) | copy-start | bytes 786436
  77.3 3.2 %copy-start.1 = (s32[128,2]{0,1:T(2,128)S(1)}, s32[128,2]{0,1:T(2,128)}, u32[]{:S(2)}) copy-start(s32[128,2]{0,1:T(2,128)} %param.10) | copy-start | bytes 3076
  77.3 3.2 %copy-start.2 = (s32[128,2]{0,1:T(2,128)S(1)}, s32[128,2]{0,1:T(2,128)}, u32[]{:S(2)}) copy-start(s32[128,2]{0,1:T(2,128)} %param.11) | copy-start | bytes 3076

commit v16 on v15

--- a/solution.py
+++ b/solution.py
@@ -16,13 +16,15 @@
     ("ffnN0 yN2", "yN1 zN3"),
     ("cR0N1 yN3 zC1 zC2", "yN2 cR0N1"),
     ("ffnN1 cN2 yR0", "yN3 zC1 zC2 cN2"),
-    ("cR1N3 ffnN2 yC1C2 zC3", "yR0 cR1N3"),
-    ("cR2 ffnN3 cR3 yR1 totalR0", "yC1C2 zC3 cR2"),
-    ("", "yR1 cR3"),
-    ("yR2 yR3 totalR1 zR1", "yR2 zR1"),
-    ("totalR2 zR2 yC3 cC0", "yR3 cC0"),
-    ("totalR3 zR3 cC1C2", "yC3 zR2 cC1C2"),
-    ("cC3 gradC0", "zR3 cC3"),
+    ("cR1N3 ffnN2 yC1 zC3", "yR0 cR1N3"),
+    ("cR2 ffnN3 yR1 totalR0", "yC1 zC3 cR2"),
+    ("cR3 yR2", "yR1"),
+    ("totalR1 zR1", "cR3"),
+    ("yR3 cC0", "yR2 cC0"),
+    ("totalR2 zR2 yC2", "yR3 zR1"),
+    ("totalR3 zR3 yC3 cC1", "yC2 zR2 cC1"),
+    ("cC2 gradC0", "yC3 zR3 cC2"),
+    ("cC3", None),
 )
 TILE = 256
 LINK_WORK = 10 << 30
@@ -465,8 +467,8 @@
         "total": lambda kind, g: total(g),
         "load": lambda kind, g: load(),
         "grad": lambda kind, g: first_grad(
-            [(0,), (1,), (2,)],
-            [("C", "own", (i,)) for i in range(3)] + [("c", "C", i) for i in range(3)],
+            [(0,), (1,)],
+            [("C", "own", (0,)), ("C", "own", (1,)), ("c", "C", 0), ("c", "C", 1)],
         ),
     }
     def name_of(act):
@@ -489,10 +491,14 @@
                 kernels.append(live["turned", name[1][1:]])
             if name[0] == "grad":
                 kernels.append(live["first"])
+        if lands is None:
+            break
         land(*map(name_of, lands.split()), earlier=kernels)
+    if ("c", ("C", 3)) in flying:
+        live["c", "C", 3] = flying.pop(("c", ("C", 3)))
     grad_down = last_grad(
-        [(3,)],
-        [("C", "own", (3,)), ("c", "C", 3)],
+        [(2,), (3,)],
+        [("C", "own", (2,)), ("C", "own", (3,)), ("c", "C", 2), ("c", "C", 3)],
     )
     mixed = call(
         functools.partial(combine_kernel, experts),

time: 84.3 us -> 79.9 us (0.948)
  starting transfers between devices: 33.2 us -> 29.3 us
    ppermute x9, starting transfers between devices: 19.5 us -> 14.3 us  [turn(): return lax.ppermute(value, 'expert', to)]
    ppermute x9, waiting for transfers between devices: 14.1 us -> 16.4 us  [turn(): return lax.ppermute(value, 'expert', to)]
    ppermute x20 -> x22, waiting for transfers between devices: 12.9 us -> 10.7 us  [swap(): lax.ppermute(value, 'expert', [(i, i ^ mask) for i in range(devices)])]
    ppermute x20 -> x22, starting transfers between devices: 13.6 us -> 15 us  [swap(): lax.ppermute(value, 'expert', [(i, i ^ mask) for i in range(devices)])]
    pallas_call x1, Pallas kernels: 2.94 us -> 1.87 us  [first_grad(): call(functools.partial(first_grad_kernel, plan), 24, 'first_grad', out_sh...]
  transfers between devices with their start and end apart: 29 -> 31, of which waited for: 15 -> 13; matrix products, arithmetic and copies ran while one was open for 0% -> 0% of each run, Pallas kernels for 21% -> 22%
where the time goes in v16:
time: 79.9 us; the launch traced here: 79.8 us
  starting transfers between devices  29.3 us (37%)
  waiting for transfers between devices  27.1 us (34%)
  Pallas kernels  22.2 us (28%)
  between operations  1.18 us (1%)
    ppermute x9, waiting for transfers between devices, turn(): return lax.ppermute(value, 'expert', to)  16.4 us
    ppermute x22, starting transfers between devices, swap(): lax.ppermute(value, 'expert', [(i, i ^ mask) for i in range(devices)])  15 us
    ppermute x9, starting transfers between devices, turn(): return lax.ppermute(value, 'expert', to)  14.3 us
    ppermute x22, waiting for transfers between devices, swap(): lax.ppermute(value, 'expert', [(i, i ^ mask) for i in range(devices)])  10.7 us
    pallas_call x4, Pallas kernels, ffn(): call(functools.partial(ffn_kernel, len(pieces)), 24, 'ffn', out_shape=[ja...  10.5 us
    pallas_call x1, Pallas kernels, load(): call(load_kernel, 16, 'load', out_shape=[weight, weight, jax.ShapeDtypeSt...  2.88 us
    pallas_call x1, Pallas kernels, last_grad(): call(functools.partial(last_grad_kernel, plan), 24, 'last_grad', out_shap...  2.71 us
    pallas_call x1, Pallas kernels, send(): call(functools.partial(send_kernel, experts), 16, 'send', out_shape=[piec...  1.92 us
  transfers between devices with their start and end apart: 31, of which 13 were waited for; matrix products, arithmetic and copies ran while one was open for 0% of the time, Pallas kernels for 22%

profile of v16, /device:TPU:0, one launch (start us, length us, event | category | flops | bytes accessed | tf_op | source)
XLA Modules:
  0.0 79.8 jit_solution(7668904786328261030)
XLA Ops:
  0.6 1.9 %send.1 = (bf16[96,1024]{1,0:T(8,128)(2,1)S(1)}, bf16[96,1024]{1,0:T(8,128)(2,1)S(1)}, bf16[96,1024]{1,0:T(8,128)(2,1)S(1)}, bf16[96,1024]{1,0:T(8,128)(2,1)S(1)...) custom-call(s32[1]{0:T(128)} %bitcast.plane_ref, ...), custom_call_target="tpu_custom_call" | custom-call | tf_op jit(solution)/shard_map/send/pallas_call | solution.py:388
  2.6 3.1 %collective-permute-start = (bf16[96,1024]{1,0:T(8,128)(2,1)S(1)}, bf16[96,1024]{1,0:T(8,128)(2,1)S(1)}, u32[]{:S(2)}, u32[]{:S(2)}) collective-permute-start(bf16[96,1024]{1,0:T(8,128)(2,1)S(1)} %get-tuple-element.255), channel_id=1, source_target_pairs={{0,4},{1,5},{2,6},{3,7},{4,8},{5,9},{6,10},{7,11},{8,12},{9,13},{1... | collective-permute-start | bytes 589832 | tf_op jit(solution)/shard_map/ppermute | solution.py:276
  5.7 2.1 %collective-permute-start.1 = (bf16[96,1024]{1,0:T(8,128)(2,1)S(1)}, bf16[96,1024]{1,0:T(8,128)(2,1)S(1)}, u32[]{:S(2)}, u32[]{:S(2)}) collective-permute-start(bf16[96,1024]{1,0:T(8,128)(2,1)S(1)} %get-tuple-element.256), channel_id=1, source_target_pairs={{0,12},{1,13},{2,14},{3,15},{4,0},{5,1},{6,2},{7,3},{8,4},{9,5},{1... | collective-permute-start | bytes 589832 | tf_op jit(solution)/shard_map/ppermute | solution.py:276
  7.8 1.7 %collective-permute-start.2 = (bf16[96,1024]{1,0:T(8,128)(2,1)S(1)}, bf16[96,1024]{1,0:T(8,128)(2,1)S(1)}, u32[]{:S(2)}, u32[]{:S(2)}) collective-permute-start(bf16[96,1024]{1,0:T(8,128)(2,1)S(1)} %get-tuple-element.288.first_ref), channel_id=1, source_target_pairs={{0,2},{1,3},{2,0},{3,1},{4,6},{5,7},{6,4},{7,5},{8,10},{9,11},{10,... | collective-permute-start | bytes 589832 | tf_op jit(solution)/shard_map/ppermute | solution.py:272
  9.4 2.9 %load.1 = (bf16[1024,1024]{1,0:T(8,128)(2,1)S(1)}, bf16[1024,1024]{1,0:T(8,128)(2,1)S(1)}, bf16[1024,1024]{1,0:T(8,128)(2,1)S(1)}) custom-call(bf16[1,1024,1024]{2,1,0:T(8,128)(2,1)} %refs_0_.2, bf16[1,1024,1024]{2,1,0:T(8,128)(2,1)} %refs_1_.3, bf16[1,1024,1024]{2,1,0:T(8,128)(2,1)} %refs_2_.1), custom_call_target="tpu_custom_call" | custom-call | tf_op jit(solution)/shard_map/load/pallas_call | solution.py:403
  13.7 2.5 %collective-permute-done.1.refs_1_ = bf16[96,1024]{1,0:T(8,128)(2,1)S(1)} collective-permute-done((bf16[96,1024]{1,0:T(8,128)(2,1)S(1)}, bf16[96,1024]{1,0:T(8,128)(2,1)S(1)}, u32[]{:S(2)}, u32[]{:S(2)}) %collective-permute-start.1) | collective-permute-done | bytes 196640 | tf_op jit(solution)/shard_map/ppermute | solution.py:276
  16.2 1.5 %collective-permute-start.3 = (bf16[96,1024]{1,0:T(8,128)(2,1)S(1)}, bf16[96,1024]{1,0:T(8,128)(2,1)S(1)}, u32[]{:S(2)}, u32[]{:S(2)}) collective-permute-start(bf16[96,1024]{1,0:T(8,128)(2,1)S(1)} %get-tuple-element.320.first_ref), channel_id=1, source_target_pairs={{0,2},{1,3},{2,0},{3,1},{4,6},{5,7},{6,4},{7,5},{8,10},{9,11},{10,... | collective-permute-start | bytes 589832 | tf_op jit(solution)/shard_map/ppermute | solution.py:272
  17.9 1.5 %collective-permute-done.5.refs_0_ = bf16[96,1024]{1,0:T(8,128)(2,1)S(1)} collective-permute-done((bf16[96,1024]{1,0:T(8,128)(2,1)S(1)}, bf16[96,1024]{1,0:T(8,128)(2,1)S(1)}, u32[]{:S(2)}, u32[]{:S(2)}) %collective-permute-start.5) | collective-permute-done | bytes 196640 | tf_op jit(solution)/shard_map/ppermute | solution.py:272
  20.1 2.6 %ffn.4 = (bf16[1024,384]{1,0:T(8,128)(2,1)S(1)}, bf16[192,1024]{1,0:T(8,128)(2,1)S(1)}, bf16[192,1024]{1,0:T(8,128)(2,1)S(1)}) custom-call(bf16[192,1024]{1,0:T(8,128)(2,1)S(1)} %pair.10.refs_0_, bf16[192,1024]{1,0:T(8,128)(2,1)S(1)} %land_core.8.refs_1_, bf16[1024,1024]{1,0:T(8,128)(2,1)S(1)} %get-tuple-element.371.refs_2_, ...), custom_call_target="tpu_custom_call" | custom-call | tf_op jit(solution)/shard_map/ffn/pallas_call | solution.py:370
  22.7 2.5 %collective-permute-done.4.refs_1_ = bf16[96,1024]{1,0:T(8,128)(2,1)S(1)} collective-permute-done((bf16[96,1024]{1,0:T(8,128)(2,1)S(1)}, bf16[96,1024]{1,0:T(8,128)(2,1)S(1)}, u32[]{:S(2)}, u32[]{:S(2)}) %collective-permute-start.4) | collective-permute-done | bytes 196640 | tf_op jit(solution)/shard_map/ppermute | solution.py:276
  25.2 1.5 %collective-permute-start.7 = (bf16[96,1024]{1,0:T(8,128)(2,1)S(1)}, bf16[96,1024]{1,0:T(8,128)(2,1)S(1)}, u32[]{:S(2)}, u32[]{:S(2)}) collective-permute-start(bf16[96,1024]{1,0:T(8,128)(2,1)S(1)} %get-tuple-element.359.first_ref), channel_id=1, source_target_pairs={{0,2},{1,3},{2,0},{3,1},{4,6},{5,7},{6,4},{7,5},{8,10},{9,11},{10,... | collective-permute-start | bytes 589832 | tf_op jit(solution)/shard_map/ppermute | solution.py:272
  26.8 1.1 %collective-permute-start.8 = (bf16[96,1024]{1,0:T(8,128)(2,1)S(1)}, bf16[96,1024]{1,0:T(8,128)(2,1)S(1)}, u32[]{:S(2)}, u32[]{:S(2)}) collective-permute-start(bf16[96,1024]{1,0:T(8,128)(2,1)S(1)} %get-tuple-element.309), channel_id=1, source_target_pairs={{0,4},{1,5},{2,6},{3,7},{4,8},{5,9},{6,10},{7,11},{8,12},{9,13},{1... | collective-permute-start | bytes 589832 | tf_op jit(solution)/shard_map/ppermute | solution.py:276
  27.9 2.7 %collective-permute-start.9 = (bf16[96,1024]{1,0:T(8,128)(2,1)S(1)}, bf16[96,1024]{1,0:T(8,128)(2,1)S(1)}, u32[]{:S(2)}, u32[]{:S(2)}) collective-permute-start(bf16[96,1024]{1,0:T(8,128)(2,1)S(1)} %get-tuple-element.310), channel_id=1, source_target_pairs={{0,12},{1,13},{2,14},{3,15},{4,0},{5,1},{6,2},{7,3},{8,4},{9,5},{1... | collective-permute-start | bytes 589832 | tf_op jit(solution)/shard_map/ppermute | solution.py:276
  30.8 2.3 %collective-permute-done.11.refs_0_ = bf16[384,1024]{1,0:T(8,128)(2,1)S(1)} collective-permute-done((bf16[384,1024]{1,0:T(8,128)(2,1)S(1)}, bf16[384,1024]{1,0:T(8,128)(2,1)S(1)}, u32[]{:S(2)}, u32[]{:S(2)}) %collective-permute-start.11) | collective-permute-done | bytes 786464 | tf_op jit(solution)/shard_map/ppermute | solution.py:272
  34.0 2.6 %ffn.5 = (bf16[1024,384]{1,0:T(8,128)(2,1)S(1)}, bf16[192,1024]{1,0:T(8,128)(2,1)S(1)}, bf16[192,1024]{1,0:T(8,128)(2,1)S(1)}) custom-call(bf16[192,1024]{1,0:T(8,128)(2,1)S(1)} %pair.11.second_ref.refs_0_, bf16[192,1024]{1,0:T(8,128)(2,1)S(1)} %get-tuple-element.326.refs_1_, bf16[1024,1024]{1,0:T(8,128)(2,1)S(1)} %get-tuple-element.371.refs_2_, ...), custom_call_target="tpu_custom_call" | custom-call | tf_op jit(solution)/shard_map/ffn/pallas_call | solution.py:370
  36.6 2.4 %collective-permute-done.9.refs_2_ = bf16[96,1024]{1,0:T(8,128)(2,1)S(1)} collective-permute-done((bf16[96,1024]{1,0:T(8,128)(2,1)S(1)}, bf16[96,1024]{1,0:T(8,128)(2,1)S(1)}, u32[]{:S(2)}, u32[]{:S(2)}) %collective-permute-start.9) | collective-permute-done | bytes 196640 | tf_op jit(solution)/shard_map/ppermute | solution.py:276
  39.5 1.5 %collective-permute-start.14 = (bf16[96,1024]{1,0:T(8,128)(2,1)S(1)}, bf16[96,1024]{1,0:T(8,128)(2,1)S(1)}, u32[]{:S(2)}, u32[]{:S(2)}) collective-permute-start(bf16[96,1024]{1,0:T(8,128)(2,1)S(1)} %land.15), channel_id=1, source_target_pairs={{0,8},{1,9},{2,10},{3,11},{4,12},{5,13},{6,14},{7,15},{8,0},{9,1},... | collective-permute-start | bytes 589832 | tf_op jit(solution)/shard_map/ppermute | solution.py:276
  41.2 2.6 %ffn.6 = (bf16[1024,384]{1,0:T(8,128)(2,1)S(1)}, bf16[192,1024]{1,0:T(8,128)(2,1)S(1)}, bf16[192,1024]{1,0:T(8,128)(2,1)S(1)}) custom-call(bf16[192,1024]{1,0:T(8,128)(2,1)S(1)} %pair.13.refs_0_, bf16[192,1024]{1,0:T(8,128)(2,1)S(1)} %land_core.10.refs_1_, bf16[1024,1024]{1,0:T(8,128)(2,1)S(1)} %get-tuple-element.371.refs_2_, ...), custom_call_target="tpu_custom_call" | custom-call | tf_op jit(solution)/shard_map/ffn/pallas_call | solution.py:370
  44.6 1.6 %collective-permute-start.18 = (bf16[96,1024]{1,0:T(8,128)(2,1)S(1)}, bf16[96,1024]{1,0:T(8,128)(2,1)S(1)}, u32[]{:S(2)}, u32[]{:S(2)}) collective-permute-start(bf16[96,1024]{1,0:T(8,128)(2,1)S(1)} %fold.5), channel_id=1, source_target_pairs={{0,2},{1,3},{2,0},{3,1},{4,6},{5,7},{6,4},{7,5},{8,10},{9,11},{10,... | collective-permute-start | bytes 589832 | tf_op jit(solution)/shard_map/ppermute | solution.py:272
  46.2 2.6 %ffn.7 = (bf16[1024,384]{1,0:T(8,128)(2,1)S(1)}, bf16[192,1024]{1,0:T(8,128)(2,1)S(1)}, bf16[192,1024]{1,0:T(8,128)(2,1)S(1)}) custom-call(bf16[192,1024]{1,0:T(8,128)(2,1)S(1)} %pair.14.second_ref.refs_0_, bf16[192,1024]{1,0:T(8,128)(2,1)S(1)} %get-tuple-element.370.refs_1_, bf16[1024,1024]{1,0:T(8,128)(2,1)S(1)} %get-tuple-element.371.refs_2_, ...), custom_call_target="tpu_custom_call" | custom-call | tf_op jit(solution)/shard_map/ffn/pallas_call | solution.py:370
  48.8 2.1 %collective-permute-done.14.refs_1_ = bf16[96,1024]{1,0:T(8,128)(2,1)S(1)} collective-permute-done((bf16[96,1024]{1,0:T(8,128)(2,1)S(1)}, bf16[96,1024]{1,0:T(8,128)(2,1)S(1)}, u32[]{:S(2)}, u32[]{:S(2)}) %collective-permute-start.14) | collective-permute-done | bytes 196640 | tf_op jit(solution)/shard_map/ppermute | solution.py:276
  51.5 1.6 %collective-permute-start.20 = (bf16[96,1024]{1,0:T(8,128)(2,1)S(1)}, bf16[96,1024]{1,0:T(8,128)(2,1)S(1)}, u32[]{:S(2)}, u32[]{:S(2)}) collective-permute-start(bf16[96,1024]{1,0:T(8,128)(2,1)S(1)} %fold.6), channel_id=1, source_target_pairs={{0,2},{1,3},{2,0},{3,1},{4,6},{5,7},{6,4},{7,5},{8,10},{9,11},{10,... | collective-permute-start | bytes 589832 | tf_op jit(solution)/shard_map/ppermute | solution.py:272
  53.2 1.7 %collective-permute-start.23 = (bf16[96,1024]{1,0:T(8,128)(2,1)S(1)}, bf16[96,1024]{1,0:T(8,128)(2,1)S(1)}, u32[]{:S(2)}, u32[]{:S(2)}) collective-permute-start(bf16[96,1024]{1,0:T(8,128)(2,1)S(1)} %total.5), channel_id=1, source_target_pairs={{0,12},{1,13},{2,14},{3,15},{4,0},{5,1},{6,2},{7,3},{8,4},{9,5},{1... | collective-permute-start | bytes 589832 | tf_op jit(solution)/shard_map/ppermute | solution.py:276
  55.6 3.7 %collective-permute-done.20.refs_0_ = bf16[96,1024]{1,0:T(8,128)(2,1)S(1)} collective-permute-done((bf16[96,1024]{1,0:T(8,128)(2,1)S(1)}, bf16[96,1024]{1,0:T(8,128)(2,1)S(1)}, u32[]{:S(2)}, u32[]{:S(2)}) %collective-permute-start.20) | collective-permute-done | bytes 196640 | tf_op jit(solution)/shard_map/ppermute | solution.py:272
  59.7 1.6 %collective-permute-start.24 = (bf16[96,1024]{1,0:T(8,128)(2,1)S(1)}, bf16[96,1024]{1,0:T(8,128)(2,1)S(1)}, u32[]{:S(2)}, u32[]{:S(2)}) collective-permute-start(bf16[96,1024]{1,0:T(8,128)(2,1)S(1)} %get-tuple-element.493.first_ref), channel_id=1, source_target_pairs={{0,2},{1,3},{2,0},{3,1},{4,6},{5,7},{6,4},{7,5},{8,10},{9,11},{10,... | collective-permute-start | bytes 589832 | tf_op jit(solution)/shard_map/ppermute | solution.py:272
  61.3 2.3 %collective-permute-done.22.refs_0_ = bf16[96,1024]{1,0:T(8,128)(2,1)S(1)} collective-permute-done((bf16[96,1024]{1,0:T(8,128)(2,1)S(1)}, bf16[96,1024]{1,0:T(8,128)(2,1)S(1)}, u32[]{:S(2)}, u32[]{:S(2)}) %collective-permute-start.22) | collective-permute-done | bytes 196640 | tf_op jit(solution)/shard_map/ppermute | solution.py:272
  64.6 1.5 %collective-permute-start.27 = (bf16[96,1024]{1,0:T(8,128)(2,1)S(1)}, bf16[96,1024]{1,0:T(8,128)(2,1)S(1)}, u32[]{:S(2)}, u32[]{:S(2)}) collective-permute-start(bf16[96,1024]{1,0:T(8,128)(2,1)S(1)} %get-tuple-element.505.first_ref), channel_id=1, source_target_pairs={{0,2},{1,3},{2,0},{3,1},{4,6},{5,7},{6,4},{7,5},{8,10},{9,11},{10,... | collective-permute-start | bytes 589832 | tf_op jit(solution)/shard_map/ppermute | solution.py:272
  66.2 2.6 %collective-permute-done.25.refs_1_ = bf16[96,1024]{1,0:T(8,128)(2,1)S(1)} collective-permute-done((bf16[96,1024]{1,0:T(8,128)(2,1)S(1)}, bf16[96,1024]{1,0:T(8,128)(2,1)S(1)}, u32[]{:S(2)}, u32[]{:S(2)}) %collective-permute-start.25) | collective-permute-done | bytes 196640 | tf_op jit(solution)/shard_map/ppermute | solution.py:276
  69.0 1.9 %first_grad.1.refs_2_.first_ref = f32[1024,1024]{1,0:T(8,128)S(1)} custom-call(bf16[1024,384]{1,0:T(8,128)(2,1)S(1)} %get-tuple-element.480.refs_2_.refs_0_, bf16[1024,384]{1,0:T(8,128)(2,1)S(1)} %get-tuple-element.481.refs_3_.refs_1_, bf16[192,1024]{1,0:T(8,128)(2,1)S(1)} %pair.16.refs_2_, bf16[192,1024]{1,0:T(8,128)(2,1)S(1)} %pair.17.refs_3_, ...), custom_call_target="tpu_custom_call" | custom-call | tf_op jit(solution)/shard_map/first_grad/pallas_call | solution.py:438
  70.9 4.2 %collective-permute-done.28.refs_1_ = bf16[96,1024]{1,0:T(8,128)(2,1)S(1)} collective-permute-done((bf16[96,1024]{1,0:T(8,128)(2,1)S(1)}, bf16[96,1024]{1,0:T(8,128)(2,1)S(1)}, u32[]{:S(2)}, u32[]{:S(2)}) %collective-permute-start.28) | collective-permute-done | bytes 196640 | tf_op jit(solution)/shard_map/ppermute | solution.py:276
  75.2 1.4 %combine.1 = bf16[128,1024]{1,0:T(8,128)(2,1)} custom-call(s32[1]{0:T(128)} %bitcast.plane_ref, bf16[128,1024]{1,0:T(8,128)(2,1)S(1)} %copy-done, s32[2,128]{1,0:T(2,128)S(1)} %bitcast.5, s32[2,128]{1,0:T(2,128)S(1)} %bitcast.7, bf16[96,1024]{1,0:T(8,128)(2,1)S(1)} %total.4.refs_0_, bf16[96,1024]{1,0:T(8,128)(2,1)S(1)} %get-tuple-element.498.refs_1_, ...), custom_call_target="tpu_custom_call" | custom-call | tf_op jit(solution)/shard_map/combine/pallas_call | solution.py:503
  76.9 2.7 %last_grad.1 = bf16[1,1024,1024]{2,1,0:T(8,128)(2,1)} custom-call(f32[1024,1024]{1,0:T(8,128)S(1)} %first_grad.1.refs_2_.first_ref, bf16[1024,384]{1,0:T(8,128)(2,1)S(1)} %get-tuple-element.502.refs_1_.refs_0_, bf16[1024,384]{1,0:T(8,128)(2,1)S(1)} %get-tuple-element.503.refs_2_.refs_1_, bf16[192,1024]{1,0:T(8,128)(2,1)S(1)} %pair.18.refs_2_, ...), custom_call_target="tpu_custom_call" | custom-call | tf_op jit(solution)/shard_map/last_grad/pallas_call | solution.py:450
  (87 shorter events, 7.9 us)
Async XLA Ops:
  2.6 11.1 %collective-permute-start = (bf16[96,1024]{1,0:T(8,128)(2,1)S(1)}, bf16[96,1024]{1,0:T(8,128)(2,1)S(1)}, u32[]{:S(2)}, u32[]{:S(2)}) collective-permute-start(bf16[96,1024]{1,0:T(8,128)(2,1)S(1)} %get-tuple-element.255), channel_id=1, source_target_pairs={{0,4},{1,5},{2,6},{3,7},{4,8},{5,9},{6,10},{7,11},{8,12},{9,13},{1... | collective-permute-start | bytes 589832 | tf_op jit(solution)/shard_map/ppermute | solution.py:276
  5.7 10.6 %collective-permute-start.1 = (bf16[96,1024]{1,0:T(8,128)(2,1)S(1)}, bf16[96,1024]{1,0:T(8,128)(2,1)S(1)}, u32[]{:S(2)}, u32[]{:S(2)}) collective-permute-start(bf16[96,1024]{1,0:T(8,128)(2,1)S(1)} %get-tuple-element.256), channel_id=1, source_target_pairs={{0,12},{1,13},{2,14},{3,15},{4,0},{5,1},{6,2},{7,3},{8,4},{9,5},{1... | collective-permute-start | bytes 589832 | tf_op jit(solution)/shard_map/ppermute | solution.py:276
  7.8 8.5 %collective-permute-start.2 = (bf16[96,1024]{1,0:T(8,128)(2,1)S(1)}, bf16[96,1024]{1,0:T(8,128)(2,1)S(1)}, u32[]{:S(2)}, u32[]{:S(2)}) collective-permute-start(bf16[96,1024]{1,0:T(8,128)(2,1)S(1)} %get-tuple-element.288.first_ref), channel_id=1, source_target_pairs={{0,2},{1,3},{2,0},{3,1},{4,6},{5,7},{6,4},{7,5},{8,10},{9,11},{10,... | collective-permute-start | bytes 589832 | tf_op jit(solution)/shard_map/ppermute | solution.py:272
  12.3 12.9 %collective-permute-start.4 = (bf16[96,1024]{1,0:T(8,128)(2,1)S(1)}, bf16[96,1024]{1,0:T(8,128)(2,1)S(1)}, u32[]{:S(2)}, u32[]{:S(2)}) collective-permute-start(bf16[96,1024]{1,0:T(8,128)(2,1)S(1)} %get-tuple-element.268), channel_id=1, source_target_pairs={{0,8},{1,9},{2,10},{3,11},{4,12},{5,13},{6,14},{7,15},{8,0},{9,1},... | collective-permute-start | bytes 589832 | tf_op jit(solution)/shard_map/ppermute | solution.py:276
  13.2 6.2 %collective-permute-start.5 = (bf16[96,1024]{1,0:T(8,128)(2,1)S(1)}, bf16[96,1024]{1,0:T(8,128)(2,1)S(1)}, u32[]{:S(2)}, u32[]{:S(2)}) collective-permute-start(bf16[96,1024]{1,0:T(8,128)(2,1)S(1)} %get-tuple-element.441.first_ref), channel_id=1, source_target_pairs={{0,2},{1,3},{2,0},{3,1},{4,6},{5,7},{6,4},{7,5},{8,10},{9,11},{10,... | collective-permute-start | bytes 589832 | tf_op jit(solution)/shard_map/ppermute | solution.py:272
  16.2 9.0 %collective-permute-start.3 = (bf16[96,1024]{1,0:T(8,128)(2,1)S(1)}, bf16[96,1024]{1,0:T(8,128)(2,1)S(1)}, u32[]{:S(2)}, u32[]{:S(2)}) collective-permute-start(bf16[96,1024]{1,0:T(8,128)(2,1)S(1)} %get-tuple-element.320.first_ref), channel_id=1, source_target_pairs={{0,2},{1,3},{2,0},{3,1},{4,6},{5,7},{6,4},{7,5},{8,10},{9,11},{10,... | collective-permute-start | bytes 589832 | tf_op jit(solution)/shard_map/ppermute | solution.py:272
  17.8 1.8 %collective-permute-start.6 = (bf16[192,1024]{1,0:T(8,128)(2,1)S(1)}, bf16[192,1024]{1,0:T(8,128)(2,1)S(1)}, u32[]{:S(2)}, u32[]{:S(2)}) collective-permute-start(bf16[192,1024]{1,0:T(8,128)(2,1)S(1)} %pair.10.refs_0_), channel_id=1, source_target_pairs={{0,1},{1,0},{2,3},{3,2},{4,5},{5,4},{6,7},{7,6},{8,9},{9,8},{10,11... | collective-permute-start | bytes 1179656 | tf_op jit(solution)/shard_map/ppermute | solution.py:272
  19.6 11.2 %collective-permute-start.10 = (bf16[96,1024]{1,0:T(8,128)(2,1)S(1)}, bf16[96,1024]{1,0:T(8,128)(2,1)S(1)}, u32[]{:S(2)}, u32[]{:S(2)}) collective-permute-start(bf16[96,1024]{1,0:T(8,128)(2,1)S(1)} %get-tuple-element.342.first_ref), channel_id=1, source_target_pairs={{0,2},{1,3},{2,0},{3,1},{4,6},{5,7},{6,4},{7,5},{8,10},{9,11},{10,... | collective-permute-start | bytes 589832 | tf_op jit(solution)/shard_map/ppermute | solution.py:272
  25.2 11.3 %collective-permute-start.7 = (bf16[96,1024]{1,0:T(8,128)(2,1)S(1)}, bf16[96,1024]{1,0:T(8,128)(2,1)S(1)}, u32[]{:S(2)}, u32[]{:S(2)}) collective-permute-start(bf16[96,1024]{1,0:T(8,128)(2,1)S(1)} %get-tuple-element.359.first_ref), channel_id=1, source_target_pairs={{0,2},{1,3},{2,0},{3,1},{4,6},{5,7},{6,4},{7,5},{8,10},{9,11},{10,... | collective-permute-start | bytes 589832 | tf_op jit(solution)/shard_map/ppermute | solution.py:272
  26.8 9.8 %collective-permute-start.8 = (bf16[96,1024]{1,0:T(8,128)(2,1)S(1)}, bf16[96,1024]{1,0:T(8,128)(2,1)S(1)}, u32[]{:S(2)}, u32[]{:S(2)}) collective-permute-start(bf16[96,1024]{1,0:T(8,128)(2,1)S(1)} %get-tuple-element.309), channel_id=1, source_target_pairs={{0,4},{1,5},{2,6},{3,7},{4,8},{5,9},{6,10},{7,11},{8,12},{9,13},{1... | collective-permute-start | bytes 589832 | tf_op jit(solution)/shard_map/ppermute | solution.py:276
  27.9 11.2 %collective-permute-start.9 = (bf16[96,1024]{1,0:T(8,128)(2,1)S(1)}, bf16[96,1024]{1,0:T(8,128)(2,1)S(1)}, u32[]{:S(2)}, u32[]{:S(2)}) collective-permute-start(bf16[96,1024]{1,0:T(8,128)(2,1)S(1)} %get-tuple-element.310), channel_id=1, source_target_pairs={{0,12},{1,13},{2,14},{3,15},{4,0},{5,1},{6,2},{7,3},{8,4},{9,5},{1... | collective-permute-start | bytes 589832 | tf_op jit(solution)/shard_map/ppermute | solution.py:276
  30.7 2.4 %collective-permute-start.11 = (bf16[384,1024]{1,0:T(8,128)(2,1)S(1)}, bf16[384,1024]{1,0:T(8,128)(2,1)S(1)}, u32[]{:S(2)}, u32[]{:S(2)}) collective-permute-start(bf16[384,1024]{1,0:T(8,128)(2,1)S(1)} %pair.12), channel_id=1, source_target_pairs={{0,1},{1,0},{2,3},{3,2},{4,5},{5,4},{6,7},{7,6},{8,9},{9,8},{10,11... | collective-permute-start | bytes 2359304 | tf_op jit(solution)/shard_map/ppermute | solution.py:272
  33.1 6.0 %collective-permute-start.12 = (bf16[192,1024]{1,0:T(8,128)(2,1)S(1)}, bf16[192,1024]{1,0:T(8,128)(2,1)S(1)}, u32[]{:S(2)}, u32[]{:S(2)}) collective-permute-start(bf16[192,1024]{1,0:T(8,128)(2,1)S(1)} %pair.13.refs_0_), channel_id=1, source_target_pairs={{0,1},{1,0},{2,3},{3,2},{4,5},{5,4},{6,7},{7,6},{8,9},{9,8},{10,11... | collective-permute-start | bytes 1179656 | tf_op jit(solution)/shard_map/ppermute | solution.py:272
  33.4 10.5 %collective-permute-start.15 = (bf16[96,1024]{1,0:T(8,128)(2,1)S(1)}, bf16[96,1024]{1,0:T(8,128)(2,1)S(1)}, u32[]{:S(2)}, u32[]{:S(2)}) collective-permute-start(bf16[96,1024]{1,0:T(8,128)(2,1)S(1)} %fold.4), channel_id=1, source_target_pairs={{0,2},{1,3},{2,0},{3,1},{4,6},{5,7},{6,4},{7,5},{8,10},{9,11},{10,... | collective-permute-start | bytes 589832 | tf_op jit(solution)/shard_map/ppermute | solution.py:272
  39.0 9.8 %collective-permute-start.13 = (bf16[96,1024]{1,0:T(8,128)(2,1)S(1)}, bf16[96,1024]{1,0:T(8,128)(2,1)S(1)}, u32[]{:S(2)}, u32[]{:S(2)}) collective-permute-start(bf16[96,1024]{1,0:T(8,128)(2,1)S(1)} %get-tuple-element.476.first_ref), channel_id=1, source_target_pairs={{0,2},{1,3},{2,0},{3,1},{4,6},{5,7},{6,4},{7,5},{8,10},{9,11},{10,... | collective-permute-start | bytes 589832 | tf_op jit(solution)/shard_map/ppermute | solution.py:272
  39.5 11.3 %collective-permute-start.14 = (bf16[96,1024]{1,0:T(8,128)(2,1)S(1)}, bf16[96,1024]{1,0:T(8,128)(2,1)S(1)}, u32[]{:S(2)}, u32[]{:S(2)}) collective-permute-start(bf16[96,1024]{1,0:T(8,128)(2,1)S(1)} %land.15), channel_id=1, source_target_pairs={{0,8},{1,9},{2,10},{3,11},{4,12},{5,13},{6,14},{7,15},{8,0},{9,1},... | collective-permute-start | bytes 589832 | tf_op jit(solution)/shard_map/ppermute | solution.py:276
  41.2 2.7 %collective-permute-start.16 = (bf16[384,1024]{1,0:T(8,128)(2,1)S(1)}, bf16[384,1024]{1,0:T(8,128)(2,1)S(1)}, u32[]{:S(2)}, u32[]{:S(2)}) collective-permute-start(bf16[384,1024]{1,0:T(8,128)(2,1)S(1)} %pair.15), channel_id=1, source_target_pairs={{0,1},{1,0},{2,3},{3,2},{4,5},{5,4},{6,7},{7,6},{8,9},{9,8},{10,11... | collective-permute-start | bytes 2359304 | tf_op jit(solution)/shard_map/ppermute | solution.py:272
  43.9 7.0 %collective-permute-start.17 = (bf16[192,1024]{1,0:T(8,128)(2,1)S(1)}, bf16[192,1024]{1,0:T(8,128)(2,1)S(1)}, u32[]{:S(2)}, u32[]{:S(2)}) collective-permute-start(bf16[192,1024]{1,0:T(8,128)(2,1)S(1)} %get-tuple-element.392), channel_id=1, source_target_pairs={{0,1},{1,0},{2,3},{3,2},{4,5},{5,4},{6,7},{7,6},{8,9},{9,8},{10,11... | collective-permute-start | bytes 1179656 | tf_op jit(solution)/shard_map/ppermute | solution.py:272
  44.6 6.9 %collective-permute-start.18 = (bf16[96,1024]{1,0:T(8,128)(2,1)S(1)}, bf16[96,1024]{1,0:T(8,128)(2,1)S(1)}, u32[]{:S(2)}, u32[]{:S(2)}) collective-permute-start(bf16[96,1024]{1,0:T(8,128)(2,1)S(1)} %fold.5), channel_id=1, source_target_pairs={{0,2},{1,3},{2,0},{3,1},{4,6},{5,7},{6,4},{7,5},{8,10},{9,11},{10,... | collective-permute-start | bytes 589832 | tf_op jit(solution)/shard_map/ppermute | solution.py:272
  51.0 3.9 %collective-permute-start.19 = (bf16[192,1024]{1,0:T(8,128)(2,1)S(1)}, bf16[192,1024]{1,0:T(8,128)(2,1)S(1)}, u32[]{:S(2)}, u32[]{:S(2)}) collective-permute-start(bf16[192,1024]{1,0:T(8,128)(2,1)S(1)} %get-tuple-element.427), channel_id=1, source_target_pairs={{0,1},{1,0},{2,3},{3,2},{4,5},{5,4},{6,7},{7,6},{8,9},{9,8},{10,11... | collective-permute-start | bytes 1179656 | tf_op jit(solution)/shard_map/ppermute | solution.py:272
  51.5 7.8 %collective-permute-start.20 = (bf16[96,1024]{1,0:T(8,128)(2,1)S(1)}, bf16[96,1024]{1,0:T(8,128)(2,1)S(1)}, u32[]{:S(2)}, u32[]{:S(2)}) collective-permute-start(bf16[96,1024]{1,0:T(8,128)(2,1)S(1)} %fold.6), channel_id=1, source_target_pairs={{0,2},{1,3},{2,0},{3,1},{4,6},{5,7},{6,4},{7,5},{8,10},{9,11},{10,... | collective-permute-start | bytes 589832 | tf_op jit(solution)/shard_map/ppermute | solution.py:272
  53.2 8.1 %collective-permute-start.23 = (bf16[96,1024]{1,0:T(8,128)(2,1)S(1)}, bf16[96,1024]{1,0:T(8,128)(2,1)S(1)}, u32[]{:S(2)}, u32[]{:S(2)}) collective-permute-start(bf16[96,1024]{1,0:T(8,128)(2,1)S(1)} %total.5), channel_id=1, source_target_pairs={{0,12},{1,13},{2,14},{3,15},{4,0},{5,1},{6,2},{7,3},{8,4},{9,5},{1... | collective-permute-start | bytes 589832 | tf_op jit(solution)/shard_map/ppermute | solution.py:276
  55.0 8.6 %collective-permute-start.22 = (bf16[96,1024]{1,0:T(8,128)(2,1)S(1)}, bf16[96,1024]{1,0:T(8,128)(2,1)S(1)}, u32[]{:S(2)}, u32[]{:S(2)}) collective-permute-start(bf16[96,1024]{1,0:T(8,128)(2,1)S(1)} %fold.7), channel_id=1, source_target_pairs={{0,2},{1,3},{2,0},{3,1},{4,6},{5,7},{6,4},{7,5},{8,10},{9,11},{10,... | collective-permute-start | bytes 589832 | tf_op jit(solution)/shard_map/ppermute | solution.py:272
  55.6 3.8 %collective-permute-start.21 = (bf16[192,1024]{1,0:T(8,128)(2,1)S(1)}, bf16[192,1024]{1,0:T(8,128)(2,1)S(1)}, u32[]{:S(2)}, u32[]{:S(2)}) collective-permute-start(bf16[192,1024]{1,0:T(8,128)(2,1)S(1)} %pair.16.refs_2_), channel_id=1, source_target_pairs={{0,1},{1,0},{2,3},{3,2},{4,5},{5,4},{6,7},{7,6},{8,9},{9,8},{10,11... | collective-permute-start | bytes 1179656 | tf_op jit(solution)/shard_map/ppermute | solution.py:272
  59.4 9.4 %collective-permute-start.25 = (bf16[96,1024]{1,0:T(8,128)(2,1)S(1)}, bf16[96,1024]{1,0:T(8,128)(2,1)S(1)}, u32[]{:S(2)}, u32[]{:S(2)}) collective-permute-start(bf16[96,1024]{1,0:T(8,128)(2,1)S(1)} %total.6), channel_id=1, source_target_pairs={{0,4},{1,5},{2,6},{3,7},{4,8},{5,9},{6,10},{7,11},{8,12},{9,13},{1... | collective-permute-start | bytes 589832 | tf_op jit(solution)/shard_map/ppermute | solution.py:276
  59.7 9.2 %collective-permute-start.24 = (bf16[96,1024]{1,0:T(8,128)(2,1)S(1)}, bf16[96,1024]{1,0:T(8,128)(2,1)S(1)}, u32[]{:S(2)}, u32[]{:S(2)}) collective-permute-start(bf16[96,1024]{1,0:T(8,128)(2,1)S(1)} %get-tuple-element.493.first_ref), channel_id=1, source_target_pairs={{0,2},{1,3},{2,0},{3,1},{4,6},{5,7},{6,4},{7,5},{8,10},{9,11},{10,... | collective-permute-start | bytes 589832 | tf_op jit(solution)/shard_map/ppermute | solution.py:272
  63.6 11.4 %collective-permute-start.28 = (bf16[96,1024]{1,0:T(8,128)(2,1)S(1)}, bf16[96,1024]{1,0:T(8,128)(2,1)S(1)}, u32[]{:S(2)}, u32[]{:S(2)}) collective-permute-start(bf16[96,1024]{1,0:T(8,128)(2,1)S(1)} %total.7), channel_id=1, source_target_pairs={{0,8},{1,9},{2,10},{3,11},{4,12},{5,13},{6,14},{7,15},{8,0},{9,1},... | collective-permute-start | bytes 589832 | tf_op jit(solution)/shard_map/ppermute | solution.py:276
  64.6 10.5 %collective-permute-start.27 = (bf16[96,1024]{1,0:T(8,128)(2,1)S(1)}, bf16[96,1024]{1,0:T(8,128)(2,1)S(1)}, u32[]{:S(2)}, u32[]{:S(2)}) collective-permute-start(bf16[96,1024]{1,0:T(8,128)(2,1)S(1)} %get-tuple-element.505.first_ref), channel_id=1, source_target_pairs={{0,2},{1,3},{2,0},{3,1},{4,6},{5,7},{6,4},{7,5},{8,10},{9,11},{10,... | collective-permute-start | bytes 589832 | tf_op jit(solution)/shard_map/ppermute | solution.py:272
  66.1 2.7 %collective-permute-start.26 = (bf16[192,1024]{1,0:T(8,128)(2,1)S(1)}, bf16[192,1024]{1,0:T(8,128)(2,1)S(1)}, u32[]{:S(2)}, u32[]{:S(2)}) collective-permute-start(bf16[192,1024]{1,0:T(8,128)(2,1)S(1)} %pair.17.refs_3_), channel_id=1, source_target_pairs={{0,1},{1,0},{2,3},{3,2},{4,5},{5,4},{6,7},{7,6},{8,9},{9,8},{10,11... | collective-permute-start | bytes 1179656 | tf_op jit(solution)/shard_map/ppermute | solution.py:272
  68.9 6.2 %collective-permute-start.29 = (bf16[192,1024]{1,0:T(8,128)(2,1)S(1)}, bf16[192,1024]{1,0:T(8,128)(2,1)S(1)}, u32[]{:S(2)}, u32[]{:S(2)}) collective-permute-start(bf16[192,1024]{1,0:T(8,128)(2,1)S(1)} %pair.18.refs_2_), channel_id=1, source_target_pairs={{0,1},{1,0},{2,3},{3,2},{4,5},{5,4},{6,7},{7,6},{8,9},{9,8},{10,11... | collective-permute-start | bytes 1179656 | tf_op jit(solution)/shard_map/ppermute | solution.py:272
  70.8 4.4 %copy-start = (bf16[128,1024]{1,0:T(8,128)(2,1)S(1)}, bf16[128,1024]{1,0:T(8,128)(2,1)}, u32[]{:S(2)}) copy-start(bf16[128,1024]{1,0:T(8,128)(2,1)} %tokens_ref.1) | copy-start | bytes 786436
  75.1 1.8 %collective-permute-start.30 = (bf16[192,1024]{1,0:T(8,128)(2,1)S(1)}, bf16[192,1024]{1,0:T(8,128)(2,1)S(1)}, u32[]{:S(2)}, u32[]{:S(2)}) collective-permute-start(bf16[192,1024]{1,0:T(8,128)(2,1)S(1)} %pair.19.refs_3_), channel_id=1, source_target_pairs={{0,1},{1,0},{2,3},{3,2},{4,5},{5,4},{6,7},{7,6},{8,9},{9,8},{10,11... | collective-permute-start | bytes 1179656 | tf_op jit(solution)/shard_map/ppermute | solution.py:272
  (2 other events, 8.7 us)

commit v17 on v16

--- a/solution.py
+++ b/solution.py
@@ -17,11 +17,10 @@
     ("cR0N1 yN3 zC1 zC2", "yN2 cR0N1"),
     ("ffnN1 cN2 yR0", "yN3 zC1 zC2 cN2"),
     ("cR1N3 ffnN2 yC1 zC3", "yR0 cR1N3"),
-    ("cR2 ffnN3 yR1 totalR0", "yC1 zC3 cR2"),
-    ("cR3 yR2", "yR1"),
-    ("totalR1 zR1", "cR3"),
-    ("yR3 cC0", "yR2 cC0"),
-    ("totalR2 zR2 yC2", "yR3 zR1"),
+    ("cR2 ffnN3 cR3 yR1 totalR0", "yC1 zC3 cR2"),
+    ("yR2", "yR1 cR3"),
+    ("totalR1 zR1 yR3", "yR2"),
+    ("totalR2 zR2 yC2 cC0", "zR1 yR3 cC0"),
     ("totalR3 zR3 yC3 cC1", "yC2 zR2 cC1"),
     ("cC2 gradC0", "yC3 zR3 cC2"),
     ("cC3", None),

time: 79.9 us -> 80 us (level)
  waiting for transfers between devices: 27.1 us -> 28.1 us
  starting transfers between devices: 29.3 us -> 28.4 us
    ppermute x9, waiting for transfers between devices: 16.4 us -> 17.5 us  [turn(): return lax.ppermute(value, 'expert', to)]
  transfers between devices with their start and end apart: 31 -> 31, of which waited for: 13 -> 12; matrix products, arithmetic and copies ran while one was open for 0% -> 0% of each run, Pallas kernels for 22% -> 22%
where the time goes in v17:
time: 80 us; the launch traced here: 79.9 us
  starting transfers between devices  28.4 us (36%)
  waiting for transfers between devices  28.1 us (35%)
  Pallas kernels  22.2 us (28%)
  between operations  1.2 us (2%)
    ppermute x9, waiting for transfers between devices, turn(): return lax.ppermute(value, 'expert', to)  17.5 us
    ppermute x22, starting transfers between devices, swap(): lax.ppermute(value, 'expert', [(i, i ^ mask) for i in range(devices)])  14.3 us
    ppermute x9, starting transfers between devices, turn(): return lax.ppermute(value, 'expert', to)  14.1 us
    ppermute x22, waiting for transfers between devices, swap(): lax.ppermute(value, 'expert', [(i, i ^ mask) for i in range(devices)])  10.5 us
    pallas_call x4, Pallas kernels, ffn(): call(functools.partial(ffn_kernel, len(pieces)), 24, 'ffn', out_shape=[ja...  10.5 us
    pallas_call x1, Pallas kernels, load(): call(load_kernel, 16, 'load', out_shape=[weight, weight, jax.ShapeDtypeSt...  2.88 us
    pallas_call x1, Pallas kernels, last_grad(): call(functools.partial(last_grad_kernel, plan), 24, 'last_grad', out_shap...  2.71 us
    pallas_call x1, Pallas kernels, send(): call(functools.partial(send_kernel, experts), 16, 'send', out_shape=[piec...  1.92 us
  transfers between devices with their start and end apart: 31, of which 12 were waited for; matrix products, arithmetic and copies ran while one was open for 0% of the time, Pallas kernels for 22%

profile of v17, /device:TPU:0, one launch (start us, length us, event | category | flops | bytes accessed | tf_op | source)
XLA Modules:
  0.0 79.9 jit_solution(15076618126769123958)
XLA Ops:
  0.6 1.9 %send.1 = (bf16[96,1024]{1,0:T(8,128)(2,1)S(1)}, bf16[96,1024]{1,0:T(8,128)(2,1)S(1)}, bf16[96,1024]{1,0:T(8,128)(2,1)S(1)}, bf16[96,1024]{1,0:T(8,128)(2,1)S(1)...) custom-call(s32[1]{0:T(128)} %bitcast.plane_ref, ...), custom_call_target="tpu_custom_call" | custom-call | tf_op jit(solution)/shard_map/send/pallas_call | solution.py:387
  2.6 3.1 %collective-permute-start = (bf16[96,1024]{1,0:T(8,128)(2,1)S(1)}, bf16[96,1024]{1,0:T(8,128)(2,1)S(1)}, u32[]{:S(2)}, u32[]{:S(2)}) collective-permute-start(bf16[96,1024]{1,0:T(8,128)(2,1)S(1)} %get-tuple-element.241), channel_id=1, source_target_pairs={{0,4},{1,5},{2,6},{3,7},{4,8},{5,9},{6,10},{7,11},{8,12},{9,13},{1... | collective-permute-start | bytes 589832 | tf_op jit(solution)/shard_map/ppermute | solution.py:275
  5.7 2.1 %collective-permute-start.1 = (bf16[96,1024]{1,0:T(8,128)(2,1)S(1)}, bf16[96,1024]{1,0:T(8,128)(2,1)S(1)}, u32[]{:S(2)}, u32[]{:S(2)}) collective-permute-start(bf16[96,1024]{1,0:T(8,128)(2,1)S(1)} %get-tuple-element.242), channel_id=1, source_target_pairs={{0,12},{1,13},{2,14},{3,15},{4,0},{5,1},{6,2},{7,3},{8,4},{9,5},{1... | collective-permute-start | bytes 589832 | tf_op jit(solution)/shard_map/ppermute | solution.py:275
  7.8 1.7 %collective-permute-start.2 = (bf16[96,1024]{1,0:T(8,128)(2,1)S(1)}, bf16[96,1024]{1,0:T(8,128)(2,1)S(1)}, u32[]{:S(2)}, u32[]{:S(2)}) collective-permute-start(bf16[96,1024]{1,0:T(8,128)(2,1)S(1)} %get-tuple-element.274.first_ref), channel_id=1, source_target_pairs={{0,2},{1,3},{2,0},{3,1},{4,6},{5,7},{6,4},{7,5},{8,10},{9,11},{10,... | collective-permute-start | bytes 589832 | tf_op jit(solution)/shard_map/ppermute | solution.py:271
  9.4 2.9 %load.1 = (bf16[1024,1024]{1,0:T(8,128)(2,1)S(1)}, bf16[1024,1024]{1,0:T(8,128)(2,1)S(1)}, bf16[1024,1024]{1,0:T(8,128)(2,1)S(1)}) custom-call(bf16[1,1024,1024]{2,1,0:T(8,128)(2,1)} %refs_0_.2, bf16[1,1024,1024]{2,1,0:T(8,128)(2,1)} %refs_1_.3, bf16[1,1024,1024]{2,1,0:T(8,128)(2,1)} %refs_2_.1), custom_call_target="tpu_custom_call" | custom-call | tf_op jit(solution)/shard_map/load/pallas_call | solution.py:402
  13.7 2.5 %collective-permute-done.1.refs_1_ = bf16[96,1024]{1,0:T(8,128)(2,1)S(1)} collective-permute-done((bf16[96,1024]{1,0:T(8,128)(2,1)S(1)}, bf16[96,1024]{1,0:T(8,128)(2,1)S(1)}, u32[]{:S(2)}, u32[]{:S(2)}) %collective-permute-start.1) | collective-permute-done | bytes 196640 | tf_op jit(solution)/shard_map/ppermute | solution.py:275
  16.2 1.5 %collective-permute-start.3 = (bf16[96,1024]{1,0:T(8,128)(2,1)S(1)}, bf16[96,1024]{1,0:T(8,128)(2,1)S(1)}, u32[]{:S(2)}, u32[]{:S(2)}) collective-permute-start(bf16[96,1024]{1,0:T(8,128)(2,1)S(1)} %get-tuple-element.306.first_ref), channel_id=1, source_target_pairs={{0,2},{1,3},{2,0},{3,1},{4,6},{5,7},{6,4},{7,5},{8,10},{9,11},{10,... | collective-permute-start | bytes 589832 | tf_op jit(solution)/shard_map/ppermute | solution.py:271
  17.9 1.5 %collective-permute-done.5.refs_0_ = bf16[96,1024]{1,0:T(8,128)(2,1)S(1)} collective-permute-done((bf16[96,1024]{1,0:T(8,128)(2,1)S(1)}, bf16[96,1024]{1,0:T(8,128)(2,1)S(1)}, u32[]{:S(2)}, u32[]{:S(2)}) %collective-permute-start.5) | collective-permute-done | bytes 196640 | tf_op jit(solution)/shard_map/ppermute | solution.py:271
  20.1 2.6 %ffn.4 = (bf16[1024,384]{1,0:T(8,128)(2,1)S(1)}, bf16[192,1024]{1,0:T(8,128)(2,1)S(1)}, bf16[192,1024]{1,0:T(8,128)(2,1)S(1)}) custom-call(bf16[192,1024]{1,0:T(8,128)(2,1)S(1)} %pair.10.refs_0_, bf16[192,1024]{1,0:T(8,128)(2,1)S(1)} %land_core.9.refs_1_, bf16[1024,1024]{1,0:T(8,128)(2,1)S(1)} %get-tuple-element.357.refs_2_, ...), custom_call_target="tpu_custom_call" | custom-call | tf_op jit(solution)/shard_map/ffn/pallas_call | solution.py:369
  22.7 2.5 %collective-permute-done.4.refs_1_ = bf16[96,1024]{1,0:T(8,128)(2,1)S(1)} collective-permute-done((bf16[96,1024]{1,0:T(8,128)(2,1)S(1)}, bf16[96,1024]{1,0:T(8,128)(2,1)S(1)}, u32[]{:S(2)}, u32[]{:S(2)}) %collective-permute-start.4) | collective-permute-done | bytes 196640 | tf_op jit(solution)/shard_map/ppermute | solution.py:275
  25.2 1.5 %collective-permute-start.7 = (bf16[96,1024]{1,0:T(8,128)(2,1)S(1)}, bf16[96,1024]{1,0:T(8,128)(2,1)S(1)}, u32[]{:S(2)}, u32[]{:S(2)}) collective-permute-start(bf16[96,1024]{1,0:T(8,128)(2,1)S(1)} %get-tuple-element.345.first_ref), channel_id=1, source_target_pairs={{0,2},{1,3},{2,0},{3,1},{4,6},{5,7},{6,4},{7,5},{8,10},{9,11},{10,... | collective-permute-start | bytes 589832 | tf_op jit(solution)/shard_map/ppermute | solution.py:271
  26.8 1.1 %collective-permute-start.8 = (bf16[96,1024]{1,0:T(8,128)(2,1)S(1)}, bf16[96,1024]{1,0:T(8,128)(2,1)S(1)}, u32[]{:S(2)}, u32[]{:S(2)}) collective-permute-start(bf16[96,1024]{1,0:T(8,128)(2,1)S(1)} %get-tuple-element.295), channel_id=1, source_target_pairs={{0,4},{1,5},{2,6},{3,7},{4,8},{5,9},{6,10},{7,11},{8,12},{9,13},{1... | collective-permute-start | bytes 589832 | tf_op jit(solution)/shard_map/ppermute | solution.py:275
  27.9 2.7 %collective-permute-start.9 = (bf16[96,1024]{1,0:T(8,128)(2,1)S(1)}, bf16[96,1024]{1,0:T(8,128)(2,1)S(1)}, u32[]{:S(2)}, u32[]{:S(2)}) collective-permute-start(bf16[96,1024]{1,0:T(8,128)(2,1)S(1)} %get-tuple-element.296), channel_id=1, source_target_pairs={{0,12},{1,13},{2,14},{3,15},{4,0},{5,1},{6,2},{7,3},{8,4},{9,5},{1... | collective-permute-start | bytes 589832 | tf_op jit(solution)/shard_map/ppermute | solution.py:275
  30.8 2.3 %collective-permute-done.11.refs_0_ = bf16[384,1024]{1,0:T(8,128)(2,1)S(1)} collective-permute-done((bf16[384,1024]{1,0:T(8,128)(2,1)S(1)}, bf16[384,1024]{1,0:T(8,128)(2,1)S(1)}, u32[]{:S(2)}, u32[]{:S(2)}) %collective-permute-start.11) | collective-permute-done | bytes 786464 | tf_op jit(solution)/shard_map/ppermute | solution.py:271
  34.0 2.6 %ffn.5 = (bf16[1024,384]{1,0:T(8,128)(2,1)S(1)}, bf16[192,1024]{1,0:T(8,128)(2,1)S(1)}, bf16[192,1024]{1,0:T(8,128)(2,1)S(1)}) custom-call(bf16[192,1024]{1,0:T(8,128)(2,1)S(1)} %pair.11.second_ref.refs_0_, bf16[192,1024]{1,0:T(8,128)(2,1)S(1)} %get-tuple-element.312.refs_1_, bf16[1024,1024]{1,0:T(8,128)(2,1)S(1)} %get-tuple-element.357.refs_2_, ...), custom_call_target="tpu_custom_call" | custom-call | tf_op jit(solution)/shard_map/ffn/pallas_call | solution.py:369
  36.6 2.4 %collective-permute-done.9.refs_2_ = bf16[96,1024]{1,0:T(8,128)(2,1)S(1)} collective-permute-done((bf16[96,1024]{1,0:T(8,128)(2,1)S(1)}, bf16[96,1024]{1,0:T(8,128)(2,1)S(1)}, u32[]{:S(2)}, u32[]{:S(2)}) %collective-permute-start.9) | collective-permute-done | bytes 196640 | tf_op jit(solution)/shard_map/ppermute | solution.py:275
  39.5 1.5 %collective-permute-start.14 = (bf16[96,1024]{1,0:T(8,128)(2,1)S(1)}, bf16[96,1024]{1,0:T(8,128)(2,1)S(1)}, u32[]{:S(2)}, u32[]{:S(2)}) collective-permute-start(bf16[96,1024]{1,0:T(8,128)(2,1)S(1)} %land.14), channel_id=1, source_target_pairs={{0,8},{1,9},{2,10},{3,11},{4,12},{5,13},{6,14},{7,15},{8,0},{9,1},... | collective-permute-start | bytes 589832 | tf_op jit(solution)/shard_map/ppermute | solution.py:275
  41.2 2.6 %ffn.6 = (bf16[1024,384]{1,0:T(8,128)(2,1)S(1)}, bf16[192,1024]{1,0:T(8,128)(2,1)S(1)}, bf16[192,1024]{1,0:T(8,128)(2,1)S(1)}) custom-call(bf16[192,1024]{1,0:T(8,128)(2,1)S(1)} %pair.13.refs_0_, bf16[192,1024]{1,0:T(8,128)(2,1)S(1)} %land_core.11.refs_1_, bf16[1024,1024]{1,0:T(8,128)(2,1)S(1)} %get-tuple-element.357.refs_2_, ...), custom_call_target="tpu_custom_call" | custom-call | tf_op jit(solution)/shard_map/ffn/pallas_call | solution.py:369
  44.6 1.6 %collective-permute-start.18 = (bf16[96,1024]{1,0:T(8,128)(2,1)S(1)}, bf16[96,1024]{1,0:T(8,128)(2,1)S(1)}, u32[]{:S(2)}, u32[]{:S(2)}) collective-permute-start(bf16[96,1024]{1,0:T(8,128)(2,1)S(1)} %fold.5), channel_id=1, source_target_pairs={{0,2},{1,3},{2,0},{3,1},{4,6},{5,7},{6,4},{7,5},{8,10},{9,11},{10,... | collective-permute-start | bytes 589832 | tf_op jit(solution)/shard_map/ppermute | solution.py:271
  46.2 2.6 %ffn.7 = (bf16[1024,384]{1,0:T(8,128)(2,1)S(1)}, bf16[192,1024]{1,0:T(8,128)(2,1)S(1)}, bf16[192,1024]{1,0:T(8,128)(2,1)S(1)}) custom-call(bf16[192,1024]{1,0:T(8,128)(2,1)S(1)} %pair.14.second_ref.refs_0_, bf16[192,1024]{1,0:T(8,128)(2,1)S(1)} %get-tuple-element.356.refs_1_, bf16[1024,1024]{1,0:T(8,128)(2,1)S(1)} %get-tuple-element.357.refs_2_, ...), custom_call_target="tpu_custom_call" | custom-call | tf_op jit(solution)/shard_map/ffn/pallas_call | solution.py:369
  48.9 2.0 %collective-permute-done.14.refs_1_ = bf16[96,1024]{1,0:T(8,128)(2,1)S(1)} collective-permute-done((bf16[96,1024]{1,0:T(8,128)(2,1)S(1)}, bf16[96,1024]{1,0:T(8,128)(2,1)S(1)}, u32[]{:S(2)}, u32[]{:S(2)}) %collective-permute-start.14) | collective-permute-done | bytes 196640 | tf_op jit(solution)/shard_map/ppermute | solution.py:275
  51.0 1.6 %collective-permute-start.20 = (bf16[96,1024]{1,0:T(8,128)(2,1)S(1)}, bf16[96,1024]{1,0:T(8,128)(2,1)S(1)}, u32[]{:S(2)}, u32[]{:S(2)}) collective-permute-start(bf16[96,1024]{1,0:T(8,128)(2,1)S(1)} %fold.6), channel_id=1, source_target_pairs={{0,2},{1,3},{2,0},{3,1},{4,6},{5,7},{6,4},{7,5},{8,10},{9,11},{10,... | collective-permute-start | bytes 589832 | tf_op jit(solution)/shard_map/ppermute | solution.py:271
  53.3 1.6 %collective-permute-start.21 = (bf16[96,1024]{1,0:T(8,128)(2,1)S(1)}, bf16[96,1024]{1,0:T(8,128)(2,1)S(1)}, u32[]{:S(2)}, u32[]{:S(2)}) collective-permute-start(bf16[96,1024]{1,0:T(8,128)(2,1)S(1)} %total.5), channel_id=1, source_target_pairs={{0,12},{1,13},{2,14},{3,15},{4,0},{5,1},{6,2},{7,3},{8,4},{9,5},{1... | collective-permute-start | bytes 589832 | tf_op jit(solution)/shard_map/ppermute | solution.py:275
  54.9 4.0 %collective-permute-done.20.refs_0_ = bf16[96,1024]{1,0:T(8,128)(2,1)S(1)} collective-permute-done((bf16[96,1024]{1,0:T(8,128)(2,1)S(1)}, bf16[96,1024]{1,0:T(8,128)(2,1)S(1)}, u32[]{:S(2)}, u32[]{:S(2)}) %collective-permute-start.20) | collective-permute-done | bytes 196640 | tf_op jit(solution)/shard_map/ppermute | solution.py:271
  59.3 1.6 %collective-permute-start.24 = (bf16[96,1024]{1,0:T(8,128)(2,1)S(1)}, bf16[96,1024]{1,0:T(8,128)(2,1)S(1)}, u32[]{:S(2)}, u32[]{:S(2)}) collective-permute-start(bf16[96,1024]{1,0:T(8,128)(2,1)S(1)} %get-tuple-element.465.first_ref), channel_id=1, source_target_pairs={{0,2},{1,3},{2,0},{3,1},{4,6},{5,7},{6,4},{7,5},{8,10},{9,11},{10,... | collective-permute-start | bytes 589832 | tf_op jit(solution)/shard_map/ppermute | solution.py:271
  60.9 2.2 %collective-permute-done.22.refs_1_ = bf16[96,1024]{1,0:T(8,128)(2,1)S(1)} collective-permute-done((bf16[96,1024]{1,0:T(8,128)(2,1)S(1)}, bf16[96,1024]{1,0:T(8,128)(2,1)S(1)}, u32[]{:S(2)}, u32[]{:S(2)}) %collective-permute-start.22) | collective-permute-done | bytes 196640 | tf_op jit(solution)/shard_map/ppermute | solution.py:271
  63.2 0.9 %collective-permute-start.28 = (bf16[96,1024]{1,0:T(8,128)(2,1)S(1)}, bf16[96,1024]{1,0:T(8,128)(2,1)S(1)}, u32[]{:S(2)}, u32[]{:S(2)}) collective-permute-start(bf16[96,1024]{1,0:T(8,128)(2,1)S(1)} %total.7), channel_id=1, source_target_pairs={{0,8},{1,9},{2,10},{3,11},{4,12},{5,13},{6,14},{7,15},{8,0},{9,1},... | collective-permute-start | bytes 589832 | tf_op jit(solution)/shard_map/ppermute | solution.py:275
  65.0 1.7 %collective-permute-done.25.refs_1_ = bf16[96,1024]{1,0:T(8,128)(2,1)S(1)} collective-permute-done((bf16[96,1024]{1,0:T(8,128)(2,1)S(1)}, bf16[96,1024]{1,0:T(8,128)(2,1)S(1)}, u32[]{:S(2)}, u32[]{:S(2)}) %collective-permute-start.25) | collective-permute-done | bytes 196640 | tf_op jit(solution)/shard_map/ppermute | solution.py:275
  66.9 1.9 %first_grad.1.refs_2_.first_ref = f32[1024,1024]{1,0:T(8,128)S(1)} custom-call(bf16[1024,384]{1,0:T(8,128)(2,1)S(1)} %get-tuple-element.452.refs_2_.refs_0_, bf16[1024,384]{1,0:T(8,128)(2,1)S(1)} %get-tuple-element.453.refs_3_.refs_1_, bf16[192,1024]{1,0:T(8,128)(2,1)S(1)} %pair.16.refs_2_, bf16[192,1024]{1,0:T(8,128)(2,1)S(1)} %pair.17.refs_3_, ...), custom_call_target="tpu_custom_call" | custom-call | tf_op jit(solution)/shard_map/first_grad/pallas_call | solution.py:437
  68.9 6.3 %collective-permute-done.28.refs_1_ = bf16[96,1024]{1,0:T(8,128)(2,1)S(1)} collective-permute-done((bf16[96,1024]{1,0:T(8,128)(2,1)S(1)}, bf16[96,1024]{1,0:T(8,128)(2,1)S(1)}, u32[]{:S(2)}, u32[]{:S(2)}) %collective-permute-start.28) | collective-permute-done | bytes 196640 | tf_op jit(solution)/shard_map/ppermute | solution.py:275
  75.3 1.4 %combine.1 = bf16[128,1024]{1,0:T(8,128)(2,1)} custom-call(s32[1]{0:T(128)} %bitcast.plane_ref, bf16[128,1024]{1,0:T(8,128)(2,1)S(1)} %copy-done, s32[2,128]{1,0:T(2,128)S(1)} %bitcast.5, s32[2,128]{1,0:T(2,128)S(1)} %bitcast.7, bf16[96,1024]{1,0:T(8,128)(2,1)S(1)} %total.4.refs_0_, bf16[96,1024]{1,0:T(8,128)(2,1)S(1)} %get-tuple-element.470.refs_1_, ...), custom_call_target="tpu_custom_call" | custom-call | tf_op jit(solution)/shard_map/combine/pallas_call | solution.py:502
  77.0 2.7 %last_grad.1 = bf16[1,1024,1024]{2,1,0:T(8,128)(2,1)} custom-call(f32[1024,1024]{1,0:T(8,128)S(1)} %first_grad.1.refs_2_.first_ref, bf16[1024,384]{1,0:T(8,128)(2,1)S(1)} %get-tuple-element.474.refs_1_.refs_0_, bf16[1024,384]{1,0:T(8,128)(2,1)S(1)} %get-tuple-element.475.refs_2_.refs_1_, bf16[192,1024]{1,0:T(8,128)(2,1)S(1)} %pair.18.refs_2_, ...), custom_call_target="tpu_custom_call" | custom-call | tf_op jit(solution)/shard_map/last_grad/pallas_call | solution.py:449
  (87 shorter events, 7.4 us)
Async XLA Ops:
  2.6 11.1 %collective-permute-start = (bf16[96,1024]{1,0:T(8,128)(2,1)S(1)}, bf16[96,1024]{1,0:T(8,128)(2,1)S(1)}, u32[]{:S(2)}, u32[]{:S(2)}) collective-permute-start(bf16[96,1024]{1,0:T(8,128)(2,1)S(1)} %get-tuple-element.241), channel_id=1, source_target_pairs={{0,4},{1,5},{2,6},{3,7},{4,8},{5,9},{6,10},{7,11},{8,12},{9,13},{1... | collective-permute-start | bytes 589832 | tf_op jit(solution)/shard_map/ppermute | solution.py:275
  5.7 10.6 %collective-permute-start.1 = (bf16[96,1024]{1,0:T(8,128)(2,1)S(1)}, bf16[96,1024]{1,0:T(8,128)(2,1)S(1)}, u32[]{:S(2)}, u32[]{:S(2)}) collective-permute-start(bf16[96,1024]{1,0:T(8,128)(2,1)S(1)} %get-tuple-element.242), channel_id=1, source_target_pairs={{0,12},{1,13},{2,14},{3,15},{4,0},{5,1},{6,2},{7,3},{8,4},{9,5},{1... | collective-permute-start | bytes 589832 | tf_op jit(solution)/shard_map/ppermute | solution.py:275
  7.8 8.5 %collective-permute-start.2 = (bf16[96,1024]{1,0:T(8,128)(2,1)S(1)}, bf16[96,1024]{1,0:T(8,128)(2,1)S(1)}, u32[]{:S(2)}, u32[]{:S(2)}) collective-permute-start(bf16[96,1024]{1,0:T(8,128)(2,1)S(1)} %get-tuple-element.274.first_ref), channel_id=1, source_target_pairs={{0,2},{1,3},{2,0},{3,1},{4,6},{5,7},{6,4},{7,5},{8,10},{9,11},{10,... | collective-permute-start | bytes 589832 | tf_op jit(solution)/shard_map/ppermute | solution.py:271
  12.3 12.9 %collective-permute-start.4 = (bf16[96,1024]{1,0:T(8,128)(2,1)S(1)}, bf16[96,1024]{1,0:T(8,128)(2,1)S(1)}, u32[]{:S(2)}, u32[]{:S(2)}) collective-permute-start(bf16[96,1024]{1,0:T(8,128)(2,1)S(1)} %get-tuple-element.254), channel_id=1, source_target_pairs={{0,8},{1,9},{2,10},{3,11},{4,12},{5,13},{6,14},{7,15},{8,0},{9,1},... | collective-permute-start | bytes 589832 | tf_op jit(solution)/shard_map/ppermute | solution.py:275
  13.2 6.2 %collective-permute-start.5 = (bf16[96,1024]{1,0:T(8,128)(2,1)S(1)}, bf16[96,1024]{1,0:T(8,128)(2,1)S(1)}, u32[]{:S(2)}, u32[]{:S(2)}) collective-permute-start(bf16[96,1024]{1,0:T(8,128)(2,1)S(1)} %get-tuple-element.430.first_ref), channel_id=1, source_target_pairs={{0,2},{1,3},{2,0},{3,1},{4,6},{5,7},{6,4},{7,5},{8,10},{9,11},{10,... | collective-permute-start | bytes 589832 | tf_op jit(solution)/shard_map/ppermute | solution.py:271
  16.2 9.0 %collective-permute-start.3 = (bf16[96,1024]{1,0:T(8,128)(2,1)S(1)}, bf16[96,1024]{1,0:T(8,128)(2,1)S(1)}, u32[]{:S(2)}, u32[]{:S(2)}) collective-permute-start(bf16[96,1024]{1,0:T(8,128)(2,1)S(1)} %get-tuple-element.306.first_ref), channel_id=1, source_target_pairs={{0,2},{1,3},{2,0},{3,1},{4,6},{5,7},{6,4},{7,5},{8,10},{9,11},{10,... | collective-permute-start | bytes 589832 | tf_op jit(solution)/shard_map/ppermute | solution.py:271
  17.8 1.8 %collective-permute-start.6 = (bf16[192,1024]{1,0:T(8,128)(2,1)S(1)}, bf16[192,1024]{1,0:T(8,128)(2,1)S(1)}, u32[]{:S(2)}, u32[]{:S(2)}) collective-permute-start(bf16[192,1024]{1,0:T(8,128)(2,1)S(1)} %pair.10.refs_0_), channel_id=1, source_target_pairs={{0,1},{1,0},{2,3},{3,2},{4,5},{5,4},{6,7},{7,6},{8,9},{9,8},{10,11... | collective-permute-start | bytes 1179656 | tf_op jit(solution)/shard_map/ppermute | solution.py:271
  19.6 11.2 %collective-permute-start.10 = (bf16[96,1024]{1,0:T(8,128)(2,1)S(1)}, bf16[96,1024]{1,0:T(8,128)(2,1)S(1)}, u32[]{:S(2)}, u32[]{:S(2)}) collective-permute-start(bf16[96,1024]{1,0:T(8,128)(2,1)S(1)} %get-tuple-element.328.first_ref), channel_id=1, source_target_pairs={{0,2},{1,3},{2,0},{3,1},{4,6},{5,7},{6,4},{7,5},{8,10},{9,11},{10,... | collective-permute-start | bytes 589832 | tf_op jit(solution)/shard_map/ppermute | solution.py:271
  25.2 11.3 %collective-permute-start.7 = (bf16[96,1024]{1,0:T(8,128)(2,1)S(1)}, bf16[96,1024]{1,0:T(8,128)(2,1)S(1)}, u32[]{:S(2)}, u32[]{:S(2)}) collective-permute-start(bf16[96,1024]{1,0:T(8,128)(2,1)S(1)} %get-tuple-element.345.first_ref), channel_id=1, source_target_pairs={{0,2},{1,3},{2,0},{3,1},{4,6},{5,7},{6,4},{7,5},{8,10},{9,11},{10,... | collective-permute-start | bytes 589832 | tf_op jit(solution)/shard_map/ppermute | solution.py:271
  26.8 9.8 %collective-permute-start.8 = (bf16[96,1024]{1,0:T(8,128)(2,1)S(1)}, bf16[96,1024]{1,0:T(8,128)(2,1)S(1)}, u32[]{:S(2)}, u32[]{:S(2)}) collective-permute-start(bf16[96,1024]{1,0:T(8,128)(2,1)S(1)} %get-tuple-element.295), channel_id=1, source_target_pairs={{0,4},{1,5},{2,6},{3,7},{4,8},{5,9},{6,10},{7,11},{8,12},{9,13},{1... | collective-permute-start | bytes 589832 | tf_op jit(solution)/shard_map/ppermute | solution.py:275
  27.9 11.2 %collective-permute-start.9 = (bf16[96,1024]{1,0:T(8,128)(2,1)S(1)}, bf16[96,1024]{1,0:T(8,128)(2,1)S(1)}, u32[]{:S(2)}, u32[]{:S(2)}) collective-permute-start(bf16[96,1024]{1,0:T(8,128)(2,1)S(1)} %get-tuple-element.296), channel_id=1, source_target_pairs={{0,12},{1,13},{2,14},{3,15},{4,0},{5,1},{6,2},{7,3},{8,4},{9,5},{1... | collective-permute-start | bytes 589832 | tf_op jit(solution)/shard_map/ppermute | solution.py:275
  30.7 2.4 %collective-permute-start.11 = (bf16[384,1024]{1,0:T(8,128)(2,1)S(1)}, bf16[384,1024]{1,0:T(8,128)(2,1)S(1)}, u32[]{:S(2)}, u32[]{:S(2)}) collective-permute-start(bf16[384,1024]{1,0:T(8,128)(2,1)S(1)} %pair.12), channel_id=1, source_target_pairs={{0,1},{1,0},{2,3},{3,2},{4,5},{5,4},{6,7},{7,6},{8,9},{9,8},{10,11... | collective-permute-start | bytes 2359304 | tf_op jit(solution)/shard_map/ppermute | solution.py:271
  33.1 6.0 %collective-permute-start.12 = (bf16[192,1024]{1,0:T(8,128)(2,1)S(1)}, bf16[192,1024]{1,0:T(8,128)(2,1)S(1)}, u32[]{:S(2)}, u32[]{:S(2)}) collective-permute-start(bf16[192,1024]{1,0:T(8,128)(2,1)S(1)} %pair.13.refs_0_), channel_id=1, source_target_pairs={{0,1},{1,0},{2,3},{3,2},{4,5},{5,4},{6,7},{7,6},{8,9},{9,8},{10,11... | collective-permute-start | bytes 1179656 | tf_op jit(solution)/shard_map/ppermute | solution.py:271
  33.4 10.5 %collective-permute-start.15 = (bf16[96,1024]{1,0:T(8,128)(2,1)S(1)}, bf16[96,1024]{1,0:T(8,128)(2,1)S(1)}, u32[]{:S(2)}, u32[]{:S(2)}) collective-permute-start(bf16[96,1024]{1,0:T(8,128)(2,1)S(1)} %fold.4), channel_id=1, source_target_pairs={{0,2},{1,3},{2,0},{3,1},{4,6},{5,7},{6,4},{7,5},{8,10},{9,11},{10,... | collective-permute-start | bytes 589832 | tf_op jit(solution)/shard_map/ppermute | solution.py:271
  39.0 9.8 %collective-permute-start.13 = (bf16[96,1024]{1,0:T(8,128)(2,1)S(1)}, bf16[96,1024]{1,0:T(8,128)(2,1)S(1)}, u32[]{:S(2)}, u32[]{:S(2)}) collective-permute-start(bf16[96,1024]{1,0:T(8,128)(2,1)S(1)} %get-tuple-element.448.first_ref), channel_id=1, source_target_pairs={{0,2},{1,3},{2,0},{3,1},{4,6},{5,7},{6,4},{7,5},{8,10},{9,11},{10,... | collective-permute-start | bytes 589832 | tf_op jit(solution)/shard_map/ppermute | solution.py:271
  39.5 11.3 %collective-permute-start.14 = (bf16[96,1024]{1,0:T(8,128)(2,1)S(1)}, bf16[96,1024]{1,0:T(8,128)(2,1)S(1)}, u32[]{:S(2)}, u32[]{:S(2)}) collective-permute-start(bf16[96,1024]{1,0:T(8,128)(2,1)S(1)} %land.14), channel_id=1, source_target_pairs={{0,8},{1,9},{2,10},{3,11},{4,12},{5,13},{6,14},{7,15},{8,0},{9,1},... | collective-permute-start | bytes 589832 | tf_op jit(solution)/shard_map/ppermute | solution.py:275
  41.2 2.7 %collective-permute-start.16 = (bf16[384,1024]{1,0:T(8,128)(2,1)S(1)}, bf16[384,1024]{1,0:T(8,128)(2,1)S(1)}, u32[]{:S(2)}, u32[]{:S(2)}) collective-permute-start(bf16[384,1024]{1,0:T(8,128)(2,1)S(1)} %pair.15), channel_id=1, source_target_pairs={{0,1},{1,0},{2,3},{3,2},{4,5},{5,4},{6,7},{7,6},{8,9},{9,8},{10,11... | collective-permute-start | bytes 2359304 | tf_op jit(solution)/shard_map/ppermute | solution.py:271
  43.9 7.0 %collective-permute-start.17 = (bf16[192,1024]{1,0:T(8,128)(2,1)S(1)}, bf16[192,1024]{1,0:T(8,128)(2,1)S(1)}, u32[]{:S(2)}, u32[]{:S(2)}) collective-permute-start(bf16[192,1024]{1,0:T(8,128)(2,1)S(1)} %get-tuple-element.377), channel_id=1, source_target_pairs={{0,1},{1,0},{2,3},{3,2},{4,5},{5,4},{6,7},{7,6},{8,9},{9,8},{10,11... | collective-permute-start | bytes 1179656 | tf_op jit(solution)/shard_map/ppermute | solution.py:271
  44.6 8.0 %collective-permute-start.18 = (bf16[96,1024]{1,0:T(8,128)(2,1)S(1)}, bf16[96,1024]{1,0:T(8,128)(2,1)S(1)}, u32[]{:S(2)}, u32[]{:S(2)}) collective-permute-start(bf16[96,1024]{1,0:T(8,128)(2,1)S(1)} %fold.5), channel_id=1, source_target_pairs={{0,2},{1,3},{2,0},{3,1},{4,6},{5,7},{6,4},{7,5},{8,10},{9,11},{10,... | collective-permute-start | bytes 589832 | tf_op jit(solution)/shard_map/ppermute | solution.py:271
  48.8 3.8 %collective-permute-start.19 = (bf16[192,1024]{1,0:T(8,128)(2,1)S(1)}, bf16[192,1024]{1,0:T(8,128)(2,1)S(1)}, u32[]{:S(2)}, u32[]{:S(2)}) collective-permute-start(bf16[192,1024]{1,0:T(8,128)(2,1)S(1)} %get-tuple-element.395), channel_id=1, source_target_pairs={{0,1},{1,0},{2,3},{3,2},{4,5},{5,4},{6,7},{7,6},{8,9},{9,8},{10,11... | collective-permute-start | bytes 1179656 | tf_op jit(solution)/shard_map/ppermute | solution.py:271
  51.0 7.9 %collective-permute-start.20 = (bf16[96,1024]{1,0:T(8,128)(2,1)S(1)}, bf16[96,1024]{1,0:T(8,128)(2,1)S(1)}, u32[]{:S(2)}, u32[]{:S(2)}) collective-permute-start(bf16[96,1024]{1,0:T(8,128)(2,1)S(1)} %fold.6), channel_id=1, source_target_pairs={{0,2},{1,3},{2,0},{3,1},{4,6},{5,7},{6,4},{7,5},{8,10},{9,11},{10,... | collective-permute-start | bytes 589832 | tf_op jit(solution)/shard_map/ppermute | solution.py:271
  52.7 10.5 %collective-permute-start.22 = (bf16[96,1024]{1,0:T(8,128)(2,1)S(1)}, bf16[96,1024]{1,0:T(8,128)(2,1)S(1)}, u32[]{:S(2)}, u32[]{:S(2)}) collective-permute-start(bf16[96,1024]{1,0:T(8,128)(2,1)S(1)} %fold.7), channel_id=1, source_target_pairs={{0,2},{1,3},{2,0},{3,1},{4,6},{5,7},{6,4},{7,5},{8,10},{9,11},{10,... | collective-permute-start | bytes 589832 | tf_op jit(solution)/shard_map/ppermute | solution.py:271
  53.3 9.8 %collective-permute-start.21 = (bf16[96,1024]{1,0:T(8,128)(2,1)S(1)}, bf16[96,1024]{1,0:T(8,128)(2,1)S(1)}, u32[]{:S(2)}, u32[]{:S(2)}) collective-permute-start(bf16[96,1024]{1,0:T(8,128)(2,1)S(1)} %total.5), channel_id=1, source_target_pairs={{0,12},{1,13},{2,14},{3,15},{4,0},{5,1},{6,2},{7,3},{8,4},{9,5},{1... | collective-permute-start | bytes 589832 | tf_op jit(solution)/shard_map/ppermute | solution.py:275
  59.0 7.7 %collective-permute-start.25 = (bf16[96,1024]{1,0:T(8,128)(2,1)S(1)}, bf16[96,1024]{1,0:T(8,128)(2,1)S(1)}, u32[]{:S(2)}, u32[]{:S(2)}) collective-permute-start(bf16[96,1024]{1,0:T(8,128)(2,1)S(1)} %total.6), channel_id=1, source_target_pairs={{0,4},{1,5},{2,6},{3,7},{4,8},{5,9},{6,10},{7,11},{8,12},{9,13},{1... | collective-permute-start | bytes 589832 | tf_op jit(solution)/shard_map/ppermute | solution.py:275
  59.3 7.5 %collective-permute-start.24 = (bf16[96,1024]{1,0:T(8,128)(2,1)S(1)}, bf16[96,1024]{1,0:T(8,128)(2,1)S(1)}, u32[]{:S(2)}, u32[]{:S(2)}) collective-permute-start(bf16[96,1024]{1,0:T(8,128)(2,1)S(1)} %get-tuple-element.465.first_ref), channel_id=1, source_target_pairs={{0,2},{1,3},{2,0},{3,1},{4,6},{5,7},{6,4},{7,5},{8,10},{9,11},{10,... | collective-permute-start | bytes 589832 | tf_op jit(solution)/shard_map/ppermute | solution.py:271
  60.9 2.3 %collective-permute-start.23 = (bf16[192,1024]{1,0:T(8,128)(2,1)S(1)}, bf16[192,1024]{1,0:T(8,128)(2,1)S(1)}, u32[]{:S(2)}, u32[]{:S(2)}) collective-permute-start(bf16[192,1024]{1,0:T(8,128)(2,1)S(1)} %pair.16.refs_2_), channel_id=1, source_target_pairs={{0,1},{1,0},{2,3},{3,2},{4,5},{5,4},{6,7},{7,6},{8,9},{9,8},{10,11... | collective-permute-start | bytes 1179656 | tf_op jit(solution)/shard_map/ppermute | solution.py:271
  63.2 11.9 %collective-permute-start.28 = (bf16[96,1024]{1,0:T(8,128)(2,1)S(1)}, bf16[96,1024]{1,0:T(8,128)(2,1)S(1)}, u32[]{:S(2)}, u32[]{:S(2)}) collective-permute-start(bf16[96,1024]{1,0:T(8,128)(2,1)S(1)} %total.7), channel_id=1, source_target_pairs={{0,8},{1,9},{2,10},{3,11},{4,12},{5,13},{6,14},{7,15},{8,0},{9,1},... | collective-permute-start | bytes 589832 | tf_op jit(solution)/shard_map/ppermute | solution.py:275
  64.2 11.0 %collective-permute-start.27 = (bf16[96,1024]{1,0:T(8,128)(2,1)S(1)}, bf16[96,1024]{1,0:T(8,128)(2,1)S(1)}, u32[]{:S(2)}, u32[]{:S(2)}) collective-permute-start(bf16[96,1024]{1,0:T(8,128)(2,1)S(1)} %get-tuple-element.477.first_ref), channel_id=1, source_target_pairs={{0,2},{1,3},{2,0},{3,1},{4,6},{5,7},{6,4},{7,5},{8,10},{9,11},{10,... | collective-permute-start | bytes 589832 | tf_op jit(solution)/shard_map/ppermute | solution.py:271
  64.9 1.8 %collective-permute-start.26 = (bf16[192,1024]{1,0:T(8,128)(2,1)S(1)}, bf16[192,1024]{1,0:T(8,128)(2,1)S(1)}, u32[]{:S(2)}, u32[]{:S(2)}) collective-permute-start(bf16[192,1024]{1,0:T(8,128)(2,1)S(1)} %pair.17.refs_3_), channel_id=1, source_target_pairs={{0,1},{1,0},{2,3},{3,2},{4,5},{5,4},{6,7},{7,6},{8,9},{9,8},{10,11... | collective-permute-start | bytes 1179656 | tf_op jit(solution)/shard_map/ppermute | solution.py:271
  66.8 8.4 %collective-permute-start.29 = (bf16[192,1024]{1,0:T(8,128)(2,1)S(1)}, bf16[192,1024]{1,0:T(8,128)(2,1)S(1)}, u32[]{:S(2)}, u32[]{:S(2)}) collective-permute-start(bf16[192,1024]{1,0:T(8,128)(2,1)S(1)} %pair.18.refs_2_), channel_id=1, source_target_pairs={{0,1},{1,0},{2,3},{3,2},{4,5},{5,4},{6,7},{7,6},{8,9},{9,8},{10,11... | collective-permute-start | bytes 1179656 | tf_op jit(solution)/shard_map/ppermute | solution.py:271
  68.8 6.5 %copy-start = (bf16[128,1024]{1,0:T(8,128)(2,1)S(1)}, bf16[128,1024]{1,0:T(8,128)(2,1)}, u32[]{:S(2)}) copy-start(bf16[128,1024]{1,0:T(8,128)(2,1)} %tokens_ref.1) | copy-start | bytes 786436
  75.2 1.8 %collective-permute-start.30 = (bf16[192,1024]{1,0:T(8,128)(2,1)S(1)}, bf16[192,1024]{1,0:T(8,128)(2,1)S(1)}, u32[]{:S(2)}, u32[]{:S(2)}) collective-permute-start(bf16[192,1024]{1,0:T(8,128)(2,1)S(1)} %pair.19.refs_3_), channel_id=1, source_target_pairs={{0,1},{1,0},{2,3},{3,2},{4,5},{5,4},{6,7},{7,6},{8,9},{9,8},{10,11... | collective-permute-start | bytes 1179656 | tf_op jit(solution)/shard_map/ppermute | solution.py:271
  (2 other events, 12.9 us)

commit v18 on v16

--- a/solution.py
+++ b/solution.py
@@ -14,17 +14,17 @@
     ("yC0 zN3", "zN1 zN2 yN0"),
     ("cN0 yN1", "yC0 cN0"),
     ("ffnN0 yN2", "yN1 zN3"),
-    ("cR0N1 yN3 zC1 zC2", "yN2 cR0N1"),
-    ("ffnN1 cN2 yR0", "yN3 zC1 zC2 cN2"),
-    ("cR1N3 ffnN2 yC1 zC3", "yR0 cR1N3"),
-    ("cR2 ffnN3 yR1 totalR0", "yC1 zC3 cR2"),
-    ("cR3 yR2", "yR1"),
+    ("cR0N1 yN3 zC3", "yN2 cR0N1"),
+    ("ffnN1 cN2 yR0", "yN3 zC3 cN2"),
+    ("cR1N3 ffnN2 yC3 zC1", "yR0 cR1N3"),
+    ("cR2 ffnN3 yR1 zC2 totalR0", "zC1 yC3 cR2"),
+    ("cR3 yR2", "yR1 zC2"),
     ("totalR1 zR1", "cR3"),
     ("yR3 cC0", "yR2 cC0"),
-    ("totalR2 zR2 yC2", "yR3 zR1"),
-    ("totalR3 zR3 yC3 cC1", "yC2 zR2 cC1"),
-    ("cC2 gradC0", "yC3 zR3 cC2"),
-    ("cC3", None),
+    ("totalR2 zR2 yC1", "zR1 yR3"),
+    ("totalR3 zR3 yC2 cC3", "yC1 zR2 cC3"),
+    ("cC1 gradC0", "yC2 zR3 cC1"),
+    ("cC2", None),
 )
 TILE = 256
 LINK_WORK = 10 << 30
@@ -467,8 +467,8 @@
         "total": lambda kind, g: total(g),
         "load": lambda kind, g: load(),
         "grad": lambda kind, g: first_grad(
-            [(0,), (1,)],
-            [("C", "own", (0,)), ("C", "own", (1,)), ("c", "C", 0), ("c", "C", 1)],
+            [(0,), (3,), (1,)],
+            [("C", "own", (i,)) for i in (0, 3, 1)] + [("c", "C", i) for i in (0, 3)],
         ),
     }
     def name_of(act):
@@ -494,11 +494,10 @@
         if lands is None:
             break
         land(*map(name_of, lands.split()), earlier=kernels)
-    if ("c", ("C", 3)) in flying:
-        live["c", "C", 3] = flying.pop(("c", ("C", 3)))
+    live["c", "C", 2] = flying.pop(("c", ("C", 2)))
     grad_down = last_grad(
-        [(2,), (3,)],
-        [("C", "own", (2,)), ("C", "own", (3,)), ("c", "C", 2), ("c", "C", 3)],
+        [(1,), (2,)],
+        [("C", "own", (2,)), ("c", "C", 1), ("c", "C", 2)],
     )
     mixed = call(
         functools.partial(combine_kernel, experts),

time: 79.9 us -> 80.2 us (level)
  starting transfers between devices: 29.3 us -> 27 us
  waiting for transfers between devices: 27.1 us -> 29.2 us
    ppermute x22, waiting for transfers between devices: 10.7 us -> 14.6 us  [swap(): lax.ppermute(value, 'expert', [(i, i ^ mask) for i in range(devices)])]
    ppermute x22, starting transfers between devices: 15 us -> 12 us  [swap(): lax.ppermute(value, 'expert', [(i, i ^ mask) for i in range(devices)])]
    ppermute x9, waiting for transfers between devices: 16.4 us -> 14.6 us  [turn(): return lax.ppermute(value, 'expert', to)]
  transfers between devices with their start and end apart: 31 -> 31, of which waited for: 13 -> 13; matrix products, arithmetic and copies ran while one was open for 0% -> 0% of each run, Pallas kernels for 22% -> 23%
where the time goes in v18:
time: 80.2 us; the launch traced here: 80.1 us
  waiting for transfers between devices  29.2 us (36%)
  starting transfers between devices  27 us (34%)
  Pallas kernels  22.6 us (28%)
  between operations  1.21 us (2%)
    ppermute x9, starting transfers between devices, turn(): return lax.ppermute(value, 'expert', to)  15 us
    ppermute x22, waiting for transfers between devices, swap(): lax.ppermute(value, 'expert', [(i, i ^ mask) for i in range(devices)])  14.6 us
    ppermute x9, waiting for transfers between devices, turn(): return lax.ppermute(value, 'expert', to)  14.6 us
    ppermute x22, starting transfers between devices, swap(): lax.ppermute(value, 'expert', [(i, i ^ mask) for i in range(devices)])  12 us
    pallas_call x4, Pallas kernels, ffn(): call(functools.partial(ffn_kernel, len(pieces)), 24, 'ffn', out_shape=[ja...  10.5 us
    pallas_call x1, Pallas kernels, load(): call(load_kernel, 16, 'load', out_shape=[weight, weight, jax.ShapeDtypeSt...  2.88 us
    pallas_call x1, Pallas kernels, last_grad(): call(functools.partial(last_grad_kernel, plan), 24, 'last_grad', out_shap...  2.66 us
    pallas_call x1, Pallas kernels, first_grad(): call(functools.partial(first_grad_kernel, plan), 24, 'first_grad', out_sh...  2.4 us
  transfers between devices with their start and end apart: 31, of which 13 were waited for; matrix products, arithmetic and copies ran while one was open for 0% of the time, Pallas kernels for 23%

profile of v18, /device:TPU:0, one launch (start us, length us, event | category | flops | bytes accessed | tf_op | source)
XLA Modules:
  0.0 80.1 jit_solution(2514224419192385792)
XLA Ops:
  0.6 1.9 %send.1 = (bf16[96,1024]{1,0:T(8,128)(2,1)S(1)}, bf16[96,1024]{1,0:T(8,128)(2,1)S(1)}, bf16[96,1024]{1,0:T(8,128)(2,1)S(1)}, bf16[96,1024]{1,0:T(8,128)(2,1)S(1)...) custom-call(s32[1]{0:T(128)} %bitcast.plane_ref, ...), custom_call_target="tpu_custom_call" | custom-call | tf_op jit(solution)/shard_map/send/pallas_call | solution.py:388
  2.6 3.1 %collective-permute-start = (bf16[96,1024]{1,0:T(8,128)(2,1)S(1)}, bf16[96,1024]{1,0:T(8,128)(2,1)S(1)}, u32[]{:S(2)}, u32[]{:S(2)}) collective-permute-start(bf16[96,1024]{1,0:T(8,128)(2,1)S(1)} %get-tuple-element.255), channel_id=1, source_target_pairs={{0,4},{1,5},{2,6},{3,7},{4,8},{5,9},{6,10},{7,11},{8,12},{9,13},{1... | collective-permute-start | bytes 589832 | tf_op jit(solution)/shard_map/ppermute | solution.py:276
  5.7 2.1 %collective-permute-start.1 = (bf16[96,1024]{1,0:T(8,128)(2,1)S(1)}, bf16[96,1024]{1,0:T(8,128)(2,1)S(1)}, u32[]{:S(2)}, u32[]{:S(2)}) collective-permute-start(bf16[96,1024]{1,0:T(8,128)(2,1)S(1)} %get-tuple-element.256), channel_id=1, source_target_pairs={{0,12},{1,13},{2,14},{3,15},{4,0},{5,1},{6,2},{7,3},{8,4},{9,5},{1... | collective-permute-start | bytes 589832 | tf_op jit(solution)/shard_map/ppermute | solution.py:276
  7.8 1.7 %collective-permute-start.2 = (bf16[96,1024]{1,0:T(8,128)(2,1)S(1)}, bf16[96,1024]{1,0:T(8,128)(2,1)S(1)}, u32[]{:S(2)}, u32[]{:S(2)}) collective-permute-start(bf16[96,1024]{1,0:T(8,128)(2,1)S(1)} %get-tuple-element.288.first_ref), channel_id=1, source_target_pairs={{0,2},{1,3},{2,0},{3,1},{4,6},{5,7},{6,4},{7,5},{8,10},{9,11},{10,... | collective-permute-start | bytes 589832 | tf_op jit(solution)/shard_map/ppermute | solution.py:272
  9.4 2.9 %load.1 = (bf16[1024,1024]{1,0:T(8,128)(2,1)S(1)}, bf16[1024,1024]{1,0:T(8,128)(2,1)S(1)}, bf16[1024,1024]{1,0:T(8,128)(2,1)S(1)}) custom-call(bf16[1,1024,1024]{2,1,0:T(8,128)(2,1)} %refs_0_.2, bf16[1,1024,1024]{2,1,0:T(8,128)(2,1)} %refs_1_.3, bf16[1,1024,1024]{2,1,0:T(8,128)(2,1)} %refs_2_.1), custom_call_target="tpu_custom_call" | custom-call | tf_op jit(solution)/shard_map/load/pallas_call | solution.py:403
  12.3 0.9 %collective-permute-start.4 = (bf16[96,1024]{1,0:T(8,128)(2,1)S(1)}, bf16[96,1024]{1,0:T(8,128)(2,1)S(1)}, u32[]{:S(2)}, u32[]{:S(2)}) collective-permute-start(bf16[96,1024]{1,0:T(8,128)(2,1)S(1)} %get-tuple-element.268), channel_id=1, source_target_pairs={{0,8},{1,9},{2,10},{3,11},{4,12},{5,13},{6,14},{7,15},{8,0},{9,1},... | collective-permute-start | bytes 589832 | tf_op jit(solution)/shard_map/ppermute | solution.py:276
  13.7 2.5 %collective-permute-done.1.refs_1_ = bf16[96,1024]{1,0:T(8,128)(2,1)S(1)} collective-permute-done((bf16[96,1024]{1,0:T(8,128)(2,1)S(1)}, bf16[96,1024]{1,0:T(8,128)(2,1)S(1)}, u32[]{:S(2)}, u32[]{:S(2)}) %collective-permute-start.1) | collective-permute-done | bytes 196640 | tf_op jit(solution)/shard_map/ppermute | solution.py:276
  16.2 1.5 %collective-permute-start.3 = (bf16[96,1024]{1,0:T(8,128)(2,1)S(1)}, bf16[96,1024]{1,0:T(8,128)(2,1)S(1)}, u32[]{:S(2)}, u32[]{:S(2)}) collective-permute-start(bf16[96,1024]{1,0:T(8,128)(2,1)S(1)} %get-tuple-element.319.first_ref), channel_id=1, source_target_pairs={{0,2},{1,3},{2,0},{3,1},{4,6},{5,7},{6,4},{7,5},{8,10},{9,11},{10,... | collective-permute-start | bytes 589832 | tf_op jit(solution)/shard_map/ppermute | solution.py:272
  17.9 1.5 %collective-permute-done.5.refs_0_ = bf16[96,1024]{1,0:T(8,128)(2,1)S(1)} collective-permute-done((bf16[96,1024]{1,0:T(8,128)(2,1)S(1)}, bf16[96,1024]{1,0:T(8,128)(2,1)S(1)}, u32[]{:S(2)}, u32[]{:S(2)}) %collective-permute-start.5) | collective-permute-done | bytes 196640 | tf_op jit(solution)/shard_map/ppermute | solution.py:272
  19.6 0.5 collective-permute-start.7
  20.1 2.6 %ffn.4 = (bf16[1024,384]{1,0:T(8,128)(2,1)S(1)}, bf16[192,1024]{1,0:T(8,128)(2,1)S(1)}, bf16[192,1024]{1,0:T(8,128)(2,1)S(1)}) custom-call(bf16[192,1024]{1,0:T(8,128)(2,1)S(1)} %pair.10.refs_0_, bf16[192,1024]{1,0:T(8,128)(2,1)S(1)} %land_core.8.refs_1_, bf16[1024,1024]{1,0:T(8,128)(2,1)S(1)} %get-tuple-element.371.refs_2_, ...), custom_call_target="tpu_custom_call" | custom-call | tf_op jit(solution)/shard_map/ffn/pallas_call | solution.py:370
  22.7 2.5 %collective-permute-done.4.refs_1_ = bf16[96,1024]{1,0:T(8,128)(2,1)S(1)} collective-permute-done((bf16[96,1024]{1,0:T(8,128)(2,1)S(1)}, bf16[96,1024]{1,0:T(8,128)(2,1)S(1)}, u32[]{:S(2)}, u32[]{:S(2)}) %collective-permute-start.4) | collective-permute-done | bytes 196640 | tf_op jit(solution)/shard_map/ppermute | solution.py:276
  25.2 3.1 %collective-permute-start.10 = (bf16[96,1024]{1,0:T(8,128)(2,1)S(1)}, bf16[96,1024]{1,0:T(8,128)(2,1)S(1)}, u32[]{:S(2)}, u32[]{:S(2)}) collective-permute-start(bf16[96,1024]{1,0:T(8,128)(2,1)S(1)} %land.15), channel_id=1, source_target_pairs={{0,8},{1,9},{2,10},{3,11},{4,12},{5,13},{6,14},{7,15},{8,0},{9,1},... | collective-permute-start | bytes 589832 | tf_op jit(solution)/shard_map/ppermute | solution.py:276
  28.4 1.5 %collective-permute-start.9 = (bf16[96,1024]{1,0:T(8,128)(2,1)S(1)}, bf16[96,1024]{1,0:T(8,128)(2,1)S(1)}, u32[]{:S(2)}, u32[]{:S(2)}) collective-permute-start(bf16[96,1024]{1,0:T(8,128)(2,1)S(1)} %get-tuple-element.359.first_ref), channel_id=1, source_target_pairs={{0,2},{1,3},{2,0},{3,1},{4,6},{5,7},{6,4},{7,5},{8,10},{9,11},{10,... | collective-permute-start | bytes 589832 | tf_op jit(solution)/shard_map/ppermute | solution.py:272
  30.1 2.3 %collective-permute-done.8.refs_0_ = bf16[384,1024]{1,0:T(8,128)(2,1)S(1)} collective-permute-done((bf16[384,1024]{1,0:T(8,128)(2,1)S(1)}, bf16[384,1024]{1,0:T(8,128)(2,1)S(1)}, u32[]{:S(2)}, u32[]{:S(2)}) %collective-permute-start.8) | collective-permute-done | bytes 786464 | tf_op jit(solution)/shard_map/ppermute | solution.py:272
  32.7 0.6 collective-permute-start.14
  33.3 2.6 %ffn.5 = (bf16[1024,384]{1,0:T(8,128)(2,1)S(1)}, bf16[192,1024]{1,0:T(8,128)(2,1)S(1)}, bf16[192,1024]{1,0:T(8,128)(2,1)S(1)}) custom-call(bf16[192,1024]{1,0:T(8,128)(2,1)S(1)} %pair.11.second_ref.refs_0_, bf16[192,1024]{1,0:T(8,128)(2,1)S(1)} %get-tuple-element.327.refs_1_, bf16[1024,1024]{1,0:T(8,128)(2,1)S(1)} %get-tuple-element.371.refs_2_, ...), custom_call_target="tpu_custom_call" | custom-call | tf_op jit(solution)/shard_map/ffn/pallas_call | solution.py:370
  36.3 1.7 %collective-permute-start.13 = (bf16[96,1024]{1,0:T(8,128)(2,1)S(1)}, bf16[96,1024]{1,0:T(8,128)(2,1)S(1)}, u32[]{:S(2)}, u32[]{:S(2)}) collective-permute-start(bf16[96,1024]{1,0:T(8,128)(2,1)S(1)} %get-tuple-element.477.first_ref), channel_id=1, source_target_pairs={{0,2},{1,3},{2,0},{3,1},{4,6},{5,7},{6,4},{7,5},{8,10},{9,11},{10,... | collective-permute-start | bytes 589832 | tf_op jit(solution)/shard_map/ppermute | solution.py:272
  38.2 2.6 %ffn.6 = (bf16[1024,384]{1,0:T(8,128)(2,1)S(1)}, bf16[192,1024]{1,0:T(8,128)(2,1)S(1)}, bf16[192,1024]{1,0:T(8,128)(2,1)S(1)}) custom-call(bf16[192,1024]{1,0:T(8,128)(2,1)S(1)} %pair.13.refs_0_, bf16[192,1024]{1,0:T(8,128)(2,1)S(1)} %land_core.10.refs_1_, bf16[1024,1024]{1,0:T(8,128)(2,1)S(1)} %get-tuple-element.371.refs_2_, ...), custom_call_target="tpu_custom_call" | custom-call | tf_op jit(solution)/shard_map/ffn/pallas_call | solution.py:370
  40.8 3.8 %collective-permute-start.18 = (bf16[96,1024]{1,0:T(8,128)(2,1)S(1)}, bf16[96,1024]{1,0:T(8,128)(2,1)S(1)}, u32[]{:S(2)}, u32[]{:S(2)}) collective-permute-start(bf16[96,1024]{1,0:T(8,128)(2,1)S(1)} %get-tuple-element.376), channel_id=1, source_target_pairs={{0,12},{1,13},{2,14},{3,15},{4,0},{5,1},{6,2},{7,3},{8,4},{9,5},{1... | collective-permute-start | bytes 589832 | tf_op jit(solution)/shard_map/ppermute | solution.py:276
  45.4 2.6 %ffn.7 = (bf16[1024,384]{1,0:T(8,128)(2,1)S(1)}, bf16[192,1024]{1,0:T(8,128)(2,1)S(1)}, bf16[192,1024]{1,0:T(8,128)(2,1)S(1)}) custom-call(bf16[192,1024]{1,0:T(8,128)(2,1)S(1)} %pair.14.second_ref.refs_0_, bf16[192,1024]{1,0:T(8,128)(2,1)S(1)} %get-tuple-element.370.refs_1_, bf16[1024,1024]{1,0:T(8,128)(2,1)S(1)} %get-tuple-element.371.refs_2_, ...), custom_call_target="tpu_custom_call" | custom-call | tf_op jit(solution)/shard_map/ffn/pallas_call | solution.py:370
  48.2 1.2 %collective-permute-done.18.refs_1_ = bf16[96,1024]{1,0:T(8,128)(2,1)S(1)} collective-permute-done((bf16[96,1024]{1,0:T(8,128)(2,1)S(1)}, bf16[96,1024]{1,0:T(8,128)(2,1)S(1)}, u32[]{:S(2)}, u32[]{:S(2)}) %collective-permute-start.18) | collective-permute-done | bytes 196640 | tf_op jit(solution)/shard_map/ppermute | solution.py:276
  49.4 2.7 %collective-permute-done.17.refs_0_ = bf16[96,1024]{1,0:T(8,128)(2,1)S(1)} collective-permute-done((bf16[96,1024]{1,0:T(8,128)(2,1)S(1)}, bf16[96,1024]{1,0:T(8,128)(2,1)S(1)}, u32[]{:S(2)}, u32[]{:S(2)}) %collective-permute-start.17) | collective-permute-done | bytes 196640 | tf_op jit(solution)/shard_map/ppermute | solution.py:272
  52.7 1.7 %collective-permute-start.22 = (bf16[96,1024]{1,0:T(8,128)(2,1)S(1)}, bf16[96,1024]{1,0:T(8,128)(2,1)S(1)}, u32[]{:S(2)}, u32[]{:S(2)}) collective-permute-start(bf16[96,1024]{1,0:T(8,128)(2,1)S(1)} %total.5), channel_id=1, source_target_pairs={{0,12},{1,13},{2,14},{3,15},{4,0},{5,1},{6,2},{7,3},{8,4},{9,5},{1... | collective-permute-start | bytes 589832 | tf_op jit(solution)/shard_map/ppermute | solution.py:276
  54.4 1.7 %collective-permute-start.23 = (bf16[96,1024]{1,0:T(8,128)(2,1)S(1)}, bf16[96,1024]{1,0:T(8,128)(2,1)S(1)}, u32[]{:S(2)}, u32[]{:S(2)}) collective-permute-start(bf16[96,1024]{1,0:T(8,128)(2,1)S(1)} %fold.7), channel_id=1, source_target_pairs={{0,2},{1,3},{2,0},{3,1},{4,6},{5,7},{6,4},{7,5},{8,10},{9,11},{10,... | collective-permute-start | bytes 589832 | tf_op jit(solution)/shard_map/ppermute | solution.py:272
  56.2 3.8 %collective-permute-done.20.refs_0_ = bf16[96,1024]{1,0:T(8,128)(2,1)S(1)} collective-permute-done((bf16[96,1024]{1,0:T(8,128)(2,1)S(1)}, bf16[96,1024]{1,0:T(8,128)(2,1)S(1)}, u32[]{:S(2)}, u32[]{:S(2)}) %collective-permute-start.20) | collective-permute-done | bytes 196640 | tf_op jit(solution)/shard_map/ppermute | solution.py:272
  60.5 3.8 %collective-permute-done.23.refs_1_ = bf16[96,1024]{1,0:T(8,128)(2,1)S(1)} collective-permute-done((bf16[96,1024]{1,0:T(8,128)(2,1)S(1)}, bf16[96,1024]{1,0:T(8,128)(2,1)S(1)}, u32[]{:S(2)}, u32[]{:S(2)}) %collective-permute-start.23) | collective-permute-done | bytes 196640 | tf_op jit(solution)/shard_map/ppermute | solution.py:272
  64.8 4.4 %collective-permute-done.25.refs_1_ = bf16[96,1024]{1,0:T(8,128)(2,1)S(1)} collective-permute-done((bf16[96,1024]{1,0:T(8,128)(2,1)S(1)}, bf16[96,1024]{1,0:T(8,128)(2,1)S(1)}, u32[]{:S(2)}, u32[]{:S(2)}) %collective-permute-start.25) | collective-permute-done | bytes 196640 | tf_op jit(solution)/shard_map/ppermute | solution.py:276
  69.3 2.4 %first_grad.1.refs_2_.first_ref = f32[1024,1024]{1,0:T(8,128)S(1)} custom-call(bf16[1024,384]{1,0:T(8,128)(2,1)S(1)} %get-tuple-element.481.refs_2_.refs_0_, bf16[1024,384]{1,0:T(8,128)(2,1)S(1)} %get-tuple-element.484.refs_2_.refs_1_, bf16[1024,384]{1,0:T(8,128)(2,1)S(1)} %get-tuple-element.503.refs_2_.refs_0_, bf16[192,1024]{1,0:T(8,128)(2,1)S(1)} %pair.16.refs_3_, ...), custom_call_target="tpu_custom_call" | custom-call | tf_op jit(solution)/shard_map/first_grad/pallas_call | solution.py:438
  71.8 3.6 %collective-permute-done.28.refs_1_ = bf16[96,1024]{1,0:T(8,128)(2,1)S(1)} collective-permute-done((bf16[96,1024]{1,0:T(8,128)(2,1)S(1)}, bf16[96,1024]{1,0:T(8,128)(2,1)S(1)}, u32[]{:S(2)}, u32[]{:S(2)}) %collective-permute-start.28) | collective-permute-done | bytes 196640 | tf_op jit(solution)/shard_map/ppermute | solution.py:276
  75.6 1.4 %combine.1 = bf16[128,1024]{1,0:T(8,128)(2,1)} custom-call(s32[1]{0:T(128)} %bitcast.plane_ref, bf16[128,1024]{1,0:T(8,128)(2,1)S(1)} %copy-done, s32[2,128]{1,0:T(2,128)S(1)} %bitcast.5, s32[2,128]{1,0:T(2,128)S(1)} %bitcast.7, bf16[96,1024]{1,0:T(8,128)(2,1)S(1)} %total.4.refs_0_, bf16[96,1024]{1,0:T(8,128)(2,1)S(1)} %get-tuple-element.499.refs_1_, ...), custom_call_target="tpu_custom_call" | custom-call | tf_op jit(solution)/shard_map/combine/pallas_call | solution.py:502
  77.3 2.7 %last_grad.1 = bf16[1,1024,1024]{2,1,0:T(8,128)(2,1)} custom-call(f32[1024,1024]{1,0:T(8,128)S(1)} %first_grad.1.refs_2_.first_ref, bf16[1024,384]{1,0:T(8,128)(2,1)S(1)} %get-tuple-element.503.refs_2_.refs_0_, bf16[1024,384]{1,0:T(8,128)(2,1)S(1)} %get-tuple-element.504.refs_1_, bf16[192,1024]{1,0:T(8,128)(2,1)S(1)} %pair.19.refs_2_, ...), custom_call_target="tpu_custom_call" | custom-call | tf_op jit(solution)/shard_map/last_grad/pallas_call | solution.py:450
  (87 shorter events, 4.9 us)
Async XLA Ops:
  2.6 11.1 %collective-permute-start = (bf16[96,1024]{1,0:T(8,128)(2,1)S(1)}, bf16[96,1024]{1,0:T(8,128)(2,1)S(1)}, u32[]{:S(2)}, u32[]{:S(2)}) collective-permute-start(bf16[96,1024]{1,0:T(8,128)(2,1)S(1)} %get-tuple-element.255), channel_id=1, source_target_pairs={{0,4},{1,5},{2,6},{3,7},{4,8},{5,9},{6,10},{7,11},{8,12},{9,13},{1... | collective-permute-start | bytes 589832 | tf_op jit(solution)/shard_map/ppermute | solution.py:276
  5.7 10.6 %collective-permute-start.1 = (bf16[96,1024]{1,0:T(8,128)(2,1)S(1)}, bf16[96,1024]{1,0:T(8,128)(2,1)S(1)}, u32[]{:S(2)}, u32[]{:S(2)}) collective-permute-start(bf16[96,1024]{1,0:T(8,128)(2,1)S(1)} %get-tuple-element.256), channel_id=1, source_target_pairs={{0,12},{1,13},{2,14},{3,15},{4,0},{5,1},{6,2},{7,3},{8,4},{9,5},{1... | collective-permute-start | bytes 589832 | tf_op jit(solution)/shard_map/ppermute | solution.py:276
  7.8 8.5 %collective-permute-start.2 = (bf16[96,1024]{1,0:T(8,128)(2,1)S(1)}, bf16[96,1024]{1,0:T(8,128)(2,1)S(1)}, u32[]{:S(2)}, u32[]{:S(2)}) collective-permute-start(bf16[96,1024]{1,0:T(8,128)(2,1)S(1)} %get-tuple-element.288.first_ref), channel_id=1, source_target_pairs={{0,2},{1,3},{2,0},{3,1},{4,6},{5,7},{6,4},{7,5},{8,10},{9,11},{10,... | collective-permute-start | bytes 589832 | tf_op jit(solution)/shard_map/ppermute | solution.py:272
  12.3 12.9 %collective-permute-start.4 = (bf16[96,1024]{1,0:T(8,128)(2,1)S(1)}, bf16[96,1024]{1,0:T(8,128)(2,1)S(1)}, u32[]{:S(2)}, u32[]{:S(2)}) collective-permute-start(bf16[96,1024]{1,0:T(8,128)(2,1)S(1)} %get-tuple-element.268), channel_id=1, source_target_pairs={{0,8},{1,9},{2,10},{3,11},{4,12},{5,13},{6,14},{7,15},{8,0},{9,1},... | collective-permute-start | bytes 589832 | tf_op jit(solution)/shard_map/ppermute | solution.py:276
  13.2 6.2 %collective-permute-start.5 = (bf16[96,1024]{1,0:T(8,128)(2,1)S(1)}, bf16[96,1024]{1,0:T(8,128)(2,1)S(1)}, u32[]{:S(2)}, u32[]{:S(2)}) collective-permute-start(bf16[96,1024]{1,0:T(8,128)(2,1)S(1)} %get-tuple-element.442.first_ref), channel_id=1, source_target_pairs={{0,2},{1,3},{2,0},{3,1},{4,6},{5,7},{6,4},{7,5},{8,10},{9,11},{10,... | collective-permute-start | bytes 589832 | tf_op jit(solution)/shard_map/ppermute | solution.py:272
  16.2 9.0 %collective-permute-start.3 = (bf16[96,1024]{1,0:T(8,128)(2,1)S(1)}, bf16[96,1024]{1,0:T(8,128)(2,1)S(1)}, u32[]{:S(2)}, u32[]{:S(2)}) collective-permute-start(bf16[96,1024]{1,0:T(8,128)(2,1)S(1)} %get-tuple-element.319.first_ref), channel_id=1, source_target_pairs={{0,2},{1,3},{2,0},{3,1},{4,6},{5,7},{6,4},{7,5},{8,10},{9,11},{10,... | collective-permute-start | bytes 589832 | tf_op jit(solution)/shard_map/ppermute | solution.py:272
  17.8 1.8 %collective-permute-start.6 = (bf16[192,1024]{1,0:T(8,128)(2,1)S(1)}, bf16[192,1024]{1,0:T(8,128)(2,1)S(1)}, u32[]{:S(2)}, u32[]{:S(2)}) collective-permute-start(bf16[192,1024]{1,0:T(8,128)(2,1)S(1)} %pair.10.refs_0_), channel_id=1, source_target_pairs={{0,1},{1,0},{2,3},{3,2},{4,5},{5,4},{6,7},{7,6},{8,9},{9,8},{10,11... | collective-permute-start | bytes 1179656 | tf_op jit(solution)/shard_map/ppermute | solution.py:272
  19.6 10.5 %collective-permute-start.7 = (bf16[96,1024]{1,0:T(8,128)(2,1)S(1)}, bf16[96,1024]{1,0:T(8,128)(2,1)S(1)}, u32[]{:S(2)}, u32[]{:S(2)}) collective-permute-start(bf16[96,1024]{1,0:T(8,128)(2,1)S(1)} %get-tuple-element.342.first_ref), channel_id=1, source_target_pairs={{0,2},{1,3},{2,0},{3,1},{4,6},{5,7},{6,4},{7,5},{8,10},{9,11},{10,... | collective-permute-start | bytes 589832 | tf_op jit(solution)/shard_map/ppermute | solution.py:272
  25.2 11.0 %collective-permute-start.10 = (bf16[96,1024]{1,0:T(8,128)(2,1)S(1)}, bf16[96,1024]{1,0:T(8,128)(2,1)S(1)}, u32[]{:S(2)}, u32[]{:S(2)}) collective-permute-start(bf16[96,1024]{1,0:T(8,128)(2,1)S(1)} %land.15), channel_id=1, source_target_pairs={{0,8},{1,9},{2,10},{3,11},{4,12},{5,13},{6,14},{7,15},{8,0},{9,1},... | collective-permute-start | bytes 589832 | tf_op jit(solution)/shard_map/ppermute | solution.py:276
  28.4 7.8 %collective-permute-start.9 = (bf16[96,1024]{1,0:T(8,128)(2,1)S(1)}, bf16[96,1024]{1,0:T(8,128)(2,1)S(1)}, u32[]{:S(2)}, u32[]{:S(2)}) collective-permute-start(bf16[96,1024]{1,0:T(8,128)(2,1)S(1)} %get-tuple-element.359.first_ref), channel_id=1, source_target_pairs={{0,2},{1,3},{2,0},{3,1},{4,6},{5,7},{6,4},{7,5},{8,10},{9,11},{10,... | collective-permute-start | bytes 589832 | tf_op jit(solution)/shard_map/ppermute | solution.py:272
  30.0 2.4 %collective-permute-start.8 = (bf16[384,1024]{1,0:T(8,128)(2,1)S(1)}, bf16[384,1024]{1,0:T(8,128)(2,1)S(1)}, u32[]{:S(2)}, u32[]{:S(2)}) collective-permute-start(bf16[384,1024]{1,0:T(8,128)(2,1)S(1)} %pair.12), channel_id=1, source_target_pairs={{0,1},{1,0},{2,3},{3,2},{4,5},{5,4},{6,7},{7,6},{8,9},{9,8},{10,11... | collective-permute-start | bytes 2359304 | tf_op jit(solution)/shard_map/ppermute | solution.py:272
  32.4 3.8 %collective-permute-start.11 = (bf16[192,1024]{1,0:T(8,128)(2,1)S(1)}, bf16[192,1024]{1,0:T(8,128)(2,1)S(1)}, u32[]{:S(2)}, u32[]{:S(2)}) collective-permute-start(bf16[192,1024]{1,0:T(8,128)(2,1)S(1)} %pair.13.refs_0_), channel_id=1, source_target_pairs={{0,1},{1,0},{2,3},{3,2},{4,5},{5,4},{6,7},{7,6},{8,9},{9,8},{10,11... | collective-permute-start | bytes 1179656 | tf_op jit(solution)/shard_map/ppermute | solution.py:272
  32.7 8.1 %collective-permute-start.14 = (bf16[96,1024]{1,0:T(8,128)(2,1)S(1)}, bf16[96,1024]{1,0:T(8,128)(2,1)S(1)}, u32[]{:S(2)}, u32[]{:S(2)}) collective-permute-start(bf16[96,1024]{1,0:T(8,128)(2,1)S(1)} %fold.4), channel_id=1, source_target_pairs={{0,2},{1,3},{2,0},{3,1},{4,6},{5,7},{6,4},{7,5},{8,10},{9,11},{10,... | collective-permute-start | bytes 589832 | tf_op jit(solution)/shard_map/ppermute | solution.py:272
  36.2 11.8 %collective-permute-start.12 = (bf16[96,1024]{1,0:T(8,128)(2,1)S(1)}, bf16[96,1024]{1,0:T(8,128)(2,1)S(1)}, u32[]{:S(2)}, u32[]{:S(2)}) collective-permute-start(bf16[96,1024]{1,0:T(8,128)(2,1)S(1)} %get-tuple-element.346), channel_id=1, source_target_pairs={{0,4},{1,5},{2,6},{3,7},{4,8},{5,9},{6,10},{7,11},{8,12},{9,13},{1... | collective-permute-start | bytes 589832 | tf_op jit(solution)/shard_map/ppermute | solution.py:276
  36.3 11.8 %collective-permute-start.13 = (bf16[96,1024]{1,0:T(8,128)(2,1)S(1)}, bf16[96,1024]{1,0:T(8,128)(2,1)S(1)}, u32[]{:S(2)}, u32[]{:S(2)}) collective-permute-start(bf16[96,1024]{1,0:T(8,128)(2,1)S(1)} %get-tuple-element.477.first_ref), channel_id=1, source_target_pairs={{0,2},{1,3},{2,0},{3,1},{4,6},{5,7},{6,4},{7,5},{8,10},{9,11},{10,... | collective-permute-start | bytes 589832 | tf_op jit(solution)/shard_map/ppermute | solution.py:272
  38.1 2.7 %collective-permute-start.15 = (bf16[384,1024]{1,0:T(8,128)(2,1)S(1)}, bf16[384,1024]{1,0:T(8,128)(2,1)S(1)}, u32[]{:S(2)}, u32[]{:S(2)}) collective-permute-start(bf16[384,1024]{1,0:T(8,128)(2,1)S(1)} %pair.15), channel_id=1, source_target_pairs={{0,1},{1,0},{2,3},{3,2},{4,5},{5,4},{6,7},{7,6},{8,9},{9,8},{10,11... | collective-permute-start | bytes 2359304 | tf_op jit(solution)/shard_map/ppermute | solution.py:272
  40.8 8.6 %collective-permute-start.18 = (bf16[96,1024]{1,0:T(8,128)(2,1)S(1)}, bf16[96,1024]{1,0:T(8,128)(2,1)S(1)}, u32[]{:S(2)}, u32[]{:S(2)}) collective-permute-start(bf16[96,1024]{1,0:T(8,128)(2,1)S(1)} %get-tuple-element.376), channel_id=1, source_target_pairs={{0,12},{1,13},{2,14},{3,15},{4,0},{5,1},{6,2},{7,3},{8,4},{9,5},{1... | collective-permute-start | bytes 589832 | tf_op jit(solution)/shard_map/ppermute | solution.py:276
  44.6 3.5 %collective-permute-start.16 = (bf16[192,1024]{1,0:T(8,128)(2,1)S(1)}, bf16[192,1024]{1,0:T(8,128)(2,1)S(1)}, u32[]{:S(2)}, u32[]{:S(2)}) collective-permute-start(bf16[192,1024]{1,0:T(8,128)(2,1)S(1)} %get-tuple-element.392), channel_id=1, source_target_pairs={{0,1},{1,0},{2,3},{3,2},{4,5},{5,4},{6,7},{7,6},{8,9},{9,8},{10,11... | collective-permute-start | bytes 1179656 | tf_op jit(solution)/shard_map/ppermute | solution.py:272
  44.9 7.2 %collective-permute-start.17 = (bf16[96,1024]{1,0:T(8,128)(2,1)S(1)}, bf16[96,1024]{1,0:T(8,128)(2,1)S(1)}, u32[]{:S(2)}, u32[]{:S(2)}) collective-permute-start(bf16[96,1024]{1,0:T(8,128)(2,1)S(1)} %fold.5), channel_id=1, source_target_pairs={{0,2},{1,3},{2,0},{3,1},{4,6},{5,7},{6,4},{7,5},{8,10},{9,11},{10,... | collective-permute-start | bytes 589832 | tf_op jit(solution)/shard_map/ppermute | solution.py:272
  48.2 6.2 %collective-permute-start.19 = (bf16[192,1024]{1,0:T(8,128)(2,1)S(1)}, bf16[192,1024]{1,0:T(8,128)(2,1)S(1)}, u32[]{:S(2)}, u32[]{:S(2)}) collective-permute-start(bf16[192,1024]{1,0:T(8,128)(2,1)S(1)} %get-tuple-element.428), channel_id=1, source_target_pairs={{0,1},{1,0},{2,3},{3,2},{4,5},{5,4},{6,7},{7,6},{8,9},{9,8},{10,11... | collective-permute-start | bytes 1179656 | tf_op jit(solution)/shard_map/ppermute | solution.py:272
  52.2 7.9 %collective-permute-start.20 = (bf16[96,1024]{1,0:T(8,128)(2,1)S(1)}, bf16[96,1024]{1,0:T(8,128)(2,1)S(1)}, u32[]{:S(2)}, u32[]{:S(2)}) collective-permute-start(bf16[96,1024]{1,0:T(8,128)(2,1)S(1)} %fold.6), channel_id=1, source_target_pairs={{0,2},{1,3},{2,0},{3,1},{4,6},{5,7},{6,4},{7,5},{8,10},{9,11},{10,... | collective-permute-start | bytes 589832 | tf_op jit(solution)/shard_map/ppermute | solution.py:272
  52.7 7.8 %collective-permute-start.22 = (bf16[96,1024]{1,0:T(8,128)(2,1)S(1)}, bf16[96,1024]{1,0:T(8,128)(2,1)S(1)}, u32[]{:S(2)}, u32[]{:S(2)}) collective-permute-start(bf16[96,1024]{1,0:T(8,128)(2,1)S(1)} %total.5), channel_id=1, source_target_pairs={{0,12},{1,13},{2,14},{3,15},{4,0},{5,1},{6,2},{7,3},{8,4},{9,5},{1... | collective-permute-start | bytes 589832 | tf_op jit(solution)/shard_map/ppermute | solution.py:276
  54.4 9.9 %collective-permute-start.23 = (bf16[96,1024]{1,0:T(8,128)(2,1)S(1)}, bf16[96,1024]{1,0:T(8,128)(2,1)S(1)}, u32[]{:S(2)}, u32[]{:S(2)}) collective-permute-start(bf16[96,1024]{1,0:T(8,128)(2,1)S(1)} %fold.7), channel_id=1, source_target_pairs={{0,2},{1,3},{2,0},{3,1},{4,6},{5,7},{6,4},{7,5},{8,10},{9,11},{10,... | collective-permute-start | bytes 589832 | tf_op jit(solution)/shard_map/ppermute | solution.py:272
  56.1 3.9 %collective-permute-start.21 = (bf16[192,1024]{1,0:T(8,128)(2,1)S(1)}, bf16[192,1024]{1,0:T(8,128)(2,1)S(1)}, u32[]{:S(2)}, u32[]{:S(2)}) collective-permute-start(bf16[192,1024]{1,0:T(8,128)(2,1)S(1)} %pair.16.refs_3_), channel_id=1, source_target_pairs={{0,1},{1,0},{2,3},{3,2},{4,5},{5,4},{6,7},{7,6},{8,9},{9,8},{10,11... | collective-permute-start | bytes 1179656 | tf_op jit(solution)/shard_map/ppermute | solution.py:272
  60.1 9.0 %collective-permute-start.25 = (bf16[96,1024]{1,0:T(8,128)(2,1)S(1)}, bf16[96,1024]{1,0:T(8,128)(2,1)S(1)}, u32[]{:S(2)}, u32[]{:S(2)}) collective-permute-start(bf16[96,1024]{1,0:T(8,128)(2,1)S(1)} %total.6), channel_id=1, source_target_pairs={{0,4},{1,5},{2,6},{3,7},{4,8},{5,9},{6,10},{7,11},{8,12},{9,13},{1... | collective-permute-start | bytes 589832 | tf_op jit(solution)/shard_map/ppermute | solution.py:276
  60.4 8.8 %collective-permute-start.24 = (bf16[96,1024]{1,0:T(8,128)(2,1)S(1)}, bf16[96,1024]{1,0:T(8,128)(2,1)S(1)}, u32[]{:S(2)}, u32[]{:S(2)}) collective-permute-start(bf16[96,1024]{1,0:T(8,128)(2,1)S(1)} %get-tuple-element.491.first_ref), channel_id=1, source_target_pairs={{0,2},{1,3},{2,0},{3,1},{4,6},{5,7},{6,4},{7,5},{8,10},{9,11},{10,... | collective-permute-start | bytes 589832 | tf_op jit(solution)/shard_map/ppermute | solution.py:272
  64.4 11.1 %collective-permute-start.28 = (bf16[96,1024]{1,0:T(8,128)(2,1)S(1)}, bf16[96,1024]{1,0:T(8,128)(2,1)S(1)}, u32[]{:S(2)}, u32[]{:S(2)}) collective-permute-start(bf16[96,1024]{1,0:T(8,128)(2,1)S(1)} %total.7), channel_id=1, source_target_pairs={{0,8},{1,9},{2,10},{3,11},{4,12},{5,13},{6,14},{7,15},{8,0},{9,1},... | collective-permute-start | bytes 589832 | tf_op jit(solution)/shard_map/ppermute | solution.py:276
  64.4 11.0 %collective-permute-start.27 = (bf16[96,1024]{1,0:T(8,128)(2,1)S(1)}, bf16[96,1024]{1,0:T(8,128)(2,1)S(1)}, u32[]{:S(2)}, u32[]{:S(2)}) collective-permute-start(bf16[96,1024]{1,0:T(8,128)(2,1)S(1)} %get-tuple-element.505.first_ref), channel_id=1, source_target_pairs={{0,2},{1,3},{2,0},{3,1},{4,6},{5,7},{6,4},{7,5},{8,10},{9,11},{10,... | collective-permute-start | bytes 589832 | tf_op jit(solution)/shard_map/ppermute | solution.py:272
  64.7 4.5 %collective-permute-start.26 = (bf16[192,1024]{1,0:T(8,128)(2,1)S(1)}, bf16[192,1024]{1,0:T(8,128)(2,1)S(1)}, u32[]{:S(2)}, u32[]{:S(2)}) collective-permute-start(bf16[192,1024]{1,0:T(8,128)(2,1)S(1)} %pair.17.refs_4_), channel_id=1, source_target_pairs={{0,1},{1,0},{2,3},{3,2},{4,5},{5,4},{6,7},{7,6},{8,9},{9,8},{10,11... | collective-permute-start | bytes 1179656 | tf_op jit(solution)/shard_map/ppermute | solution.py:272
  69.2 6.2 %collective-permute-start.29 = (bf16[192,1024]{1,0:T(8,128)(2,1)S(1)}, bf16[192,1024]{1,0:T(8,128)(2,1)S(1)}, u32[]{:S(2)}, u32[]{:S(2)}) collective-permute-start(bf16[192,1024]{1,0:T(8,128)(2,1)S(1)} %pair.18.refs_5_), channel_id=1, source_target_pairs={{0,1},{1,0},{2,3},{3,2},{4,5},{5,4},{6,7},{7,6},{8,9},{9,8},{10,11... | collective-permute-start | bytes 1179656 | tf_op jit(solution)/shard_map/ppermute | solution.py:272
  71.7 3.8 %copy-start = (bf16[128,1024]{1,0:T(8,128)(2,1)S(1)}, bf16[128,1024]{1,0:T(8,128)(2,1)}, u32[]{:S(2)}) copy-start(bf16[128,1024]{1,0:T(8,128)(2,1)} %tokens_ref.1) | copy-start | bytes 786436
  75.5 1.8 %collective-permute-start.30 = (bf16[192,1024]{1,0:T(8,128)(2,1)S(1)}, bf16[192,1024]{1,0:T(8,128)(2,1)S(1)}, u32[]{:S(2)}, u32[]{:S(2)}) collective-permute-start(bf16[192,1024]{1,0:T(8,128)(2,1)S(1)} %pair.19.refs_2_), channel_id=1, source_target_pairs={{0,1},{1,0},{2,3},{3,2},{4,5},{5,4},{6,7},{7,6},{8,9},{9,8},{10,11... | collective-permute-start | bytes 1179656 | tf_op jit(solution)/shard_map/ppermute | solution.py:272
  (2 other events, 7.6 us)

commit v19 on v18

--- a/solution.py
+++ b/solution.py
@@ -17,9 +17,9 @@
     ("cR0N1 yN3 zC3", "yN2 cR0N1"),
     ("ffnN1 cN2 yR0", "yN3 zC3 cN2"),
     ("cR1N3 ffnN2 yC3 zC1", "yR0 cR1N3"),
-    ("cR2 ffnN3 yR1 zC2 totalR0", "zC1 yC3 cR2"),
-    ("cR3 yR2", "yR1 zC2"),
-    ("totalR1 zR1", "cR3"),
+    ("cR2 ffnN3 yR1 totalR0", "zC1 yC3 cR2"),
+    ("cR3 yR2 zC2", "yR1"),
+    ("totalR1 zR1", "zC2 cR3"),
     ("yR3 cC0", "yR2 cC0"),
     ("totalR2 zR2 yC1", "zR1 yR3"),
     ("totalR3 zR3 yC2 cC3", "yC1 zR2 cC3"),

time: 80.2 us -> 80.4 us (level)
  starting transfers between devices: 27 us -> 31.3 us
  waiting for transfers between devices: 29.2 us -> 25.1 us
    ppermute x22, waiting for transfers between devices: 14.6 us -> 10.2 us  [swap(): lax.ppermute(value, 'expert', [(i, i ^ mask) for i in range(devices)])]
    ppermute x22, starting transfers between devices: 12 us -> 15.2 us  [swap(): lax.ppermute(value, 'expert', [(i, i ^ mask) for i in range(devices)])]
    ppermute x9, starting transfers between devices: 15 us -> 16 us  [turn(): return lax.ppermute(value, 'expert', to)]
  transfers between devices with their start and end apart: 31 -> 31, of which waited for: 13 -> 14; matrix products, arithmetic and copies ran while one was open for 0% -> 0% of each run, Pallas kernels for 23% -> 22%
where the time goes in v19:
time: 80.4 us; the launch traced here: 80.2 us
  starting transfers between devices  31.3 us (39%)
  waiting for transfers between devices  25.1 us (31%)
  Pallas kernels  22.6 us (28%)
  between operations  1.17 us (1%)
    ppermute x9, starting transfers between devices, turn(): return lax.ppermute(value, 'expert', to)  16 us
    ppermute x22, starting transfers between devices, swap(): lax.ppermute(value, 'expert', [(i, i ^ mask) for i in range(devices)])  15.2 us
    ppermute x9, waiting for transfers between devices, turn(): return lax.ppermute(value, 'expert', to)  14.9 us
    pallas_call x4, Pallas kernels, ffn(): call(functools.partial(ffn_kernel, len(pieces)), 24, 'ffn', out_shape=[ja...  10.5 us
    ppermute x22, waiting for transfers between devices, swap(): lax.ppermute(value, 'expert', [(i, i ^ mask) for i in range(devices)])  10.2 us
    pallas_call x1, Pallas kernels, load(): call(load_kernel, 16, 'load', out_shape=[weight, weight, jax.ShapeDtypeSt...  2.88 us
    pallas_call x1, Pallas kernels, last_grad(): call(functools.partial(last_grad_kernel, plan), 24, 'last_grad', out_shap...  2.66 us
    pallas_call x1, Pallas kernels, first_grad(): call(functools.partial(first_grad_kernel, plan), 24, 'first_grad', out_sh...  2.4 us
  transfers between devices with their start and end apart: 31, of which 14 were waited for; matrix products, arithmetic and copies ran while one was open for 0% of the time, Pallas kernels for 22%

profile of v19, /device:TPU:0, one launch (start us, length us, event | category | flops | bytes accessed | tf_op | source)
XLA Modules:
  0.0 80.2 jit_solution(9781735486991715624)
XLA Ops:
  0.6 1.9 %send.1 = (bf16[96,1024]{1,0:T(8,128)(2,1)S(1)}, bf16[96,1024]{1,0:T(8,128)(2,1)S(1)}, bf16[96,1024]{1,0:T(8,128)(2,1)S(1)}, bf16[96,1024]{1,0:T(8,128)(2,1)S(1)...) custom-call(s32[1]{0:T(128)} %bitcast.plane_ref, ...), custom_call_target="tpu_custom_call" | custom-call | tf_op jit(solution)/shard_map/send/pallas_call | solution.py:388
  2.6 3.1 %collective-permute-start = (bf16[96,1024]{1,0:T(8,128)(2,1)S(1)}, bf16[96,1024]{1,0:T(8,128)(2,1)S(1)}, u32[]{:S(2)}, u32[]{:S(2)}) collective-permute-start(bf16[96,1024]{1,0:T(8,128)(2,1)S(1)} %get-tuple-element.254), channel_id=1, source_target_pairs={{0,4},{1,5},{2,6},{3,7},{4,8},{5,9},{6,10},{7,11},{8,12},{9,13},{1... | collective-permute-start | bytes 589832 | tf_op jit(solution)/shard_map/ppermute | solution.py:276
  5.7 2.1 %collective-permute-start.1 = (bf16[96,1024]{1,0:T(8,128)(2,1)S(1)}, bf16[96,1024]{1,0:T(8,128)(2,1)S(1)}, u32[]{:S(2)}, u32[]{:S(2)}) collective-permute-start(bf16[96,1024]{1,0:T(8,128)(2,1)S(1)} %get-tuple-element.255), channel_id=1, source_target_pairs={{0,12},{1,13},{2,14},{3,15},{4,0},{5,1},{6,2},{7,3},{8,4},{9,5},{1... | collective-permute-start | bytes 589832 | tf_op jit(solution)/shard_map/ppermute | solution.py:276
  7.8 1.7 %collective-permute-start.2 = (bf16[96,1024]{1,0:T(8,128)(2,1)S(1)}, bf16[96,1024]{1,0:T(8,128)(2,1)S(1)}, u32[]{:S(2)}, u32[]{:S(2)}) collective-permute-start(bf16[96,1024]{1,0:T(8,128)(2,1)S(1)} %get-tuple-element.287.first_ref), channel_id=1, source_target_pairs={{0,2},{1,3},{2,0},{3,1},{4,6},{5,7},{6,4},{7,5},{8,10},{9,11},{10,... | collective-permute-start | bytes 589832 | tf_op jit(solution)/shard_map/ppermute | solution.py:272
  9.4 2.9 %load.1 = (bf16[1024,1024]{1,0:T(8,128)(2,1)S(1)}, bf16[1024,1024]{1,0:T(8,128)(2,1)S(1)}, bf16[1024,1024]{1,0:T(8,128)(2,1)S(1)}) custom-call(bf16[1,1024,1024]{2,1,0:T(8,128)(2,1)} %refs_0_.2, bf16[1,1024,1024]{2,1,0:T(8,128)(2,1)} %refs_1_.3, bf16[1,1024,1024]{2,1,0:T(8,128)(2,1)} %refs_2_.1), custom_call_target="tpu_custom_call" | custom-call | tf_op jit(solution)/shard_map/load/pallas_call | solution.py:403
  12.3 0.9 %collective-permute-start.4 = (bf16[96,1024]{1,0:T(8,128)(2,1)S(1)}, bf16[96,1024]{1,0:T(8,128)(2,1)S(1)}, u32[]{:S(2)}, u32[]{:S(2)}) collective-permute-start(bf16[96,1024]{1,0:T(8,128)(2,1)S(1)} %get-tuple-element.267), channel_id=1, source_target_pairs={{0,8},{1,9},{2,10},{3,11},{4,12},{5,13},{6,14},{7,15},{8,0},{9,1},... | collective-permute-start | bytes 589832 | tf_op jit(solution)/shard_map/ppermute | solution.py:276
  13.7 2.5 %collective-permute-done.1.refs_1_ = bf16[96,1024]{1,0:T(8,128)(2,1)S(1)} collective-permute-done((bf16[96,1024]{1,0:T(8,128)(2,1)S(1)}, bf16[96,1024]{1,0:T(8,128)(2,1)S(1)}, u32[]{:S(2)}, u32[]{:S(2)}) %collective-permute-start.1) | collective-permute-done | bytes 196640 | tf_op jit(solution)/shard_map/ppermute | solution.py:276
  16.2 1.5 %collective-permute-start.3 = (bf16[96,1024]{1,0:T(8,128)(2,1)S(1)}, bf16[96,1024]{1,0:T(8,128)(2,1)S(1)}, u32[]{:S(2)}, u32[]{:S(2)}) collective-permute-start(bf16[96,1024]{1,0:T(8,128)(2,1)S(1)} %get-tuple-element.318.first_ref), channel_id=1, source_target_pairs={{0,2},{1,3},{2,0},{3,1},{4,6},{5,7},{6,4},{7,5},{8,10},{9,11},{10,... | collective-permute-start | bytes 589832 | tf_op jit(solution)/shard_map/ppermute | solution.py:272
  17.9 1.5 %collective-permute-done.5.refs_0_ = bf16[96,1024]{1,0:T(8,128)(2,1)S(1)} collective-permute-done((bf16[96,1024]{1,0:T(8,128)(2,1)S(1)}, bf16[96,1024]{1,0:T(8,128)(2,1)S(1)}, u32[]{:S(2)}, u32[]{:S(2)}) %collective-permute-start.5) | collective-permute-done | bytes 196640 | tf_op jit(solution)/shard_map/ppermute | solution.py:272
  20.1 2.6 %ffn.4 = (bf16[1024,384]{1,0:T(8,128)(2,1)S(1)}, bf16[192,1024]{1,0:T(8,128)(2,1)S(1)}, bf16[192,1024]{1,0:T(8,128)(2,1)S(1)}) custom-call(bf16[192,1024]{1,0:T(8,128)(2,1)S(1)} %pair.10.refs_0_, bf16[192,1024]{1,0:T(8,128)(2,1)S(1)} %land_core.9.refs_1_, bf16[1024,1024]{1,0:T(8,128)(2,1)S(1)} %get-tuple-element.370.refs_2_, ...), custom_call_target="tpu_custom_call" | custom-call | tf_op jit(solution)/shard_map/ffn/pallas_call | solution.py:370
  22.7 2.5 %collective-permute-done.4.refs_1_ = bf16[96,1024]{1,0:T(8,128)(2,1)S(1)} collective-permute-done((bf16[96,1024]{1,0:T(8,128)(2,1)S(1)}, bf16[96,1024]{1,0:T(8,128)(2,1)S(1)}, u32[]{:S(2)}, u32[]{:S(2)}) %collective-permute-start.4) | collective-permute-done | bytes 196640 | tf_op jit(solution)/shard_map/ppermute | solution.py:276
  25.2 3.1 %collective-permute-start.10 = (bf16[96,1024]{1,0:T(8,128)(2,1)S(1)}, bf16[96,1024]{1,0:T(8,128)(2,1)S(1)}, u32[]{:S(2)}, u32[]{:S(2)}) collective-permute-start(bf16[96,1024]{1,0:T(8,128)(2,1)S(1)} %land.15), channel_id=1, source_target_pairs={{0,8},{1,9},{2,10},{3,11},{4,12},{5,13},{6,14},{7,15},{8,0},{9,1},... | collective-permute-start | bytes 589832 | tf_op jit(solution)/shard_map/ppermute | solution.py:276
  28.4 1.5 %collective-permute-start.9 = (bf16[96,1024]{1,0:T(8,128)(2,1)S(1)}, bf16[96,1024]{1,0:T(8,128)(2,1)S(1)}, u32[]{:S(2)}, u32[]{:S(2)}) collective-permute-start(bf16[96,1024]{1,0:T(8,128)(2,1)S(1)} %get-tuple-element.358.first_ref), channel_id=1, source_target_pairs={{0,2},{1,3},{2,0},{3,1},{4,6},{5,7},{6,4},{7,5},{8,10},{9,11},{10,... | collective-permute-start | bytes 589832 | tf_op jit(solution)/shard_map/ppermute | solution.py:272
  30.1 2.3 %collective-permute-done.8.refs_0_ = bf16[384,1024]{1,0:T(8,128)(2,1)S(1)} collective-permute-done((bf16[384,1024]{1,0:T(8,128)(2,1)S(1)}, bf16[384,1024]{1,0:T(8,128)(2,1)S(1)}, u32[]{:S(2)}, u32[]{:S(2)}) %collective-permute-start.8) | collective-permute-done | bytes 786464 | tf_op jit(solution)/shard_map/ppermute | solution.py:272
  33.3 2.6 %ffn.5 = (bf16[1024,384]{1,0:T(8,128)(2,1)S(1)}, bf16[192,1024]{1,0:T(8,128)(2,1)S(1)}, bf16[192,1024]{1,0:T(8,128)(2,1)S(1)}) custom-call(bf16[192,1024]{1,0:T(8,128)(2,1)S(1)} %pair.11.second_ref.refs_0_, bf16[192,1024]{1,0:T(8,128)(2,1)S(1)} %get-tuple-element.326.refs_1_, bf16[1024,1024]{1,0:T(8,128)(2,1)S(1)} %get-tuple-element.370.refs_2_, ...), custom_call_target="tpu_custom_call" | custom-call | tf_op jit(solution)/shard_map/ffn/pallas_call | solution.py:370
  36.3 1.7 %collective-permute-start.13 = (bf16[96,1024]{1,0:T(8,128)(2,1)S(1)}, bf16[96,1024]{1,0:T(8,128)(2,1)S(1)}, u32[]{:S(2)}, u32[]{:S(2)}) collective-permute-start(bf16[96,1024]{1,0:T(8,128)(2,1)S(1)} %get-tuple-element.475.first_ref), channel_id=1, source_target_pairs={{0,2},{1,3},{2,0},{3,1},{4,6},{5,7},{6,4},{7,5},{8,10},{9,11},{10,... | collective-permute-start | bytes 589832 | tf_op jit(solution)/shard_map/ppermute | solution.py:272
  38.2 2.6 %ffn.6 = (bf16[1024,384]{1,0:T(8,128)(2,1)S(1)}, bf16[192,1024]{1,0:T(8,128)(2,1)S(1)}, bf16[192,1024]{1,0:T(8,128)(2,1)S(1)}) custom-call(bf16[192,1024]{1,0:T(8,128)(2,1)S(1)} %pair.13.refs_0_, bf16[192,1024]{1,0:T(8,128)(2,1)S(1)} %land_core.11.refs_1_, bf16[1024,1024]{1,0:T(8,128)(2,1)S(1)} %get-tuple-element.370.refs_2_, ...), custom_call_target="tpu_custom_call" | custom-call | tf_op jit(solution)/shard_map/ffn/pallas_call | solution.py:370
  41.9 2.6 %ffn.7 = (bf16[1024,384]{1,0:T(8,128)(2,1)S(1)}, bf16[192,1024]{1,0:T(8,128)(2,1)S(1)}, bf16[192,1024]{1,0:T(8,128)(2,1)S(1)}) custom-call(bf16[192,1024]{1,0:T(8,128)(2,1)S(1)} %pair.14.second_ref.refs_0_, bf16[192,1024]{1,0:T(8,128)(2,1)S(1)} %get-tuple-element.369.refs_1_, bf16[1024,1024]{1,0:T(8,128)(2,1)S(1)} %get-tuple-element.370.refs_2_, ...), custom_call_target="tpu_custom_call" | custom-call | tf_op jit(solution)/shard_map/ffn/pallas_call | solution.py:370
  45.0 3.5 %collective-permute-start.18 = (bf16[96,1024]{1,0:T(8,128)(2,1)S(1)}, bf16[96,1024]{1,0:T(8,128)(2,1)S(1)}, u32[]{:S(2)}, u32[]{:S(2)}) collective-permute-start(bf16[96,1024]{1,0:T(8,128)(2,1)S(1)} %get-tuple-element.394), channel_id=1, source_target_pairs={{0,12},{1,13},{2,14},{3,15},{4,0},{5,1},{6,2},{7,3},{8,4},{9,5},{1... | collective-permute-start | bytes 589832 | tf_op jit(solution)/shard_map/ppermute | solution.py:276
  48.6 1.7 %collective-permute-start.20 = (bf16[96,1024]{1,0:T(8,128)(2,1)S(1)}, bf16[96,1024]{1,0:T(8,128)(2,1)S(1)}, u32[]{:S(2)}, u32[]{:S(2)}) collective-permute-start(bf16[96,1024]{1,0:T(8,128)(2,1)S(1)} %fold.6), channel_id=1, source_target_pairs={{0,2},{1,3},{2,0},{3,1},{4,6},{5,7},{6,4},{7,5},{8,10},{9,11},{10,... | collective-permute-start | bytes 589832 | tf_op jit(solution)/shard_map/ppermute | solution.py:272
  50.3 2.4 %collective-permute-start.22 = (bf16[96,1024]{1,0:T(8,128)(2,1)S(1)}, bf16[96,1024]{1,0:T(8,128)(2,1)S(1)}, u32[]{:S(2)}, u32[]{:S(2)}) collective-permute-start(bf16[96,1024]{1,0:T(8,128)(2,1)S(1)} %total.5), channel_id=1, source_target_pairs={{0,12},{1,13},{2,14},{3,15},{4,0},{5,1},{6,2},{7,3},{8,4},{9,5},{1... | collective-permute-start | bytes 589832 | tf_op jit(solution)/shard_map/ppermute | solution.py:276
  53.3 1.2 %collective-permute-done.19.refs_0_ = bf16[192,1024]{1,0:T(8,128)(2,1)S(1)} collective-permute-done((bf16[192,1024]{1,0:T(8,128)(2,1)S(1)}, bf16[192,1024]{1,0:T(8,128)(2,1)S(1)}, u32[]{:S(2)}, u32[]{:S(2)}) %collective-permute-start.19) | collective-permute-done | bytes 393248 | tf_op jit(solution)/shard_map/ppermute | solution.py:272
  54.5 1.7 %collective-permute-start.23 = (bf16[96,1024]{1,0:T(8,128)(2,1)S(1)}, bf16[96,1024]{1,0:T(8,128)(2,1)S(1)}, u32[]{:S(2)}, u32[]{:S(2)}) collective-permute-start(bf16[96,1024]{1,0:T(8,128)(2,1)S(1)} %fold.7), channel_id=1, source_target_pairs={{0,2},{1,3},{2,0},{3,1},{4,6},{5,7},{6,4},{7,5},{8,10},{9,11},{10,... | collective-permute-start | bytes 589832 | tf_op jit(solution)/shard_map/ppermute | solution.py:272
  56.4 1.7 %collective-permute-done.21.refs_0_ = bf16[192,1024]{1,0:T(8,128)(2,1)S(1)} collective-permute-done((bf16[192,1024]{1,0:T(8,128)(2,1)S(1)}, bf16[192,1024]{1,0:T(8,128)(2,1)S(1)}, u32[]{:S(2)}, u32[]{:S(2)}) %collective-permute-start.21) | collective-permute-done | bytes 393248 | tf_op jit(solution)/shard_map/ppermute | solution.py:272
  58.8 3.0 %collective-permute-done.23.refs_1_ = bf16[96,1024]{1,0:T(8,128)(2,1)S(1)} collective-permute-done((bf16[96,1024]{1,0:T(8,128)(2,1)S(1)}, bf16[96,1024]{1,0:T(8,128)(2,1)S(1)}, u32[]{:S(2)}, u32[]{:S(2)}) %collective-permute-start.23) | collective-permute-done | bytes 196640 | tf_op jit(solution)/shard_map/ppermute | solution.py:272
  61.9 0.6 collective-permute-start.28
  62.6 1.6 %collective-permute-start.27 = (bf16[96,1024]{1,0:T(8,128)(2,1)S(1)}, bf16[96,1024]{1,0:T(8,128)(2,1)S(1)}, u32[]{:S(2)}, u32[]{:S(2)}) collective-permute-start(bf16[96,1024]{1,0:T(8,128)(2,1)S(1)} %land.23.first_ref), channel_id=1, source_target_pairs={{0,2},{1,3},{2,0},{3,1},{4,6},{5,7},{6,4},{7,5},{8,10},{9,11},{10,... | collective-permute-start | bytes 589832 | tf_op jit(solution)/shard_map/ppermute | solution.py:272
  64.3 3.7 %collective-permute-done.25.refs_1_ = bf16[96,1024]{1,0:T(8,128)(2,1)S(1)} collective-permute-done((bf16[96,1024]{1,0:T(8,128)(2,1)S(1)}, bf16[96,1024]{1,0:T(8,128)(2,1)S(1)}, u32[]{:S(2)}, u32[]{:S(2)}) %collective-permute-start.25) | collective-permute-done | bytes 196640 | tf_op jit(solution)/shard_map/ppermute | solution.py:276
  68.1 2.4 %first_grad.1.refs_2_.first_ref = f32[1024,1024]{1,0:T(8,128)S(1)} custom-call(bf16[1024,384]{1,0:T(8,128)(2,1)S(1)} %get-tuple-element.479.refs_2_.refs_0_, bf16[1024,384]{1,0:T(8,128)(2,1)S(1)} %get-tuple-element.482.refs_2_.refs_1_, bf16[1024,384]{1,0:T(8,128)(2,1)S(1)} %get-tuple-element.501.refs_2_.refs_0_, bf16[192,1024]{1,0:T(8,128)(2,1)S(1)} %pair.16.refs_3_, ...), custom_call_target="tpu_custom_call" | custom-call | tf_op jit(solution)/shard_map/first_grad/pallas_call | solution.py:438
  70.6 5.0 %collective-permute-done.28.refs_1_ = bf16[96,1024]{1,0:T(8,128)(2,1)S(1)} collective-permute-done((bf16[96,1024]{1,0:T(8,128)(2,1)S(1)}, bf16[96,1024]{1,0:T(8,128)(2,1)S(1)}, u32[]{:S(2)}, u32[]{:S(2)}) %collective-permute-start.28) | collective-permute-done | bytes 196640 | tf_op jit(solution)/shard_map/ppermute | solution.py:276
  75.7 1.4 %combine.1 = bf16[128,1024]{1,0:T(8,128)(2,1)} custom-call(s32[1]{0:T(128)} %bitcast.plane_ref, bf16[128,1024]{1,0:T(8,128)(2,1)S(1)} %copy-done, s32[2,128]{1,0:T(2,128)S(1)} %bitcast.5, s32[2,128]{1,0:T(2,128)S(1)} %bitcast.7, bf16[96,1024]{1,0:T(8,128)(2,1)S(1)} %total.4.refs_0_, bf16[96,1024]{1,0:T(8,128)(2,1)S(1)} %get-tuple-element.497.refs_1_, ...), custom_call_target="tpu_custom_call" | custom-call | tf_op jit(solution)/shard_map/combine/pallas_call | solution.py:502
  77.4 2.7 %last_grad.1 = bf16[1,1024,1024]{2,1,0:T(8,128)(2,1)} custom-call(f32[1024,1024]{1,0:T(8,128)S(1)} %first_grad.1.refs_2_.first_ref, bf16[1024,384]{1,0:T(8,128)(2,1)S(1)} %get-tuple-element.501.refs_2_.refs_0_, bf16[1024,384]{1,0:T(8,128)(2,1)S(1)} %get-tuple-element.502.refs_1_, bf16[192,1024]{1,0:T(8,128)(2,1)S(1)} %pair.19.refs_2_, ...), custom_call_target="tpu_custom_call" | custom-call | tf_op jit(solution)/shard_map/last_grad/pallas_call | solution.py:450
  (88 shorter events, 6.7 us)
Async XLA Ops:
  2.6 11.1 %collective-permute-start = (bf16[96,1024]{1,0:T(8,128)(2,1)S(1)}, bf16[96,1024]{1,0:T(8,128)(2,1)S(1)}, u32[]{:S(2)}, u32[]{:S(2)}) collective-permute-start(bf16[96,1024]{1,0:T(8,128)(2,1)S(1)} %get-tuple-element.254), channel_id=1, source_target_pairs={{0,4},{1,5},{2,6},{3,7},{4,8},{5,9},{6,10},{7,11},{8,12},{9,13},{1... | collective-permute-start | bytes 589832 | tf_op jit(solution)/shard_map/ppermute | solution.py:276
  5.7 10.6 %collective-permute-start.1 = (bf16[96,1024]{1,0:T(8,128)(2,1)S(1)}, bf16[96,1024]{1,0:T(8,128)(2,1)S(1)}, u32[]{:S(2)}, u32[]{:S(2)}) collective-permute-start(bf16[96,1024]{1,0:T(8,128)(2,1)S(1)} %get-tuple-element.255), channel_id=1, source_target_pairs={{0,12},{1,13},{2,14},{3,15},{4,0},{5,1},{6,2},{7,3},{8,4},{9,5},{1... | collective-permute-start | bytes 589832 | tf_op jit(solution)/shard_map/ppermute | solution.py:276
  7.8 8.5 %collective-permute-start.2 = (bf16[96,1024]{1,0:T(8,128)(2,1)S(1)}, bf16[96,1024]{1,0:T(8,128)(2,1)S(1)}, u32[]{:S(2)}, u32[]{:S(2)}) collective-permute-start(bf16[96,1024]{1,0:T(8,128)(2,1)S(1)} %get-tuple-element.287.first_ref), channel_id=1, source_target_pairs={{0,2},{1,3},{2,0},{3,1},{4,6},{5,7},{6,4},{7,5},{8,10},{9,11},{10,... | collective-permute-start | bytes 589832 | tf_op jit(solution)/shard_map/ppermute | solution.py:272
  12.3 12.9 %collective-permute-start.4 = (bf16[96,1024]{1,0:T(8,128)(2,1)S(1)}, bf16[96,1024]{1,0:T(8,128)(2,1)S(1)}, u32[]{:S(2)}, u32[]{:S(2)}) collective-permute-start(bf16[96,1024]{1,0:T(8,128)(2,1)S(1)} %get-tuple-element.267), channel_id=1, source_target_pairs={{0,8},{1,9},{2,10},{3,11},{4,12},{5,13},{6,14},{7,15},{8,0},{9,1},... | collective-permute-start | bytes 589832 | tf_op jit(solution)/shard_map/ppermute | solution.py:276
  13.2 6.2 %collective-permute-start.5 = (bf16[96,1024]{1,0:T(8,128)(2,1)S(1)}, bf16[96,1024]{1,0:T(8,128)(2,1)S(1)}, u32[]{:S(2)}, u32[]{:S(2)}) collective-permute-start(bf16[96,1024]{1,0:T(8,128)(2,1)S(1)} %get-tuple-element.440.first_ref), channel_id=1, source_target_pairs={{0,2},{1,3},{2,0},{3,1},{4,6},{5,7},{6,4},{7,5},{8,10},{9,11},{10,... | collective-permute-start | bytes 589832 | tf_op jit(solution)/shard_map/ppermute | solution.py:272
  16.2 9.0 %collective-permute-start.3 = (bf16[96,1024]{1,0:T(8,128)(2,1)S(1)}, bf16[96,1024]{1,0:T(8,128)(2,1)S(1)}, u32[]{:S(2)}, u32[]{:S(2)}) collective-permute-start(bf16[96,1024]{1,0:T(8,128)(2,1)S(1)} %get-tuple-element.318.first_ref), channel_id=1, source_target_pairs={{0,2},{1,3},{2,0},{3,1},{4,6},{5,7},{6,4},{7,5},{8,10},{9,11},{10,... | collective-permute-start | bytes 589832 | tf_op jit(solution)/shard_map/ppermute | solution.py:272
  17.8 1.8 %collective-permute-start.6 = (bf16[192,1024]{1,0:T(8,128)(2,1)S(1)}, bf16[192,1024]{1,0:T(8,128)(2,1)S(1)}, u32[]{:S(2)}, u32[]{:S(2)}) collective-permute-start(bf16[192,1024]{1,0:T(8,128)(2,1)S(1)} %pair.10.refs_0_), channel_id=1, source_target_pairs={{0,1},{1,0},{2,3},{3,2},{4,5},{5,4},{6,7},{7,6},{8,9},{9,8},{10,11... | collective-permute-start | bytes 1179656 | tf_op jit(solution)/shard_map/ppermute | solution.py:272
  19.6 10.5 %collective-permute-start.7 = (bf16[96,1024]{1,0:T(8,128)(2,1)S(1)}, bf16[96,1024]{1,0:T(8,128)(2,1)S(1)}, u32[]{:S(2)}, u32[]{:S(2)}) collective-permute-start(bf16[96,1024]{1,0:T(8,128)(2,1)S(1)} %get-tuple-element.341.first_ref), channel_id=1, source_target_pairs={{0,2},{1,3},{2,0},{3,1},{4,6},{5,7},{6,4},{7,5},{8,10},{9,11},{10,... | collective-permute-start | bytes 589832 | tf_op jit(solution)/shard_map/ppermute | solution.py:272
  25.2 11.0 %collective-permute-start.10 = (bf16[96,1024]{1,0:T(8,128)(2,1)S(1)}, bf16[96,1024]{1,0:T(8,128)(2,1)S(1)}, u32[]{:S(2)}, u32[]{:S(2)}) collective-permute-start(bf16[96,1024]{1,0:T(8,128)(2,1)S(1)} %land.15), channel_id=1, source_target_pairs={{0,8},{1,9},{2,10},{3,11},{4,12},{5,13},{6,14},{7,15},{8,0},{9,1},... | collective-permute-start | bytes 589832 | tf_op jit(solution)/shard_map/ppermute | solution.py:276
  28.4 7.8 %collective-permute-start.9 = (bf16[96,1024]{1,0:T(8,128)(2,1)S(1)}, bf16[96,1024]{1,0:T(8,128)(2,1)S(1)}, u32[]{:S(2)}, u32[]{:S(2)}) collective-permute-start(bf16[96,1024]{1,0:T(8,128)(2,1)S(1)} %get-tuple-element.358.first_ref), channel_id=1, source_target_pairs={{0,2},{1,3},{2,0},{3,1},{4,6},{5,7},{6,4},{7,5},{8,10},{9,11},{10,... | collective-permute-start | bytes 589832 | tf_op jit(solution)/shard_map/ppermute | solution.py:272
  30.0 2.4 %collective-permute-start.8 = (bf16[384,1024]{1,0:T(8,128)(2,1)S(1)}, bf16[384,1024]{1,0:T(8,128)(2,1)S(1)}, u32[]{:S(2)}, u32[]{:S(2)}) collective-permute-start(bf16[384,1024]{1,0:T(8,128)(2,1)S(1)} %pair.12), channel_id=1, source_target_pairs={{0,1},{1,0},{2,3},{3,2},{4,5},{5,4},{6,7},{7,6},{8,9},{9,8},{10,11... | collective-permute-start | bytes 2359304 | tf_op jit(solution)/shard_map/ppermute | solution.py:272
  32.4 3.8 %collective-permute-start.11 = (bf16[192,1024]{1,0:T(8,128)(2,1)S(1)}, bf16[192,1024]{1,0:T(8,128)(2,1)S(1)}, u32[]{:S(2)}, u32[]{:S(2)}) collective-permute-start(bf16[192,1024]{1,0:T(8,128)(2,1)S(1)} %pair.13.refs_0_), channel_id=1, source_target_pairs={{0,1},{1,0},{2,3},{3,2},{4,5},{5,4},{6,7},{7,6},{8,9},{9,8},{10,11... | collective-permute-start | bytes 1179656 | tf_op jit(solution)/shard_map/ppermute | solution.py:272
  32.7 8.1 %collective-permute-start.14 = (bf16[96,1024]{1,0:T(8,128)(2,1)S(1)}, bf16[96,1024]{1,0:T(8,128)(2,1)S(1)}, u32[]{:S(2)}, u32[]{:S(2)}) collective-permute-start(bf16[96,1024]{1,0:T(8,128)(2,1)S(1)} %fold.4), channel_id=1, source_target_pairs={{0,2},{1,3},{2,0},{3,1},{4,6},{5,7},{6,4},{7,5},{8,10},{9,11},{10,... | collective-permute-start | bytes 589832 | tf_op jit(solution)/shard_map/ppermute | solution.py:272
  36.2 8.7 %collective-permute-start.12 = (bf16[96,1024]{1,0:T(8,128)(2,1)S(1)}, bf16[96,1024]{1,0:T(8,128)(2,1)S(1)}, u32[]{:S(2)}, u32[]{:S(2)}) collective-permute-start(bf16[96,1024]{1,0:T(8,128)(2,1)S(1)} %get-tuple-element.345), channel_id=1, source_target_pairs={{0,4},{1,5},{2,6},{3,7},{4,8},{5,9},{6,10},{7,11},{8,12},{9,13},{1... | collective-permute-start | bytes 589832 | tf_op jit(solution)/shard_map/ppermute | solution.py:276
  36.3 8.6 %collective-permute-start.13 = (bf16[96,1024]{1,0:T(8,128)(2,1)S(1)}, bf16[96,1024]{1,0:T(8,128)(2,1)S(1)}, u32[]{:S(2)}, u32[]{:S(2)}) collective-permute-start(bf16[96,1024]{1,0:T(8,128)(2,1)S(1)} %get-tuple-element.475.first_ref), channel_id=1, source_target_pairs={{0,2},{1,3},{2,0},{3,1},{4,6},{5,7},{6,4},{7,5},{8,10},{9,11},{10,... | collective-permute-start | bytes 589832 | tf_op jit(solution)/shard_map/ppermute | solution.py:272
  38.1 2.7 %collective-permute-start.15 = (bf16[384,1024]{1,0:T(8,128)(2,1)S(1)}, bf16[384,1024]{1,0:T(8,128)(2,1)S(1)}, u32[]{:S(2)}, u32[]{:S(2)}) collective-permute-start(bf16[384,1024]{1,0:T(8,128)(2,1)S(1)} %pair.15), channel_id=1, source_target_pairs={{0,1},{1,0},{2,3},{3,2},{4,5},{5,4},{6,7},{7,6},{8,9},{9,8},{10,11... | collective-permute-start | bytes 2359304 | tf_op jit(solution)/shard_map/ppermute | solution.py:272
  40.8 4.2 %collective-permute-start.16 = (bf16[192,1024]{1,0:T(8,128)(2,1)S(1)}, bf16[192,1024]{1,0:T(8,128)(2,1)S(1)}, u32[]{:S(2)}, u32[]{:S(2)}) collective-permute-start(bf16[192,1024]{1,0:T(8,128)(2,1)S(1)} %get-tuple-element.391), channel_id=1, source_target_pairs={{0,1},{1,0},{2,3},{3,2},{4,5},{5,4},{6,7},{7,6},{8,9},{9,8},{10,11... | collective-permute-start | bytes 1179656 | tf_op jit(solution)/shard_map/ppermute | solution.py:272
  41.5 7.0 %collective-permute-start.17 = (bf16[96,1024]{1,0:T(8,128)(2,1)S(1)}, bf16[96,1024]{1,0:T(8,128)(2,1)S(1)}, u32[]{:S(2)}, u32[]{:S(2)}) collective-permute-start(bf16[96,1024]{1,0:T(8,128)(2,1)S(1)} %fold.5), channel_id=1, source_target_pairs={{0,2},{1,3},{2,0},{3,1},{4,6},{5,7},{6,4},{7,5},{8,10},{9,11},{10,... | collective-permute-start | bytes 589832 | tf_op jit(solution)/shard_map/ppermute | solution.py:272
  45.0 8.3 %collective-permute-start.18 = (bf16[96,1024]{1,0:T(8,128)(2,1)S(1)}, bf16[96,1024]{1,0:T(8,128)(2,1)S(1)}, u32[]{:S(2)}, u32[]{:S(2)}) collective-permute-start(bf16[96,1024]{1,0:T(8,128)(2,1)S(1)} %get-tuple-element.394), channel_id=1, source_target_pairs={{0,12},{1,13},{2,14},{3,15},{4,0},{5,1},{6,2},{7,3},{8,4},{9,5},{1... | collective-permute-start | bytes 589832 | tf_op jit(solution)/shard_map/ppermute | solution.py:276
  48.6 7.8 %collective-permute-start.20 = (bf16[96,1024]{1,0:T(8,128)(2,1)S(1)}, bf16[96,1024]{1,0:T(8,128)(2,1)S(1)}, u32[]{:S(2)}, u32[]{:S(2)}) collective-permute-start(bf16[96,1024]{1,0:T(8,128)(2,1)S(1)} %fold.6), channel_id=1, source_target_pairs={{0,2},{1,3},{2,0},{3,1},{4,6},{5,7},{6,4},{7,5},{8,10},{9,11},{10,... | collective-permute-start | bytes 589832 | tf_op jit(solution)/shard_map/ppermute | solution.py:272
  50.3 8.5 %collective-permute-start.22 = (bf16[96,1024]{1,0:T(8,128)(2,1)S(1)}, bf16[96,1024]{1,0:T(8,128)(2,1)S(1)}, u32[]{:S(2)}, u32[]{:S(2)}) collective-permute-start(bf16[96,1024]{1,0:T(8,128)(2,1)S(1)} %total.5), channel_id=1, source_target_pairs={{0,12},{1,13},{2,14},{3,15},{4,0},{5,1},{6,2},{7,3},{8,4},{9,5},{1... | collective-permute-start | bytes 589832 | tf_op jit(solution)/shard_map/ppermute | solution.py:276
  52.8 1.7 %collective-permute-start.19 = (bf16[192,1024]{1,0:T(8,128)(2,1)S(1)}, bf16[192,1024]{1,0:T(8,128)(2,1)S(1)}, u32[]{:S(2)}, u32[]{:S(2)}) collective-permute-start(bf16[192,1024]{1,0:T(8,128)(2,1)S(1)} %get-tuple-element.425), channel_id=1, source_target_pairs={{0,1},{1,0},{2,3},{3,2},{4,5},{5,4},{6,7},{7,6},{8,9},{9,8},{10,11... | collective-permute-start | bytes 1179656 | tf_op jit(solution)/shard_map/ppermute | solution.py:272
  54.5 7.3 %collective-permute-start.23 = (bf16[96,1024]{1,0:T(8,128)(2,1)S(1)}, bf16[96,1024]{1,0:T(8,128)(2,1)S(1)}, u32[]{:S(2)}, u32[]{:S(2)}) collective-permute-start(bf16[96,1024]{1,0:T(8,128)(2,1)S(1)} %fold.7), channel_id=1, source_target_pairs={{0,2},{1,3},{2,0},{3,1},{4,6},{5,7},{6,4},{7,5},{8,10},{9,11},{10,... | collective-permute-start | bytes 589832 | tf_op jit(solution)/shard_map/ppermute | solution.py:272
  56.3 1.8 %collective-permute-start.21 = (bf16[192,1024]{1,0:T(8,128)(2,1)S(1)}, bf16[192,1024]{1,0:T(8,128)(2,1)S(1)}, u32[]{:S(2)}, u32[]{:S(2)}) collective-permute-start(bf16[192,1024]{1,0:T(8,128)(2,1)S(1)} %pair.16.refs_3_), channel_id=1, source_target_pairs={{0,1},{1,0},{2,3},{3,2},{4,5},{5,4},{6,7},{7,6},{8,9},{9,8},{10,11... | collective-permute-start | bytes 1179656 | tf_op jit(solution)/shard_map/ppermute | solution.py:272
  58.1 9.9 %collective-permute-start.25 = (bf16[96,1024]{1,0:T(8,128)(2,1)S(1)}, bf16[96,1024]{1,0:T(8,128)(2,1)S(1)}, u32[]{:S(2)}, u32[]{:S(2)}) collective-permute-start(bf16[96,1024]{1,0:T(8,128)(2,1)S(1)} %total.6), channel_id=1, source_target_pairs={{0,4},{1,5},{2,6},{3,7},{4,8},{5,9},{6,10},{7,11},{8,12},{9,13},{1... | collective-permute-start | bytes 589832 | tf_op jit(solution)/shard_map/ppermute | solution.py:276
  58.4 9.6 %collective-permute-start.24 = (bf16[96,1024]{1,0:T(8,128)(2,1)S(1)}, bf16[96,1024]{1,0:T(8,128)(2,1)S(1)}, u32[]{:S(2)}, u32[]{:S(2)}) collective-permute-start(bf16[96,1024]{1,0:T(8,128)(2,1)S(1)} %get-tuple-element.489.first_ref), channel_id=1, source_target_pairs={{0,2},{1,3},{2,0},{3,1},{4,6},{5,7},{6,4},{7,5},{8,10},{9,11},{10,... | collective-permute-start | bytes 589832 | tf_op jit(solution)/shard_map/ppermute | solution.py:272
  61.9 13.6 %collective-permute-start.28 = (bf16[96,1024]{1,0:T(8,128)(2,1)S(1)}, bf16[96,1024]{1,0:T(8,128)(2,1)S(1)}, u32[]{:S(2)}, u32[]{:S(2)}) collective-permute-start(bf16[96,1024]{1,0:T(8,128)(2,1)S(1)} %total.7), channel_id=1, source_target_pairs={{0,8},{1,9},{2,10},{3,11},{4,12},{5,13},{6,14},{7,15},{8,0},{9,1},... | collective-permute-start | bytes 589832 | tf_op jit(solution)/shard_map/ppermute | solution.py:276
  62.6 13.0 %collective-permute-start.27 = (bf16[96,1024]{1,0:T(8,128)(2,1)S(1)}, bf16[96,1024]{1,0:T(8,128)(2,1)S(1)}, u32[]{:S(2)}, u32[]{:S(2)}) collective-permute-start(bf16[96,1024]{1,0:T(8,128)(2,1)S(1)} %land.23.first_ref), channel_id=1, source_target_pairs={{0,2},{1,3},{2,0},{3,1},{4,6},{5,7},{6,4},{7,5},{8,10},{9,11},{10,... | collective-permute-start | bytes 589832 | tf_op jit(solution)/shard_map/ppermute | solution.py:272
  64.2 3.8 %collective-permute-start.26 = (bf16[192,1024]{1,0:T(8,128)(2,1)S(1)}, bf16[192,1024]{1,0:T(8,128)(2,1)S(1)}, u32[]{:S(2)}, u32[]{:S(2)}) collective-permute-start(bf16[192,1024]{1,0:T(8,128)(2,1)S(1)} %pair.17.refs_4_), channel_id=1, source_target_pairs={{0,1},{1,0},{2,3},{3,2},{4,5},{5,4},{6,7},{7,6},{8,9},{9,8},{10,11... | collective-permute-start | bytes 1179656 | tf_op jit(solution)/shard_map/ppermute | solution.py:272
  68.1 7.5 %collective-permute-start.29 = (bf16[192,1024]{1,0:T(8,128)(2,1)S(1)}, bf16[192,1024]{1,0:T(8,128)(2,1)S(1)}, u32[]{:S(2)}, u32[]{:S(2)}) collective-permute-start(bf16[192,1024]{1,0:T(8,128)(2,1)S(1)} %pair.18.refs_5_), channel_id=1, source_target_pairs={{0,1},{1,0},{2,3},{3,2},{4,5},{5,4},{6,7},{7,6},{8,9},{9,8},{10,11... | collective-permute-start | bytes 1179656 | tf_op jit(solution)/shard_map/ppermute | solution.py:272
  70.5 5.1 %copy-start = (bf16[128,1024]{1,0:T(8,128)(2,1)S(1)}, bf16[128,1024]{1,0:T(8,128)(2,1)}, u32[]{:S(2)}) copy-start(bf16[128,1024]{1,0:T(8,128)(2,1)} %tokens_ref.1) | copy-start | bytes 786436
  75.6 1.8 %collective-permute-start.30 = (bf16[192,1024]{1,0:T(8,128)(2,1)S(1)}, bf16[192,1024]{1,0:T(8,128)(2,1)S(1)}, u32[]{:S(2)}, u32[]{:S(2)}) collective-permute-start(bf16[192,1024]{1,0:T(8,128)(2,1)S(1)} %pair.19.refs_2_), channel_id=1, source_target_pairs={{0,1},{1,0},{2,3},{3,2},{4,5},{5,4},{6,7},{7,6},{8,9},{9,8},{10,11... | collective-permute-start | bytes 1179656 | tf_op jit(solution)/shard_map/ppermute | solution.py:272
  (2 other events, 10.2 us)

commit v20 on v17

--- a/solution.py
+++ b/solution.py
@@ -10,7 +10,7 @@
 HSPLIT = 4
 GROUPS = 4
 PLAN = (
-    ("yN0 zN1 zN2 loadW0", ""),
+    ("yN0 zN1 zN2 sendC0 loadW0", ""),
     ("yC0 zN3", "zN1 zN2 yN0"),
     ("cN0 yN1", "yC0 cN0"),
     ("ffnN0 yN2", "yN1 zN3"),
@@ -90,27 +90,33 @@
     return copies
 
 
-def send_kernel(experts, plane_ref, *refs):
-    sources, refs = refs[:5], refs[5:]
-    row_outs, grad_outs = refs[:experts], refs[experts : 2 * experts]
-    targets, semaphores = refs[2 * experts : -1], refs[-1]
-    tokens_ref, cot_ref, routes_ref, nums_ref, gain_ref = targets
+def send_rows_kernel(experts, plane_ref, *refs):
+    sources, outs, targets, semaphores = refs[:3], refs[3 : 3 + experts], refs[-4:-1], refs[-1]
+    tokens_ref, routes_ref, gain_ref = targets
     copies = fetch(semaphores, *zip(sources, targets))
+    copies[1].wait()
+    placings = placing_of(routes_ref[...], plane_ref[0], experts, outs[0].shape[0])
     copies[2].wait()
-    copies[3].wait()
-    routes = routes_ref[...]
-    placings = placing_of(routes, plane_ref[0], experts, row_outs[0].shape[0])
-    gates = gates_of(routes, nums_ref[...], plane_ref[0], experts)
-    copies[4].wait()
     copies[0].wait()
     frames = tokens_ref[...].astype(F32)
     inverse = lax.rsqrt(jnp.mean(frames * frames, -1, keepdims=True) + 1e-06)
     normed = (frames * inverse * gain_ref[...]).astype(BF16)
-    for out, placing in zip(row_outs, placings):
+    for out, placing in zip(outs, placings):
         out[...] = jnp.dot(placing.astype(BF16), normed, preferred_element_type=F32).astype(BF16)
+
+
+def send_grads_kernel(experts, plane_ref, *refs):
+    sources, outs, targets, semaphores = refs[:3], refs[3 : 3 + experts], refs[-4:-1], refs[-1]
+    cot_ref, routes_ref, nums_ref = targets
+    copies = fetch(semaphores, *zip(sources, targets))
     copies[1].wait()
+    copies[2].wait()
+    routes = routes_ref[...]
+    placings = placing_of(routes, plane_ref[0], experts, outs[0].shape[0])
+    gates = gates_of(routes, nums_ref[...], plane_ref[0], experts)
+    copies[0].wait()
     cot = cot_ref[...]
-    for s, (out, placing) in enumerate(zip(grad_outs, placings)):
+    for s, (out, placing) in enumerate(zip(outs, placings)):
         picked = jnp.dot(placing.astype(BF16), cot, preferred_element_type=F32)
         gate = jnp.sum(placing * gates[s : s + 1, :], -1, keepdims=True)
         out[...] = (gate * picked).astype(BF16)
@@ -302,7 +308,7 @@
         joined = [name for name in names + quick if name[0] in "cy"]
         values = [flying.pop(name) for name in names]
         if not names:
-            names, values = [("C", groups[-1][-1])], [live["C", groups[-1][-1]]]
+            names, values = [("N", groups[-1][-1])], [live["N", groups[-1][-1]]]
         values = through(values, "land", LINK_WORK, earlier)
         landed = list(zip(names, values))
         if quick:
@@ -382,20 +388,24 @@
     def in_hbm(*values):
         return [pltpu.with_memory_space_constraint(v, pltpu.HBM) for v in values]
 
-    def send():
-        sources = (tokens, cotangent, routes, gate_nums, gain)
+    def send(kind, kernel, sources):
         values = call(
-            functools.partial(send_kernel, experts),
+            functools.partial(kernel, experts),
             16,
-            "send",
-            out_shape=[piece] * (2 * experts),
-            in_specs=[scalar] + [anywhere] * len(sources),
-            out_specs=whole(2 * experts),
+            kernel.__name__[:-7],
+            out_shape=[piece] * experts,
+            in_specs=[scalar] + [anywhere] * 3,
+            out_specs=whole(experts),
             scratch_shapes=[pltpu.VMEM(v.shape, v.dtype) for v in sources]
-            + [pltpu.SemaphoreType.DMA((len(sources),))],
+            + [pltpu.SemaphoreType.DMA((3,))],
         )(plane, *in_hbm(*sources))
-        live.update({("N", s): value for s, value in enumerate(values[:experts])})
-        live.update({("C", s): value for s, value in enumerate(values[experts:])})
+        live.update({(kind, s): value for s, value in enumerate(values)})
+
+    def send_grads(kind, g):
+        if (kind, groups[-1][-1]) in live:
+            return
+        first = after(cotangent, live["N", groups[-1][-1]])
+        send(kind, send_grads_kernel, (first, routes, gate_nums))
 
     def load():
         weight = jax.ShapeDtypeStruct((width, hidden_width), BF16)
@@ -407,7 +417,7 @@
             in_specs=[anywhere] * 3,
             out_specs=whole(3),
             scratch_shapes=[pltpu.SemaphoreType.DMA((3,))],
-        )(*in_hbm(after(w_gate, live["C", groups[-1][-1]]), w_up, w_down))
+        )(*in_hbm(after(w_gate, live["N", groups[-1][-1]]), w_up, w_down))
         live.update({("w", i): value for i, value in enumerate(values)})
 
     def grad_call(turned, pieces):
@@ -465,9 +475,10 @@
         "ffn": lambda kind, g: ffn(g),
         "total": lambda kind, g: total(g),
         "load": lambda kind, g: load(),
+        "send": send_grads,
         "grad": lambda kind, g: first_grad(
-            [(0,), (1,)],
-            [("C", "own", (0,)), ("C", "own", (1,)), ("c", "C", 0), ("c", "C", 1)],
+            [(0,), (1,), (2,)],
+            [("C", "own", (i,)) for i in (0, 1, 2)] + [("c", "C", i) for i in (0, 1)],
         ),
     }
     def name_of(act):
@@ -475,8 +486,9 @@
         items = [(marks[i], int(marks[i + 1])) for i in range(0, len(marks), 2)]
         return (act[: len(act) - len(marks)],) + tuple(items)
 
-    send()
+    send("N", send_rows_kernel, (tokens, routes, gain))
     if shifts > 1:
+        send_grads("C", 0)
         z("N", 0)
         z("C", 0)
         land(("z", ("N", 0)), ("z", ("C", 0)))
@@ -492,12 +504,16 @@
                 kernels.append(live["first"])
         if lands is None:
             break
+        if lands == "none":
+            name = "C", groups[-1][-1]
+            (live[name],) = through([live[name]], "step")
+            sync()
+            continue
         land(*map(name_of, lands.split()), earlier=kernels)
-    if ("c", ("C", 3)) in flying:
-        live["c", "C", 3] = flying.pop(("c", ("C", 3)))
+    live["c", "C", 3] = flying.pop(("c", ("C", 3)))
     grad_down = last_grad(
         [(2,), (3,)],
-        [("C", "own", (2,)), ("C", "own", (3,)), ("c", "C", 2), ("c", "C", 3)],
+        [("C", "own", (3,)), ("c", "C", 2), ("c", "C", 3)],
     )
     mixed = call(
         functools.partial(combine_kernel, experts),

time: 80 us -> 79.6 us (level)
  Pallas kernels: 22.2 us -> 23.5 us
  waiting for transfers between devices: 28.1 us -> 27.2 us
  starting transfers between devices: 28.4 us -> 27.5 us
    ppermute x9, waiting for transfers between devices: 17.5 us -> 12.6 us  [turn(): return lax.ppermute(value, 'expert', to)]
    ppermute x22, waiting for transfers between devices: 10.5 us -> 14.6 us  [swap(): lax.ppermute(value, 'expert', [(i, i ^ mask) for i in range(devices)])]
    pallas_call x1 -> x2, Pallas kernels: 1.92 us -> 2.83 us  [send(): call(functools.partial(kernel, experts), 16, kernel.__name__[:-7], out_sh...]
  transfers between devices with their start and end apart: 31 -> 31, of which waited for: 12 -> 12; matrix products, arithmetic and copies ran while one was open for 0% -> 0% of each run, Pallas kernels for 22% -> 24%
where the time goes in v20:
time: 79.6 us; the launch traced here: 79.5 us
  starting transfers between devices  27.5 us (35%)
  waiting for transfers between devices  27.2 us (34%)
  Pallas kernels  23.5 us (30%)
  between operations  1.22 us (2%)
    ppermute x22, waiting for transfers between devices, swap(): lax.ppermute(value, 'expert', [(i, i ^ mask) for i in range(devices)])  14.6 us
    ppermute x9, starting transfers between devices, turn(): return lax.ppermute(value, 'expert', to)  13.9 us
    ppermute x22, starting transfers between devices, swap(): lax.ppermute(value, 'expert', [(i, i ^ mask) for i in range(devices)])  13.6 us
    ppermute x9, waiting for transfers between devices, turn(): return lax.ppermute(value, 'expert', to)  12.6 us
    pallas_call x4, Pallas kernels, ffn(): call(functools.partial(ffn_kernel, len(pieces)), 24, 'ffn', out_shape=[ja...  10.5 us
    pallas_call x1, Pallas kernels, load(): call(load_kernel, 16, 'load', out_shape=[weight, weight, jax.ShapeDtypeSt...  2.89 us
    pallas_call x2, Pallas kernels, send(): call(functools.partial(kernel, experts), 16, kernel.__name__[:-7], out_sh...  2.83 us
    pallas_call x1, Pallas kernels, last_grad(): call(functools.partial(last_grad_kernel, plan), 24, 'last_grad', out_shap...  2.66 us
  transfers between devices with their start and end apart: 31, of which 12 were waited for; matrix products, arithmetic and copies ran while one was open for 0% of the time, Pallas kernels for 24%

profile of v20, /device:TPU:0, one launch (start us, length us, event | category | flops | bytes accessed | tf_op | source)
XLA Modules:
  0.0 79.5 jit_solution(12097175690337686732)
XLA Ops:
  0.6 1.5 %send_rows.1 = (bf16[96,1024]{1,0:T(8,128)(2,1)S(1)}, bf16[96,1024]{1,0:T(8,128)(2,1)S(1)}, bf16[96,1024]{1,0:T(8,128)(2,1)S(1)}, bf16[96,1024]{1,0:T(8,128)(2,1)S(1)}) custom-call(s32[1]{0:T(128)} %bitcast.plane_ref, bf16[128,1024]{1,0:T(8,128)(2,1)} %tokens_ref.1, s32[2,128]{1,0:T(2,128)} %bitcast.4, f32[1,1024]{1,0:T(1,128)} %bitcast.9), custom_call_target="tpu_custom_call" | custom-call | tf_op jit(solution)/shard_map/send_rows/pallas_call | solution.py:392
  2.1 3.1 %collective-permute-start = (bf16[96,1024]{1,0:T(8,128)(2,1)S(1)}, bf16[96,1024]{1,0:T(8,128)(2,1)S(1)}, u32[]{:S(2)}, u32[]{:S(2)}) collective-permute-start(bf16[96,1024]{1,0:T(8,128)(2,1)S(1)} %get-tuple-element.241), channel_id=1, source_target_pairs={{0,4},{1,5},{2,6},{3,7},{4,8},{5,9},{6,10},{7,11},{8,12},{9,13},{1... | collective-permute-start | bytes 589832 | tf_op jit(solution)/shard_map/ppermute | solution.py:281
  5.2 2.1 %collective-permute-start.1 = (bf16[96,1024]{1,0:T(8,128)(2,1)S(1)}, bf16[96,1024]{1,0:T(8,128)(2,1)S(1)}, u32[]{:S(2)}, u32[]{:S(2)}) collective-permute-start(bf16[96,1024]{1,0:T(8,128)(2,1)S(1)} %get-tuple-element.242), channel_id=1, source_target_pairs={{0,12},{1,13},{2,14},{3,15},{4,0},{5,1},{6,2},{7,3},{8,4},{9,5},{1... | collective-permute-start | bytes 589832 | tf_op jit(solution)/shard_map/ppermute | solution.py:281
  7.3 1.7 %collective-permute-start.2 = (bf16[96,1024]{1,0:T(8,128)(2,1)S(1)}, bf16[96,1024]{1,0:T(8,128)(2,1)S(1)}, u32[]{:S(2)}, u32[]{:S(2)}) collective-permute-start(bf16[96,1024]{1,0:T(8,128)(2,1)S(1)} %get-tuple-element.275.first_ref), channel_id=1, source_target_pairs={{0,2},{1,3},{2,0},{3,1},{4,6},{5,7},{6,4},{7,5},{8,10},{9,11},{10,... | collective-permute-start | bytes 589832 | tf_op jit(solution)/shard_map/ppermute | solution.py:277
  9.0 1.4 %send_grads.1 = (bf16[96,1024]{1,0:T(8,128)(2,1)S(1)}, bf16[96,1024]{1,0:T(8,128)(2,1)S(1)}, bf16[96,1024]{1,0:T(8,128)(2,1)S(1)}, bf16[96,1024]{1,0:T(8,128)(2,1)S(1)}) custom-call(s32[1]{0:T(128)} %bitcast.plane_ref, bf16[128,1024]{1,0:T(8,128)(2,1)} %refs_0_.2, s32[2,128]{1,0:T(2,128)} %bitcast.5, s32[2,128]{1,0:T(2,128)} %bitcast.7), custom_call_target="tpu_custom_call" | custom-call | tf_op jit(solution)/shard_map/send_grads/pallas_call | solution.py:392
  10.3 2.9 %load.1 = (bf16[1024,1024]{1,0:T(8,128)(2,1)S(1)}, bf16[1024,1024]{1,0:T(8,128)(2,1)S(1)}, bf16[1024,1024]{1,0:T(8,128)(2,1)S(1)}) custom-call(bf16[1,1024,1024]{2,1,0:T(8,128)(2,1)} %refs_0_.3, bf16[1,1024,1024]{2,1,0:T(8,128)(2,1)} %refs_1_.1, bf16[1,1024,1024]{2,1,0:T(8,128)(2,1)} %refs_2_.1), custom_call_target="tpu_custom_call" | custom-call | tf_op jit(solution)/shard_map/load/pallas_call | solution.py:412
  14.6 1.2 %collective-permute-done.1.refs_1_ = bf16[96,1024]{1,0:T(8,128)(2,1)S(1)} collective-permute-done((bf16[96,1024]{1,0:T(8,128)(2,1)S(1)}, bf16[96,1024]{1,0:T(8,128)(2,1)S(1)}, u32[]{:S(2)}, u32[]{:S(2)}) %collective-permute-start.1) | collective-permute-done | bytes 196640 | tf_op jit(solution)/shard_map/ppermute | solution.py:281
  15.8 1.5 %collective-permute-start.3 = (bf16[96,1024]{1,0:T(8,128)(2,1)S(1)}, bf16[96,1024]{1,0:T(8,128)(2,1)S(1)}, u32[]{:S(2)}, u32[]{:S(2)}) collective-permute-start(bf16[96,1024]{1,0:T(8,128)(2,1)S(1)} %get-tuple-element.307.first_ref), channel_id=1, source_target_pairs={{0,2},{1,3},{2,0},{3,1},{4,6},{5,7},{6,4},{7,5},{8,10},{9,11},{10,... | collective-permute-start | bytes 589832 | tf_op jit(solution)/shard_map/ppermute | solution.py:277
  17.4 4.3 %collective-permute-done.5.refs_0_ = bf16[96,1024]{1,0:T(8,128)(2,1)S(1)} collective-permute-done((bf16[96,1024]{1,0:T(8,128)(2,1)S(1)}, bf16[96,1024]{1,0:T(8,128)(2,1)S(1)}, u32[]{:S(2)}, u32[]{:S(2)}) %collective-permute-start.5) | collective-permute-done | bytes 196640 | tf_op jit(solution)/shard_map/ppermute | solution.py:277
  21.8 2.6 %ffn.4 = (bf16[1024,384]{1,0:T(8,128)(2,1)S(1)}, bf16[192,1024]{1,0:T(8,128)(2,1)S(1)}, bf16[192,1024]{1,0:T(8,128)(2,1)S(1)}) custom-call(bf16[192,1024]{1,0:T(8,128)(2,1)S(1)} %pair.10.refs_0_, bf16[192,1024]{1,0:T(8,128)(2,1)S(1)} %land_core.9.refs_1_, bf16[1024,1024]{1,0:T(8,128)(2,1)S(1)} %get-tuple-element.358.refs_2_, ...), custom_call_target="tpu_custom_call" | custom-call | tf_op jit(solution)/shard_map/ffn/pallas_call | solution.py:375
  24.8 1.2 %collective-permute-done.3.refs_0_ = bf16[96,1024]{1,0:T(8,128)(2,1)S(1)} collective-permute-done((bf16[96,1024]{1,0:T(8,128)(2,1)S(1)}, bf16[96,1024]{1,0:T(8,128)(2,1)S(1)}, u32[]{:S(2)}, u32[]{:S(2)}) %collective-permute-start.3) | collective-permute-done | bytes 196640 | tf_op jit(solution)/shard_map/ppermute | solution.py:277
  26.5 0.9 %collective-permute-start.8 = (bf16[96,1024]{1,0:T(8,128)(2,1)S(1)}, bf16[96,1024]{1,0:T(8,128)(2,1)S(1)}, u32[]{:S(2)}, u32[]{:S(2)}) collective-permute-start(bf16[96,1024]{1,0:T(8,128)(2,1)S(1)} %get-tuple-element.296), channel_id=1, source_target_pairs={{0,4},{1,5},{2,6},{3,7},{4,8},{5,9},{6,10},{7,11},{8,12},{9,13},{1... | collective-permute-start | bytes 589832 | tf_op jit(solution)/shard_map/ppermute | solution.py:281
  27.4 2.9 %collective-permute-start.9 = (bf16[96,1024]{1,0:T(8,128)(2,1)S(1)}, bf16[96,1024]{1,0:T(8,128)(2,1)S(1)}, u32[]{:S(2)}, u32[]{:S(2)}) collective-permute-start(bf16[96,1024]{1,0:T(8,128)(2,1)S(1)} %get-tuple-element.297), channel_id=1, source_target_pairs={{0,12},{1,13},{2,14},{3,15},{4,0},{5,1},{6,2},{7,3},{8,4},{9,5},{1... | collective-permute-start | bytes 589832 | tf_op jit(solution)/shard_map/ppermute | solution.py:281
  30.5 2.3 %collective-permute-done.11.refs_0_ = bf16[384,1024]{1,0:T(8,128)(2,1)S(1)} collective-permute-done((bf16[384,1024]{1,0:T(8,128)(2,1)S(1)}, bf16[384,1024]{1,0:T(8,128)(2,1)S(1)}, u32[]{:S(2)}, u32[]{:S(2)}) %collective-permute-start.11) | collective-permute-done | bytes 786464 | tf_op jit(solution)/shard_map/ppermute | solution.py:277
  33.1 1.6 %collective-permute-start.15 = (bf16[96,1024]{1,0:T(8,128)(2,1)S(1)}, bf16[96,1024]{1,0:T(8,128)(2,1)S(1)}, u32[]{:S(2)}, u32[]{:S(2)}) collective-permute-start(bf16[96,1024]{1,0:T(8,128)(2,1)S(1)} %fold.4), channel_id=1, source_target_pairs={{0,2},{1,3},{2,0},{3,1},{4,6},{5,7},{6,4},{7,5},{8,10},{9,11},{10,... | collective-permute-start | bytes 589832 | tf_op jit(solution)/shard_map/ppermute | solution.py:277
  34.7 2.6 %ffn.5 = (bf16[1024,384]{1,0:T(8,128)(2,1)S(1)}, bf16[192,1024]{1,0:T(8,128)(2,1)S(1)}, bf16[192,1024]{1,0:T(8,128)(2,1)S(1)}) custom-call(bf16[192,1024]{1,0:T(8,128)(2,1)S(1)} %pair.11.second_ref.refs_0_, bf16[192,1024]{1,0:T(8,128)(2,1)S(1)} %get-tuple-element.313.refs_1_, bf16[1024,1024]{1,0:T(8,128)(2,1)S(1)} %get-tuple-element.358.refs_2_, ...), custom_call_target="tpu_custom_call" | custom-call | tf_op jit(solution)/shard_map/ffn/pallas_call | solution.py:375
  37.3 1.3 %collective-permute-done.9.refs_2_ = bf16[96,1024]{1,0:T(8,128)(2,1)S(1)} collective-permute-done((bf16[96,1024]{1,0:T(8,128)(2,1)S(1)}, bf16[96,1024]{1,0:T(8,128)(2,1)S(1)}, u32[]{:S(2)}, u32[]{:S(2)}) %collective-permute-start.9) | collective-permute-done | bytes 196640 | tf_op jit(solution)/shard_map/ppermute | solution.py:281
  39.1 1.5 %collective-permute-start.14 = (bf16[96,1024]{1,0:T(8,128)(2,1)S(1)}, bf16[96,1024]{1,0:T(8,128)(2,1)S(1)}, u32[]{:S(2)}, u32[]{:S(2)}) collective-permute-start(bf16[96,1024]{1,0:T(8,128)(2,1)S(1)} %get-tuple-element.334), channel_id=1, source_target_pairs={{0,8},{1,9},{2,10},{3,11},{4,12},{5,13},{6,14},{7,15},{8,0},{9,1},... | collective-permute-start | bytes 589832 | tf_op jit(solution)/shard_map/ppermute | solution.py:281
  40.8 2.6 %ffn.6 = (bf16[1024,384]{1,0:T(8,128)(2,1)S(1)}, bf16[192,1024]{1,0:T(8,128)(2,1)S(1)}, bf16[192,1024]{1,0:T(8,128)(2,1)S(1)}) custom-call(bf16[192,1024]{1,0:T(8,128)(2,1)S(1)} %pair.13.refs_0_, bf16[192,1024]{1,0:T(8,128)(2,1)S(1)} %land_core.11.refs_1_, bf16[1024,1024]{1,0:T(8,128)(2,1)S(1)} %get-tuple-element.358.refs_2_, ...), custom_call_target="tpu_custom_call" | custom-call | tf_op jit(solution)/shard_map/ffn/pallas_call | solution.py:375
  44.1 1.6 %collective-permute-start.18 = (bf16[96,1024]{1,0:T(8,128)(2,1)S(1)}, bf16[96,1024]{1,0:T(8,128)(2,1)S(1)}, u32[]{:S(2)}, u32[]{:S(2)}) collective-permute-start(bf16[96,1024]{1,0:T(8,128)(2,1)S(1)} %fold.5), channel_id=1, source_target_pairs={{0,2},{1,3},{2,0},{3,1},{4,6},{5,7},{6,4},{7,5},{8,10},{9,11},{10,... | collective-permute-start | bytes 589832 | tf_op jit(solution)/shard_map/ppermute | solution.py:277
  45.7 2.6 %ffn.7 = (bf16[1024,384]{1,0:T(8,128)(2,1)S(1)}, bf16[192,1024]{1,0:T(8,128)(2,1)S(1)}, bf16[192,1024]{1,0:T(8,128)(2,1)S(1)}) custom-call(bf16[192,1024]{1,0:T(8,128)(2,1)S(1)} %pair.14.second_ref.refs_0_, bf16[192,1024]{1,0:T(8,128)(2,1)S(1)} %get-tuple-element.357.refs_1_, bf16[1024,1024]{1,0:T(8,128)(2,1)S(1)} %get-tuple-element.358.refs_2_, ...), custom_call_target="tpu_custom_call" | custom-call | tf_op jit(solution)/shard_map/ffn/pallas_call | solution.py:375
  48.4 2.1 %collective-permute-done.14.refs_1_ = bf16[96,1024]{1,0:T(8,128)(2,1)S(1)} collective-permute-done((bf16[96,1024]{1,0:T(8,128)(2,1)S(1)}, bf16[96,1024]{1,0:T(8,128)(2,1)S(1)}, u32[]{:S(2)}, u32[]{:S(2)}) %collective-permute-start.14) | collective-permute-done | bytes 196640 | tf_op jit(solution)/shard_map/ppermute | solution.py:281
  50.7 1.4 %collective-permute-start.20 = (bf16[96,1024]{1,0:T(8,128)(2,1)S(1)}, bf16[96,1024]{1,0:T(8,128)(2,1)S(1)}, u32[]{:S(2)}, u32[]{:S(2)}) collective-permute-start(bf16[96,1024]{1,0:T(8,128)(2,1)S(1)} %fold.6), channel_id=1, source_target_pairs={{0,2},{1,3},{2,0},{3,1},{4,6},{5,7},{6,4},{7,5},{8,10},{9,11},{10,... | collective-permute-start | bytes 589832 | tf_op jit(solution)/shard_map/ppermute | solution.py:277
  53.0 1.5 %collective-permute-start.21 = (bf16[96,1024]{1,0:T(8,128)(2,1)S(1)}, bf16[96,1024]{1,0:T(8,128)(2,1)S(1)}, u32[]{:S(2)}, u32[]{:S(2)}) collective-permute-start(bf16[96,1024]{1,0:T(8,128)(2,1)S(1)} %total.5), channel_id=1, source_target_pairs={{0,12},{1,13},{2,14},{3,15},{4,0},{5,1},{6,2},{7,3},{8,4},{9,5},{1... | collective-permute-start | bytes 589832 | tf_op jit(solution)/shard_map/ppermute | solution.py:281
  54.5 4.1 %collective-permute-done.20.refs_0_ = bf16[96,1024]{1,0:T(8,128)(2,1)S(1)} collective-permute-done((bf16[96,1024]{1,0:T(8,128)(2,1)S(1)}, bf16[96,1024]{1,0:T(8,128)(2,1)S(1)}, u32[]{:S(2)}, u32[]{:S(2)}) %collective-permute-start.20) | collective-permute-done | bytes 196640 | tf_op jit(solution)/shard_map/ppermute | solution.py:277
  58.9 1.5 %collective-permute-start.24 = (bf16[96,1024]{1,0:T(8,128)(2,1)S(1)}, bf16[96,1024]{1,0:T(8,128)(2,1)S(1)}, u32[]{:S(2)}, u32[]{:S(2)}) collective-permute-start(bf16[96,1024]{1,0:T(8,128)(2,1)S(1)} %get-tuple-element.463.first_ref), channel_id=1, source_target_pairs={{0,2},{1,3},{2,0},{3,1},{4,6},{5,7},{6,4},{7,5},{8,10},{9,11},{10,... | collective-permute-start | bytes 589832 | tf_op jit(solution)/shard_map/ppermute | solution.py:277
  60.5 2.3 %collective-permute-done.22.refs_1_ = bf16[96,1024]{1,0:T(8,128)(2,1)S(1)} collective-permute-done((bf16[96,1024]{1,0:T(8,128)(2,1)S(1)}, bf16[96,1024]{1,0:T(8,128)(2,1)S(1)}, u32[]{:S(2)}, u32[]{:S(2)}) %collective-permute-start.22) | collective-permute-done | bytes 196640 | tf_op jit(solution)/shard_map/ppermute | solution.py:277
  64.5 1.9 %collective-permute-done.25.refs_1_ = bf16[96,1024]{1,0:T(8,128)(2,1)S(1)} collective-permute-done((bf16[96,1024]{1,0:T(8,128)(2,1)S(1)}, bf16[96,1024]{1,0:T(8,128)(2,1)S(1)}, u32[]{:S(2)}, u32[]{:S(2)}) %collective-permute-start.25) | collective-permute-done | bytes 196640 | tf_op jit(solution)/shard_map/ppermute | solution.py:281
  66.5 2.4 %first_grad.1.refs_2_.first_ref = f32[1024,1024]{1,0:T(8,128)S(1)} custom-call(bf16[1024,384]{1,0:T(8,128)(2,1)S(1)} %get-tuple-element.453.refs_2_.refs_0_, bf16[1024,384]{1,0:T(8,128)(2,1)S(1)} %get-tuple-element.454.refs_3_.refs_1_, bf16[1024,384]{1,0:T(8,128)(2,1)S(1)} %get-tuple-element.475.refs_1_.refs_2_.refs_0_, bf16[192,1024]{1,0:T(8,128)(2,1)S(1)} %pair.16.refs_3_, ...), custom_call_target="tpu_custom_call" | custom-call | tf_op jit(solution)/shard_map/first_grad/pallas_call | solution.py:447
  69.0 5.8 %collective-permute-done.28.refs_1_ = bf16[96,1024]{1,0:T(8,128)(2,1)S(1)} collective-permute-done((bf16[96,1024]{1,0:T(8,128)(2,1)S(1)}, bf16[96,1024]{1,0:T(8,128)(2,1)S(1)}, u32[]{:S(2)}, u32[]{:S(2)}) %collective-permute-start.28) | collective-permute-done | bytes 196640 | tf_op jit(solution)/shard_map/ppermute | solution.py:281
  75.0 1.4 %combine.1 = bf16[128,1024]{1,0:T(8,128)(2,1)} custom-call(s32[1]{0:T(128)} %bitcast.plane_ref, bf16[128,1024]{1,0:T(8,128)(2,1)S(1)} %copy-done, s32[2,128]{1,0:T(2,128)S(1)} %bitcast.6, s32[2,128]{1,0:T(2,128)S(1)} %bitcast.8, bf16[96,1024]{1,0:T(8,128)(2,1)S(1)} %total.4.refs_0_, bf16[96,1024]{1,0:T(8,128)(2,1)S(1)} %get-tuple-element.471.refs_1_, ...), custom_call_target="tpu_custom_call" | custom-call | tf_op jit(solution)/shard_map/combine/pallas_call | solution.py:518
  76.6 2.7 %last_grad.1 = bf16[1,1024,1024]{2,1,0:T(8,128)(2,1)} custom-call(f32[1024,1024]{1,0:T(8,128)S(1)} %first_grad.1.refs_2_.first_ref, bf16[1024,384]{1,0:T(8,128)(2,1)S(1)} %get-tuple-element.475.refs_1_.refs_2_.refs_0_, bf16[1024,384]{1,0:T(8,128)(2,1)S(1)} %get-tuple-element.476.refs_2_.refs_1_, bf16[192,1024]{1,0:T(8,128)(2,1)S(1)} %pair.19.refs_2_, ...), custom_call_target="tpu_custom_call" | custom-call | tf_op jit(solution)/shard_map/last_grad/pallas_call | solution.py:459
  (88 shorter events, 7.9 us)
Async XLA Ops:
  2.1 12.5 %collective-permute-start = (bf16[96,1024]{1,0:T(8,128)(2,1)S(1)}, bf16[96,1024]{1,0:T(8,128)(2,1)S(1)}, u32[]{:S(2)}, u32[]{:S(2)}) collective-permute-start(bf16[96,1024]{1,0:T(8,128)(2,1)S(1)} %get-tuple-element.241), channel_id=1, source_target_pairs={{0,4},{1,5},{2,6},{3,7},{4,8},{5,9},{6,10},{7,11},{8,12},{9,13},{1... | collective-permute-start | bytes 589832 | tf_op jit(solution)/shard_map/ppermute | solution.py:281
  5.2 10.6 %collective-permute-start.1 = (bf16[96,1024]{1,0:T(8,128)(2,1)S(1)}, bf16[96,1024]{1,0:T(8,128)(2,1)S(1)}, u32[]{:S(2)}, u32[]{:S(2)}) collective-permute-start(bf16[96,1024]{1,0:T(8,128)(2,1)S(1)} %get-tuple-element.242), channel_id=1, source_target_pairs={{0,12},{1,13},{2,14},{3,15},{4,0},{5,1},{6,2},{7,3},{8,4},{9,5},{1... | collective-permute-start | bytes 589832 | tf_op jit(solution)/shard_map/ppermute | solution.py:281
  7.3 8.5 %collective-permute-start.2 = (bf16[96,1024]{1,0:T(8,128)(2,1)S(1)}, bf16[96,1024]{1,0:T(8,128)(2,1)S(1)}, u32[]{:S(2)}, u32[]{:S(2)}) collective-permute-start(bf16[96,1024]{1,0:T(8,128)(2,1)S(1)} %get-tuple-element.275.first_ref), channel_id=1, source_target_pairs={{0,2},{1,3},{2,0},{3,1},{4,6},{5,7},{6,4},{7,5},{8,10},{9,11},{10,... | collective-permute-start | bytes 589832 | tf_op jit(solution)/shard_map/ppermute | solution.py:277
  13.2 11.5 %collective-permute-start.4 = (bf16[96,1024]{1,0:T(8,128)(2,1)S(1)}, bf16[96,1024]{1,0:T(8,128)(2,1)S(1)}, u32[]{:S(2)}, u32[]{:S(2)}) collective-permute-start(bf16[96,1024]{1,0:T(8,128)(2,1)S(1)} %land.14), channel_id=1, source_target_pairs={{0,8},{1,9},{2,10},{3,11},{4,12},{5,13},{6,14},{7,15},{8,0},{9,1},... | collective-permute-start | bytes 589832 | tf_op jit(solution)/shard_map/ppermute | solution.py:281
  14.1 7.7 %collective-permute-start.5 = (bf16[96,1024]{1,0:T(8,128)(2,1)S(1)}, bf16[96,1024]{1,0:T(8,128)(2,1)S(1)}, u32[]{:S(2)}, u32[]{:S(2)}) collective-permute-start(bf16[96,1024]{1,0:T(8,128)(2,1)S(1)} %get-tuple-element.431.first_ref), channel_id=1, source_target_pairs={{0,2},{1,3},{2,0},{3,1},{4,6},{5,7},{6,4},{7,5},{8,10},{9,11},{10,... | collective-permute-start | bytes 589832 | tf_op jit(solution)/shard_map/ppermute | solution.py:277
  15.8 10.2 %collective-permute-start.3 = (bf16[96,1024]{1,0:T(8,128)(2,1)S(1)}, bf16[96,1024]{1,0:T(8,128)(2,1)S(1)}, u32[]{:S(2)}, u32[]{:S(2)}) collective-permute-start(bf16[96,1024]{1,0:T(8,128)(2,1)S(1)} %get-tuple-element.307.first_ref), channel_id=1, source_target_pairs={{0,2},{1,3},{2,0},{3,1},{4,6},{5,7},{6,4},{7,5},{8,10},{9,11},{10,... | collective-permute-start | bytes 589832 | tf_op jit(solution)/shard_map/ppermute | solution.py:277
  17.3 4.4 %collective-permute-start.6 = (bf16[192,1024]{1,0:T(8,128)(2,1)S(1)}, bf16[192,1024]{1,0:T(8,128)(2,1)S(1)}, u32[]{:S(2)}, u32[]{:S(2)}) collective-permute-start(bf16[192,1024]{1,0:T(8,128)(2,1)S(1)} %pair.10.refs_0_), channel_id=1, source_target_pairs={{0,1},{1,0},{2,3},{3,2},{4,5},{5,4},{6,7},{7,6},{8,9},{9,8},{10,11... | collective-permute-start | bytes 1179656 | tf_op jit(solution)/shard_map/ppermute | solution.py:277
  21.8 8.7 %collective-permute-start.10 = (bf16[96,1024]{1,0:T(8,128)(2,1)S(1)}, bf16[96,1024]{1,0:T(8,128)(2,1)S(1)}, u32[]{:S(2)}, u32[]{:S(2)}) collective-permute-start(bf16[96,1024]{1,0:T(8,128)(2,1)S(1)} %get-tuple-element.329.first_ref), channel_id=1, source_target_pairs={{0,2},{1,3},{2,0},{3,1},{4,6},{5,7},{6,4},{7,5},{8,10},{9,11},{10,... | collective-permute-start | bytes 589832 | tf_op jit(solution)/shard_map/ppermute | solution.py:277
  26.0 11.3 %collective-permute-start.7 = (bf16[96,1024]{1,0:T(8,128)(2,1)S(1)}, bf16[96,1024]{1,0:T(8,128)(2,1)S(1)}, u32[]{:S(2)}, u32[]{:S(2)}) collective-permute-start(bf16[96,1024]{1,0:T(8,128)(2,1)S(1)} %get-tuple-element.346.first_ref), channel_id=1, source_target_pairs={{0,2},{1,3},{2,0},{3,1},{4,6},{5,7},{6,4},{7,5},{8,10},{9,11},{10,... | collective-permute-start | bytes 589832 | tf_op jit(solution)/shard_map/ppermute | solution.py:277
  26.5 10.8 %collective-permute-start.8 = (bf16[96,1024]{1,0:T(8,128)(2,1)S(1)}, bf16[96,1024]{1,0:T(8,128)(2,1)S(1)}, u32[]{:S(2)}, u32[]{:S(2)}) collective-permute-start(bf16[96,1024]{1,0:T(8,128)(2,1)S(1)} %get-tuple-element.296), channel_id=1, source_target_pairs={{0,4},{1,5},{2,6},{3,7},{4,8},{5,9},{6,10},{7,11},{8,12},{9,13},{1... | collective-permute-start | bytes 589832 | tf_op jit(solution)/shard_map/ppermute | solution.py:281
  27.4 11.2 %collective-permute-start.9 = (bf16[96,1024]{1,0:T(8,128)(2,1)S(1)}, bf16[96,1024]{1,0:T(8,128)(2,1)S(1)}, u32[]{:S(2)}, u32[]{:S(2)}) collective-permute-start(bf16[96,1024]{1,0:T(8,128)(2,1)S(1)} %get-tuple-element.297), channel_id=1, source_target_pairs={{0,12},{1,13},{2,14},{3,15},{4,0},{5,1},{6,2},{7,3},{8,4},{9,5},{1... | collective-permute-start | bytes 589832 | tf_op jit(solution)/shard_map/ppermute | solution.py:281
  30.4 2.4 %collective-permute-start.11 = (bf16[384,1024]{1,0:T(8,128)(2,1)S(1)}, bf16[384,1024]{1,0:T(8,128)(2,1)S(1)}, u32[]{:S(2)}, u32[]{:S(2)}) collective-permute-start(bf16[384,1024]{1,0:T(8,128)(2,1)S(1)} %pair.12), channel_id=1, source_target_pairs={{0,1},{1,0},{2,3},{3,2},{4,5},{5,4},{6,7},{7,6},{8,9},{9,8},{10,11... | collective-permute-start | bytes 2359304 | tf_op jit(solution)/shard_map/ppermute | solution.py:277
  32.8 5.8 %collective-permute-start.12 = (bf16[192,1024]{1,0:T(8,128)(2,1)S(1)}, bf16[192,1024]{1,0:T(8,128)(2,1)S(1)}, u32[]{:S(2)}, u32[]{:S(2)}) collective-permute-start(bf16[192,1024]{1,0:T(8,128)(2,1)S(1)} %pair.13.refs_0_), channel_id=1, source_target_pairs={{0,1},{1,0},{2,3},{3,2},{4,5},{5,4},{6,7},{7,6},{8,9},{9,8},{10,11... | collective-permute-start | bytes 1179656 | tf_op jit(solution)/shard_map/ppermute | solution.py:277
  33.1 10.3 %collective-permute-start.15 = (bf16[96,1024]{1,0:T(8,128)(2,1)S(1)}, bf16[96,1024]{1,0:T(8,128)(2,1)S(1)}, u32[]{:S(2)}, u32[]{:S(2)}) collective-permute-start(bf16[96,1024]{1,0:T(8,128)(2,1)S(1)} %fold.4), channel_id=1, source_target_pairs={{0,2},{1,3},{2,0},{3,1},{4,6},{5,7},{6,4},{7,5},{8,10},{9,11},{10,... | collective-permute-start | bytes 589832 | tf_op jit(solution)/shard_map/ppermute | solution.py:277
  38.6 9.8 %collective-permute-start.13 = (bf16[96,1024]{1,0:T(8,128)(2,1)S(1)}, bf16[96,1024]{1,0:T(8,128)(2,1)S(1)}, u32[]{:S(2)}, u32[]{:S(2)}) collective-permute-start(bf16[96,1024]{1,0:T(8,128)(2,1)S(1)} %get-tuple-element.449.first_ref), channel_id=1, source_target_pairs={{0,2},{1,3},{2,0},{3,1},{4,6},{5,7},{6,4},{7,5},{8,10},{9,11},{10,... | collective-permute-start | bytes 589832 | tf_op jit(solution)/shard_map/ppermute | solution.py:277
  39.1 11.5 %collective-permute-start.14 = (bf16[96,1024]{1,0:T(8,128)(2,1)S(1)}, bf16[96,1024]{1,0:T(8,128)(2,1)S(1)}, u32[]{:S(2)}, u32[]{:S(2)}) collective-permute-start(bf16[96,1024]{1,0:T(8,128)(2,1)S(1)} %get-tuple-element.334), channel_id=1, source_target_pairs={{0,8},{1,9},{2,10},{3,11},{4,12},{5,13},{6,14},{7,15},{8,0},{9,1},... | collective-permute-start | bytes 589832 | tf_op jit(solution)/shard_map/ppermute | solution.py:281
  40.7 2.7 %collective-permute-start.16 = (bf16[384,1024]{1,0:T(8,128)(2,1)S(1)}, bf16[384,1024]{1,0:T(8,128)(2,1)S(1)}, u32[]{:S(2)}, u32[]{:S(2)}) collective-permute-start(bf16[384,1024]{1,0:T(8,128)(2,1)S(1)} %pair.15), channel_id=1, source_target_pairs={{0,1},{1,0},{2,3},{3,2},{4,5},{5,4},{6,7},{7,6},{8,9},{9,8},{10,11... | collective-permute-start | bytes 2359304 | tf_op jit(solution)/shard_map/ppermute | solution.py:277
  43.5 7.2 %collective-permute-start.17 = (bf16[192,1024]{1,0:T(8,128)(2,1)S(1)}, bf16[192,1024]{1,0:T(8,128)(2,1)S(1)}, u32[]{:S(2)}, u32[]{:S(2)}) collective-permute-start(bf16[192,1024]{1,0:T(8,128)(2,1)S(1)} %get-tuple-element.378), channel_id=1, source_target_pairs={{0,1},{1,0},{2,3},{3,2},{4,5},{5,4},{6,7},{7,6},{8,9},{9,8},{10,11... | collective-permute-start | bytes 1179656 | tf_op jit(solution)/shard_map/ppermute | solution.py:277
  44.1 8.0 %collective-permute-start.18 = (bf16[96,1024]{1,0:T(8,128)(2,1)S(1)}, bf16[96,1024]{1,0:T(8,128)(2,1)S(1)}, u32[]{:S(2)}, u32[]{:S(2)}) collective-permute-start(bf16[96,1024]{1,0:T(8,128)(2,1)S(1)} %fold.5), channel_id=1, source_target_pairs={{0,2},{1,3},{2,0},{3,1},{4,6},{5,7},{6,4},{7,5},{8,10},{9,11},{10,... | collective-permute-start | bytes 589832 | tf_op jit(solution)/shard_map/ppermute | solution.py:277
  48.3 3.8 %collective-permute-start.19 = (bf16[192,1024]{1,0:T(8,128)(2,1)S(1)}, bf16[192,1024]{1,0:T(8,128)(2,1)S(1)}, u32[]{:S(2)}, u32[]{:S(2)}) collective-permute-start(bf16[192,1024]{1,0:T(8,128)(2,1)S(1)} %get-tuple-element.396), channel_id=1, source_target_pairs={{0,1},{1,0},{2,3},{3,2},{4,5},{5,4},{6,7},{7,6},{8,9},{9,8},{10,11... | collective-permute-start | bytes 1179656 | tf_op jit(solution)/shard_map/ppermute | solution.py:277
  50.7 7.9 %collective-permute-start.20 = (bf16[96,1024]{1,0:T(8,128)(2,1)S(1)}, bf16[96,1024]{1,0:T(8,128)(2,1)S(1)}, u32[]{:S(2)}, u32[]{:S(2)}) collective-permute-start(bf16[96,1024]{1,0:T(8,128)(2,1)S(1)} %fold.6), channel_id=1, source_target_pairs={{0,2},{1,3},{2,0},{3,1},{4,6},{5,7},{6,4},{7,5},{8,10},{9,11},{10,... | collective-permute-start | bytes 589832 | tf_op jit(solution)/shard_map/ppermute | solution.py:277
  52.2 10.6 %collective-permute-start.22 = (bf16[96,1024]{1,0:T(8,128)(2,1)S(1)}, bf16[96,1024]{1,0:T(8,128)(2,1)S(1)}, u32[]{:S(2)}, u32[]{:S(2)}) collective-permute-start(bf16[96,1024]{1,0:T(8,128)(2,1)S(1)} %fold.7), channel_id=1, source_target_pairs={{0,2},{1,3},{2,0},{3,1},{4,6},{5,7},{6,4},{7,5},{8,10},{9,11},{10,... | collective-permute-start | bytes 589832 | tf_op jit(solution)/shard_map/ppermute | solution.py:277
  53.0 9.8 %collective-permute-start.21 = (bf16[96,1024]{1,0:T(8,128)(2,1)S(1)}, bf16[96,1024]{1,0:T(8,128)(2,1)S(1)}, u32[]{:S(2)}, u32[]{:S(2)}) collective-permute-start(bf16[96,1024]{1,0:T(8,128)(2,1)S(1)} %total.5), channel_id=1, source_target_pairs={{0,12},{1,13},{2,14},{3,15},{4,0},{5,1},{6,2},{7,3},{8,4},{9,5},{1... | collective-permute-start | bytes 589832 | tf_op jit(solution)/shard_map/ppermute | solution.py:281
  58.7 7.7 %collective-permute-start.25 = (bf16[96,1024]{1,0:T(8,128)(2,1)S(1)}, bf16[96,1024]{1,0:T(8,128)(2,1)S(1)}, u32[]{:S(2)}, u32[]{:S(2)}) collective-permute-start(bf16[96,1024]{1,0:T(8,128)(2,1)S(1)} %total.6), channel_id=1, source_target_pairs={{0,4},{1,5},{2,6},{3,7},{4,8},{5,9},{6,10},{7,11},{8,12},{9,13},{1... | collective-permute-start | bytes 589832 | tf_op jit(solution)/shard_map/ppermute | solution.py:281
  58.9 7.5 %collective-permute-start.24 = (bf16[96,1024]{1,0:T(8,128)(2,1)S(1)}, bf16[96,1024]{1,0:T(8,128)(2,1)S(1)}, u32[]{:S(2)}, u32[]{:S(2)}) collective-permute-start(bf16[96,1024]{1,0:T(8,128)(2,1)S(1)} %get-tuple-element.463.first_ref), channel_id=1, source_target_pairs={{0,2},{1,3},{2,0},{3,1},{4,6},{5,7},{6,4},{7,5},{8,10},{9,11},{10,... | collective-permute-start | bytes 589832 | tf_op jit(solution)/shard_map/ppermute | solution.py:277
  60.4 2.4 %collective-permute-start.23 = (bf16[192,1024]{1,0:T(8,128)(2,1)S(1)}, bf16[192,1024]{1,0:T(8,128)(2,1)S(1)}, u32[]{:S(2)}, u32[]{:S(2)}) collective-permute-start(bf16[192,1024]{1,0:T(8,128)(2,1)S(1)} %pair.16.refs_3_), channel_id=1, source_target_pairs={{0,1},{1,0},{2,3},{3,2},{4,5},{5,4},{6,7},{7,6},{8,9},{9,8},{10,11... | collective-permute-start | bytes 1179656 | tf_op jit(solution)/shard_map/ppermute | solution.py:277
  62.9 11.9 %collective-permute-start.28 = (bf16[96,1024]{1,0:T(8,128)(2,1)S(1)}, bf16[96,1024]{1,0:T(8,128)(2,1)S(1)}, u32[]{:S(2)}, u32[]{:S(2)}) collective-permute-start(bf16[96,1024]{1,0:T(8,128)(2,1)S(1)} %total.7), channel_id=1, source_target_pairs={{0,8},{1,9},{2,10},{3,11},{4,12},{5,13},{6,14},{7,15},{8,0},{9,1},... | collective-permute-start | bytes 589832 | tf_op jit(solution)/shard_map/ppermute | solution.py:281
  63.7 11.1 %collective-permute-start.27 = (bf16[96,1024]{1,0:T(8,128)(2,1)S(1)}, bf16[96,1024]{1,0:T(8,128)(2,1)S(1)}, u32[]{:S(2)}, u32[]{:S(2)}) collective-permute-start(bf16[96,1024]{1,0:T(8,128)(2,1)S(1)} %get-tuple-element.477.first_ref), channel_id=1, source_target_pairs={{0,2},{1,3},{2,0},{3,1},{4,6},{5,7},{6,4},{7,5},{8,10},{9,11},{10,... | collective-permute-start | bytes 589832 | tf_op jit(solution)/shard_map/ppermute | solution.py:277
  64.5 1.9 %collective-permute-start.26 = (bf16[192,1024]{1,0:T(8,128)(2,1)S(1)}, bf16[192,1024]{1,0:T(8,128)(2,1)S(1)}, u32[]{:S(2)}, u32[]{:S(2)}) collective-permute-start(bf16[192,1024]{1,0:T(8,128)(2,1)S(1)} %pair.17.refs_4_), channel_id=1, source_target_pairs={{0,1},{1,0},{2,3},{3,2},{4,5},{5,4},{6,7},{7,6},{8,9},{9,8},{10,11... | collective-permute-start | bytes 1179656 | tf_op jit(solution)/shard_map/ppermute | solution.py:277
  66.5 8.3 %collective-permute-start.29 = (bf16[192,1024]{1,0:T(8,128)(2,1)S(1)}, bf16[192,1024]{1,0:T(8,128)(2,1)S(1)}, u32[]{:S(2)}, u32[]{:S(2)}) collective-permute-start(bf16[192,1024]{1,0:T(8,128)(2,1)S(1)} %pair.18.refs_5_), channel_id=1, source_target_pairs={{0,1},{1,0},{2,3},{3,2},{4,5},{5,4},{6,7},{7,6},{8,9},{9,8},{10,11... | collective-permute-start | bytes 1179656 | tf_op jit(solution)/shard_map/ppermute | solution.py:277
  68.9 6.0 %copy-start = (bf16[128,1024]{1,0:T(8,128)(2,1)S(1)}, bf16[128,1024]{1,0:T(8,128)(2,1)}, u32[]{:S(2)}) copy-start(bf16[128,1024]{1,0:T(8,128)(2,1)} %tokens_ref.1) | copy-start | bytes 786436
  74.8 1.8 %collective-permute-start.30 = (bf16[192,1024]{1,0:T(8,128)(2,1)S(1)}, bf16[192,1024]{1,0:T(8,128)(2,1)S(1)}, u32[]{:S(2)}, u32[]{:S(2)}) collective-permute-start(bf16[192,1024]{1,0:T(8,128)(2,1)S(1)} %pair.19.refs_2_), channel_id=1, source_target_pairs={{0,1},{1,0},{2,3},{3,2},{4,5},{5,4},{6,7},{7,6},{8,9},{9,8},{10,11... | collective-permute-start | bytes 1179656 | tf_op jit(solution)/shard_map/ppermute | solution.py:277
  (2 other events, 12.0 us)

commit v21 on v20

--- a/solution.py
+++ b/solution.py
@@ -15,14 +15,14 @@
     ("cN0 yN1", "yC0 cN0"),
     ("ffnN0 yN2", "yN1 zN3"),
     ("cR0N1 yN3 zC1 zC2", "yN2 cR0N1"),
-    ("ffnN1 cN2 yR0", "yN3 zC1 zC2 cN2"),
-    ("cR1N3 ffnN2 yC1 zC3", "yR0 cR1N3"),
-    ("cR2 ffnN3 cR3 yR1 totalR0", "yC1 zC3 cR2"),
+    ("ffnN1 cN2C0", "yN3 zC1 zC2 cN2C0"),
+    ("cR1N3 ffnN2 yC1 zC3", "cR1N3"),
+    ("cR2 ffnN3 cR3 yR1", "yC1 zC3 cR2"),
     ("yR2", "yR1 cR3"),
     ("totalR1 zR1 yR3", "yR2"),
-    ("totalR2 zR2 yC2 cC0", "zR1 yR3 cC0"),
-    ("totalR3 zR3 yC3 cC1", "yC2 zR2 cC1"),
-    ("cC2 gradC0", "yC3 zR3 cC2"),
+    ("totalR2 zR2 yC2R0", "zR1 yR3"),
+    ("totalR3 zR3 yC3 cC1", "yC2R0 zR2 cC1"),
+    ("totalR0 cC2 gradC0", "yC3 zR3 cC2"),
     ("cC3", None),
 )
 TILE = 256

time: 79.6 us -> 83.6 us (1.050)
  starting transfers between devices: 27.5 us -> 29.3 us
  waiting for transfers between devices: 27.2 us -> 28.6 us
    ppermute x9, waiting for transfers between devices: 12.6 us -> 19.5 us  [turn(): return lax.ppermute(value, 'expert', to)]
    ppermute x22 -> x20, waiting for transfers between devices: 14.6 us -> 9.05 us  [swap(): lax.ppermute(value, 'expert', [(i, i ^ mask) for i in range(devices)])]
    ppermute x9, starting transfers between devices: 13.9 us -> 15.9 us  [turn(): return lax.ppermute(value, 'expert', to)]
    ppermute x22 -> x20, starting transfers between devices: 13.6 us -> 13.4 us  [swap(): lax.ppermute(value, 'expert', [(i, i ^ mask) for i in range(devices)])]
  transfers between devices with their start and end apart: 31 -> 29, of which waited for: 12 -> 11; matrix products, arithmetic and copies ran while one was open for 0% -> 0% of each run, Pallas kernels for 24% -> 23%
where the time goes in v21:
time: 83.6 us; the launch traced here: 83.4 us
  starting transfers between devices  29.3 us (35%)
  waiting for transfers between devices  28.6 us (34%)
  Pallas kernels  23.7 us (28%)
  between operations  1.15 us (1%)
    ppermute x9, waiting for transfers between devices, turn(): return lax.ppermute(value, 'expert', to)  19.5 us
    ppermute x9, starting transfers between devices, turn(): return lax.ppermute(value, 'expert', to)  15.9 us
    ppermute x20, starting transfers between devices, swap(): lax.ppermute(value, 'expert', [(i, i ^ mask) for i in range(devices)])  13.4 us
    pallas_call x4, Pallas kernels, ffn(): call(functools.partial(ffn_kernel, len(pieces)), 24, 'ffn', out_shape=[ja...  10.5 us
    ppermute x20, waiting for transfers between devices, swap(): lax.ppermute(value, 'expert', [(i, i ^ mask) for i in range(devices)])  9.05 us
    pallas_call x1, Pallas kernels, load(): call(load_kernel, 16, 'load', out_shape=[weight, weight, jax.ShapeDtypeSt...  2.89 us
    pallas_call x2, Pallas kernels, send(): call(functools.partial(kernel, experts), 16, kernel.__name__[:-7], out_sh...  2.83 us
    pallas_call x1, Pallas kernels, last_grad(): call(functools.partial(last_grad_kernel, plan), 24, 'last_grad', out_shap...  2.66 us
  transfers between devices with their start and end apart: 29, of which 11 were waited for; matrix products, arithmetic and copies ran while one was open for 0% of the time, Pallas kernels for 23%

profile of v21, /device:TPU:0, one launch (start us, length us, event | category | flops | bytes accessed | tf_op | source)
XLA Modules:
  0.0 83.4 jit_solution(5062758988569562832)
XLA Ops:
  0.6 1.5 %send_rows.1 = (bf16[96,1024]{1,0:T(8,128)(2,1)S(1)}, bf16[96,1024]{1,0:T(8,128)(2,1)S(1)}, bf16[96,1024]{1,0:T(8,128)(2,1)S(1)}, bf16[96,1024]{1,0:T(8,128)(2,1)S(1)}) custom-call(s32[1]{0:T(128)} %bitcast.plane_ref, bf16[128,1024]{1,0:T(8,128)(2,1)} %tokens_ref.1, s32[2,128]{1,0:T(2,128)} %bitcast.4, f32[1,1024]{1,0:T(1,128)} %bitcast.9), custom_call_target="tpu_custom_call" | custom-call | tf_op jit(solution)/shard_map/send_rows/pallas_call | solution.py:392
  2.1 3.1 %collective-permute-start = (bf16[96,1024]{1,0:T(8,128)(2,1)S(1)}, bf16[96,1024]{1,0:T(8,128)(2,1)S(1)}, u32[]{:S(2)}, u32[]{:S(2)}) collective-permute-start(bf16[96,1024]{1,0:T(8,128)(2,1)S(1)} %get-tuple-element.246), channel_id=1, source_target_pairs={{0,4},{1,5},{2,6},{3,7},{4,8},{5,9},{6,10},{7,11},{8,12},{9,13},{1... | collective-permute-start | bytes 589832 | tf_op jit(solution)/shard_map/ppermute | solution.py:281
  5.2 2.1 %collective-permute-start.1 = (bf16[96,1024]{1,0:T(8,128)(2,1)S(1)}, bf16[96,1024]{1,0:T(8,128)(2,1)S(1)}, u32[]{:S(2)}, u32[]{:S(2)}) collective-permute-start(bf16[96,1024]{1,0:T(8,128)(2,1)S(1)} %get-tuple-element.247), channel_id=1, source_target_pairs={{0,12},{1,13},{2,14},{3,15},{4,0},{5,1},{6,2},{7,3},{8,4},{9,5},{1... | collective-permute-start | bytes 589832 | tf_op jit(solution)/shard_map/ppermute | solution.py:281
  7.3 1.7 %collective-permute-start.2 = (bf16[96,1024]{1,0:T(8,128)(2,1)S(1)}, bf16[96,1024]{1,0:T(8,128)(2,1)S(1)}, u32[]{:S(2)}, u32[]{:S(2)}) collective-permute-start(bf16[96,1024]{1,0:T(8,128)(2,1)S(1)} %get-tuple-element.280.first_ref), channel_id=1, source_target_pairs={{0,2},{1,3},{2,0},{3,1},{4,6},{5,7},{6,4},{7,5},{8,10},{9,11},{10,... | collective-permute-start | bytes 589832 | tf_op jit(solution)/shard_map/ppermute | solution.py:277
  9.0 1.4 %send_grads.1 = (bf16[96,1024]{1,0:T(8,128)(2,1)S(1)}, bf16[96,1024]{1,0:T(8,128)(2,1)S(1)}, bf16[96,1024]{1,0:T(8,128)(2,1)S(1)}, bf16[96,1024]{1,0:T(8,128)(2,1)S(1)}) custom-call(s32[1]{0:T(128)} %bitcast.plane_ref, bf16[128,1024]{1,0:T(8,128)(2,1)} %refs_0_.2, s32[2,128]{1,0:T(2,128)} %bitcast.5, s32[2,128]{1,0:T(2,128)} %bitcast.7), custom_call_target="tpu_custom_call" | custom-call | tf_op jit(solution)/shard_map/send_grads/pallas_call | solution.py:392
  10.3 2.9 %load.1 = (bf16[1024,1024]{1,0:T(8,128)(2,1)S(1)}, bf16[1024,1024]{1,0:T(8,128)(2,1)S(1)}, bf16[1024,1024]{1,0:T(8,128)(2,1)S(1)}) custom-call(bf16[1,1024,1024]{2,1,0:T(8,128)(2,1)} %refs_0_.3, bf16[1,1024,1024]{2,1,0:T(8,128)(2,1)} %refs_1_.1, bf16[1,1024,1024]{2,1,0:T(8,128)(2,1)} %refs_2_.1), custom_call_target="tpu_custom_call" | custom-call | tf_op jit(solution)/shard_map/load/pallas_call | solution.py:412
  15.9 1.6 %collective-permute-start.3 = (bf16[96,1024]{1,0:T(8,128)(2,1)S(1)}, bf16[96,1024]{1,0:T(8,128)(2,1)S(1)}, u32[]{:S(2)}, u32[]{:S(2)}) collective-permute-start(bf16[96,1024]{1,0:T(8,128)(2,1)S(1)} %get-tuple-element.312.first_ref), channel_id=1, source_target_pairs={{0,2},{1,3},{2,0},{3,1},{4,6},{5,7},{6,4},{7,5},{8,10},{9,11},{10,... | collective-permute-start | bytes 589832 | tf_op jit(solution)/shard_map/ppermute | solution.py:277
  17.5 1.9 %collective-permute-done.5.refs_0_ = bf16[96,1024]{1,0:T(8,128)(2,1)S(1)} collective-permute-done((bf16[96,1024]{1,0:T(8,128)(2,1)S(1)}, bf16[96,1024]{1,0:T(8,128)(2,1)S(1)}, u32[]{:S(2)}, u32[]{:S(2)}) %collective-permute-start.5) | collective-permute-done | bytes 196640 | tf_op jit(solution)/shard_map/ppermute | solution.py:277
  19.7 2.6 %ffn.4 = (bf16[1024,384]{1,0:T(8,128)(2,1)S(1)}, bf16[192,1024]{1,0:T(8,128)(2,1)S(1)}, bf16[192,1024]{1,0:T(8,128)(2,1)S(1)}) custom-call(bf16[192,1024]{1,0:T(8,128)(2,1)S(1)} %pair.12.refs_0_, bf16[192,1024]{1,0:T(8,128)(2,1)S(1)} %land_core.7.refs_1_, bf16[1024,1024]{1,0:T(8,128)(2,1)S(1)} %get-tuple-element.363.refs_2_, ...), custom_call_target="tpu_custom_call" | custom-call | tf_op jit(solution)/shard_map/ffn/pallas_call | solution.py:375
  22.4 2.4 %collective-permute-done.4.refs_1_ = bf16[96,1024]{1,0:T(8,128)(2,1)S(1)} collective-permute-done((bf16[96,1024]{1,0:T(8,128)(2,1)S(1)}, bf16[96,1024]{1,0:T(8,128)(2,1)S(1)}, u32[]{:S(2)}, u32[]{:S(2)}) %collective-permute-start.4) | collective-permute-done | bytes 196640 | tf_op jit(solution)/shard_map/ppermute | solution.py:281
  24.9 1.6 %collective-permute-start.7 = (bf16[96,1024]{1,0:T(8,128)(2,1)S(1)}, bf16[96,1024]{1,0:T(8,128)(2,1)S(1)}, u32[]{:S(2)}, u32[]{:S(2)}) collective-permute-start(bf16[96,1024]{1,0:T(8,128)(2,1)S(1)} %get-tuple-element.352.first_ref), channel_id=1, source_target_pairs={{0,2},{1,3},{2,0},{3,1},{4,6},{5,7},{6,4},{7,5},{8,10},{9,11},{10,... | collective-permute-start | bytes 589832 | tf_op jit(solution)/shard_map/ppermute | solution.py:277
  26.5 1.2 %collective-permute-start.8 = (bf16[96,1024]{1,0:T(8,128)(2,1)S(1)}, bf16[96,1024]{1,0:T(8,128)(2,1)S(1)}, u32[]{:S(2)}, u32[]{:S(2)}) collective-permute-start(bf16[96,1024]{1,0:T(8,128)(2,1)S(1)} %get-tuple-element.301), channel_id=1, source_target_pairs={{0,4},{1,5},{2,6},{3,7},{4,8},{5,9},{6,10},{7,11},{8,12},{9,13},{1... | collective-permute-start | bytes 589832 | tf_op jit(solution)/shard_map/ppermute | solution.py:281
  27.7 2.6 %collective-permute-start.9 = (bf16[96,1024]{1,0:T(8,128)(2,1)S(1)}, bf16[96,1024]{1,0:T(8,128)(2,1)S(1)}, u32[]{:S(2)}, u32[]{:S(2)}) collective-permute-start(bf16[96,1024]{1,0:T(8,128)(2,1)S(1)} %get-tuple-element.302), channel_id=1, source_target_pairs={{0,12},{1,13},{2,14},{3,15},{4,0},{5,1},{6,2},{7,3},{8,4},{9,5},{1... | collective-permute-start | bytes 589832 | tf_op jit(solution)/shard_map/ppermute | solution.py:281
  30.6 2.6 %ffn.5 = (bf16[1024,384]{1,0:T(8,128)(2,1)S(1)}, bf16[192,1024]{1,0:T(8,128)(2,1)S(1)}, bf16[192,1024]{1,0:T(8,128)(2,1)S(1)}) custom-call(bf16[192,1024]{1,0:T(8,128)(2,1)S(1)} %pair.13.second_ref.refs_0_, bf16[192,1024]{1,0:T(8,128)(2,1)S(1)} %get-tuple-element.318.refs_1_, bf16[1024,1024]{1,0:T(8,128)(2,1)S(1)} %get-tuple-element.363.refs_2_, ...), custom_call_target="tpu_custom_call" | custom-call | tf_op jit(solution)/shard_map/ffn/pallas_call | solution.py:375
  33.3 2.8 %collective-permute-done.8.refs_1_ = bf16[96,1024]{1,0:T(8,128)(2,1)S(1)} collective-permute-done((bf16[96,1024]{1,0:T(8,128)(2,1)S(1)}, bf16[96,1024]{1,0:T(8,128)(2,1)S(1)}, u32[]{:S(2)}, u32[]{:S(2)}) %collective-permute-start.8) | collective-permute-done | bytes 196640 | tf_op jit(solution)/shard_map/ppermute | solution.py:281
  36.1 3.4 %collective-permute-done.9.refs_2_ = bf16[96,1024]{1,0:T(8,128)(2,1)S(1)} collective-permute-done((bf16[96,1024]{1,0:T(8,128)(2,1)S(1)}, bf16[96,1024]{1,0:T(8,128)(2,1)S(1)}, u32[]{:S(2)}, u32[]{:S(2)}) %collective-permute-start.9) | collective-permute-done | bytes 196640 | tf_op jit(solution)/shard_map/ppermute | solution.py:281
  40.3 2.6 %collective-permute-start.14 = (bf16[96,1024]{1,0:T(8,128)(2,1)S(1)}, bf16[96,1024]{1,0:T(8,128)(2,1)S(1)}, u32[]{:S(2)}, u32[]{:S(2)}) collective-permute-start(bf16[96,1024]{1,0:T(8,128)(2,1)S(1)} %get-tuple-element.339), channel_id=1, source_target_pairs={{0,8},{1,9},{2,10},{3,11},{4,12},{5,13},{6,14},{7,15},{8,0},{9,1},... | collective-permute-start | bytes 589832 | tf_op jit(solution)/shard_map/ppermute | solution.py:281
  42.9 2.6 %ffn.6 = (bf16[1024,384]{1,0:T(8,128)(2,1)S(1)}, bf16[192,1024]{1,0:T(8,128)(2,1)S(1)}, bf16[192,1024]{1,0:T(8,128)(2,1)S(1)}) custom-call(bf16[192,1024]{1,0:T(8,128)(2,1)S(1)} %pair.15.first_ref.refs_0_, bf16[192,1024]{1,0:T(8,128)(2,1)S(1)} %get-tuple-element.355.refs_1_, bf16[1024,1024]{1,0:T(8,128)(2,1)S(1)} %get-tuple-element.363.refs_2_, ...), custom_call_target="tpu_custom_call" | custom-call | tf_op jit(solution)/shard_map/ffn/pallas_call | solution.py:375
  45.8 1.6 %collective-permute-start.17 = (bf16[96,1024]{1,0:T(8,128)(2,1)S(1)}, bf16[96,1024]{1,0:T(8,128)(2,1)S(1)}, u32[]{:S(2)}, u32[]{:S(2)}) collective-permute-start(bf16[96,1024]{1,0:T(8,128)(2,1)S(1)} %fold.4), channel_id=1, source_target_pairs={{0,2},{1,3},{2,0},{3,1},{4,6},{5,7},{6,4},{7,5},{8,10},{9,11},{10,... | collective-permute-start | bytes 589832 | tf_op jit(solution)/shard_map/ppermute | solution.py:277
  47.4 2.6 %ffn.7 = (bf16[1024,384]{1,0:T(8,128)(2,1)S(1)}, bf16[192,1024]{1,0:T(8,128)(2,1)S(1)}, bf16[192,1024]{1,0:T(8,128)(2,1)S(1)}) custom-call(bf16[192,1024]{1,0:T(8,128)(2,1)S(1)} %pair.18.second_ref.refs_0_, bf16[192,1024]{1,0:T(8,128)(2,1)S(1)} %get-tuple-element.362.refs_1_, bf16[1024,1024]{1,0:T(8,128)(2,1)S(1)} %get-tuple-element.363.refs_2_, ...), custom_call_target="tpu_custom_call" | custom-call | tf_op jit(solution)/shard_map/ffn/pallas_call | solution.py:375
  50.3 2.2 %collective-permute-done.14.refs_1_ = bf16[96,1024]{1,0:T(8,128)(2,1)S(1)} collective-permute-done((bf16[96,1024]{1,0:T(8,128)(2,1)S(1)}, bf16[96,1024]{1,0:T(8,128)(2,1)S(1)}, u32[]{:S(2)}, u32[]{:S(2)}) %collective-permute-start.14) | collective-permute-done | bytes 196640 | tf_op jit(solution)/shard_map/ppermute | solution.py:281
  52.5 1.6 %collective-permute-start.19 = (bf16[96,1024]{1,0:T(8,128)(2,1)S(1)}, bf16[96,1024]{1,0:T(8,128)(2,1)S(1)}, u32[]{:S(2)}, u32[]{:S(2)}) collective-permute-start(bf16[96,1024]{1,0:T(8,128)(2,1)S(1)} %fold.5), channel_id=1, source_target_pairs={{0,2},{1,3},{2,0},{3,1},{4,6},{5,7},{6,4},{7,5},{8,10},{9,11},{10,... | collective-permute-start | bytes 589832 | tf_op jit(solution)/shard_map/ppermute | solution.py:277
  54.9 2.3 %collective-permute-start.20 = (bf16[96,1024]{1,0:T(8,128)(2,1)S(1)}, bf16[96,1024]{1,0:T(8,128)(2,1)S(1)}, u32[]{:S(2)}, u32[]{:S(2)}) collective-permute-start(bf16[96,1024]{1,0:T(8,128)(2,1)S(1)} %total.4), channel_id=1, source_target_pairs={{0,12},{1,13},{2,14},{3,15},{4,0},{5,1},{6,2},{7,3},{8,4},{9,5},{1... | collective-permute-start | bytes 589832 | tf_op jit(solution)/shard_map/ppermute | solution.py:281
  57.2 3.2 %collective-permute-done.19.refs_0_ = bf16[96,1024]{1,0:T(8,128)(2,1)S(1)} collective-permute-done((bf16[96,1024]{1,0:T(8,128)(2,1)S(1)}, bf16[96,1024]{1,0:T(8,128)(2,1)S(1)}, u32[]{:S(2)}, u32[]{:S(2)}) %collective-permute-start.19) | collective-permute-done | bytes 196640 | tf_op jit(solution)/shard_map/ppermute | solution.py:277
  60.4 1.6 %collective-permute-start.22 = (bf16[192,1024]{1,0:T(8,128)(2,1)S(1)}, bf16[192,1024]{1,0:T(8,128)(2,1)S(1)}, u32[]{:S(2)}, u32[]{:S(2)}) collective-permute-start(bf16[192,1024]{1,0:T(8,128)(2,1)S(1)} %pair.20), channel_id=1, source_target_pairs={{0,2},{1,3},{2,0},{3,1},{4,6},{5,7},{6,4},{7,5},{8,10},{9,11},{10,... | collective-permute-start | bytes 1179656 | tf_op jit(solution)/shard_map/ppermute | solution.py:277
  62.4 2.2 %collective-permute-done.21.refs_1_ = bf16[96,1024]{1,0:T(8,128)(2,1)S(1)} collective-permute-done((bf16[96,1024]{1,0:T(8,128)(2,1)S(1)}, bf16[96,1024]{1,0:T(8,128)(2,1)S(1)}, u32[]{:S(2)}, u32[]{:S(2)}) %collective-permute-start.21) | collective-permute-done | bytes 196640 | tf_op jit(solution)/shard_map/ppermute | solution.py:277
  66.5 4.8 %collective-permute-done.23.refs_1_ = bf16[96,1024]{1,0:T(8,128)(2,1)S(1)} collective-permute-done((bf16[96,1024]{1,0:T(8,128)(2,1)S(1)}, bf16[96,1024]{1,0:T(8,128)(2,1)S(1)}, u32[]{:S(2)}, u32[]{:S(2)}) %collective-permute-start.23) | collective-permute-done | bytes 196640 | tf_op jit(solution)/shard_map/ppermute | solution.py:281
  71.2 1.8 %collective-permute-done.22.refs_0_ = bf16[192,1024]{1,0:T(8,128)(2,1)S(1)} collective-permute-done((bf16[192,1024]{1,0:T(8,128)(2,1)S(1)}, bf16[192,1024]{1,0:T(8,128)(2,1)S(1)}, u32[]{:S(2)}, u32[]{:S(2)}) %collective-permute-start.22) | collective-permute-done | bytes 393248 | tf_op jit(solution)/shard_map/ppermute | solution.py:277
  73.1 2.4 %first_grad.1.refs_2_.first_ref = f32[1024,1024]{1,0:T(8,128)S(1)} custom-call(bf16[1024,384]{1,0:T(8,128)(2,1)S(1)} %get-tuple-element.460.refs_2_.refs_0_, bf16[1024,384]{1,0:T(8,128)(2,1)S(1)} %get-tuple-element.461.refs_3_.refs_1_, bf16[1024,384]{1,0:T(8,128)(2,1)S(1)} %get-tuple-element.485.refs_1_.refs_2_.refs_0_, ...), custom_call_target="tpu_custom_call" | custom-call | tf_op jit(solution)/shard_map/first_grad/pallas_call | solution.py:447
  75.6 2.7 %collective-permute-done.26.refs_1_ = bf16[96,1024]{1,0:T(8,128)(2,1)S(1)} collective-permute-done((bf16[96,1024]{1,0:T(8,128)(2,1)S(1)}, bf16[96,1024]{1,0:T(8,128)(2,1)S(1)}, u32[]{:S(2)}, u32[]{:S(2)}) %collective-permute-start.26) | collective-permute-done | bytes 196640 | tf_op jit(solution)/shard_map/ppermute | solution.py:281
  79.2 1.4 %combine.1 = bf16[128,1024]{1,0:T(8,128)(2,1)} custom-call(s32[1]{0:T(128)} %bitcast.plane_ref, bf16[128,1024]{1,0:T(8,128)(2,1)S(1)} %copy-done, s32[2,128]{1,0:T(2,128)S(1)} %bitcast.6, s32[2,128]{1,0:T(2,128)S(1)} %bitcast.8, bf16[96,1024]{1,0:T(8,128)(2,1)S(1)} %total.7.refs_0_, bf16[96,1024]{1,0:T(8,128)(2,1)S(1)} %get-tuple-element.481.refs_1_, ...), custom_call_target="tpu_custom_call" | custom-call | tf_op jit(solution)/shard_map/combine/pallas_call | solution.py:518
  80.6 2.7 %last_grad.1 = bf16[1,1024,1024]{2,1,0:T(8,128)(2,1)} custom-call(f32[1024,1024]{1,0:T(8,128)S(1)} %first_grad.1.refs_2_.first_ref, bf16[1024,384]{1,0:T(8,128)(2,1)S(1)} %get-tuple-element.485.refs_1_.refs_2_.refs_0_, bf16[1024,384]{1,0:T(8,128)(2,1)S(1)} %get-tuple-element.486.refs_2_.refs_1_, bf16[192,1024]{1,0:T(8,128)(2,1)S(1)} %pair.23.refs_2_, ...), custom_call_target="tpu_custom_call" | custom-call | tf_op jit(solution)/shard_map/last_grad/pallas_call | solution.py:459
  (86 shorter events, 8.7 us)
Async XLA Ops:
  2.1 12.5 %collective-permute-start = (bf16[96,1024]{1,0:T(8,128)(2,1)S(1)}, bf16[96,1024]{1,0:T(8,128)(2,1)S(1)}, u32[]{:S(2)}, u32[]{:S(2)}) collective-permute-start(bf16[96,1024]{1,0:T(8,128)(2,1)S(1)} %get-tuple-element.246), channel_id=1, source_target_pairs={{0,4},{1,5},{2,6},{3,7},{4,8},{5,9},{6,10},{7,11},{8,12},{9,13},{1... | collective-permute-start | bytes 589832 | tf_op jit(solution)/shard_map/ppermute | solution.py:281
  5.2 10.6 %collective-permute-start.1 = (bf16[96,1024]{1,0:T(8,128)(2,1)S(1)}, bf16[96,1024]{1,0:T(8,128)(2,1)S(1)}, u32[]{:S(2)}, u32[]{:S(2)}) collective-permute-start(bf16[96,1024]{1,0:T(8,128)(2,1)S(1)} %get-tuple-element.247), channel_id=1, source_target_pairs={{0,12},{1,13},{2,14},{3,15},{4,0},{5,1},{6,2},{7,3},{8,4},{9,5},{1... | collective-permute-start | bytes 589832 | tf_op jit(solution)/shard_map/ppermute | solution.py:281
  7.3 8.5 %collective-permute-start.2 = (bf16[96,1024]{1,0:T(8,128)(2,1)S(1)}, bf16[96,1024]{1,0:T(8,128)(2,1)S(1)}, u32[]{:S(2)}, u32[]{:S(2)}) collective-permute-start(bf16[96,1024]{1,0:T(8,128)(2,1)S(1)} %get-tuple-element.280.first_ref), channel_id=1, source_target_pairs={{0,2},{1,3},{2,0},{3,1},{4,6},{5,7},{6,4},{7,5},{8,10},{9,11},{10,... | collective-permute-start | bytes 589832 | tf_op jit(solution)/shard_map/ppermute | solution.py:277
  13.2 6.1 %collective-permute-start.5 = (bf16[96,1024]{1,0:T(8,128)(2,1)S(1)}, bf16[96,1024]{1,0:T(8,128)(2,1)S(1)}, u32[]{:S(2)}, u32[]{:S(2)}) collective-permute-start(bf16[96,1024]{1,0:T(8,128)(2,1)S(1)} %get-tuple-element.334.first_ref), channel_id=1, source_target_pairs={{0,2},{1,3},{2,0},{3,1},{4,6},{5,7},{6,4},{7,5},{8,10},{9,11},{10,... | collective-permute-start | bytes 589832 | tf_op jit(solution)/shard_map/ppermute | solution.py:277
  13.6 11.1 %collective-permute-start.4 = (bf16[96,1024]{1,0:T(8,128)(2,1)S(1)}, bf16[96,1024]{1,0:T(8,128)(2,1)S(1)}, u32[]{:S(2)}, u32[]{:S(2)}) collective-permute-start(bf16[96,1024]{1,0:T(8,128)(2,1)S(1)} %land.14), channel_id=1, source_target_pairs={{0,8},{1,9},{2,10},{3,11},{4,12},{5,13},{6,14},{7,15},{8,0},{9,1},... | collective-permute-start | bytes 589832 | tf_op jit(solution)/shard_map/ppermute | solution.py:281
  15.8 3.6 %collective-permute-start.6 = (bf16[192,1024]{1,0:T(8,128)(2,1)S(1)}, bf16[192,1024]{1,0:T(8,128)(2,1)S(1)}, u32[]{:S(2)}, u32[]{:S(2)}) collective-permute-start(bf16[192,1024]{1,0:T(8,128)(2,1)S(1)} %pair.12.refs_0_), channel_id=1, source_target_pairs={{0,1},{1,0},{2,3},{3,2},{4,5},{5,4},{6,7},{7,6},{8,9},{9,8},{10,11... | collective-permute-start | bytes 1179656 | tf_op jit(solution)/shard_map/ppermute | solution.py:277
  15.9 8.9 %collective-permute-start.3 = (bf16[96,1024]{1,0:T(8,128)(2,1)S(1)}, bf16[96,1024]{1,0:T(8,128)(2,1)S(1)}, u32[]{:S(2)}, u32[]{:S(2)}) collective-permute-start(bf16[96,1024]{1,0:T(8,128)(2,1)S(1)} %get-tuple-element.312.first_ref), channel_id=1, source_target_pairs={{0,2},{1,3},{2,0},{3,1},{4,6},{5,7},{6,4},{7,5},{8,10},{9,11},{10,... | collective-permute-start | bytes 589832 | tf_op jit(solution)/shard_map/ppermute | solution.py:277
  19.4 11.0 %collective-permute-start.10 = (bf16[96,1024]{1,0:T(8,128)(2,1)S(1)}, bf16[96,1024]{1,0:T(8,128)(2,1)S(1)}, u32[]{:S(2)}, u32[]{:S(2)}) collective-permute-start(bf16[96,1024]{1,0:T(8,128)(2,1)S(1)} %get-tuple-element.332.first_ref), channel_id=1, source_target_pairs={{0,2},{1,3},{2,0},{3,1},{4,6},{5,7},{6,4},{7,5},{8,10},{9,11},{10,... | collective-permute-start | bytes 589832 | tf_op jit(solution)/shard_map/ppermute | solution.py:277
  24.9 5.5 %collective-permute-start.11 = (bf16[384,1024]{1,0:T(8,128)(2,1)S(1)}, bf16[384,1024]{1,0:T(8,128)(2,1)S(1)}, u32[]{:S(2)}, u32[]{:S(2)}) collective-permute-start(bf16[384,1024]{1,0:T(8,128)(2,1)S(1)} %pair.14), channel_id=1, source_target_pairs={{0,1},{1,0},{2,3},{3,2},{4,5},{5,4},{6,7},{7,6},{8,9},{9,8},{10,11... | collective-permute-start | bytes 2359304 | tf_op jit(solution)/shard_map/ppermute | solution.py:277
  24.9 8.3 %collective-permute-start.7 = (bf16[96,1024]{1,0:T(8,128)(2,1)S(1)}, bf16[96,1024]{1,0:T(8,128)(2,1)S(1)}, u32[]{:S(2)}, u32[]{:S(2)}) collective-permute-start(bf16[96,1024]{1,0:T(8,128)(2,1)S(1)} %get-tuple-element.352.first_ref), channel_id=1, source_target_pairs={{0,2},{1,3},{2,0},{3,1},{4,6},{5,7},{6,4},{7,5},{8,10},{9,11},{10,... | collective-permute-start | bytes 589832 | tf_op jit(solution)/shard_map/ppermute | solution.py:277
  26.5 9.5 %collective-permute-start.8 = (bf16[96,1024]{1,0:T(8,128)(2,1)S(1)}, bf16[96,1024]{1,0:T(8,128)(2,1)S(1)}, u32[]{:S(2)}, u32[]{:S(2)}) collective-permute-start(bf16[96,1024]{1,0:T(8,128)(2,1)S(1)} %get-tuple-element.301), channel_id=1, source_target_pairs={{0,4},{1,5},{2,6},{3,7},{4,8},{5,9},{6,10},{7,11},{8,12},{9,13},{1... | collective-permute-start | bytes 589832 | tf_op jit(solution)/shard_map/ppermute | solution.py:281
  27.7 11.8 %collective-permute-start.9 = (bf16[96,1024]{1,0:T(8,128)(2,1)S(1)}, bf16[96,1024]{1,0:T(8,128)(2,1)S(1)}, u32[]{:S(2)}, u32[]{:S(2)}) collective-permute-start(bf16[96,1024]{1,0:T(8,128)(2,1)S(1)} %get-tuple-element.302), channel_id=1, source_target_pairs={{0,12},{1,13},{2,14},{3,15},{4,0},{5,1},{6,2},{7,3},{8,4},{9,5},{1... | collective-permute-start | bytes 589832 | tf_op jit(solution)/shard_map/ppermute | solution.py:281
  30.5 9.0 %collective-permute-start.12 = (bf16[384,1024]{1,0:T(8,128)(2,1)S(1)}, bf16[384,1024]{1,0:T(8,128)(2,1)S(1)}, u32[]{:S(2)}, u32[]{:S(2)}) collective-permute-start(bf16[384,1024]{1,0:T(8,128)(2,1)S(1)} %pair.17), channel_id=1, source_target_pairs={{0,1},{1,0},{2,3},{3,2},{4,5},{5,4},{6,7},{7,6},{8,9},{9,8},{10,11... | collective-permute-start | bytes 2359304 | tf_op jit(solution)/shard_map/ppermute | solution.py:277
  39.6 6.0 %collective-permute-start.15 = (bf16[384,1024]{1,0:T(8,128)(2,1)S(1)}, bf16[384,1024]{1,0:T(8,128)(2,1)S(1)}, u32[]{:S(2)}, u32[]{:S(2)}) collective-permute-start(bf16[384,1024]{1,0:T(8,128)(2,1)S(1)} %pair.19), channel_id=1, source_target_pairs={{0,1},{1,0},{2,3},{3,2},{4,5},{5,4},{6,7},{7,6},{8,9},{9,8},{10,11... | collective-permute-start | bytes 2359304 | tf_op jit(solution)/shard_map/ppermute | solution.py:277
  39.8 10.5 %collective-permute-start.13 = (bf16[96,1024]{1,0:T(8,128)(2,1)S(1)}, bf16[96,1024]{1,0:T(8,128)(2,1)S(1)}, u32[]{:S(2)}, u32[]{:S(2)}) collective-permute-start(bf16[96,1024]{1,0:T(8,128)(2,1)S(1)} %get-tuple-element.456.first_ref), channel_id=1, source_target_pairs={{0,2},{1,3},{2,0},{3,1},{4,6},{5,7},{6,4},{7,5},{8,10},{9,11},{10,... | collective-permute-start | bytes 589832 | tf_op jit(solution)/shard_map/ppermute | solution.py:277
  40.3 12.1 %collective-permute-start.14 = (bf16[96,1024]{1,0:T(8,128)(2,1)S(1)}, bf16[96,1024]{1,0:T(8,128)(2,1)S(1)}, u32[]{:S(2)}, u32[]{:S(2)}) collective-permute-start(bf16[96,1024]{1,0:T(8,128)(2,1)S(1)} %get-tuple-element.339), channel_id=1, source_target_pairs={{0,8},{1,9},{2,10},{3,11},{4,12},{5,13},{6,14},{7,15},{8,0},{9,1},... | collective-permute-start | bytes 589832 | tf_op jit(solution)/shard_map/ppermute | solution.py:281
  45.6 6.8 %collective-permute-start.16 = (bf16[192,1024]{1,0:T(8,128)(2,1)S(1)}, bf16[192,1024]{1,0:T(8,128)(2,1)S(1)}, u32[]{:S(2)}, u32[]{:S(2)}) collective-permute-start(bf16[192,1024]{1,0:T(8,128)(2,1)S(1)} %get-tuple-element.382), channel_id=1, source_target_pairs={{0,1},{1,0},{2,3},{3,2},{4,5},{5,4},{6,7},{7,6},{8,9},{9,8},{10,11... | collective-permute-start | bytes 1179656 | tf_op jit(solution)/shard_map/ppermute | solution.py:277
  45.8 8.4 %collective-permute-start.17 = (bf16[96,1024]{1,0:T(8,128)(2,1)S(1)}, bf16[96,1024]{1,0:T(8,128)(2,1)S(1)}, u32[]{:S(2)}, u32[]{:S(2)}) collective-permute-start(bf16[96,1024]{1,0:T(8,128)(2,1)S(1)} %fold.4), channel_id=1, source_target_pairs={{0,2},{1,3},{2,0},{3,1},{4,6},{5,7},{6,4},{7,5},{8,10},{9,11},{10,... | collective-permute-start | bytes 589832 | tf_op jit(solution)/shard_map/ppermute | solution.py:277
  50.0 4.2 %collective-permute-start.18 = (bf16[192,1024]{1,0:T(8,128)(2,1)S(1)}, bf16[192,1024]{1,0:T(8,128)(2,1)S(1)}, u32[]{:S(2)}, u32[]{:S(2)}) collective-permute-start(bf16[192,1024]{1,0:T(8,128)(2,1)S(1)} %get-tuple-element.401), channel_id=1, source_target_pairs={{0,1},{1,0},{2,3},{3,2},{4,5},{5,4},{6,7},{7,6},{8,9},{9,8},{10,11... | collective-permute-start | bytes 1179656 | tf_op jit(solution)/shard_map/ppermute | solution.py:277
  52.5 7.8 %collective-permute-start.19 = (bf16[96,1024]{1,0:T(8,128)(2,1)S(1)}, bf16[96,1024]{1,0:T(8,128)(2,1)S(1)}, u32[]{:S(2)}, u32[]{:S(2)}) collective-permute-start(bf16[96,1024]{1,0:T(8,128)(2,1)S(1)} %fold.5), channel_id=1, source_target_pairs={{0,2},{1,3},{2,0},{3,1},{4,6},{5,7},{6,4},{7,5},{8,10},{9,11},{10,... | collective-permute-start | bytes 589832 | tf_op jit(solution)/shard_map/ppermute | solution.py:277
  54.2 10.4 %collective-permute-start.21 = (bf16[96,1024]{1,0:T(8,128)(2,1)S(1)}, bf16[96,1024]{1,0:T(8,128)(2,1)S(1)}, u32[]{:S(2)}, u32[]{:S(2)}) collective-permute-start(bf16[96,1024]{1,0:T(8,128)(2,1)S(1)} %fold.6), channel_id=1, source_target_pairs={{0,2},{1,3},{2,0},{3,1},{4,6},{5,7},{6,4},{7,5},{8,10},{9,11},{10,... | collective-permute-start | bytes 589832 | tf_op jit(solution)/shard_map/ppermute | solution.py:277
  54.9 9.7 %collective-permute-start.20 = (bf16[96,1024]{1,0:T(8,128)(2,1)S(1)}, bf16[96,1024]{1,0:T(8,128)(2,1)S(1)}, u32[]{:S(2)}, u32[]{:S(2)}) collective-permute-start(bf16[96,1024]{1,0:T(8,128)(2,1)S(1)} %total.4), channel_id=1, source_target_pairs={{0,12},{1,13},{2,14},{3,15},{4,0},{5,1},{6,2},{7,3},{8,4},{9,5},{1... | collective-permute-start | bytes 589832 | tf_op jit(solution)/shard_map/ppermute | solution.py:281
  60.4 12.6 %collective-permute-start.22 = (bf16[192,1024]{1,0:T(8,128)(2,1)S(1)}, bf16[192,1024]{1,0:T(8,128)(2,1)S(1)}, u32[]{:S(2)}, u32[]{:S(2)}) collective-permute-start(bf16[192,1024]{1,0:T(8,128)(2,1)S(1)} %pair.20), channel_id=1, source_target_pairs={{0,2},{1,3},{2,0},{3,1},{4,6},{5,7},{6,4},{7,5},{8,10},{9,11},{10,... | collective-permute-start | bytes 1179656 | tf_op jit(solution)/shard_map/ppermute | solution.py:277
  62.1 9.1 %collective-permute-start.23 = (bf16[96,1024]{1,0:T(8,128)(2,1)S(1)}, bf16[96,1024]{1,0:T(8,128)(2,1)S(1)}, u32[]{:S(2)}, u32[]{:S(2)}) collective-permute-start(bf16[96,1024]{1,0:T(8,128)(2,1)S(1)} %total.5), channel_id=1, source_target_pairs={{0,4},{1,5},{2,6},{3,7},{4,8},{5,9},{6,10},{7,11},{8,12},{9,13},{1... | collective-permute-start | bytes 589832 | tf_op jit(solution)/shard_map/ppermute | solution.py:281
  64.6 8.4 %collective-permute-start.24 = (bf16[192,1024]{1,0:T(8,128)(2,1)S(1)}, bf16[192,1024]{1,0:T(8,128)(2,1)S(1)}, u32[]{:S(2)}, u32[]{:S(2)}) collective-permute-start(bf16[192,1024]{1,0:T(8,128)(2,1)S(1)} %pair.21.refs_4_), channel_id=1, source_target_pairs={{0,1},{1,0},{2,3},{3,2},{4,5},{5,4},{6,7},{7,6},{8,9},{9,8},{10,11... | collective-permute-start | bytes 1179656 | tf_op jit(solution)/shard_map/ppermute | solution.py:277
  64.8 13.5 %collective-permute-start.26 = (bf16[96,1024]{1,0:T(8,128)(2,1)S(1)}, bf16[96,1024]{1,0:T(8,128)(2,1)S(1)}, u32[]{:S(2)}, u32[]{:S(2)}) collective-permute-start(bf16[96,1024]{1,0:T(8,128)(2,1)S(1)} %total.6), channel_id=1, source_target_pairs={{0,8},{1,9},{2,10},{3,11},{4,12},{5,13},{6,14},{7,15},{8,0},{9,1},... | collective-permute-start | bytes 589832 | tf_op jit(solution)/shard_map/ppermute | solution.py:281
  65.6 12.7 %collective-permute-start.25 = (bf16[96,1024]{1,0:T(8,128)(2,1)S(1)}, bf16[96,1024]{1,0:T(8,128)(2,1)S(1)}, u32[]{:S(2)}, u32[]{:S(2)}) collective-permute-start(bf16[96,1024]{1,0:T(8,128)(2,1)S(1)} %get-tuple-element.487.first_ref), channel_id=1, source_target_pairs={{0,2},{1,3},{2,0},{3,1},{4,6},{5,7},{6,4},{7,5},{8,10},{9,11},{10,... | collective-permute-start | bytes 589832 | tf_op jit(solution)/shard_map/ppermute | solution.py:277
  73.1 5.3 %collective-permute-start.27 = (bf16[192,1024]{1,0:T(8,128)(2,1)S(1)}, bf16[192,1024]{1,0:T(8,128)(2,1)S(1)}, u32[]{:S(2)}, u32[]{:S(2)}) collective-permute-start(bf16[192,1024]{1,0:T(8,128)(2,1)S(1)} %pair.22.refs_5_), channel_id=1, source_target_pairs={{0,1},{1,0},{2,3},{3,2},{4,5},{5,4},{6,7},{7,6},{8,9},{9,8},{10,11... | collective-permute-start | bytes 1179656 | tf_op jit(solution)/shard_map/ppermute | solution.py:277
  78.3 1.0 %copy-start = (bf16[128,1024]{1,0:T(8,128)(2,1)S(1)}, bf16[128,1024]{1,0:T(8,128)(2,1)}, u32[]{:S(2)}) copy-start(bf16[128,1024]{1,0:T(8,128)(2,1)} %tokens_ref.1) | copy-start | bytes 786436
  78.3 1.0 %copy-start.1 = (s32[128,2]{0,1:T(2,128)S(1)}, s32[128,2]{0,1:T(2,128)}, u32[]{:S(2)}) copy-start(s32[128,2]{0,1:T(2,128)} %param.10) | copy-start | bytes 3076
  78.3 0.9 %copy-start.2 = (s32[128,2]{0,1:T(2,128)S(1)}, s32[128,2]{0,1:T(2,128)}, u32[]{:S(2)}) copy-start(s32[128,2]{0,1:T(2,128)} %param.11) | copy-start | bytes 3076
  78.4 2.2 %collective-permute-start.28 = (bf16[192,1024]{1,0:T(8,128)(2,1)S(1)}, bf16[192,1024]{1,0:T(8,128)(2,1)S(1)}, u32[]{:S(2)}, u32[]{:S(2)}) collective-permute-start(bf16[192,1024]{1,0:T(8,128)(2,1)S(1)} %pair.23.refs_2_), channel_id=1, source_target_pairs={{0,1},{1,0},{2,3},{3,2},{4,5},{5,4},{6,7},{7,6},{8,9},{9,8},{10,11... | collective-permute-start | bytes 1179656 | tf_op jit(solution)/shard_map/ppermute | solution.py:277

commit v22 on v20

--- a/solution.py
+++ b/solution.py
@@ -10,12 +10,12 @@
 HSPLIT = 4
 GROUPS = 4
 PLAN = (
-    ("yN0 zN1 zN2 sendC0 loadW0", ""),
-    ("yC0 zN3", "zN1 zN2 yN0"),
+    ("yN0 zN2 zN1 sendC0 loadW0", ""),
+    ("yC0 zN3", "zN2 zN1 yN0"),
     ("cN0 yN1", "yC0 cN0"),
     ("ffnN0 yN2", "yN1 zN3"),
-    ("cR0N1 yN3 zC1 zC2", "yN2 cR0N1"),
-    ("ffnN1 cN2 yR0", "yN3 zC1 zC2 cN2"),
+    ("cR0N1 yN3 zC2 zC1", "yN2 cR0N1"),
+    ("ffnN1 cN2 yR0", "yN3 zC2 zC1 cN2"),
     ("cR1N3 ffnN2 yC1 zC3", "yR0 cR1N3"),
     ("cR2 ffnN3 cR3 yR1 totalR0", "yC1 zC3 cR2"),
     ("yR2", "yR1 cR3"),

time: 79.6 us -> 77.9 us (0.979)
  waiting for transfers between devices: 27.2 us -> 21.3 us
  starting transfers between devices: 27.5 us -> 31.6 us
    ppermute x22, waiting for transfers between devices: 14.6 us -> 11.2 us  [swap(): lax.ppermute(value, 'expert', [(i, i ^ mask) for i in range(devices)])]
    ppermute x9, starting transfers between devices: 13.9 us -> 17.1 us  [turn(): return lax.ppermute(value, 'expert', to)]
    ppermute x9, waiting for transfers between devices: 12.6 us -> 10.1 us  [turn(): return lax.ppermute(value, 'expert', to)]
    ppermute x22, starting transfers between devices: 13.6 us -> 14.6 us  [swap(): lax.ppermute(value, 'expert', [(i, i ^ mask) for i in range(devices)])]
  transfers between devices with their start and end apart: 31 -> 31, of which waited for: 12 -> 13; matrix products, arithmetic and copies ran while one was open for 0% -> 0% of each run, Pallas kernels for 24% -> 25%
where the time goes in v22:
time: 77.9 us; the launch traced here: 77.7 us
  starting transfers between devices  31.6 us (41%)
  Pallas kernels  23.6 us (30%)
  waiting for transfers between devices  21.3 us (27%)
  between operations  1.18 us (2%)
    ppermute x9, starting transfers between devices, turn(): return lax.ppermute(value, 'expert', to)  17.1 us
    ppermute x22, starting transfers between devices, swap(): lax.ppermute(value, 'expert', [(i, i ^ mask) for i in range(devices)])  14.6 us
    ppermute x22, waiting for transfers between devices, swap(): lax.ppermute(value, 'expert', [(i, i ^ mask) for i in range(devices)])  11.2 us
    pallas_call x4, Pallas kernels, ffn(): call(functools.partial(ffn_kernel, len(pieces)), 24, 'ffn', out_shape=[ja...  10.5 us
    ppermute x9, waiting for transfers between devices, turn(): return lax.ppermute(value, 'expert', to)  10.1 us
    pallas_call x1, Pallas kernels, load(): call(load_kernel, 16, 'load', out_shape=[weight, weight, jax.ShapeDtypeSt...  2.89 us
    pallas_call x2, Pallas kernels, send(): call(functools.partial(kernel, experts), 16, kernel.__name__[:-7], out_sh...  2.83 us
    pallas_call x1, Pallas kernels, last_grad(): call(functools.partial(last_grad_kernel, plan), 24, 'last_grad', out_shap...  2.66 us
  transfers between devices with their start and end apart: 31, of which 13 were waited for; matrix products, arithmetic and copies ran while one was open for 0% of the time, Pallas kernels for 25%

profile of v22, /device:TPU:0, one launch (start us, length us, event | category | flops | bytes accessed | tf_op | source)
XLA Modules:
  0.0 77.7 jit_solution(2759570652152462316)
XLA Ops:
  0.6 1.5 %send_rows.1 = (bf16[96,1024]{1,0:T(8,128)(2,1)S(1)}, bf16[96,1024]{1,0:T(8,128)(2,1)S(1)}, bf16[96,1024]{1,0:T(8,128)(2,1)S(1)}, bf16[96,1024]{1,0:T(8,128)(2,1)S(1)}) custom-call(s32[1]{0:T(128)} %bitcast.plane_ref, bf16[128,1024]{1,0:T(8,128)(2,1)} %tokens_ref.1, s32[2,128]{1,0:T(2,128)} %bitcast.4, f32[1,1024]{1,0:T(1,128)} %bitcast.9), custom_call_target="tpu_custom_call" | custom-call | tf_op jit(solution)/shard_map/send_rows/pallas_call | solution.py:392
  2.1 5.1 %collective-permute-start = (bf16[96,1024]{1,0:T(8,128)(2,1)S(1)}, bf16[96,1024]{1,0:T(8,128)(2,1)S(1)}, u32[]{:S(2)}, u32[]{:S(2)}) collective-permute-start(bf16[96,1024]{1,0:T(8,128)(2,1)S(1)} %get-tuple-element.241), channel_id=1, source_target_pairs={{0,12},{1,13},{2,14},{3,15},{4,0},{5,1},{6,2},{7,3},{8,4},{9,5},{1... | collective-permute-start | bytes 589832 | tf_op jit(solution)/shard_map/ppermute | solution.py:281
  7.2 1.5 %collective-permute-start.2 = (bf16[96,1024]{1,0:T(8,128)(2,1)S(1)}, bf16[96,1024]{1,0:T(8,128)(2,1)S(1)}, u32[]{:S(2)}, u32[]{:S(2)}) collective-permute-start(bf16[96,1024]{1,0:T(8,128)(2,1)S(1)} %get-tuple-element.275.first_ref), channel_id=1, source_target_pairs={{0,2},{1,3},{2,0},{3,1},{4,6},{5,7},{6,4},{7,5},{8,10},{9,11},{10,... | collective-permute-start | bytes 589832 | tf_op jit(solution)/shard_map/ppermute | solution.py:277
  8.8 1.4 %send_grads.1 = (bf16[96,1024]{1,0:T(8,128)(2,1)S(1)}, bf16[96,1024]{1,0:T(8,128)(2,1)S(1)}, bf16[96,1024]{1,0:T(8,128)(2,1)S(1)}, bf16[96,1024]{1,0:T(8,128)(2,1)S(1)}) custom-call(s32[1]{0:T(128)} %bitcast.plane_ref, bf16[128,1024]{1,0:T(8,128)(2,1)} %refs_0_.2, s32[2,128]{1,0:T(2,128)} %bitcast.5, s32[2,128]{1,0:T(2,128)} %bitcast.7), custom_call_target="tpu_custom_call" | custom-call | tf_op jit(solution)/shard_map/send_grads/pallas_call | solution.py:392
  10.1 2.9 %load.1 = (bf16[1024,1024]{1,0:T(8,128)(2,1)S(1)}, bf16[1024,1024]{1,0:T(8,128)(2,1)S(1)}, bf16[1024,1024]{1,0:T(8,128)(2,1)S(1)}) custom-call(bf16[1,1024,1024]{2,1,0:T(8,128)(2,1)} %refs_0_.3, bf16[1,1024,1024]{2,1,0:T(8,128)(2,1)} %refs_1_.1, bf16[1,1024,1024]{2,1,0:T(8,128)(2,1)} %refs_2_.1), custom_call_target="tpu_custom_call" | custom-call | tf_op jit(solution)/shard_map/load/pallas_call | solution.py:412
  13.0 1.1 %collective-permute-start.4 = (bf16[96,1024]{1,0:T(8,128)(2,1)S(1)}, bf16[96,1024]{1,0:T(8,128)(2,1)S(1)}, u32[]{:S(2)}, u32[]{:S(2)}) collective-permute-start(bf16[96,1024]{1,0:T(8,128)(2,1)S(1)} %land.14), channel_id=1, source_target_pairs={{0,8},{1,9},{2,10},{3,11},{4,12},{5,13},{6,14},{7,15},{8,0},{9,1},... | collective-permute-start | bytes 589832 | tf_op jit(solution)/shard_map/ppermute | solution.py:281
  14.6 2.1 %collective-permute-done.1.refs_1_ = bf16[96,1024]{1,0:T(8,128)(2,1)S(1)} collective-permute-done((bf16[96,1024]{1,0:T(8,128)(2,1)S(1)}, bf16[96,1024]{1,0:T(8,128)(2,1)S(1)}, u32[]{:S(2)}, u32[]{:S(2)}) %collective-permute-start.1) | collective-permute-done | bytes 196640 | tf_op jit(solution)/shard_map/ppermute | solution.py:281
  16.8 2.1 %collective-permute-start.3 = (bf16[96,1024]{1,0:T(8,128)(2,1)S(1)}, bf16[96,1024]{1,0:T(8,128)(2,1)S(1)}, u32[]{:S(2)}, u32[]{:S(2)}) collective-permute-start(bf16[96,1024]{1,0:T(8,128)(2,1)S(1)} %get-tuple-element.307.first_ref), channel_id=1, source_target_pairs={{0,2},{1,3},{2,0},{3,1},{4,6},{5,7},{6,4},{7,5},{8,10},{9,11},{10,... | collective-permute-start | bytes 589832 | tf_op jit(solution)/shard_map/ppermute | solution.py:277
  18.9 2.5 %collective-permute-done.5.refs_0_ = bf16[96,1024]{1,0:T(8,128)(2,1)S(1)} collective-permute-done((bf16[96,1024]{1,0:T(8,128)(2,1)S(1)}, bf16[96,1024]{1,0:T(8,128)(2,1)S(1)}, u32[]{:S(2)}, u32[]{:S(2)}) %collective-permute-start.5) | collective-permute-done | bytes 196640 | tf_op jit(solution)/shard_map/ppermute | solution.py:277
  21.4 2.6 %ffn.4 = (bf16[1024,384]{1,0:T(8,128)(2,1)S(1)}, bf16[192,1024]{1,0:T(8,128)(2,1)S(1)}, bf16[192,1024]{1,0:T(8,128)(2,1)S(1)}) custom-call(bf16[192,1024]{1,0:T(8,128)(2,1)S(1)} %pair.10.refs_0_, bf16[192,1024]{1,0:T(8,128)(2,1)S(1)} %land_core.9.refs_1_, bf16[1024,1024]{1,0:T(8,128)(2,1)S(1)} %get-tuple-element.358.refs_2_, ...), custom_call_target="tpu_custom_call" | custom-call | tf_op jit(solution)/shard_map/ffn/pallas_call | solution.py:375
  24.1 0.9 %collective-permute-done.4.refs_1_ = bf16[96,1024]{1,0:T(8,128)(2,1)S(1)} collective-permute-done((bf16[96,1024]{1,0:T(8,128)(2,1)S(1)}, bf16[96,1024]{1,0:T(8,128)(2,1)S(1)}, u32[]{:S(2)}, u32[]{:S(2)}) %collective-permute-start.4) | collective-permute-done | bytes 196640 | tf_op jit(solution)/shard_map/ppermute | solution.py:281
  24.9 1.5 %collective-permute-start.7 = (bf16[96,1024]{1,0:T(8,128)(2,1)S(1)}, bf16[96,1024]{1,0:T(8,128)(2,1)S(1)}, u32[]{:S(2)}, u32[]{:S(2)}) collective-permute-start(bf16[96,1024]{1,0:T(8,128)(2,1)S(1)} %get-tuple-element.346.first_ref), channel_id=1, source_target_pairs={{0,2},{1,3},{2,0},{3,1},{4,6},{5,7},{6,4},{7,5},{8,10},{9,11},{10,... | collective-permute-start | bytes 589832 | tf_op jit(solution)/shard_map/ppermute | solution.py:277
  26.5 3.1 %collective-permute-start.8 = (bf16[96,1024]{1,0:T(8,128)(2,1)S(1)}, bf16[96,1024]{1,0:T(8,128)(2,1)S(1)}, u32[]{:S(2)}, u32[]{:S(2)}) collective-permute-start(bf16[96,1024]{1,0:T(8,128)(2,1)S(1)} %get-tuple-element.296), channel_id=1, source_target_pairs={{0,12},{1,13},{2,14},{3,15},{4,0},{5,1},{6,2},{7,3},{8,4},{9,5},{1... | collective-permute-start | bytes 589832 | tf_op jit(solution)/shard_map/ppermute | solution.py:281
  30.0 2.3 %collective-permute-done.11.refs_0_ = bf16[384,1024]{1,0:T(8,128)(2,1)S(1)} collective-permute-done((bf16[384,1024]{1,0:T(8,128)(2,1)S(1)}, bf16[384,1024]{1,0:T(8,128)(2,1)S(1)}, u32[]{:S(2)}, u32[]{:S(2)}) %collective-permute-start.11) | collective-permute-done | bytes 786464 | tf_op jit(solution)/shard_map/ppermute | solution.py:277
  32.6 1.3 %collective-permute-start.15 = (bf16[96,1024]{1,0:T(8,128)(2,1)S(1)}, bf16[96,1024]{1,0:T(8,128)(2,1)S(1)}, u32[]{:S(2)}, u32[]{:S(2)}) collective-permute-start(bf16[96,1024]{1,0:T(8,128)(2,1)S(1)} %fold.4), channel_id=1, source_target_pairs={{0,2},{1,3},{2,0},{3,1},{4,6},{5,7},{6,4},{7,5},{8,10},{9,11},{10,... | collective-permute-start | bytes 589832 | tf_op jit(solution)/shard_map/ppermute | solution.py:277
  33.9 2.6 %ffn.5 = (bf16[1024,384]{1,0:T(8,128)(2,1)S(1)}, bf16[192,1024]{1,0:T(8,128)(2,1)S(1)}, bf16[192,1024]{1,0:T(8,128)(2,1)S(1)}) custom-call(bf16[192,1024]{1,0:T(8,128)(2,1)S(1)} %pair.11.second_ref.refs_0_, bf16[192,1024]{1,0:T(8,128)(2,1)S(1)} %get-tuple-element.313.refs_1_, bf16[1024,1024]{1,0:T(8,128)(2,1)S(1)} %get-tuple-element.358.refs_2_, ...), custom_call_target="tpu_custom_call" | custom-call | tf_op jit(solution)/shard_map/ffn/pallas_call | solution.py:375
  37.4 1.5 %collective-permute-start.13 = (bf16[96,1024]{1,0:T(8,128)(2,1)S(1)}, bf16[96,1024]{1,0:T(8,128)(2,1)S(1)}, u32[]{:S(2)}, u32[]{:S(2)}) collective-permute-start(bf16[96,1024]{1,0:T(8,128)(2,1)S(1)} %get-tuple-element.449.first_ref), channel_id=1, source_target_pairs={{0,2},{1,3},{2,0},{3,1},{4,6},{5,7},{6,4},{7,5},{8,10},{9,11},{10,... | collective-permute-start | bytes 589832 | tf_op jit(solution)/shard_map/ppermute | solution.py:277
  39.0 1.1 %collective-permute-start.14 = (bf16[96,1024]{1,0:T(8,128)(2,1)S(1)}, bf16[96,1024]{1,0:T(8,128)(2,1)S(1)}, u32[]{:S(2)}, u32[]{:S(2)}) collective-permute-start(bf16[96,1024]{1,0:T(8,128)(2,1)S(1)} %get-tuple-element.334), channel_id=1, source_target_pairs={{0,8},{1,9},{2,10},{3,11},{4,12},{5,13},{6,14},{7,15},{8,0},{9,1},... | collective-permute-start | bytes 589832 | tf_op jit(solution)/shard_map/ppermute | solution.py:281
  40.2 2.6 %ffn.6 = (bf16[1024,384]{1,0:T(8,128)(2,1)S(1)}, bf16[192,1024]{1,0:T(8,128)(2,1)S(1)}, bf16[192,1024]{1,0:T(8,128)(2,1)S(1)}) custom-call(bf16[192,1024]{1,0:T(8,128)(2,1)S(1)} %pair.13.refs_0_, bf16[192,1024]{1,0:T(8,128)(2,1)S(1)} %land_core.11.refs_1_, bf16[1024,1024]{1,0:T(8,128)(2,1)S(1)} %get-tuple-element.358.refs_2_, ...), custom_call_target="tpu_custom_call" | custom-call | tf_op jit(solution)/shard_map/ffn/pallas_call | solution.py:375
  44.4 2.6 %ffn.7 = (bf16[1024,384]{1,0:T(8,128)(2,1)S(1)}, bf16[192,1024]{1,0:T(8,128)(2,1)S(1)}, bf16[192,1024]{1,0:T(8,128)(2,1)S(1)}) custom-call(bf16[192,1024]{1,0:T(8,128)(2,1)S(1)} %pair.14.second_ref.refs_0_, bf16[192,1024]{1,0:T(8,128)(2,1)S(1)} %get-tuple-element.357.refs_1_, bf16[1024,1024]{1,0:T(8,128)(2,1)S(1)} %get-tuple-element.358.refs_2_, ...), custom_call_target="tpu_custom_call" | custom-call | tf_op jit(solution)/shard_map/ffn/pallas_call | solution.py:375
  47.1 2.1 %collective-permute-done.14.refs_1_ = bf16[96,1024]{1,0:T(8,128)(2,1)S(1)} collective-permute-done((bf16[96,1024]{1,0:T(8,128)(2,1)S(1)}, bf16[96,1024]{1,0:T(8,128)(2,1)S(1)}, u32[]{:S(2)}, u32[]{:S(2)}) %collective-permute-start.14) | collective-permute-done | bytes 196640 | tf_op jit(solution)/shard_map/ppermute | solution.py:281
  49.4 1.3 %collective-permute-start.20 = (bf16[96,1024]{1,0:T(8,128)(2,1)S(1)}, bf16[96,1024]{1,0:T(8,128)(2,1)S(1)}, u32[]{:S(2)}, u32[]{:S(2)}) collective-permute-start(bf16[96,1024]{1,0:T(8,128)(2,1)S(1)} %fold.6), channel_id=1, source_target_pairs={{0,2},{1,3},{2,0},{3,1},{4,6},{5,7},{6,4},{7,5},{8,10},{9,11},{10,... | collective-permute-start | bytes 589832 | tf_op jit(solution)/shard_map/ppermute | solution.py:277
  50.7 0.9 %collective-permute-start.22 = (bf16[96,1024]{1,0:T(8,128)(2,1)S(1)}, bf16[96,1024]{1,0:T(8,128)(2,1)S(1)}, u32[]{:S(2)}, u32[]{:S(2)}) collective-permute-start(bf16[96,1024]{1,0:T(8,128)(2,1)S(1)} %fold.7), channel_id=1, source_target_pairs={{0,2},{1,3},{2,0},{3,1},{4,6},{5,7},{6,4},{7,5},{8,10},{9,11},{10,... | collective-permute-start | bytes 589832 | tf_op jit(solution)/shard_map/ppermute | solution.py:277
  51.7 2.4 %collective-permute-start.21 = (bf16[96,1024]{1,0:T(8,128)(2,1)S(1)}, bf16[96,1024]{1,0:T(8,128)(2,1)S(1)}, u32[]{:S(2)}, u32[]{:S(2)}) collective-permute-start(bf16[96,1024]{1,0:T(8,128)(2,1)S(1)} %total.5), channel_id=1, source_target_pairs={{0,12},{1,13},{2,14},{3,15},{4,0},{5,1},{6,2},{7,3},{8,4},{9,5},{1... | collective-permute-start | bytes 589832 | tf_op jit(solution)/shard_map/ppermute | solution.py:281
  54.1 2.7 %collective-permute-done.20.refs_0_ = bf16[96,1024]{1,0:T(8,128)(2,1)S(1)} collective-permute-done((bf16[96,1024]{1,0:T(8,128)(2,1)S(1)}, bf16[96,1024]{1,0:T(8,128)(2,1)S(1)}, u32[]{:S(2)}, u32[]{:S(2)}) %collective-permute-start.20) | collective-permute-done | bytes 196640 | tf_op jit(solution)/shard_map/ppermute | solution.py:277
  58.9 1.3 %collective-permute-done.23.refs_0_ = bf16[192,1024]{1,0:T(8,128)(2,1)S(1)} collective-permute-done((bf16[192,1024]{1,0:T(8,128)(2,1)S(1)}, bf16[192,1024]{1,0:T(8,128)(2,1)S(1)}, u32[]{:S(2)}, u32[]{:S(2)}) %collective-permute-start.23) | collective-permute-done | bytes 393248 | tf_op jit(solution)/shard_map/ppermute | solution.py:277
  60.3 3.3 %collective-permute-start.28 = (bf16[96,1024]{1,0:T(8,128)(2,1)S(1)}, bf16[96,1024]{1,0:T(8,128)(2,1)S(1)}, u32[]{:S(2)}, u32[]{:S(2)}) collective-permute-start(bf16[96,1024]{1,0:T(8,128)(2,1)S(1)} %total.7), channel_id=1, source_target_pairs={{0,8},{1,9},{2,10},{3,11},{4,12},{5,13},{6,14},{7,15},{8,0},{9,1},... | collective-permute-start | bytes 589832 | tf_op jit(solution)/shard_map/ppermute | solution.py:281
  64.6 1.6 %collective-permute-done.26.refs_0_ = bf16[192,1024]{1,0:T(8,128)(2,1)S(1)} collective-permute-done((bf16[192,1024]{1,0:T(8,128)(2,1)S(1)}, bf16[192,1024]{1,0:T(8,128)(2,1)S(1)}, u32[]{:S(2)}, u32[]{:S(2)}) %collective-permute-start.26) | collective-permute-done | bytes 393248 | tf_op jit(solution)/shard_map/ppermute | solution.py:277
  66.5 2.4 %first_grad.1.refs_2_.first_ref = f32[1024,1024]{1,0:T(8,128)S(1)} custom-call(bf16[1024,384]{1,0:T(8,128)(2,1)S(1)} %get-tuple-element.453.refs_2_.refs_0_, bf16[1024,384]{1,0:T(8,128)(2,1)S(1)} %get-tuple-element.454.refs_3_.refs_1_, bf16[1024,384]{1,0:T(8,128)(2,1)S(1)} %get-tuple-element.475.refs_1_.refs_2_.refs_0_, bf16[192,1024]{1,0:T(8,128)(2,1)S(1)} %pair.16.refs_3_, ...), custom_call_target="tpu_custom_call" | custom-call | tf_op jit(solution)/shard_map/first_grad/pallas_call | solution.py:447
  68.9 4.1 %collective-permute-done.28.refs_1_ = bf16[96,1024]{1,0:T(8,128)(2,1)S(1)} collective-permute-done((bf16[96,1024]{1,0:T(8,128)(2,1)S(1)}, bf16[96,1024]{1,0:T(8,128)(2,1)S(1)}, u32[]{:S(2)}, u32[]{:S(2)}) %collective-permute-start.28) | collective-permute-done | bytes 196640 | tf_op jit(solution)/shard_map/ppermute | solution.py:281
  73.2 1.4 %combine.1 = bf16[128,1024]{1,0:T(8,128)(2,1)} custom-call(s32[1]{0:T(128)} %bitcast.plane_ref, bf16[128,1024]{1,0:T(8,128)(2,1)S(1)} %copy-done, s32[2,128]{1,0:T(2,128)S(1)} %bitcast.6, s32[2,128]{1,0:T(2,128)S(1)} %bitcast.8, bf16[96,1024]{1,0:T(8,128)(2,1)S(1)} %total.4.refs_0_, bf16[96,1024]{1,0:T(8,128)(2,1)S(1)} %get-tuple-element.471.refs_1_, ...), custom_call_target="tpu_custom_call" | custom-call | tf_op jit(solution)/shard_map/combine/pallas_call | solution.py:518
  74.9 2.7 %last_grad.1 = bf16[1,1024,1024]{2,1,0:T(8,128)(2,1)} custom-call(f32[1024,1024]{1,0:T(8,128)S(1)} %first_grad.1.refs_2_.first_ref, bf16[1024,384]{1,0:T(8,128)(2,1)S(1)} %get-tuple-element.475.refs_1_.refs_2_.refs_0_, bf16[1024,384]{1,0:T(8,128)(2,1)S(1)} %get-tuple-element.476.refs_2_.refs_1_, bf16[192,1024]{1,0:T(8,128)(2,1)S(1)} %pair.19.refs_2_, ...), custom_call_target="tpu_custom_call" | custom-call | tf_op jit(solution)/shard_map/last_grad/pallas_call | solution.py:459
  (88 shorter events, 8.1 us)
Async XLA Ops:
  2.1 12.5 %collective-permute-start = (bf16[96,1024]{1,0:T(8,128)(2,1)S(1)}, bf16[96,1024]{1,0:T(8,128)(2,1)S(1)}, u32[]{:S(2)}, u32[]{:S(2)}) collective-permute-start(bf16[96,1024]{1,0:T(8,128)(2,1)S(1)} %get-tuple-element.241), channel_id=1, source_target_pairs={{0,12},{1,13},{2,14},{3,15},{4,0},{5,1},{6,2},{7,3},{8,4},{9,5},{1... | collective-permute-start | bytes 589832 | tf_op jit(solution)/shard_map/ppermute | solution.py:281
  7.2 9.5 %collective-permute-start.1 = (bf16[96,1024]{1,0:T(8,128)(2,1)S(1)}, bf16[96,1024]{1,0:T(8,128)(2,1)S(1)}, u32[]{:S(2)}, u32[]{:S(2)}) collective-permute-start(bf16[96,1024]{1,0:T(8,128)(2,1)S(1)} %get-tuple-element.242), channel_id=1, source_target_pairs={{0,4},{1,5},{2,6},{3,7},{4,8},{5,9},{6,10},{7,11},{8,12},{9,13},{1... | collective-permute-start | bytes 589832 | tf_op jit(solution)/shard_map/ppermute | solution.py:281
  7.2 9.5 %collective-permute-start.2 = (bf16[96,1024]{1,0:T(8,128)(2,1)S(1)}, bf16[96,1024]{1,0:T(8,128)(2,1)S(1)}, u32[]{:S(2)}, u32[]{:S(2)}) collective-permute-start(bf16[96,1024]{1,0:T(8,128)(2,1)S(1)} %get-tuple-element.275.first_ref), channel_id=1, source_target_pairs={{0,2},{1,3},{2,0},{3,1},{4,6},{5,7},{6,4},{7,5},{8,10},{9,11},{10,... | collective-permute-start | bytes 589832 | tf_op jit(solution)/shard_map/ppermute | solution.py:277
  13.0 11.9 %collective-permute-start.4 = (bf16[96,1024]{1,0:T(8,128)(2,1)S(1)}, bf16[96,1024]{1,0:T(8,128)(2,1)S(1)}, u32[]{:S(2)}, u32[]{:S(2)}) collective-permute-start(bf16[96,1024]{1,0:T(8,128)(2,1)S(1)} %land.14), channel_id=1, source_target_pairs={{0,8},{1,9},{2,10},{3,11},{4,12},{5,13},{6,14},{7,15},{8,0},{9,1},... | collective-permute-start | bytes 589832 | tf_op jit(solution)/shard_map/ppermute | solution.py:281
  14.1 7.3 %collective-permute-start.5 = (bf16[96,1024]{1,0:T(8,128)(2,1)S(1)}, bf16[96,1024]{1,0:T(8,128)(2,1)S(1)}, u32[]{:S(2)}, u32[]{:S(2)}) collective-permute-start(bf16[96,1024]{1,0:T(8,128)(2,1)S(1)} %get-tuple-element.431.first_ref), channel_id=1, source_target_pairs={{0,2},{1,3},{2,0},{3,1},{4,6},{5,7},{6,4},{7,5},{8,10},{9,11},{10,... | collective-permute-start | bytes 589832 | tf_op jit(solution)/shard_map/ppermute | solution.py:277
  16.8 8.2 %collective-permute-start.3 = (bf16[96,1024]{1,0:T(8,128)(2,1)S(1)}, bf16[96,1024]{1,0:T(8,128)(2,1)S(1)}, u32[]{:S(2)}, u32[]{:S(2)}) collective-permute-start(bf16[96,1024]{1,0:T(8,128)(2,1)S(1)} %get-tuple-element.307.first_ref), channel_id=1, source_target_pairs={{0,2},{1,3},{2,0},{3,1},{4,6},{5,7},{6,4},{7,5},{8,10},{9,11},{10,... | collective-permute-start | bytes 589832 | tf_op jit(solution)/shard_map/ppermute | solution.py:277
  18.9 2.6 %collective-permute-start.6 = (bf16[192,1024]{1,0:T(8,128)(2,1)S(1)}, bf16[192,1024]{1,0:T(8,128)(2,1)S(1)}, u32[]{:S(2)}, u32[]{:S(2)}) collective-permute-start(bf16[192,1024]{1,0:T(8,128)(2,1)S(1)} %pair.10.refs_0_), channel_id=1, source_target_pairs={{0,1},{1,0},{2,3},{3,2},{4,5},{5,4},{6,7},{7,6},{8,9},{9,8},{10,11... | collective-permute-start | bytes 1179656 | tf_op jit(solution)/shard_map/ppermute | solution.py:277
  21.4 8.6 %collective-permute-start.10 = (bf16[96,1024]{1,0:T(8,128)(2,1)S(1)}, bf16[96,1024]{1,0:T(8,128)(2,1)S(1)}, u32[]{:S(2)}, u32[]{:S(2)}) collective-permute-start(bf16[96,1024]{1,0:T(8,128)(2,1)S(1)} %get-tuple-element.329.first_ref), channel_id=1, source_target_pairs={{0,2},{1,3},{2,0},{3,1},{4,6},{5,7},{6,4},{7,5},{8,10},{9,11},{10,... | collective-permute-start | bytes 589832 | tf_op jit(solution)/shard_map/ppermute | solution.py:277
  24.9 11.6 %collective-permute-start.7 = (bf16[96,1024]{1,0:T(8,128)(2,1)S(1)}, bf16[96,1024]{1,0:T(8,128)(2,1)S(1)}, u32[]{:S(2)}, u32[]{:S(2)}) collective-permute-start(bf16[96,1024]{1,0:T(8,128)(2,1)S(1)} %get-tuple-element.346.first_ref), channel_id=1, source_target_pairs={{0,2},{1,3},{2,0},{3,1},{4,6},{5,7},{6,4},{7,5},{8,10},{9,11},{10,... | collective-permute-start | bytes 589832 | tf_op jit(solution)/shard_map/ppermute | solution.py:277
  26.5 10.1 %collective-permute-start.8 = (bf16[96,1024]{1,0:T(8,128)(2,1)S(1)}, bf16[96,1024]{1,0:T(8,128)(2,1)S(1)}, u32[]{:S(2)}, u32[]{:S(2)}) collective-permute-start(bf16[96,1024]{1,0:T(8,128)(2,1)S(1)} %get-tuple-element.296), channel_id=1, source_target_pairs={{0,12},{1,13},{2,14},{3,15},{4,0},{5,1},{6,2},{7,3},{8,4},{9,5},{1... | collective-permute-start | bytes 589832 | tf_op jit(solution)/shard_map/ppermute | solution.py:281
  29.6 7.8 %collective-permute-start.9 = (bf16[96,1024]{1,0:T(8,128)(2,1)S(1)}, bf16[96,1024]{1,0:T(8,128)(2,1)S(1)}, u32[]{:S(2)}, u32[]{:S(2)}) collective-permute-start(bf16[96,1024]{1,0:T(8,128)(2,1)S(1)} %get-tuple-element.297), channel_id=1, source_target_pairs={{0,4},{1,5},{2,6},{3,7},{4,8},{5,9},{6,10},{7,11},{8,12},{9,13},{1... | collective-permute-start | bytes 589832 | tf_op jit(solution)/shard_map/ppermute | solution.py:281
  29.9 2.4 %collective-permute-start.11 = (bf16[384,1024]{1,0:T(8,128)(2,1)S(1)}, bf16[384,1024]{1,0:T(8,128)(2,1)S(1)}, u32[]{:S(2)}, u32[]{:S(2)}) collective-permute-start(bf16[384,1024]{1,0:T(8,128)(2,1)S(1)} %pair.12), channel_id=1, source_target_pairs={{0,1},{1,0},{2,3},{3,2},{4,5},{5,4},{6,7},{7,6},{8,9},{9,8},{10,11... | collective-permute-start | bytes 2359304 | tf_op jit(solution)/shard_map/ppermute | solution.py:277
  32.3 5.1 %collective-permute-start.12 = (bf16[192,1024]{1,0:T(8,128)(2,1)S(1)}, bf16[192,1024]{1,0:T(8,128)(2,1)S(1)}, u32[]{:S(2)}, u32[]{:S(2)}) collective-permute-start(bf16[192,1024]{1,0:T(8,128)(2,1)S(1)} %pair.13.refs_0_), channel_id=1, source_target_pairs={{0,1},{1,0},{2,3},{3,2},{4,5},{5,4},{6,7},{7,6},{8,9},{9,8},{10,11... | collective-permute-start | bytes 1179656 | tf_op jit(solution)/shard_map/ppermute | solution.py:277
  32.6 10.2 %collective-permute-start.15 = (bf16[96,1024]{1,0:T(8,128)(2,1)S(1)}, bf16[96,1024]{1,0:T(8,128)(2,1)S(1)}, u32[]{:S(2)}, u32[]{:S(2)}) collective-permute-start(bf16[96,1024]{1,0:T(8,128)(2,1)S(1)} %fold.4), channel_id=1, source_target_pairs={{0,2},{1,3},{2,0},{3,1},{4,6},{5,7},{6,4},{7,5},{8,10},{9,11},{10,... | collective-permute-start | bytes 589832 | tf_op jit(solution)/shard_map/ppermute | solution.py:277
  37.4 9.7 %collective-permute-start.13 = (bf16[96,1024]{1,0:T(8,128)(2,1)S(1)}, bf16[96,1024]{1,0:T(8,128)(2,1)S(1)}, u32[]{:S(2)}, u32[]{:S(2)}) collective-permute-start(bf16[96,1024]{1,0:T(8,128)(2,1)S(1)} %get-tuple-element.449.first_ref), channel_id=1, source_target_pairs={{0,2},{1,3},{2,0},{3,1},{4,6},{5,7},{6,4},{7,5},{8,10},{9,11},{10,... | collective-permute-start | bytes 589832 | tf_op jit(solution)/shard_map/ppermute | solution.py:277
  39.0 10.3 %collective-permute-start.14 = (bf16[96,1024]{1,0:T(8,128)(2,1)S(1)}, bf16[96,1024]{1,0:T(8,128)(2,1)S(1)}, u32[]{:S(2)}, u32[]{:S(2)}) collective-permute-start(bf16[96,1024]{1,0:T(8,128)(2,1)S(1)} %get-tuple-element.334), channel_id=1, source_target_pairs={{0,8},{1,9},{2,10},{3,11},{4,12},{5,13},{6,14},{7,15},{8,0},{9,1},... | collective-permute-start | bytes 589832 | tf_op jit(solution)/shard_map/ppermute | solution.py:281
  40.1 2.7 %collective-permute-start.16 = (bf16[384,1024]{1,0:T(8,128)(2,1)S(1)}, bf16[384,1024]{1,0:T(8,128)(2,1)S(1)}, u32[]{:S(2)}, u32[]{:S(2)}) collective-permute-start(bf16[384,1024]{1,0:T(8,128)(2,1)S(1)} %pair.15), channel_id=1, source_target_pairs={{0,1},{1,0},{2,3},{3,2},{4,5},{5,4},{6,7},{7,6},{8,9},{9,8},{10,11... | collective-permute-start | bytes 2359304 | tf_op jit(solution)/shard_map/ppermute | solution.py:277
  42.9 6.4 %collective-permute-start.17 = (bf16[192,1024]{1,0:T(8,128)(2,1)S(1)}, bf16[192,1024]{1,0:T(8,128)(2,1)S(1)}, u32[]{:S(2)}, u32[]{:S(2)}) collective-permute-start(bf16[192,1024]{1,0:T(8,128)(2,1)S(1)} %get-tuple-element.378), channel_id=1, source_target_pairs={{0,1},{1,0},{2,3},{3,2},{4,5},{5,4},{6,7},{7,6},{8,9},{9,8},{10,11... | collective-permute-start | bytes 1179656 | tf_op jit(solution)/shard_map/ppermute | solution.py:277
  43.6 7.1 %collective-permute-start.18 = (bf16[96,1024]{1,0:T(8,128)(2,1)S(1)}, bf16[96,1024]{1,0:T(8,128)(2,1)S(1)}, u32[]{:S(2)}, u32[]{:S(2)}) collective-permute-start(bf16[96,1024]{1,0:T(8,128)(2,1)S(1)} %fold.5), channel_id=1, source_target_pairs={{0,2},{1,3},{2,0},{3,1},{4,6},{5,7},{6,4},{7,5},{8,10},{9,11},{10,... | collective-permute-start | bytes 589832 | tf_op jit(solution)/shard_map/ppermute | solution.py:277
  47.0 3.6 %collective-permute-start.19 = (bf16[192,1024]{1,0:T(8,128)(2,1)S(1)}, bf16[192,1024]{1,0:T(8,128)(2,1)S(1)}, u32[]{:S(2)}, u32[]{:S(2)}) collective-permute-start(bf16[192,1024]{1,0:T(8,128)(2,1)S(1)} %get-tuple-element.396), channel_id=1, source_target_pairs={{0,1},{1,0},{2,3},{3,2},{4,5},{5,4},{6,7},{7,6},{8,9},{9,8},{10,11... | collective-permute-start | bytes 1179656 | tf_op jit(solution)/shard_map/ppermute | solution.py:277
  49.4 7.5 %collective-permute-start.20 = (bf16[96,1024]{1,0:T(8,128)(2,1)S(1)}, bf16[96,1024]{1,0:T(8,128)(2,1)S(1)}, u32[]{:S(2)}, u32[]{:S(2)}) collective-permute-start(bf16[96,1024]{1,0:T(8,128)(2,1)S(1)} %fold.6), channel_id=1, source_target_pairs={{0,2},{1,3},{2,0},{3,1},{4,6},{5,7},{6,4},{7,5},{8,10},{9,11},{10,... | collective-permute-start | bytes 589832 | tf_op jit(solution)/shard_map/ppermute | solution.py:277
  50.7 8.2 %collective-permute-start.22 = (bf16[96,1024]{1,0:T(8,128)(2,1)S(1)}, bf16[96,1024]{1,0:T(8,128)(2,1)S(1)}, u32[]{:S(2)}, u32[]{:S(2)}) collective-permute-start(bf16[96,1024]{1,0:T(8,128)(2,1)S(1)} %fold.7), channel_id=1, source_target_pairs={{0,2},{1,3},{2,0},{3,1},{4,6},{5,7},{6,4},{7,5},{8,10},{9,11},{10,... | collective-permute-start | bytes 589832 | tf_op jit(solution)/shard_map/ppermute | solution.py:277
  51.7 7.3 %collective-permute-start.21 = (bf16[96,1024]{1,0:T(8,128)(2,1)S(1)}, bf16[96,1024]{1,0:T(8,128)(2,1)S(1)}, u32[]{:S(2)}, u32[]{:S(2)}) collective-permute-start(bf16[96,1024]{1,0:T(8,128)(2,1)S(1)} %total.5), channel_id=1, source_target_pairs={{0,12},{1,13},{2,14},{3,15},{4,0},{5,1},{6,2},{7,3},{8,4},{9,5},{1... | collective-permute-start | bytes 589832 | tf_op jit(solution)/shard_map/ppermute | solution.py:281
  56.9 7.7 %collective-permute-start.25 = (bf16[96,1024]{1,0:T(8,128)(2,1)S(1)}, bf16[96,1024]{1,0:T(8,128)(2,1)S(1)}, u32[]{:S(2)}, u32[]{:S(2)}) collective-permute-start(bf16[96,1024]{1,0:T(8,128)(2,1)S(1)} %total.6), channel_id=1, source_target_pairs={{0,4},{1,5},{2,6},{3,7},{4,8},{5,9},{6,10},{7,11},{8,12},{9,13},{1... | collective-permute-start | bytes 589832 | tf_op jit(solution)/shard_map/ppermute | solution.py:281
  57.6 7.0 %collective-permute-start.24 = (bf16[96,1024]{1,0:T(8,128)(2,1)S(1)}, bf16[96,1024]{1,0:T(8,128)(2,1)S(1)}, u32[]{:S(2)}, u32[]{:S(2)}) collective-permute-start(bf16[96,1024]{1,0:T(8,128)(2,1)S(1)} %get-tuple-element.463.first_ref), channel_id=1, source_target_pairs={{0,2},{1,3},{2,0},{3,1},{4,6},{5,7},{6,4},{7,5},{8,10},{9,11},{10,... | collective-permute-start | bytes 589832 | tf_op jit(solution)/shard_map/ppermute | solution.py:277
  58.5 1.8 %collective-permute-start.23 = (bf16[192,1024]{1,0:T(8,128)(2,1)S(1)}, bf16[192,1024]{1,0:T(8,128)(2,1)S(1)}, u32[]{:S(2)}, u32[]{:S(2)}) collective-permute-start(bf16[192,1024]{1,0:T(8,128)(2,1)S(1)} %pair.16.refs_3_), channel_id=1, source_target_pairs={{0,1},{1,0},{2,3},{3,2},{4,5},{5,4},{6,7},{7,6},{8,9},{9,8},{10,11... | collective-permute-start | bytes 1179656 | tf_op jit(solution)/shard_map/ppermute | solution.py:277
  60.3 12.7 %collective-permute-start.28 = (bf16[96,1024]{1,0:T(8,128)(2,1)S(1)}, bf16[96,1024]{1,0:T(8,128)(2,1)S(1)}, u32[]{:S(2)}, u32[]{:S(2)}) collective-permute-start(bf16[96,1024]{1,0:T(8,128)(2,1)S(1)} %total.7), channel_id=1, source_target_pairs={{0,8},{1,9},{2,10},{3,11},{4,12},{5,13},{6,14},{7,15},{8,0},{9,1},... | collective-permute-start | bytes 589832 | tf_op jit(solution)/shard_map/ppermute | solution.py:281
  63.6 9.4 %collective-permute-start.27 = (bf16[96,1024]{1,0:T(8,128)(2,1)S(1)}, bf16[96,1024]{1,0:T(8,128)(2,1)S(1)}, u32[]{:S(2)}, u32[]{:S(2)}) collective-permute-start(bf16[96,1024]{1,0:T(8,128)(2,1)S(1)} %get-tuple-element.477.first_ref), channel_id=1, source_target_pairs={{0,2},{1,3},{2,0},{3,1},{4,6},{5,7},{6,4},{7,5},{8,10},{9,11},{10,... | collective-permute-start | bytes 589832 | tf_op jit(solution)/shard_map/ppermute | solution.py:277
  64.5 1.8 %collective-permute-start.26 = (bf16[192,1024]{1,0:T(8,128)(2,1)S(1)}, bf16[192,1024]{1,0:T(8,128)(2,1)S(1)}, u32[]{:S(2)}, u32[]{:S(2)}) collective-permute-start(bf16[192,1024]{1,0:T(8,128)(2,1)S(1)} %pair.17.refs_4_), channel_id=1, source_target_pairs={{0,1},{1,0},{2,3},{3,2},{4,5},{5,4},{6,7},{7,6},{8,9},{9,8},{10,11... | collective-permute-start | bytes 1179656 | tf_op jit(solution)/shard_map/ppermute | solution.py:277
  66.3 6.8 %collective-permute-start.29 = (bf16[192,1024]{1,0:T(8,128)(2,1)S(1)}, bf16[192,1024]{1,0:T(8,128)(2,1)S(1)}, u32[]{:S(2)}, u32[]{:S(2)}) collective-permute-start(bf16[192,1024]{1,0:T(8,128)(2,1)S(1)} %pair.18.refs_5_), channel_id=1, source_target_pairs={{0,1},{1,0},{2,3},{3,2},{4,5},{5,4},{6,7},{7,6},{8,9},{9,8},{10,11... | collective-permute-start | bytes 1179656 | tf_op jit(solution)/shard_map/ppermute | solution.py:277
  68.9 4.3 %copy-start = (bf16[128,1024]{1,0:T(8,128)(2,1)S(1)}, bf16[128,1024]{1,0:T(8,128)(2,1)}, u32[]{:S(2)}) copy-start(bf16[128,1024]{1,0:T(8,128)(2,1)} %tokens_ref.1) | copy-start | bytes 786436
  73.1 1.8 %collective-permute-start.30 = (bf16[192,1024]{1,0:T(8,128)(2,1)S(1)}, bf16[192,1024]{1,0:T(8,128)(2,1)S(1)}, u32[]{:S(2)}, u32[]{:S(2)}) collective-permute-start(bf16[192,1024]{1,0:T(8,128)(2,1)S(1)} %pair.19.refs_2_), channel_id=1, source_target_pairs={{0,1},{1,0},{2,3},{3,2},{4,5},{5,4},{6,7},{7,6},{8,9},{9,8},{10,11... | collective-permute-start | bytes 1179656 | tf_op jit(solution)/shard_map/ppermute | solution.py:277
  (2 other events, 8.5 us)

commit v23 on v22

--- a/solution.py
+++ b/solution.py
@@ -19,8 +19,8 @@
     ("cR1N3 ffnN2 yC1 zC3", "yR0 cR1N3"),
     ("cR2 ffnN3 cR3 yR1 totalR0", "yC1 zC3 cR2"),
     ("yR2", "yR1 cR3"),
-    ("totalR1 zR1 yR3", "yR2"),
-    ("totalR2 zR2 yC2 cC0", "zR1 yR3 cC0"),
+    ("totalR1 zR1 yR3 cC0", "yR2 cC0"),
+    ("totalR2 zR2 yC2", "zR1 yR3"),
     ("totalR3 zR3 yC3 cC1", "yC2 zR2 cC1"),
     ("cC2 gradC0", "yC3 zR3 cC2"),
     ("cC3", None),

time: 77.9 us -> 78.2 us (level)
  waiting for transfers between devices: 21.3 us -> 22.3 us
    ppermute x9, waiting for transfers between devices: 10.1 us -> 14 us  [turn(): return lax.ppermute(value, 'expert', to)]
    ppermute x22, waiting for transfers between devices: 11.2 us -> 8.22 us  [swap(): lax.ppermute(value, 'expert', [(i, i ^ mask) for i in range(devices)])]
  transfers between devices with their start and end apart: 31 -> 31, of which waited for: 13 -> 11; matrix products, arithmetic and copies ran while one was open for 0% -> 0% of each run, Pallas kernels for 25% -> 25%
where the time goes in v23:
time: 78.2 us; the launch traced here: 78 us
  starting transfers between devices  31 us (40%)
  Pallas kernels  23.6 us (30%)
  waiting for transfers between devices  22.3 us (29%)
  between operations  1.19 us (2%)
    ppermute x9, starting transfers between devices, turn(): return lax.ppermute(value, 'expert', to)  16.6 us
    ppermute x22, starting transfers between devices, swap(): lax.ppermute(value, 'expert', [(i, i ^ mask) for i in range(devices)])  14.4 us
    ppermute x9, waiting for transfers between devices, turn(): return lax.ppermute(value, 'expert', to)  14 us
    pallas_call x4, Pallas kernels, ffn(): call(functools.partial(ffn_kernel, len(pieces)), 24, 'ffn', out_shape=[ja...  10.5 us
    ppermute x22, waiting for transfers between devices, swap(): lax.ppermute(value, 'expert', [(i, i ^ mask) for i in range(devices)])  8.22 us
    pallas_call x1, Pallas kernels, load(): call(load_kernel, 16, 'load', out_shape=[weight, weight, jax.ShapeDtypeSt...  2.89 us
    pallas_call x2, Pallas kernels, send(): call(functools.partial(kernel, experts), 16, kernel.__name__[:-7], out_sh...  2.83 us
    pallas_call x1, Pallas kernels, last_grad(): call(functools.partial(last_grad_kernel, plan), 24, 'last_grad', out_shap...  2.66 us
  transfers between devices with their start and end apart: 31, of which 11 were waited for; matrix products, arithmetic and copies ran while one was open for 0% of the time, Pallas kernels for 25%

profile of v23, /device:TPU:0, one launch (start us, length us, event | category | flops | bytes accessed | tf_op | source)
XLA Modules:
  0.0 78.0 jit_solution(8482867878819001368)
XLA Ops:
  0.6 1.5 %send_rows.1 = (bf16[96,1024]{1,0:T(8,128)(2,1)S(1)}, bf16[96,1024]{1,0:T(8,128)(2,1)S(1)}, bf16[96,1024]{1,0:T(8,128)(2,1)S(1)}, bf16[96,1024]{1,0:T(8,128)(2,1)S(1)}) custom-call(s32[1]{0:T(128)} %bitcast.plane_ref, bf16[128,1024]{1,0:T(8,128)(2,1)} %tokens_ref.1, s32[2,128]{1,0:T(2,128)} %bitcast.4, f32[1,1024]{1,0:T(1,128)} %bitcast.9), custom_call_target="tpu_custom_call" | custom-call | tf_op jit(solution)/shard_map/send_rows/pallas_call | solution.py:392
  2.1 5.1 %collective-permute-start = (bf16[96,1024]{1,0:T(8,128)(2,1)S(1)}, bf16[96,1024]{1,0:T(8,128)(2,1)S(1)}, u32[]{:S(2)}, u32[]{:S(2)}) collective-permute-start(bf16[96,1024]{1,0:T(8,128)(2,1)S(1)} %get-tuple-element.241), channel_id=1, source_target_pairs={{0,12},{1,13},{2,14},{3,15},{4,0},{5,1},{6,2},{7,3},{8,4},{9,5},{1... | collective-permute-start | bytes 589832 | tf_op jit(solution)/shard_map/ppermute | solution.py:281
  7.2 1.5 %collective-permute-start.2 = (bf16[96,1024]{1,0:T(8,128)(2,1)S(1)}, bf16[96,1024]{1,0:T(8,128)(2,1)S(1)}, u32[]{:S(2)}, u32[]{:S(2)}) collective-permute-start(bf16[96,1024]{1,0:T(8,128)(2,1)S(1)} %get-tuple-element.275.first_ref), channel_id=1, source_target_pairs={{0,2},{1,3},{2,0},{3,1},{4,6},{5,7},{6,4},{7,5},{8,10},{9,11},{10,... | collective-permute-start | bytes 589832 | tf_op jit(solution)/shard_map/ppermute | solution.py:277
  8.8 1.4 %send_grads.1 = (bf16[96,1024]{1,0:T(8,128)(2,1)S(1)}, bf16[96,1024]{1,0:T(8,128)(2,1)S(1)}, bf16[96,1024]{1,0:T(8,128)(2,1)S(1)}, bf16[96,1024]{1,0:T(8,128)(2,1)S(1)}) custom-call(s32[1]{0:T(128)} %bitcast.plane_ref, bf16[128,1024]{1,0:T(8,128)(2,1)} %refs_0_.2, s32[2,128]{1,0:T(2,128)} %bitcast.5, s32[2,128]{1,0:T(2,128)} %bitcast.7), custom_call_target="tpu_custom_call" | custom-call | tf_op jit(solution)/shard_map/send_grads/pallas_call | solution.py:392
  10.1 2.9 %load.1 = (bf16[1024,1024]{1,0:T(8,128)(2,1)S(1)}, bf16[1024,1024]{1,0:T(8,128)(2,1)S(1)}, bf16[1024,1024]{1,0:T(8,128)(2,1)S(1)}) custom-call(bf16[1,1024,1024]{2,1,0:T(8,128)(2,1)} %refs_0_.3, bf16[1,1024,1024]{2,1,0:T(8,128)(2,1)} %refs_1_.1, bf16[1,1024,1024]{2,1,0:T(8,128)(2,1)} %refs_2_.1), custom_call_target="tpu_custom_call" | custom-call | tf_op jit(solution)/shard_map/load/pallas_call | solution.py:412
  13.0 1.1 %collective-permute-start.4 = (bf16[96,1024]{1,0:T(8,128)(2,1)S(1)}, bf16[96,1024]{1,0:T(8,128)(2,1)S(1)}, u32[]{:S(2)}, u32[]{:S(2)}) collective-permute-start(bf16[96,1024]{1,0:T(8,128)(2,1)S(1)} %land.14), channel_id=1, source_target_pairs={{0,8},{1,9},{2,10},{3,11},{4,12},{5,13},{6,14},{7,15},{8,0},{9,1},... | collective-permute-start | bytes 589832 | tf_op jit(solution)/shard_map/ppermute | solution.py:281
  14.6 2.1 %collective-permute-done.1.refs_1_ = bf16[96,1024]{1,0:T(8,128)(2,1)S(1)} collective-permute-done((bf16[96,1024]{1,0:T(8,128)(2,1)S(1)}, bf16[96,1024]{1,0:T(8,128)(2,1)S(1)}, u32[]{:S(2)}, u32[]{:S(2)}) %collective-permute-start.1) | collective-permute-done | bytes 196640 | tf_op jit(solution)/shard_map/ppermute | solution.py:281
  16.8 2.1 %collective-permute-start.3 = (bf16[96,1024]{1,0:T(8,128)(2,1)S(1)}, bf16[96,1024]{1,0:T(8,128)(2,1)S(1)}, u32[]{:S(2)}, u32[]{:S(2)}) collective-permute-start(bf16[96,1024]{1,0:T(8,128)(2,1)S(1)} %get-tuple-element.307.first_ref), channel_id=1, source_target_pairs={{0,2},{1,3},{2,0},{3,1},{4,6},{5,7},{6,4},{7,5},{8,10},{9,11},{10,... | collective-permute-start | bytes 589832 | tf_op jit(solution)/shard_map/ppermute | solution.py:277
  18.9 2.5 %collective-permute-done.5.refs_0_ = bf16[96,1024]{1,0:T(8,128)(2,1)S(1)} collective-permute-done((bf16[96,1024]{1,0:T(8,128)(2,1)S(1)}, bf16[96,1024]{1,0:T(8,128)(2,1)S(1)}, u32[]{:S(2)}, u32[]{:S(2)}) %collective-permute-start.5) | collective-permute-done | bytes 196640 | tf_op jit(solution)/shard_map/ppermute | solution.py:277
  21.4 2.6 %ffn.4 = (bf16[1024,384]{1,0:T(8,128)(2,1)S(1)}, bf16[192,1024]{1,0:T(8,128)(2,1)S(1)}, bf16[192,1024]{1,0:T(8,128)(2,1)S(1)}) custom-call(bf16[192,1024]{1,0:T(8,128)(2,1)S(1)} %pair.10.refs_0_, bf16[192,1024]{1,0:T(8,128)(2,1)S(1)} %land_core.9.refs_1_, bf16[1024,1024]{1,0:T(8,128)(2,1)S(1)} %get-tuple-element.358.refs_2_, ...), custom_call_target="tpu_custom_call" | custom-call | tf_op jit(solution)/shard_map/ffn/pallas_call | solution.py:375
  24.1 0.9 %collective-permute-done.4.refs_1_ = bf16[96,1024]{1,0:T(8,128)(2,1)S(1)} collective-permute-done((bf16[96,1024]{1,0:T(8,128)(2,1)S(1)}, bf16[96,1024]{1,0:T(8,128)(2,1)S(1)}, u32[]{:S(2)}, u32[]{:S(2)}) %collective-permute-start.4) | collective-permute-done | bytes 196640 | tf_op jit(solution)/shard_map/ppermute | solution.py:281
  24.9 1.5 %collective-permute-start.7 = (bf16[96,1024]{1,0:T(8,128)(2,1)S(1)}, bf16[96,1024]{1,0:T(8,128)(2,1)S(1)}, u32[]{:S(2)}, u32[]{:S(2)}) collective-permute-start(bf16[96,1024]{1,0:T(8,128)(2,1)S(1)} %get-tuple-element.346.first_ref), channel_id=1, source_target_pairs={{0,2},{1,3},{2,0},{3,1},{4,6},{5,7},{6,4},{7,5},{8,10},{9,11},{10,... | collective-permute-start | bytes 589832 | tf_op jit(solution)/shard_map/ppermute | solution.py:277
  26.5 3.1 %collective-permute-start.8 = (bf16[96,1024]{1,0:T(8,128)(2,1)S(1)}, bf16[96,1024]{1,0:T(8,128)(2,1)S(1)}, u32[]{:S(2)}, u32[]{:S(2)}) collective-permute-start(bf16[96,1024]{1,0:T(8,128)(2,1)S(1)} %get-tuple-element.296), channel_id=1, source_target_pairs={{0,12},{1,13},{2,14},{3,15},{4,0},{5,1},{6,2},{7,3},{8,4},{9,5},{1... | collective-permute-start | bytes 589832 | tf_op jit(solution)/shard_map/ppermute | solution.py:281
  30.0 2.3 %collective-permute-done.11.refs_0_ = bf16[384,1024]{1,0:T(8,128)(2,1)S(1)} collective-permute-done((bf16[384,1024]{1,0:T(8,128)(2,1)S(1)}, bf16[384,1024]{1,0:T(8,128)(2,1)S(1)}, u32[]{:S(2)}, u32[]{:S(2)}) %collective-permute-start.11) | collective-permute-done | bytes 786464 | tf_op jit(solution)/shard_map/ppermute | solution.py:277
  32.6 1.3 %collective-permute-start.15 = (bf16[96,1024]{1,0:T(8,128)(2,1)S(1)}, bf16[96,1024]{1,0:T(8,128)(2,1)S(1)}, u32[]{:S(2)}, u32[]{:S(2)}) collective-permute-start(bf16[96,1024]{1,0:T(8,128)(2,1)S(1)} %fold.4), channel_id=1, source_target_pairs={{0,2},{1,3},{2,0},{3,1},{4,6},{5,7},{6,4},{7,5},{8,10},{9,11},{10,... | collective-permute-start | bytes 589832 | tf_op jit(solution)/shard_map/ppermute | solution.py:277
  33.9 2.6 %ffn.5 = (bf16[1024,384]{1,0:T(8,128)(2,1)S(1)}, bf16[192,1024]{1,0:T(8,128)(2,1)S(1)}, bf16[192,1024]{1,0:T(8,128)(2,1)S(1)}) custom-call(bf16[192,1024]{1,0:T(8,128)(2,1)S(1)} %pair.11.second_ref.refs_0_, bf16[192,1024]{1,0:T(8,128)(2,1)S(1)} %get-tuple-element.313.refs_1_, bf16[1024,1024]{1,0:T(8,128)(2,1)S(1)} %get-tuple-element.358.refs_2_, ...), custom_call_target="tpu_custom_call" | custom-call | tf_op jit(solution)/shard_map/ffn/pallas_call | solution.py:375
  37.4 1.5 %collective-permute-start.13 = (bf16[96,1024]{1,0:T(8,128)(2,1)S(1)}, bf16[96,1024]{1,0:T(8,128)(2,1)S(1)}, u32[]{:S(2)}, u32[]{:S(2)}) collective-permute-start(bf16[96,1024]{1,0:T(8,128)(2,1)S(1)} %get-tuple-element.449.first_ref), channel_id=1, source_target_pairs={{0,2},{1,3},{2,0},{3,1},{4,6},{5,7},{6,4},{7,5},{8,10},{9,11},{10,... | collective-permute-start | bytes 589832 | tf_op jit(solution)/shard_map/ppermute | solution.py:277
  39.0 1.1 %collective-permute-start.14 = (bf16[96,1024]{1,0:T(8,128)(2,1)S(1)}, bf16[96,1024]{1,0:T(8,128)(2,1)S(1)}, u32[]{:S(2)}, u32[]{:S(2)}) collective-permute-start(bf16[96,1024]{1,0:T(8,128)(2,1)S(1)} %get-tuple-element.334), channel_id=1, source_target_pairs={{0,8},{1,9},{2,10},{3,11},{4,12},{5,13},{6,14},{7,15},{8,0},{9,1},... | collective-permute-start | bytes 589832 | tf_op jit(solution)/shard_map/ppermute | solution.py:281
  40.2 2.6 %ffn.6 = (bf16[1024,384]{1,0:T(8,128)(2,1)S(1)}, bf16[192,1024]{1,0:T(8,128)(2,1)S(1)}, bf16[192,1024]{1,0:T(8,128)(2,1)S(1)}) custom-call(bf16[192,1024]{1,0:T(8,128)(2,1)S(1)} %pair.13.refs_0_, bf16[192,1024]{1,0:T(8,128)(2,1)S(1)} %land_core.11.refs_1_, bf16[1024,1024]{1,0:T(8,128)(2,1)S(1)} %get-tuple-element.358.refs_2_, ...), custom_call_target="tpu_custom_call" | custom-call | tf_op jit(solution)/shard_map/ffn/pallas_call | solution.py:375
  43.6 0.8 %collective-permute-start.18 = (bf16[96,1024]{1,0:T(8,128)(2,1)S(1)}, bf16[96,1024]{1,0:T(8,128)(2,1)S(1)}, u32[]{:S(2)}, u32[]{:S(2)}) collective-permute-start(bf16[96,1024]{1,0:T(8,128)(2,1)S(1)} %fold.5), channel_id=1, source_target_pairs={{0,2},{1,3},{2,0},{3,1},{4,6},{5,7},{6,4},{7,5},{8,10},{9,11},{10,... | collective-permute-start | bytes 589832 | tf_op jit(solution)/shard_map/ppermute | solution.py:277
  44.4 2.6 %ffn.7 = (bf16[1024,384]{1,0:T(8,128)(2,1)S(1)}, bf16[192,1024]{1,0:T(8,128)(2,1)S(1)}, bf16[192,1024]{1,0:T(8,128)(2,1)S(1)}) custom-call(bf16[192,1024]{1,0:T(8,128)(2,1)S(1)} %pair.14.second_ref.refs_0_, bf16[192,1024]{1,0:T(8,128)(2,1)S(1)} %get-tuple-element.357.refs_1_, bf16[1024,1024]{1,0:T(8,128)(2,1)S(1)} %get-tuple-element.358.refs_2_, ...), custom_call_target="tpu_custom_call" | custom-call | tf_op jit(solution)/shard_map/ffn/pallas_call | solution.py:375
  47.1 2.1 %collective-permute-done.14.refs_1_ = bf16[96,1024]{1,0:T(8,128)(2,1)S(1)} collective-permute-done((bf16[96,1024]{1,0:T(8,128)(2,1)S(1)}, bf16[96,1024]{1,0:T(8,128)(2,1)S(1)}, u32[]{:S(2)}, u32[]{:S(2)}) %collective-permute-start.14) | collective-permute-done | bytes 196640 | tf_op jit(solution)/shard_map/ppermute | solution.py:281
  49.4 1.3 %collective-permute-start.20 = (bf16[96,1024]{1,0:T(8,128)(2,1)S(1)}, bf16[96,1024]{1,0:T(8,128)(2,1)S(1)}, u32[]{:S(2)}, u32[]{:S(2)}) collective-permute-start(bf16[96,1024]{1,0:T(8,128)(2,1)S(1)} %fold.6), channel_id=1, source_target_pairs={{0,2},{1,3},{2,0},{3,1},{4,6},{5,7},{6,4},{7,5},{8,10},{9,11},{10,... | collective-permute-start | bytes 589832 | tf_op jit(solution)/shard_map/ppermute | solution.py:277
  50.7 0.9 %collective-permute-start.23 = (bf16[96,1024]{1,0:T(8,128)(2,1)S(1)}, bf16[96,1024]{1,0:T(8,128)(2,1)S(1)}, u32[]{:S(2)}, u32[]{:S(2)}) collective-permute-start(bf16[96,1024]{1,0:T(8,128)(2,1)S(1)} %fold.7), channel_id=1, source_target_pairs={{0,2},{1,3},{2,0},{3,1},{4,6},{5,7},{6,4},{7,5},{8,10},{9,11},{10,... | collective-permute-start | bytes 589832 | tf_op jit(solution)/shard_map/ppermute | solution.py:277
  51.7 2.4 %collective-permute-start.22 = (bf16[96,1024]{1,0:T(8,128)(2,1)S(1)}, bf16[96,1024]{1,0:T(8,128)(2,1)S(1)}, u32[]{:S(2)}, u32[]{:S(2)}) collective-permute-start(bf16[96,1024]{1,0:T(8,128)(2,1)S(1)} %total.5), channel_id=1, source_target_pairs={{0,12},{1,13},{2,14},{3,15},{4,0},{5,1},{6,2},{7,3},{8,4},{9,5},{1... | collective-permute-start | bytes 589832 | tf_op jit(solution)/shard_map/ppermute | solution.py:281
  54.2 2.6 %collective-permute-done.20.refs_0_ = bf16[96,1024]{1,0:T(8,128)(2,1)S(1)} collective-permute-done((bf16[96,1024]{1,0:T(8,128)(2,1)S(1)}, bf16[96,1024]{1,0:T(8,128)(2,1)S(1)}, u32[]{:S(2)}, u32[]{:S(2)}) %collective-permute-start.20) | collective-permute-done | bytes 196640 | tf_op jit(solution)/shard_map/ppermute | solution.py:277
  59.0 2.8 %collective-permute-start.28 = (bf16[96,1024]{1,0:T(8,128)(2,1)S(1)}, bf16[96,1024]{1,0:T(8,128)(2,1)S(1)}, u32[]{:S(2)}, u32[]{:S(2)}) collective-permute-start(bf16[96,1024]{1,0:T(8,128)(2,1)S(1)} %total.7), channel_id=1, source_target_pairs={{0,8},{1,9},{2,10},{3,11},{4,12},{5,13},{6,14},{7,15},{8,0},{9,1},... | collective-permute-start | bytes 589832 | tf_op jit(solution)/shard_map/ppermute | solution.py:281
  62.7 3.4 %collective-permute-done.25.refs_1_ = bf16[96,1024]{1,0:T(8,128)(2,1)S(1)} collective-permute-done((bf16[96,1024]{1,0:T(8,128)(2,1)S(1)}, bf16[96,1024]{1,0:T(8,128)(2,1)S(1)}, u32[]{:S(2)}, u32[]{:S(2)}) %collective-permute-start.25) | collective-permute-done | bytes 196640 | tf_op jit(solution)/shard_map/ppermute | solution.py:281
  66.3 2.4 %first_grad.1.refs_2_.first_ref = f32[1024,1024]{1,0:T(8,128)S(1)} custom-call(bf16[1024,384]{1,0:T(8,128)(2,1)S(1)} %get-tuple-element.453.refs_2_.refs_0_, bf16[1024,384]{1,0:T(8,128)(2,1)S(1)} %get-tuple-element.454.refs_3_.refs_1_, bf16[1024,384]{1,0:T(8,128)(2,1)S(1)} %get-tuple-element.475.refs_1_.refs_2_.refs_0_, bf16[192,1024]{1,0:T(8,128)(2,1)S(1)} %pair.16.refs_3_, ...), custom_call_target="tpu_custom_call" | custom-call | tf_op jit(solution)/shard_map/first_grad/pallas_call | solution.py:447
  68.7 4.7 %collective-permute-done.28.refs_1_ = bf16[96,1024]{1,0:T(8,128)(2,1)S(1)} collective-permute-done((bf16[96,1024]{1,0:T(8,128)(2,1)S(1)}, bf16[96,1024]{1,0:T(8,128)(2,1)S(1)}, u32[]{:S(2)}, u32[]{:S(2)}) %collective-permute-start.28) | collective-permute-done | bytes 196640 | tf_op jit(solution)/shard_map/ppermute | solution.py:281
  73.5 1.4 %combine.1 = bf16[128,1024]{1,0:T(8,128)(2,1)} custom-call(s32[1]{0:T(128)} %bitcast.plane_ref, bf16[128,1024]{1,0:T(8,128)(2,1)S(1)} %copy-done, s32[2,128]{1,0:T(2,128)S(1)} %bitcast.6, s32[2,128]{1,0:T(2,128)S(1)} %bitcast.8, bf16[96,1024]{1,0:T(8,128)(2,1)S(1)} %total.4.refs_0_, bf16[96,1024]{1,0:T(8,128)(2,1)S(1)} %get-tuple-element.471.refs_1_, ...), custom_call_target="tpu_custom_call" | custom-call | tf_op jit(solution)/shard_map/combine/pallas_call | solution.py:518
  75.2 2.7 %last_grad.1 = bf16[1,1024,1024]{2,1,0:T(8,128)(2,1)} custom-call(f32[1024,1024]{1,0:T(8,128)S(1)} %first_grad.1.refs_2_.first_ref, bf16[1024,384]{1,0:T(8,128)(2,1)S(1)} %get-tuple-element.475.refs_1_.refs_2_.refs_0_, bf16[1024,384]{1,0:T(8,128)(2,1)S(1)} %get-tuple-element.476.refs_2_.refs_1_, bf16[192,1024]{1,0:T(8,128)(2,1)S(1)} %pair.19.refs_2_, ...), custom_call_target="tpu_custom_call" | custom-call | tf_op jit(solution)/shard_map/last_grad/pallas_call | solution.py:459
  (88 shorter events, 7.1 us)
Async XLA Ops:
  2.1 12.5 %collective-permute-start = (bf16[96,1024]{1,0:T(8,128)(2,1)S(1)}, bf16[96,1024]{1,0:T(8,128)(2,1)S(1)}, u32[]{:S(2)}, u32[]{:S(2)}) collective-permute-start(bf16[96,1024]{1,0:T(8,128)(2,1)S(1)} %get-tuple-element.241), channel_id=1, source_target_pairs={{0,12},{1,13},{2,14},{3,15},{4,0},{5,1},{6,2},{7,3},{8,4},{9,5},{1... | collective-permute-start | bytes 589832 | tf_op jit(solution)/shard_map/ppermute | solution.py:281
  7.2 9.5 %collective-permute-start.1 = (bf16[96,1024]{1,0:T(8,128)(2,1)S(1)}, bf16[96,1024]{1,0:T(8,128)(2,1)S(1)}, u32[]{:S(2)}, u32[]{:S(2)}) collective-permute-start(bf16[96,1024]{1,0:T(8,128)(2,1)S(1)} %get-tuple-element.242), channel_id=1, source_target_pairs={{0,4},{1,5},{2,6},{3,7},{4,8},{5,9},{6,10},{7,11},{8,12},{9,13},{1... | collective-permute-start | bytes 589832 | tf_op jit(solution)/shard_map/ppermute | solution.py:281
  7.2 9.5 %collective-permute-start.2 = (bf16[96,1024]{1,0:T(8,128)(2,1)S(1)}, bf16[96,1024]{1,0:T(8,128)(2,1)S(1)}, u32[]{:S(2)}, u32[]{:S(2)}) collective-permute-start(bf16[96,1024]{1,0:T(8,128)(2,1)S(1)} %get-tuple-element.275.first_ref), channel_id=1, source_target_pairs={{0,2},{1,3},{2,0},{3,1},{4,6},{5,7},{6,4},{7,5},{8,10},{9,11},{10,... | collective-permute-start | bytes 589832 | tf_op jit(solution)/shard_map/ppermute | solution.py:277
  13.0 11.9 %collective-permute-start.4 = (bf16[96,1024]{1,0:T(8,128)(2,1)S(1)}, bf16[96,1024]{1,0:T(8,128)(2,1)S(1)}, u32[]{:S(2)}, u32[]{:S(2)}) collective-permute-start(bf16[96,1024]{1,0:T(8,128)(2,1)S(1)} %land.14), channel_id=1, source_target_pairs={{0,8},{1,9},{2,10},{3,11},{4,12},{5,13},{6,14},{7,15},{8,0},{9,1},... | collective-permute-start | bytes 589832 | tf_op jit(solution)/shard_map/ppermute | solution.py:281
  14.1 7.3 %collective-permute-start.5 = (bf16[96,1024]{1,0:T(8,128)(2,1)S(1)}, bf16[96,1024]{1,0:T(8,128)(2,1)S(1)}, u32[]{:S(2)}, u32[]{:S(2)}) collective-permute-start(bf16[96,1024]{1,0:T(8,128)(2,1)S(1)} %get-tuple-element.414.first_ref), channel_id=1, source_target_pairs={{0,2},{1,3},{2,0},{3,1},{4,6},{5,7},{6,4},{7,5},{8,10},{9,11},{10,... | collective-permute-start | bytes 589832 | tf_op jit(solution)/shard_map/ppermute | solution.py:277
  16.8 8.2 %collective-permute-start.3 = (bf16[96,1024]{1,0:T(8,128)(2,1)S(1)}, bf16[96,1024]{1,0:T(8,128)(2,1)S(1)}, u32[]{:S(2)}, u32[]{:S(2)}) collective-permute-start(bf16[96,1024]{1,0:T(8,128)(2,1)S(1)} %get-tuple-element.307.first_ref), channel_id=1, source_target_pairs={{0,2},{1,3},{2,0},{3,1},{4,6},{5,7},{6,4},{7,5},{8,10},{9,11},{10,... | collective-permute-start | bytes 589832 | tf_op jit(solution)/shard_map/ppermute | solution.py:277
  18.9 2.6 %collective-permute-start.6 = (bf16[192,1024]{1,0:T(8,128)(2,1)S(1)}, bf16[192,1024]{1,0:T(8,128)(2,1)S(1)}, u32[]{:S(2)}, u32[]{:S(2)}) collective-permute-start(bf16[192,1024]{1,0:T(8,128)(2,1)S(1)} %pair.10.refs_0_), channel_id=1, source_target_pairs={{0,1},{1,0},{2,3},{3,2},{4,5},{5,4},{6,7},{7,6},{8,9},{9,8},{10,11... | collective-permute-start | bytes 1179656 | tf_op jit(solution)/shard_map/ppermute | solution.py:277
  21.4 8.6 %collective-permute-start.10 = (bf16[96,1024]{1,0:T(8,128)(2,1)S(1)}, bf16[96,1024]{1,0:T(8,128)(2,1)S(1)}, u32[]{:S(2)}, u32[]{:S(2)}) collective-permute-start(bf16[96,1024]{1,0:T(8,128)(2,1)S(1)} %get-tuple-element.329.first_ref), channel_id=1, source_target_pairs={{0,2},{1,3},{2,0},{3,1},{4,6},{5,7},{6,4},{7,5},{8,10},{9,11},{10,... | collective-permute-start | bytes 589832 | tf_op jit(solution)/shard_map/ppermute | solution.py:277
  24.9 11.6 %collective-permute-start.7 = (bf16[96,1024]{1,0:T(8,128)(2,1)S(1)}, bf16[96,1024]{1,0:T(8,128)(2,1)S(1)}, u32[]{:S(2)}, u32[]{:S(2)}) collective-permute-start(bf16[96,1024]{1,0:T(8,128)(2,1)S(1)} %get-tuple-element.346.first_ref), channel_id=1, source_target_pairs={{0,2},{1,3},{2,0},{3,1},{4,6},{5,7},{6,4},{7,5},{8,10},{9,11},{10,... | collective-permute-start | bytes 589832 | tf_op jit(solution)/shard_map/ppermute | solution.py:277
  26.5 10.1 %collective-permute-start.8 = (bf16[96,1024]{1,0:T(8,128)(2,1)S(1)}, bf16[96,1024]{1,0:T(8,128)(2,1)S(1)}, u32[]{:S(2)}, u32[]{:S(2)}) collective-permute-start(bf16[96,1024]{1,0:T(8,128)(2,1)S(1)} %get-tuple-element.296), channel_id=1, source_target_pairs={{0,12},{1,13},{2,14},{3,15},{4,0},{5,1},{6,2},{7,3},{8,4},{9,5},{1... | collective-permute-start | bytes 589832 | tf_op jit(solution)/shard_map/ppermute | solution.py:281
  29.6 7.8 %collective-permute-start.9 = (bf16[96,1024]{1,0:T(8,128)(2,1)S(1)}, bf16[96,1024]{1,0:T(8,128)(2,1)S(1)}, u32[]{:S(2)}, u32[]{:S(2)}) collective-permute-start(bf16[96,1024]{1,0:T(8,128)(2,1)S(1)} %get-tuple-element.297), channel_id=1, source_target_pairs={{0,4},{1,5},{2,6},{3,7},{4,8},{5,9},{6,10},{7,11},{8,12},{9,13},{1... | collective-permute-start | bytes 589832 | tf_op jit(solution)/shard_map/ppermute | solution.py:281
  29.9 2.4 %collective-permute-start.11 = (bf16[384,1024]{1,0:T(8,128)(2,1)S(1)}, bf16[384,1024]{1,0:T(8,128)(2,1)S(1)}, u32[]{:S(2)}, u32[]{:S(2)}) collective-permute-start(bf16[384,1024]{1,0:T(8,128)(2,1)S(1)} %pair.12), channel_id=1, source_target_pairs={{0,1},{1,0},{2,3},{3,2},{4,5},{5,4},{6,7},{7,6},{8,9},{9,8},{10,11... | collective-permute-start | bytes 2359304 | tf_op jit(solution)/shard_map/ppermute | solution.py:277
  32.3 5.1 %collective-permute-start.12 = (bf16[192,1024]{1,0:T(8,128)(2,1)S(1)}, bf16[192,1024]{1,0:T(8,128)(2,1)S(1)}, u32[]{:S(2)}, u32[]{:S(2)}) collective-permute-start(bf16[192,1024]{1,0:T(8,128)(2,1)S(1)} %pair.13.refs_0_), channel_id=1, source_target_pairs={{0,1},{1,0},{2,3},{3,2},{4,5},{5,4},{6,7},{7,6},{8,9},{9,8},{10,11... | collective-permute-start | bytes 1179656 | tf_op jit(solution)/shard_map/ppermute | solution.py:277
  32.6 10.2 %collective-permute-start.15 = (bf16[96,1024]{1,0:T(8,128)(2,1)S(1)}, bf16[96,1024]{1,0:T(8,128)(2,1)S(1)}, u32[]{:S(2)}, u32[]{:S(2)}) collective-permute-start(bf16[96,1024]{1,0:T(8,128)(2,1)S(1)} %fold.4), channel_id=1, source_target_pairs={{0,2},{1,3},{2,0},{3,1},{4,6},{5,7},{6,4},{7,5},{8,10},{9,11},{10,... | collective-permute-start | bytes 589832 | tf_op jit(solution)/shard_map/ppermute | solution.py:277
  37.4 9.7 %collective-permute-start.13 = (bf16[96,1024]{1,0:T(8,128)(2,1)S(1)}, bf16[96,1024]{1,0:T(8,128)(2,1)S(1)}, u32[]{:S(2)}, u32[]{:S(2)}) collective-permute-start(bf16[96,1024]{1,0:T(8,128)(2,1)S(1)} %get-tuple-element.449.first_ref), channel_id=1, source_target_pairs={{0,2},{1,3},{2,0},{3,1},{4,6},{5,7},{6,4},{7,5},{8,10},{9,11},{10,... | collective-permute-start | bytes 589832 | tf_op jit(solution)/shard_map/ppermute | solution.py:277
  39.0 10.3 %collective-permute-start.14 = (bf16[96,1024]{1,0:T(8,128)(2,1)S(1)}, bf16[96,1024]{1,0:T(8,128)(2,1)S(1)}, u32[]{:S(2)}, u32[]{:S(2)}) collective-permute-start(bf16[96,1024]{1,0:T(8,128)(2,1)S(1)} %get-tuple-element.334), channel_id=1, source_target_pairs={{0,8},{1,9},{2,10},{3,11},{4,12},{5,13},{6,14},{7,15},{8,0},{9,1},... | collective-permute-start | bytes 589832 | tf_op jit(solution)/shard_map/ppermute | solution.py:281
  40.1 2.7 %collective-permute-start.16 = (bf16[384,1024]{1,0:T(8,128)(2,1)S(1)}, bf16[384,1024]{1,0:T(8,128)(2,1)S(1)}, u32[]{:S(2)}, u32[]{:S(2)}) collective-permute-start(bf16[384,1024]{1,0:T(8,128)(2,1)S(1)} %pair.15), channel_id=1, source_target_pairs={{0,1},{1,0},{2,3},{3,2},{4,5},{5,4},{6,7},{7,6},{8,9},{9,8},{10,11... | collective-permute-start | bytes 2359304 | tf_op jit(solution)/shard_map/ppermute | solution.py:277
  42.9 6.4 %collective-permute-start.17 = (bf16[192,1024]{1,0:T(8,128)(2,1)S(1)}, bf16[192,1024]{1,0:T(8,128)(2,1)S(1)}, u32[]{:S(2)}, u32[]{:S(2)}) collective-permute-start(bf16[192,1024]{1,0:T(8,128)(2,1)S(1)} %get-tuple-element.378), channel_id=1, source_target_pairs={{0,1},{1,0},{2,3},{3,2},{4,5},{5,4},{6,7},{7,6},{8,9},{9,8},{10,11... | collective-permute-start | bytes 1179656 | tf_op jit(solution)/shard_map/ppermute | solution.py:277
  43.6 7.1 %collective-permute-start.18 = (bf16[96,1024]{1,0:T(8,128)(2,1)S(1)}, bf16[96,1024]{1,0:T(8,128)(2,1)S(1)}, u32[]{:S(2)}, u32[]{:S(2)}) collective-permute-start(bf16[96,1024]{1,0:T(8,128)(2,1)S(1)} %fold.5), channel_id=1, source_target_pairs={{0,2},{1,3},{2,0},{3,1},{4,6},{5,7},{6,4},{7,5},{8,10},{9,11},{10,... | collective-permute-start | bytes 589832 | tf_op jit(solution)/shard_map/ppermute | solution.py:277
  47.0 3.6 %collective-permute-start.19 = (bf16[192,1024]{1,0:T(8,128)(2,1)S(1)}, bf16[192,1024]{1,0:T(8,128)(2,1)S(1)}, u32[]{:S(2)}, u32[]{:S(2)}) collective-permute-start(bf16[192,1024]{1,0:T(8,128)(2,1)S(1)} %get-tuple-element.396), channel_id=1, source_target_pairs={{0,1},{1,0},{2,3},{3,2},{4,5},{5,4},{6,7},{7,6},{8,9},{9,8},{10,11... | collective-permute-start | bytes 1179656 | tf_op jit(solution)/shard_map/ppermute | solution.py:277
  49.4 7.5 %collective-permute-start.20 = (bf16[96,1024]{1,0:T(8,128)(2,1)S(1)}, bf16[96,1024]{1,0:T(8,128)(2,1)S(1)}, u32[]{:S(2)}, u32[]{:S(2)}) collective-permute-start(bf16[96,1024]{1,0:T(8,128)(2,1)S(1)} %fold.6), channel_id=1, source_target_pairs={{0,2},{1,3},{2,0},{3,1},{4,6},{5,7},{6,4},{7,5},{8,10},{9,11},{10,... | collective-permute-start | bytes 589832 | tf_op jit(solution)/shard_map/ppermute | solution.py:277
  50.7 8.2 %collective-permute-start.23 = (bf16[96,1024]{1,0:T(8,128)(2,1)S(1)}, bf16[96,1024]{1,0:T(8,128)(2,1)S(1)}, u32[]{:S(2)}, u32[]{:S(2)}) collective-permute-start(bf16[96,1024]{1,0:T(8,128)(2,1)S(1)} %fold.7), channel_id=1, source_target_pairs={{0,2},{1,3},{2,0},{3,1},{4,6},{5,7},{6,4},{7,5},{8,10},{9,11},{10,... | collective-permute-start | bytes 589832 | tf_op jit(solution)/shard_map/ppermute | solution.py:277
  51.7 7.3 %collective-permute-start.22 = (bf16[96,1024]{1,0:T(8,128)(2,1)S(1)}, bf16[96,1024]{1,0:T(8,128)(2,1)S(1)}, u32[]{:S(2)}, u32[]{:S(2)}) collective-permute-start(bf16[96,1024]{1,0:T(8,128)(2,1)S(1)} %total.5), channel_id=1, source_target_pairs={{0,12},{1,13},{2,14},{3,15},{4,0},{5,1},{6,2},{7,3},{8,4},{9,5},{1... | collective-permute-start | bytes 589832 | tf_op jit(solution)/shard_map/ppermute | solution.py:281
  54.1 2.7 %collective-permute-start.21 = (bf16[192,1024]{1,0:T(8,128)(2,1)S(1)}, bf16[192,1024]{1,0:T(8,128)(2,1)S(1)}, u32[]{:S(2)}, u32[]{:S(2)}) collective-permute-start(bf16[192,1024]{1,0:T(8,128)(2,1)S(1)} %pair.16.refs_3_), channel_id=1, source_target_pairs={{0,1},{1,0},{2,3},{3,2},{4,5},{5,4},{6,7},{7,6},{8,9},{9,8},{10,11... | collective-permute-start | bytes 1179656 | tf_op jit(solution)/shard_map/ppermute | solution.py:277
  56.9 9.2 %collective-permute-start.25 = (bf16[96,1024]{1,0:T(8,128)(2,1)S(1)}, bf16[96,1024]{1,0:T(8,128)(2,1)S(1)}, u32[]{:S(2)}, u32[]{:S(2)}) collective-permute-start(bf16[96,1024]{1,0:T(8,128)(2,1)S(1)} %total.6), channel_id=1, source_target_pairs={{0,4},{1,5},{2,6},{3,7},{4,8},{5,9},{6,10},{7,11},{8,12},{9,13},{1... | collective-permute-start | bytes 589832 | tf_op jit(solution)/shard_map/ppermute | solution.py:281
  57.6 8.5 %collective-permute-start.24 = (bf16[96,1024]{1,0:T(8,128)(2,1)S(1)}, bf16[96,1024]{1,0:T(8,128)(2,1)S(1)}, u32[]{:S(2)}, u32[]{:S(2)}) collective-permute-start(bf16[96,1024]{1,0:T(8,128)(2,1)S(1)} %get-tuple-element.463.first_ref), channel_id=1, source_target_pairs={{0,2},{1,3},{2,0},{3,1},{4,6},{5,7},{6,4},{7,5},{8,10},{9,11},{10,... | collective-permute-start | bytes 589832 | tf_op jit(solution)/shard_map/ppermute | solution.py:277
  59.0 14.4 %collective-permute-start.28 = (bf16[96,1024]{1,0:T(8,128)(2,1)S(1)}, bf16[96,1024]{1,0:T(8,128)(2,1)S(1)}, u32[]{:S(2)}, u32[]{:S(2)}) collective-permute-start(bf16[96,1024]{1,0:T(8,128)(2,1)S(1)} %total.7), channel_id=1, source_target_pairs={{0,8},{1,9},{2,10},{3,11},{4,12},{5,13},{6,14},{7,15},{8,0},{9,1},... | collective-permute-start | bytes 589832 | tf_op jit(solution)/shard_map/ppermute | solution.py:281
  61.8 11.6 %collective-permute-start.27 = (bf16[96,1024]{1,0:T(8,128)(2,1)S(1)}, bf16[96,1024]{1,0:T(8,128)(2,1)S(1)}, u32[]{:S(2)}, u32[]{:S(2)}) collective-permute-start(bf16[96,1024]{1,0:T(8,128)(2,1)S(1)} %get-tuple-element.477.first_ref), channel_id=1, source_target_pairs={{0,2},{1,3},{2,0},{3,1},{4,6},{5,7},{6,4},{7,5},{8,10},{9,11},{10,... | collective-permute-start | bytes 589832 | tf_op jit(solution)/shard_map/ppermute | solution.py:277
  62.7 3.5 %collective-permute-start.26 = (bf16[192,1024]{1,0:T(8,128)(2,1)S(1)}, bf16[192,1024]{1,0:T(8,128)(2,1)S(1)}, u32[]{:S(2)}, u32[]{:S(2)}) collective-permute-start(bf16[192,1024]{1,0:T(8,128)(2,1)S(1)} %pair.17.refs_4_), channel_id=1, source_target_pairs={{0,1},{1,0},{2,3},{3,2},{4,5},{5,4},{6,7},{7,6},{8,9},{9,8},{10,11... | collective-permute-start | bytes 1179656 | tf_op jit(solution)/shard_map/ppermute | solution.py:277
  66.2 7.2 %collective-permute-start.29 = (bf16[192,1024]{1,0:T(8,128)(2,1)S(1)}, bf16[192,1024]{1,0:T(8,128)(2,1)S(1)}, u32[]{:S(2)}, u32[]{:S(2)}) collective-permute-start(bf16[192,1024]{1,0:T(8,128)(2,1)S(1)} %pair.18.refs_5_), channel_id=1, source_target_pairs={{0,1},{1,0},{2,3},{3,2},{4,5},{5,4},{6,7},{7,6},{8,9},{9,8},{10,11... | collective-permute-start | bytes 1179656 | tf_op jit(solution)/shard_map/ppermute | solution.py:277
  68.7 4.8 %copy-start = (bf16[128,1024]{1,0:T(8,128)(2,1)S(1)}, bf16[128,1024]{1,0:T(8,128)(2,1)}, u32[]{:S(2)}) copy-start(bf16[128,1024]{1,0:T(8,128)(2,1)} %tokens_ref.1) | copy-start | bytes 786436
  73.4 1.8 %collective-permute-start.30 = (bf16[192,1024]{1,0:T(8,128)(2,1)S(1)}, bf16[192,1024]{1,0:T(8,128)(2,1)S(1)}, u32[]{:S(2)}, u32[]{:S(2)}) collective-permute-start(bf16[192,1024]{1,0:T(8,128)(2,1)S(1)} %pair.19.refs_2_), channel_id=1, source_target_pairs={{0,1},{1,0},{2,3},{3,2},{4,5},{5,4},{6,7},{7,6},{8,9},{9,8},{10,11... | collective-permute-start | bytes 1179656 | tf_op jit(solution)/shard_map/ppermute | solution.py:277
  (2 other events, 9.7 us)
